TPU v7x, 32 devices: a whole 2x2x4 slice. The times are simulated.
32 devices in a mesh: groups: 2 (over y), tensor: 4 (over z), seq: 2 (over x), dp: 2 (over core).
Axes of the slice: x: 2, y: 2, z: 4, core: 2. Of those that a mesh axis runs over, the one named last changes fastest.
Arguments:
- inputs: bfloat16 [8, 512, 8192], P(('groups', 'dp'), 'seq', 'tensor'), parts along dimension 0, may hold values from -6 to 6
- base_weight: bfloat16 [8192, 8192], P(None, 'tensor'), may hold values from -0.09375 to 0.09375
- shrink_table: bfloat16 [8, 8192, 64], P('groups', 'tensor'), parts along dimension 0, may hold values from -0.0625 to 0.0625
- expand_table: bfloat16 [8, 64, 8192], P('groups', None, 'tensor'), parts along dimension 0, may hold values from -0.75 to 0.75
- adapter_ids: int32 [8], P(('groups', 'dp')), parts along dimension 0, may hold values from 0 to 3
Outputs:
- projected: bfloat16 [8, 512, 8192], P(('groups', 'dp'), 'seq', 'tensor'), parts along dimension 0
There are 2 independent parts, one for each index of `groups`. A program takes and returns all parts, laid end to end along the dimension named above; an argument that names none is the same for every part. Nothing has to cross between parts.
All inputs are finite; a program needn't handle non-finite values.
Results may differ from a plain program's by a relative error of at most 0.0075.
Values may be sent and summed in bfloat16 or wider, within the bound.
No kernel may reach another device: no remote copies, remote signals or barrier semaphores. Data moves between devices by JAX's collectives and lax.ppermute only.
A program may use at most 128 MiB of HBM per device.

v0:
```python
import jax
import jax.numpy as jnp
from jax import lax
from jax.sharding import PartitionSpec as P


def local(inputs, base_weight, shrink_table, expand_table, adapter_ids):
    adapters = shrink_table.shape[0]
    picker = (adapter_ids[:, None] == jnp.arange(adapters, dtype=jnp.int32)[None, :]).astype(
        jnp.bfloat16
    )
    local_shrink = jnp.einsum(
        "ca,adr->cdr", picker, shrink_table, preferred_element_type=jnp.float32
    ).astype(jnp.bfloat16)
    local_expand = jnp.einsum(
        "ca,are->cre", picker, expand_table, preferred_element_type=jnp.float32
    ).astype(jnp.bfloat16)
    partial_shrink = jnp.einsum(
        "ctd,cdr->ctr", inputs, local_shrink, preferred_element_type=jnp.float32
    )
    base = jnp.einsum(
        "ctd,de->cte",
        lax.all_gather(inputs, "tensor", axis=2, tiled=True),
        base_weight,
        preferred_element_type=jnp.float32,
    )
    shrink_total = lax.psum(partial_shrink.astype(jnp.bfloat16), "tensor")
    adapted = jnp.einsum(
        "ctr,cre->cte", shrink_total, local_expand, preferred_element_type=jnp.float32
    )
    return (base + adapted).astype(jnp.bfloat16)


def solution(mesh):
    return jax.shard_map(
        local,
        mesh=mesh,
        in_specs=(
            P(("groups", "dp"), "seq", "tensor"),
            P(None, "tensor"),
            P("groups", "tensor", None),
            P("groups", None, "tensor"),
            P(("groups", "dp")),
        ),
        out_specs=P(("groups", "dp"), "seq", "tensor"),
        check_vma=False,
    )
```

profile of v0, /device:TPU:0, one launch (start us, length us, event | category | flops | bytes accessed | tf_op | source)
XLA Modules:
  0.0 207.0 jit_solution(13790461597033359237)
XLA Ops:
  6.5 0.0 copy-start
  6.5 0.0 copy-start.1
  6.5 0.0 all-gather.2.cloned.1.call-start
  6.5 0.7 all-gather.2.cloned.1.call-update
  7.3 0.0 copy-start.2
  7.3 0.0 all-reduce.2.cloned.1.call-start
  7.3 0.4 copy-done
  7.8 2.5 %fusion.6 = bf16[2,2048,64]{1,0,2:T(2,128)(2,1)} fusion(bf16[4,2048,64]{1,2,0:T(8,128)(2,1)S(1)} %copy-done, s32[2]{0:T(128)} %param.9), kind=kOutput, calls=%fused_computation.9 | convolution fusion | flops 2097160 | bytes 1572872 | tf_op jit(solution)/shard_map/ca,adr->cdr/dot_general | solution.py:12
  10.2 2.3 %copy.7 = bf16[2,2048,64]{2,1,0:T(8,128)(2,1)} copy(bf16[2,2048,64]{1,0,2:T(2,128)(2,1)} %fusion.6) | data formatting | bytes 1048576 | tf_op jit(solution)/shard_map/ca,adr->cdr/dot_general | solution.py:12
  12.5 0.0 copy-done.1
  12.5 2.6 %fusion.2 = bf16[2,256,64]{1,2,0:T(8,128)(2,1)} fusion(bf16[2,256,2048]{2,1,0:T(8,128)(2,1)S(1)} %copy-done.1, bf16[2,2048,64]{2,1,0:T(8,128)(2,1)} %copy.7), kind=kOutput, calls=%fused_computation.4 | convolution fusion | flops 134250496 | bytes 2686976 | tf_op jit(solution)/shard_map/ctd,cdr->ctr/dot_general | solution.py:18
  15.1 0.0 all-reduce.2.cloned.1.call-update
  15.1 0.0 copy-done.2
  15.1 2.2 %fusion.4 = bf16[2,64,2048]{2,0,1:T(2,128)(2,1)S(1)} fusion(bf16[4,64,2048]{2,1,0:T(8,128)(2,1)} %param.8, s32[2]{0:T(128)S(1)} %copy-done.2), kind=kOutput, calls=%fused_computation.7 | convolution fusion | flops 2097160 | bytes 1572872 | tf_op jit(solution)/shard_map/ca,are->cre/dot_general | solution.py:15
  17.3 144.0 %all-gather.2.cloned.1.call-done = bf16[2,256,8192]{2,1,0:T(8,128)(2,1)} async-done(((bf16[2,256,2048]{2,1,0:T(8,128)(2,1)}), bf16[2,256,8192]{2,1,0:T(8,128)(2,1)}) %all-gather.2.cloned.1.call-update) | async-done | bytes 8388624 | tf_op jit(solution)/shard_map/all_gather | solution.py:23
  161.3 24.8 %fusion = f32[2,256,2048]{2,1,0:T(8,128)} fusion(bf16[2,256,8192]{2,1,0:T(8,128)(2,1)} %all-gather.2.cloned.1.call-done, bf16[8192,2048]{1,0:T(8,128)(2,1)} %param.6), kind=kOutput, calls=%fused_computation | convolution fusion | flops 17179869184 | bytes 46137344 | tf_op jit(solution)/shard_map/ctd,de->cte/dot_general | solution.py:21
  186.1 9.8 %all-reduce.2.cloned.1.call-done = bf16[2,256,64]{1,2,0:T(8,128)(2,1)} async-done(((bf16[2,256,64]{1,2,0:T(8,128)(2,1)}), bf16[2,256,64]{1,2,0:T(8,128)(2,1)}) %all-reduce.2.cloned.1.call-update) | async-done | bytes 65552 | tf_op jit(solution)/shard_map/psum | solution.py:27
  195.8 4.3 %add_convert_fusion = bf16[2,256,2048]{2,1,0:T(8,128)(2,1)} fusion(f32[2,256,2048]{2,1,0:T(8,128)} %fusion, bf16[2,256,64]{1,2,0:T(8,128)(2,1)} %all-reduce.2.cloned.1.call-done, bf16[2,64,2048]{2,0,1:T(2,128)(2,1)S(1)} %fusion.4), kind=kOutput, calls=%fused_computation.2 | convolution fusion | flops 136314880 | bytes 6881280 | tf_op jit(solution)/shard_map/ctr,cre->cte/dot_general | solution.py:28
Async XLA Ops:
  6.5 1.2 copy-start
  6.5 6.0 %copy-start.1 = (bf16[2,256,2048]{2,1,0:T(8,128)(2,1)S(1)}, bf16[2,256,2048]{2,1,0:T(8,128)(2,1)}, u32[]{:S(2)}) copy-start(bf16[2,256,2048]{2,1,0:T(8,128)(2,1)} %param.5) | copy-start | bytes 6291460
  6.5 154.8 %all-gather.2.cloned.1.call-start = ((), (), s32[]{:S(2)}) async-start(), calls=%async_computation | async-start | bytes 10485760 | tf_op jit(solution)/shard_map/all_gather | solution.py:23
  7.3 7.9 %copy-start.2 = (s32[2]{0:T(128)S(1)}, s32[2]{0:T(128)}, u32[]{:S(2)}) copy-start(s32[2]{0:T(128)} %param.9) | copy-start | bytes 28
  7.3 188.5 %all-reduce.2.cloned.1.call-start = ((), (), s32[]{:S(2)}) async-start(), calls=%async_computation.1 | async-start | bytes 131072 | tf_op jit(solution)/shard_map/psum | solution.py:27
Sparse Core Ops, SparseCore 0:
  8.9 152.3 all-gather.1
  163.6 32.1 all-reduce.1
where the time goes:
time: 207 us
  waiting for transfers between devices  154 us (74%)
  matrix products  36.3 us (18%)
  between operations  13.4 us (6%)
  local copies, waits for them, and re-layouts  2.73 us (1%)
    all_gather x1, waiting for transfers between devices, local(): lax.all_gather(inputs, 'tensor', axis=2, tiled=True)  144 us
    dot_general x1, matrix products, local(): jnp.einsum('ctd,de->cte', lax.all_gather(inputs, 'tensor', axis=2, tiled=...  24.8 us
    psum x1, waiting for transfers between devices, local(): shrink_total = lax.psum(partial_shrink.astype(jnp.bfloat16), 'tensor')  9.77 us
    dot_general x1, matrix products, local(): jnp.einsum('ctr,cre->cte', shrink_total, local_expand, preferred_element_...  4.32 us
  transfers between devices with their start and end apart: 2, of which 2 were waited for; matrix products, arithmetic and copies ran while one was open for 17% of the time, Pallas kernels for 0%

commit v1 on v0

v1 whole, which is shorter than its diff:
```python
import jax
import jax.numpy as jnp
from jax import lax
from jax.sharding import PartitionSpec as P

F32, BF16 = jnp.float32, jnp.bfloat16


def low_rank(inputs, shrink_table, expand_table, adapter_ids):
    chats, span, _ = inputs.shape
    rank = shrink_table.shape[-1]
    partial = jnp.concatenate(
        [
            jnp.dot(inputs[c], shrink_table[adapter_ids[c]], preferred_element_type=F32).astype(BF16)
            for c in range(chats)
        ]
    )
    every = lax.all_gather(partial.reshape(-1, 2 * rank), "tensor")
    shrunk = jnp.sum(every.astype(F32), axis=0).astype(BF16).reshape(chats, span, rank)
    return jnp.concatenate(
        [
            jnp.dot(shrunk[c], expand_table[adapter_ids[c]], preferred_element_type=F32)
            for c in range(chats)
        ]
    )


def make_local(n):
    right = [(i, (i + 1) % n) for i in range(n)]
    left = [(i, (i - 1) % n) for i in range(n)]

    def local(inputs, base_weight, shrink_table, expand_table, adapter_ids):
        chats, span, width = inputs.shape
        here = lax.axis_index("tensor")
        own = inputs.reshape(chats * span, width)

        def product(block, owner, first=0):
            rows = lax.dynamic_slice_in_dim(
                base_weight, lax.rem(owner + 2 * n, n) * width + first, block.shape[1], axis=0
            )
            return jnp.dot(block, rows, preferred_element_type=F32)

        total = low_rank(inputs, shrink_table, expand_table, adapter_ids) + product(own, here)
        from_left = from_right = own
        for step in range(1, (n - 1) // 2 + 1):
            from_left = lax.ppermute(from_left, "tensor", right)
            from_right = lax.ppermute(from_right, "tensor", left)
            total = total + product(from_left, here - step)
            total = total + product(from_right, here + step)
        if n % 2 == 0:
            half = width // 2
            one = lax.ppermute(from_left[:, :half], "tensor", right)
            two = lax.ppermute(from_right[:, half:], "tensor", left)
            total = total + product(one, here - n // 2)
            total = total + product(two, here - n // 2, half)
        return total.astype(BF16).reshape(chats, span, -1)

    return local


def solution(mesh):
    return jax.shard_map(
        make_local(mesh.shape["tensor"]),
        mesh=mesh,
        in_specs=(
            P(("groups", "dp"), "seq", "tensor"),
            P(None, "tensor"),
            P("groups", "tensor", None),
            P("groups", None, "tensor"),
            P(("groups", "dp")),
        ),
        out_specs=P(("groups", "dp"), "seq", "tensor"),
        check_vma=False,
    )
```

time: 207 us -> 175 us (0.85)
  waiting for transfers between devices: 154 us -> 26.2 us
  blocking collectives: 0 us -> 90.4 us
  between operations: 13.4 us -> 4.14 us
  starting transfers between devices: 0.04 us -> 9.26 us
  matrix products: 36.3 us -> 40.6 us
    all_gather x1 -> x0, waiting for transfers between devices: 144 us -> none  [local(): lax.all_gather(inputs, 'tensor', axis=2, tiled=True)]
    all_gather x0 -> x1, blocking collectives: none -> 90.4 us  [low_rank(): every = lax.all_gather(partial.reshape(-1, 2 * rank), 'tensor')]
    ppermute x0 -> x4, waiting for transfers between devices: none -> 26.2 us  [the longest x1 26.2 us: local(): one = lax.ppermute(from_left[:, :half], 'tensor', right)]
    psum x1 -> x0, waiting for transfers between devices: 9.77 us -> none  [local(): shrink_total = lax.psum(partial_shrink.astype(jnp.bfloat16), 'tensor')]
    ppermute x0 -> x4, starting transfers between devices: none -> 9.26 us  [the longest x1 5.05 us: local(): from_right = lax.ppermute(from_right, 'tensor', left)]
    dot_general x5 -> x9, matrix products: 36.3 us -> 40.6 us  [the longest x5 36.2 us: product(): return jnp.dot(block, rows, preferred_element_type=F32)]
    slice x0 -> x4, local copies, waits for them, and re-layouts: none -> 2.77 us  [the longest x1 1.38 us: low_rank(): adapter_ids[c]]
    dot_general x1 -> x0, local copies, waits for them, and re-layouts: 2.28 us -> none  [local(): jnp.einsum('ca,adr->cdr', picker, shrink_table, preferred_element_type=jn...]
  transfers between devices with their start and end apart: 2 -> 4, of which waited for: 2 -> 1; matrix products, arithmetic and copies ran while one was open for 17% -> 20% of each run, Pallas kernels for 0% -> 0%
where the time goes in v1:
time: 175 us
  blocking collectives  90.4 us (52%)
  matrix products  40.6 us (23%)
  waiting for transfers between devices  26.2 us (15%)
  starting transfers between devices  9.26 us (5%)
  between operations  4.14 us (2%)
  local copies, waits for them, and re-layouts  3.93 us (2%)
    all_gather x1, blocking collectives, low_rank(): every = lax.all_gather(partial.reshape(-1, 2 * rank), 'tensor')  90.4 us
    dot_general x5, matrix products, product(): return jnp.dot(block, rows, preferred_element_type=F32)  36.2 us
    ppermute x1, waiting for transfers between devices, local(): one = lax.ppermute(from_left[:, :half], 'tensor', right)  26.2 us
    ppermute x1, starting transfers between devices, local(): from_right = lax.ppermute(from_right, 'tensor', left)  5.05 us
    ppermute x1, starting transfers between devices, local(): two = lax.ppermute(from_right[:, half:], 'tensor', left)  4.15 us
    dot_general x2, matrix products, low_rank(): jnp.dot(inputs[c], shrink_table[adapter_ids[c]], preferred_element_type=F32)  3.52 us
  transfers between devices with their start and end apart: 4, of which 1 were waited for; matrix products, arithmetic and copies ran while one was open for 20% of the time, Pallas kernels for 0%

profile of v1, /device:TPU:0, one launch (start us, length us, event | category | flops | bytes accessed | tf_op | source)
XLA Modules:
  0.0 174.6 jit_solution(16970052094193638066)
XLA Ops:
  0.0 5.0 %collective-permute-start.1 = (bf16[512,2048]{1,0:T(8,128)(2,1)}, bf16[512,2048]{1,0:T(8,128)(2,1)S(1)}, u32[]{:S(2)}, u32[]{:S(2)}) collective-permute-start(bf16[512,2048]{1,0:T(8,128)(2,1)} %bitcast.43), channel_id=1, source_target_pairs={{0,12},{4,0},{8,4},{12,8},{1,13},{5,1},{9,5},{13,9},{2,14},{6,2},{... | collective-permute-start | bytes 6291464 | tf_op jit(solution)/shard_map/ppermute | solution.py:47
  5.1 0.0 collective-permute-start
  5.1 1.4 fusion.43
  10.4 1.8 %fusion.17 = bf16[256,64]{0,1:T(8,128)(2,1)S(1)} fusion(bf16[2,256,2048]{2,1,0:T(8,128)(2,1)} %param.5, bf16[4,2048,64]{1,2,0:T(8,128)(2,1)} %param.7, s32[]{:T(128)S(6)} %select_n.23), kind=kOutput, calls=%fused_computation.18 | convolution fusion | flops 67125248 | bytes 1343492 | tf_op jit(solution)/shard_map/dot_general | solution.py:14
  12.2 1.8 %fusion.18 = bf16[256,64]{0,1:T(8,128)(2,1)S(1)} fusion(bf16[2,256,2048]{2,1,0:T(8,128)(2,1)} %param.5, bf16[4,2048,64]{1,2,0:T(8,128)(2,1)} %param.7, s32[]{:T(128)S(6)} %select_n.24), kind=kOutput, calls=%fused_computation.19 | convolution fusion | flops 67125248 | bytes 1343492 | tf_op jit(solution)/shard_map/dot_general | solution.py:14
  14.0 0.1 copy.7
  14.1 0.1 all_gather_reshape.3
  14.2 90.4 %all_gather.3 = bf16[4,256,128]{2,1,0:T(8,128)(2,1)S(1)} all-gather(bf16[1,256,128]{2,1,0:T(8,128)(2,1)S(1)} %all_gather_reshape.3), channel_id=1, replica_groups=mesh['groups'=2,'tensor'=4,'seq'=2,'dp'=2] {'tensor'}, dimensions={0}, use_global_device_ids=true | all-gather | bytes 327680 | tf_op jit(solution)/shard_map/all_gather | solution.py:18
  104.7 0.1 squeeze.38
  104.7 0.1 squeeze.40
  104.9 0.0 copy-start.2
  104.9 0.4 fusion.23
  105.3 0.4 fusion.25
  105.7 0.7 copy-done.2
  106.5 7.0 %fusion.4 = f32[2048,512]{0,1:T(8,128)S(1)} fusion(bf16[512,2048]{1,0:T(8,128)(2,1)S(1)} %bitcast.45, bf16[8192,2048]{1,0:T(8,128)(2,1)} %param.6, s32[]{:T(128)S(6)} %select_n.25), kind=kOutput, calls=%fused_computation.4 | convolution fusion | flops 4294967296 | bytes 14680068 | tf_op jit(solution)/shard_map/dot_general | solution.py:41
  113.4 0.1 slice.39
  113.5 4.1 %collective-permute-start.3 = (bf16[512,1024]{1,0:T(8,128)(2,1)S(1)}, bf16[512,1024]{1,0:T(8,128)(2,1)}, u32[]{:S(2)}, u32[]{:S(2)}) collective-permute-start(bf16[512,1024]{1,0:T(8,128)(2,1)S(1)} %slice.39), channel_id=1, source_target_pairs={{0,12},{4,0},{8,4},{12,8},{1,13},{5,1},{9,5},{13,9},{2,14},{6,2},{... | collective-permute-start | bytes 3145736 | tf_op jit(solution)/shard_map/ppermute | solution.py:53
  117.7 1.3 slice.38
  119.0 0.1 collective-permute-start.2
  119.1 6.9 %fusion = f32[2048,512]{0,1:T(8,128)S(1)} fusion(bf16[512,2048]{1,0:T(8,128)(2,1)S(1)} %collective-permute-done.1, bf16[8192,2048]{1,0:T(8,128)(2,1)} %param.6, s32[]{:T(128)S(6)} %select_n.27), kind=kOutput, calls=%fused_computation | convolution fusion | flops 4294967296 | bytes 14680068 | tf_op jit(solution)/shard_map/dot_general | solution.py:41
  126.0 7.6 %fusion.2 = f32[2048,512]{0,1:T(8,128)S(1)} fusion(bf16[512,2048]{1,0:T(8,128)(2,1)} %collective-permute-done, bf16[8192,2048]{1,0:T(8,128)(2,1)} %param.6, s32[]{:T(128)S(6)} %select_n.26), kind=kOutput, calls=%fused_computation.2 | convolution fusion | flops 4294967296 | bytes 14680068 | tf_op jit(solution)/shard_map/dot_general | solution.py:41
  133.6 26.2 %collective-permute-done.2 = bf16[512,1024]{1,0:T(8,128)(2,1)S(1)} collective-permute-done((bf16[512,1024]{1,0:T(8,128)(2,1)S(1)}, bf16[512,1024]{1,0:T(8,128)(2,1)S(1)}, u32[]{:S(2)}, u32[]{:S(2)}) %collective-permute-start.2) | collective-permute-done | bytes 1048608 | tf_op jit(solution)/shard_map/ppermute | solution.py:52
  159.8 6.5 %fusion.13 = f32[2048,512]{0,1:T(8,128)} fusion(bf16[512,1024]{1,0:T(8,128)(2,1)S(1)} %collective-permute-done.2, bf16[8192,2048]{1,0:T(8,128)(2,1)} %param.6, s32[]{:T(128)S(6)} %select_n.28), kind=kOutput, calls=%fused_computation.14 | convolution fusion | flops 2147483648 | bytes 9437188 | tf_op jit(solution)/shard_map/dot_general | solution.py:41
  166.2 8.3 %fusion.10 = bf16[512,2048]{1,0:T(8,128)(2,1)} fusion(f32[256,2048]{1,0:T(8,128)S(1)} %fusion.23, f32[256,2048]{1,0:T(8,128)S(1)} %fusion.25, f32[2048,512]{0,1:T(8,128)} %fusion.13, f32[2048,512]{0,1:T(8,128)S(1)} %fusion, f32[2048,512]{0,1:T(8,128)S(1)} %fusion.2, f32[2048,512]{0,1:T(8,128)S(1)} %fusion.4, bf16[512,1024]{1,0:T(8,128)(2,1)} %collective-permute-done.3, ...), kind=kOutput, calls=%fused_computation.11 | convolution fusion | flops 2154823680 | bytes 28311556 | tf_op jit(solution)/shard_map/dot_general | solution.py:41
  (10 shorter events, 0.1 us)
Async XLA Ops:
  0.0 104.9 %copy-start = (bf16[4,64,2048]{2,1,0:T(8,128)(2,1)S(1)}, bf16[4,64,2048]{2,1,0:T(8,128)(2,1)}, u32[]{:S(2)}) copy-start(bf16[4,64,2048]{2,1,0:T(8,128)(2,1)} %param.8) | copy-start | bytes 3145732
  0.0 113.4 %collective-permute-start.1 = (bf16[512,2048]{1,0:T(8,128)(2,1)}, bf16[512,2048]{1,0:T(8,128)(2,1)S(1)}, u32[]{:S(2)}, u32[]{:S(2)}) collective-permute-start(bf16[512,2048]{1,0:T(8,128)(2,1)} %bitcast.43), channel_id=1, source_target_pairs={{0,12},{4,0},{8,4},{12,8},{1,13},{5,1},{9,5},{13,9},{2,14},{6,2},{... | collective-permute-start | bytes 6291464 | tf_op jit(solution)/shard_map/ppermute | solution.py:47
  5.1 112.6 %collective-permute-start = (bf16[512,2048]{1,0:T(8,128)(2,1)}, bf16[512,2048]{1,0:T(8,128)(2,1)}, u32[]{:S(2)}, u32[]{:S(2)}) collective-permute-start(bf16[512,2048]{1,0:T(8,128)(2,1)} %bitcast.44), channel_id=1, source_target_pairs={{0,4},{4,8},{8,12},{12,0},{1,5},{5,9},{9,13},{13,1},{2,6},{6,10},{... | collective-permute-start | bytes 6291464 | tf_op jit(solution)/shard_map/ppermute | solution.py:46
  104.9 1.6 copy-start.2
  113.5 52.7 %collective-permute-start.3 = (bf16[512,1024]{1,0:T(8,128)(2,1)S(1)}, bf16[512,1024]{1,0:T(8,128)(2,1)}, u32[]{:S(2)}, u32[]{:S(2)}) collective-permute-start(bf16[512,1024]{1,0:T(8,128)(2,1)S(1)} %slice.39), channel_id=1, source_target_pairs={{0,12},{4,0},{8,4},{12,8},{1,13},{5,1},{9,5},{13,9},{2,14},{6,2},{... | collective-permute-start | bytes 3145736 | tf_op jit(solution)/shard_map/ppermute | solution.py:53
  119.0 40.8 %collective-permute-start.2 = (bf16[512,1024]{1,0:T(8,128)(2,1)S(1)}, bf16[512,1024]{1,0:T(8,128)(2,1)S(1)}, u32[]{:S(2)}, u32[]{:S(2)}) collective-permute-start(bf16[512,1024]{1,0:T(8,128)(2,1)S(1)} %slice.38), channel_id=1, source_target_pairs={{0,4},{4,8},{8,12},{12,0},{1,5},{5,9},{9,13},{13,1},{2,6},{6,10},{... | collective-permute-start | bytes 3145736 | tf_op jit(solution)/shard_map/ppermute | solution.py:52
  166.2 8.3 %copy-start.1 = (bf16[4,64,2048]{2,1,0:T(8,128)(2,1)S(1)}, bf16[4,64,2048]{2,1,0:T(8,128)(2,1)}, u32[]{:S(2)}) copy-start(bf16[4,64,2048]{2,1,0:T(8,128)(2,1)} %param.8) | copy-start | bytes 3145732

commit v2 on v1

v2 whole, which is shorter than its diff:
```python
import jax
import jax.numpy as jnp
from jax import lax
from jax.sharding import PartitionSpec as P

F32, BF16 = jnp.float32, jnp.bfloat16
PLANE = ("groups", "seq", "dp")


def shrink(inputs, shrink_table, adapter_ids):
    return jnp.concatenate(
        [
            jnp.dot(inputs[c], shrink_table[adapter_ids[c]], preferred_element_type=F32).astype(BF16)
            for c in range(inputs.shape[0])
        ]
    )


def expand(shrunk, expand_table, adapter_ids):
    chats = adapter_ids.shape[0]
    parts = shrunk.reshape(chats, -1, shrunk.shape[-1])
    return [
        jnp.dot(parts[c], expand_table[adapter_ids[c]], preferred_element_type=F32)
        for c in range(chats)
    ]


def ring(n):
    right = [(i, (i + 1) % n) for i in range(n)]
    left = [(i, (i - 1) % n) for i in range(n)]

    def local(inputs, base_weight, shrink_table, expand_table, adapter_ids):
        chats, span, width = inputs.shape
        here = lax.axis_index("tensor")
        own = inputs.reshape(chats * span, width)

        def product(block, owner, first=0):
            rows = lax.dynamic_slice_in_dim(
                base_weight, lax.rem(owner + 2 * n, n) * width + first, block.shape[1], axis=0
            )
            return jnp.dot(block, rows, preferred_element_type=F32)

        shrunk = lax.psum(shrink(inputs, shrink_table, adapter_ids), "tensor")
        total = product(own, here)
        from_left = from_right = own
        for step in range(1, (n - 1) // 2 + 1):
            from_left = lax.ppermute(from_left, "tensor", right)
            from_right = lax.ppermute(from_right, "tensor", left)
            total = total + product(from_left, here - step)
            total = total + product(from_right, here + step)
        if n > 1 and n % 2 == 0:
            half = width // 2
            one = lax.ppermute(from_left[:, :half], "tensor", right)
            two = lax.ppermute(from_right[:, half:], "tensor", left)
            total = total + product(one, here - n // 2)
            total = total + product(two, here - n // 2, half)
        total = total + jnp.concatenate(expand(shrunk, expand_table, adapter_ids))
        return total.astype(BF16).reshape(chats, span, -1)

    return local


INWARD = [(0, 1), (3, 2)]
OUTWARD = [(1, 0), (2, 3)]
ACROSS = [(1, 2), (2, 1)]
SWAP = INWARD + OUTWARD


def send(block, pairs):
    return lax.ppermute(block, "tensor", pairs)


def after(block, *earlier):
    return lax.optimization_barrier((block,) + earlier)[0]


def line(inputs, base_weight, shrink_table, expand_table, adapter_ids):
    chats, span, width = inputs.shape
    rows = chats * span
    here = lax.axis_index("tensor")
    is_end = (here == 0) | (here == 3)
    far_mid = jnp.where(here < 2, 2, 1)
    far_end = jnp.where(here < 2, 3, 0)
    own = inputs.reshape(rows, width)
    place = lax.axis_index(PLANE)
    plane = lax.axis_size(PLANE)

    chunk = rows // 4
    cuts = [slice(i * chunk, (i + 1) * chunk) for i in range(4)]

    def product(block, owner):
        part = lax.dynamic_slice_in_dim(base_weight, owner * width, width, axis=0)
        return jnp.dot(block, part, preferred_element_type=F32)

    pieces = 4
    share = 2 * width // (pieces * plane)
    lent, seen = [], []

    def inward(block):
        got = send(after(block, *seen[-2:-1]), INWARD)
        seen.append(got)
        return got

    for piece in range(pieces):
        owner = far_mid if piece < pieces // 2 else far_end
        first = owner * width + (piece % (pieces // 2)) * (2 * width // pieces) + place * share
        got = inward(lax.dynamic_slice_in_dim(base_weight, first, share, axis=0))
        lent.append(lax.all_gather(got, PLANE, tiled=True))

    mate_out = send(own, OUTWARD)
    across = send(own, ACROSS)
    mate_in = [inward(own[cut]) for cut in cuts]
    across_end = [send(block, ACROSS) for block in mate_in]
    half = 2 * chunk
    mid_out = send(across[:half], OUTWARD)
    end_out = [send(block, OUTWARD) for block in across_end[:2]]

    partial = shrink(inputs, shrink_table, adapter_ids)
    mate_partial = send(partial, SWAP)
    both = send(jnp.stack([partial, mate_partial]), ACROSS)
    shrunk = (
        partial.astype(F32) + mate_partial.astype(F32) + both[0].astype(F32) + both[1].astype(F32)
    ).astype(BF16)
    shrunk = jnp.where(is_end, send(shrunk, OUTWARD), shrunk)

    width2 = 2 * width // pieces

    def lent_product(block, which):
        return sum(
            jnp.dot(
                block[:, i * width2 : (i + 1) * width2],
                lent[which * (pieces // 2) + i],
                preferred_element_type=F32,
            )
            for i in range(pieces // 2)
        )

    made = lent_product(across[half:], 0)
    done = [
        send(
            (made[i * chunk : (i + 1) * chunk] + lent_product(across_end[2 + i], 1)).astype(BF16),
            OUTWARD,
        )
        for i in range(2)
    ]

    mate = jnp.concatenate(
        [jnp.where(is_end, mate_out[cut], got) for cut, got in zip(cuts, mate_in)]
    )
    total = product(own, here) + product(mate, here ^ 1)
    total = total + jnp.concatenate(expand(shrunk, expand_table, adapter_ids))
    first_mid = jnp.where(is_end, mid_out, across[:half])
    first_end = jnp.concatenate(
        [jnp.where(is_end, out, got) for out, got in zip(end_out, across_end[:2])]
    )
    top = total[:half] + product(first_mid, far_mid) + product(first_end, far_end)
    bottom = total[half:] + product(across[half:], far_mid)
    outs = [top.astype(BF16)]
    for i in range(2):
        part = bottom[i * chunk : (i + 1) * chunk] + product(across_end[2 + i], far_end)
        outs.append((part + done[i].astype(F32)).astype(BF16))
    return jnp.concatenate(outs).reshape(chats, span, -1)


def solution(mesh):
    n = mesh.shape["tensor"]
    return jax.shard_map(
        line if n == 4 else ring(n),
        mesh=mesh,
        in_specs=(
            P(("groups", "dp"), "seq", "tensor"),
            P(None, "tensor"),
            P("groups", "tensor", None),
            P("groups", None, "tensor"),
            P(("groups", "dp")),
        ),
        out_specs=P(("groups", "dp"), "seq", "tensor"),
        check_vma=False,
    )
```

time: 175 us -> 245 us (1.40)
  blocking collectives: 90.4 us -> 0 us
  starting transfers between devices: 9.26 us -> 75.5 us
  matrix products: 40.6 us -> 77.1 us
  waiting for transfers between devices: 26.2 us -> 59 us
  between operations: 4.14 us -> 17.4 us
  local copies, waits for them, and re-layouts: 3.93 us -> 10.6 us
  other arithmetic: 0.05 us -> 4.28 us
    all_gather x1 -> x0, blocking collectives: 90.4 us -> none  [low_rank(): every = lax.all_gather(partial.reshape(-1, 2 * rank), 'tensor')]
    ppermute x4 -> x22, starting transfers between devices: 9.26 us -> 75.4 us  [send(): return lax.ppermute(block, 'tensor', pairs)]
    dot_general x9 -> x17, matrix products: 40.6 us -> 77.1 us  [the longest x7 53.5 us: product(): return jnp.dot(block, part, preferred_element_type=F32)]
    ppermute x4 -> x22, waiting for transfers between devices: 26.2 us -> 58.9 us  [send(): return lax.ppermute(block, 'tensor', pairs)]
    dynamic_slice x0 -> x1, local copies, waits for them, and re-layouts: none -> 2.57 us  [line(): got = inward(lax.dynamic_slice_in_dim(base_weight, first, share, axis=0))]
    unnamed x6 -> x36, local copies, waits for them, and re-layouts: 0.76 us -> 3.23 us
  transfers between devices with their start and end apart: 4 -> 26, of which waited for: 1 -> 9; matrix products, arithmetic and copies ran while one was open for 20% -> 33% of each run, Pallas kernels for 0% -> 0%
where the time goes in v2:
time: 245 us; the launch traced here: 244 us
  matrix products  77.1 us (31%)
  starting transfers between devices  75.5 us (31%)
  waiting for transfers between devices  59 us (24%)
  between operations  17.4 us (7%)
  local copies, waits for them, and re-layouts  10.6 us (4%)
  other arithmetic  4.28 us (2%)
    ppermute x22, starting transfers between devices, send(): return lax.ppermute(block, 'tensor', pairs)  75.4 us
    ppermute x22, waiting for transfers between devices, send(): return lax.ppermute(block, 'tensor', pairs)  58.9 us
    dot_general x7, matrix products, product(): return jnp.dot(block, part, preferred_element_type=F32)  53.5 us
    dot_general x6, matrix products, lent_product(): jnp.dot(block[:, i * width2:(i + 1) * width2], lent[which * (pieces // 2)...  19.1 us
  transfers between devices with their start and end apart: 26, of which 9 were waited for; matrix products, arithmetic and copies ran while one was open for 33% of the time, Pallas kernels for 0%

profile of v2, /device:TPU:0, one launch (start us, length us, event | category | flops | bytes accessed | tf_op | source)
XLA Modules:
  0.0 244.0 jit_solution(14148773325243122956)
XLA Ops:
  9.1 4.9 %collective-permute-start.4 = (bf16[128,2048]{1,0:T(8,128)(2,1)S(1)}, bf16[128,2048]{1,0:T(8,128)(2,1)S(1)}, u32[]{:S(2)}, u32[]{:S(2)}) collective-permute-start(bf16[128,2048]{1,0:T(8,128)(2,1)S(1)} %get-tuple-element.18), channel_id=1, source_target_pairs={{0,4},{12,8},{1,5},{13,9},{2,6},{14,10},{3,7},{15,11},{16,20},{28,... | collective-permute-start | bytes 1572872 | tf_op jit(solution)/shard_map/ppermute | solution.py:70
  14.1 11.1 %collective-permute-done.4 = bf16[128,2048]{1,0:T(8,128)(2,1)S(1)} collective-permute-done((bf16[128,2048]{1,0:T(8,128)(2,1)S(1)}, bf16[128,2048]{1,0:T(8,128)(2,1)S(1)}, u32[]{:S(2)}, u32[]{:S(2)}) %collective-permute-start.4) | collective-permute-done | bytes 524320 | tf_op jit(solution)/shard_map/ppermute | solution.py:70
  26.1 4.4 %collective-permute-start.1 = (bf16[128,2048]{1,0:T(8,128)(2,1)S(1)}, bf16[128,2048]{1,0:T(8,128)(2,1)S(1)}, u32[]{:S(2)}, u32[]{:S(2)}) collective-permute-start(bf16[128,2048]{1,0:T(8,128)(2,1)S(1)} %get-tuple-element.17), channel_id=1, source_target_pairs={{0,4},{12,8},{1,5},{13,9},{2,6},{14,10},{3,7},{15,11},{16,20},{28,... | collective-permute-start | bytes 1572872 | tf_op jit(solution)/shard_map/ppermute | solution.py:70
  30.5 10.3 %collective-permute-done.1 = bf16[128,2048]{1,0:T(8,128)(2,1)S(1)} collective-permute-done((bf16[128,2048]{1,0:T(8,128)(2,1)S(1)}, bf16[128,2048]{1,0:T(8,128)(2,1)S(1)}, u32[]{:S(2)}, u32[]{:S(2)}) %collective-permute-start.1) | collective-permute-done | bytes 524320 | tf_op jit(solution)/shard_map/ppermute | solution.py:70
  41.7 4.4 %collective-permute-start.5 = (bf16[128,2048]{1,0:T(8,128)(2,1)S(1)}, bf16[128,2048]{1,0:T(8,128)(2,1)S(1)}, u32[]{:S(2)}, u32[]{:S(2)}) collective-permute-start(bf16[128,2048]{1,0:T(8,128)(2,1)S(1)} %get-tuple-element.13), channel_id=1, source_target_pairs={{0,4},{12,8},{1,5},{13,9},{2,6},{14,10},{3,7},{15,11},{16,20},{28,... | collective-permute-start | bytes 1572872 | tf_op jit(solution)/shard_map/ppermute | solution.py:70
  46.1 9.5 %collective-permute-done.5 = bf16[128,2048]{1,0:T(8,128)(2,1)S(1)} collective-permute-done((bf16[128,2048]{1,0:T(8,128)(2,1)S(1)}, bf16[128,2048]{1,0:T(8,128)(2,1)S(1)}, u32[]{:S(2)}, u32[]{:S(2)}) %collective-permute-start.5) | collective-permute-done | bytes 524320 | tf_op jit(solution)/shard_map/ppermute | solution.py:70
  64.7 6.6 %collective-permute-start.2 = (bf16[128,2048]{1,0:T(8,128)(2,1)}, bf16[128,2048]{1,0:T(8,128)(2,1)}, u32[]{:S(2)}, u32[]{:S(2)}) collective-permute-start(bf16[128,2048]{1,0:T(8,128)(2,1)} %get-tuple-element.11), channel_id=1, source_target_pairs={{0,4},{12,8},{1,5},{13,9},{2,6},{14,10},{3,7},{15,11},{16,20},{28,... | collective-permute-start | bytes 1572872 | tf_op jit(solution)/shard_map/ppermute | solution.py:70
  74.5 6.0 %collective-permute-done.9 = bf16[512,64]{0,1:T(8,128)(2,1)S(1)} collective-permute-done((bf16[512,64]{0,1:T(8,128)(2,1)S(1)}, bf16[512,64]{0,1:T(8,128)(2,1)S(1)}, u32[]{:S(2)}, u32[]{:S(2)}) %collective-permute-start.9) | collective-permute-done | bytes 65568 | tf_op jit(solution)/shard_map/ppermute | solution.py:70
  86.3 27.3 %collective-permute-start.3 = (bf16[128,2048]{1,0:T(8,128)(2,1)}, bf16[128,2048]{1,0:T(8,128)(2,1)}, u32[]{:S(2)}, u32[]{:S(2)}) collective-permute-start(bf16[128,2048]{1,0:T(8,128)(2,1)} %get-tuple-element.12), channel_id=1, source_target_pairs={{0,4},{12,8},{1,5},{13,9},{2,6},{14,10},{3,7},{15,11},{16,20},{28,... | collective-permute-start | bytes 1572872 | tf_op jit(solution)/shard_map/ppermute | solution.py:70
  115.7 10.5 %fusion.2 = f32[2048,512]{0,1:T(8,128)} fusion(bf16[512,2048]{1,0:T(8,128)(2,1)} %bitcast, bf16[8192,2048]{1,0:T(8,128)(2,1)} %param.6, s32[]{:T(128)S(6)} %select_n.86), kind=kOutput, calls=%fused_computation.2 | convolution fusion | flops 4294967296 | bytes 14680068 | tf_op jit(solution)/shard_map/dot_general | solution.py:93
  126.2 4.4 %collective-permute-start.7 = (bf16[128,2048]{1,0:T(8,128)(2,1)}, bf16[128,2048]{1,0:T(8,128)(2,1)}, u32[]{:S(2)}, u32[]{:S(2)}) collective-permute-start(bf16[128,2048]{1,0:T(8,128)(2,1)} %get-tuple-element.15), channel_id=1, source_target_pairs={{0,4},{12,8},{1,5},{13,9},{2,6},{14,10},{3,7},{15,11},{16,20},{28,... | collective-permute-start | bytes 1572872 | tf_op jit(solution)/shard_map/ppermute | solution.py:70
  130.6 6.0 %collective-permute-done.6 = bf16[128,2048]{1,0:T(8,128)(2,1)} collective-permute-done((bf16[128,2048]{1,0:T(8,128)(2,1)}, bf16[128,2048]{1,0:T(8,128)(2,1)}, u32[]{:S(2)}, u32[]{:S(2)}) %collective-permute-start.6) | collective-permute-done | bytes 524320 | tf_op jit(solution)/shard_map/ppermute | solution.py:70
  136.7 5.2 %collective-permute-start.8 = (bf16[128,2048]{1,0:T(8,128)(2,1)}, bf16[128,2048]{1,0:T(8,128)(2,1)}, u32[]{:S(2)}, u32[]{:S(2)}) collective-permute-start(bf16[128,2048]{1,0:T(8,128)(2,1)} %get-tuple-element.16), channel_id=1, source_target_pairs={{0,4},{12,8},{1,5},{13,9},{2,6},{14,10},{3,7},{15,11},{16,20},{28,... | collective-permute-start | bytes 1572872 | tf_op jit(solution)/shard_map/ppermute | solution.py:70
  157.1 10.9 %maximum_add_fusion = f32[512,2048]{1,0:T(8,128)S(1)} fusion(f32[256,2048]{1,0:T(8,128)S(1)} %fusion.80, f32[256,2048]{1,0:T(8,128)S(1)} %fusion.82, f32[2048,512]{0,1:T(8,128)} %fusion.2, bf16[8192,2048]{1,0:T(8,128)(2,1)} %param.6, s32[]{:T(128)S(6)} %select_n.98, bf16[128,2048]{1,0:T(8,128)(2,1)S(1)} %get-tuple-element.22, ...), kind=kOutput, calls=%fused_computation.14 | convolution fusion | flops 4306501632 | bytes 23068676 | tf_op jit(solution)/shard_map/dot_general | solution.py:93
  168.0 9.0 %slice_add_fusion = f32[256,2048]{1,0:T(8,128)} fusion(f32[512,2048]{1,0:T(8,128)S(1)} %maximum_add_fusion, bf16[8192,2048]{1,0:T(8,128)(2,1)} %param.6, s32[]{:T(128)S(6)} %select_n.105, bf16[512,2048]{1,0:T(8,128)(2,1)} %collective-permute-done.12), kind=kOutput, calls=%fused_computation.33 | convolution fusion | flops 2148007936 | bytes 13631492 | tf_op jit(solution)/shard_map/dot_general | solution.py:93
  177.0 5.9 %collective-permute-done.15 = bf16[128,2048]{1,0:T(8,128)(2,1)S(1)} collective-permute-done((bf16[128,2048]{1,0:T(8,128)(2,1)S(1)}, bf16[128,2048]{1,0:T(8,128)(2,1)S(1)}, u32[]{:S(2)}, u32[]{:S(2)}) %collective-permute-start.15) | collective-permute-done | bytes 524320 | tf_op jit(solution)/shard_map/ppermute | solution.py:70
  183.8 4.8 %collective-permute-done.17 = bf16[128,2048]{1,0:T(8,128)(2,1)S(1)} collective-permute-done((bf16[128,2048]{1,0:T(8,128)(2,1)S(1)}, bf16[128,2048]{1,0:T(8,128)(2,1)S(1)}, u32[]{:S(2)}, u32[]{:S(2)}) %collective-permute-start.17) | collective-permute-done | bytes 524320 | tf_op jit(solution)/shard_map/ppermute | solution.py:70
  189.4 7.5 %fusion.6 = f32[256,2048]{1,0:T(8,128)} fusion(bf16[8192,2048]{1,0:T(8,128)(2,1)} %param.6, s32[]{:T(128)S(6)} %select_n.105, bf16[256,2048]{1,0:T(8,128)(2,1)S(1)} %collective-permute-done.13, pred[]{:T(512)S(6)} %or.3, bf16[512,2048]{1,0:T(8,128)(2,1)} %collective-permute-done.12), kind=kOutput, calls=%fused_computation.6 | convolution fusion | flops 2148007936 | bytes 12582917 | tf_op jit(solution)/shard_map/dot_general | solution.py:93
  196.9 4.9 %fusion.71 = f32[2048,256]{0,1:T(8,128)} fusion(bf16[1024,2048]{1,0:T(8,128)(2,1)} %all-gather.7.cloned.1.call-done, bf16[512,2048]{1,0:T(8,128)(2,1)} %collective-permute-done.12), kind=kOutput, calls=%fused_computation.57 | convolution fusion | flops 1073741824 | bytes 6815744 | tf_op jit(solution)/shard_map/dot_general | solution.py:130
  201.8 4.3 %fusion.22 = f32[256,2048]{1,0:T(8,128)S(1)} fusion(f32[2048,256]{0,1:T(8,128)} %fusion.71, bf16[1024,2048]{1,0:T(8,128)(2,1)} %all-gather.5.cloned.1.call-done, bf16[512,2048]{1,0:T(8,128)(2,1)} %collective-permute-done.12), kind=kOutput, calls=%fused_computation.19 | convolution fusion | flops 1074266112 | bytes 8912896 | tf_op jit(solution)/shard_map/dot_general | solution.py:130
  210.0 3.2 %fusion.46 = bf16[128,2048]{1,0:T(8,128)(2,1)S(1)} fusion(f32[128,2048]{1,0:T(8,128)S(1)} %fusion.77, bf16[1024,2048]{1,0:T(8,128)(2,1)} %all-gather.9.cloned.1.call-done, f32[256,2048]{1,0:T(8,128)S(1)} %fusion.22, bf16[128,2048]{1,0:T(8,128)(2,1)} %copy-done.4), kind=kOutput, calls=%fused_computation.31 | convolution fusion | flops 537657344 | bytes 7077888 | tf_op jit(solution)/shard_map/dot_general | solution.py:130
  220.3 5.9 %fusion.23 = bf16[256,2048]{1,0:T(8,128)(2,1)S(1)} fusion(bf16[8192,2048]{1,0:T(8,128)(2,1)} %param.6, s32[]{:T(128)S(6)} %select_n.108, f32[256,2048]{1,0:T(8,128)S(1)} %copy-done.17, f32[512,2048]{1,0:T(8,128)S(1)} %copy-done.16, bf16[128,2048]{1,0:T(8,128)(2,1)S(1)} %copy-done.11, bf16[128,2048]{1,0:T(8,128)(2,1)S(1)} %copy-done.10), kind=kOutput, calls=%fused_computation.20 | convolution fusion | flops 2151153664 | bytes 14680068 | tf_op jit(solution)/shard_map/dot_general | solution.py:93
  226.2 4.8 %fusion.40 = bf16[128,2048]{1,0:T(8,128)(2,1)S(1)} fusion(bf16[128,2048]{1,0:T(8,128)(2,1)S(1)} %copy-done.5, bf16[8192,2048]{1,0:T(8,128)(2,1)} %param.6, s32[]{:T(128)S(6)} %select_n.108, f32[256,2048]{1,0:T(8,128)S(1)} %copy-done.6, bf16[128,2048]{1,0:T(8,128)(2,1)S(1)} %collective-permute-done.19), kind=kOutput, calls=%fused_computation.29 | convolution fusion | flops 1074790400 | bytes 11010052 | tf_op jit(solution)/shard_map/dot_general | solution.py:93
  230.9 5.0 %fusion.43 = bf16[128,2048]{1,0:T(8,128)(2,1)S(1)} fusion(bf16[128,2048]{1,0:T(8,128)(2,1)} %collective-permute-done.20, bf16[8192,2048]{1,0:T(8,128)(2,1)} %param.6, s32[]{:T(128)S(6)} %select_n.108, f32[256,2048]{1,0:T(8,128)S(1)} %copy-done.6, bf16[128,2048]{1,0:T(8,128)(2,1)S(1)} %collective-permute-done.21), kind=kOutput, calls=%fused_computation.30 | convolution fusion | flops 1074790400 | bytes 11010052 | tf_op jit(solution)/shard_map/dot_general | solution.py:93
  (97 shorter events, 49.7 us)
Async XLA Ops:
  6.5 190.3 %all-gather.7.cloned.1.call-start = ((), (), s32[]{:S(2)}) async-start(), calls=%async_computation.1 | async-start | bytes 4718592 | tf_op jit(solution)/shard_map/all_gather | solution.py:108
  9.1 16.1 %collective-permute-start.4 = (bf16[128,2048]{1,0:T(8,128)(2,1)S(1)}, bf16[128,2048]{1,0:T(8,128)(2,1)S(1)}, u32[]{:S(2)}, u32[]{:S(2)}) collective-permute-start(bf16[128,2048]{1,0:T(8,128)(2,1)S(1)} %get-tuple-element.18), channel_id=1, source_target_pairs={{0,4},{12,8},{1,5},{13,9},{2,6},{14,10},{3,7},{15,11},{16,20},{28,... | collective-permute-start | bytes 1572872 | tf_op jit(solution)/shard_map/ppermute | solution.py:70
  26.0 175.8 %all-gather.5.cloned.1.call-start = ((), (), s32[]{:S(2)}) async-start(), calls=%async_computation | async-start | bytes 4718592 | tf_op jit(solution)/shard_map/all_gather | solution.py:108
  26.1 14.7 %collective-permute-start.1 = (bf16[128,2048]{1,0:T(8,128)(2,1)S(1)}, bf16[128,2048]{1,0:T(8,128)(2,1)S(1)}, u32[]{:S(2)}, u32[]{:S(2)}) collective-permute-start(bf16[128,2048]{1,0:T(8,128)(2,1)S(1)} %get-tuple-element.17), channel_id=1, source_target_pairs={{0,4},{12,8},{1,5},{13,9},{2,6},{14,10},{3,7},{15,11},{16,20},{28,... | collective-permute-start | bytes 1572872 | tf_op jit(solution)/shard_map/ppermute | solution.py:70
  41.6 165.3 %all-gather.11.cloned.1.call-start = ((), (), s32[]{:S(2)}) async-start(), calls=%async_computation.3 | async-start | bytes 4718592 | tf_op jit(solution)/shard_map/all_gather | solution.py:108
  41.7 13.9 %collective-permute-start.5 = (bf16[128,2048]{1,0:T(8,128)(2,1)S(1)}, bf16[128,2048]{1,0:T(8,128)(2,1)S(1)}, u32[]{:S(2)}, u32[]{:S(2)}) collective-permute-start(bf16[128,2048]{1,0:T(8,128)(2,1)S(1)} %get-tuple-element.13), channel_id=1, source_target_pairs={{0,4},{12,8},{1,5},{13,9},{2,6},{14,10},{3,7},{15,11},{16,20},{28,... | collective-permute-start | bytes 1572872 | tf_op jit(solution)/shard_map/ppermute | solution.py:70
  56.4 153.6 %all-gather.9.cloned.1.call-start = ((), (), s32[]{:S(2)}) async-start(), calls=%async_computation.2 | async-start | bytes 4718592 | tf_op jit(solution)/shard_map/all_gather | solution.py:108
  56.4 86.1 %collective-permute-start.12 = (bf16[512,2048]{1,0:T(8,128)(2,1)}, bf16[512,2048]{1,0:T(8,128)(2,1)}, u32[]{:S(2)}, u32[]{:S(2)}) collective-permute-start(bf16[512,2048]{1,0:T(8,128)(2,1)} %bitcast), channel_id=1, source_target_pairs={{4,8},{8,4},{5,9},{9,5},{6,10},{10,6},{7,11},{11,7},{20,24},{24,20... | collective-permute-start | bytes 6291464 | tf_op jit(solution)/shard_map/ppermute | solution.py:70
  64.7 16.6 %collective-permute-start.2 = (bf16[128,2048]{1,0:T(8,128)(2,1)}, bf16[128,2048]{1,0:T(8,128)(2,1)}, u32[]{:S(2)}, u32[]{:S(2)}) collective-permute-start(bf16[128,2048]{1,0:T(8,128)(2,1)} %get-tuple-element.11), channel_id=1, source_target_pairs={{0,4},{12,8},{1,5},{13,9},{2,6},{14,10},{3,7},{15,11},{16,20},{28,... | collective-permute-start | bytes 1572872 | tf_op jit(solution)/shard_map/ppermute | solution.py:70
  73.1 7.4 %collective-permute-start.9 = (bf16[512,64]{0,1:T(8,128)(2,1)S(1)}, bf16[512,64]{0,1:T(8,128)(2,1)S(1)}, u32[]{:S(2)}, u32[]{:S(2)}) collective-permute-start(bf16[512,64]{0,1:T(8,128)(2,1)S(1)} %get-tuple-element.30), channel_id=1, source_target_pairs={{0,4},{12,8},{4,0},{8,12},{1,5},{13,9},{5,1},{9,13},{2,6},{14,10},... | collective-permute-start | bytes 196616 | tf_op jit(solution)/shard_map/ppermute | solution.py:70
  73.2 82.1 %collective-permute-start = (bf16[512,2048]{1,0:T(8,128)(2,1)}, bf16[512,2048]{1,0:T(8,128)(2,1)S(1)}, u32[]{:S(2)}, u32[]{:S(2)}) collective-permute-start(bf16[512,2048]{1,0:T(8,128)(2,1)} %bitcast), channel_id=1, source_target_pairs={{4,0},{8,12},{5,1},{9,13},{6,2},{10,14},{7,3},{11,15},{20,16},{24,... | collective-permute-start | bytes 6291464 | tf_op jit(solution)/shard_map/ppermute | solution.py:70
  85.0 41.2 %collective-permute-start.11 = (bf16[512,64]{0,1:T(8,128)(2,1)S(1)}, bf16[512,64]{0,1:T(8,128)(2,1)S(1)}, u32[]{:S(2)}, u32[]{:S(2)}) collective-permute-start(bf16[512,64]{0,1:T(8,128)(2,1)S(1)} %fusion.90), channel_id=1, source_target_pairs={{4,0},{8,12},{5,1},{9,13},{6,2},{10,14},{7,3},{11,15},{20,16},{24,... | collective-permute-start | bytes 196616 | tf_op jit(solution)/shard_map/ppermute | solution.py:70
  86.3 39.9 %collective-permute-start.3 = (bf16[128,2048]{1,0:T(8,128)(2,1)}, bf16[128,2048]{1,0:T(8,128)(2,1)}, u32[]{:S(2)}, u32[]{:S(2)}) collective-permute-start(bf16[128,2048]{1,0:T(8,128)(2,1)} %get-tuple-element.12), channel_id=1, source_target_pairs={{0,4},{12,8},{1,5},{13,9},{2,6},{14,10},{3,7},{15,11},{16,20},{28,... | collective-permute-start | bytes 1572872 | tf_op jit(solution)/shard_map/ppermute | solution.py:70
  113.6 23.1 %collective-permute-start.6 = (bf16[128,2048]{1,0:T(8,128)(2,1)}, bf16[128,2048]{1,0:T(8,128)(2,1)}, u32[]{:S(2)}, u32[]{:S(2)}) collective-permute-start(bf16[128,2048]{1,0:T(8,128)(2,1)} %get-tuple-element.14), channel_id=1, source_target_pairs={{0,4},{12,8},{1,5},{13,9},{2,6},{14,10},{3,7},{15,11},{16,20},{28,... | collective-permute-start | bytes 1572872 | tf_op jit(solution)/shard_map/ppermute | solution.py:70
  126.2 21.7 %collective-permute-start.7 = (bf16[128,2048]{1,0:T(8,128)(2,1)}, bf16[128,2048]{1,0:T(8,128)(2,1)}, u32[]{:S(2)}, u32[]{:S(2)}) collective-permute-start(bf16[128,2048]{1,0:T(8,128)(2,1)} %get-tuple-element.15), channel_id=1, source_target_pairs={{0,4},{12,8},{1,5},{13,9},{2,6},{14,10},{3,7},{15,11},{16,20},{28,... | collective-permute-start | bytes 1572872 | tf_op jit(solution)/shard_map/ppermute | solution.py:70
  136.7 18.0 %collective-permute-start.8 = (bf16[128,2048]{1,0:T(8,128)(2,1)}, bf16[128,2048]{1,0:T(8,128)(2,1)}, u32[]{:S(2)}, u32[]{:S(2)}) collective-permute-start(bf16[128,2048]{1,0:T(8,128)(2,1)} %get-tuple-element.16), channel_id=1, source_target_pairs={{0,4},{12,8},{1,5},{13,9},{2,6},{14,10},{3,7},{15,11},{16,20},{28,... | collective-permute-start | bytes 1572872 | tf_op jit(solution)/shard_map/ppermute | solution.py:70
  142.5 8.0 %collective-permute-start.16 = (bf16[128,2048]{1,0:T(8,128)(2,1)}, bf16[128,2048]{1,0:T(8,128)(2,1)S(1)}, u32[]{:S(2)}, u32[]{:S(2)}) collective-permute-start(bf16[128,2048]{1,0:T(8,128)(2,1)} %collective-permute-done.6), channel_id=1, source_target_pairs={{4,8},{8,4},{5,9},{9,5},{6,10},{10,6},{7,11},{11,7},{20,24},{24,20... | collective-permute-start | bytes 1572872 | tf_op jit(solution)/shard_map/ppermute | solution.py:70
  147.9 41.5 %collective-permute-start.13 = (bf16[256,2048]{1,0:T(8,128)(2,1)S(1)}, bf16[256,2048]{1,0:T(8,128)(2,1)S(1)}, u32[]{:S(2)}, u32[]{:S(2)}) collective-permute-start(bf16[256,2048]{1,0:T(8,128)(2,1)S(1)} %slice.141), channel_id=1, source_target_pairs={{4,0},{8,12},{5,1},{9,13},{6,2},{10,14},{7,3},{11,15},{20,16},{24,... | collective-permute-start | bytes 3145736 | tf_op jit(solution)/shard_map/ppermute | solution.py:70
  149.2 33.7 %collective-permute-start.15 = (bf16[128,2048]{1,0:T(8,128)(2,1)S(1)}, bf16[128,2048]{1,0:T(8,128)(2,1)S(1)}, u32[]{:S(2)}, u32[]{:S(2)}) collective-permute-start(bf16[128,2048]{1,0:T(8,128)(2,1)S(1)} %collective-permute-done.14), channel_id=1, source_target_pairs={{4,0},{8,12},{5,1},{9,13},{6,2},{10,14},{7,3},{11,15},{20,16},{24,... | collective-permute-start | bytes 1572872 | tf_op jit(solution)/shard_map/ppermute | solution.py:70
  150.5 38.1 %collective-permute-start.17 = (bf16[128,2048]{1,0:T(8,128)(2,1)S(1)}, bf16[128,2048]{1,0:T(8,128)(2,1)S(1)}, u32[]{:S(2)}, u32[]{:S(2)}) collective-permute-start(bf16[128,2048]{1,0:T(8,128)(2,1)S(1)} %collective-permute-done.16), channel_id=1, source_target_pairs={{4,0},{8,12},{5,1},{9,13},{6,2},{10,14},{7,3},{11,15},{20,16},{24,... | collective-permute-start | bytes 1572872 | tf_op jit(solution)/shard_map/ppermute | solution.py:70
  154.6 51.5 %collective-permute-start.18 = (bf16[128,2048]{1,0:T(8,128)(2,1)}, bf16[128,2048]{1,0:T(8,128)(2,1)S(1)}, u32[]{:S(2)}, u32[]{:S(2)}) collective-permute-start(bf16[128,2048]{1,0:T(8,128)(2,1)} %collective-permute-done.7), channel_id=1, source_target_pairs={{4,8},{8,4},{5,9},{9,5},{6,10},{10,6},{7,11},{11,7},{20,24},{24,20... | collective-permute-start | bytes 1572872 | tf_op jit(solution)/shard_map/ppermute | solution.py:70
  155.3 59.4 %collective-permute-start.20 = (bf16[128,2048]{1,0:T(8,128)(2,1)}, bf16[128,2048]{1,0:T(8,128)(2,1)}, u32[]{:S(2)}, u32[]{:S(2)}) collective-permute-start(bf16[128,2048]{1,0:T(8,128)(2,1)} %collective-permute-done.8), channel_id=1, source_target_pairs={{4,8},{8,4},{5,9},{9,5},{6,10},{10,6},{7,11},{11,7},{20,24},{24,20... | collective-permute-start | bytes 1572872 | tf_op jit(solution)/shard_map/ppermute | solution.py:70
  213.1 13.0 %collective-permute-start.19 = (bf16[128,2048]{1,0:T(8,128)(2,1)S(1)}, bf16[128,2048]{1,0:T(8,128)(2,1)S(1)}, u32[]{:S(2)}, u32[]{:S(2)}) collective-permute-start(bf16[128,2048]{1,0:T(8,128)(2,1)S(1)} %fusion.46), channel_id=1, source_target_pairs={{4,0},{8,12},{5,1},{9,13},{6,2},{10,14},{7,3},{11,15},{20,16},{24,... | collective-permute-start | bytes 1572872 | tf_op jit(solution)/shard_map/ppermute | solution.py:70
  218.6 12.4 %collective-permute-start.21 = (bf16[128,2048]{1,0:T(8,128)(2,1)S(1)}, bf16[128,2048]{1,0:T(8,128)(2,1)S(1)}, u32[]{:S(2)}, u32[]{:S(2)}) collective-permute-start(bf16[128,2048]{1,0:T(8,128)(2,1)S(1)} %fusion.47), channel_id=1, source_target_pairs={{4,0},{8,12},{5,1},{9,13},{6,2},{10,14},{7,3},{11,15},{20,16},{24,... | collective-permute-start | bytes 1572872 | tf_op jit(solution)/shard_map/ppermute | solution.py:70
  (20 other events, 282.9 us)
Sparse Core Ops, SparseCore 0:
  26.1 37.8 all-gather.6
  65.9 36.7 all-gather.4
  104.6 36.7 all-gather.10
  143.1 36.7 all-gather.8

commit v3 on v1

v3 whole, which is shorter than its diff:
```python
import jax
import jax.numpy as jnp
from jax import lax
from jax.sharding import PartitionSpec as P

F32, BF16 = jnp.float32, jnp.bfloat16


def shrink(inputs, shrink_table, adapter_ids):
    return jnp.concatenate(
        [
            jnp.dot(inputs[c], shrink_table[adapter_ids[c]], preferred_element_type=F32).astype(BF16)
            for c in range(inputs.shape[0])
        ]
    )


def expand(shrunk, expand_table, adapter_ids):
    chats = adapter_ids.shape[0]
    parts = shrunk.reshape(chats, -1, shrunk.shape[-1])
    return [
        jnp.dot(parts[c], expand_table[adapter_ids[c]], preferred_element_type=F32)
        for c in range(chats)
    ]


def ring(n):
    right = [(i, (i + 1) % n) for i in range(n)]
    left = [(i, (i - 1) % n) for i in range(n)]

    def local(inputs, base_weight, shrink_table, expand_table, adapter_ids):
        chats, span, width = inputs.shape
        here = lax.axis_index("tensor")
        own = inputs.reshape(chats * span, width)

        def product(block, owner, first=0):
            rows = lax.dynamic_slice_in_dim(
                base_weight, lax.rem(owner + 2 * n, n) * width + first, block.shape[1], axis=0
            )
            return jnp.dot(block, rows, preferred_element_type=F32)

        shrunk = lax.psum(shrink(inputs, shrink_table, adapter_ids), "tensor")
        total = product(own, here)
        from_left = from_right = own
        for step in range(1, (n - 1) // 2 + 1):
            from_left = lax.ppermute(from_left, "tensor", right)
            from_right = lax.ppermute(from_right, "tensor", left)
            total = total + product(from_left, here - step)
            total = total + product(from_right, here + step)
        if n > 1 and n % 2 == 0:
            half = width // 2
            one = lax.ppermute(from_left[:, :half], "tensor", right)
            two = lax.ppermute(from_right[:, half:], "tensor", left)
            total = total + product(one, here - n // 2)
            total = total + product(two, here - n // 2, half)
        total = total + jnp.concatenate(expand(shrunk, expand_table, adapter_ids))
        return total.astype(BF16).reshape(chats, span, -1)

    return local


INWARD = [(0, 1), (3, 2)]
OUTWARD = [(1, 0), (2, 3)]
ACROSS = [(1, 2), (2, 1)]


def send(block, pairs):
    return lax.ppermute(block, "tensor", pairs)


def line(inputs, base_weight, shrink_table, expand_table, adapter_ids):
    chats, span, width = inputs.shape
    rows = chats * span
    here = lax.axis_index("tensor")
    is_end = (here == 0) | (here == 3)
    far_mid = jnp.where(here < 2, 2, 1)
    far_end = jnp.where(here < 2, 3, 0)
    own = inputs.reshape(rows, width)
    half, quarter = rows // 2, rows // 4

    def product(block, owner):
        part = lax.dynamic_slice_in_dim(base_weight, owner * width, width, axis=0)
        return jnp.dot(block, part, preferred_element_type=F32)

    across_own = [send(own[:half], ACROSS), send(own[half:], ACROSS)]
    mate_out = send(own, OUTWARD)
    mate_in = send(own, INWARD)
    across_mate = [send(mate_in[:half], ACROSS), send(mate_in[half:], ACROSS)]
    mid_out = [send(block, OUTWARD) for block in across_own]
    end_out = [
        send(block, OUTWARD)
        for block in (across_mate[0], across_mate[1][:quarter], across_mate[1][quarter:])
    ]

    shrunk = lax.psum(shrink(inputs, shrink_table, adapter_ids), "tensor")
    total = product(own, here) + jnp.concatenate(expand(shrunk, expand_table, adapter_ids))
    total = total + product(jnp.where(is_end, mate_out, mate_in), here ^ 1)
    outs = []
    for i, cut in enumerate((slice(0, half), slice(half, rows))):
        part = total[cut] + product(jnp.where(is_end, mid_out[i], across_own[i]), far_mid)
        if i == 0:
            outs.append(part + product(jnp.where(is_end, end_out[0], across_mate[0]), far_end))
        else:
            for j, sub in enumerate((slice(0, quarter), slice(quarter, half))):
                block = jnp.where(is_end, end_out[1 + j], across_mate[1][sub])
                outs.append(part[sub] + product(block, far_end))
    return jnp.concatenate([o.astype(BF16) for o in outs]).reshape(chats, span, -1)


def solution(mesh):
    n = mesh.shape["tensor"]
    return jax.shard_map(
        line if n == 4 else ring(n),
        mesh=mesh,
        in_specs=(
            P(("groups", "dp"), "seq", "tensor"),
            P(None, "tensor"),
            P("groups", "tensor", None),
            P("groups", None, "tensor"),
            P(("groups", "dp")),
        ),
        out_specs=P(("groups", "dp"), "seq", "tensor"),
        check_vma=False,
    )
```

time: 175 us -> 197 us (1.13)
  blocking collectives: 90.4 us -> 0 us
  waiting for transfers between devices: 26.2 us -> 103 us
  between operations: 4.14 us -> 17.6 us
  starting transfers between devices: 9.26 us -> 19.3 us
  matrix products: 40.6 us -> 50.1 us
  other arithmetic: 0.05 us -> 2.08 us
    all_gather x1 -> x0, blocking collectives: 90.4 us -> none  [low_rank(): every = lax.all_gather(partial.reshape(-1, 2 * rank), 'tensor')]
    ppermute x4 -> x11, waiting for transfers between devices: 26.2 us -> 78.9 us  [send(): return lax.ppermute(block, 'tensor', pairs)]
    psum x0 -> x1, waiting for transfers between devices: none -> 23.8 us  [line(): shrunk = lax.psum(shrink(inputs, shrink_table, adapter_ids), 'tensor')]
    ppermute x4 -> x11, starting transfers between devices: 9.26 us -> 19.3 us  [send(): return lax.ppermute(block, 'tensor', pairs)]
    dot_general x9 -> x11, matrix products: 40.6 us -> 50.1 us  [the longest x7 44 us: product(): return jnp.dot(block, part, preferred_element_type=F32)]
    concatenate x1 -> x2, other arithmetic: 0.01 us -> 2.08 us  [the longest x1 1.46 us: line(): jnp.concatenate([o.astype(BF16) for o in outs]).reshape(chats, span, -1)]
  transfers between devices with their start and end apart: 4 -> 12, of which waited for: 1 -> 5; matrix products, arithmetic and copies ran while one was open for 20% -> 25% of each run, Pallas kernels for 0% -> 0%
where the time goes in v3:
time: 197 us; the launch traced here: 196 us
  waiting for transfers between devices  103 us (52%)
  matrix products  50.1 us (25%)
  starting transfers between devices  19.3 us (10%)
  between operations  17.6 us (9%)
  local copies, waits for them, and re-layouts  4.61 us (2%)
  other arithmetic  2.08 us (1%)
    ppermute x11, waiting for transfers between devices, send(): return lax.ppermute(block, 'tensor', pairs)  78.9 us
    dot_general x7, matrix products, product(): return jnp.dot(block, part, preferred_element_type=F32)  44 us
    psum x1, waiting for transfers between devices, line(): shrunk = lax.psum(shrink(inputs, shrink_table, adapter_ids), 'tensor')  23.8 us
    ppermute x11, starting transfers between devices, send(): return lax.ppermute(block, 'tensor', pairs)  19.3 us
  transfers between devices with their start and end apart: 12, of which 5 were waited for; matrix products, arithmetic and copies ran while one was open for 25% of the time, Pallas kernels for 0%

profile of v3, /device:TPU:0, one launch (start us, length us, event | category | flops | bytes accessed | tf_op | source)
XLA Modules:
  0.0 196.4 jit_solution(33817321224861067)
XLA Ops:
  6.5 6.5 %collective-permute-start.1 = (bf16[512,2048]{1,0:T(8,128)(2,1)}, bf16[512,2048]{1,0:T(8,128)(2,1)}, u32[]{:S(2)}, u32[]{:S(2)}) collective-permute-start(bf16[512,2048]{1,0:T(8,128)(2,1)} %bitcast.29), channel_id=1, source_target_pairs={{0,4},{12,8},{1,5},{13,9},{2,6},{14,10},{3,7},{15,11},{16,20},{28,... | collective-permute-start | bytes 6291464 | tf_op jit(solution)/shard_map/ppermute | solution.py:68
  14.4 1.4 fusion.80
  19.1 1.8 fusion.31
  21.6 1.8 fusion.32
  24.0 1.4 slice_bitcast_fusion.1
  25.4 1.7 collective-permute-start.2
  27.2 1.6 collective-permute-start.6
  28.8 9.4 %fusion.2 = f32[2048,512]{0,1:T(8,128)} fusion(bf16[512,2048]{1,0:T(8,128)(2,1)S(1)} %bitcast.31, bf16[8192,2048]{1,0:T(8,128)(2,1)} %param.6, s32[]{:T(128)S(6)} %select_n.66), kind=kOutput, calls=%fused_computation.2 | convolution fusion | flops 4294967296 | bytes 14680068 | tf_op jit(solution)/shard_map/dot_general | solution.py:83
  38.2 23.8 %all-reduce.2.cloned.1.call-done = bf16[512,64]{0,1:T(8,128)(2,1)} async-done(((bf16[512,64]{0,1:T(8,128)(2,1)}), bf16[512,64]{0,1:T(8,128)(2,1)}) %all-reduce.2.cloned.1.call-update) | async-done | bytes 65552 | tf_op jit(solution)/shard_map/psum | solution.py:95
  61.9 1.4 fusion.55
  64.5 1.3 collective-permute-start.3
  67.1 1.7 fusion.78
  70.3 7.7 %fusion.14 = f32[512,2048]{1,0:T(8,128)S(1)} fusion(f32[256,2048]{1,0:T(8,128)S(1)} %fusion.53, f32[256,2048]{1,0:T(8,128)S(1)} %fusion.55, f32[2048,512]{0,1:T(8,128)S(1)} %copy-done.3, bf16[8192,2048]{1,0:T(8,128)(2,1)} %param.6, s32[]{:T(128)S(6)} %select_n.71, bf16[512,2048]{1,0:T(8,128)(2,1)} %collective-permute-done, ...), kind=kOutput, calls=%fused_computation.15 | convolution fusion | flops 4299161600 | bytes 25165828 | tf_op jit(solution)/shard_map/dot_general | solution.py:83
  80.7 1.5 collective-permute-start.5
  82.2 29.8 %collective-permute-done.7 = bf16[256,2048]{1,0:T(8,128)(2,1)S(1)} collective-permute-done((bf16[256,2048]{1,0:T(8,128)(2,1)}, bf16[256,2048]{1,0:T(8,128)(2,1)S(1)}, u32[]{:S(2)}, u32[]{:S(2)}) %collective-permute-start.7) | collective-permute-done | bytes 1048608 | tf_op jit(solution)/shard_map/ppermute | solution.py:68
  112.0 5.8 %fusion.20 = f32[256,2048]{1,0:T(8,128)S(1)} fusion(bf16[8192,2048]{1,0:T(8,128)(2,1)} %param.6, s32[]{:T(128)S(6)} %select_n.75, f32[512,2048]{1,0:T(8,128)S(1)} %fusion.14, bf16[256,2048]{1,0:T(8,128)(2,1)S(1)} %collective-permute-done.7, bf16[256,2048]{1,0:T(8,128)(2,1)} %collective-permute-done.6, pred[]{:T(512)S(6)} %or.3), kind=kOutput, calls=%fused_computation.17 | convolution fusion | flops 2148532224 | bytes 14680069 | tf_op jit(solution)/shard_map/dot_general | solution.py:83
  117.8 28.0 %collective-permute-done.9 = bf16[128,2048]{1,0:T(8,128)(2,1)S(1)} collective-permute-done((bf16[128,2048]{1,0:T(8,128)(2,1)S(1)}, bf16[128,2048]{1,0:T(8,128)(2,1)S(1)}, u32[]{:S(2)}, u32[]{:S(2)}) %collective-permute-start.9) | collective-permute-done | bytes 524320 | tf_op jit(solution)/shard_map/ppermute | solution.py:68
  145.7 4.7 %fusion.34 = bf16[128,2048]{1,0:T(8,128)(2,1)S(1)} fusion(f32[256,2048]{1,0:T(8,128)S(1)} %fusion.20, bf16[8192,2048]{1,0:T(8,128)(2,1)} %param.6, s32[]{:T(128)S(6)} %select_n.78, bf16[128,2048]{1,0:T(8,128)(2,1)S(1)} %collective-permute-done.9, pred[]{:T(512)S(6)} %or.3, bf16[256,2048]{1,0:T(8,128)(2,1)S(1)} %collective-permute-done.8), kind=kOutput, calls=%fused_computation.30 | convolution fusion | flops 1074528256 | bytes 11010053 | tf_op jit(solution)/shard_map/dot_general | solution.py:83
  150.5 6.5 %collective-permute-done.10 = bf16[128,2048]{1,0:T(8,128)(2,1)S(1)} collective-permute-done((bf16[128,2048]{1,0:T(8,128)(2,1)S(1)}, bf16[128,2048]{1,0:T(8,128)(2,1)S(1)}, u32[]{:S(2)}, u32[]{:S(2)}) %collective-permute-start.10) | collective-permute-done | bytes 524320 | tf_op jit(solution)/shard_map/ppermute | solution.py:68
  157.0 4.7 %fusion.33 = bf16[128,2048]{1,0:T(8,128)(2,1)S(1)} fusion(f32[256,2048]{1,0:T(8,128)S(1)} %fusion.20, bf16[8192,2048]{1,0:T(8,128)(2,1)} %param.6, s32[]{:T(128)S(6)} %select_n.78, bf16[128,2048]{1,0:T(8,128)(2,1)S(1)} %collective-permute-done.10, pred[]{:T(512)S(6)} %or.3, bf16[256,2048]{1,0:T(8,128)(2,1)S(1)} %collective-permute-done.8), kind=kOutput, calls=%fused_computation.28 | convolution fusion | flops 1074528256 | bytes 11010053 | tf_op jit(solution)/shard_map/dot_general | solution.py:83
  161.7 14.6 %collective-permute-done.5 = bf16[256,2048]{1,0:T(8,128)(2,1)S(1)} collective-permute-done((bf16[256,2048]{1,0:T(8,128)(2,1)S(1)}, bf16[256,2048]{1,0:T(8,128)(2,1)S(1)}, u32[]{:S(2)}, u32[]{:S(2)}) %collective-permute-start.5) | collective-permute-done | bytes 1048608 | tf_op jit(solution)/shard_map/ppermute | solution.py:68
  176.3 5.7 %fusion.12 = f32[256,2048]{1,0:T(8,128)S(1)} fusion(bf16[8192,2048]{1,0:T(8,128)(2,1)} %param.6, s32[]{:T(128)S(6)} %select_n.78, bf16[256,2048]{1,0:T(8,128)(2,1)S(1)} %collective-permute-done.5, bf16[256,2048]{1,0:T(8,128)(2,1)S(1)} %collective-permute-done.4, pred[]{:T(512)S(6)} %or.3), kind=kOutput, calls=%fused_computation.12 | convolution fusion | flops 2148007936 | bytes 12582917 | tf_op jit(solution)/shard_map/dot_general | solution.py:83
  182.1 6.0 %fusion.26 = bf16[256,2048]{1,0:T(8,128)(2,1)S(1)} fusion(f32[256,2048]{1,0:T(8,128)S(1)} %fusion.12, bf16[8192,2048]{1,0:T(8,128)(2,1)} %param.6, s32[]{:T(128)S(6)} %select_n.75, f32[512,2048]{1,0:T(8,128)S(1)} %fusion.14, bf16[256,2048]{1,0:T(8,128)(2,1)S(1)} %collective-permute-done.3, bf16[256,2048]{1,0:T(8,128)(2,1)} %collective-permute-done.2, ...), kind=kOutput, calls=%fused_computation.19 | convolution fusion | flops 2149580800 | bytes 15728645 | tf_op jit(solution)/shard_map/dot_general | solution.py:83
  188.1 1.5 pad_maximum_fusion
  (26 shorter events, 8.6 us)
Async XLA Ops:
  6.5 55.4 %copy-start = (bf16[4,64,2048]{2,1,0:T(8,128)(2,1)S(1)}, bf16[4,64,2048]{2,1,0:T(8,128)(2,1)}, u32[]{:S(2)}) copy-start(bf16[4,64,2048]{2,1,0:T(8,128)(2,1)} %param.8) | copy-start | bytes 3145732
  6.5 17.4 %copy-start.2 = (bf16[2,256,2048]{2,1,0:T(8,128)(2,1)S(1)}, bf16[2,256,2048]{2,1,0:T(8,128)(2,1)}, u32[]{:S(2)}) copy-start(bf16[2,256,2048]{2,1,0:T(8,128)(2,1)} %param.5) | copy-start | bytes 6291460
  6.5 55.4 %all-reduce.2.cloned.1.call-start = ((), (), s32[]{:S(2)}) async-start(), calls=%async_computation | async-start | bytes 131072 | tf_op jit(solution)/shard_map/psum | solution.py:95
  6.5 60.6 %collective-permute-start.1 = (bf16[512,2048]{1,0:T(8,128)(2,1)}, bf16[512,2048]{1,0:T(8,128)(2,1)}, u32[]{:S(2)}, u32[]{:S(2)}) collective-permute-start(bf16[512,2048]{1,0:T(8,128)(2,1)} %bitcast.29), channel_id=1, source_target_pairs={{0,4},{12,8},{1,5},{13,9},{2,6},{14,10},{3,7},{15,11},{16,20},{28,... | collective-permute-start | bytes 6291464 | tf_op jit(solution)/shard_map/ppermute | solution.py:68
  13.1 57.2 %collective-permute-start = (bf16[512,2048]{1,0:T(8,128)(2,1)}, bf16[512,2048]{1,0:T(8,128)(2,1)}, u32[]{:S(2)}, u32[]{:S(2)}) collective-permute-start(bf16[512,2048]{1,0:T(8,128)(2,1)} %bitcast.30), channel_id=1, source_target_pairs={{4,0},{8,12},{5,1},{9,13},{6,2},{10,14},{7,3},{11,15},{20,16},{24,... | collective-permute-start | bytes 6291464 | tf_op jit(solution)/shard_map/ppermute | solution.py:68
  25.4 39.1 %collective-permute-start.2 = (bf16[256,2048]{1,0:T(8,128)(2,1)}, bf16[256,2048]{1,0:T(8,128)(2,1)}, u32[]{:S(2)}, u32[]{:S(2)}) collective-permute-start(bf16[256,2048]{1,0:T(8,128)(2,1)} %get-tuple-element.5), channel_id=1, source_target_pairs={{4,8},{8,4},{5,9},{9,5},{6,10},{10,6},{7,11},{11,7},{20,24},{24,20... | collective-permute-start | bytes 3145736 | tf_op jit(solution)/shard_map/ppermute | solution.py:68
  27.2 38.7 %collective-permute-start.6 = (bf16[256,2048]{1,0:T(8,128)(2,1)}, bf16[256,2048]{1,0:T(8,128)(2,1)}, u32[]{:S(2)}, u32[]{:S(2)}) collective-permute-start(bf16[256,2048]{1,0:T(8,128)(2,1)} %get-tuple-element.6), channel_id=1, source_target_pairs={{4,8},{8,4},{5,9},{9,5},{6,10},{10,6},{7,11},{11,7},{20,24},{24,20... | collective-permute-start | bytes 3145736 | tf_op jit(solution)/shard_map/ppermute | solution.py:68
  61.9 8.4 %copy-start.3 = (f32[2048,512]{0,1:T(8,128)S(1)}, f32[2048,512]{0,1:T(8,128)}, u32[]{:S(2)}) copy-start(f32[2048,512]{0,1:T(8,128)} %fusion.2) | copy-start | bytes 12582916
  64.5 117.5 %collective-permute-start.3 = (bf16[256,2048]{1,0:T(8,128)(2,1)}, bf16[256,2048]{1,0:T(8,128)(2,1)S(1)}, u32[]{:S(2)}, u32[]{:S(2)}) collective-permute-start(bf16[256,2048]{1,0:T(8,128)(2,1)} %collective-permute-done.2), channel_id=1, source_target_pairs={{4,0},{8,12},{5,1},{9,13},{6,2},{10,14},{7,3},{11,15},{20,16},{24,... | collective-permute-start | bytes 3145736 | tf_op jit(solution)/shard_map/ppermute | solution.py:68
  65.8 46.2 %collective-permute-start.7 = (bf16[256,2048]{1,0:T(8,128)(2,1)}, bf16[256,2048]{1,0:T(8,128)(2,1)S(1)}, u32[]{:S(2)}, u32[]{:S(2)}) collective-permute-start(bf16[256,2048]{1,0:T(8,128)(2,1)} %collective-permute-done.6), channel_id=1, source_target_pairs={{4,0},{8,12},{5,1},{9,13},{6,2},{10,14},{7,3},{11,15},{20,16},{24,... | collective-permute-start | bytes 3145736 | tf_op jit(solution)/shard_map/ppermute | solution.py:68
  68.8 11.9 %collective-permute-start.4 = (bf16[256,2048]{1,0:T(8,128)(2,1)S(1)}, bf16[256,2048]{1,0:T(8,128)(2,1)S(1)}, u32[]{:S(2)}, u32[]{:S(2)}) collective-permute-start(bf16[256,2048]{1,0:T(8,128)(2,1)S(1)} %get-tuple-element.7), channel_id=1, source_target_pairs={{4,8},{8,4},{5,9},{9,5},{6,10},{10,6},{7,11},{11,7},{20,24},{24,20... | collective-permute-start | bytes 3145736 | tf_op jit(solution)/shard_map/ppermute | solution.py:68
  69.6 8.4 %collective-permute-start.8 = (bf16[256,2048]{1,0:T(8,128)(2,1)S(1)}, bf16[256,2048]{1,0:T(8,128)(2,1)S(1)}, u32[]{:S(2)}, u32[]{:S(2)}) collective-permute-start(bf16[256,2048]{1,0:T(8,128)(2,1)S(1)} %get-tuple-element.8), channel_id=1, source_target_pairs={{4,8},{8,4},{5,9},{9,5},{6,10},{10,6},{7,11},{11,7},{20,24},{24,20... | collective-permute-start | bytes 3145736 | tf_op jit(solution)/shard_map/ppermute | solution.py:68
  78.1 67.7 %collective-permute-start.9 = (bf16[128,2048]{1,0:T(8,128)(2,1)S(1)}, bf16[128,2048]{1,0:T(8,128)(2,1)S(1)}, u32[]{:S(2)}, u32[]{:S(2)}) collective-permute-start(bf16[128,2048]{1,0:T(8,128)(2,1)S(1)} %get-tuple-element.9), channel_id=1, source_target_pairs={{4,0},{8,12},{5,1},{9,13},{6,2},{10,14},{7,3},{11,15},{20,16},{24,... | collective-permute-start | bytes 1572872 | tf_op jit(solution)/shard_map/ppermute | solution.py:68
  79.4 77.6 %collective-permute-start.10 = (bf16[128,2048]{1,0:T(8,128)(2,1)S(1)}, bf16[128,2048]{1,0:T(8,128)(2,1)S(1)}, u32[]{:S(2)}, u32[]{:S(2)}) collective-permute-start(bf16[128,2048]{1,0:T(8,128)(2,1)S(1)} %get-tuple-element.10), channel_id=1, source_target_pairs={{4,0},{8,12},{5,1},{9,13},{6,2},{10,14},{7,3},{11,15},{20,16},{24,... | collective-permute-start | bytes 1572872 | tf_op jit(solution)/shard_map/ppermute | solution.py:68
  80.7 95.6 %collective-permute-start.5 = (bf16[256,2048]{1,0:T(8,128)(2,1)S(1)}, bf16[256,2048]{1,0:T(8,128)(2,1)S(1)}, u32[]{:S(2)}, u32[]{:S(2)}) collective-permute-start(bf16[256,2048]{1,0:T(8,128)(2,1)S(1)} %collective-permute-done.4), channel_id=1, source_target_pairs={{4,0},{8,12},{5,1},{9,13},{6,2},{10,14},{7,3},{11,15},{20,16},{24,... | collective-permute-start | bytes 3145736 | tf_op jit(solution)/shard_map/ppermute | solution.py:68
  182.1 7.4 %copy-start.1 = (bf16[4,64,2048]{2,1,0:T(8,128)(2,1)S(1)}, bf16[4,64,2048]{2,1,0:T(8,128)(2,1)}, u32[]{:S(2)}) copy-start(bf16[4,64,2048]{2,1,0:T(8,128)(2,1)} %param.8) | copy-start | bytes 3145732
Sparse Core Ops, SparseCore 0:
  24.1 37.7 all-reduce.1

commit v4 on v3

--- a/solution.py
+++ b/solution.py
@@ -68,6 +68,10 @@
     return lax.ppermute(block, "tensor", pairs)
 
 
+def after(block, *earlier):
+    return lax.optimization_barrier((block,) + earlier)[0]
+
+
 def line(inputs, base_weight, shrink_table, expand_table, adapter_ids):
     chats, span, width = inputs.shape
     rows = chats * span
@@ -92,9 +96,11 @@
         for block in (across_mate[0], across_mate[1][:quarter], across_mate[1][quarter:])
     ]
 
-    shrunk = lax.psum(shrink(inputs, shrink_table, adapter_ids), "tensor")
-    total = product(own, here) + jnp.concatenate(expand(shrunk, expand_table, adapter_ids))
-    total = total + product(jnp.where(is_end, mate_out, mate_in), here ^ 1)
+    partial = shrink(inputs, shrink_table, adapter_ids)
+    shrunk = lax.psum(after(partial, across_own[0]), "tensor")
+    total = product(own, here) + product(jnp.where(is_end, mate_out, mate_in), here ^ 1)
+    shrunk = after(shrunk, across_mate[0])
+    total = total + jnp.concatenate(expand(shrunk, expand_table, adapter_ids))
     outs = []
     for i, cut in enumerate((slice(0, half), slice(half, rows))):
         part = total[cut] + product(jnp.where(is_end, mid_out[i], across_own[i]), far_mid)

time: 197 us -> 194 us (0.985)
  waiting for transfers between devices: 103 us -> 96.5 us
  local copies, waits for them, and re-layouts: 4.61 us -> 6.59 us
    ppermute x11, waiting for transfers between devices: 78.9 us -> 70 us  [send(): return lax.ppermute(block, 'tensor', pairs)]
    psum x1, waiting for transfers between devices: 23.8 us -> 26.5 us  [line(): shrunk = lax.psum(after(partial, across_own[0]), 'tensor')]
  transfers between devices with their start and end apart: 12 -> 12, of which waited for: 5 -> 6; matrix products, arithmetic and copies ran while one was open for 25% -> 27% of each run, Pallas kernels for 0% -> 0%
where the time goes in v4:
time: 194 us
  waiting for transfers between devices  96.5 us (50%)
  matrix products  50.9 us (26%)
  starting transfers between devices  20.3 us (10%)
  between operations  17.1 us (9%)
  local copies, waits for them, and re-layouts  6.59 us (3%)
  other arithmetic  2.2 us (1%)
    ppermute x11, waiting for transfers between devices, send(): return lax.ppermute(block, 'tensor', pairs)  70 us
    dot_general x7, matrix products, product(): return jnp.dot(block, part, preferred_element_type=F32)  45.7 us
    psum x1, waiting for transfers between devices, line(): shrunk = lax.psum(after(partial, across_own[0]), 'tensor')  26.5 us
    ppermute x11, starting transfers between devices, send(): return lax.ppermute(block, 'tensor', pairs)  20.3 us
  transfers between devices with their start and end apart: 12, of which 6 were waited for; matrix products, arithmetic and copies ran while one was open for 27% of the time, Pallas kernels for 0%

profile of v4, /device:TPU:0, one launch (start us, length us, event | category | flops | bytes accessed | tf_op | source)
XLA Modules:
  0.0 193.6 jit_solution(9335215579966407913)
XLA Ops:
  6.5 6.4 %collective-permute-start.1 = (bf16[512,2048]{1,0:T(8,128)(2,1)}, bf16[512,2048]{1,0:T(8,128)(2,1)}, u32[]{:S(2)}, u32[]{:S(2)}) collective-permute-start(bf16[512,2048]{1,0:T(8,128)(2,1)} %bitcast.31), channel_id=1, source_target_pairs={{0,4},{12,8},{1,5},{13,9},{2,6},{14,10},{3,7},{15,11},{16,20},{28,... | collective-permute-start | bytes 6291464 | tf_op jit(solution)/shard_map/ppermute | solution.py:68
  14.2 2.8 %slice_bitcast_fusion = (bf16[256,2048]{1,0:T(8,128)(2,1)S(1)}, bf16[256,2048]{1,0:T(8,128)(2,1)}) fusion(bf16[2,256,2048]{2,1,0:T(8,128)(2,1)} %param.5), kind=kLoop, calls=%fused_computation.34 | loop fusion | bytes 4194304 | tf_op jit(solution)/shard_map/squeeze | solution.py:12
  17.0 1.7 collective-permute-start.2
  18.7 1.7 collective-permute-start.6
  24.6 1.8 fusion.30
  26.3 30.5 %collective-permute-done.1 = bf16[512,2048]{1,0:T(8,128)(2,1)} collective-permute-done((bf16[512,2048]{1,0:T(8,128)(2,1)}, bf16[512,2048]{1,0:T(8,128)(2,1)}, u32[]{:S(2)}, u32[]{:S(2)}) %collective-permute-start.1) | collective-permute-done | bytes 2097184 | tf_op jit(solution)/shard_map/ppermute | solution.py:68
  56.8 3.1 %fusion.77 = (bf16[256,2048]{1,0:T(8,128)(2,1)}, bf16[256,2048]{1,0:T(8,128)(2,1)}) fusion(bf16[512,2048]{1,0:T(8,128)(2,1)} %collective-permute-done.1), kind=kLoop, calls=%fused_computation.69 | loop fusion | bytes 4194304 | tf_op jit(solution)/shard_map/slice | solution.py:92
  59.9 1.6 collective-permute-start.3
  62.3 1.8 fusion.31
  64.7 10.5 %fusion.2 = f32[2048,512]{0,1:T(8,128)} fusion(bf16[512,2048]{1,0:T(8,128)(2,1)} %bitcast.33, bf16[8192,2048]{1,0:T(8,128)(2,1)} %param.6, s32[]{:T(128)S(6)} %select_n.66), kind=kOutput, calls=%fused_computation.2 | convolution fusion | flops 4294967296 | bytes 14680068 | tf_op jit(solution)/shard_map/dot_general | solution.py:87
  77.8 26.5 %all-reduce.2.cloned.1.call-done = bf16[512,64]{0,1:T(8,128)(2,1)} async-done(((bf16[512,64]{0,1:T(8,128)(2,1)}), bf16[512,64]{0,1:T(8,128)(2,1)}) %all-reduce.2.cloned.1.call-update) | async-done | bytes 65552 | tf_op jit(solution)/shard_map/psum | solution.py:100
  104.4 1.6 collective-permute-start.9
  109.0 1.5 collective-permute-start.5
  110.5 7.7 %maximum_add_fusion = f32[512,2048]{1,0:T(8,128)S(1)} fusion(f32[256,2048]{1,0:T(8,128)S(1)} %fusion.52, f32[256,2048]{1,0:T(8,128)S(1)} %fusion.54, f32[2048,512]{0,1:T(8,128)S(1)} %copy-done.4, bf16[8192,2048]{1,0:T(8,128)(2,1)} %param.6, s32[]{:T(128)S(6)} %select_n.69, bf16[512,2048]{1,0:T(8,128)(2,1)} %collective-permute-done, ...), kind=kOutput, calls=%fused_computation.14 | convolution fusion | flops 4299161600 | bytes 25165828 | tf_op jit(solution)/shard_map/dot_general | solution.py:87
  118.1 12.3 %collective-permute-done.7 = bf16[256,2048]{1,0:T(8,128)(2,1)} collective-permute-done((bf16[256,2048]{1,0:T(8,128)(2,1)}, bf16[256,2048]{1,0:T(8,128)(2,1)}, u32[]{:S(2)}, u32[]{:S(2)}) %collective-permute-start.7) | collective-permute-done | bytes 1048608 | tf_op jit(solution)/shard_map/ppermute | solution.py:68
  130.4 6.1 %fusion.19 = f32[256,2048]{1,0:T(8,128)S(1)} fusion(bf16[8192,2048]{1,0:T(8,128)(2,1)} %param.6, s32[]{:T(128)S(6)} %select_n.75, f32[512,2048]{1,0:T(8,128)S(1)} %maximum_add_fusion, bf16[256,2048]{1,0:T(8,128)(2,1)} %collective-permute-done.7, bf16[256,2048]{1,0:T(8,128)(2,1)} %collective-permute-done.6, pred[]{:T(512)S(6)} %or.3), kind=kOutput, calls=%fused_computation.17 | convolution fusion | flops 2148532224 | bytes 14680069 | tf_op jit(solution)/shard_map/dot_general | solution.py:87
  136.5 5.0 %collective-permute-done.9 = bf16[128,2048]{1,0:T(8,128)(2,1)S(1)} collective-permute-done((bf16[128,2048]{1,0:T(8,128)(2,1)S(1)}, bf16[128,2048]{1,0:T(8,128)(2,1)S(1)}, u32[]{:S(2)}, u32[]{:S(2)}) %collective-permute-start.9) | collective-permute-done | bytes 524320 | tf_op jit(solution)/shard_map/ppermute | solution.py:68
  141.6 4.7 %fusion.33 = bf16[128,2048]{1,0:T(8,128)(2,1)S(1)} fusion(f32[256,2048]{1,0:T(8,128)S(1)} %fusion.19, bf16[8192,2048]{1,0:T(8,128)(2,1)} %param.6, s32[]{:T(128)S(6)} %select_n.78, bf16[128,2048]{1,0:T(8,128)(2,1)S(1)} %collective-permute-done.9, pred[]{:T(512)S(6)} %or.3, bf16[256,2048]{1,0:T(8,128)(2,1)S(1)} %collective-permute-done.8), kind=kOutput, calls=%fused_computation.30 | convolution fusion | flops 1074528256 | bytes 11010053 | tf_op jit(solution)/shard_map/dot_general | solution.py:87
  146.3 6.5 %collective-permute-done.10 = bf16[128,2048]{1,0:T(8,128)(2,1)S(1)} collective-permute-done((bf16[128,2048]{1,0:T(8,128)(2,1)S(1)}, bf16[128,2048]{1,0:T(8,128)(2,1)S(1)}, u32[]{:S(2)}, u32[]{:S(2)}) %collective-permute-start.10) | collective-permute-done | bytes 524320 | tf_op jit(solution)/shard_map/ppermute | solution.py:68
  152.8 4.7 %fusion.32 = bf16[128,2048]{1,0:T(8,128)(2,1)S(1)} fusion(f32[256,2048]{1,0:T(8,128)S(1)} %fusion.19, bf16[8192,2048]{1,0:T(8,128)(2,1)} %param.6, s32[]{:T(128)S(6)} %select_n.78, bf16[128,2048]{1,0:T(8,128)(2,1)S(1)} %collective-permute-done.10, pred[]{:T(512)S(6)} %or.3, bf16[256,2048]{1,0:T(8,128)(2,1)S(1)} %collective-permute-done.8), kind=kOutput, calls=%fused_computation.28 | convolution fusion | flops 1074528256 | bytes 11010053 | tf_op jit(solution)/shard_map/dot_general | solution.py:87
  157.5 15.7 %collective-permute-done.5 = bf16[256,2048]{1,0:T(8,128)(2,1)S(1)} collective-permute-done((bf16[256,2048]{1,0:T(8,128)(2,1)}, bf16[256,2048]{1,0:T(8,128)(2,1)S(1)}, u32[]{:S(2)}, u32[]{:S(2)}) %collective-permute-start.5) | collective-permute-done | bytes 1048608 | tf_op jit(solution)/shard_map/ppermute | solution.py:68
  173.2 5.7 %fusion.12 = f32[256,2048]{1,0:T(8,128)S(1)} fusion(bf16[8192,2048]{1,0:T(8,128)(2,1)} %param.6, s32[]{:T(128)S(6)} %select_n.78, bf16[256,2048]{1,0:T(8,128)(2,1)S(1)} %collective-permute-done.5, bf16[256,2048]{1,0:T(8,128)(2,1)} %collective-permute-done.3, pred[]{:T(512)S(6)} %or.3), kind=kOutput, calls=%fused_computation.12 | convolution fusion | flops 2148007936 | bytes 12582917 | tf_op jit(solution)/shard_map/dot_general | solution.py:87
  178.9 6.3 %fusion.25 = bf16[256,2048]{1,0:T(8,128)(2,1)S(1)} fusion(f32[256,2048]{1,0:T(8,128)S(1)} %fusion.12, bf16[8192,2048]{1,0:T(8,128)(2,1)} %param.6, s32[]{:T(128)S(6)} %select_n.75, f32[512,2048]{1,0:T(8,128)S(1)} %maximum_add_fusion, bf16[256,2048]{1,0:T(8,128)(2,1)} %collective-permute-done.4, bf16[256,2048]{1,0:T(8,128)(2,1)} %collective-permute-done.2, ...), kind=kOutput, calls=%fused_computation.19 | convolution fusion | flops 2149580800 | bytes 15728645 | tf_op jit(solution)/shard_map/dot_general | solution.py:87
  185.2 1.6 pad_maximum_fusion
  (28 shorter events, 8.9 us)
Async XLA Ops:
  6.5 100.7 %copy-start = (bf16[4,64,2048]{2,1,0:T(8,128)(2,1)S(1)}, bf16[4,64,2048]{2,1,0:T(8,128)(2,1)}, u32[]{:S(2)}) copy-start(bf16[4,64,2048]{2,1,0:T(8,128)(2,1)} %param.8) | copy-start | bytes 3145732
  6.5 13.9 %copy-start.3 = (s32[2]{0:T(128)S(1)}, s32[2]{0:T(128)}, u32[]{:S(2)}) copy-start(s32[2]{0:T(128)} %param.9) | copy-start | bytes 28
  6.5 97.7 %all-reduce.2.cloned.1.call-start = ((), (), s32[]{:S(2)}) async-start(), calls=%async_computation | async-start | bytes 131072 | tf_op jit(solution)/shard_map/psum | solution.py:100
  6.5 50.2 %collective-permute-start.1 = (bf16[512,2048]{1,0:T(8,128)(2,1)}, bf16[512,2048]{1,0:T(8,128)(2,1)}, u32[]{:S(2)}, u32[]{:S(2)}) collective-permute-start(bf16[512,2048]{1,0:T(8,128)(2,1)} %bitcast.31), channel_id=1, source_target_pairs={{0,4},{12,8},{1,5},{13,9},{2,6},{14,10},{3,7},{15,11},{16,20},{28,... | collective-permute-start | bytes 6291464 | tf_op jit(solution)/shard_map/ppermute | solution.py:68
  13.0 96.0 %collective-permute-start = (bf16[512,2048]{1,0:T(8,128)(2,1)}, bf16[512,2048]{1,0:T(8,128)(2,1)}, u32[]{:S(2)}, u32[]{:S(2)}) collective-permute-start(bf16[512,2048]{1,0:T(8,128)(2,1)} %bitcast.32), channel_id=1, source_target_pairs={{4,0},{8,12},{5,1},{9,13},{6,2},{10,14},{7,3},{11,15},{20,16},{24,... | collective-permute-start | bytes 6291464 | tf_op jit(solution)/shard_map/ppermute | solution.py:68
  17.0 47.6 %collective-permute-start.2 = (bf16[256,2048]{1,0:T(8,128)(2,1)}, bf16[256,2048]{1,0:T(8,128)(2,1)}, u32[]{:S(2)}, u32[]{:S(2)}) collective-permute-start(bf16[256,2048]{1,0:T(8,128)(2,1)} %get-tuple-element.12), channel_id=1, source_target_pairs={{4,8},{8,4},{5,9},{9,5},{6,10},{10,6},{7,11},{11,7},{20,24},{24,20... | collective-permute-start | bytes 3145736 | tf_op jit(solution)/shard_map/ppermute | solution.py:68
  18.7 57.7 %collective-permute-start.6 = (bf16[256,2048]{1,0:T(8,128)(2,1)S(1)}, bf16[256,2048]{1,0:T(8,128)(2,1)}, u32[]{:S(2)}, u32[]{:S(2)}) collective-permute-start(bf16[256,2048]{1,0:T(8,128)(2,1)S(1)} %get-tuple-element.11), channel_id=1, source_target_pairs={{4,8},{8,4},{5,9},{9,5},{6,10},{10,6},{7,11},{11,7},{20,24},{24,20... | collective-permute-start | bytes 3145736 | tf_op jit(solution)/shard_map/ppermute | solution.py:68
  59.9 44.4 %collective-permute-start.3 = (bf16[256,2048]{1,0:T(8,128)(2,1)}, bf16[256,2048]{1,0:T(8,128)(2,1)}, u32[]{:S(2)}, u32[]{:S(2)}) collective-permute-start(bf16[256,2048]{1,0:T(8,128)(2,1)} %get-tuple-element.10), channel_id=1, source_target_pairs={{4,8},{8,4},{5,9},{9,5},{6,10},{10,6},{7,11},{11,7},{20,24},{24,20... | collective-permute-start | bytes 3145736 | tf_op jit(solution)/shard_map/ppermute | solution.py:68
  61.5 42.7 %collective-permute-start.8 = (bf16[256,2048]{1,0:T(8,128)(2,1)}, bf16[256,2048]{1,0:T(8,128)(2,1)S(1)}, u32[]{:S(2)}, u32[]{:S(2)}) collective-permute-start(bf16[256,2048]{1,0:T(8,128)(2,1)} %get-tuple-element.9), channel_id=1, source_target_pairs={{4,8},{8,4},{5,9},{9,5},{6,10},{10,6},{7,11},{11,7},{20,24},{24,20... | collective-permute-start | bytes 3145736 | tf_op jit(solution)/shard_map/ppermute | solution.py:68
  75.2 103.7 %collective-permute-start.4 = (bf16[256,2048]{1,0:T(8,128)(2,1)}, bf16[256,2048]{1,0:T(8,128)(2,1)}, u32[]{:S(2)}, u32[]{:S(2)}) collective-permute-start(bf16[256,2048]{1,0:T(8,128)(2,1)} %collective-permute-done.2), channel_id=1, source_target_pairs={{4,0},{8,12},{5,1},{9,13},{6,2},{10,14},{7,3},{11,15},{20,16},{24,... | collective-permute-start | bytes 3145736 | tf_op jit(solution)/shard_map/ppermute | solution.py:68
  76.5 54.0 %collective-permute-start.7 = (bf16[256,2048]{1,0:T(8,128)(2,1)}, bf16[256,2048]{1,0:T(8,128)(2,1)}, u32[]{:S(2)}, u32[]{:S(2)}) collective-permute-start(bf16[256,2048]{1,0:T(8,128)(2,1)} %collective-permute-done.6), channel_id=1, source_target_pairs={{4,0},{8,12},{5,1},{9,13},{6,2},{10,14},{7,3},{11,15},{20,16},{24,... | collective-permute-start | bytes 3145736 | tf_op jit(solution)/shard_map/ppermute | solution.py:68
  104.3 4.2 %copy-start.2 = (bf16[512,64]{0,1:T(8,128)(2,1)S(1)}, bf16[512,64]{0,1:T(8,128)(2,1)}, u32[]{:S(2)}) copy-start(bf16[512,64]{0,1:T(8,128)(2,1)} %all-reduce.2.cloned.1.call-done) | copy-start | bytes 196612
  104.3 6.2 %copy-start.4 = (f32[2048,512]{0,1:T(8,128)S(1)}, f32[2048,512]{0,1:T(8,128)}, u32[]{:S(2)}) copy-start(f32[2048,512]{0,1:T(8,128)} %fusion.2) | copy-start | bytes 12582916
  104.4 37.2 %collective-permute-start.9 = (bf16[128,2048]{1,0:T(8,128)(2,1)S(1)}, bf16[128,2048]{1,0:T(8,128)(2,1)S(1)}, u32[]{:S(2)}, u32[]{:S(2)}) collective-permute-start(bf16[128,2048]{1,0:T(8,128)(2,1)S(1)} %get-tuple-element.13), channel_id=1, source_target_pairs={{4,0},{8,12},{5,1},{9,13},{6,2},{10,14},{7,3},{11,15},{20,16},{24,... | collective-permute-start | bytes 1572872 | tf_op jit(solution)/shard_map/ppermute | solution.py:68
  106.0 46.8 %collective-permute-start.10 = (bf16[128,2048]{1,0:T(8,128)(2,1)S(1)}, bf16[128,2048]{1,0:T(8,128)(2,1)S(1)}, u32[]{:S(2)}, u32[]{:S(2)}) collective-permute-start(bf16[128,2048]{1,0:T(8,128)(2,1)S(1)} %get-tuple-element.14), channel_id=1, source_target_pairs={{4,0},{8,12},{5,1},{9,13},{6,2},{10,14},{7,3},{11,15},{20,16},{24,... | collective-permute-start | bytes 1572872 | tf_op jit(solution)/shard_map/ppermute | solution.py:68
  109.0 64.2 %collective-permute-start.5 = (bf16[256,2048]{1,0:T(8,128)(2,1)}, bf16[256,2048]{1,0:T(8,128)(2,1)S(1)}, u32[]{:S(2)}, u32[]{:S(2)}) collective-permute-start(bf16[256,2048]{1,0:T(8,128)(2,1)} %collective-permute-done.3), channel_id=1, source_target_pairs={{4,0},{8,12},{5,1},{9,13},{6,2},{10,14},{7,3},{11,15},{20,16},{24,... | collective-permute-start | bytes 3145736 | tf_op jit(solution)/shard_map/ppermute | solution.py:68
  178.9 7.9 %copy-start.1 = (bf16[4,64,2048]{2,1,0:T(8,128)(2,1)S(1)}, bf16[4,64,2048]{2,1,0:T(8,128)(2,1)}, u32[]{:S(2)}) copy-start(bf16[4,64,2048]{2,1,0:T(8,128)(2,1)} %param.8) | copy-start | bytes 3145732
Sparse Core Ops, SparseCore 0:
  64.8 39.4 all-reduce.1

commit v5 on v4

--- a/solution.py
+++ b/solution.py
@@ -62,6 +62,7 @@
 INWARD = [(0, 1), (3, 2)]
 OUTWARD = [(1, 0), (2, 3)]
 ACROSS = [(1, 2), (2, 1)]
+SWAP = INWARD + OUTWARD
 
 
 def send(block, pairs):
@@ -80,36 +81,37 @@
     far_mid = jnp.where(here < 2, 2, 1)
     far_end = jnp.where(here < 2, 3, 0)
     own = inputs.reshape(rows, width)
-    half, quarter = rows // 2, rows // 4
+    cuts = [slice(0, rows // 2), slice(rows // 2, 3 * rows // 4), slice(3 * rows // 4, rows)]
 
     def product(block, owner):
         part = lax.dynamic_slice_in_dim(base_weight, owner * width, width, axis=0)
         return jnp.dot(block, part, preferred_element_type=F32)
 
-    across_own = [send(own[:half], ACROSS), send(own[half:], ACROSS)]
     mate_out = send(own, OUTWARD)
     mate_in = send(own, INWARD)
-    across_mate = [send(mate_in[:half], ACROSS), send(mate_in[half:], ACROSS)]
-    mid_out = [send(block, OUTWARD) for block in across_own]
-    end_out = [
-        send(block, OUTWARD)
-        for block in (across_mate[0], across_mate[1][:quarter], across_mate[1][quarter:])
+    across_own = send(own, ACROSS)
+    partial = shrink(inputs, shrink_table, adapter_ids)
+    mate_partial = send(partial, SWAP)
+    total = product(own, here)
+
+    mate_in = after(mate_in, total)
+    across_mate = send(mate_in, ACROSS)
+    mid_out = send(across_own, OUTWARD)
+    both = send(jnp.stack([partial, mate_partial]), ACROSS)
+    total = total + product(jnp.where(is_end, mate_out, mate_in), here ^ 1)
+
+    across_mate = after(across_mate, total)
+    end_out = [send(across_mate[cut], OUTWARD) for cut in cuts]
+    shrunk = (
+        partial.astype(F32) + mate_partial.astype(F32) + both[0].astype(F32) + both[1].astype(F32)
+    ).astype(BF16)
+    shrunk = jnp.where(is_end, send(shrunk, OUTWARD), shrunk)
+    total = total + product(jnp.where(is_end, mid_out, across_own), far_mid)
+    total = total + jnp.concatenate(expand(shrunk, expand_table, adapter_ids))
+    outs = [
+        total[cut] + product(jnp.where(is_end, out, across_mate[cut]), far_end)
+        for cut, out in zip(cuts, end_out)
     ]
-
-    partial = shrink(inputs, shrink_table, adapter_ids)
-    shrunk = lax.psum(after(partial, across_own[0]), "tensor")
-    total = product(own, here) + product(jnp.where(is_end, mate_out, mate_in), here ^ 1)
-    shrunk = after(shrunk, across_mate[0])
-    total = total + jnp.concatenate(expand(shrunk, expand_table, adapter_ids))
-    outs = []
-    for i, cut in enumerate((slice(0, half), slice(half, rows))):
-        part = total[cut] + product(jnp.where(is_end, mid_out[i], across_own[i]), far_mid)
-        if i == 0:
-            outs.append(part + product(jnp.where(is_end, end_out[0], across_mate[0]), far_end))
-        else:
-            for j, sub in enumerate((slice(0, quarter), slice(quarter, half))):
-                block = jnp.where(is_end, end_out[1 + j], across_mate[1][sub])
-                outs.append(part[sub] + product(block, far_end))
     return jnp.concatenate([o.astype(BF16) for o in outs]).reshape(chats, span, -1)
 
 

time: 194 us -> 179 us (0.923)
  between operations: 17.1 us -> 4.09 us
  waiting for transfers between devices: 96.5 us -> 103 us
  local copies, waits for them, and re-layouts: 6.59 us -> 1.49 us
  starting transfers between devices: 20.3 us -> 17.9 us
    ppermute x11, waiting for transfers between devices: 70 us -> 103 us  [send(): return lax.ppermute(block, 'tensor', pairs)]
    psum x1 -> x0, waiting for transfers between devices: 26.5 us -> none  [line(): shrunk = lax.psum(after(partial, across_own[0]), 'tensor')]
    slice x2, local copies, waits for them, and re-layouts: 3.21 us -> 0.14 us  [line(): end_out = [send(across_mate[cut], OUTWARD) for cut in cuts]]
    squeeze x1 -> x0, local copies, waits for them, and re-layouts: 2.76 us -> none  [shrink(): inputs[c]]
    ppermute x11, starting transfers between devices: 20.3 us -> 17.9 us  [send(): return lax.ppermute(block, 'tensor', pairs)]
    dot_general x7 -> x6, matrix products: 45.7 us -> 45.5 us  [product(): return jnp.dot(block, part, preferred_element_type=F32)]
  transfers between devices with their start and end apart: 12 -> 11, of which waited for: 6 -> 5; matrix products, arithmetic and copies ran while one was open for 27% -> 26% of each run, Pallas kernels for 0% -> 0%
where the time goes in v5:
time: 179 us; the launch traced here: 178 us
  waiting for transfers between devices  103 us (58%)
  matrix products  50 us (28%)
  starting transfers between devices  17.9 us (10%)
  between operations  4.09 us (2%)
    ppermute x11, waiting for transfers between devices, send(): return lax.ppermute(block, 'tensor', pairs)  103 us
    dot_general x6, matrix products, product(): return jnp.dot(block, part, preferred_element_type=F32)  45.5 us
    ppermute x11, starting transfers between devices, send(): return lax.ppermute(block, 'tensor', pairs)  17.9 us
  transfers between devices with their start and end apart: 11, of which 5 were waited for; matrix products, arithmetic and copies ran while one was open for 26% of the time, Pallas kernels for 0%

profile of v5, /device:TPU:0, one launch (start us, length us, event | category | flops | bytes accessed | tf_op | source)
XLA Modules:
  0.0 178.3 jit_solution(14639951209103933173)
XLA Ops:
  0.0 6.4 %collective-permute-start.1 = (bf16[512,2048]{1,0:T(8,128)(2,1)}, bf16[512,2048]{1,0:T(8,128)(2,1)}, u32[]{:S(2)}, u32[]{:S(2)}) collective-permute-start(bf16[512,2048]{1,0:T(8,128)(2,1)} %bitcast.43), channel_id=1, source_target_pairs={{0,4},{12,8},{1,5},{13,9},{2,6},{14,10},{3,7},{15,11},{16,20},{28,... | collective-permute-start | bytes 6291464 | tf_op jit(solution)/shard_map/ppermute | solution.py:69
  6.4 2.0 %collective-permute-start.2 = (bf16[512,2048]{1,0:T(8,128)(2,1)}, bf16[512,2048]{1,0:T(8,128)(2,1)}, u32[]{:S(2)}, u32[]{:S(2)}) collective-permute-start(bf16[512,2048]{1,0:T(8,128)(2,1)} %bitcast.44), channel_id=1, source_target_pairs={{4,8},{8,4},{5,9},{9,5},{6,10},{10,6},{7,11},{11,7},{20,24},{24,20... | collective-permute-start | bytes 6291464 | tf_op jit(solution)/shard_map/ppermute | solution.py:69
  8.4 1.3 fusion.79
  11.7 1.8 fusion.25
  15.4 1.8 fusion.26
  17.2 1.3 collective-permute-start
  18.6 33.0 %collective-permute-done.4 = bf16[512,64]{0,1:T(8,128)(2,1)S(1)} collective-permute-done((bf16[512,64]{0,1:T(8,128)(2,1)S(1)}, bf16[512,64]{0,1:T(8,128)(2,1)S(1)}, u32[]{:S(2)}, u32[]{:S(2)}) %collective-permute-start.4) | collective-permute-done | bytes 65568 | tf_op jit(solution)/shard_map/ppermute | solution.py:69
  52.2 10.5 %fusion.12 = f32[512,2048]{1,0:T(8,128)} fusion(bf16[512,2048]{1,0:T(8,128)(2,1)} %bitcast.46, bf16[8192,2048]{1,0:T(8,128)(2,1)} %param.6, s32[]{:T(128)S(6)} %select_n.69), kind=kOutput, calls=%fused_computation.13 | convolution fusion | flops 4294967296 | bytes 14680068 | tf_op jit(solution)/shard_map/dot_general | solution.py:88
  62.7 0.8 collective-permute-start.7
  63.6 1.3 collective-permute-start.6
  64.9 9.0 %collective-permute-done.6 = bf16[512,64]{0,1:T(8,128)(2,1)S(1)} collective-permute-done((bf16[512,64]{0,1:T(8,128)(2,1)S(1)}, bf16[512,64]{0,1:T(8,128)(2,1)S(1)}, u32[]{:S(2)}, u32[]{:S(2)}) %collective-permute-start.6) | collective-permute-done | bytes 65568 | tf_op jit(solution)/shard_map/ppermute | solution.py:69
  74.0 1.3 collective-permute-start.3
  76.2 10.5 %fusion.15 = f32[512,2048]{1,0:T(8,128)} fusion(f32[512,2048]{1,0:T(8,128)S(1)} %copy-done.2, bf16[8192,2048]{1,0:T(8,128)(2,1)} %param.6, s32[]{:T(128)S(6)} %select_n.72, bf16[512,2048]{1,0:T(8,128)(2,1)} %collective-permute-done, bf16[512,2048]{1,0:T(8,128)(2,1)} %collective-permute-done.1, pred[]{:T(512)S(6)} %or.3), kind=kOutput, calls=%fused_computation.14 | convolution fusion | flops 4297064448 | bytes 20971524 | tf_op jit(solution)/shard_map/dot_general | solution.py:88
  86.8 1.3 collective-permute-start.8
  88.2 1.3 collective-permute-start.9
  89.5 1.5 collective-permute-start.10
  91.0 33.7 %collective-permute-done.3 = bf16[512,2048]{1,0:T(8,128)(2,1)S(1)} collective-permute-done((bf16[512,2048]{1,0:T(8,128)(2,1)}, bf16[512,2048]{1,0:T(8,128)(2,1)S(1)}, u32[]{:S(2)}, u32[]{:S(2)}) %collective-permute-start.3) | collective-permute-done | bytes 2097184 | tf_op jit(solution)/shard_map/ppermute | solution.py:69
  124.7 9.2 %maximum_add_fusion = f32[512,2048]{1,0:T(8,128)S(1)} fusion(f32[256,2048]{1,0:T(8,128)S(1)} %fusion.51, f32[256,2048]{1,0:T(8,128)S(1)} %fusion.53, f32[512,2048]{1,0:T(8,128)} %fusion.15, bf16[8192,2048]{1,0:T(8,128)(2,1)} %param.6, s32[]{:T(128)S(6)} %select_n.75, bf16[512,2048]{1,0:T(8,128)(2,1)S(1)} %collective-permute-done.3, ...), kind=kOutput, calls=%fused_computation.12 | convolution fusion | flops 4299161600 | bytes 25165828 | tf_op jit(solution)/shard_map/dot_general | solution.py:88
  133.9 24.5 %collective-permute-done.9 = bf16[128,2048]{1,0:T(8,128)(2,1)S(1)} collective-permute-done((bf16[128,2048]{1,0:T(8,128)(2,1)S(1)}, bf16[128,2048]{1,0:T(8,128)(2,1)S(1)}, u32[]{:S(2)}, u32[]{:S(2)}) %collective-permute-start.9) | collective-permute-done | bytes 524320 | tf_op jit(solution)/shard_map/ppermute | solution.py:69
  158.4 4.7 %fusion.28 = bf16[128,2048]{1,0:T(8,128)(2,1)S(1)} fusion(f32[512,2048]{1,0:T(8,128)S(1)} %maximum_add_fusion, bf16[8192,2048]{1,0:T(8,128)(2,1)} %param.6, s32[]{:T(128)S(6)} %select_n.83, bf16[128,2048]{1,0:T(8,128)(2,1)S(1)} %collective-permute-done.9, pred[]{:T(512)S(6)} %or.3, bf16[512,2048]{1,0:T(8,128)(2,1)S(1)} %collective-permute-done.7), kind=kOutput, calls=%fused_computation.29 | convolution fusion | flops 1074528256 | bytes 11010053 | tf_op jit(solution)/shard_map/dot_general | solution.py:88
  163.1 3.1 %collective-permute-done.10 = bf16[128,2048]{1,0:T(8,128)(2,1)S(1)} collective-permute-done((bf16[128,2048]{1,0:T(8,128)(2,1)S(1)}, bf16[128,2048]{1,0:T(8,128)(2,1)S(1)}, u32[]{:S(2)}, u32[]{:S(2)}) %collective-permute-start.10) | collective-permute-done | bytes 524320 | tf_op jit(solution)/shard_map/ppermute | solution.py:69
  166.2 4.7 %fusion.27 = bf16[128,2048]{1,0:T(8,128)(2,1)S(1)} fusion(f32[512,2048]{1,0:T(8,128)S(1)} %maximum_add_fusion, bf16[8192,2048]{1,0:T(8,128)(2,1)} %param.6, s32[]{:T(128)S(6)} %select_n.83, bf16[128,2048]{1,0:T(8,128)(2,1)S(1)} %collective-permute-done.10, pred[]{:T(512)S(6)} %or.3, bf16[512,2048]{1,0:T(8,128)(2,1)S(1)} %collective-permute-done.7), kind=kOutput, calls=%fused_computation.27 | convolution fusion | flops 1074528256 | bytes 11010053 | tf_op jit(solution)/shard_map/dot_general | solution.py:88
  171.0 5.9 %fusion.20 = bf16[256,2048]{1,0:T(8,128)(2,1)S(1)} fusion(f32[512,2048]{1,0:T(8,128)S(1)} %maximum_add_fusion, bf16[8192,2048]{1,0:T(8,128)(2,1)} %param.6, s32[]{:T(128)S(6)} %select_n.83, bf16[256,2048]{1,0:T(8,128)(2,1)S(1)} %collective-permute-done.8, pred[]{:T(512)S(6)} %or.3, bf16[512,2048]{1,0:T(8,128)(2,1)S(1)} %collective-permute-done.7), kind=kOutput, calls=%fused_computation.16 | convolution fusion | flops 2149056512 | bytes 13631493 | tf_op jit(solution)/shard_map/dot_general | solution.py:88
  176.8 1.5 pad_maximum_fusion
  (22 shorter events, 1.9 us)
Async XLA Ops:
  0.0 75.3 %copy-start = (bf16[4,64,2048]{2,1,0:T(8,128)(2,1)S(1)}, bf16[4,64,2048]{2,1,0:T(8,128)(2,1)}, u32[]{:S(2)}) copy-start(bf16[4,64,2048]{2,1,0:T(8,128)(2,1)} %param.8) | copy-start | bytes 3145732
  0.0 62.7 %collective-permute-start.1 = (bf16[512,2048]{1,0:T(8,128)(2,1)}, bf16[512,2048]{1,0:T(8,128)(2,1)}, u32[]{:S(2)}, u32[]{:S(2)}) collective-permute-start(bf16[512,2048]{1,0:T(8,128)(2,1)} %bitcast.43), channel_id=1, source_target_pairs={{0,4},{12,8},{1,5},{13,9},{2,6},{14,10},{3,7},{15,11},{16,20},{28,... | collective-permute-start | bytes 6291464 | tf_op jit(solution)/shard_map/ppermute | solution.py:69
  6.4 67.6 %collective-permute-start.2 = (bf16[512,2048]{1,0:T(8,128)(2,1)}, bf16[512,2048]{1,0:T(8,128)(2,1)}, u32[]{:S(2)}, u32[]{:S(2)}) collective-permute-start(bf16[512,2048]{1,0:T(8,128)(2,1)} %bitcast.44), channel_id=1, source_target_pairs={{4,8},{8,4},{5,9},{9,5},{6,10},{10,6},{7,11},{11,7},{20,24},{24,20... | collective-permute-start | bytes 6291464 | tf_op jit(solution)/shard_map/ppermute | solution.py:69
  17.2 34.4 %collective-permute-start.4 = (bf16[512,64]{0,1:T(8,128)(2,1)S(1)}, bf16[512,64]{0,1:T(8,128)(2,1)S(1)}, u32[]{:S(2)}, u32[]{:S(2)}) collective-permute-start(bf16[512,64]{0,1:T(8,128)(2,1)S(1)} %get-tuple-element.12), channel_id=1, source_target_pairs={{0,4},{12,8},{4,0},{8,12},{1,5},{13,9},{5,1},{9,13},{2,6},{14,10},... | collective-permute-start | bytes 196616 | tf_op jit(solution)/shard_map/ppermute | solution.py:69
  17.2 59.0 %collective-permute-start = (bf16[512,2048]{1,0:T(8,128)(2,1)}, bf16[512,2048]{1,0:T(8,128)(2,1)}, u32[]{:S(2)}, u32[]{:S(2)}) collective-permute-start(bf16[512,2048]{1,0:T(8,128)(2,1)} %bitcast.45), channel_id=1, source_target_pairs={{4,0},{8,12},{5,1},{9,13},{6,2},{10,14},{7,3},{11,15},{20,16},{24,... | collective-permute-start | bytes 6291464 | tf_op jit(solution)/shard_map/ppermute | solution.py:69
  51.6 12.0 %collective-permute-start.5 = (bf16[2,512,64]{1,2,0:T(8,128)(2,1)S(1)}, bf16[2,512,64]{1,2,0:T(8,128)(2,1)S(1)}, u32[]{:S(2)}, u32[]{:S(2)}) collective-permute-start(bf16[2,512,64]{1,2,0:T(8,128)(2,1)S(1)} %pad_maximum_fusion.1), channel_id=1, source_target_pairs={{4,8},{8,4},{5,9},{9,5},{6,10},{10,6},{7,11},{11,7},{20,24},{24,20... | collective-permute-start | bytes 393224 | tf_op jit(solution)/shard_map/ppermute | solution.py:69
  62.7 24.0 %collective-permute-start.7 = (bf16[512,2048]{1,0:T(8,128)(2,1)}, bf16[512,2048]{1,0:T(8,128)(2,1)S(1)}, u32[]{:S(2)}, u32[]{:S(2)}) collective-permute-start(bf16[512,2048]{1,0:T(8,128)(2,1)} %collective-permute-done.1), channel_id=1, source_target_pairs={{4,8},{8,4},{5,9},{9,5},{6,10},{10,6},{7,11},{11,7},{20,24},{24,20... | collective-permute-start | bytes 6291464 | tf_op jit(solution)/shard_map/ppermute | solution.py:69
  63.6 10.4 %collective-permute-start.6 = (bf16[512,64]{0,1:T(8,128)(2,1)S(1)}, bf16[512,64]{0,1:T(8,128)(2,1)S(1)}, u32[]{:S(2)}, u32[]{:S(2)}) collective-permute-start(bf16[512,64]{0,1:T(8,128)(2,1)S(1)} %fusion.61), channel_id=1, source_target_pairs={{4,0},{8,12},{5,1},{9,13},{6,2},{10,14},{7,3},{11,15},{20,16},{24,... | collective-permute-start | bytes 196616 | tf_op jit(solution)/shard_map/ppermute | solution.py:69
  64.9 11.3 %copy-start.2 = (f32[512,2048]{1,0:T(8,128)S(1)}, f32[512,2048]{1,0:T(8,128)}, u32[]{:S(2)}) copy-start(f32[512,2048]{1,0:T(8,128)} %fusion.12) | copy-start | bytes 12582916
  74.0 50.7 %collective-permute-start.3 = (bf16[512,2048]{1,0:T(8,128)(2,1)}, bf16[512,2048]{1,0:T(8,128)(2,1)S(1)}, u32[]{:S(2)}, u32[]{:S(2)}) collective-permute-start(bf16[512,2048]{1,0:T(8,128)(2,1)} %collective-permute-done.2), channel_id=1, source_target_pairs={{4,0},{8,12},{5,1},{9,13},{6,2},{10,14},{7,3},{11,15},{20,16},{24,... | collective-permute-start | bytes 6291464 | tf_op jit(solution)/shard_map/ppermute | solution.py:69
  86.8 84.1 %collective-permute-start.8 = (bf16[256,2048]{1,0:T(8,128)(2,1)S(1)}, bf16[256,2048]{1,0:T(8,128)(2,1)S(1)}, u32[]{:S(2)}, u32[]{:S(2)}) collective-permute-start(bf16[256,2048]{1,0:T(8,128)(2,1)S(1)} %slice.58), channel_id=1, source_target_pairs={{4,0},{8,12},{5,1},{9,13},{6,2},{10,14},{7,3},{11,15},{20,16},{24,... | collective-permute-start | bytes 3145736 | tf_op jit(solution)/shard_map/ppermute | solution.py:69
  88.2 70.2 %collective-permute-start.9 = (bf16[128,2048]{1,0:T(8,128)(2,1)S(1)}, bf16[128,2048]{1,0:T(8,128)(2,1)S(1)}, u32[]{:S(2)}, u32[]{:S(2)}) collective-permute-start(bf16[128,2048]{1,0:T(8,128)(2,1)S(1)} %get-tuple-element.9), channel_id=1, source_target_pairs={{4,0},{8,12},{5,1},{9,13},{6,2},{10,14},{7,3},{11,15},{20,16},{24,... | collective-permute-start | bytes 1572872 | tf_op jit(solution)/shard_map/ppermute | solution.py:69
  89.5 76.7 %collective-permute-start.10 = (bf16[128,2048]{1,0:T(8,128)(2,1)S(1)}, bf16[128,2048]{1,0:T(8,128)(2,1)S(1)}, u32[]{:S(2)}, u32[]{:S(2)}) collective-permute-start(bf16[128,2048]{1,0:T(8,128)(2,1)S(1)} %get-tuple-element.10), channel_id=1, source_target_pairs={{4,0},{8,12},{5,1},{9,13},{6,2},{10,14},{7,3},{11,15},{20,16},{24,... | collective-permute-start | bytes 1572872 | tf_op jit(solution)/shard_map/ppermute | solution.py:69
  170.9 7.3 %copy-start.1 = (bf16[4,64,2048]{2,1,0:T(8,128)(2,1)S(1)}, bf16[4,64,2048]{2,1,0:T(8,128)(2,1)}, u32[]{:S(2)}) copy-start(bf16[4,64,2048]{2,1,0:T(8,128)(2,1)} %param.8) | copy-start | bytes 3145732

commit v6 on v5

--- a/solution.py
+++ b/solution.py
@@ -81,38 +81,44 @@
     far_mid = jnp.where(here < 2, 2, 1)
     far_end = jnp.where(here < 2, 3, 0)
     own = inputs.reshape(rows, width)
-    cuts = [slice(0, rows // 2), slice(rows // 2, 3 * rows // 4), slice(3 * rows // 4, rows)]
+    half, last = width // 2, width // 8
 
-    def product(block, owner):
-        part = lax.dynamic_slice_in_dim(base_weight, owner * width, width, axis=0)
+    def product(block, owner, first=0):
+        part = lax.dynamic_slice_in_dim(base_weight, owner * width + first, block.shape[1], axis=0)
         return jnp.dot(block, part, preferred_element_type=F32)
 
     mate_out = send(own, OUTWARD)
     mate_in = send(own, INWARD)
-    across_own = send(own, ACROSS)
+    mid = [send(own[:, :half], ACROSS), send(own[:, half:], ACROSS)]
     partial = shrink(inputs, shrink_table, adapter_ids)
     mate_partial = send(partial, SWAP)
     total = product(own, here)
 
-    mate_in = after(mate_in, total)
-    across_mate = send(mate_in, ACROSS)
-    mid_out = send(across_own, OUTWARD)
+    mid_out = [send(after(mid[0], total), OUTWARD)]
+    mate_in, mate_partial = lax.optimization_barrier((mate_in, mate_partial, mid[0], total))[:2]
     both = send(jnp.stack([partial, mate_partial]), ACROSS)
+    end = [send(mate_in[:, :half], ACROSS), send(mate_in[:, half:], ACROSS)]
+    mid_out.append(send(mid[1], OUTWARD))
     total = total + product(jnp.where(is_end, mate_out, mate_in), here ^ 1)
 
-    across_mate = after(across_mate, total)
-    end_out = [send(across_mate[cut], OUTWARD) for cut in cuts]
+    end[0], both = lax.optimization_barrier((end[0], both, total))[:2]
+    end_out = [send(end[0], OUTWARD)]
     shrunk = (
         partial.astype(F32) + mate_partial.astype(F32) + both[0].astype(F32) + both[1].astype(F32)
     ).astype(BF16)
     shrunk = jnp.where(is_end, send(shrunk, OUTWARD), shrunk)
-    total = total + product(jnp.where(is_end, mid_out, across_own), far_mid)
+    total = total + product(jnp.where(is_end, mid_out[0], mid[0]), far_mid)
+
+    late = after(end[1], total)
+    end_out += [send(late[:, : half - last], OUTWARD), send(late[:, half - last :], OUTWARD)]
+    total = total + product(jnp.where(is_end, mid_out[1], mid[1]), far_mid, half)
     total = total + jnp.concatenate(expand(shrunk, expand_table, adapter_ids))
-    outs = [
-        total[cut] + product(jnp.where(is_end, out, across_mate[cut]), far_end)
-        for cut, out in zip(cuts, end_out)
-    ]
-    return jnp.concatenate([o.astype(BF16) for o in outs]).reshape(chats, span, -1)
+    total = total + product(jnp.where(is_end, end_out[0], end[0]), far_end)
+    block = jnp.where(is_end, after(end_out[1], total), late[:, : half - last])
+    total = total + product(block, far_end, half)
+    block = jnp.where(is_end, after(end_out[2], total), late[:, half - last :])
+    total = total + product(block, far_end, width - last)
+    return total.astype(BF16).reshape(chats, span, -1)
 
 
 def solution(mesh):

time: 179 us -> 173 us (0.966)
  starting transfers between devices: 17.9 us -> 28.1 us
  waiting for transfers between devices: 103 us -> 93.6 us
  matrix products: 50 us -> 41.3 us
  local copies, waits for them, and re-layouts: 1.49 us -> 5.48 us
    ppermute x11 -> x14, starting transfers between devices: 17.9 us -> 28.1 us  [send(): return lax.ppermute(block, 'tensor', pairs)]
    ppermute x11 -> x14, waiting for transfers between devices: 103 us -> 93.6 us  [send(): return lax.ppermute(block, 'tensor', pairs)]
    dot_general x6 -> x7, matrix products: 45.5 us -> 37.7 us  [product(): return jnp.dot(block, part, preferred_element_type=F32)]
    slice x2 -> x4, local copies, waits for them, and re-layouts: 0.14 us -> 4.85 us  [the longest x1 3.03 us: line(): mid = [send(own[:, :half], ACROSS), send(own[:, half:], ACROSS)]]
  transfers between devices with their start and end apart: 11 -> 14, of which waited for: 5 -> 5; matrix products, arithmetic and copies ran while one was open for 26% -> 25% of each run, Pallas kernels for 0% -> 0%
where the time goes in v6:
time: 173 us
  waiting for transfers between devices  93.6 us (54%)
  matrix products  41.3 us (24%)
  starting transfers between devices  28.1 us (16%)
  local copies, waits for them, and re-layouts  5.48 us (3%)
  between operations  4.01 us (2%)
    ppermute x14, waiting for transfers between devices, send(): return lax.ppermute(block, 'tensor', pairs)  93.6 us
    dot_general x7, matrix products, product(): return jnp.dot(block, part, preferred_element_type=F32)  37.7 us
    ppermute x14, starting transfers between devices, send(): return lax.ppermute(block, 'tensor', pairs)  28.1 us
  transfers between devices with their start and end apart: 14, of which 5 were waited for; matrix products, arithmetic and copies ran while one was open for 25% of the time, Pallas kernels for 0%

profile of v6, /device:TPU:0, one launch (start us, length us, event | category | flops | bytes accessed | tf_op | source)
XLA Modules:
  0.0 172.6 jit_solution(9564191782596775492)
XLA Ops:
  0.0 6.6 %collective-permute-start.1 = (bf16[512,2048]{1,0:T(8,128)(2,1)}, bf16[512,2048]{1,0:T(8,128)(2,1)}, u32[]{:S(2)}, u32[]{:S(2)}) collective-permute-start(bf16[512,2048]{1,0:T(8,128)(2,1)} %bitcast.38), channel_id=1, source_target_pairs={{0,4},{12,8},{1,5},{13,9},{2,6},{14,10},{3,7},{15,11},{16,20},{28,... | collective-permute-start | bytes 6291464 | tf_op jit(solution)/shard_map/ppermute | solution.py:69
  7.8 3.0 %fusion.74 = (bf16[512,1024]{1,0:T(8,128)(2,1)}, bf16[512,1024]{1,0:T(8,128)(2,1)}) fusion(bf16[512,2048]{1,0:T(8,128)(2,1)} %bitcast.40), kind=kLoop, calls=%fused_computation.73 | loop fusion | bytes 4194304 | tf_op jit(solution)/shard_map/slice | solution.py:92
  10.9 1.7 %collective-permute-start.5 = (bf16[512,1024]{1,0:T(8,128)(2,1)}, bf16[512,1024]{1,0:T(8,128)(2,1)}, u32[]{:S(2)}, u32[]{:S(2)}) collective-permute-start(bf16[512,1024]{1,0:T(8,128)(2,1)} %get-tuple-element.23), channel_id=1, source_target_pairs={{4,8},{8,4},{5,9},{9,5},{6,10},{10,6},{7,11},{11,7},{20,24},{24,20... | collective-permute-start | bytes 3145736 | tf_op jit(solution)/shard_map/ppermute | solution.py:69
  12.6 1.6 collective-permute-start.3
  18.6 1.4 fusion.29
  20.0 1.4 fusion.30
  21.5 6.6 %collective-permute-start.2 = (bf16[512,64]{0,1:T(8,128)(2,1)S(1)}, bf16[512,64]{0,1:T(8,128)(2,1)S(1)}, u32[]{:S(2)}, u32[]{:S(2)}) collective-permute-start(bf16[512,64]{0,1:T(8,128)(2,1)S(1)} %get-tuple-element.26), channel_id=1, source_target_pairs={{0,4},{12,8},{4,0},{8,12},{1,5},{13,9},{5,1},{9,13},{2,6},{14,10},... | collective-permute-start | bytes 196616 | tf_op jit(solution)/shard_map/ppermute | solution.py:69
  28.0 9.4 %fusion.11 = f32[512,2048]{1,0:T(8,128)} fusion(bf16[512,2048]{1,0:T(8,128)(2,1)S(1)} %bitcast.41, bf16[8192,2048]{1,0:T(8,128)(2,1)} %param.6, s32[]{:T(128)S(6)} %select_n.84), kind=kOutput, calls=%fused_computation.13 | convolution fusion | flops 4294967296 | bytes 14680068 | tf_op jit(solution)/shard_map/dot_general | solution.py:88
  37.4 1.5 collective-permute-start.4
  38.9 1.3 collective-permute-start.6
  40.2 16.9 %collective-permute-done.2 = bf16[512,64]{0,1:T(8,128)(2,1)S(1)} collective-permute-done((bf16[512,64]{0,1:T(8,128)(2,1)S(1)}, bf16[512,64]{0,1:T(8,128)(2,1)S(1)}, u32[]{:S(2)}, u32[]{:S(2)}) %collective-permute-start.2) | collective-permute-done | bytes 65568 | tf_op jit(solution)/shard_map/ppermute | solution.py:69
  57.8 1.7 fusion.73
  61.1 7.6 %fusion.16 = f32[512,2048]{1,0:T(8,128)S(1)} fusion(f32[512,2048]{1,0:T(8,128)S(1)} %copy-done.3, bf16[8192,2048]{1,0:T(8,128)(2,1)} %param.6, s32[]{:T(128)S(6)} %select_n.89, bf16[512,2048]{1,0:T(8,128)(2,1)} %collective-permute-done, bf16[512,2048]{1,0:T(8,128)(2,1)} %collective-permute-done.1, pred[]{:T(512)S(6)} %or.3), kind=kOutput, calls=%fused_computation.16 | convolution fusion | flops 4297064448 | bytes 20971524 | tf_op jit(solution)/shard_map/dot_general | solution.py:88
  68.8 1.3 collective-permute-start.9
  71.4 18.1 %collective-permute-done.4 = bf16[512,1024]{1,0:T(8,128)(2,1)S(1)} collective-permute-done((bf16[512,1024]{1,0:T(8,128)(2,1)}, bf16[512,1024]{1,0:T(8,128)(2,1)S(1)}, u32[]{:S(2)}, u32[]{:S(2)}) %collective-permute-start.4) | collective-permute-done | bytes 1048608 | tf_op jit(solution)/shard_map/ppermute | solution.py:69
  89.4 4.5 %fusion.22 = f32[512,2048]{1,0:T(8,128)S(1)} fusion(f32[512,2048]{1,0:T(8,128)S(1)} %fusion.16, bf16[8192,2048]{1,0:T(8,128)(2,1)} %param.6, s32[]{:T(128)S(6)} %select_n.93, bf16[512,1024]{1,0:T(8,128)(2,1)S(1)} %collective-permute-done.4, bf16[512,1024]{1,0:T(8,128)(2,1)} %collective-permute-done.3, pred[]{:T(512)S(6)} %or.3), kind=kOutput, calls=%fused_computation.18 | convolution fusion | flops 2149056512 | bytes 14680069 | tf_op jit(solution)/shard_map/dot_general | solution.py:88
  95.4 1.5 collective-permute-start.12
  96.9 26.8 %collective-permute-done.9 = bf16[512,64]{0,1:T(8,128)(2,1)S(1)} collective-permute-done((bf16[512,64]{0,1:T(8,128)(2,1)S(1)}, bf16[512,64]{0,1:T(8,128)(2,1)S(1)}, u32[]{:S(2)}, u32[]{:S(2)}) %collective-permute-start.9) | collective-permute-done | bytes 65568 | tf_op jit(solution)/shard_map/ppermute | solution.py:69
  124.6 21.5 %collective-permute-done.10 = bf16[512,1024]{1,0:T(8,128)(2,1)S(1)} collective-permute-done((bf16[512,1024]{1,0:T(8,128)(2,1)S(1)}, bf16[512,1024]{1,0:T(8,128)(2,1)S(1)}, u32[]{:S(2)}, u32[]{:S(2)}) %collective-permute-start.10) | collective-permute-done | bytes 1048608 | tf_op jit(solution)/shard_map/ppermute | solution.py:69
  146.2 4.5 %fusion.5 = f32[512,2048]{1,0:T(8,128)S(1)} fusion(bf16[8192,2048]{1,0:T(8,128)(2,1)} %param.6, s32[]{:T(128)S(6)} %select_n.100, bf16[512,1024]{1,0:T(8,128)(2,1)S(1)} %collective-permute-done.10, bf16[512,1024]{1,0:T(8,128)(2,1)S(1)} %collective-permute-done.7, pred[]{:T(512)S(6)} %or.3), kind=kOutput, calls=%fused_computation.7 | convolution fusion | flops 2148007936 | bytes 10485765 | tf_op jit(solution)/shard_map/dot_general | solution.py:88
  150.7 4.7 %fusion.4 = f32[512,2048]{1,0:T(8,128)S(1)} fusion(f32[512,2048]{1,0:T(8,128)S(1)} %fusion.5, f32[256,2048]{1,0:T(8,128)S(1)} %fusion.44, f32[256,2048]{1,0:T(8,128)S(1)} %fusion.46, f32[512,2048]{1,0:T(8,128)S(1)} %fusion.22, bf16[8192,2048]{1,0:T(8,128)(2,1)} %param.6, s32[]{:T(128)S(6)} %select_n.95, bf16[512,1024]{1,0:T(8,128)(2,1)S(1)} %collective-permute-done.6, ...), kind=kOutput, calls=%fused_computation.5 | convolution fusion | flops 2152202240 | bytes 23068676 | tf_op jit(solution)/shard_map/dot_general | solution.py:88
  155.4 10.3 %collective-permute-done.12 = bf16[512,768]{1,0:T(8,128)(2,1)S(1)} collective-permute-done((bf16[512,768]{1,0:T(8,128)(2,1)S(1)}, bf16[512,768]{1,0:T(8,128)(2,1)S(1)}, u32[]{:S(2)}, u32[]{:S(2)}) %collective-permute-start.12) | collective-permute-done | bytes 786464 | tf_op jit(solution)/shard_map/ppermute | solution.py:69
  165.6 3.7 %fusion.19 = f32[512,2048]{1,0:T(8,128)S(1)} fusion(f32[512,2048]{1,0:T(8,128)S(1)} %fusion.4, bf16[8192,2048]{1,0:T(8,128)(2,1)} %param.6, s32[]{:T(128)S(6)} %select_n.103, bf16[512,768]{1,0:T(8,128)(2,1)S(1)} %collective-permute-done.12, pred[]{:T(512)S(6)} %or.3, bf16[512,1024]{1,0:T(8,128)(2,1)S(1)} %collective-permute-done.11), kind=kOutput, calls=%fused_computation.17 | convolution fusion | flops 1612054528 | bytes 13107205 | tf_op jit(solution)/shard_map/dot_general | solution.py:88
  169.3 3.3 %add_convert_fusion = bf16[512,2048]{1,0:T(8,128)(2,1)} fusion(f32[512,2048]{1,0:T(8,128)S(1)} %fusion.19, bf16[8192,2048]{1,0:T(8,128)(2,1)} %param.6, s32[]{:T(128)S(6)} %select_n.106, bf16[512,256]{1,0:T(8,128)(2,1)S(1)} %collective-permute-done.13, pred[]{:T(512)S(6)} %or.3, bf16[512,1024]{1,0:T(8,128)(2,1)S(1)} %collective-permute-done.11), kind=kOutput, calls=%fused_computation.6 | convolution fusion | flops 539099136 | bytes 7864325 | tf_op jit(solution)/shard_map/dot_general | solution.py:88
  (32 shorter events, 7.7 us)
Async XLA Ops:
  0.0 123.7 %copy-start = (bf16[4,64,2048]{2,1,0:T(8,128)(2,1)S(1)}, bf16[4,64,2048]{2,1,0:T(8,128)(2,1)}, u32[]{:S(2)}) copy-start(bf16[4,64,2048]{2,1,0:T(8,128)(2,1)} %param.8) | copy-start | bytes 3145732
  0.0 18.6 %copy-start.1 = (bf16[2,256,2048]{2,1,0:T(8,128)(2,1)S(1)}, bf16[2,256,2048]{2,1,0:T(8,128)(2,1)}, u32[]{:S(2)}) copy-start(bf16[2,256,2048]{2,1,0:T(8,128)(2,1)} %param.5) | copy-start | bytes 6291460
  0.0 14.3 %copy-start.2 = (s32[2]{0:T(128)S(1)}, s32[2]{0:T(128)}, u32[]{:S(2)}) copy-start(s32[2]{0:T(128)} %param.9) | copy-start | bytes 28
  0.0 57.1 %collective-permute-start.1 = (bf16[512,2048]{1,0:T(8,128)(2,1)}, bf16[512,2048]{1,0:T(8,128)(2,1)}, u32[]{:S(2)}, u32[]{:S(2)}) collective-permute-start(bf16[512,2048]{1,0:T(8,128)(2,1)} %bitcast.38), channel_id=1, source_target_pairs={{0,4},{12,8},{1,5},{13,9},{2,6},{14,10},{3,7},{15,11},{16,20},{28,... | collective-permute-start | bytes 6291464 | tf_op jit(solution)/shard_map/ppermute | solution.py:69
  6.6 53.7 %collective-permute-start = (bf16[512,2048]{1,0:T(8,128)(2,1)}, bf16[512,2048]{1,0:T(8,128)(2,1)}, u32[]{:S(2)}, u32[]{:S(2)}) collective-permute-start(bf16[512,2048]{1,0:T(8,128)(2,1)} %bitcast.39), channel_id=1, source_target_pairs={{4,0},{8,12},{5,1},{9,13},{6,2},{10,14},{7,3},{11,15},{20,16},{24,... | collective-permute-start | bytes 6291464 | tf_op jit(solution)/shard_map/ppermute | solution.py:69
  10.9 28.1 %collective-permute-start.5 = (bf16[512,1024]{1,0:T(8,128)(2,1)}, bf16[512,1024]{1,0:T(8,128)(2,1)}, u32[]{:S(2)}, u32[]{:S(2)}) collective-permute-start(bf16[512,1024]{1,0:T(8,128)(2,1)} %get-tuple-element.23), channel_id=1, source_target_pairs={{4,8},{8,4},{5,9},{9,5},{6,10},{10,6},{7,11},{11,7},{20,24},{24,20... | collective-permute-start | bytes 3145736 | tf_op jit(solution)/shard_map/ppermute | solution.py:69
  12.6 24.8 %collective-permute-start.3 = (bf16[512,1024]{1,0:T(8,128)(2,1)}, bf16[512,1024]{1,0:T(8,128)(2,1)}, u32[]{:S(2)}, u32[]{:S(2)}) collective-permute-start(bf16[512,1024]{1,0:T(8,128)(2,1)} %get-tuple-element.24), channel_id=1, source_target_pairs={{4,8},{8,4},{5,9},{9,5},{6,10},{10,6},{7,11},{11,7},{20,24},{24,20... | collective-permute-start | bytes 3145736 | tf_op jit(solution)/shard_map/ppermute | solution.py:69
  21.5 35.7 %collective-permute-start.2 = (bf16[512,64]{0,1:T(8,128)(2,1)S(1)}, bf16[512,64]{0,1:T(8,128)(2,1)S(1)}, u32[]{:S(2)}, u32[]{:S(2)}) collective-permute-start(bf16[512,64]{0,1:T(8,128)(2,1)S(1)} %get-tuple-element.26), channel_id=1, source_target_pairs={{0,4},{12,8},{4,0},{8,12},{1,5},{13,9},{5,1},{9,13},{2,6},{14,10},... | collective-permute-start | bytes 196616 | tf_op jit(solution)/shard_map/ppermute | solution.py:69
  37.4 23.7 %copy-start.3 = (f32[512,2048]{1,0:T(8,128)S(1)}, f32[512,2048]{1,0:T(8,128)}, u32[]{:S(2)}) copy-start(f32[512,2048]{1,0:T(8,128)} %fusion.11) | copy-start | bytes 12582916
  37.4 52.1 %collective-permute-start.4 = (bf16[512,1024]{1,0:T(8,128)(2,1)}, bf16[512,1024]{1,0:T(8,128)(2,1)S(1)}, u32[]{:S(2)}, u32[]{:S(2)}) collective-permute-start(bf16[512,1024]{1,0:T(8,128)(2,1)} %collective-permute-done.3), channel_id=1, source_target_pairs={{4,0},{8,12},{5,1},{9,13},{6,2},{10,14},{7,3},{11,15},{20,16},{24,... | collective-permute-start | bytes 3145736 | tf_op jit(solution)/shard_map/ppermute | solution.py:69
  38.9 111.8 %collective-permute-start.6 = (bf16[512,1024]{1,0:T(8,128)(2,1)}, bf16[512,1024]{1,0:T(8,128)(2,1)S(1)}, u32[]{:S(2)}, u32[]{:S(2)}) collective-permute-start(bf16[512,1024]{1,0:T(8,128)(2,1)} %collective-permute-done.5), channel_id=1, source_target_pairs={{4,0},{8,12},{5,1},{9,13},{6,2},{10,14},{7,3},{11,15},{20,16},{24,... | collective-permute-start | bytes 3145736 | tf_op jit(solution)/shard_map/ppermute | solution.py:69
  57.2 11.5 %collective-permute-start.8 = (bf16[2,512,64]{1,2,0:T(8,128)(2,1)S(1)}, bf16[2,512,64]{1,2,0:T(8,128)(2,1)S(1)}, u32[]{:S(2)}, u32[]{:S(2)}) collective-permute-start(bf16[2,512,64]{1,2,0:T(8,128)(2,1)S(1)} %pad_maximum_fusion), channel_id=1, source_target_pairs={{4,8},{8,4},{5,9},{9,5},{6,10},{10,6},{7,11},{11,7},{20,24},{24,20... | collective-permute-start | bytes 393224 | tf_op jit(solution)/shard_map/ppermute | solution.py:69
  59.6 34.4 %collective-permute-start.11 = (bf16[512,1024]{1,0:T(8,128)(2,1)S(1)}, bf16[512,1024]{1,0:T(8,128)(2,1)S(1)}, u32[]{:S(2)}, u32[]{:S(2)}) collective-permute-start(bf16[512,1024]{1,0:T(8,128)(2,1)S(1)} %get-tuple-element.21), channel_id=1, source_target_pairs={{4,8},{8,4},{5,9},{9,5},{6,10},{10,6},{7,11},{11,7},{20,24},{24,20... | collective-permute-start | bytes 3145736 | tf_op jit(solution)/shard_map/ppermute | solution.py:69
  60.3 8.4 %collective-permute-start.7 = (bf16[512,1024]{1,0:T(8,128)(2,1)S(1)}, bf16[512,1024]{1,0:T(8,128)(2,1)S(1)}, u32[]{:S(2)}, u32[]{:S(2)}) collective-permute-start(bf16[512,1024]{1,0:T(8,128)(2,1)S(1)} %get-tuple-element.22), channel_id=1, source_target_pairs={{4,8},{8,4},{5,9},{9,5},{6,10},{10,6},{7,11},{11,7},{20,24},{24,20... | collective-permute-start | bytes 3145736 | tf_op jit(solution)/shard_map/ppermute | solution.py:69
  68.8 54.9 %collective-permute-start.9 = (bf16[512,64]{0,1:T(8,128)(2,1)S(1)}, bf16[512,64]{0,1:T(8,128)(2,1)S(1)}, u32[]{:S(2)}, u32[]{:S(2)}) collective-permute-start(bf16[512,64]{0,1:T(8,128)(2,1)S(1)} %fusion.56), channel_id=1, source_target_pairs={{4,0},{8,12},{5,1},{9,13},{6,2},{10,14},{7,3},{11,15},{20,16},{24,... | collective-permute-start | bytes 196616 | tf_op jit(solution)/shard_map/ppermute | solution.py:69
  70.1 76.1 %collective-permute-start.10 = (bf16[512,1024]{1,0:T(8,128)(2,1)S(1)}, bf16[512,1024]{1,0:T(8,128)(2,1)S(1)}, u32[]{:S(2)}, u32[]{:S(2)}) collective-permute-start(bf16[512,1024]{1,0:T(8,128)(2,1)S(1)} %collective-permute-done.7), channel_id=1, source_target_pairs={{4,0},{8,12},{5,1},{9,13},{6,2},{10,14},{7,3},{11,15},{20,16},{24,... | collective-permute-start | bytes 3145736 | tf_op jit(solution)/shard_map/ppermute | solution.py:69
  94.1 75.2 %collective-permute-start.13 = (bf16[512,256]{1,0:T(8,128)(2,1)S(1)}, bf16[512,256]{1,0:T(8,128)(2,1)S(1)}, u32[]{:S(2)}, u32[]{:S(2)}) collective-permute-start(bf16[512,256]{1,0:T(8,128)(2,1)S(1)} %slice.61), channel_id=1, source_target_pairs={{4,0},{8,12},{5,1},{9,13},{6,2},{10,14},{7,3},{11,15},{20,16},{24,... | collective-permute-start | bytes 786440 | tf_op jit(solution)/shard_map/ppermute | solution.py:69
  95.4 70.2 %collective-permute-start.12 = (bf16[512,768]{1,0:T(8,128)(2,1)S(1)}, bf16[512,768]{1,0:T(8,128)(2,1)S(1)}, u32[]{:S(2)}, u32[]{:S(2)}) collective-permute-start(bf16[512,768]{1,0:T(8,128)(2,1)S(1)} %slice.60), channel_id=1, source_target_pairs={{4,0},{8,12},{5,1},{9,13},{6,2},{10,14},{7,3},{11,15},{20,16},{24,... | collective-permute-start | bytes 2359304 | tf_op jit(solution)/shard_map/ppermute | solution.py:69

commit v7 on v6

--- a/solution.py
+++ b/solution.py
@@ -89,15 +89,17 @@
 
     mate_out = send(own, OUTWARD)
     mate_in = send(own, INWARD)
-    mid = [send(own[:, :half], ACROSS), send(own[:, half:], ACROSS)]
+    mid = [send(own[:, :half], ACROSS)]
+    mid.append(send(after(own[:, half:], mid[0]), ACROSS))
     partial = shrink(inputs, shrink_table, adapter_ids)
     mate_partial = send(partial, SWAP)
     total = product(own, here)
 
     mid_out = [send(after(mid[0], total), OUTWARD)]
-    mate_in, mate_partial = lax.optimization_barrier((mate_in, mate_partial, mid[0], total))[:2]
+    mate_in, mate_partial = lax.optimization_barrier((mate_in, mate_partial, mid[1], total))[:2]
     both = send(jnp.stack([partial, mate_partial]), ACROSS)
-    end = [send(mate_in[:, :half], ACROSS), send(mate_in[:, half:], ACROSS)]
+    end = [send(mate_in[:, :half], ACROSS)]
+    end.append(send(after(mate_in[:, half:], end[0]), ACROSS))
     mid_out.append(send(mid[1], OUTWARD))
     total = total + product(jnp.where(is_end, mate_out, mate_in), here ^ 1)
 
@@ -110,6 +112,7 @@
     total = total + product(jnp.where(is_end, mid_out[0], mid[0]), far_mid)
 
     late = after(end[1], total)
+    shrunk = after(shrunk, late)
     end_out += [send(late[:, : half - last], OUTWARD), send(late[:, half - last :], OUTWARD)]
     total = total + product(jnp.where(is_end, mid_out[1], mid[1]), far_mid, half)
     total = total + jnp.concatenate(expand(shrunk, expand_table, adapter_ids))

time: 173 us -> 158 us (0.913)
  waiting for transfers between devices: 93.6 us -> 68.4 us
  starting transfers between devices: 28.1 us -> 38.2 us
    ppermute x14, waiting for transfers between devices: 93.6 us -> 68.4 us  [send(): return lax.ppermute(block, 'tensor', pairs)]
    ppermute x14, starting transfers between devices: 28.1 us -> 38.2 us  [send(): return lax.ppermute(block, 'tensor', pairs)]
  transfers between devices with their start and end apart: 14 -> 14, of which waited for: 5 -> 6; matrix products, arithmetic and copies ran while one was open for 25% -> 26% of each run, Pallas kernels for 0% -> 0%
where the time goes in v7:
time: 158 us
  waiting for transfers between devices  68.4 us (43%)
  matrix products  41.3 us (26%)
  starting transfers between devices  38.2 us (24%)
  local copies, waits for them, and re-layouts  5.65 us (4%)
  between operations  4.01 us (3%)
    ppermute x14, waiting for transfers between devices, send(): return lax.ppermute(block, 'tensor', pairs)  68.4 us
    ppermute x14, starting transfers between devices, send(): return lax.ppermute(block, 'tensor', pairs)  38.2 us
    dot_general x7, matrix products, product(): return jnp.dot(block, part, preferred_element_type=F32)  37.6 us
    slice x1, local copies, waits for them, and re-layouts, line(): mid = [send(own[:, :half], ACROSS)]  3.2 us
  transfers between devices with their start and end apart: 14, of which 6 were waited for; matrix products, arithmetic and copies ran while one was open for 26% of the time, Pallas kernels for 0%

profile of v7, /device:TPU:0, one launch (start us, length us, event | category | flops | bytes accessed | tf_op | source)
XLA Modules:
  0.0 157.6 jit_solution(14526048526770867430)
XLA Ops:
  0.0 3.2 %fusion.74 = (bf16[512,1024]{1,0:T(8,128)(2,1)}, bf16[512,1024]{1,0:T(8,128)(2,1)}) fusion(bf16[512,2048]{1,0:T(8,128)(2,1)} %bitcast.38), kind=kLoop, calls=%fused_computation.73 | loop fusion | bytes 4194304 | tf_op jit(solution)/shard_map/slice | solution.py:92
  3.2 1.7 %collective-permute-start.3 = (bf16[512,1024]{1,0:T(8,128)(2,1)}, bf16[512,1024]{1,0:T(8,128)(2,1)}, u32[]{:S(2)}, u32[]{:S(2)}) collective-permute-start(bf16[512,1024]{1,0:T(8,128)(2,1)} %get-tuple-element.29), channel_id=1, source_target_pairs={{4,8},{8,4},{5,9},{9,5},{6,10},{10,6},{7,11},{11,7},{20,24},{24,20... | collective-permute-start | bytes 3145736 | tf_op jit(solution)/shard_map/ppermute | solution.py:69
  4.9 8.1 %collective-permute-start.1 = (bf16[512,2048]{1,0:T(8,128)(2,1)S(1)}, bf16[512,2048]{1,0:T(8,128)(2,1)}, u32[]{:S(2)}, u32[]{:S(2)}) collective-permute-start(bf16[512,2048]{1,0:T(8,128)(2,1)S(1)} %bitcast.39), channel_id=1, source_target_pairs={{0,4},{12,8},{1,5},{13,9},{2,6},{14,10},{3,7},{15,11},{16,20},{28,... | collective-permute-start | bytes 6291464 | tf_op jit(solution)/shard_map/ppermute | solution.py:69
  18.7 1.4 fusion.29
  20.1 1.6 %collective-permute-start.4 = (bf16[512,1024]{1,0:T(8,128)(2,1)}, bf16[512,1024]{1,0:T(8,128)(2,1)}, u32[]{:S(2)}, u32[]{:S(2)}) collective-permute-start(bf16[512,1024]{1,0:T(8,128)(2,1)} %get-tuple-element.16), channel_id=1, source_target_pairs={{4,8},{8,4},{5,9},{9,5},{6,10},{10,6},{7,11},{11,7},{20,24},{24,20... | collective-permute-start | bytes 3145736 | tf_op jit(solution)/shard_map/ppermute | solution.py:69
  21.7 1.4 fusion.30
  23.1 15.2 %collective-permute-start.2 = (bf16[512,64]{0,1:T(8,128)(2,1)S(1)}, bf16[512,64]{0,1:T(8,128)(2,1)S(1)}, u32[]{:S(2)}, u32[]{:S(2)}) collective-permute-start(bf16[512,64]{0,1:T(8,128)(2,1)S(1)} %get-tuple-element.32), channel_id=1, source_target_pairs={{0,4},{12,8},{4,0},{8,12},{1,5},{13,9},{5,1},{9,13},{2,6},{14,10},... | collective-permute-start | bytes 196616 | tf_op jit(solution)/shard_map/ppermute | solution.py:69
  38.3 9.4 %fusion.11 = f32[512,2048]{1,0:T(8,128)} fusion(bf16[512,2048]{1,0:T(8,128)(2,1)S(1)} %bitcast.41, bf16[8192,2048]{1,0:T(8,128)(2,1)} %param.6, s32[]{:T(128)S(6)} %select_n.84), kind=kOutput, calls=%fused_computation.13 | convolution fusion | flops 4294967296 | bytes 14680068 | tf_op jit(solution)/shard_map/dot_general | solution.py:88
  47.7 1.5 collective-permute-start.5
  49.2 15.6 %collective-permute-done.2 = bf16[512,64]{0,1:T(8,128)(2,1)S(1)} collective-permute-done((bf16[512,64]{0,1:T(8,128)(2,1)S(1)}, bf16[512,64]{0,1:T(8,128)(2,1)S(1)}, u32[]{:S(2)}, u32[]{:S(2)}) %collective-permute-start.2) | collective-permute-done | bytes 65568 | tf_op jit(solution)/shard_map/ppermute | solution.py:69
  64.9 1.7 %fusion.73 = (bf16[512,1024]{1,0:T(8,128)(2,1)S(1)}, bf16[512,1024]{1,0:T(8,128)(2,1)S(1)}) fusion(bf16[512,2048]{1,0:T(8,128)(2,1)} %collective-permute-done.1), kind=kLoop, calls=%fused_computation.72 | loop fusion | bytes 4194304 | tf_op jit(solution)/shard_map/slice | solution.py:102
  68.0 1.3 collective-permute-start.6
  69.3 7.6 %fusion.16 = f32[512,2048]{1,0:T(8,128)S(1)} fusion(f32[512,2048]{1,0:T(8,128)S(1)} %copy-done.3, bf16[8192,2048]{1,0:T(8,128)(2,1)} %param.6, s32[]{:T(128)S(6)} %select_n.89, bf16[512,2048]{1,0:T(8,128)(2,1)} %collective-permute-done, bf16[512,2048]{1,0:T(8,128)(2,1)} %collective-permute-done.1, pred[]{:T(512)S(6)} %or.3), kind=kOutput, calls=%fused_computation.16 | convolution fusion | flops 4297064448 | bytes 20971524 | tf_op jit(solution)/shard_map/dot_general | solution.py:88
  77.8 1.3 collective-permute-start.9
  80.4 7.0 %collective-permute-done.5 = bf16[512,1024]{1,0:T(8,128)(2,1)S(1)} collective-permute-done((bf16[512,1024]{1,0:T(8,128)(2,1)}, bf16[512,1024]{1,0:T(8,128)(2,1)S(1)}, u32[]{:S(2)}, u32[]{:S(2)}) %collective-permute-start.5) | collective-permute-done | bytes 1048608 | tf_op jit(solution)/shard_map/ppermute | solution.py:69
  87.3 4.5 %fusion.22 = f32[512,2048]{1,0:T(8,128)S(1)} fusion(f32[512,2048]{1,0:T(8,128)S(1)} %fusion.16, bf16[8192,2048]{1,0:T(8,128)(2,1)} %param.6, s32[]{:T(128)S(6)} %select_n.93, bf16[512,1024]{1,0:T(8,128)(2,1)S(1)} %collective-permute-done.5, bf16[512,1024]{1,0:T(8,128)(2,1)} %collective-permute-done.3, pred[]{:T(512)S(6)} %or.3), kind=kOutput, calls=%fused_computation.18 | convolution fusion | flops 2149056512 | bytes 14680069 | tf_op jit(solution)/shard_map/dot_general | solution.py:88
  91.9 19.3 %collective-permute-done.9 = bf16[512,64]{0,1:T(8,128)(2,1)S(1)} collective-permute-done((bf16[512,64]{0,1:T(8,128)(2,1)S(1)}, bf16[512,64]{0,1:T(8,128)(2,1)S(1)}, u32[]{:S(2)}, u32[]{:S(2)}) %collective-permute-start.9) | collective-permute-done | bytes 65568 | tf_op jit(solution)/shard_map/ppermute | solution.py:69
  112.6 1.5 collective-permute-start.13
  115.0 18.6 %collective-permute-done.11 = bf16[512,1024]{1,0:T(8,128)(2,1)S(1)} collective-permute-done((bf16[512,1024]{1,0:T(8,128)(2,1)S(1)}, bf16[512,1024]{1,0:T(8,128)(2,1)S(1)}, u32[]{:S(2)}, u32[]{:S(2)}) %collective-permute-start.11) | collective-permute-done | bytes 1048608 | tf_op jit(solution)/shard_map/ppermute | solution.py:69
  133.7 4.5 %fusion.5 = f32[512,2048]{1,0:T(8,128)S(1)} fusion(bf16[8192,2048]{1,0:T(8,128)(2,1)} %param.6, s32[]{:T(128)S(6)} %select_n.100, bf16[512,1024]{1,0:T(8,128)(2,1)S(1)} %collective-permute-done.11, bf16[512,1024]{1,0:T(8,128)(2,1)S(1)} %collective-permute-done.7, pred[]{:T(512)S(6)} %or.3), kind=kOutput, calls=%fused_computation.7 | convolution fusion | flops 2148007936 | bytes 10485765 | tf_op jit(solution)/shard_map/dot_general | solution.py:88
  138.2 4.7 %fusion.4 = f32[512,2048]{1,0:T(8,128)S(1)} fusion(f32[512,2048]{1,0:T(8,128)S(1)} %fusion.5, f32[256,2048]{1,0:T(8,128)S(1)} %fusion.44, f32[256,2048]{1,0:T(8,128)S(1)} %fusion.46, f32[512,2048]{1,0:T(8,128)S(1)} %fusion.22, bf16[8192,2048]{1,0:T(8,128)(2,1)} %param.6, s32[]{:T(128)S(6)} %select_n.95, bf16[512,1024]{1,0:T(8,128)(2,1)S(1)} %collective-permute-done.6, ...), kind=kOutput, calls=%fused_computation.5 | convolution fusion | flops 2152202240 | bytes 23068676 | tf_op jit(solution)/shard_map/dot_general | solution.py:88
  142.9 7.6 %collective-permute-done.12 = bf16[512,768]{1,0:T(8,128)(2,1)S(1)} collective-permute-done((bf16[512,768]{1,0:T(8,128)(2,1)S(1)}, bf16[512,768]{1,0:T(8,128)(2,1)S(1)}, u32[]{:S(2)}, u32[]{:S(2)}) %collective-permute-start.12) | collective-permute-done | bytes 786464 | tf_op jit(solution)/shard_map/ppermute | solution.py:69
  150.5 3.7 %fusion.19 = f32[512,2048]{1,0:T(8,128)S(1)} fusion(f32[512,2048]{1,0:T(8,128)S(1)} %fusion.4, bf16[8192,2048]{1,0:T(8,128)(2,1)} %param.6, s32[]{:T(128)S(6)} %select_n.103, bf16[512,768]{1,0:T(8,128)(2,1)S(1)} %collective-permute-done.12, pred[]{:T(512)S(6)} %or.3, bf16[512,1024]{1,0:T(8,128)(2,1)S(1)} %collective-permute-done.10), kind=kOutput, calls=%fused_computation.17 | convolution fusion | flops 1612054528 | bytes 13107205 | tf_op jit(solution)/shard_map/dot_general | solution.py:88
  154.4 3.3 %add_convert_fusion = bf16[512,2048]{1,0:T(8,128)(2,1)} fusion(f32[512,2048]{1,0:T(8,128)S(1)} %fusion.19, bf16[8192,2048]{1,0:T(8,128)(2,1)} %param.6, s32[]{:T(128)S(6)} %select_n.106, bf16[512,256]{1,0:T(8,128)(2,1)S(1)} %collective-permute-done.13, pred[]{:T(512)S(6)} %or.3, bf16[512,1024]{1,0:T(8,128)(2,1)S(1)} %collective-permute-done.10), kind=kOutput, calls=%fused_computation.6 | convolution fusion | flops 539099136 | bytes 7864325 | tf_op jit(solution)/shard_map/dot_general | solution.py:88
  (32 shorter events, 7.9 us)
Async XLA Ops:
  0.0 114.1 %copy-start = (bf16[4,64,2048]{2,1,0:T(8,128)(2,1)S(1)}, bf16[4,64,2048]{2,1,0:T(8,128)(2,1)}, u32[]{:S(2)}) copy-start(bf16[4,64,2048]{2,1,0:T(8,128)(2,1)} %param.8) | copy-start | bytes 3145732
  0.0 4.9 %copy-start.1 = (bf16[2,256,2048]{2,1,0:T(8,128)(2,1)S(1)}, bf16[2,256,2048]{2,1,0:T(8,128)(2,1)}, u32[]{:S(2)}) copy-start(bf16[2,256,2048]{2,1,0:T(8,128)(2,1)} %param.5) | copy-start | bytes 6291460
  0.0 14.3 %copy-start.2 = (s32[2]{0:T(128)S(1)}, s32[2]{0:T(128)}, u32[]{:S(2)}) copy-start(s32[2]{0:T(128)} %param.9) | copy-start | bytes 28
  3.2 16.9 %collective-permute-start.3 = (bf16[512,1024]{1,0:T(8,128)(2,1)}, bf16[512,1024]{1,0:T(8,128)(2,1)}, u32[]{:S(2)}, u32[]{:S(2)}) collective-permute-start(bf16[512,1024]{1,0:T(8,128)(2,1)} %get-tuple-element.29), channel_id=1, source_target_pairs={{4,8},{8,4},{5,9},{9,5},{6,10},{10,6},{7,11},{11,7},{20,24},{24,20... | collective-permute-start | bytes 3145736 | tf_op jit(solution)/shard_map/ppermute | solution.py:69
  4.9 59.9 %collective-permute-start.1 = (bf16[512,2048]{1,0:T(8,128)(2,1)S(1)}, bf16[512,2048]{1,0:T(8,128)(2,1)}, u32[]{:S(2)}, u32[]{:S(2)}) collective-permute-start(bf16[512,2048]{1,0:T(8,128)(2,1)S(1)} %bitcast.39), channel_id=1, source_target_pairs={{0,4},{12,8},{1,5},{13,9},{2,6},{14,10},{3,7},{15,11},{16,20},{28,... | collective-permute-start | bytes 6291464 | tf_op jit(solution)/shard_map/ppermute | solution.py:69
  13.0 56.3 %collective-permute-start = (bf16[512,2048]{1,0:T(8,128)(2,1)S(1)}, bf16[512,2048]{1,0:T(8,128)(2,1)}, u32[]{:S(2)}, u32[]{:S(2)}) collective-permute-start(bf16[512,2048]{1,0:T(8,128)(2,1)S(1)} %bitcast.40), channel_id=1, source_target_pairs={{4,0},{8,12},{5,1},{9,13},{6,2},{10,14},{7,3},{11,15},{20,16},{24,... | collective-permute-start | bytes 6291464 | tf_op jit(solution)/shard_map/ppermute | solution.py:69
  20.1 44.8 %collective-permute-start.4 = (bf16[512,1024]{1,0:T(8,128)(2,1)}, bf16[512,1024]{1,0:T(8,128)(2,1)}, u32[]{:S(2)}, u32[]{:S(2)}) collective-permute-start(bf16[512,1024]{1,0:T(8,128)(2,1)} %get-tuple-element.16), channel_id=1, source_target_pairs={{4,8},{8,4},{5,9},{9,5},{6,10},{10,6},{7,11},{11,7},{20,24},{24,20... | collective-permute-start | bytes 3145736 | tf_op jit(solution)/shard_map/ppermute | solution.py:69
  23.1 41.7 %collective-permute-start.2 = (bf16[512,64]{0,1:T(8,128)(2,1)S(1)}, bf16[512,64]{0,1:T(8,128)(2,1)S(1)}, u32[]{:S(2)}, u32[]{:S(2)}) collective-permute-start(bf16[512,64]{0,1:T(8,128)(2,1)S(1)} %get-tuple-element.32), channel_id=1, source_target_pairs={{0,4},{12,8},{4,0},{8,12},{1,5},{13,9},{5,1},{9,13},{2,6},{14,10},... | collective-permute-start | bytes 196616 | tf_op jit(solution)/shard_map/ppermute | solution.py:69
  47.7 21.7 %copy-start.3 = (f32[512,2048]{1,0:T(8,128)S(1)}, f32[512,2048]{1,0:T(8,128)}, u32[]{:S(2)}) copy-start(f32[512,2048]{1,0:T(8,128)} %fusion.11) | copy-start | bytes 12582916
  47.7 39.7 %collective-permute-start.5 = (bf16[512,1024]{1,0:T(8,128)(2,1)}, bf16[512,1024]{1,0:T(8,128)(2,1)S(1)}, u32[]{:S(2)}, u32[]{:S(2)}) collective-permute-start(bf16[512,1024]{1,0:T(8,128)(2,1)} %collective-permute-done.3), channel_id=1, source_target_pairs={{4,0},{8,12},{5,1},{9,13},{6,2},{10,14},{7,3},{11,15},{20,16},{24,... | collective-permute-start | bytes 3145736 | tf_op jit(solution)/shard_map/ppermute | solution.py:69
  66.6 10.4 %collective-permute-start.7 = (bf16[512,1024]{1,0:T(8,128)(2,1)S(1)}, bf16[512,1024]{1,0:T(8,128)(2,1)S(1)}, u32[]{:S(2)}, u32[]{:S(2)}) collective-permute-start(bf16[512,1024]{1,0:T(8,128)(2,1)S(1)} %get-tuple-element.28), channel_id=1, source_target_pairs={{4,8},{8,4},{5,9},{9,5},{6,10},{10,6},{7,11},{11,7},{20,24},{24,20... | collective-permute-start | bytes 3145736 | tf_op jit(solution)/shard_map/ppermute | solution.py:69
  67.3 10.4 %collective-permute-start.8 = (bf16[2,512,64]{1,2,0:T(8,128)(2,1)S(1)}, bf16[2,512,64]{1,2,0:T(8,128)(2,1)S(1)}, u32[]{:S(2)}, u32[]{:S(2)}) collective-permute-start(bf16[2,512,64]{1,2,0:T(8,128)(2,1)S(1)} %pad_maximum_fusion), channel_id=1, source_target_pairs={{4,8},{8,4},{5,9},{9,5},{6,10},{10,6},{7,11},{11,7},{20,24},{24,20... | collective-permute-start | bytes 393224 | tf_op jit(solution)/shard_map/ppermute | solution.py:69
  68.0 70.2 %collective-permute-start.6 = (bf16[512,1024]{1,0:T(8,128)(2,1)}, bf16[512,1024]{1,0:T(8,128)(2,1)S(1)}, u32[]{:S(2)}, u32[]{:S(2)}) collective-permute-start(bf16[512,1024]{1,0:T(8,128)(2,1)} %collective-permute-done.4), channel_id=1, source_target_pairs={{4,0},{8,12},{5,1},{9,13},{6,2},{10,14},{7,3},{11,15},{20,16},{24,... | collective-permute-start | bytes 3145736 | tf_op jit(solution)/shard_map/ppermute | solution.py:69
  77.0 34.2 %collective-permute-start.10 = (bf16[512,1024]{1,0:T(8,128)(2,1)S(1)}, bf16[512,1024]{1,0:T(8,128)(2,1)S(1)}, u32[]{:S(2)}, u32[]{:S(2)}) collective-permute-start(bf16[512,1024]{1,0:T(8,128)(2,1)S(1)} %get-tuple-element.21), channel_id=1, source_target_pairs={{4,8},{8,4},{5,9},{9,5},{6,10},{10,6},{7,11},{11,7},{20,24},{24,20... | collective-permute-start | bytes 3145736 | tf_op jit(solution)/shard_map/ppermute | solution.py:69
  77.8 33.4 %collective-permute-start.9 = (bf16[512,64]{0,1:T(8,128)(2,1)S(1)}, bf16[512,64]{0,1:T(8,128)(2,1)S(1)}, u32[]{:S(2)}, u32[]{:S(2)}) collective-permute-start(bf16[512,64]{0,1:T(8,128)(2,1)S(1)} %fusion.56), channel_id=1, source_target_pairs={{4,0},{8,12},{5,1},{9,13},{6,2},{10,14},{7,3},{11,15},{20,16},{24,... | collective-permute-start | bytes 196616 | tf_op jit(solution)/shard_map/ppermute | solution.py:69
  79.1 54.6 %collective-permute-start.11 = (bf16[512,1024]{1,0:T(8,128)(2,1)S(1)}, bf16[512,1024]{1,0:T(8,128)(2,1)S(1)}, u32[]{:S(2)}, u32[]{:S(2)}) collective-permute-start(bf16[512,1024]{1,0:T(8,128)(2,1)S(1)} %collective-permute-done.7), channel_id=1, source_target_pairs={{4,0},{8,12},{5,1},{9,13},{6,2},{10,14},{7,3},{11,15},{20,16},{24,... | collective-permute-start | bytes 3145736 | tf_op jit(solution)/shard_map/ppermute | solution.py:69
  111.3 39.2 %collective-permute-start.12 = (bf16[512,768]{1,0:T(8,128)(2,1)S(1)}, bf16[512,768]{1,0:T(8,128)(2,1)S(1)}, u32[]{:S(2)}, u32[]{:S(2)}) collective-permute-start(bf16[512,768]{1,0:T(8,128)(2,1)S(1)} %slice.60), channel_id=1, source_target_pairs={{4,0},{8,12},{5,1},{9,13},{6,2},{10,14},{7,3},{11,15},{20,16},{24,... | collective-permute-start | bytes 2359304 | tf_op jit(solution)/shard_map/ppermute | solution.py:69
  112.6 41.7 %collective-permute-start.13 = (bf16[512,256]{1,0:T(8,128)(2,1)S(1)}, bf16[512,256]{1,0:T(8,128)(2,1)S(1)}, u32[]{:S(2)}, u32[]{:S(2)}) collective-permute-start(bf16[512,256]{1,0:T(8,128)(2,1)S(1)} %slice.61), channel_id=1, source_target_pairs={{4,0},{8,12},{5,1},{9,13},{6,2},{10,14},{7,3},{11,15},{20,16},{24,... | collective-permute-start | bytes 786440 | tf_op jit(solution)/shard_map/ppermute | solution.py:69

commit v8 on v7

--- a/solution.py
+++ b/solution.py
@@ -87,20 +87,21 @@
         part = lax.dynamic_slice_in_dim(base_weight, owner * width + first, block.shape[1], axis=0)
         return jnp.dot(block, part, preferred_element_type=F32)
 
+    mid = send(own, ACROSS)
     mate_out = send(own, OUTWARD)
     mate_in = send(own, INWARD)
-    mid = [send(own[:, :half], ACROSS)]
-    mid.append(send(after(own[:, half:], mid[0]), ACROSS))
     partial = shrink(inputs, shrink_table, adapter_ids)
     mate_partial = send(partial, SWAP)
     total = product(own, here)
 
-    mid_out = [send(after(mid[0], total), OUTWARD)]
-    mate_in, mate_partial = lax.optimization_barrier((mate_in, mate_partial, mid[1], total))[:2]
+    mid = after(mid, total)
+    mid_out = send(mid, OUTWARD)
+    mate_in, mate_out, mate_partial = lax.optimization_barrier(
+        (mate_in, mate_out, mate_partial, mid)
+    )[:3]
     both = send(jnp.stack([partial, mate_partial]), ACROSS)
     end = [send(mate_in[:, :half], ACROSS)]
     end.append(send(after(mate_in[:, half:], end[0]), ACROSS))
-    mid_out.append(send(mid[1], OUTWARD))
     total = total + product(jnp.where(is_end, mate_out, mate_in), here ^ 1)
 
     end[0], both = lax.optimization_barrier((end[0], both, total))[:2]
@@ -109,14 +110,13 @@
         partial.astype(F32) + mate_partial.astype(F32) + both[0].astype(F32) + both[1].astype(F32)
     ).astype(BF16)
     shrunk = jnp.where(is_end, send(shrunk, OUTWARD), shrunk)
-    total = total + product(jnp.where(is_end, mid_out[0], mid[0]), far_mid)
 
-    late = after(end[1], total)
-    shrunk = after(shrunk, late)
+    late = after(end[1], end[0])
     end_out += [send(late[:, : half - last], OUTWARD), send(late[:, half - last :], OUTWARD)]
-    total = total + product(jnp.where(is_end, mid_out[1], mid[1]), far_mid, half)
+    mid_out, shrunk = lax.optimization_barrier((mid_out, shrunk, late))[:2]
+    total = total + product(jnp.where(is_end, mid_out, mid), far_mid)
     total = total + jnp.concatenate(expand(shrunk, expand_table, adapter_ids))
-    total = total + product(jnp.where(is_end, end_out[0], end[0]), far_end)
+    total = total + product(jnp.where(is_end, after(end_out[0], total), end[0]), far_end)
     block = jnp.where(is_end, after(end_out[1], total), late[:, : half - last])
     total = total + product(block, far_end, half)
     block = jnp.where(is_end, after(end_out[2], total), late[:, half - last :])

time: 158 us -> 162 us (1.025)
  waiting for transfers between devices: 68.4 us -> 83.4 us
  starting transfers between devices: 38.2 us -> 23.9 us
  matrix products: 41.3 us -> 46 us
  local copies, waits for them, and re-layouts: 5.65 us -> 3.34 us
    ppermute x14 -> x12, waiting for transfers between devices: 68.4 us -> 83.4 us  [send(): return lax.ppermute(block, 'tensor', pairs)]
    ppermute x14 -> x12, starting transfers between devices: 38.2 us -> 23.9 us  [send(): return lax.ppermute(block, 'tensor', pairs)]
    dot_general x7 -> x6, matrix products: 37.6 us -> 41.6 us  [product(): return jnp.dot(block, part, preferred_element_type=F32)]
    slice x1 -> x0, local copies, waits for them, and re-layouts: 3.2 us -> none  [line(): mid = [send(own[:, :half], ACROSS)]]
  transfers between devices with their start and end apart: 14 -> 12, of which waited for: 6 -> 4; matrix products, arithmetic and copies ran while one was open for 26% -> 27% of each run, Pallas kernels for 0% -> 0%
where the time goes in v8:
time: 162 us; the launch traced here: 161 us
  waiting for transfers between devices  83.4 us (51%)
  matrix products  46 us (28%)
  starting transfers between devices  23.9 us (15%)
  between operations  4.24 us (3%)
  local copies, waits for them, and re-layouts  3.34 us (2%)
    ppermute x12, waiting for transfers between devices, send(): return lax.ppermute(block, 'tensor', pairs)  83.4 us
    dot_general x6, matrix products, product(): return jnp.dot(block, part, preferred_element_type=F32)  41.6 us
    ppermute x12, starting transfers between devices, send(): return lax.ppermute(block, 'tensor', pairs)  23.9 us
    dot_general x2, matrix products, shrink(): jnp.dot(inputs[c], shrink_table[adapter_ids[c]], preferred_element_type=F32)  3.52 us
  transfers between devices with their start and end apart: 12, of which 4 were waited for; matrix products, arithmetic and copies ran while one was open for 27% of the time, Pallas kernels for 0%

profile of v8, /device:TPU:0, one launch (start us, length us, event | category | flops | bytes accessed | tf_op | source)
XLA Modules:
  0.0 161.1 jit_solution(15727898033478785106)
XLA Ops:
  0.0 2.2 %collective-permute-start.3 = (bf16[512,2048]{1,0:T(8,128)(2,1)}, bf16[512,2048]{1,0:T(8,128)(2,1)}, u32[]{:S(2)}, u32[]{:S(2)}) collective-permute-start(bf16[512,2048]{1,0:T(8,128)(2,1)} %bitcast.39), channel_id=1, source_target_pairs={{4,8},{8,4},{5,9},{9,5},{6,10},{10,6},{7,11},{11,7},{20,24},{24,20... | collective-permute-start | bytes 6291464 | tf_op jit(solution)/shard_map/ppermute | solution.py:69
  2.2 6.5 %collective-permute-start = (bf16[512,2048]{1,0:T(8,128)(2,1)}, bf16[512,2048]{1,0:T(8,128)(2,1)S(1)}, u32[]{:S(2)}, u32[]{:S(2)}) collective-permute-start(bf16[512,2048]{1,0:T(8,128)(2,1)} %bitcast.40), channel_id=1, source_target_pairs={{0,4},{12,8},{1,5},{13,9},{2,6},{14,10},{3,7},{15,11},{16,20},{28,... | collective-permute-start | bytes 6291464 | tf_op jit(solution)/shard_map/ppermute | solution.py:69
  8.7 1.3 collective-permute-start.1
  10.0 1.4 fusion.68
  15.4 1.8 %fusion.28 = bf16[256,64]{0,1:T(8,128)(2,1)S(1)} fusion(bf16[2,256,2048]{2,1,0:T(8,128)(2,1)} %param.5, bf16[4,2048,64]{1,2,0:T(8,128)(2,1)} %param.7, s32[]{:T(128)S(6)} %select_n.79), kind=kOutput, calls=%fused_computation.22 | convolution fusion | flops 67125248 | bytes 1343492 | tf_op jit(solution)/shard_map/dot_general | solution.py:12
  17.1 1.8 %fusion.29 = bf16[256,64]{0,1:T(8,128)(2,1)S(1)} fusion(bf16[2,256,2048]{2,1,0:T(8,128)(2,1)} %param.5, bf16[4,2048,64]{1,2,0:T(8,128)(2,1)} %param.7, s32[]{:T(128)S(6)} %select_n.80), kind=kOutput, calls=%fused_computation.23 | convolution fusion | flops 67125248 | bytes 1343492 | tf_op jit(solution)/shard_map/dot_general | solution.py:12
  18.9 4.1 %collective-permute-start.2 = (bf16[512,64]{0,1:T(8,128)(2,1)S(1)}, bf16[512,64]{0,1:T(8,128)(2,1)S(1)}, u32[]{:S(2)}, u32[]{:S(2)}) collective-permute-start(bf16[512,64]{0,1:T(8,128)(2,1)S(1)} %get-tuple-element.34), channel_id=1, source_target_pairs={{0,4},{12,8},{4,0},{8,12},{1,5},{13,9},{5,1},{9,13},{2,6},{14,10},... | collective-permute-start | bytes 196616 | tf_op jit(solution)/shard_map/ppermute | solution.py:69
  23.0 10.5 %fusion.8 = f32[512,2048]{1,0:T(8,128)} fusion(bf16[512,2048]{1,0:T(8,128)(2,1)} %bitcast.42, bf16[8192,2048]{1,0:T(8,128)(2,1)} %param.6, s32[]{:T(128)S(6)} %select_n.77), kind=kOutput, calls=%fused_computation.10 | convolution fusion | flops 4294967296 | bytes 14680068 | tf_op jit(solution)/shard_map/dot_general | solution.py:88
  33.5 25.6 %collective-permute-done.2 = bf16[512,64]{0,1:T(8,128)(2,1)S(1)} collective-permute-done((bf16[512,64]{0,1:T(8,128)(2,1)S(1)}, bf16[512,64]{0,1:T(8,128)(2,1)S(1)}, u32[]{:S(2)}, u32[]{:S(2)}) %collective-permute-start.2) | collective-permute-done | bytes 65568 | tf_op jit(solution)/shard_map/ppermute | solution.py:69
  59.0 1.8 %fusion.67 = (bf16[512,1024]{1,0:T(8,128)(2,1)}, bf16[512,1024]{1,0:T(8,128)(2,1)}) fusion(bf16[512,2048]{1,0:T(8,128)(2,1)S(1)} %collective-permute-done), kind=kLoop, calls=%fused_computation.66 | loop fusion | bytes 4194304 | tf_op jit(solution)/shard_map/slice | solution.py:104
  60.8 1.6 %collective-permute-start.5 = (bf16[512,1024]{1,0:T(8,128)(2,1)}, bf16[512,1024]{1,0:T(8,128)(2,1)}, u32[]{:S(2)}, u32[]{:S(2)}) collective-permute-start(bf16[512,1024]{1,0:T(8,128)(2,1)} %get-tuple-element.32), channel_id=1, source_target_pairs={{4,8},{8,4},{5,9},{9,5},{6,10},{10,6},{7,11},{11,7},{20,24},{24,20... | collective-permute-start | bytes 3145736 | tf_op jit(solution)/shard_map/ppermute | solution.py:69
  62.5 1.3 collective-permute-start.4
  65.2 11.7 %fusion.13 = f32[512,2048]{1,0:T(8,128)} fusion(f32[512,2048]{1,0:T(8,128)} %fusion.8, bf16[8192,2048]{1,0:T(8,128)(2,1)} %param.6, s32[]{:T(128)S(6)} %select_n.82, bf16[512,2048]{1,0:T(8,128)(2,1)} %collective-permute-done.1, bf16[512,2048]{1,0:T(8,128)(2,1)} %copy-done.2, pred[]{:T(512)S(6)} %or.3), kind=kOutput, calls=%fused_computation.13 | convolution fusion | flops 4297064448 | bytes 20971524 | tf_op jit(solution)/shard_map/dot_general | solution.py:88
  77.0 1.3 collective-permute-start.7
  78.3 1.6 collective-permute-start.9
  79.9 34.7 %collective-permute-done.7 = bf16[512,64]{0,1:T(8,128)(2,1)S(1)} collective-permute-done((bf16[512,64]{0,1:T(8,128)(2,1)S(1)}, bf16[512,64]{0,1:T(8,128)(2,1)S(1)}, u32[]{:S(2)}, u32[]{:S(2)}) %collective-permute-start.7) | collective-permute-done | bytes 65568 | tf_op jit(solution)/shard_map/ppermute | solution.py:69
  115.6 1.3 collective-permute-start.10
  116.9 7.7 %maximum_add_fusion = f32[512,2048]{1,0:T(8,128)S(1)} fusion(f32[256,2048]{1,0:T(8,128)S(1)} %fusion.39, f32[256,2048]{1,0:T(8,128)S(1)} %fusion.41, f32[512,2048]{1,0:T(8,128)S(1)} %copy-done.3, bf16[8192,2048]{1,0:T(8,128)(2,1)} %param.6, s32[]{:T(128)S(6)} %select_n.87, bf16[512,2048]{1,0:T(8,128)(2,1)} %collective-permute-done.4, ...), kind=kOutput, calls=%fused_computation.6 | convolution fusion | flops 4299161600 | bytes 25165828 | tf_op jit(solution)/shard_map/dot_general | solution.py:88
  124.6 12.4 %collective-permute-done.9 = bf16[512,1024]{1,0:T(8,128)(2,1)S(1)} collective-permute-done((bf16[512,1024]{1,0:T(8,128)(2,1)}, bf16[512,1024]{1,0:T(8,128)(2,1)S(1)}, u32[]{:S(2)}, u32[]{:S(2)}) %collective-permute-start.9) | collective-permute-done | bytes 1048608 | tf_op jit(solution)/shard_map/ppermute | solution.py:69
  137.0 1.5 collective-permute-start.11
  138.5 4.6 %fusion.21 = f32[512,2048]{1,0:T(8,128)S(1)} fusion(f32[512,2048]{1,0:T(8,128)S(1)} %maximum_add_fusion, bf16[8192,2048]{1,0:T(8,128)(2,1)} %param.6, s32[]{:T(128)S(6)} %select_n.91, bf16[512,1024]{1,0:T(8,128)(2,1)S(1)} %collective-permute-done.9, bf16[512,1024]{1,0:T(8,128)(2,1)} %collective-permute-done.5, pred[]{:T(512)S(6)} %or.3), kind=kOutput, calls=%fused_computation.15 | convolution fusion | flops 2149056512 | bytes 14680069 | tf_op jit(solution)/shard_map/dot_general | solution.py:88
  143.1 10.8 %collective-permute-done.10 = bf16[512,768]{1,0:T(8,128)(2,1)S(1)} collective-permute-done((bf16[512,768]{1,0:T(8,128)(2,1)S(1)}, bf16[512,768]{1,0:T(8,128)(2,1)S(1)}, u32[]{:S(2)}, u32[]{:S(2)}) %collective-permute-start.10) | collective-permute-done | bytes 786464 | tf_op jit(solution)/shard_map/ppermute | solution.py:69
  153.9 3.8 %fusion.18 = f32[512,2048]{1,0:T(8,128)S(1)} fusion(f32[512,2048]{1,0:T(8,128)S(1)} %fusion.21, bf16[8192,2048]{1,0:T(8,128)(2,1)} %param.6, s32[]{:T(128)S(6)} %select_n.94, bf16[512,768]{1,0:T(8,128)(2,1)S(1)} %collective-permute-done.10, pred[]{:T(512)S(6)} %or.3, bf16[512,1024]{1,0:T(8,128)(2,1)S(1)} %collective-permute-done.8), kind=kOutput, calls=%fused_computation.14 | convolution fusion | flops 1612054528 | bytes 13107205 | tf_op jit(solution)/shard_map/dot_general | solution.py:88
  157.7 3.3 %add_convert_fusion = bf16[512,2048]{1,0:T(8,128)(2,1)} fusion(f32[512,2048]{1,0:T(8,128)S(1)} %fusion.18, bf16[8192,2048]{1,0:T(8,128)(2,1)} %param.6, s32[]{:T(128)S(6)} %select_n.97, bf16[512,256]{1,0:T(8,128)(2,1)S(1)} %collective-permute-done.11, pred[]{:T(512)S(6)} %or.3, bf16[512,1024]{1,0:T(8,128)(2,1)S(1)} %collective-permute-done.8), kind=kOutput, calls=%fused_computation.7 | convolution fusion | flops 539099136 | bytes 7864325 | tf_op jit(solution)/shard_map/dot_general | solution.py:88
  (26 shorter events, 2.5 us)
Async XLA Ops:
  0.0 114.6 %copy-start = (bf16[4,64,2048]{2,1,0:T(8,128)(2,1)S(1)}, bf16[4,64,2048]{2,1,0:T(8,128)(2,1)}, u32[]{:S(2)}) copy-start(bf16[4,64,2048]{2,1,0:T(8,128)(2,1)} %param.8) | copy-start | bytes 3145732
  0.0 33.5 %collective-permute-start.3 = (bf16[512,2048]{1,0:T(8,128)(2,1)}, bf16[512,2048]{1,0:T(8,128)(2,1)}, u32[]{:S(2)}, u32[]{:S(2)}) collective-permute-start(bf16[512,2048]{1,0:T(8,128)(2,1)} %bitcast.39), channel_id=1, source_target_pairs={{4,8},{8,4},{5,9},{9,5},{6,10},{10,6},{7,11},{11,7},{20,24},{24,20... | collective-permute-start | bytes 6291464 | tf_op jit(solution)/shard_map/ppermute | solution.py:69
  2.2 56.9 %collective-permute-start = (bf16[512,2048]{1,0:T(8,128)(2,1)}, bf16[512,2048]{1,0:T(8,128)(2,1)S(1)}, u32[]{:S(2)}, u32[]{:S(2)}) collective-permute-start(bf16[512,2048]{1,0:T(8,128)(2,1)} %bitcast.40), channel_id=1, source_target_pairs={{0,4},{12,8},{1,5},{13,9},{2,6},{14,10},{3,7},{15,11},{16,20},{28,... | collective-permute-start | bytes 6291464 | tf_op jit(solution)/shard_map/ppermute | solution.py:69
  8.7 50.3 %collective-permute-start.1 = (bf16[512,2048]{1,0:T(8,128)(2,1)}, bf16[512,2048]{1,0:T(8,128)(2,1)}, u32[]{:S(2)}, u32[]{:S(2)}) collective-permute-start(bf16[512,2048]{1,0:T(8,128)(2,1)} %bitcast.41), channel_id=1, source_target_pairs={{4,0},{8,12},{5,1},{9,13},{6,2},{10,14},{7,3},{11,15},{20,16},{24,... | collective-permute-start | bytes 6291464 | tf_op jit(solution)/shard_map/ppermute | solution.py:69
  18.9 40.1 %collective-permute-start.2 = (bf16[512,64]{0,1:T(8,128)(2,1)S(1)}, bf16[512,64]{0,1:T(8,128)(2,1)S(1)}, u32[]{:S(2)}, u32[]{:S(2)}) collective-permute-start(bf16[512,64]{0,1:T(8,128)(2,1)S(1)} %get-tuple-element.34), channel_id=1, source_target_pairs={{0,4},{12,8},{4,0},{8,12},{1,5},{13,9},{5,1},{9,13},{2,6},{14,10},... | collective-permute-start | bytes 196616 | tf_op jit(solution)/shard_map/ppermute | solution.py:69
  59.0 5.5 %copy-start.2 = (bf16[512,2048]{1,0:T(8,128)(2,1)}, bf16[512,2048]{1,0:T(8,128)(2,1)S(1)}, u32[]{:S(2)}) copy-start(bf16[512,2048]{1,0:T(8,128)(2,1)S(1)} %collective-permute-done) | copy-start | bytes 6291460
  60.8 3.6 %collective-permute-start.5 = (bf16[512,1024]{1,0:T(8,128)(2,1)}, bf16[512,1024]{1,0:T(8,128)(2,1)}, u32[]{:S(2)}, u32[]{:S(2)}) collective-permute-start(bf16[512,1024]{1,0:T(8,128)(2,1)} %get-tuple-element.32), channel_id=1, source_target_pairs={{4,8},{8,4},{5,9},{9,5},{6,10},{10,6},{7,11},{11,7},{20,24},{24,20... | collective-permute-start | bytes 3145736 | tf_op jit(solution)/shard_map/ppermute | solution.py:69
  62.5 52.1 %collective-permute-start.4 = (bf16[512,2048]{1,0:T(8,128)(2,1)}, bf16[512,2048]{1,0:T(8,128)(2,1)}, u32[]{:S(2)}, u32[]{:S(2)}) collective-permute-start(bf16[512,2048]{1,0:T(8,128)(2,1)} %collective-permute-done.3), channel_id=1, source_target_pairs={{4,0},{8,12},{5,1},{9,13},{6,2},{10,14},{7,3},{11,15},{20,16},{24,... | collective-permute-start | bytes 6291464 | tf_op jit(solution)/shard_map/ppermute | solution.py:69
  63.8 13.1 %collective-permute-start.6 = (bf16[2,512,64]{1,2,0:T(8,128)(2,1)S(1)}, bf16[2,512,64]{1,2,0:T(8,128)(2,1)S(1)}, u32[]{:S(2)}, u32[]{:S(2)}) collective-permute-start(bf16[2,512,64]{1,2,0:T(8,128)(2,1)S(1)} %pad_maximum_fusion), channel_id=1, source_target_pairs={{4,8},{8,4},{5,9},{9,5},{6,10},{10,6},{7,11},{11,7},{20,24},{24,20... | collective-permute-start | bytes 393224 | tf_op jit(solution)/shard_map/ppermute | solution.py:69
  64.5 50.1 %collective-permute-start.8 = (bf16[512,1024]{1,0:T(8,128)(2,1)}, bf16[512,1024]{1,0:T(8,128)(2,1)S(1)}, u32[]{:S(2)}, u32[]{:S(2)}) collective-permute-start(bf16[512,1024]{1,0:T(8,128)(2,1)} %get-tuple-element.23), channel_id=1, source_target_pairs={{4,8},{8,4},{5,9},{9,5},{6,10},{10,6},{7,11},{11,7},{20,24},{24,20... | collective-permute-start | bytes 3145736 | tf_op jit(solution)/shard_map/ppermute | solution.py:69
  77.0 37.6 %collective-permute-start.7 = (bf16[512,64]{0,1:T(8,128)(2,1)S(1)}, bf16[512,64]{0,1:T(8,128)(2,1)S(1)}, u32[]{:S(2)}, u32[]{:S(2)}) collective-permute-start(bf16[512,64]{0,1:T(8,128)(2,1)S(1)} %fusion.51), channel_id=1, source_target_pairs={{4,0},{8,12},{5,1},{9,13},{6,2},{10,14},{7,3},{11,15},{20,16},{24,... | collective-permute-start | bytes 196616 | tf_op jit(solution)/shard_map/ppermute | solution.py:69
  78.3 38.6 %copy-start.3 = (f32[512,2048]{1,0:T(8,128)S(1)}, f32[512,2048]{1,0:T(8,128)}, u32[]{:S(2)}) copy-start(f32[512,2048]{1,0:T(8,128)} %fusion.13) | copy-start | bytes 12582916
  78.3 58.7 %collective-permute-start.9 = (bf16[512,1024]{1,0:T(8,128)(2,1)}, bf16[512,1024]{1,0:T(8,128)(2,1)S(1)}, u32[]{:S(2)}, u32[]{:S(2)}) collective-permute-start(bf16[512,1024]{1,0:T(8,128)(2,1)} %collective-permute-done.5), channel_id=1, source_target_pairs={{4,0},{8,12},{5,1},{9,13},{6,2},{10,14},{7,3},{11,15},{20,16},{24,... | collective-permute-start | bytes 3145736 | tf_op jit(solution)/shard_map/ppermute | solution.py:69
  115.6 38.3 %collective-permute-start.10 = (bf16[512,768]{1,0:T(8,128)(2,1)S(1)}, bf16[512,768]{1,0:T(8,128)(2,1)S(1)}, u32[]{:S(2)}, u32[]{:S(2)}) collective-permute-start(bf16[512,768]{1,0:T(8,128)(2,1)S(1)} %slice.52), channel_id=1, source_target_pairs={{4,0},{8,12},{5,1},{9,13},{6,2},{10,14},{7,3},{11,15},{20,16},{24,... | collective-permute-start | bytes 2359304 | tf_op jit(solution)/shard_map/ppermute | solution.py:69
  137.0 20.7 %collective-permute-start.11 = (bf16[512,256]{1,0:T(8,128)(2,1)S(1)}, bf16[512,256]{1,0:T(8,128)(2,1)S(1)}, u32[]{:S(2)}, u32[]{:S(2)}) collective-permute-start(bf16[512,256]{1,0:T(8,128)(2,1)S(1)} %slice.53), channel_id=1, source_target_pairs={{4,0},{8,12},{5,1},{9,13},{6,2},{10,14},{7,3},{11,15},{20,16},{24,... | collective-permute-start | bytes 786440 | tf_op jit(solution)/shard_map/ppermute | solution.py:69
  153.9 7.2 %copy-start.1 = (bf16[4,64,2048]{2,1,0:T(8,128)(2,1)S(1)}, bf16[4,64,2048]{2,1,0:T(8,128)(2,1)}, u32[]{:S(2)}) copy-start(bf16[4,64,2048]{2,1,0:T(8,128)(2,1)} %param.8) | copy-start | bytes 3145732

commit v9 on v7

--- a/solution.py
+++ b/solution.py
@@ -62,7 +62,6 @@
 INWARD = [(0, 1), (3, 2)]
 OUTWARD = [(1, 0), (2, 3)]
 ACROSS = [(1, 2), (2, 1)]
-SWAP = INWARD + OUTWARD
 
 
 def send(block, pairs):
@@ -90,16 +89,16 @@
     mate_out = send(own, OUTWARD)
     mate_in = send(own, INWARD)
     mid = [send(own[:, :half], ACROSS)]
-    mid.append(send(after(own[:, half:], mid[0]), ACROSS))
     partial = shrink(inputs, shrink_table, adapter_ids)
-    mate_partial = send(partial, SWAP)
+    mid.append(send(after(own, partial)[:, half:], ACROSS))
+    mate_partial = send(partial, INWARD)
     total = product(own, here)
 
     mid_out = [send(after(mid[0], total), OUTWARD)]
     mate_in, mate_partial = lax.optimization_barrier((mate_in, mate_partial, mid[1], total))[:2]
     both = send(jnp.stack([partial, mate_partial]), ACROSS)
     end = [send(mate_in[:, :half], ACROSS)]
-    end.append(send(after(mate_in[:, half:], end[0]), ACROSS))
+    end.append(send(after(mate_in, end[0])[:, half:], ACROSS))
     mid_out.append(send(mid[1], OUTWARD))
     total = total + product(jnp.where(is_end, mate_out, mate_in), here ^ 1)
 

time: 158 us -> 151 us (0.956)
  starting transfers between devices: 38.2 us -> 29.6 us
  waiting for transfers between devices: 68.4 us -> 65 us
  matrix products: 41.3 us -> 44.2 us
  local copies, waits for them, and re-layouts: 5.65 us -> 7.43 us
    ppermute x14, starting transfers between devices: 38.2 us -> 29.6 us  [send(): return lax.ppermute(block, 'tensor', pairs)]
    ppermute x14, waiting for transfers between devices: 68.4 us -> 65 us  [send(): return lax.ppermute(block, 'tensor', pairs)]
    dot_general x7, matrix products: 37.6 us -> 39.8 us  [product(): return jnp.dot(block, part, preferred_element_type=F32)]
    slice x1 -> x3, local copies, waits for them, and re-layouts: 1.71 us -> 3.67 us  [the longest x1 1.29 us: line(): end.append(send(after(mate_in, end[0])[:, half:], ACROSS))]
  transfers between devices with their start and end apart: 14 -> 14, of which waited for: 6 -> 7; matrix products, arithmetic and copies ran while one was open for 26% -> 32% of each run, Pallas kernels for 0% -> 0%
where the time goes in v9:
time: 151 us; the launch traced here: 150 us
  waiting for transfers between devices  65 us (43%)
  matrix products  44.2 us (29%)
  starting transfers between devices  29.6 us (20%)
  local copies, waits for them, and re-layouts  7.43 us (5%)
  between operations  3.95 us (3%)
    ppermute x14, waiting for transfers between devices, send(): return lax.ppermute(block, 'tensor', pairs)  65 us
    dot_general x7, matrix products, product(): return jnp.dot(block, part, preferred_element_type=F32)  39.8 us
    ppermute x14, starting transfers between devices, send(): return lax.ppermute(block, 'tensor', pairs)  29.6 us
    dot_general x2, matrix products, shrink(): jnp.dot(inputs[c], shrink_table[adapter_ids[c]], preferred_element_type=F32)  3.52 us
  transfers between devices with their start and end apart: 14, of which 7 were waited for; matrix products, arithmetic and copies ran while one was open for 32% of the time, Pallas kernels for 0%

profile of v9, /device:TPU:0, one launch (start us, length us, event | category | flops | bytes accessed | tf_op | source)
XLA Modules:
  0.0 150.3 jit_solution(14771456747471257848)
XLA Ops:
  0.0 6.5 %collective-permute-start.1 = (bf16[512,2048]{1,0:T(8,128)(2,1)}, bf16[512,2048]{1,0:T(8,128)(2,1)}, u32[]{:S(2)}, u32[]{:S(2)}) collective-permute-start(bf16[512,2048]{1,0:T(8,128)(2,1)} %bitcast.38), channel_id=1, source_target_pairs={{0,4},{12,8},{1,5},{13,9},{2,6},{14,10},{3,7},{15,11},{16,20},{28,... | collective-permute-start | bytes 6291464 | tf_op jit(solution)/shard_map/ppermute | solution.py:68
  7.8 2.3 %slice.62 = bf16[512,1024]{1,0:T(8,128)(2,1)} slice(bf16[512,2048]{1,0:T(8,128)(2,1)} %bitcast.40), slice={[0:512], [0:1024]} | slice | bytes 2097152 | tf_op jit(solution)/shard_map/slice | solution.py:91
  10.1 1.7 %collective-permute-start.4 = (bf16[512,1024]{1,0:T(8,128)(2,1)}, bf16[512,1024]{1,0:T(8,128)(2,1)}, u32[]{:S(2)}, u32[]{:S(2)}) collective-permute-start(bf16[512,1024]{1,0:T(8,128)(2,1)} %slice.62), channel_id=1, source_target_pairs={{4,8},{8,4},{5,9},{9,5},{6,10},{10,6},{7,11},{11,7},{20,24},{24,20... | collective-permute-start | bytes 3145736 | tf_op jit(solution)/shard_map/ppermute | solution.py:68
  11.8 1.4 fusion.73
  16.9 1.8 %fusion.29 = bf16[256,64]{0,1:T(8,128)(2,1)S(1)} fusion(bf16[2,256,2048]{2,1,0:T(8,128)(2,1)} %param.5, bf16[4,2048,64]{1,2,0:T(8,128)(2,1)} %param.7, s32[]{:T(128)S(6)} %select_n.86), kind=kOutput, calls=%fused_computation.23 | convolution fusion | flops 67125248 | bytes 1343492 | tf_op jit(solution)/shard_map/dot_general | solution.py:12
  18.7 1.8 %fusion.30 = bf16[256,64]{0,1:T(8,128)(2,1)S(1)} fusion(bf16[2,256,2048]{2,1,0:T(8,128)(2,1)} %param.5, bf16[4,2048,64]{1,2,0:T(8,128)(2,1)} %param.7, s32[]{:T(128)S(6)} %select_n.87), kind=kOutput, calls=%fused_computation.24 | convolution fusion | flops 67125248 | bytes 1343492 | tf_op jit(solution)/shard_map/dot_general | solution.py:12
  21.5 1.6 %collective-permute-start.3 = (bf16[512,1024]{1,0:T(8,128)(2,1)}, bf16[512,1024]{1,0:T(8,128)(2,1)}, u32[]{:S(2)}, u32[]{:S(2)}) collective-permute-start(bf16[512,1024]{1,0:T(8,128)(2,1)} %slice.52), channel_id=1, source_target_pairs={{4,8},{8,4},{5,9},{9,5},{6,10},{10,6},{7,11},{11,7},{20,24},{24,20... | collective-permute-start | bytes 3145736 | tf_op jit(solution)/shard_map/ppermute | solution.py:68
  23.2 8.4 %collective-permute-start.2 = (bf16[512,64]{0,1:T(8,128)(2,1)S(1)}, bf16[512,64]{0,1:T(8,128)(2,1)S(1)}, u32[]{:S(2)}, u32[]{:S(2)}) collective-permute-start(bf16[512,64]{0,1:T(8,128)(2,1)S(1)} %get-tuple-element.28), channel_id=1, source_target_pairs={{0,4},{12,8},{1,5},{13,9},{2,6},{14,10},{3,7},{15,11},{16,20},{28,... | collective-permute-start | bytes 196616 | tf_op jit(solution)/shard_map/ppermute | solution.py:68
  31.6 9.4 %fusion.11 = f32[512,2048]{1,0:T(8,128)} fusion(bf16[512,2048]{1,0:T(8,128)(2,1)S(1)} %bitcast.42, bf16[8192,2048]{1,0:T(8,128)(2,1)} %param.6, s32[]{:T(128)S(6)} %select_n.84), kind=kOutput, calls=%fused_computation.13 | convolution fusion | flops 4294967296 | bytes 14680068 | tf_op jit(solution)/shard_map/dot_general | solution.py:87
  43.6 8.1 %collective-permute-done.2 = bf16[512,64]{0,1:T(8,128)(2,1)S(1)} collective-permute-done((bf16[512,64]{0,1:T(8,128)(2,1)S(1)}, bf16[512,64]{0,1:T(8,128)(2,1)S(1)}, u32[]{:S(2)}, u32[]{:S(2)}) %collective-permute-start.2) | collective-permute-done | bytes 65568 | tf_op jit(solution)/shard_map/ppermute | solution.py:68
  51.7 1.3 slice.54
  54.4 2.9 %collective-permute-done = bf16[512,2048]{1,0:T(8,128)(2,1)} collective-permute-done((bf16[512,2048]{1,0:T(8,128)(2,1)}, bf16[512,2048]{1,0:T(8,128)(2,1)}, u32[]{:S(2)}, u32[]{:S(2)}) %collective-permute-start) | collective-permute-done | bytes 2097184 | tf_op jit(solution)/shard_map/ppermute | solution.py:68
  57.3 9.7 %fusion.16 = f32[512,2048]{1,0:T(8,128)S(1)} fusion(f32[512,2048]{1,0:T(8,128)} %fusion.11, bf16[8192,2048]{1,0:T(8,128)(2,1)} %param.6, s32[]{:T(128)S(6)} %select_n.89, bf16[512,2048]{1,0:T(8,128)(2,1)} %collective-permute-done, bf16[512,2048]{1,0:T(8,128)(2,1)} %collective-permute-done.1, pred[]{:T(512)S(6)} %or.3), kind=kOutput, calls=%fused_computation.16 | convolution fusion | flops 4297064448 | bytes 20971524 | tf_op jit(solution)/shard_map/dot_general | solution.py:87
  67.0 1.3 slice.57
  71.7 7.9 %collective-permute-done.5 = bf16[512,1024]{1,0:T(8,128)(2,1)S(1)} collective-permute-done((bf16[512,1024]{1,0:T(8,128)(2,1)}, bf16[512,1024]{1,0:T(8,128)(2,1)S(1)}, u32[]{:S(2)}, u32[]{:S(2)}) %collective-permute-start.5) | collective-permute-done | bytes 1048608 | tf_op jit(solution)/shard_map/ppermute | solution.py:68
  79.7 4.5 %fusion.22 = f32[512,2048]{1,0:T(8,128)S(1)} fusion(f32[512,2048]{1,0:T(8,128)S(1)} %fusion.16, bf16[8192,2048]{1,0:T(8,128)(2,1)} %param.6, s32[]{:T(128)S(6)} %select_n.93, bf16[512,1024]{1,0:T(8,128)(2,1)S(1)} %collective-permute-done.5, bf16[512,1024]{1,0:T(8,128)(2,1)} %collective-permute-done.4, pred[]{:T(512)S(6)} %or.3), kind=kOutput, calls=%fused_computation.18 | convolution fusion | flops 2149056512 | bytes 14680069 | tf_op jit(solution)/shard_map/dot_general | solution.py:87
  84.2 19.3 %collective-permute-done.9 = bf16[512,64]{0,1:T(8,128)(2,1)S(1)} collective-permute-done((bf16[512,64]{0,1:T(8,128)(2,1)S(1)}, bf16[512,64]{0,1:T(8,128)(2,1)S(1)}, u32[]{:S(2)}, u32[]{:S(2)}) %collective-permute-start.9) | collective-permute-done | bytes 65568 | tf_op jit(solution)/shard_map/ppermute | solution.py:68
  105.0 1.5 collective-permute-start.13
  107.4 18.6 %collective-permute-done.11 = bf16[512,1024]{1,0:T(8,128)(2,1)S(1)} collective-permute-done((bf16[512,1024]{1,0:T(8,128)(2,1)S(1)}, bf16[512,1024]{1,0:T(8,128)(2,1)S(1)}, u32[]{:S(2)}, u32[]{:S(2)}) %collective-permute-start.11) | collective-permute-done | bytes 1048608 | tf_op jit(solution)/shard_map/ppermute | solution.py:68
  126.0 4.5 %fusion.5 = f32[512,2048]{1,0:T(8,128)S(1)} fusion(bf16[8192,2048]{1,0:T(8,128)(2,1)} %param.6, s32[]{:T(128)S(6)} %select_n.100, bf16[512,1024]{1,0:T(8,128)(2,1)S(1)} %collective-permute-done.11, bf16[512,1024]{1,0:T(8,128)(2,1)S(1)} %collective-permute-done.7, pred[]{:T(512)S(6)} %or.3), kind=kOutput, calls=%fused_computation.7 | convolution fusion | flops 2148007936 | bytes 10485765 | tf_op jit(solution)/shard_map/dot_general | solution.py:87
  130.6 4.7 %fusion.4 = f32[512,2048]{1,0:T(8,128)S(1)} fusion(f32[512,2048]{1,0:T(8,128)S(1)} %fusion.5, f32[256,2048]{1,0:T(8,128)S(1)} %fusion.44, f32[256,2048]{1,0:T(8,128)S(1)} %fusion.46, f32[512,2048]{1,0:T(8,128)S(1)} %fusion.22, bf16[8192,2048]{1,0:T(8,128)(2,1)} %param.6, s32[]{:T(128)S(6)} %select_n.95, bf16[512,1024]{1,0:T(8,128)(2,1)S(1)} %collective-permute-done.6, ...), kind=kOutput, calls=%fused_computation.5 | convolution fusion | flops 2152202240 | bytes 23068676 | tf_op jit(solution)/shard_map/dot_general | solution.py:87
  135.2 7.6 %collective-permute-done.12 = bf16[512,768]{1,0:T(8,128)(2,1)S(1)} collective-permute-done((bf16[512,768]{1,0:T(8,128)(2,1)S(1)}, bf16[512,768]{1,0:T(8,128)(2,1)S(1)}, u32[]{:S(2)}, u32[]{:S(2)}) %collective-permute-start.12) | collective-permute-done | bytes 786464 | tf_op jit(solution)/shard_map/ppermute | solution.py:68
  142.9 3.7 %fusion.19 = f32[512,2048]{1,0:T(8,128)S(1)} fusion(f32[512,2048]{1,0:T(8,128)S(1)} %fusion.4, bf16[8192,2048]{1,0:T(8,128)(2,1)} %param.6, s32[]{:T(128)S(6)} %select_n.103, bf16[512,768]{1,0:T(8,128)(2,1)S(1)} %collective-permute-done.12, pred[]{:T(512)S(6)} %or.3, bf16[512,1024]{1,0:T(8,128)(2,1)S(1)} %collective-permute-done.10), kind=kOutput, calls=%fused_computation.17 | convolution fusion | flops 1612054528 | bytes 13107205 | tf_op jit(solution)/shard_map/dot_general | solution.py:87
  147.0 3.3 %add_convert_fusion = bf16[512,2048]{1,0:T(8,128)(2,1)} fusion(f32[512,2048]{1,0:T(8,128)S(1)} %fusion.19, bf16[8192,2048]{1,0:T(8,128)(2,1)} %param.6, s32[]{:T(128)S(6)} %select_n.106, bf16[512,256]{1,0:T(8,128)(2,1)S(1)} %collective-permute-done.13, pred[]{:T(512)S(6)} %or.3, bf16[512,1024]{1,0:T(8,128)(2,1)S(1)} %collective-permute-done.10), kind=kOutput, calls=%fused_computation.6 | convolution fusion | flops 539099136 | bytes 7864325 | tf_op jit(solution)/shard_map/dot_general | solution.py:87
  (30 shorter events, 12.5 us)
Async XLA Ops:
  0.0 106.5 %copy-start = (bf16[4,64,2048]{2,1,0:T(8,128)(2,1)S(1)}, bf16[4,64,2048]{2,1,0:T(8,128)(2,1)}, u32[]{:S(2)}) copy-start(bf16[4,64,2048]{2,1,0:T(8,128)(2,1)} %param.8) | copy-start | bytes 3145732
  0.0 20.4 %copy-start.1 = (bf16[2,256,2048]{2,1,0:T(8,128)(2,1)S(1)}, bf16[2,256,2048]{2,1,0:T(8,128)(2,1)}, u32[]{:S(2)}) copy-start(bf16[2,256,2048]{2,1,0:T(8,128)(2,1)} %param.5) | copy-start | bytes 6291460
  0.0 51.7 %collective-permute-start.1 = (bf16[512,2048]{1,0:T(8,128)(2,1)}, bf16[512,2048]{1,0:T(8,128)(2,1)}, u32[]{:S(2)}, u32[]{:S(2)}) collective-permute-start(bf16[512,2048]{1,0:T(8,128)(2,1)} %bitcast.38), channel_id=1, source_target_pairs={{0,4},{12,8},{1,5},{13,9},{2,6},{14,10},{3,7},{15,11},{16,20},{28,... | collective-permute-start | bytes 6291464 | tf_op jit(solution)/shard_map/ppermute | solution.py:68
  6.5 50.8 %collective-permute-start = (bf16[512,2048]{1,0:T(8,128)(2,1)}, bf16[512,2048]{1,0:T(8,128)(2,1)}, u32[]{:S(2)}, u32[]{:S(2)}) collective-permute-start(bf16[512,2048]{1,0:T(8,128)(2,1)} %bitcast.39), channel_id=1, source_target_pairs={{4,0},{8,12},{5,1},{9,13},{6,2},{10,14},{7,3},{11,15},{20,16},{24,... | collective-permute-start | bytes 6291464 | tf_op jit(solution)/shard_map/ppermute | solution.py:68
  10.1 30.9 %collective-permute-start.4 = (bf16[512,1024]{1,0:T(8,128)(2,1)}, bf16[512,1024]{1,0:T(8,128)(2,1)}, u32[]{:S(2)}, u32[]{:S(2)}) collective-permute-start(bf16[512,1024]{1,0:T(8,128)(2,1)} %slice.62), channel_id=1, source_target_pairs={{4,8},{8,4},{5,9},{9,5},{6,10},{10,6},{7,11},{11,7},{20,24},{24,20... | collective-permute-start | bytes 3145736 | tf_op jit(solution)/shard_map/ppermute | solution.py:68
  21.5 20.7 %collective-permute-start.3 = (bf16[512,1024]{1,0:T(8,128)(2,1)}, bf16[512,1024]{1,0:T(8,128)(2,1)}, u32[]{:S(2)}, u32[]{:S(2)}) collective-permute-start(bf16[512,1024]{1,0:T(8,128)(2,1)} %slice.52), channel_id=1, source_target_pairs={{4,8},{8,4},{5,9},{9,5},{6,10},{10,6},{7,11},{11,7},{20,24},{24,20... | collective-permute-start | bytes 3145736 | tf_op jit(solution)/shard_map/ppermute | solution.py:68
  23.2 28.5 %collective-permute-start.2 = (bf16[512,64]{0,1:T(8,128)(2,1)S(1)}, bf16[512,64]{0,1:T(8,128)(2,1)S(1)}, u32[]{:S(2)}, u32[]{:S(2)}) collective-permute-start(bf16[512,64]{0,1:T(8,128)(2,1)S(1)} %get-tuple-element.28), channel_id=1, source_target_pairs={{0,4},{12,8},{1,5},{13,9},{2,6},{14,10},{3,7},{15,11},{16,20},{28,... | collective-permute-start | bytes 196616 | tf_op jit(solution)/shard_map/ppermute | solution.py:68
  41.0 38.7 %collective-permute-start.5 = (bf16[512,1024]{1,0:T(8,128)(2,1)}, bf16[512,1024]{1,0:T(8,128)(2,1)S(1)}, u32[]{:S(2)}, u32[]{:S(2)}) collective-permute-start(bf16[512,1024]{1,0:T(8,128)(2,1)} %collective-permute-done.4), channel_id=1, source_target_pairs={{4,0},{8,12},{5,1},{9,13},{6,2},{10,14},{7,3},{11,15},{20,16},{24,... | collective-permute-start | bytes 3145736 | tf_op jit(solution)/shard_map/ppermute | solution.py:68
  42.3 88.3 %collective-permute-start.6 = (bf16[512,1024]{1,0:T(8,128)(2,1)}, bf16[512,1024]{1,0:T(8,128)(2,1)S(1)}, u32[]{:S(2)}, u32[]{:S(2)}) collective-permute-start(bf16[512,1024]{1,0:T(8,128)(2,1)} %collective-permute-done.3), channel_id=1, source_target_pairs={{4,0},{8,12},{5,1},{9,13},{6,2},{10,14},{7,3},{11,15},{20,16},{24,... | collective-permute-start | bytes 3145736 | tf_op jit(solution)/shard_map/ppermute | solution.py:68
  53.0 14.0 %collective-permute-start.7 = (bf16[512,1024]{1,0:T(8,128)(2,1)S(1)}, bf16[512,1024]{1,0:T(8,128)(2,1)S(1)}, u32[]{:S(2)}, u32[]{:S(2)}) collective-permute-start(bf16[512,1024]{1,0:T(8,128)(2,1)S(1)} %slice.54), channel_id=1, source_target_pairs={{4,8},{8,4},{5,9},{9,5},{6,10},{10,6},{7,11},{11,7},{20,24},{24,20... | collective-permute-start | bytes 3145736 | tf_op jit(solution)/shard_map/ppermute | solution.py:68
  53.7 15.3 %collective-permute-start.8 = (bf16[2,512,64]{1,2,0:T(8,128)(2,1)S(1)}, bf16[2,512,64]{1,2,0:T(8,128)(2,1)S(1)}, u32[]{:S(2)}, u32[]{:S(2)}) collective-permute-start(bf16[2,512,64]{1,2,0:T(8,128)(2,1)S(1)} %pad_maximum_fusion), channel_id=1, source_target_pairs={{4,8},{8,4},{5,9},{9,5},{6,10},{10,6},{7,11},{11,7},{20,24},{24,20... | collective-permute-start | bytes 393224 | tf_op jit(solution)/shard_map/ppermute | solution.py:68
  68.3 35.2 %collective-permute-start.10 = (bf16[512,1024]{1,0:T(8,128)(2,1)S(1)}, bf16[512,1024]{1,0:T(8,128)(2,1)S(1)}, u32[]{:S(2)}, u32[]{:S(2)}) collective-permute-start(bf16[512,1024]{1,0:T(8,128)(2,1)S(1)} %slice.57), channel_id=1, source_target_pairs={{4,8},{8,4},{5,9},{9,5},{6,10},{10,6},{7,11},{11,7},{20,24},{24,20... | collective-permute-start | bytes 3145736 | tf_op jit(solution)/shard_map/ppermute | solution.py:68
  69.1 34.4 %collective-permute-start.9 = (bf16[512,64]{0,1:T(8,128)(2,1)S(1)}, bf16[512,64]{0,1:T(8,128)(2,1)S(1)}, u32[]{:S(2)}, u32[]{:S(2)}) collective-permute-start(bf16[512,64]{0,1:T(8,128)(2,1)S(1)} %fusion.56), channel_id=1, source_target_pairs={{4,0},{8,12},{5,1},{9,13},{6,2},{10,14},{7,3},{11,15},{20,16},{24,... | collective-permute-start | bytes 196616 | tf_op jit(solution)/shard_map/ppermute | solution.py:68
  70.4 55.6 %collective-permute-start.11 = (bf16[512,1024]{1,0:T(8,128)(2,1)S(1)}, bf16[512,1024]{1,0:T(8,128)(2,1)S(1)}, u32[]{:S(2)}, u32[]{:S(2)}) collective-permute-start(bf16[512,1024]{1,0:T(8,128)(2,1)S(1)} %collective-permute-done.7), channel_id=1, source_target_pairs={{4,0},{8,12},{5,1},{9,13},{6,2},{10,14},{7,3},{11,15},{20,16},{24,... | collective-permute-start | bytes 3145736 | tf_op jit(solution)/shard_map/ppermute | solution.py:68
  103.7 39.2 %collective-permute-start.12 = (bf16[512,768]{1,0:T(8,128)(2,1)S(1)}, bf16[512,768]{1,0:T(8,128)(2,1)S(1)}, u32[]{:S(2)}, u32[]{:S(2)}) collective-permute-start(bf16[512,768]{1,0:T(8,128)(2,1)S(1)} %slice.60), channel_id=1, source_target_pairs={{4,0},{8,12},{5,1},{9,13},{6,2},{10,14},{7,3},{11,15},{20,16},{24,... | collective-permute-start | bytes 2359304 | tf_op jit(solution)/shard_map/ppermute | solution.py:68
  105.0 42.0 %collective-permute-start.13 = (bf16[512,256]{1,0:T(8,128)(2,1)S(1)}, bf16[512,256]{1,0:T(8,128)(2,1)S(1)}, u32[]{:S(2)}, u32[]{:S(2)}) collective-permute-start(bf16[512,256]{1,0:T(8,128)(2,1)S(1)} %slice.61), channel_id=1, source_target_pairs={{4,0},{8,12},{5,1},{9,13},{6,2},{10,14},{7,3},{11,15},{20,16},{24,... | collective-permute-start | bytes 786440 | tf_op jit(solution)/shard_map/ppermute | solution.py:68

commit v10 on v9

--- a/solution.py
+++ b/solution.py
@@ -80,14 +80,14 @@
     far_mid = jnp.where(here < 2, 2, 1)
     far_end = jnp.where(here < 2, 3, 0)
     own = inputs.reshape(rows, width)
-    half, last = width // 2, width // 8
+    half, last = width // 2, width // 16
 
     def product(block, owner, first=0):
         part = lax.dynamic_slice_in_dim(base_weight, owner * width + first, block.shape[1], axis=0)
         return jnp.dot(block, part, preferred_element_type=F32)
 
+    mate_in = send(own, INWARD)
     mate_out = send(own, OUTWARD)
-    mate_in = send(own, INWARD)
     mid = [send(own[:, :half], ACROSS)]
     partial = shrink(inputs, shrink_table, adapter_ids)
     mid.append(send(after(own, partial)[:, half:], ACROSS))
@@ -95,7 +95,9 @@
     total = product(own, here)
 
     mid_out = [send(after(mid[0], total), OUTWARD)]
-    mate_in, mate_partial = lax.optimization_barrier((mate_in, mate_partial, mid[1], total))[:2]
+    mate_in, mate_out, mate_partial = lax.optimization_barrier(
+        (mate_in, mate_out, mate_partial, mid[1], total)
+    )[:3]
     both = send(jnp.stack([partial, mate_partial]), ACROSS)
     end = [send(mate_in[:, :half], ACROSS)]
     end.append(send(after(mate_in, end[0])[:, half:], ACROSS))

time: 151 us -> 154 us (1.020)
  waiting for transfers between devices: 65 us -> 67.3 us
    ppermute x14, waiting for transfers between devices: 65 us -> 67.3 us  [send(): return lax.ppermute(block, 'tensor', pairs)]
  transfers between devices with their start and end apart: 14 -> 14, of which waited for: 7 -> 6; matrix products, arithmetic and copies ran while one was open for 32% -> 32% of each run, Pallas kernels for 0% -> 0%
where the time goes in v10:
time: 154 us; the launch traced here: 153 us
  waiting for transfers between devices  67.3 us (44%)
  matrix products  44.7 us (29%)
  starting transfers between devices  29.6 us (19%)
  local copies, waits for them, and re-layouts  7.43 us (5%)
  between operations  3.95 us (3%)
    ppermute x14, waiting for transfers between devices, send(): return lax.ppermute(block, 'tensor', pairs)  67.3 us
    dot_general x7, matrix products, product(): return jnp.dot(block, part, preferred_element_type=F32)  40.3 us
    ppermute x14, starting transfers between devices, send(): return lax.ppermute(block, 'tensor', pairs)  29.6 us
    dot_general x2, matrix products, shrink(): jnp.dot(inputs[c], shrink_table[adapter_ids[c]], preferred_element_type=F32)  3.52 us
  transfers between devices with their start and end apart: 14, of which 6 were waited for; matrix products, arithmetic and copies ran while one was open for 32% of the time, Pallas kernels for 0%

profile of v10, /device:TPU:0, one launch (start us, length us, event | category | flops | bytes accessed | tf_op | source)
XLA Modules:
  0.0 153.1 jit_solution(6682085326801915531)
XLA Ops:
  0.0 6.5 %collective-permute-start = (bf16[512,2048]{1,0:T(8,128)(2,1)}, bf16[512,2048]{1,0:T(8,128)(2,1)}, u32[]{:S(2)}, u32[]{:S(2)}) collective-permute-start(bf16[512,2048]{1,0:T(8,128)(2,1)} %bitcast.38), channel_id=1, source_target_pairs={{0,4},{12,8},{1,5},{13,9},{2,6},{14,10},{3,7},{15,11},{16,20},{28,... | collective-permute-start | bytes 6291464 | tf_op jit(solution)/shard_map/ppermute | solution.py:68
  7.8 2.3 %slice.62 = bf16[512,1024]{1,0:T(8,128)(2,1)} slice(bf16[512,2048]{1,0:T(8,128)(2,1)} %bitcast.40), slice={[0:512], [0:1024]} | slice | bytes 2097152 | tf_op jit(solution)/shard_map/slice | solution.py:91
  10.1 1.7 %collective-permute-start.4 = (bf16[512,1024]{1,0:T(8,128)(2,1)}, bf16[512,1024]{1,0:T(8,128)(2,1)}, u32[]{:S(2)}, u32[]{:S(2)}) collective-permute-start(bf16[512,1024]{1,0:T(8,128)(2,1)} %slice.62), channel_id=1, source_target_pairs={{4,8},{8,4},{5,9},{9,5},{6,10},{10,6},{7,11},{11,7},{20,24},{24,20... | collective-permute-start | bytes 3145736 | tf_op jit(solution)/shard_map/ppermute | solution.py:68
  11.8 1.4 fusion.73
  16.9 1.8 %fusion.29 = bf16[256,64]{0,1:T(8,128)(2,1)S(1)} fusion(bf16[2,256,2048]{2,1,0:T(8,128)(2,1)} %param.5, bf16[4,2048,64]{1,2,0:T(8,128)(2,1)} %param.7, s32[]{:T(128)S(6)} %select_n.86), kind=kOutput, calls=%fused_computation.23 | convolution fusion | flops 67125248 | bytes 1343492 | tf_op jit(solution)/shard_map/dot_general | solution.py:12
  18.7 1.8 %fusion.30 = bf16[256,64]{0,1:T(8,128)(2,1)S(1)} fusion(bf16[2,256,2048]{2,1,0:T(8,128)(2,1)} %param.5, bf16[4,2048,64]{1,2,0:T(8,128)(2,1)} %param.7, s32[]{:T(128)S(6)} %select_n.87), kind=kOutput, calls=%fused_computation.24 | convolution fusion | flops 67125248 | bytes 1343492 | tf_op jit(solution)/shard_map/dot_general | solution.py:12
  21.5 1.6 %collective-permute-start.3 = (bf16[512,1024]{1,0:T(8,128)(2,1)}, bf16[512,1024]{1,0:T(8,128)(2,1)}, u32[]{:S(2)}, u32[]{:S(2)}) collective-permute-start(bf16[512,1024]{1,0:T(8,128)(2,1)} %slice.52), channel_id=1, source_target_pairs={{4,8},{8,4},{5,9},{9,5},{6,10},{10,6},{7,11},{11,7},{20,24},{24,20... | collective-permute-start | bytes 3145736 | tf_op jit(solution)/shard_map/ppermute | solution.py:68
  23.2 8.4 %collective-permute-start.2 = (bf16[512,64]{0,1:T(8,128)(2,1)S(1)}, bf16[512,64]{0,1:T(8,128)(2,1)S(1)}, u32[]{:S(2)}, u32[]{:S(2)}) collective-permute-start(bf16[512,64]{0,1:T(8,128)(2,1)S(1)} %get-tuple-element.30), channel_id=1, source_target_pairs={{0,4},{12,8},{1,5},{13,9},{2,6},{14,10},{3,7},{15,11},{16,20},{28,... | collective-permute-start | bytes 196616 | tf_op jit(solution)/shard_map/ppermute | solution.py:68
  31.6 9.4 %fusion.13 = f32[512,2048]{1,0:T(8,128)} fusion(bf16[512,2048]{1,0:T(8,128)(2,1)S(1)} %bitcast.42, bf16[8192,2048]{1,0:T(8,128)(2,1)} %param.6, s32[]{:T(128)S(6)} %select_n.84), kind=kOutput, calls=%fused_computation.15 | convolution fusion | flops 4294967296 | bytes 14680068 | tf_op jit(solution)/shard_map/dot_general | solution.py:87
  43.6 8.1 %collective-permute-done.2 = bf16[512,64]{0,1:T(8,128)(2,1)S(1)} collective-permute-done((bf16[512,64]{0,1:T(8,128)(2,1)S(1)}, bf16[512,64]{0,1:T(8,128)(2,1)S(1)}, u32[]{:S(2)}, u32[]{:S(2)}) %collective-permute-start.2) | collective-permute-done | bytes 65568 | tf_op jit(solution)/shard_map/ppermute | solution.py:68
  51.7 5.6 %collective-permute-done.1 = bf16[512,2048]{1,0:T(8,128)(2,1)} collective-permute-done((bf16[512,2048]{1,0:T(8,128)(2,1)}, bf16[512,2048]{1,0:T(8,128)(2,1)}, u32[]{:S(2)}, u32[]{:S(2)}) %collective-permute-start.1) | collective-permute-done | bytes 2097184 | tf_op jit(solution)/shard_map/ppermute | solution.py:68
  57.3 1.3 slice.54
  60.0 9.7 %fusion.16 = f32[512,2048]{1,0:T(8,128)S(1)} fusion(f32[512,2048]{1,0:T(8,128)} %fusion.13, bf16[8192,2048]{1,0:T(8,128)(2,1)} %param.6, s32[]{:T(128)S(6)} %select_n.89, bf16[512,2048]{1,0:T(8,128)(2,1)} %collective-permute-done.1, bf16[512,2048]{1,0:T(8,128)(2,1)} %collective-permute-done, pred[]{:T(512)S(6)} %or.3), kind=kOutput, calls=%fused_computation.16 | convolution fusion | flops 4297064448 | bytes 20971524 | tf_op jit(solution)/shard_map/dot_general | solution.py:87
  69.8 1.3 slice.57
  74.5 5.2 %collective-permute-done.5 = bf16[512,1024]{1,0:T(8,128)(2,1)S(1)} collective-permute-done((bf16[512,1024]{1,0:T(8,128)(2,1)}, bf16[512,1024]{1,0:T(8,128)(2,1)S(1)}, u32[]{:S(2)}, u32[]{:S(2)}) %collective-permute-start.5) | collective-permute-done | bytes 1048608 | tf_op jit(solution)/shard_map/ppermute | solution.py:68
  79.7 4.5 %fusion.22 = f32[512,2048]{1,0:T(8,128)S(1)} fusion(f32[512,2048]{1,0:T(8,128)S(1)} %fusion.16, bf16[8192,2048]{1,0:T(8,128)(2,1)} %param.6, s32[]{:T(128)S(6)} %select_n.93, bf16[512,1024]{1,0:T(8,128)(2,1)S(1)} %collective-permute-done.5, bf16[512,1024]{1,0:T(8,128)(2,1)} %collective-permute-done.4, pred[]{:T(512)S(6)} %or.3), kind=kOutput, calls=%fused_computation.18 | convolution fusion | flops 2149056512 | bytes 14680069 | tf_op jit(solution)/shard_map/dot_general | solution.py:87
  84.2 19.3 %collective-permute-done.9 = bf16[512,64]{0,1:T(8,128)(2,1)S(1)} collective-permute-done((bf16[512,64]{0,1:T(8,128)(2,1)S(1)}, bf16[512,64]{0,1:T(8,128)(2,1)S(1)}, u32[]{:S(2)}, u32[]{:S(2)}) %collective-permute-start.9) | collective-permute-done | bytes 65568 | tf_op jit(solution)/shard_map/ppermute | solution.py:68
  105.0 1.5 collective-permute-start.13
  107.4 18.6 %collective-permute-done.11 = bf16[512,1024]{1,0:T(8,128)(2,1)S(1)} collective-permute-done((bf16[512,1024]{1,0:T(8,128)(2,1)S(1)}, bf16[512,1024]{1,0:T(8,128)(2,1)S(1)}, u32[]{:S(2)}, u32[]{:S(2)}) %collective-permute-start.11) | collective-permute-done | bytes 1048608 | tf_op jit(solution)/shard_map/ppermute | solution.py:68
  126.0 4.5 %fusion.5 = f32[512,2048]{1,0:T(8,128)S(1)} fusion(bf16[8192,2048]{1,0:T(8,128)(2,1)} %param.6, s32[]{:T(128)S(6)} %select_n.100, bf16[512,1024]{1,0:T(8,128)(2,1)S(1)} %collective-permute-done.11, bf16[512,1024]{1,0:T(8,128)(2,1)S(1)} %collective-permute-done.7, pred[]{:T(512)S(6)} %or.3), kind=kOutput, calls=%fused_computation.7 | convolution fusion | flops 2148007936 | bytes 10485765 | tf_op jit(solution)/shard_map/dot_general | solution.py:87
  130.6 4.7 %fusion.4 = f32[512,2048]{1,0:T(8,128)S(1)} fusion(f32[512,2048]{1,0:T(8,128)S(1)} %fusion.5, f32[256,2048]{1,0:T(8,128)S(1)} %fusion.44, f32[256,2048]{1,0:T(8,128)S(1)} %fusion.46, f32[512,2048]{1,0:T(8,128)S(1)} %fusion.22, bf16[8192,2048]{1,0:T(8,128)(2,1)} %param.6, s32[]{:T(128)S(6)} %select_n.95, bf16[512,1024]{1,0:T(8,128)(2,1)S(1)} %collective-permute-done.6, ...), kind=kOutput, calls=%fused_computation.5 | convolution fusion | flops 2152202240 | bytes 23068676 | tf_op jit(solution)/shard_map/dot_general | solution.py:87
  135.2 10.4 %collective-permute-done.12 = bf16[512,896]{1,0:T(8,128)(2,1)S(1)} collective-permute-done((bf16[512,896]{1,0:T(8,128)(2,1)S(1)}, bf16[512,896]{1,0:T(8,128)(2,1)S(1)}, u32[]{:S(2)}, u32[]{:S(2)}) %collective-permute-start.12) | collective-permute-done | bytes 917536 | tf_op jit(solution)/shard_map/ppermute | solution.py:68
  145.6 4.4 %fusion.19 = f32[512,2048]{1,0:T(8,128)S(1)} fusion(f32[512,2048]{1,0:T(8,128)S(1)} %fusion.4, bf16[8192,2048]{1,0:T(8,128)(2,1)} %param.6, s32[]{:T(128)S(6)} %select_n.103, bf16[512,896]{1,0:T(8,128)(2,1)S(1)} %collective-permute-done.12, pred[]{:T(512)S(6)} %or.3, bf16[512,1024]{1,0:T(8,128)(2,1)S(1)} %collective-permute-done.10), kind=kOutput, calls=%fused_computation.17 | convolution fusion | flops 1880555520 | bytes 13893637 | tf_op jit(solution)/shard_map/dot_general | solution.py:87
  150.0 3.1 %add_convert_fusion = bf16[512,2048]{1,0:T(8,128)(2,1)} fusion(f32[512,2048]{1,0:T(8,128)S(1)} %fusion.19, bf16[8192,2048]{1,0:T(8,128)(2,1)} %param.6, s32[]{:T(128)S(6)} %select_n.106, bf16[512,128]{1,0:T(8,128)(2,1)S(1)} %collective-permute-done.13, pred[]{:T(512)S(6)} %or.3, bf16[512,1024]{1,0:T(8,128)(2,1)S(1)} %collective-permute-done.10), kind=kOutput, calls=%fused_computation.6 | convolution fusion | flops 270598144 | bytes 7077893 | tf_op jit(solution)/shard_map/dot_general | solution.py:87
  (30 shorter events, 12.0 us)
Async XLA Ops:
  0.0 106.5 %copy-start = (bf16[4,64,2048]{2,1,0:T(8,128)(2,1)S(1)}, bf16[4,64,2048]{2,1,0:T(8,128)(2,1)}, u32[]{:S(2)}) copy-start(bf16[4,64,2048]{2,1,0:T(8,128)(2,1)} %param.8) | copy-start | bytes 3145732
  0.0 20.4 %copy-start.1 = (bf16[2,256,2048]{2,1,0:T(8,128)(2,1)S(1)}, bf16[2,256,2048]{2,1,0:T(8,128)(2,1)}, u32[]{:S(2)}) copy-start(bf16[2,256,2048]{2,1,0:T(8,128)(2,1)} %param.5) | copy-start | bytes 6291460
  0.0 51.7 %collective-permute-start = (bf16[512,2048]{1,0:T(8,128)(2,1)}, bf16[512,2048]{1,0:T(8,128)(2,1)}, u32[]{:S(2)}, u32[]{:S(2)}) collective-permute-start(bf16[512,2048]{1,0:T(8,128)(2,1)} %bitcast.38), channel_id=1, source_target_pairs={{0,4},{12,8},{1,5},{13,9},{2,6},{14,10},{3,7},{15,11},{16,20},{28,... | collective-permute-start | bytes 6291464 | tf_op jit(solution)/shard_map/ppermute | solution.py:68
  6.5 50.8 %collective-permute-start.1 = (bf16[512,2048]{1,0:T(8,128)(2,1)}, bf16[512,2048]{1,0:T(8,128)(2,1)}, u32[]{:S(2)}, u32[]{:S(2)}) collective-permute-start(bf16[512,2048]{1,0:T(8,128)(2,1)} %bitcast.39), channel_id=1, source_target_pairs={{4,0},{8,12},{5,1},{9,13},{6,2},{10,14},{7,3},{11,15},{20,16},{24,... | collective-permute-start | bytes 6291464 | tf_op jit(solution)/shard_map/ppermute | solution.py:68
  10.1 30.9 %collective-permute-start.4 = (bf16[512,1024]{1,0:T(8,128)(2,1)}, bf16[512,1024]{1,0:T(8,128)(2,1)}, u32[]{:S(2)}, u32[]{:S(2)}) collective-permute-start(bf16[512,1024]{1,0:T(8,128)(2,1)} %slice.62), channel_id=1, source_target_pairs={{4,8},{8,4},{5,9},{9,5},{6,10},{10,6},{7,11},{11,7},{20,24},{24,20... | collective-permute-start | bytes 3145736 | tf_op jit(solution)/shard_map/ppermute | solution.py:68
  21.5 20.7 %collective-permute-start.3 = (bf16[512,1024]{1,0:T(8,128)(2,1)}, bf16[512,1024]{1,0:T(8,128)(2,1)}, u32[]{:S(2)}, u32[]{:S(2)}) collective-permute-start(bf16[512,1024]{1,0:T(8,128)(2,1)} %slice.52), channel_id=1, source_target_pairs={{4,8},{8,4},{5,9},{9,5},{6,10},{10,6},{7,11},{11,7},{20,24},{24,20... | collective-permute-start | bytes 3145736 | tf_op jit(solution)/shard_map/ppermute | solution.py:68
  23.2 28.5 %collective-permute-start.2 = (bf16[512,64]{0,1:T(8,128)(2,1)S(1)}, bf16[512,64]{0,1:T(8,128)(2,1)S(1)}, u32[]{:S(2)}, u32[]{:S(2)}) collective-permute-start(bf16[512,64]{0,1:T(8,128)(2,1)S(1)} %get-tuple-element.30), channel_id=1, source_target_pairs={{0,4},{12,8},{1,5},{13,9},{2,6},{14,10},{3,7},{15,11},{16,20},{28,... | collective-permute-start | bytes 196616 | tf_op jit(solution)/shard_map/ppermute | solution.py:68
  41.0 38.7 %collective-permute-start.5 = (bf16[512,1024]{1,0:T(8,128)(2,1)}, bf16[512,1024]{1,0:T(8,128)(2,1)S(1)}, u32[]{:S(2)}, u32[]{:S(2)}) collective-permute-start(bf16[512,1024]{1,0:T(8,128)(2,1)} %collective-permute-done.4), channel_id=1, source_target_pairs={{4,0},{8,12},{5,1},{9,13},{6,2},{10,14},{7,3},{11,15},{20,16},{24,... | collective-permute-start | bytes 3145736 | tf_op jit(solution)/shard_map/ppermute | solution.py:68
  42.3 88.3 %collective-permute-start.6 = (bf16[512,1024]{1,0:T(8,128)(2,1)}, bf16[512,1024]{1,0:T(8,128)(2,1)S(1)}, u32[]{:S(2)}, u32[]{:S(2)}) collective-permute-start(bf16[512,1024]{1,0:T(8,128)(2,1)} %collective-permute-done.3), channel_id=1, source_target_pairs={{4,0},{8,12},{5,1},{9,13},{6,2},{10,14},{7,3},{11,15},{20,16},{24,... | collective-permute-start | bytes 3145736 | tf_op jit(solution)/shard_map/ppermute | solution.py:68
  58.6 11.2 %collective-permute-start.7 = (bf16[512,1024]{1,0:T(8,128)(2,1)S(1)}, bf16[512,1024]{1,0:T(8,128)(2,1)S(1)}, u32[]{:S(2)}, u32[]{:S(2)}) collective-permute-start(bf16[512,1024]{1,0:T(8,128)(2,1)S(1)} %slice.54), channel_id=1, source_target_pairs={{4,8},{8,4},{5,9},{9,5},{6,10},{10,6},{7,11},{11,7},{20,24},{24,20... | collective-permute-start | bytes 3145736 | tf_op jit(solution)/shard_map/ppermute | solution.py:68
  59.4 12.5 %collective-permute-start.8 = (bf16[2,512,64]{1,2,0:T(8,128)(2,1)S(1)}, bf16[2,512,64]{1,2,0:T(8,128)(2,1)S(1)}, u32[]{:S(2)}, u32[]{:S(2)}) collective-permute-start(bf16[2,512,64]{1,2,0:T(8,128)(2,1)S(1)} %pad_maximum_fusion), channel_id=1, source_target_pairs={{4,8},{8,4},{5,9},{9,5},{6,10},{10,6},{7,11},{11,7},{20,24},{24,20... | collective-permute-start | bytes 393224 | tf_op jit(solution)/shard_map/ppermute | solution.py:68
  71.1 32.5 %collective-permute-start.10 = (bf16[512,1024]{1,0:T(8,128)(2,1)S(1)}, bf16[512,1024]{1,0:T(8,128)(2,1)S(1)}, u32[]{:S(2)}, u32[]{:S(2)}) collective-permute-start(bf16[512,1024]{1,0:T(8,128)(2,1)S(1)} %slice.57), channel_id=1, source_target_pairs={{4,8},{8,4},{5,9},{9,5},{6,10},{10,6},{7,11},{11,7},{20,24},{24,20... | collective-permute-start | bytes 3145736 | tf_op jit(solution)/shard_map/ppermute | solution.py:68
  71.9 31.7 %collective-permute-start.9 = (bf16[512,64]{0,1:T(8,128)(2,1)S(1)}, bf16[512,64]{0,1:T(8,128)(2,1)S(1)}, u32[]{:S(2)}, u32[]{:S(2)}) collective-permute-start(bf16[512,64]{0,1:T(8,128)(2,1)S(1)} %fusion.54), channel_id=1, source_target_pairs={{4,0},{8,12},{5,1},{9,13},{6,2},{10,14},{7,3},{11,15},{20,16},{24,... | collective-permute-start | bytes 196616 | tf_op jit(solution)/shard_map/ppermute | solution.py:68
  73.2 52.8 %collective-permute-start.11 = (bf16[512,1024]{1,0:T(8,128)(2,1)S(1)}, bf16[512,1024]{1,0:T(8,128)(2,1)S(1)}, u32[]{:S(2)}, u32[]{:S(2)}) collective-permute-start(bf16[512,1024]{1,0:T(8,128)(2,1)S(1)} %collective-permute-done.7), channel_id=1, source_target_pairs={{4,0},{8,12},{5,1},{9,13},{6,2},{10,14},{7,3},{11,15},{20,16},{24,... | collective-permute-start | bytes 3145736 | tf_op jit(solution)/shard_map/ppermute | solution.py:68
  103.7 41.9 %collective-permute-start.12 = (bf16[512,896]{1,0:T(8,128)(2,1)S(1)}, bf16[512,896]{1,0:T(8,128)(2,1)S(1)}, u32[]{:S(2)}, u32[]{:S(2)}) collective-permute-start(bf16[512,896]{1,0:T(8,128)(2,1)S(1)} %slice.60), channel_id=1, source_target_pairs={{4,0},{8,12},{5,1},{9,13},{6,2},{10,14},{7,3},{11,15},{20,16},{24,... | collective-permute-start | bytes 2752520 | tf_op jit(solution)/shard_map/ppermute | solution.py:68
  105.0 45.0 %collective-permute-start.13 = (bf16[512,128]{1,0:T(8,128)(2,1)S(1)}, bf16[512,128]{1,0:T(8,128)(2,1)S(1)}, u32[]{:S(2)}, u32[]{:S(2)}) collective-permute-start(bf16[512,128]{1,0:T(8,128)(2,1)S(1)} %slice.61), channel_id=1, source_target_pairs={{4,0},{8,12},{5,1},{9,13},{6,2},{10,14},{7,3},{11,15},{20,16},{24,... | collective-permute-start | bytes 393224 | tf_op jit(solution)/shard_map/ppermute | solution.py:68

commit v11 on v9

--- a/solution.py
+++ b/solution.py
@@ -62,6 +62,7 @@
 INWARD = [(0, 1), (3, 2)]
 OUTWARD = [(1, 0), (2, 3)]
 ACROSS = [(1, 2), (2, 1)]
+SWAP = INWARD + OUTWARD
 
 
 def send(block, pairs):
@@ -86,8 +87,7 @@
         part = lax.dynamic_slice_in_dim(base_weight, owner * width + first, block.shape[1], axis=0)
         return jnp.dot(block, part, preferred_element_type=F32)
 
-    mate_out = send(own, OUTWARD)
-    mate_in = send(own, INWARD)
+    mate = send(own, SWAP)
     mid = [send(own[:, :half], ACROSS)]
     partial = shrink(inputs, shrink_table, adapter_ids)
     mid.append(send(after(own, partial)[:, half:], ACROSS))
@@ -95,12 +95,12 @@
     total = product(own, here)
 
     mid_out = [send(after(mid[0], total), OUTWARD)]
-    mate_in, mate_partial = lax.optimization_barrier((mate_in, mate_partial, mid[1], total))[:2]
+    mate, mate_partial = lax.optimization_barrier((mate, mate_partial, mid[1], total))[:2]
     both = send(jnp.stack([partial, mate_partial]), ACROSS)
-    end = [send(mate_in[:, :half], ACROSS)]
-    end.append(send(after(mate_in, end[0])[:, half:], ACROSS))
+    end = [send(mate[:, :half], ACROSS)]
+    end.append(send(after(mate, end[0])[:, half:], ACROSS))
     mid_out.append(send(mid[1], OUTWARD))
-    total = total + product(jnp.where(is_end, mate_out, mate_in), here ^ 1)
+    total = total + product(mate, here ^ 1)
 
     end[0], both = lax.optimization_barrier((end[0], both, total))[:2]
     end_out = [send(end[0], OUTWARD)]

time: 151 us -> 144 us (0.954)
  starting transfers between devices: 29.6 us -> 22 us
    ppermute x14 -> x13, starting transfers between devices: 29.6 us -> 22 us  [send(): return lax.ppermute(block, 'tensor', pairs)]
    ppermute x14 -> x13, waiting for transfers between devices: 65 us -> 66 us  [send(): return lax.ppermute(block, 'tensor', pairs)]
  transfers between devices with their start and end apart: 14 -> 13, of which waited for: 7 -> 7; matrix products, arithmetic and copies ran while one was open for 32% -> 34% of each run, Pallas kernels for 0% -> 0%
where the time goes in v11:
time: 144 us; the launch traced here: 143 us
  waiting for transfers between devices  66 us (46%)
  matrix products  44.2 us (31%)
  starting transfers between devices  22 us (15%)
  local copies, waits for them, and re-layouts  7.43 us (5%)
  between operations  3.78 us (3%)
    ppermute x13, waiting for transfers between devices, send(): return lax.ppermute(block, 'tensor', pairs)  66 us
    dot_general x7, matrix products, product(): return jnp.dot(block, part, preferred_element_type=F32)  39.8 us
    ppermute x13, starting transfers between devices, send(): return lax.ppermute(block, 'tensor', pairs)  22 us
    dot_general x2, matrix products, shrink(): jnp.dot(inputs[c], shrink_table[adapter_ids[c]], preferred_element_type=F32)  3.52 us
  transfers between devices with their start and end apart: 13, of which 7 were waited for; matrix products, arithmetic and copies ran while one was open for 34% of the time, Pallas kernels for 0%

profile of v11, /device:TPU:0, one launch (start us, length us, event | category | flops | bytes accessed | tf_op | source)
XLA Modules:
  0.0 143.4 jit_solution(11728956754966098925)
XLA Ops:
  0.0 3.0 %collective-permute-start = (bf16[512,2048]{1,0:T(8,128)(2,1)}, bf16[512,2048]{1,0:T(8,128)(2,1)}, u32[]{:S(2)}, u32[]{:S(2)}) collective-permute-start(bf16[512,2048]{1,0:T(8,128)(2,1)} %bitcast.39), channel_id=1, source_target_pairs={{0,4},{12,8},{4,0},{8,12},{1,5},{13,9},{5,1},{9,13},{2,6},{14,10},... | collective-permute-start | bytes 6291464 | tf_op jit(solution)/shard_map/ppermute | solution.py:69
  3.0 2.3 %slice.62 = bf16[512,1024]{1,0:T(8,128)(2,1)} slice(bf16[512,2048]{1,0:T(8,128)(2,1)} %bitcast.40), slice={[0:512], [0:1024]} | slice | bytes 2097152 | tf_op jit(solution)/shard_map/slice | solution.py:91
  5.3 1.7 %collective-permute-start.3 = (bf16[512,1024]{1,0:T(8,128)(2,1)}, bf16[512,1024]{1,0:T(8,128)(2,1)}, u32[]{:S(2)}, u32[]{:S(2)}) collective-permute-start(bf16[512,1024]{1,0:T(8,128)(2,1)} %slice.62), channel_id=1, source_target_pairs={{4,8},{8,4},{5,9},{9,5},{6,10},{10,6},{7,11},{11,7},{20,24},{24,20... | collective-permute-start | bytes 3145736 | tf_op jit(solution)/shard_map/ppermute | solution.py:69
  11.8 1.8 %fusion.27 = bf16[256,64]{0,1:T(8,128)(2,1)S(1)} fusion(bf16[2,256,2048]{2,1,0:T(8,128)(2,1)} %param.5, bf16[4,2048,64]{1,2,0:T(8,128)(2,1)} %param.7, s32[]{:T(128)S(6)} %select_n.77), kind=kOutput, calls=%fused_computation.21 | convolution fusion | flops 67125248 | bytes 1343492 | tf_op jit(solution)/shard_map/dot_general | solution.py:12
  13.6 1.8 %fusion.28 = bf16[256,64]{0,1:T(8,128)(2,1)S(1)} fusion(bf16[2,256,2048]{2,1,0:T(8,128)(2,1)} %param.5, bf16[4,2048,64]{1,2,0:T(8,128)(2,1)} %param.7, s32[]{:T(128)S(6)} %select_n.78), kind=kOutput, calls=%fused_computation.22 | convolution fusion | flops 67125248 | bytes 1343492 | tf_op jit(solution)/shard_map/dot_general | solution.py:12
  16.5 1.7 %collective-permute-start.2 = (bf16[512,1024]{1,0:T(8,128)(2,1)}, bf16[512,1024]{1,0:T(8,128)(2,1)}, u32[]{:S(2)}, u32[]{:S(2)}) collective-permute-start(bf16[512,1024]{1,0:T(8,128)(2,1)} %slice.52), channel_id=1, source_target_pairs={{4,8},{8,4},{5,9},{9,5},{6,10},{10,6},{7,11},{11,7},{20,24},{24,20... | collective-permute-start | bytes 3145736 | tf_op jit(solution)/shard_map/ppermute | solution.py:69
  18.2 5.5 %collective-permute-start.1 = (bf16[512,64]{0,1:T(8,128)(2,1)S(1)}, bf16[512,64]{0,1:T(8,128)(2,1)S(1)}, u32[]{:S(2)}, u32[]{:S(2)}) collective-permute-start(bf16[512,64]{0,1:T(8,128)(2,1)S(1)} %get-tuple-element.28), channel_id=1, source_target_pairs={{0,4},{12,8},{1,5},{13,9},{2,6},{14,10},{3,7},{15,11},{16,20},{28,... | collective-permute-start | bytes 196616 | tf_op jit(solution)/shard_map/ppermute | solution.py:69
  23.8 9.4 %fusion.11 = f32[512,2048]{1,0:T(8,128)} fusion(bf16[512,2048]{1,0:T(8,128)(2,1)S(1)} %bitcast.42, bf16[8192,2048]{1,0:T(8,128)(2,1)} %param.6, s32[]{:T(128)S(6)} %select_n.76), kind=kOutput, calls=%fused_computation.13 | convolution fusion | flops 4294967296 | bytes 14680068 | tf_op jit(solution)/shard_map/dot_general | solution.py:88
  34.5 1.3 collective-permute-start.5
  35.8 13.8 %collective-permute-done.1 = bf16[512,64]{0,1:T(8,128)(2,1)S(1)} collective-permute-done((bf16[512,64]{0,1:T(8,128)(2,1)S(1)}, bf16[512,64]{0,1:T(8,128)(2,1)S(1)}, u32[]{:S(2)}, u32[]{:S(2)}) %collective-permute-start.1) | collective-permute-done | bytes 65568 | tf_op jit(solution)/shard_map/ppermute | solution.py:69
  49.8 1.3 slice.54
  52.6 9.7 %fusion.16 = f32[512,2048]{1,0:T(8,128)S(1)} fusion(f32[512,2048]{1,0:T(8,128)} %fusion.11, bf16[512,2048]{1,0:T(8,128)(2,1)} %collective-permute-done, bf16[8192,2048]{1,0:T(8,128)(2,1)} %param.6, s32[]{:T(128)S(6)} %select_n.79), kind=kOutput, calls=%fused_computation.16 | convolution fusion | flops 4296015872 | bytes 18874372 | tf_op jit(solution)/shard_map/dot_general | solution.py:88
  62.3 1.3 slice.57
  64.3 1.3 collective-permute-start.8
  66.9 5.3 %collective-permute-done.4 = bf16[512,1024]{1,0:T(8,128)(2,1)S(1)} collective-permute-done((bf16[512,1024]{1,0:T(8,128)(2,1)}, bf16[512,1024]{1,0:T(8,128)(2,1)S(1)}, u32[]{:S(2)}, u32[]{:S(2)}) %collective-permute-start.4) | collective-permute-done | bytes 1048608 | tf_op jit(solution)/shard_map/ppermute | solution.py:69
  72.2 4.5 %fusion.22 = f32[512,2048]{1,0:T(8,128)S(1)} fusion(f32[512,2048]{1,0:T(8,128)S(1)} %fusion.16, bf16[8192,2048]{1,0:T(8,128)(2,1)} %param.6, s32[]{:T(128)S(6)} %select_n.83, bf16[512,1024]{1,0:T(8,128)(2,1)S(1)} %collective-permute-done.4, bf16[512,1024]{1,0:T(8,128)(2,1)} %collective-permute-done.3, pred[]{:T(512)S(6)} %or.3), kind=kOutput, calls=%fused_computation.18 | convolution fusion | flops 2149056512 | bytes 14680069 | tf_op jit(solution)/shard_map/dot_general | solution.py:88
  76.7 19.3 %collective-permute-done.8 = bf16[512,64]{0,1:T(8,128)(2,1)S(1)} collective-permute-done((bf16[512,64]{0,1:T(8,128)(2,1)S(1)}, bf16[512,64]{0,1:T(8,128)(2,1)S(1)}, u32[]{:S(2)}, u32[]{:S(2)}) %collective-permute-start.8) | collective-permute-done | bytes 65568 | tf_op jit(solution)/shard_map/ppermute | solution.py:69
  97.5 1.5 %collective-permute-start.12 = (bf16[512,256]{1,0:T(8,128)(2,1)S(1)}, bf16[512,256]{1,0:T(8,128)(2,1)S(1)}, u32[]{:S(2)}, u32[]{:S(2)}) collective-permute-start(bf16[512,256]{1,0:T(8,128)(2,1)S(1)} %slice.61), channel_id=1, source_target_pairs={{4,0},{8,12},{5,1},{9,13},{6,2},{10,14},{7,3},{11,15},{20,16},{24,... | collective-permute-start | bytes 786440 | tf_op jit(solution)/shard_map/ppermute | solution.py:69
  99.9 18.6 %collective-permute-done.10 = bf16[512,1024]{1,0:T(8,128)(2,1)S(1)} collective-permute-done((bf16[512,1024]{1,0:T(8,128)(2,1)S(1)}, bf16[512,1024]{1,0:T(8,128)(2,1)S(1)}, u32[]{:S(2)}, u32[]{:S(2)}) %collective-permute-start.10) | collective-permute-done | bytes 1048608 | tf_op jit(solution)/shard_map/ppermute | solution.py:69
  118.5 4.5 %fusion.5 = f32[512,2048]{1,0:T(8,128)S(1)} fusion(bf16[8192,2048]{1,0:T(8,128)(2,1)} %param.6, s32[]{:T(128)S(6)} %select_n.90, bf16[512,1024]{1,0:T(8,128)(2,1)S(1)} %collective-permute-done.10, bf16[512,1024]{1,0:T(8,128)(2,1)S(1)} %collective-permute-done.6, pred[]{:T(512)S(6)} %or.3), kind=kOutput, calls=%fused_computation.7 | convolution fusion | flops 2148007936 | bytes 10485765 | tf_op jit(solution)/shard_map/dot_general | solution.py:88
  123.1 4.7 %fusion.4 = f32[512,2048]{1,0:T(8,128)S(1)} fusion(f32[512,2048]{1,0:T(8,128)S(1)} %fusion.5, f32[256,2048]{1,0:T(8,128)S(1)} %fusion.42, f32[256,2048]{1,0:T(8,128)S(1)} %fusion.44, f32[512,2048]{1,0:T(8,128)S(1)} %fusion.22, bf16[8192,2048]{1,0:T(8,128)(2,1)} %param.6, s32[]{:T(128)S(6)} %select_n.85, bf16[512,1024]{1,0:T(8,128)(2,1)S(1)} %collective-permute-done.5, ...), kind=kOutput, calls=%fused_computation.5 | convolution fusion | flops 2152202240 | bytes 23068676 | tf_op jit(solution)/shard_map/dot_general | solution.py:88
  127.8 7.6 %collective-permute-done.11 = bf16[512,768]{1,0:T(8,128)(2,1)S(1)} collective-permute-done((bf16[512,768]{1,0:T(8,128)(2,1)S(1)}, bf16[512,768]{1,0:T(8,128)(2,1)S(1)}, u32[]{:S(2)}, u32[]{:S(2)}) %collective-permute-start.11) | collective-permute-done | bytes 786464 | tf_op jit(solution)/shard_map/ppermute | solution.py:69
  135.4 3.7 %fusion.19 = f32[512,2048]{1,0:T(8,128)S(1)} fusion(f32[512,2048]{1,0:T(8,128)S(1)} %fusion.4, bf16[8192,2048]{1,0:T(8,128)(2,1)} %param.6, s32[]{:T(128)S(6)} %select_n.93, bf16[512,768]{1,0:T(8,128)(2,1)S(1)} %collective-permute-done.11, pred[]{:T(512)S(6)} %or.3, bf16[512,1024]{1,0:T(8,128)(2,1)S(1)} %collective-permute-done.9), kind=kOutput, calls=%fused_computation.17 | convolution fusion | flops 1612054528 | bytes 13107205 | tf_op jit(solution)/shard_map/dot_general | solution.py:88
  140.2 3.3 %add_convert_fusion = bf16[512,2048]{1,0:T(8,128)(2,1)} fusion(f32[512,2048]{1,0:T(8,128)S(1)} %fusion.19, bf16[8192,2048]{1,0:T(8,128)(2,1)} %param.6, s32[]{:T(128)S(6)} %select_n.96, bf16[512,256]{1,0:T(8,128)(2,1)S(1)} %collective-permute-done.12, pred[]{:T(512)S(6)} %or.3, bf16[512,1024]{1,0:T(8,128)(2,1)S(1)} %collective-permute-done.9), kind=kOutput, calls=%fused_computation.6 | convolution fusion | flops 539099136 | bytes 7864325 | tf_op jit(solution)/shard_map/dot_general | solution.py:88
  (28 shorter events, 10.9 us)
Async XLA Ops:
  0.0 99.0 %copy-start = (bf16[4,64,2048]{2,1,0:T(8,128)(2,1)S(1)}, bf16[4,64,2048]{2,1,0:T(8,128)(2,1)}, u32[]{:S(2)}) copy-start(bf16[4,64,2048]{2,1,0:T(8,128)(2,1)} %param.8) | copy-start | bytes 3145732
  0.0 15.3 %copy-start.1 = (bf16[2,256,2048]{2,1,0:T(8,128)(2,1)S(1)}, bf16[2,256,2048]{2,1,0:T(8,128)(2,1)}, u32[]{:S(2)}) copy-start(bf16[2,256,2048]{2,1,0:T(8,128)(2,1)} %param.5) | copy-start | bytes 6291460
  0.0 49.8 %collective-permute-start = (bf16[512,2048]{1,0:T(8,128)(2,1)}, bf16[512,2048]{1,0:T(8,128)(2,1)}, u32[]{:S(2)}, u32[]{:S(2)}) collective-permute-start(bf16[512,2048]{1,0:T(8,128)(2,1)} %bitcast.39), channel_id=1, source_target_pairs={{0,4},{12,8},{4,0},{8,12},{1,5},{13,9},{5,1},{9,13},{2,6},{14,10},... | collective-permute-start | bytes 6291464 | tf_op jit(solution)/shard_map/ppermute | solution.py:69
  5.3 27.8 %collective-permute-start.3 = (bf16[512,1024]{1,0:T(8,128)(2,1)}, bf16[512,1024]{1,0:T(8,128)(2,1)}, u32[]{:S(2)}, u32[]{:S(2)}) collective-permute-start(bf16[512,1024]{1,0:T(8,128)(2,1)} %slice.62), channel_id=1, source_target_pairs={{4,8},{8,4},{5,9},{9,5},{6,10},{10,6},{7,11},{11,7},{20,24},{24,20... | collective-permute-start | bytes 3145736 | tf_op jit(solution)/shard_map/ppermute | solution.py:69
  16.5 17.9 %collective-permute-start.2 = (bf16[512,1024]{1,0:T(8,128)(2,1)}, bf16[512,1024]{1,0:T(8,128)(2,1)}, u32[]{:S(2)}, u32[]{:S(2)}) collective-permute-start(bf16[512,1024]{1,0:T(8,128)(2,1)} %slice.52), channel_id=1, source_target_pairs={{4,8},{8,4},{5,9},{9,5},{6,10},{10,6},{7,11},{11,7},{20,24},{24,20... | collective-permute-start | bytes 3145736 | tf_op jit(solution)/shard_map/ppermute | solution.py:69
  18.2 31.3 %collective-permute-start.1 = (bf16[512,64]{0,1:T(8,128)(2,1)S(1)}, bf16[512,64]{0,1:T(8,128)(2,1)S(1)}, u32[]{:S(2)}, u32[]{:S(2)}) collective-permute-start(bf16[512,64]{0,1:T(8,128)(2,1)S(1)} %get-tuple-element.28), channel_id=1, source_target_pairs={{0,4},{12,8},{1,5},{13,9},{2,6},{14,10},{3,7},{15,11},{16,20},{28,... | collective-permute-start | bytes 196616 | tf_op jit(solution)/shard_map/ppermute | solution.py:69
  33.2 39.0 %collective-permute-start.4 = (bf16[512,1024]{1,0:T(8,128)(2,1)}, bf16[512,1024]{1,0:T(8,128)(2,1)S(1)}, u32[]{:S(2)}, u32[]{:S(2)}) collective-permute-start(bf16[512,1024]{1,0:T(8,128)(2,1)} %collective-permute-done.3), channel_id=1, source_target_pairs={{4,0},{8,12},{5,1},{9,13},{6,2},{10,14},{7,3},{11,15},{20,16},{24,... | collective-permute-start | bytes 3145736 | tf_op jit(solution)/shard_map/ppermute | solution.py:69
  34.5 88.6 %collective-permute-start.5 = (bf16[512,1024]{1,0:T(8,128)(2,1)}, bf16[512,1024]{1,0:T(8,128)(2,1)S(1)}, u32[]{:S(2)}, u32[]{:S(2)}) collective-permute-start(bf16[512,1024]{1,0:T(8,128)(2,1)} %collective-permute-done.2), channel_id=1, source_target_pairs={{4,0},{8,12},{5,1},{9,13},{6,2},{10,14},{7,3},{11,15},{20,16},{24,... | collective-permute-start | bytes 3145736 | tf_op jit(solution)/shard_map/ppermute | solution.py:69
  51.1 11.1 %collective-permute-start.6 = (bf16[512,1024]{1,0:T(8,128)(2,1)S(1)}, bf16[512,1024]{1,0:T(8,128)(2,1)S(1)}, u32[]{:S(2)}, u32[]{:S(2)}) collective-permute-start(bf16[512,1024]{1,0:T(8,128)(2,1)S(1)} %slice.54), channel_id=1, source_target_pairs={{4,8},{8,4},{5,9},{9,5},{6,10},{10,6},{7,11},{11,7},{20,24},{24,20... | collective-permute-start | bytes 3145736 | tf_op jit(solution)/shard_map/ppermute | solution.py:69
  51.9 12.4 %collective-permute-start.7 = (bf16[2,512,64]{1,2,0:T(8,128)(2,1)S(1)}, bf16[2,512,64]{1,2,0:T(8,128)(2,1)S(1)}, u32[]{:S(2)}, u32[]{:S(2)}) collective-permute-start(bf16[2,512,64]{1,2,0:T(8,128)(2,1)S(1)} %pad_maximum_fusion), channel_id=1, source_target_pairs={{4,8},{8,4},{5,9},{9,5},{6,10},{10,6},{7,11},{11,7},{20,24},{24,20... | collective-permute-start | bytes 393224 | tf_op jit(solution)/shard_map/ppermute | solution.py:69
  63.6 32.5 %collective-permute-start.9 = (bf16[512,1024]{1,0:T(8,128)(2,1)S(1)}, bf16[512,1024]{1,0:T(8,128)(2,1)S(1)}, u32[]{:S(2)}, u32[]{:S(2)}) collective-permute-start(bf16[512,1024]{1,0:T(8,128)(2,1)S(1)} %slice.57), channel_id=1, source_target_pairs={{4,8},{8,4},{5,9},{9,5},{6,10},{10,6},{7,11},{11,7},{20,24},{24,20... | collective-permute-start | bytes 3145736 | tf_op jit(solution)/shard_map/ppermute | solution.py:69
  64.3 31.7 %collective-permute-start.8 = (bf16[512,64]{0,1:T(8,128)(2,1)S(1)}, bf16[512,64]{0,1:T(8,128)(2,1)S(1)}, u32[]{:S(2)}, u32[]{:S(2)}) collective-permute-start(bf16[512,64]{0,1:T(8,128)(2,1)S(1)} %fusion.54), channel_id=1, source_target_pairs={{4,0},{8,12},{5,1},{9,13},{6,2},{10,14},{7,3},{11,15},{20,16},{24,... | collective-permute-start | bytes 196616 | tf_op jit(solution)/shard_map/ppermute | solution.py:69
  65.6 52.9 %collective-permute-start.10 = (bf16[512,1024]{1,0:T(8,128)(2,1)S(1)}, bf16[512,1024]{1,0:T(8,128)(2,1)S(1)}, u32[]{:S(2)}, u32[]{:S(2)}) collective-permute-start(bf16[512,1024]{1,0:T(8,128)(2,1)S(1)} %collective-permute-done.6), channel_id=1, source_target_pairs={{4,0},{8,12},{5,1},{9,13},{6,2},{10,14},{7,3},{11,15},{20,16},{24,... | collective-permute-start | bytes 3145736 | tf_op jit(solution)/shard_map/ppermute | solution.py:69
  96.2 39.2 %collective-permute-start.11 = (bf16[512,768]{1,0:T(8,128)(2,1)S(1)}, bf16[512,768]{1,0:T(8,128)(2,1)S(1)}, u32[]{:S(2)}, u32[]{:S(2)}) collective-permute-start(bf16[512,768]{1,0:T(8,128)(2,1)S(1)} %slice.60), channel_id=1, source_target_pairs={{4,0},{8,12},{5,1},{9,13},{6,2},{10,14},{7,3},{11,15},{20,16},{24,... | collective-permute-start | bytes 2359304 | tf_op jit(solution)/shard_map/ppermute | solution.py:69
  97.5 42.7 %collective-permute-start.12 = (bf16[512,256]{1,0:T(8,128)(2,1)S(1)}, bf16[512,256]{1,0:T(8,128)(2,1)S(1)}, u32[]{:S(2)}, u32[]{:S(2)}) collective-permute-start(bf16[512,256]{1,0:T(8,128)(2,1)S(1)} %slice.61), channel_id=1, source_target_pairs={{4,0},{8,12},{5,1},{9,13},{6,2},{10,14},{7,3},{11,15},{20,16},{24,... | collective-permute-start | bytes 786440 | tf_op jit(solution)/shard_map/ppermute | solution.py:69

commit v12 on v11

--- a/solution.py
+++ b/solution.py
@@ -95,7 +95,7 @@
     total = product(own, here)
 
     mid_out = [send(after(mid[0], total), OUTWARD)]
-    mate, mate_partial = lax.optimization_barrier((mate, mate_partial, mid[1], total))[:2]
+    mate, mate_partial = lax.optimization_barrier((mate, mate_partial, mid[0], total))[:2]
     both = send(jnp.stack([partial, mate_partial]), ACROSS)
     end = [send(mate[:, :half], ACROSS)]
     end.append(send(after(mate, end[0])[:, half:], ACROSS))

time: 144 us -> 144 us (level)
  no operation moved by 1% of the time
where the time goes in v12:
time: 144 us; the launch traced here: 143 us
  waiting for transfers between devices  66 us (46%)
  matrix products  44.2 us (31%)
  starting transfers between devices  22 us (15%)
  local copies, waits for them, and re-layouts  7.43 us (5%)
  between operations  3.78 us (3%)
    ppermute x13, waiting for transfers between devices, send(): return lax.ppermute(block, 'tensor', pairs)  66 us
    dot_general x7, matrix products, product(): return jnp.dot(block, part, preferred_element_type=F32)  39.8 us
    ppermute x13, starting transfers between devices, send(): return lax.ppermute(block, 'tensor', pairs)  22 us
    dot_general x2, matrix products, shrink(): jnp.dot(inputs[c], shrink_table[adapter_ids[c]], preferred_element_type=F32)  3.52 us
  transfers between devices with their start and end apart: 13, of which 7 were waited for; matrix products, arithmetic and copies ran while one was open for 34% of the time, Pallas kernels for 0%

profile of v12, /device:TPU:0, one launch (start us, length us, event | category | flops | bytes accessed | tf_op | source)
XLA Modules:
  0.0 143.4 jit_solution(3708193133736326745)
XLA Ops:
  0.0 3.0 %collective-permute-start = (bf16[512,2048]{1,0:T(8,128)(2,1)}, bf16[512,2048]{1,0:T(8,128)(2,1)}, u32[]{:S(2)}, u32[]{:S(2)}) collective-permute-start(bf16[512,2048]{1,0:T(8,128)(2,1)} %bitcast.39), channel_id=1, source_target_pairs={{0,4},{12,8},{4,0},{8,12},{1,5},{13,9},{5,1},{9,13},{2,6},{14,10},... | collective-permute-start | bytes 6291464 | tf_op jit(solution)/shard_map/ppermute | solution.py:69
  3.0 2.3 %slice.62 = bf16[512,1024]{1,0:T(8,128)(2,1)} slice(bf16[512,2048]{1,0:T(8,128)(2,1)} %bitcast.40), slice={[0:512], [0:1024]} | slice | bytes 2097152 | tf_op jit(solution)/shard_map/slice | solution.py:91
  5.3 1.7 %collective-permute-start.2 = (bf16[512,1024]{1,0:T(8,128)(2,1)}, bf16[512,1024]{1,0:T(8,128)(2,1)}, u32[]{:S(2)}, u32[]{:S(2)}) collective-permute-start(bf16[512,1024]{1,0:T(8,128)(2,1)} %slice.62), channel_id=1, source_target_pairs={{4,8},{8,4},{5,9},{9,5},{6,10},{10,6},{7,11},{11,7},{20,24},{24,20... | collective-permute-start | bytes 3145736 | tf_op jit(solution)/shard_map/ppermute | solution.py:69
  11.8 1.8 %fusion.27 = bf16[256,64]{0,1:T(8,128)(2,1)S(1)} fusion(bf16[2,256,2048]{2,1,0:T(8,128)(2,1)} %param.5, bf16[4,2048,64]{1,2,0:T(8,128)(2,1)} %param.7, s32[]{:T(128)S(6)} %select_n.77), kind=kOutput, calls=%fused_computation.21 | convolution fusion | flops 67125248 | bytes 1343492 | tf_op jit(solution)/shard_map/dot_general | solution.py:12
  13.6 1.8 %fusion.28 = bf16[256,64]{0,1:T(8,128)(2,1)S(1)} fusion(bf16[2,256,2048]{2,1,0:T(8,128)(2,1)} %param.5, bf16[4,2048,64]{1,2,0:T(8,128)(2,1)} %param.7, s32[]{:T(128)S(6)} %select_n.78), kind=kOutput, calls=%fused_computation.22 | convolution fusion | flops 67125248 | bytes 1343492 | tf_op jit(solution)/shard_map/dot_general | solution.py:12
  16.5 1.7 %collective-permute-start.4 = (bf16[512,1024]{1,0:T(8,128)(2,1)}, bf16[512,1024]{1,0:T(8,128)(2,1)}, u32[]{:S(2)}, u32[]{:S(2)}) collective-permute-start(bf16[512,1024]{1,0:T(8,128)(2,1)} %slice.53), channel_id=1, source_target_pairs={{4,8},{8,4},{5,9},{9,5},{6,10},{10,6},{7,11},{11,7},{20,24},{24,20... | collective-permute-start | bytes 3145736 | tf_op jit(solution)/shard_map/ppermute | solution.py:69
  18.2 5.5 %collective-permute-start.1 = (bf16[512,64]{0,1:T(8,128)(2,1)S(1)}, bf16[512,64]{0,1:T(8,128)(2,1)S(1)}, u32[]{:S(2)}, u32[]{:S(2)}) collective-permute-start(bf16[512,64]{0,1:T(8,128)(2,1)S(1)} %get-tuple-element.28), channel_id=1, source_target_pairs={{0,4},{12,8},{1,5},{13,9},{2,6},{14,10},{3,7},{15,11},{16,20},{28,... | collective-permute-start | bytes 196616 | tf_op jit(solution)/shard_map/ppermute | solution.py:69
  23.8 9.4 %fusion.11 = f32[512,2048]{1,0:T(8,128)} fusion(bf16[512,2048]{1,0:T(8,128)(2,1)S(1)} %bitcast.42, bf16[8192,2048]{1,0:T(8,128)(2,1)} %param.6, s32[]{:T(128)S(6)} %select_n.76), kind=kOutput, calls=%fused_computation.13 | convolution fusion | flops 4294967296 | bytes 14680068 | tf_op jit(solution)/shard_map/dot_general | solution.py:88
  34.5 1.3 collective-permute-start.5
  35.8 13.8 %collective-permute-done.1 = bf16[512,64]{0,1:T(8,128)(2,1)S(1)} collective-permute-done((bf16[512,64]{0,1:T(8,128)(2,1)S(1)}, bf16[512,64]{0,1:T(8,128)(2,1)S(1)}, u32[]{:S(2)}, u32[]{:S(2)}) %collective-permute-start.1) | collective-permute-done | bytes 65568 | tf_op jit(solution)/shard_map/ppermute | solution.py:69
  49.8 1.3 slice.54
  52.6 9.7 %fusion.16 = f32[512,2048]{1,0:T(8,128)S(1)} fusion(f32[512,2048]{1,0:T(8,128)} %fusion.11, bf16[512,2048]{1,0:T(8,128)(2,1)} %collective-permute-done, bf16[8192,2048]{1,0:T(8,128)(2,1)} %param.6, s32[]{:T(128)S(6)} %select_n.79), kind=kOutput, calls=%fused_computation.16 | convolution fusion | flops 4296015872 | bytes 18874372 | tf_op jit(solution)/shard_map/dot_general | solution.py:88
  62.3 1.3 slice.57
  64.3 1.3 collective-permute-start.8
  66.9 5.3 %collective-permute-done.3 = bf16[512,1024]{1,0:T(8,128)(2,1)S(1)} collective-permute-done((bf16[512,1024]{1,0:T(8,128)(2,1)}, bf16[512,1024]{1,0:T(8,128)(2,1)S(1)}, u32[]{:S(2)}, u32[]{:S(2)}) %collective-permute-start.3) | collective-permute-done | bytes 1048608 | tf_op jit(solution)/shard_map/ppermute | solution.py:69
  72.2 4.5 %fusion.22 = f32[512,2048]{1,0:T(8,128)S(1)} fusion(f32[512,2048]{1,0:T(8,128)S(1)} %fusion.16, bf16[8192,2048]{1,0:T(8,128)(2,1)} %param.6, s32[]{:T(128)S(6)} %select_n.83, bf16[512,1024]{1,0:T(8,128)(2,1)S(1)} %collective-permute-done.3, bf16[512,1024]{1,0:T(8,128)(2,1)} %collective-permute-done.2, pred[]{:T(512)S(6)} %or.3), kind=kOutput, calls=%fused_computation.18 | convolution fusion | flops 2149056512 | bytes 14680069 | tf_op jit(solution)/shard_map/dot_general | solution.py:88
  76.7 19.3 %collective-permute-done.8 = bf16[512,64]{0,1:T(8,128)(2,1)S(1)} collective-permute-done((bf16[512,64]{0,1:T(8,128)(2,1)S(1)}, bf16[512,64]{0,1:T(8,128)(2,1)S(1)}, u32[]{:S(2)}, u32[]{:S(2)}) %collective-permute-start.8) | collective-permute-done | bytes 65568 | tf_op jit(solution)/shard_map/ppermute | solution.py:69
  97.5 1.5 %collective-permute-start.12 = (bf16[512,256]{1,0:T(8,128)(2,1)S(1)}, bf16[512,256]{1,0:T(8,128)(2,1)S(1)}, u32[]{:S(2)}, u32[]{:S(2)}) collective-permute-start(bf16[512,256]{1,0:T(8,128)(2,1)S(1)} %slice.61), channel_id=1, source_target_pairs={{4,0},{8,12},{5,1},{9,13},{6,2},{10,14},{7,3},{11,15},{20,16},{24,... | collective-permute-start | bytes 786440 | tf_op jit(solution)/shard_map/ppermute | solution.py:69
  99.9 18.6 %collective-permute-done.10 = bf16[512,1024]{1,0:T(8,128)(2,1)S(1)} collective-permute-done((bf16[512,1024]{1,0:T(8,128)(2,1)S(1)}, bf16[512,1024]{1,0:T(8,128)(2,1)S(1)}, u32[]{:S(2)}, u32[]{:S(2)}) %collective-permute-start.10) | collective-permute-done | bytes 1048608 | tf_op jit(solution)/shard_map/ppermute | solution.py:69
  118.5 4.5 %fusion.5 = f32[512,2048]{1,0:T(8,128)S(1)} fusion(bf16[8192,2048]{1,0:T(8,128)(2,1)} %param.6, s32[]{:T(128)S(6)} %select_n.90, bf16[512,1024]{1,0:T(8,128)(2,1)S(1)} %collective-permute-done.10, bf16[512,1024]{1,0:T(8,128)(2,1)S(1)} %collective-permute-done.6, pred[]{:T(512)S(6)} %or.3), kind=kOutput, calls=%fused_computation.7 | convolution fusion | flops 2148007936 | bytes 10485765 | tf_op jit(solution)/shard_map/dot_general | solution.py:88
  123.1 4.7 %fusion.4 = f32[512,2048]{1,0:T(8,128)S(1)} fusion(f32[512,2048]{1,0:T(8,128)S(1)} %fusion.5, f32[256,2048]{1,0:T(8,128)S(1)} %fusion.42, f32[256,2048]{1,0:T(8,128)S(1)} %fusion.44, f32[512,2048]{1,0:T(8,128)S(1)} %fusion.22, bf16[8192,2048]{1,0:T(8,128)(2,1)} %param.6, s32[]{:T(128)S(6)} %select_n.85, bf16[512,1024]{1,0:T(8,128)(2,1)S(1)} %collective-permute-done.5, ...), kind=kOutput, calls=%fused_computation.5 | convolution fusion | flops 2152202240 | bytes 23068676 | tf_op jit(solution)/shard_map/dot_general | solution.py:88
  127.8 7.6 %collective-permute-done.11 = bf16[512,768]{1,0:T(8,128)(2,1)S(1)} collective-permute-done((bf16[512,768]{1,0:T(8,128)(2,1)S(1)}, bf16[512,768]{1,0:T(8,128)(2,1)S(1)}, u32[]{:S(2)}, u32[]{:S(2)}) %collective-permute-start.11) | collective-permute-done | bytes 786464 | tf_op jit(solution)/shard_map/ppermute | solution.py:69
  135.4 3.7 %fusion.19 = f32[512,2048]{1,0:T(8,128)S(1)} fusion(f32[512,2048]{1,0:T(8,128)S(1)} %fusion.4, bf16[8192,2048]{1,0:T(8,128)(2,1)} %param.6, s32[]{:T(128)S(6)} %select_n.93, bf16[512,768]{1,0:T(8,128)(2,1)S(1)} %collective-permute-done.11, pred[]{:T(512)S(6)} %or.3, bf16[512,1024]{1,0:T(8,128)(2,1)S(1)} %collective-permute-done.9), kind=kOutput, calls=%fused_computation.17 | convolution fusion | flops 1612054528 | bytes 13107205 | tf_op jit(solution)/shard_map/dot_general | solution.py:88
  140.2 3.3 %add_convert_fusion = bf16[512,2048]{1,0:T(8,128)(2,1)} fusion(f32[512,2048]{1,0:T(8,128)S(1)} %fusion.19, bf16[8192,2048]{1,0:T(8,128)(2,1)} %param.6, s32[]{:T(128)S(6)} %select_n.96, bf16[512,256]{1,0:T(8,128)(2,1)S(1)} %collective-permute-done.12, pred[]{:T(512)S(6)} %or.3, bf16[512,1024]{1,0:T(8,128)(2,1)S(1)} %collective-permute-done.9), kind=kOutput, calls=%fused_computation.6 | convolution fusion | flops 539099136 | bytes 7864325 | tf_op jit(solution)/shard_map/dot_general | solution.py:88
  (28 shorter events, 10.9 us)
Async XLA Ops:
  0.0 99.0 %copy-start = (bf16[4,64,2048]{2,1,0:T(8,128)(2,1)S(1)}, bf16[4,64,2048]{2,1,0:T(8,128)(2,1)}, u32[]{:S(2)}) copy-start(bf16[4,64,2048]{2,1,0:T(8,128)(2,1)} %param.8) | copy-start | bytes 3145732
  0.0 15.3 %copy-start.1 = (bf16[2,256,2048]{2,1,0:T(8,128)(2,1)S(1)}, bf16[2,256,2048]{2,1,0:T(8,128)(2,1)}, u32[]{:S(2)}) copy-start(bf16[2,256,2048]{2,1,0:T(8,128)(2,1)} %param.5) | copy-start | bytes 6291460
  0.0 49.8 %collective-permute-start = (bf16[512,2048]{1,0:T(8,128)(2,1)}, bf16[512,2048]{1,0:T(8,128)(2,1)}, u32[]{:S(2)}, u32[]{:S(2)}) collective-permute-start(bf16[512,2048]{1,0:T(8,128)(2,1)} %bitcast.39), channel_id=1, source_target_pairs={{0,4},{12,8},{4,0},{8,12},{1,5},{13,9},{5,1},{9,13},{2,6},{14,10},... | collective-permute-start | bytes 6291464 | tf_op jit(solution)/shard_map/ppermute | solution.py:69
  5.3 27.8 %collective-permute-start.2 = (bf16[512,1024]{1,0:T(8,128)(2,1)}, bf16[512,1024]{1,0:T(8,128)(2,1)}, u32[]{:S(2)}, u32[]{:S(2)}) collective-permute-start(bf16[512,1024]{1,0:T(8,128)(2,1)} %slice.62), channel_id=1, source_target_pairs={{4,8},{8,4},{5,9},{9,5},{6,10},{10,6},{7,11},{11,7},{20,24},{24,20... | collective-permute-start | bytes 3145736 | tf_op jit(solution)/shard_map/ppermute | solution.py:69
  16.5 17.9 %collective-permute-start.4 = (bf16[512,1024]{1,0:T(8,128)(2,1)}, bf16[512,1024]{1,0:T(8,128)(2,1)}, u32[]{:S(2)}, u32[]{:S(2)}) collective-permute-start(bf16[512,1024]{1,0:T(8,128)(2,1)} %slice.53), channel_id=1, source_target_pairs={{4,8},{8,4},{5,9},{9,5},{6,10},{10,6},{7,11},{11,7},{20,24},{24,20... | collective-permute-start | bytes 3145736 | tf_op jit(solution)/shard_map/ppermute | solution.py:69
  18.2 31.3 %collective-permute-start.1 = (bf16[512,64]{0,1:T(8,128)(2,1)S(1)}, bf16[512,64]{0,1:T(8,128)(2,1)S(1)}, u32[]{:S(2)}, u32[]{:S(2)}) collective-permute-start(bf16[512,64]{0,1:T(8,128)(2,1)S(1)} %get-tuple-element.28), channel_id=1, source_target_pairs={{0,4},{12,8},{1,5},{13,9},{2,6},{14,10},{3,7},{15,11},{16,20},{28,... | collective-permute-start | bytes 196616 | tf_op jit(solution)/shard_map/ppermute | solution.py:69
  33.2 39.0 %collective-permute-start.3 = (bf16[512,1024]{1,0:T(8,128)(2,1)}, bf16[512,1024]{1,0:T(8,128)(2,1)S(1)}, u32[]{:S(2)}, u32[]{:S(2)}) collective-permute-start(bf16[512,1024]{1,0:T(8,128)(2,1)} %collective-permute-done.2), channel_id=1, source_target_pairs={{4,0},{8,12},{5,1},{9,13},{6,2},{10,14},{7,3},{11,15},{20,16},{24,... | collective-permute-start | bytes 3145736 | tf_op jit(solution)/shard_map/ppermute | solution.py:69
  34.5 88.6 %collective-permute-start.5 = (bf16[512,1024]{1,0:T(8,128)(2,1)}, bf16[512,1024]{1,0:T(8,128)(2,1)S(1)}, u32[]{:S(2)}, u32[]{:S(2)}) collective-permute-start(bf16[512,1024]{1,0:T(8,128)(2,1)} %collective-permute-done.4), channel_id=1, source_target_pairs={{4,0},{8,12},{5,1},{9,13},{6,2},{10,14},{7,3},{11,15},{20,16},{24,... | collective-permute-start | bytes 3145736 | tf_op jit(solution)/shard_map/ppermute | solution.py:69
  51.1 11.1 %collective-permute-start.6 = (bf16[512,1024]{1,0:T(8,128)(2,1)S(1)}, bf16[512,1024]{1,0:T(8,128)(2,1)S(1)}, u32[]{:S(2)}, u32[]{:S(2)}) collective-permute-start(bf16[512,1024]{1,0:T(8,128)(2,1)S(1)} %slice.54), channel_id=1, source_target_pairs={{4,8},{8,4},{5,9},{9,5},{6,10},{10,6},{7,11},{11,7},{20,24},{24,20... | collective-permute-start | bytes 3145736 | tf_op jit(solution)/shard_map/ppermute | solution.py:69
  51.9 12.4 %collective-permute-start.7 = (bf16[2,512,64]{1,2,0:T(8,128)(2,1)S(1)}, bf16[2,512,64]{1,2,0:T(8,128)(2,1)S(1)}, u32[]{:S(2)}, u32[]{:S(2)}) collective-permute-start(bf16[2,512,64]{1,2,0:T(8,128)(2,1)S(1)} %pad_maximum_fusion), channel_id=1, source_target_pairs={{4,8},{8,4},{5,9},{9,5},{6,10},{10,6},{7,11},{11,7},{20,24},{24,20... | collective-permute-start | bytes 393224 | tf_op jit(solution)/shard_map/ppermute | solution.py:69
  63.6 32.5 %collective-permute-start.9 = (bf16[512,1024]{1,0:T(8,128)(2,1)S(1)}, bf16[512,1024]{1,0:T(8,128)(2,1)S(1)}, u32[]{:S(2)}, u32[]{:S(2)}) collective-permute-start(bf16[512,1024]{1,0:T(8,128)(2,1)S(1)} %slice.57), channel_id=1, source_target_pairs={{4,8},{8,4},{5,9},{9,5},{6,10},{10,6},{7,11},{11,7},{20,24},{24,20... | collective-permute-start | bytes 3145736 | tf_op jit(solution)/shard_map/ppermute | solution.py:69
  64.3 31.7 %collective-permute-start.8 = (bf16[512,64]{0,1:T(8,128)(2,1)S(1)}, bf16[512,64]{0,1:T(8,128)(2,1)S(1)}, u32[]{:S(2)}, u32[]{:S(2)}) collective-permute-start(bf16[512,64]{0,1:T(8,128)(2,1)S(1)} %fusion.54), channel_id=1, source_target_pairs={{4,0},{8,12},{5,1},{9,13},{6,2},{10,14},{7,3},{11,15},{20,16},{24,... | collective-permute-start | bytes 196616 | tf_op jit(solution)/shard_map/ppermute | solution.py:69
  65.6 52.9 %collective-permute-start.10 = (bf16[512,1024]{1,0:T(8,128)(2,1)S(1)}, bf16[512,1024]{1,0:T(8,128)(2,1)S(1)}, u32[]{:S(2)}, u32[]{:S(2)}) collective-permute-start(bf16[512,1024]{1,0:T(8,128)(2,1)S(1)} %collective-permute-done.6), channel_id=1, source_target_pairs={{4,0},{8,12},{5,1},{9,13},{6,2},{10,14},{7,3},{11,15},{20,16},{24,... | collective-permute-start | bytes 3145736 | tf_op jit(solution)/shard_map/ppermute | solution.py:69
  96.2 39.2 %collective-permute-start.11 = (bf16[512,768]{1,0:T(8,128)(2,1)S(1)}, bf16[512,768]{1,0:T(8,128)(2,1)S(1)}, u32[]{:S(2)}, u32[]{:S(2)}) collective-permute-start(bf16[512,768]{1,0:T(8,128)(2,1)S(1)} %slice.60), channel_id=1, source_target_pairs={{4,0},{8,12},{5,1},{9,13},{6,2},{10,14},{7,3},{11,15},{20,16},{24,... | collective-permute-start | bytes 2359304 | tf_op jit(solution)/shard_map/ppermute | solution.py:69
  97.5 42.7 %collective-permute-start.12 = (bf16[512,256]{1,0:T(8,128)(2,1)S(1)}, bf16[512,256]{1,0:T(8,128)(2,1)S(1)}, u32[]{:S(2)}, u32[]{:S(2)}) collective-permute-start(bf16[512,256]{1,0:T(8,128)(2,1)S(1)} %slice.61), channel_id=1, source_target_pairs={{4,0},{8,12},{5,1},{9,13},{6,2},{10,14},{7,3},{11,15},{20,16},{24,... | collective-permute-start | bytes 786440 | tf_op jit(solution)/shard_map/ppermute | solution.py:69

commit v13 on v12

--- a/solution.py
+++ b/solution.py
@@ -96,11 +96,12 @@
 
     mid_out = [send(after(mid[0], total), OUTWARD)]
     mate, mate_partial = lax.optimization_barrier((mate, mate_partial, mid[0], total))[:2]
+    first, second = mate[:, :half], mate[:, half:]
     both = send(jnp.stack([partial, mate_partial]), ACROSS)
-    end = [send(mate[:, :half], ACROSS)]
-    end.append(send(after(mate, end[0])[:, half:], ACROSS))
-    mid_out.append(send(mid[1], OUTWARD))
+    end = [send(first, ACROSS)]
+    mid_out.append(send(after(mid[1], first), OUTWARD))
     total = total + product(mate, here ^ 1)
+    end.append(send(after(second, total), ACROSS))
 
     end[0], both = lax.optimization_barrier((end[0], both, total))[:2]
     end_out = [send(end[0], OUTWARD)]

time: 144 us -> 169 us (1.17)
  waiting for transfers between devices: 66 us -> 87.2 us
  matrix products: 44.2 us -> 48 us
    ppermute x13, waiting for transfers between devices: 66 us -> 87.2 us  [send(): return lax.ppermute(block, 'tensor', pairs)]
    dot_general x7, matrix products: 39.8 us -> 43.5 us  [product(): return jnp.dot(block, part, preferred_element_type=F32)]
  transfers between devices with their start and end apart: 13 -> 13, of which waited for: 7 -> 7; matrix products, arithmetic and copies ran while one was open for 34% -> 31% of each run, Pallas kernels for 0% -> 0%
where the time goes in v13:
time: 169 us
  waiting for transfers between devices  87.2 us (52%)
  matrix products  48 us (28%)
  starting transfers between devices  21.7 us (13%)
  local copies, waits for them, and re-layouts  7.91 us (5%)
  between operations  3.94 us (2%)
    ppermute x13, waiting for transfers between devices, send(): return lax.ppermute(block, 'tensor', pairs)  87.2 us
    dot_general x7, matrix products, product(): return jnp.dot(block, part, preferred_element_type=F32)  43.5 us
    ppermute x13, starting transfers between devices, send(): return lax.ppermute(block, 'tensor', pairs)  21.7 us
    dot_general x2, matrix products, shrink(): jnp.dot(inputs[c], shrink_table[adapter_ids[c]], preferred_element_type=F32)  3.52 us
  transfers between devices with their start and end apart: 13, of which 7 were waited for; matrix products, arithmetic and copies ran while one was open for 31% of the time, Pallas kernels for 0%

profile of v13, /device:TPU:0, one launch (start us, length us, event | category | flops | bytes accessed | tf_op | source)
XLA Modules:
  0.0 168.8 jit_solution(16593341745807253601)
XLA Ops:
  0.0 3.0 %collective-permute-start = (bf16[512,2048]{1,0:T(8,128)(2,1)}, bf16[512,2048]{1,0:T(8,128)(2,1)}, u32[]{:S(2)}, u32[]{:S(2)}) collective-permute-start(bf16[512,2048]{1,0:T(8,128)(2,1)} %bitcast.39), channel_id=1, source_target_pairs={{0,4},{12,8},{4,0},{8,12},{1,5},{13,9},{5,1},{9,13},{2,6},{14,10},... | collective-permute-start | bytes 6291464 | tf_op jit(solution)/shard_map/ppermute | solution.py:69
  3.0 2.3 %slice.62 = bf16[512,1024]{1,0:T(8,128)(2,1)} slice(bf16[512,2048]{1,0:T(8,128)(2,1)} %bitcast.40), slice={[0:512], [0:1024]} | slice | bytes 2097152 | tf_op jit(solution)/shard_map/slice | solution.py:91
  5.3 1.7 collective-permute-start.2
  7.0 1.4 fusion.72
  12.1 1.8 %fusion.27 = bf16[256,64]{0,1:T(8,128)(2,1)S(1)} fusion(bf16[2,256,2048]{2,1,0:T(8,128)(2,1)} %param.5, bf16[4,2048,64]{1,2,0:T(8,128)(2,1)} %param.7, s32[]{:T(128)S(6)} %select_n.77), kind=kOutput, calls=%fused_computation.21 | convolution fusion | flops 67125248 | bytes 1343492 | tf_op jit(solution)/shard_map/dot_general | solution.py:12
  13.8 1.8 %fusion.28 = bf16[256,64]{0,1:T(8,128)(2,1)S(1)} fusion(bf16[2,256,2048]{2,1,0:T(8,128)(2,1)} %param.5, bf16[4,2048,64]{1,2,0:T(8,128)(2,1)} %param.7, s32[]{:T(128)S(6)} %select_n.78), kind=kOutput, calls=%fused_computation.22 | convolution fusion | flops 67125248 | bytes 1343492 | tf_op jit(solution)/shard_map/dot_general | solution.py:12
  15.6 5.3 %collective-permute-start.1 = (bf16[512,64]{0,1:T(8,128)(2,1)S(1)}, bf16[512,64]{0,1:T(8,128)(2,1)S(1)}, u32[]{:S(2)}, u32[]{:S(2)}) collective-permute-start(bf16[512,64]{0,1:T(8,128)(2,1)S(1)} %get-tuple-element.32), channel_id=1, source_target_pairs={{0,4},{12,8},{1,5},{13,9},{2,6},{14,10},{3,7},{15,11},{16,20},{28,... | collective-permute-start | bytes 196616 | tf_op jit(solution)/shard_map/ppermute | solution.py:69
  22.0 1.7 %collective-permute-start.4 = (bf16[512,1024]{1,0:T(8,128)(2,1)}, bf16[512,1024]{1,0:T(8,128)(2,1)}, u32[]{:S(2)}, u32[]{:S(2)}) collective-permute-start(bf16[512,1024]{1,0:T(8,128)(2,1)} %slice.53), channel_id=1, source_target_pairs={{4,8},{8,4},{5,9},{9,5},{6,10},{10,6},{7,11},{11,7},{20,24},{24,20... | collective-permute-start | bytes 3145736 | tf_op jit(solution)/shard_map/ppermute | solution.py:69
  23.7 9.4 %fusion.11 = f32[512,2048]{1,0:T(8,128)} fusion(bf16[512,2048]{1,0:T(8,128)(2,1)S(1)} %bitcast.42, bf16[8192,2048]{1,0:T(8,128)(2,1)} %param.6, s32[]{:T(128)S(6)} %select_n.76), kind=kOutput, calls=%fused_computation.13 | convolution fusion | flops 4294967296 | bytes 14680068 | tf_op jit(solution)/shard_map/dot_general | solution.py:88
  34.4 15.2 %collective-permute-done.1 = bf16[512,64]{0,1:T(8,128)(2,1)S(1)} collective-permute-done((bf16[512,64]{0,1:T(8,128)(2,1)S(1)}, bf16[512,64]{0,1:T(8,128)(2,1)S(1)}, u32[]{:S(2)}, u32[]{:S(2)}) %collective-permute-start.1) | collective-permute-done | bytes 65568 | tf_op jit(solution)/shard_map/ppermute | solution.py:69
  49.8 11.6 %fusion.16 = f32[512,2048]{1,0:T(8,128)} fusion(f32[512,2048]{1,0:T(8,128)} %fusion.11, bf16[512,2048]{1,0:T(8,128)(2,1)} %collective-permute-done, bf16[8192,2048]{1,0:T(8,128)(2,1)} %param.6, s32[]{:T(128)S(6)} %select_n.79), kind=kOutput, calls=%fused_computation.16 | convolution fusion | flops 4296015872 | bytes 18874372 | tf_op jit(solution)/shard_map/dot_general | solution.py:88
  61.5 3.0 %fusion.71 = (bf16[512,1024]{1,0:T(8,128)(2,1)}, bf16[512,1024]{1,0:T(8,128)(2,1)}) fusion(bf16[512,2048]{1,0:T(8,128)(2,1)} %collective-permute-done), kind=kLoop, calls=%fused_computation.70 | loop fusion | bytes 4194304 | tf_op jit(solution)/shard_map/slice | solution.py:99
  66.0 1.3 collective-permute-start.5
  68.0 3.5 %collective-permute-done.3 = bf16[512,1024]{1,0:T(8,128)(2,1)} collective-permute-done((bf16[512,1024]{1,0:T(8,128)(2,1)}, bf16[512,1024]{1,0:T(8,128)(2,1)}, u32[]{:S(2)}, u32[]{:S(2)}) %collective-permute-start.3) | collective-permute-done | bytes 1048608 | tf_op jit(solution)/shard_map/ppermute | solution.py:69
  71.5 6.1 %fusion.22 = f32[512,2048]{1,0:T(8,128)S(1)} fusion(f32[512,2048]{1,0:T(8,128)} %fusion.16, bf16[8192,2048]{1,0:T(8,128)(2,1)} %param.6, s32[]{:T(128)S(6)} %select_n.83, bf16[512,1024]{1,0:T(8,128)(2,1)} %collective-permute-done.3, bf16[512,1024]{1,0:T(8,128)(2,1)} %collective-permute-done.2, pred[]{:T(512)S(6)} %or.3), kind=kOutput, calls=%fused_computation.18 | convolution fusion | flops 2149056512 | bytes 14680069 | tf_op jit(solution)/shard_map/dot_general | solution.py:88
  81.7 1.5 collective-permute-start.12
  83.2 12.8 %collective-permute-done.5 = bf16[512,1024]{1,0:T(8,128)(2,1)} collective-permute-done((bf16[512,1024]{1,0:T(8,128)(2,1)}, bf16[512,1024]{1,0:T(8,128)(2,1)}, u32[]{:S(2)}, u32[]{:S(2)}) %collective-permute-start.5) | collective-permute-done | bytes 1048608 | tf_op jit(solution)/shard_map/ppermute | solution.py:69
  96.0 4.8 %fusion.7 = f32[512,2048]{1,0:T(8,128)S(1)} fusion(bf16[8192,2048]{1,0:T(8,128)(2,1)} %param.6, s32[]{:T(128)S(6)} %select_n.85, bf16[512,1024]{1,0:T(8,128)(2,1)} %collective-permute-done.5, bf16[512,1024]{1,0:T(8,128)(2,1)} %collective-permute-done.4, pred[]{:T(512)S(6)} %or.3), kind=kOutput, calls=%fused_computation.9 | convolution fusion | flops 2148007936 | bytes 10485765 | tf_op jit(solution)/shard_map/dot_general | solution.py:88
  100.8 21.7 %collective-permute-done.8 = bf16[512,64]{0,1:T(8,128)(2,1)S(1)} collective-permute-done((bf16[512,64]{0,1:T(8,128)(2,1)S(1)}, bf16[512,64]{0,1:T(8,128)(2,1)S(1)}, u32[]{:S(2)}, u32[]{:S(2)}) %collective-permute-start.8) | collective-permute-done | bytes 65568 | tf_op jit(solution)/shard_map/ppermute | solution.py:69
  123.4 21.5 %collective-permute-done.10 = bf16[512,1024]{1,0:T(8,128)(2,1)S(1)} collective-permute-done((bf16[512,1024]{1,0:T(8,128)(2,1)S(1)}, bf16[512,1024]{1,0:T(8,128)(2,1)S(1)}, u32[]{:S(2)}, u32[]{:S(2)}) %collective-permute-start.10) | collective-permute-done | bytes 1048608 | tf_op jit(solution)/shard_map/ppermute | solution.py:69
  145.0 4.6 %fusion.4 = f32[512,2048]{1,0:T(8,128)S(1)} fusion(f32[256,2048]{1,0:T(8,128)S(1)} %fusion.42, f32[256,2048]{1,0:T(8,128)S(1)} %fusion.44, f32[512,2048]{1,0:T(8,128)S(1)} %fusion.22, f32[512,2048]{1,0:T(8,128)S(1)} %fusion.7, bf16[8192,2048]{1,0:T(8,128)(2,1)} %param.6, s32[]{:T(128)S(6)} %select_n.90, bf16[512,1024]{1,0:T(8,128)(2,1)S(1)} %collective-permute-done.10, ...), kind=kOutput, calls=%fused_computation.5 | convolution fusion | flops 2152202240 | bytes 23068676 | tf_op jit(solution)/shard_map/dot_general | solution.py:88
  149.6 12.2 %collective-permute-done.11 = bf16[512,768]{1,0:T(8,128)(2,1)S(1)} collective-permute-done((bf16[512,768]{1,0:T(8,128)(2,1)S(1)}, bf16[512,768]{1,0:T(8,128)(2,1)S(1)}, u32[]{:S(2)}, u32[]{:S(2)}) %collective-permute-start.11) | collective-permute-done | bytes 786464 | tf_op jit(solution)/shard_map/ppermute | solution.py:69
  161.8 3.7 %fusion.19 = f32[512,2048]{1,0:T(8,128)S(1)} fusion(f32[512,2048]{1,0:T(8,128)S(1)} %fusion.4, bf16[8192,2048]{1,0:T(8,128)(2,1)} %param.6, s32[]{:T(128)S(6)} %select_n.93, bf16[512,768]{1,0:T(8,128)(2,1)S(1)} %collective-permute-done.11, pred[]{:T(512)S(6)} %or.3, bf16[512,1024]{1,0:T(8,128)(2,1)S(1)} %collective-permute-done.9), kind=kOutput, calls=%fused_computation.17 | convolution fusion | flops 1612054528 | bytes 13107205 | tf_op jit(solution)/shard_map/dot_general | solution.py:88
  165.5 3.3 %add_convert_fusion = bf16[512,2048]{1,0:T(8,128)(2,1)} fusion(f32[512,2048]{1,0:T(8,128)S(1)} %fusion.19, bf16[8192,2048]{1,0:T(8,128)(2,1)} %param.6, s32[]{:T(128)S(6)} %select_n.96, bf16[512,256]{1,0:T(8,128)(2,1)S(1)} %collective-permute-done.12, pred[]{:T(512)S(6)} %or.3, bf16[512,1024]{1,0:T(8,128)(2,1)S(1)} %collective-permute-done.9), kind=kOutput, calls=%fused_computation.6 | convolution fusion | flops 539099136 | bytes 7864325 | tf_op jit(solution)/shard_map/dot_general | solution.py:88
  (27 shorter events, 9.8 us)
Async XLA Ops:
  0.0 122.5 %copy-start = (bf16[4,64,2048]{2,1,0:T(8,128)(2,1)S(1)}, bf16[4,64,2048]{2,1,0:T(8,128)(2,1)}, u32[]{:S(2)}) copy-start(bf16[4,64,2048]{2,1,0:T(8,128)(2,1)} %param.8) | copy-start | bytes 3145732
  0.0 20.9 %copy-start.1 = (bf16[2,256,2048]{2,1,0:T(8,128)(2,1)S(1)}, bf16[2,256,2048]{2,1,0:T(8,128)(2,1)}, u32[]{:S(2)}) copy-start(bf16[2,256,2048]{2,1,0:T(8,128)(2,1)} %param.5) | copy-start | bytes 6291460
  0.0 49.8 %collective-permute-start = (bf16[512,2048]{1,0:T(8,128)(2,1)}, bf16[512,2048]{1,0:T(8,128)(2,1)}, u32[]{:S(2)}, u32[]{:S(2)}) collective-permute-start(bf16[512,2048]{1,0:T(8,128)(2,1)} %bitcast.39), channel_id=1, source_target_pairs={{0,4},{12,8},{4,0},{8,12},{1,5},{13,9},{5,1},{9,13},{2,6},{14,10},... | collective-permute-start | bytes 6291464 | tf_op jit(solution)/shard_map/ppermute | solution.py:69
  5.3 27.8 %collective-permute-start.2 = (bf16[512,1024]{1,0:T(8,128)(2,1)}, bf16[512,1024]{1,0:T(8,128)(2,1)}, u32[]{:S(2)}, u32[]{:S(2)}) collective-permute-start(bf16[512,1024]{1,0:T(8,128)(2,1)} %slice.62), channel_id=1, source_target_pairs={{4,8},{8,4},{5,9},{9,5},{6,10},{10,6},{7,11},{11,7},{20,24},{24,20... | collective-permute-start | bytes 3145736 | tf_op jit(solution)/shard_map/ppermute | solution.py:69
  15.6 33.9 %collective-permute-start.1 = (bf16[512,64]{0,1:T(8,128)(2,1)S(1)}, bf16[512,64]{0,1:T(8,128)(2,1)S(1)}, u32[]{:S(2)}, u32[]{:S(2)}) collective-permute-start(bf16[512,64]{0,1:T(8,128)(2,1)S(1)} %get-tuple-element.32), channel_id=1, source_target_pairs={{0,4},{12,8},{1,5},{13,9},{2,6},{14,10},{3,7},{15,11},{16,20},{28,... | collective-permute-start | bytes 196616 | tf_op jit(solution)/shard_map/ppermute | solution.py:69
  22.0 43.9 %collective-permute-start.4 = (bf16[512,1024]{1,0:T(8,128)(2,1)}, bf16[512,1024]{1,0:T(8,128)(2,1)}, u32[]{:S(2)}, u32[]{:S(2)}) collective-permute-start(bf16[512,1024]{1,0:T(8,128)(2,1)} %slice.53), channel_id=1, source_target_pairs={{4,8},{8,4},{5,9},{9,5},{6,10},{10,6},{7,11},{11,7},{20,24},{24,20... | collective-permute-start | bytes 3145736 | tf_op jit(solution)/shard_map/ppermute | solution.py:69
  33.1 38.4 %collective-permute-start.3 = (bf16[512,1024]{1,0:T(8,128)(2,1)}, bf16[512,1024]{1,0:T(8,128)(2,1)}, u32[]{:S(2)}, u32[]{:S(2)}) collective-permute-start(bf16[512,1024]{1,0:T(8,128)(2,1)} %collective-permute-done.2), channel_id=1, source_target_pairs={{4,0},{8,12},{5,1},{9,13},{6,2},{10,14},{7,3},{11,15},{20,16},{24,... | collective-permute-start | bytes 3145736 | tf_op jit(solution)/shard_map/ppermute | solution.py:69
  64.5 13.1 %collective-permute-start.9 = (bf16[512,1024]{1,0:T(8,128)(2,1)}, bf16[512,1024]{1,0:T(8,128)(2,1)S(1)}, u32[]{:S(2)}, u32[]{:S(2)}) collective-permute-start(bf16[512,1024]{1,0:T(8,128)(2,1)} %get-tuple-element.23), channel_id=1, source_target_pairs={{4,8},{8,4},{5,9},{9,5},{6,10},{10,6},{7,11},{11,7},{20,24},{24,20... | collective-permute-start | bytes 3145736 | tf_op jit(solution)/shard_map/ppermute | solution.py:69
  65.2 12.5 %collective-permute-start.6 = (bf16[512,1024]{1,0:T(8,128)(2,1)}, bf16[512,1024]{1,0:T(8,128)(2,1)S(1)}, u32[]{:S(2)}, u32[]{:S(2)}) collective-permute-start(bf16[512,1024]{1,0:T(8,128)(2,1)} %get-tuple-element.30), channel_id=1, source_target_pairs={{4,8},{8,4},{5,9},{9,5},{6,10},{10,6},{7,11},{11,7},{20,24},{24,20... | collective-permute-start | bytes 3145736 | tf_op jit(solution)/shard_map/ppermute | solution.py:69
  66.0 30.0 %collective-permute-start.5 = (bf16[512,1024]{1,0:T(8,128)(2,1)}, bf16[512,1024]{1,0:T(8,128)(2,1)}, u32[]{:S(2)}, u32[]{:S(2)}) collective-permute-start(bf16[512,1024]{1,0:T(8,128)(2,1)} %collective-permute-done.4), channel_id=1, source_target_pairs={{4,0},{8,12},{5,1},{9,13},{6,2},{10,14},{7,3},{11,15},{20,16},{24,... | collective-permute-start | bytes 3145736 | tf_op jit(solution)/shard_map/ppermute | solution.py:69
  67.3 10.4 %collective-permute-start.7 = (bf16[2,512,64]{1,2,0:T(8,128)(2,1)S(1)}, bf16[2,512,64]{1,2,0:T(8,128)(2,1)S(1)}, u32[]{:S(2)}, u32[]{:S(2)}) collective-permute-start(bf16[2,512,64]{1,2,0:T(8,128)(2,1)S(1)} %pad_maximum_fusion), channel_id=1, source_target_pairs={{4,8},{8,4},{5,9},{9,5},{6,10},{10,6},{7,11},{11,7},{20,24},{24,20... | collective-permute-start | bytes 393224 | tf_op jit(solution)/shard_map/ppermute | solution.py:69
  77.8 44.7 %collective-permute-start.8 = (bf16[512,64]{0,1:T(8,128)(2,1)S(1)}, bf16[512,64]{0,1:T(8,128)(2,1)S(1)}, u32[]{:S(2)}, u32[]{:S(2)}) collective-permute-start(bf16[512,64]{0,1:T(8,128)(2,1)S(1)} %fusion.54), channel_id=1, source_target_pairs={{4,0},{8,12},{5,1},{9,13},{6,2},{10,14},{7,3},{11,15},{20,16},{24,... | collective-permute-start | bytes 196616 | tf_op jit(solution)/shard_map/ppermute | solution.py:69
  79.1 65.9 %collective-permute-start.10 = (bf16[512,1024]{1,0:T(8,128)(2,1)S(1)}, bf16[512,1024]{1,0:T(8,128)(2,1)S(1)}, u32[]{:S(2)}, u32[]{:S(2)}) collective-permute-start(bf16[512,1024]{1,0:T(8,128)(2,1)S(1)} %collective-permute-done.6), channel_id=1, source_target_pairs={{4,0},{8,12},{5,1},{9,13},{6,2},{10,14},{7,3},{11,15},{20,16},{24,... | collective-permute-start | bytes 3145736 | tf_op jit(solution)/shard_map/ppermute | solution.py:69
  80.4 81.4 %collective-permute-start.11 = (bf16[512,768]{1,0:T(8,128)(2,1)S(1)}, bf16[512,768]{1,0:T(8,128)(2,1)S(1)}, u32[]{:S(2)}, u32[]{:S(2)}) collective-permute-start(bf16[512,768]{1,0:T(8,128)(2,1)S(1)} %slice.60), channel_id=1, source_target_pairs={{4,0},{8,12},{5,1},{9,13},{6,2},{10,14},{7,3},{11,15},{20,16},{24,... | collective-permute-start | bytes 2359304 | tf_op jit(solution)/shard_map/ppermute | solution.py:69
  81.7 83.8 %collective-permute-start.12 = (bf16[512,256]{1,0:T(8,128)(2,1)S(1)}, bf16[512,256]{1,0:T(8,128)(2,1)S(1)}, u32[]{:S(2)}, u32[]{:S(2)}) collective-permute-start(bf16[512,256]{1,0:T(8,128)(2,1)S(1)} %slice.61), channel_id=1, source_target_pairs={{4,0},{8,12},{5,1},{9,13},{6,2},{10,14},{7,3},{11,15},{20,16},{24,... | collective-permute-start | bytes 786440 | tf_op jit(solution)/shard_map/ppermute | solution.py:69

commit v14 on v9

--- a/solution.py
+++ b/solution.py
@@ -87,23 +87,27 @@
         return jnp.dot(block, part, preferred_element_type=F32)
 
     mate_out = send(own, OUTWARD)
-    mate_in = send(own, INWARD)
-    mid = [send(own[:, :half], ACROSS)]
+    piece = own[:, :half]
+    mate_in = [send(piece, INWARD)]
+    mid = [send(piece, ACROSS)]
     partial = shrink(inputs, shrink_table, adapter_ids)
-    mid.append(send(after(own, partial)[:, half:], ACROSS))
+    piece = after(own, partial)[:, half:]
+    mate_in.append(send(piece, INWARD))
+    mid.append(send(piece, ACROSS))
     mate_partial = send(partial, INWARD)
     total = product(own, here)
 
     mid_out = [send(after(mid[0], total), OUTWARD)]
-    mate_in, mate_partial = lax.optimization_barrier((mate_in, mate_partial, mid[1], total))[:2]
+    end = [send(after(mate_in[0], total), ACROSS)]
+    mate_in[1], mate_partial = lax.optimization_barrier((mate_in[1], mate_partial, mid[0]))[:2]
     both = send(jnp.stack([partial, mate_partial]), ACROSS)
-    end = [send(mate_in[:, :half], ACROSS)]
-    end.append(send(after(mate_in, end[0])[:, half:], ACROSS))
+    end.append(send(mate_in[1], ACROSS))
     mid_out.append(send(mid[1], OUTWARD))
-    total = total + product(jnp.where(is_end, mate_out, mate_in), here ^ 1)
 
-    end[0], both = lax.optimization_barrier((end[0], both, total))[:2]
     end_out = [send(end[0], OUTWARD)]
+    mate_out, both = lax.optimization_barrier((mate_out, both, end[0], mid[1]))[:2]
+    total = total + product(jnp.where(is_end, mate_out[:, :half], mate_in[0]), here ^ 1)
+    total = total + product(jnp.where(is_end, mate_out[:, half:], mate_in[1]), here ^ 1, half)
     shrunk = (
         partial.astype(F32) + mate_partial.astype(F32) + both[0].astype(F32) + both[1].astype(F32)
     ).astype(BF16)
@@ -111,11 +115,11 @@
     total = total + product(jnp.where(is_end, mid_out[0], mid[0]), far_mid)
 
     late = after(end[1], total)
-    shrunk = after(shrunk, late)
+    shrunk, mid_out[1] = lax.optimization_barrier((shrunk, mid_out[1], late))[:2]
     end_out += [send(late[:, : half - last], OUTWARD), send(late[:, half - last :], OUTWARD)]
     total = total + product(jnp.where(is_end, mid_out[1], mid[1]), far_mid, half)
     total = total + jnp.concatenate(expand(shrunk, expand_table, adapter_ids))
-    total = total + product(jnp.where(is_end, end_out[0], end[0]), far_end)
+    total = total + product(jnp.where(is_end, after(end_out[0], total), end[0]), far_end)
     block = jnp.where(is_end, after(end_out[1], total), late[:, : half - last])
     total = total + product(block, far_end, half)
     block = jnp.where(is_end, after(end_out[2], total), late[:, half - last :])

time: 151 us -> 172 us (1.14)
  waiting for transfers between devices: 65 us -> 86.7 us
  local copies, waits for them, and re-layouts: 7.43 us -> 5.01 us
    ppermute x14 -> x15, waiting for transfers between devices: 65 us -> 86.7 us  [send(): return lax.ppermute(block, 'tensor', pairs)]
    slice x4 -> x2, local copies, waits for them, and re-layouts: 5.93 us -> 3.56 us  [the longest x1 2.49 us: line(): piece = own[:, :half]]
    ppermute x14 -> x15, starting transfers between devices: 29.6 us -> 30.6 us  [send(): return lax.ppermute(block, 'tensor', pairs)]
    dot_general x7 -> x8, matrix products: 39.8 us -> 40.2 us  [product(): return jnp.dot(block, part, preferred_element_type=F32)]
  transfers between devices with their start and end apart: 14 -> 15, of which waited for: 7 -> 4; matrix products, arithmetic and copies ran while one was open for 32% -> 26% of each run, Pallas kernels for 0% -> 0%
where the time goes in v14:
time: 172 us; the launch traced here: 171 us
  waiting for transfers between devices  86.7 us (50%)
  matrix products  44.6 us (26%)
  starting transfers between devices  30.6 us (18%)
  local copies, waits for them, and re-layouts  5.01 us (3%)
  between operations  4.16 us (2%)
    ppermute x15, waiting for transfers between devices, send(): return lax.ppermute(block, 'tensor', pairs)  86.7 us
    dot_general x8, matrix products, product(): return jnp.dot(block, part, preferred_element_type=F32)  40.2 us
    ppermute x15, starting transfers between devices, send(): return lax.ppermute(block, 'tensor', pairs)  30.6 us
    dot_general x2, matrix products, shrink(): jnp.dot(inputs[c], shrink_table[adapter_ids[c]], preferred_element_type=F32)  3.52 us
  transfers between devices with their start and end apart: 15, of which 4 were waited for; matrix products, arithmetic and copies ran while one was open for 26% of the time, Pallas kernels for 0%

profile of v14, /device:TPU:0, one launch (start us, length us, event | category | flops | bytes accessed | tf_op | source)
XLA Modules:
  0.0 171.2 jit_solution(638796976318389633)
XLA Ops:
  0.0 2.5 %slice.62 = bf16[512,1024]{1,0:T(8,128)(2,1)} slice(bf16[512,2048]{1,0:T(8,128)(2,1)} %bitcast.38), slice={[0:512], [0:1024]} | slice | bytes 2097152 | tf_op jit(solution)/shard_map/slice | solution.py:90
  2.5 1.6 collective-permute-start.3
  4.1 7.8 %collective-permute-start.5 = (bf16[512,1024]{1,0:T(8,128)(2,1)}, bf16[512,1024]{1,0:T(8,128)(2,1)}, u32[]{:S(2)}, u32[]{:S(2)}) collective-permute-start(bf16[512,1024]{1,0:T(8,128)(2,1)} %slice.62), channel_id=1, source_target_pairs={{0,4},{12,8},{1,5},{13,9},{2,6},{14,10},{3,7},{15,11},{16,20},{28,... | collective-permute-start | bytes 3145736 | tf_op jit(solution)/shard_map/ppermute | solution.py:68
  13.2 1.3 fusion.78
  17.7 1.8 %fusion.27 = bf16[256,64]{0,1:T(8,128)(2,1)S(1)} fusion(bf16[2,256,2048]{2,1,0:T(8,128)(2,1)} %param.5, bf16[4,2048,64]{1,2,0:T(8,128)(2,1)} %param.7, s32[]{:T(128)S(6)} %select_n.89), kind=kOutput, calls=%fused_computation.22 | convolution fusion | flops 67125248 | bytes 1343492 | tf_op jit(solution)/shard_map/dot_general | solution.py:12
  20.1 1.8 %fusion.28 = bf16[256,64]{0,1:T(8,128)(2,1)S(1)} fusion(bf16[2,256,2048]{2,1,0:T(8,128)(2,1)} %param.5, bf16[4,2048,64]{1,2,0:T(8,128)(2,1)} %param.7, s32[]{:T(128)S(6)} %select_n.90), kind=kOutput, calls=%fused_computation.23 | convolution fusion | flops 67125248 | bytes 1343492 | tf_op jit(solution)/shard_map/dot_general | solution.py:12
  21.9 5.9 %collective-permute-start.2 = (bf16[512,64]{0,1:T(8,128)(2,1)S(1)}, bf16[512,64]{0,1:T(8,128)(2,1)S(1)}, u32[]{:S(2)}, u32[]{:S(2)}) collective-permute-start(bf16[512,64]{0,1:T(8,128)(2,1)S(1)} %get-tuple-element.32), channel_id=1, source_target_pairs={{0,4},{12,8},{1,5},{13,9},{2,6},{14,10},{3,7},{15,11},{16,20},{28,... | collective-permute-start | bytes 196616 | tf_op jit(solution)/shard_map/ppermute | solution.py:68
  28.9 2.3 %collective-permute-start.1 = (bf16[512,1024]{1,0:T(8,128)(2,1)}, bf16[512,1024]{1,0:T(8,128)(2,1)}, u32[]{:S(2)}, u32[]{:S(2)}) collective-permute-start(bf16[512,1024]{1,0:T(8,128)(2,1)} %slice.52), channel_id=1, source_target_pairs={{0,4},{12,8},{1,5},{13,9},{2,6},{14,10},{3,7},{15,11},{16,20},{28,... | collective-permute-start | bytes 3145736 | tf_op jit(solution)/shard_map/ppermute | solution.py:68
  31.3 9.4 %fusion.12 = f32[512,2048]{1,0:T(8,128)} fusion(bf16[512,2048]{1,0:T(8,128)(2,1)S(1)} %bitcast.41, bf16[8192,2048]{1,0:T(8,128)(2,1)} %param.6, s32[]{:T(128)S(6)} %select_n.87), kind=kOutput, calls=%fused_computation.15 | convolution fusion | flops 4294967296 | bytes 14680068 | tf_op jit(solution)/shard_map/dot_general | solution.py:87
  41.4 1.6 collective-permute-start.6
  43.0 14.2 %collective-permute-done.1 = bf16[512,1024]{1,0:T(8,128)(2,1)} collective-permute-done((bf16[512,1024]{1,0:T(8,128)(2,1)}, bf16[512,1024]{1,0:T(8,128)(2,1)}, u32[]{:S(2)}, u32[]{:S(2)}) %collective-permute-start.1) | collective-permute-done | bytes 1048608 | tf_op jit(solution)/shard_map/ppermute | solution.py:68
  57.9 1.3 collective-permute-start.8
  61.4 1.3 collective-permute-start.9
  62.7 4.9 %fusion.8 = f32[512,2048]{1,0:T(8,128)S(1)} fusion(bf16[8192,2048]{1,0:T(8,128)(2,1)} %param.6, s32[]{:T(128)S(6)} %select_n.94, bf16[512,1024]{1,0:T(8,128)(2,1)} %collective-permute-done.1, bf16[512,2048]{1,0:T(8,128)(2,1)} %collective-permute-done, pred[]{:T(512)S(6)} %or.3), kind=kOutput, calls=%fused_computation.11 | convolution fusion | flops 2148007936 | bytes 10485765 | tf_op jit(solution)/shard_map/dot_general | solution.py:87
  67.5 5.0 %fusion.10 = f32[512,2048]{1,0:T(8,128)S(1)} fusion(bf16[8192,2048]{1,0:T(8,128)(2,1)} %param.6, s32[]{:T(128)S(6)} %select_n.92, bf16[512,1024]{1,0:T(8,128)(2,1)} %collective-permute-done.5, bf16[512,2048]{1,0:T(8,128)(2,1)} %collective-permute-done, pred[]{:T(512)S(6)} %or.3), kind=kOutput, calls=%fused_computation.13 | convolution fusion | flops 2148007936 | bytes 10485765 | tf_op jit(solution)/shard_map/dot_general | solution.py:87
  72.6 12.7 %collective-permute-done.8 = bf16[512,1024]{1,0:T(8,128)(2,1)S(1)} collective-permute-done((bf16[512,1024]{1,0:T(8,128)(2,1)}, bf16[512,1024]{1,0:T(8,128)(2,1)S(1)}, u32[]{:S(2)}, u32[]{:S(2)}) %collective-permute-start.8) | collective-permute-done | bytes 1048608 | tf_op jit(solution)/shard_map/ppermute | solution.py:68
  85.3 4.7 %add_add_fusion = f32[512,2048]{1,0:T(8,128)S(1)} fusion(f32[512,2048]{1,0:T(8,128)S(1)} %fusion.8, f32[512,2048]{1,0:T(8,128)S(1)} %copy-done.1, f32[512,2048]{1,0:T(8,128)S(1)} %fusion.10, bf16[8192,2048]{1,0:T(8,128)(2,1)} %param.6, s32[]{:T(128)S(6)} %select_n.97, bf16[512,1024]{1,0:T(8,128)(2,1)S(1)} %collective-permute-done.8, ...), kind=kOutput, calls=%fused_computation.10 | convolution fusion | flops 2151153664 | bytes 23068676 | tf_op jit(solution)/shard_map/dot_general | solution.py:87
  92.8 1.5 collective-permute-start.12
  94.3 21.6 %collective-permute-done.9 = bf16[512,64]{0,1:T(8,128)(2,1)S(1)} collective-permute-done((bf16[512,64]{0,1:T(8,128)(2,1)S(1)}, bf16[512,64]{0,1:T(8,128)(2,1)S(1)}, u32[]{:S(2)}, u32[]{:S(2)}) %collective-permute-start.9) | collective-permute-done | bytes 65568 | tf_op jit(solution)/shard_map/ppermute | solution.py:68
  116.8 4.6 %maximum_add_fusion = f32[512,2048]{1,0:T(8,128)S(1)} fusion(f32[256,2048]{1,0:T(8,128)S(1)} %fusion.48, f32[256,2048]{1,0:T(8,128)S(1)} %fusion.50, f32[512,2048]{1,0:T(8,128)S(1)} %add_add_fusion, bf16[8192,2048]{1,0:T(8,128)(2,1)} %param.6, s32[]{:T(128)S(6)} %select_n.101, bf16[512,1024]{1,0:T(8,128)(2,1)S(1)} %collective-permute-done.10, ...), kind=kOutput, calls=%fused_computation.2 | convolution fusion | flops 2151153664 | bytes 18874372 | tf_op jit(solution)/shard_map/dot_general | solution.py:87
  121.5 38.0 %collective-permute-done.12 = bf16[512,1024]{1,0:T(8,128)(2,1)S(1)} collective-permute-done((bf16[512,1024]{1,0:T(8,128)(2,1)}, bf16[512,1024]{1,0:T(8,128)(2,1)S(1)}, u32[]{:S(2)}, u32[]{:S(2)}) %collective-permute-start.12) | collective-permute-done | bytes 1048608 | tf_op jit(solution)/shard_map/ppermute | solution.py:68
  159.5 4.6 %fusion.22 = f32[512,2048]{1,0:T(8,128)S(1)} fusion(f32[512,2048]{1,0:T(8,128)S(1)} %maximum_add_fusion, bf16[8192,2048]{1,0:T(8,128)(2,1)} %param.6, s32[]{:T(128)S(6)} %select_n.104, bf16[512,1024]{1,0:T(8,128)(2,1)S(1)} %collective-permute-done.12, bf16[512,1024]{1,0:T(8,128)(2,1)} %collective-permute-done.6, pred[]{:T(512)S(6)} %or.3), kind=kOutput, calls=%fused_computation.19 | convolution fusion | flops 2149056512 | bytes 14680069 | tf_op jit(solution)/shard_map/dot_general | solution.py:87
  164.1 3.7 %fusion.17 = f32[512,2048]{1,0:T(8,128)S(1)} fusion(f32[512,2048]{1,0:T(8,128)S(1)} %fusion.22, bf16[8192,2048]{1,0:T(8,128)(2,1)} %param.6, s32[]{:T(128)S(6)} %select_n.107, bf16[512,768]{1,0:T(8,128)(2,1)S(1)} %collective-permute-done.13, pred[]{:T(512)S(6)} %or.3, bf16[512,1024]{1,0:T(8,128)(2,1)S(1)} %collective-permute-done.11), kind=kOutput, calls=%fused_computation.18 | convolution fusion | flops 1612054528 | bytes 13107205 | tf_op jit(solution)/shard_map/dot_general | solution.py:87
  167.9 3.3 %add_convert_fusion = bf16[512,2048]{1,0:T(8,128)(2,1)} fusion(f32[512,2048]{1,0:T(8,128)S(1)} %fusion.17, bf16[8192,2048]{1,0:T(8,128)(2,1)} %param.6, s32[]{:T(128)S(6)} %select_n.110, bf16[512,256]{1,0:T(8,128)(2,1)S(1)} %collective-permute-done.14, pred[]{:T(512)S(6)} %or.3, bf16[512,1024]{1,0:T(8,128)(2,1)S(1)} %collective-permute-done.11), kind=kOutput, calls=%fused_computation.3 | convolution fusion | flops 539099136 | bytes 7864325 | tf_op jit(solution)/shard_map/dot_general | solution.py:87
  (33 shorter events, 9.5 us)
Async XLA Ops:
  0.0 115.9 %copy-start = (bf16[4,64,2048]{2,1,0:T(8,128)(2,1)S(1)}, bf16[4,64,2048]{2,1,0:T(8,128)(2,1)}, u32[]{:S(2)}) copy-start(bf16[4,64,2048]{2,1,0:T(8,128)(2,1)} %param.8) | copy-start | bytes 3145732
  0.0 27.8 %copy-start.2 = (bf16[2,256,2048]{2,1,0:T(8,128)(2,1)S(1)}, bf16[2,256,2048]{2,1,0:T(8,128)(2,1)}, u32[]{:S(2)}) copy-start(bf16[2,256,2048]{2,1,0:T(8,128)(2,1)} %param.5) | copy-start | bytes 6291460
  2.5 54.7 %collective-permute-start.3 = (bf16[512,1024]{1,0:T(8,128)(2,1)}, bf16[512,1024]{1,0:T(8,128)(2,1)}, u32[]{:S(2)}, u32[]{:S(2)}) collective-permute-start(bf16[512,1024]{1,0:T(8,128)(2,1)} %slice.62), channel_id=1, source_target_pairs={{4,8},{8,4},{5,9},{9,5},{6,10},{10,6},{7,11},{11,7},{20,24},{24,20... | collective-permute-start | bytes 3145736 | tf_op jit(solution)/shard_map/ppermute | solution.py:68
  4.1 36.5 %collective-permute-start.5 = (bf16[512,1024]{1,0:T(8,128)(2,1)}, bf16[512,1024]{1,0:T(8,128)(2,1)}, u32[]{:S(2)}, u32[]{:S(2)}) collective-permute-start(bf16[512,1024]{1,0:T(8,128)(2,1)} %slice.62), channel_id=1, source_target_pairs={{0,4},{12,8},{1,5},{13,9},{2,6},{14,10},{3,7},{15,11},{16,20},{28,... | collective-permute-start | bytes 3145736 | tf_op jit(solution)/shard_map/ppermute | solution.py:68
  11.9 49.4 %collective-permute-start = (bf16[512,2048]{1,0:T(8,128)(2,1)}, bf16[512,2048]{1,0:T(8,128)(2,1)}, u32[]{:S(2)}, u32[]{:S(2)}) collective-permute-start(bf16[512,2048]{1,0:T(8,128)(2,1)} %bitcast.39), channel_id=1, source_target_pairs={{4,0},{8,12},{5,1},{9,13},{6,2},{10,14},{7,3},{11,15},{20,16},{24,... | collective-permute-start | bytes 6291464 | tf_op jit(solution)/shard_map/ppermute | solution.py:68
  21.9 19.4 %collective-permute-start.2 = (bf16[512,64]{0,1:T(8,128)(2,1)S(1)}, bf16[512,64]{0,1:T(8,128)(2,1)S(1)}, u32[]{:S(2)}, u32[]{:S(2)}) collective-permute-start(bf16[512,64]{0,1:T(8,128)(2,1)S(1)} %get-tuple-element.32), channel_id=1, source_target_pairs={{0,4},{12,8},{1,5},{13,9},{2,6},{14,10},{3,7},{15,11},{16,20},{28,... | collective-permute-start | bytes 196616 | tf_op jit(solution)/shard_map/ppermute | solution.py:68
  28.9 28.3 %collective-permute-start.1 = (bf16[512,1024]{1,0:T(8,128)(2,1)}, bf16[512,1024]{1,0:T(8,128)(2,1)}, u32[]{:S(2)}, u32[]{:S(2)}) collective-permute-start(bf16[512,1024]{1,0:T(8,128)(2,1)} %slice.52), channel_id=1, source_target_pairs={{0,4},{12,8},{1,5},{13,9},{2,6},{14,10},{3,7},{15,11},{16,20},{28,... | collective-permute-start | bytes 3145736 | tf_op jit(solution)/shard_map/ppermute | solution.py:68
  40.6 18.6 %collective-permute-start.7 = (bf16[512,1024]{1,0:T(8,128)(2,1)}, bf16[512,1024]{1,0:T(8,128)(2,1)S(1)}, u32[]{:S(2)}, u32[]{:S(2)}) collective-permute-start(bf16[512,1024]{1,0:T(8,128)(2,1)} %slice.52), channel_id=1, source_target_pairs={{4,8},{8,4},{5,9},{9,5},{6,10},{10,6},{7,11},{11,7},{20,24},{24,20... | collective-permute-start | bytes 3145736 | tf_op jit(solution)/shard_map/ppermute | solution.py:68
  41.4 19.9 %collective-permute-start.6 = (bf16[512,1024]{1,0:T(8,128)(2,1)}, bf16[512,1024]{1,0:T(8,128)(2,1)}, u32[]{:S(2)}, u32[]{:S(2)}) collective-permute-start(bf16[512,1024]{1,0:T(8,128)(2,1)} %collective-permute-done.5), channel_id=1, source_target_pairs={{4,8},{8,4},{5,9},{9,5},{6,10},{10,6},{7,11},{11,7},{20,24},{24,20... | collective-permute-start | bytes 3145736 | tf_op jit(solution)/shard_map/ppermute | solution.py:68
  57.2 2.8 %collective-permute-start.4 = (bf16[2,512,64]{1,2,0:T(8,128)(2,1)S(1)}, bf16[2,512,64]{1,2,0:T(8,128)(2,1)S(1)}, u32[]{:S(2)}, u32[]{:S(2)}) collective-permute-start(bf16[2,512,64]{1,2,0:T(8,128)(2,1)S(1)} %pad_maximum_fusion), channel_id=1, source_target_pairs={{4,8},{8,4},{5,9},{9,5},{6,10},{10,6},{7,11},{11,7},{20,24},{24,20... | collective-permute-start | bytes 393224 | tf_op jit(solution)/shard_map/ppermute | solution.py:68
  57.9 27.3 %collective-permute-start.8 = (bf16[512,1024]{1,0:T(8,128)(2,1)}, bf16[512,1024]{1,0:T(8,128)(2,1)S(1)}, u32[]{:S(2)}, u32[]{:S(2)}) collective-permute-start(bf16[512,1024]{1,0:T(8,128)(2,1)} %collective-permute-done.3), channel_id=1, source_target_pairs={{4,0},{8,12},{5,1},{9,13},{6,2},{10,14},{7,3},{11,15},{20,16},{24,... | collective-permute-start | bytes 3145736 | tf_op jit(solution)/shard_map/ppermute | solution.py:68
  59.3 30.8 %collective-permute-start.11 = (bf16[512,1024]{1,0:T(8,128)(2,1)}, bf16[512,1024]{1,0:T(8,128)(2,1)S(1)}, u32[]{:S(2)}, u32[]{:S(2)}) collective-permute-start(bf16[512,1024]{1,0:T(8,128)(2,1)} %collective-permute-done.1), channel_id=1, source_target_pairs={{4,8},{8,4},{5,9},{9,5},{6,10},{10,6},{7,11},{11,7},{20,24},{24,20... | collective-permute-start | bytes 3145736 | tf_op jit(solution)/shard_map/ppermute | solution.py:68
  60.0 55.9 %collective-permute-start.10 = (bf16[512,1024]{1,0:T(8,128)(2,1)S(1)}, bf16[512,1024]{1,0:T(8,128)(2,1)S(1)}, u32[]{:S(2)}, u32[]{:S(2)}) collective-permute-start(bf16[512,1024]{1,0:T(8,128)(2,1)S(1)} %collective-permute-done.7), channel_id=1, source_target_pairs={{4,0},{8,12},{5,1},{9,13},{6,2},{10,14},{7,3},{11,15},{20,16},{24,... | collective-permute-start | bytes 3145736 | tf_op jit(solution)/shard_map/ppermute | solution.py:68
  61.4 54.5 %collective-permute-start.9 = (bf16[512,64]{0,1:T(8,128)(2,1)S(1)}, bf16[512,64]{0,1:T(8,128)(2,1)S(1)}, u32[]{:S(2)}, u32[]{:S(2)}) collective-permute-start(bf16[512,64]{0,1:T(8,128)(2,1)S(1)} %fusion.60), channel_id=1, source_target_pairs={{4,0},{8,12},{5,1},{9,13},{6,2},{10,14},{7,3},{11,15},{20,16},{24,... | collective-permute-start | bytes 196616 | tf_op jit(solution)/shard_map/ppermute | solution.py:68
  67.5 17.8 %copy-start.1 = (f32[512,2048]{1,0:T(8,128)S(1)}, f32[512,2048]{1,0:T(8,128)}, u32[]{:S(2)}) copy-start(f32[512,2048]{1,0:T(8,128)} %fusion.12) | copy-start | bytes 12582916
  90.2 73.9 %collective-permute-start.13 = (bf16[512,768]{1,0:T(8,128)(2,1)S(1)}, bf16[512,768]{1,0:T(8,128)(2,1)S(1)}, u32[]{:S(2)}, u32[]{:S(2)}) collective-permute-start(bf16[512,768]{1,0:T(8,128)(2,1)S(1)} %slice.60), channel_id=1, source_target_pairs={{4,0},{8,12},{5,1},{9,13},{6,2},{10,14},{7,3},{11,15},{20,16},{24,... | collective-permute-start | bytes 2359304 | tf_op jit(solution)/shard_map/ppermute | solution.py:68
  91.5 76.4 %collective-permute-start.14 = (bf16[512,256]{1,0:T(8,128)(2,1)S(1)}, bf16[512,256]{1,0:T(8,128)(2,1)S(1)}, u32[]{:S(2)}, u32[]{:S(2)}) collective-permute-start(bf16[512,256]{1,0:T(8,128)(2,1)S(1)} %slice.61), channel_id=1, source_target_pairs={{4,0},{8,12},{5,1},{9,13},{6,2},{10,14},{7,3},{11,15},{20,16},{24,... | collective-permute-start | bytes 786440 | tf_op jit(solution)/shard_map/ppermute | solution.py:68
  92.8 66.7 %collective-permute-start.12 = (bf16[512,1024]{1,0:T(8,128)(2,1)}, bf16[512,1024]{1,0:T(8,128)(2,1)S(1)}, u32[]{:S(2)}, u32[]{:S(2)}) collective-permute-start(bf16[512,1024]{1,0:T(8,128)(2,1)} %collective-permute-done.6), channel_id=1, source_target_pairs={{4,0},{8,12},{5,1},{9,13},{6,2},{10,14},{7,3},{11,15},{20,16},{24,... | collective-permute-start | bytes 3145736 | tf_op jit(solution)/shard_map/ppermute | solution.py:68

commit v15 on v11

--- a/solution.py
+++ b/solution.py
@@ -98,7 +98,7 @@
     mate, mate_partial = lax.optimization_barrier((mate, mate_partial, mid[1], total))[:2]
     both = send(jnp.stack([partial, mate_partial]), ACROSS)
     end = [send(mate[:, :half], ACROSS)]
-    end.append(send(after(mate, end[0])[:, half:], ACROSS))
+    end.append(send(after(mate, mid_out[0])[:, half:], ACROSS))
     mid_out.append(send(mid[1], OUTWARD))
     total = total + product(mate, here ^ 1)
 

time: 144 us -> 176 us (1.22)
  waiting for transfers between devices: 66 us -> 95.9 us
  starting transfers between devices: 22 us -> 25.5 us
  matrix products: 44.2 us -> 42.1 us
    ppermute x13, waiting for transfers between devices: 66 us -> 95.9 us  [send(): return lax.ppermute(block, 'tensor', pairs)]
    ppermute x13, starting transfers between devices: 22 us -> 25.5 us  [send(): return lax.ppermute(block, 'tensor', pairs)]
    dot_general x7, matrix products: 39.8 us -> 37.7 us  [product(): return jnp.dot(block, part, preferred_element_type=F32)]
  transfers between devices with their start and end apart: 13 -> 13, of which waited for: 7 -> 6; matrix products, arithmetic and copies ran while one was open for 34% -> 27% of each run, Pallas kernels for 0% -> 0%
where the time goes in v15:
time: 176 us; the launch traced here: 175 us
  waiting for transfers between devices  95.9 us (54%)
  matrix products  42.1 us (24%)
  starting transfers between devices  25.5 us (14%)
  local copies, waits for them, and re-layouts  7.54 us (4%)
  between operations  3.99 us (2%)
    ppermute x13, waiting for transfers between devices, send(): return lax.ppermute(block, 'tensor', pairs)  95.9 us
    dot_general x7, matrix products, product(): return jnp.dot(block, part, preferred_element_type=F32)  37.7 us
    ppermute x13, starting transfers between devices, send(): return lax.ppermute(block, 'tensor', pairs)  25.5 us
    dot_general x2, matrix products, shrink(): jnp.dot(inputs[c], shrink_table[adapter_ids[c]], preferred_element_type=F32)  3.52 us
  transfers between devices with their start and end apart: 13, of which 6 were waited for; matrix products, arithmetic and copies ran while one was open for 27% of the time, Pallas kernels for 0%

profile of v15, /device:TPU:0, one launch (start us, length us, event | category | flops | bytes accessed | tf_op | source)
XLA Modules:
  0.0 175.1 jit_solution(1548338357462549488)
XLA Ops:
  0.0 3.0 %collective-permute-start = (bf16[512,2048]{1,0:T(8,128)(2,1)}, bf16[512,2048]{1,0:T(8,128)(2,1)}, u32[]{:S(2)}, u32[]{:S(2)}) collective-permute-start(bf16[512,2048]{1,0:T(8,128)(2,1)} %bitcast.39), channel_id=1, source_target_pairs={{0,4},{12,8},{4,0},{8,12},{1,5},{13,9},{5,1},{9,13},{2,6},{14,10},... | collective-permute-start | bytes 6291464 | tf_op jit(solution)/shard_map/ppermute | solution.py:69
  3.0 2.3 %slice.62 = bf16[512,1024]{1,0:T(8,128)(2,1)} slice(bf16[512,2048]{1,0:T(8,128)(2,1)} %bitcast.40), slice={[0:512], [0:1024]} | slice | bytes 2097152 | tf_op jit(solution)/shard_map/slice | solution.py:91
  5.3 1.7 collective-permute-start.3
  7.0 1.4 fusion.71
  11.4 1.8 %fusion.27 = bf16[256,64]{0,1:T(8,128)(2,1)S(1)} fusion(bf16[2,256,2048]{2,1,0:T(8,128)(2,1)} %param.5, bf16[4,2048,64]{1,2,0:T(8,128)(2,1)} %param.7, s32[]{:T(128)S(6)} %select_n.77), kind=kOutput, calls=%fused_computation.21 | convolution fusion | flops 67125248 | bytes 1343492 | tf_op jit(solution)/shard_map/dot_general | solution.py:12
  13.8 1.8 %fusion.28 = bf16[256,64]{0,1:T(8,128)(2,1)S(1)} fusion(bf16[2,256,2048]{2,1,0:T(8,128)(2,1)} %param.5, bf16[4,2048,64]{1,2,0:T(8,128)(2,1)} %param.7, s32[]{:T(128)S(6)} %select_n.78), kind=kOutput, calls=%fused_computation.22 | convolution fusion | flops 67125248 | bytes 1343492 | tf_op jit(solution)/shard_map/dot_general | solution.py:12
  16.8 1.7 collective-permute-start.2
  18.5 9.4 %fusion.11 = f32[512,2048]{1,0:T(8,128)} fusion(bf16[512,2048]{1,0:T(8,128)(2,1)S(1)} %bitcast.42, bf16[8192,2048]{1,0:T(8,128)(2,1)} %param.6, s32[]{:T(128)S(6)} %select_n.76), kind=kOutput, calls=%fused_computation.13 | convolution fusion | flops 4294967296 | bytes 14680068 | tf_op jit(solution)/shard_map/dot_general | solution.py:88
  29.1 8.8 %collective-permute-start.1 = (bf16[512,64]{0,1:T(8,128)(2,1)S(1)}, bf16[512,64]{0,1:T(8,128)(2,1)S(1)}, u32[]{:S(2)}, u32[]{:S(2)}) collective-permute-start(bf16[512,64]{0,1:T(8,128)(2,1)S(1)} %get-tuple-element.28), channel_id=1, source_target_pairs={{0,4},{12,8},{1,5},{13,9},{2,6},{14,10},{3,7},{15,11},{16,20},{28,... | collective-permute-start | bytes 196616 | tf_op jit(solution)/shard_map/ppermute | solution.py:69
  38.0 1.6 collective-permute-start.5
  39.6 10.0 %collective-permute-done.1 = bf16[512,64]{0,1:T(8,128)(2,1)S(1)} collective-permute-done((bf16[512,64]{0,1:T(8,128)(2,1)S(1)}, bf16[512,64]{0,1:T(8,128)(2,1)S(1)}, u32[]{:S(2)}, u32[]{:S(2)}) %collective-permute-start.1) | collective-permute-done | bytes 65568 | tf_op jit(solution)/shard_map/ppermute | solution.py:69
  49.8 1.3 slice.54
  51.1 21.1 %collective-permute-done.4 = bf16[512,1024]{1,0:T(8,128)(2,1)S(1)} collective-permute-done((bf16[512,1024]{1,0:T(8,128)(2,1)}, bf16[512,1024]{1,0:T(8,128)(2,1)S(1)}, u32[]{:S(2)}, u32[]{:S(2)}) %collective-permute-start.4) | collective-permute-done | bytes 1048608 | tf_op jit(solution)/shard_map/ppermute | solution.py:69
  72.2 1.3 slice.57
  75.7 7.6 %fusion.16 = f32[512,2048]{1,0:T(8,128)S(1)} fusion(f32[512,2048]{1,0:T(8,128)S(1)} %copy-done.2, bf16[512,2048]{1,0:T(8,128)(2,1)} %collective-permute-done, bf16[8192,2048]{1,0:T(8,128)(2,1)} %param.6, s32[]{:T(128)S(6)} %select_n.79), kind=kOutput, calls=%fused_computation.16 | convolution fusion | flops 4296015872 | bytes 18874372 | tf_op jit(solution)/shard_map/dot_general | solution.py:88
  85.9 4.5 %fusion.22 = f32[512,2048]{1,0:T(8,128)S(1)} fusion(f32[512,2048]{1,0:T(8,128)S(1)} %fusion.16, bf16[8192,2048]{1,0:T(8,128)(2,1)} %param.6, s32[]{:T(128)S(6)} %select_n.83, bf16[512,1024]{1,0:T(8,128)(2,1)S(1)} %collective-permute-done.4, bf16[512,1024]{1,0:T(8,128)(2,1)} %collective-permute-done.3, pred[]{:T(512)S(6)} %or.3), kind=kOutput, calls=%fused_computation.18 | convolution fusion | flops 2149056512 | bytes 14680069 | tf_op jit(solution)/shard_map/dot_general | solution.py:88
  91.9 1.5 collective-permute-start.12
  93.4 35.5 %collective-permute-done.8 = bf16[512,64]{0,1:T(8,128)(2,1)S(1)} collective-permute-done((bf16[512,64]{0,1:T(8,128)(2,1)S(1)}, bf16[512,64]{0,1:T(8,128)(2,1)S(1)}, u32[]{:S(2)}, u32[]{:S(2)}) %collective-permute-start.8) | collective-permute-done | bytes 65568 | tf_op jit(solution)/shard_map/ppermute | solution.py:69
  129.9 21.5 %collective-permute-done.10 = bf16[512,1024]{1,0:T(8,128)(2,1)S(1)} collective-permute-done((bf16[512,1024]{1,0:T(8,128)(2,1)S(1)}, bf16[512,1024]{1,0:T(8,128)(2,1)S(1)}, u32[]{:S(2)}, u32[]{:S(2)}) %collective-permute-start.10) | collective-permute-done | bytes 1048608 | tf_op jit(solution)/shard_map/ppermute | solution.py:69
  151.4 4.5 %fusion.5 = f32[512,2048]{1,0:T(8,128)S(1)} fusion(bf16[8192,2048]{1,0:T(8,128)(2,1)} %param.6, s32[]{:T(128)S(6)} %select_n.90, bf16[512,1024]{1,0:T(8,128)(2,1)S(1)} %collective-permute-done.10, bf16[512,1024]{1,0:T(8,128)(2,1)S(1)} %collective-permute-done.6, pred[]{:T(512)S(6)} %or.3), kind=kOutput, calls=%fused_computation.7 | convolution fusion | flops 2148007936 | bytes 10485765 | tf_op jit(solution)/shard_map/dot_general | solution.py:88
  156.0 4.7 %fusion.4 = f32[512,2048]{1,0:T(8,128)S(1)} fusion(f32[512,2048]{1,0:T(8,128)S(1)} %fusion.5, f32[256,2048]{1,0:T(8,128)S(1)} %fusion.42, f32[256,2048]{1,0:T(8,128)S(1)} %fusion.44, f32[512,2048]{1,0:T(8,128)S(1)} %fusion.22, bf16[8192,2048]{1,0:T(8,128)(2,1)} %param.6, s32[]{:T(128)S(6)} %select_n.85, bf16[512,1024]{1,0:T(8,128)(2,1)S(1)} %collective-permute-done.5, ...), kind=kOutput, calls=%fused_computation.5 | convolution fusion | flops 2152202240 | bytes 23068676 | tf_op jit(solution)/shard_map/dot_general | solution.py:88
  160.6 7.5 %collective-permute-done.11 = bf16[512,768]{1,0:T(8,128)(2,1)S(1)} collective-permute-done((bf16[512,768]{1,0:T(8,128)(2,1)S(1)}, bf16[512,768]{1,0:T(8,128)(2,1)S(1)}, u32[]{:S(2)}, u32[]{:S(2)}) %collective-permute-start.11) | collective-permute-done | bytes 786464 | tf_op jit(solution)/shard_map/ppermute | solution.py:69
  168.1 3.7 %fusion.19 = f32[512,2048]{1,0:T(8,128)S(1)} fusion(f32[512,2048]{1,0:T(8,128)S(1)} %fusion.4, bf16[8192,2048]{1,0:T(8,128)(2,1)} %param.6, s32[]{:T(128)S(6)} %select_n.93, bf16[512,768]{1,0:T(8,128)(2,1)S(1)} %collective-permute-done.11, pred[]{:T(512)S(6)} %or.3, bf16[512,1024]{1,0:T(8,128)(2,1)S(1)} %collective-permute-done.9), kind=kOutput, calls=%fused_computation.17 | convolution fusion | flops 1612054528 | bytes 13107205 | tf_op jit(solution)/shard_map/dot_general | solution.py:88
  171.8 3.3 %add_convert_fusion = bf16[512,2048]{1,0:T(8,128)(2,1)} fusion(f32[512,2048]{1,0:T(8,128)S(1)} %fusion.19, bf16[8192,2048]{1,0:T(8,128)(2,1)} %param.6, s32[]{:T(128)S(6)} %select_n.96, bf16[512,256]{1,0:T(8,128)(2,1)S(1)} %collective-permute-done.12, pred[]{:T(512)S(6)} %or.3, bf16[512,1024]{1,0:T(8,128)(2,1)S(1)} %collective-permute-done.9), kind=kOutput, calls=%fused_computation.6 | convolution fusion | flops 539099136 | bytes 7864325 | tf_op jit(solution)/shard_map/dot_general | solution.py:88
  (30 shorter events, 9.9 us)
Async XLA Ops:
  0.0 129.0 %copy-start = (bf16[4,64,2048]{2,1,0:T(8,128)(2,1)S(1)}, bf16[4,64,2048]{2,1,0:T(8,128)(2,1)}, u32[]{:S(2)}) copy-start(bf16[4,64,2048]{2,1,0:T(8,128)(2,1)} %param.8) | copy-start | bytes 3145732
  0.0 15.6 %copy-start.1 = (bf16[2,256,2048]{2,1,0:T(8,128)(2,1)S(1)}, bf16[2,256,2048]{2,1,0:T(8,128)(2,1)}, u32[]{:S(2)}) copy-start(bf16[2,256,2048]{2,1,0:T(8,128)(2,1)} %param.5) | copy-start | bytes 6291460
  0.0 49.8 %collective-permute-start = (bf16[512,2048]{1,0:T(8,128)(2,1)}, bf16[512,2048]{1,0:T(8,128)(2,1)}, u32[]{:S(2)}, u32[]{:S(2)}) collective-permute-start(bf16[512,2048]{1,0:T(8,128)(2,1)} %bitcast.39), channel_id=1, source_target_pairs={{0,4},{12,8},{4,0},{8,12},{1,5},{13,9},{5,1},{9,13},{2,6},{14,10},... | collective-permute-start | bytes 6291464 | tf_op jit(solution)/shard_map/ppermute | solution.py:69
  5.3 22.5 %collective-permute-start.3 = (bf16[512,1024]{1,0:T(8,128)(2,1)}, bf16[512,1024]{1,0:T(8,128)(2,1)}, u32[]{:S(2)}, u32[]{:S(2)}) collective-permute-start(bf16[512,1024]{1,0:T(8,128)(2,1)} %slice.62), channel_id=1, source_target_pairs={{4,8},{8,4},{5,9},{9,5},{6,10},{10,6},{7,11},{11,7},{20,24},{24,20... | collective-permute-start | bytes 3145736 | tf_op jit(solution)/shard_map/ppermute | solution.py:69
  16.8 21.2 %collective-permute-start.2 = (bf16[512,1024]{1,0:T(8,128)(2,1)}, bf16[512,1024]{1,0:T(8,128)(2,1)}, u32[]{:S(2)}, u32[]{:S(2)}) collective-permute-start(bf16[512,1024]{1,0:T(8,128)(2,1)} %slice.52), channel_id=1, source_target_pairs={{4,8},{8,4},{5,9},{9,5},{6,10},{10,6},{7,11},{11,7},{20,24},{24,20... | collective-permute-start | bytes 3145736 | tf_op jit(solution)/shard_map/ppermute | solution.py:69
  27.9 44.3 %collective-permute-start.4 = (bf16[512,1024]{1,0:T(8,128)(2,1)}, bf16[512,1024]{1,0:T(8,128)(2,1)S(1)}, u32[]{:S(2)}, u32[]{:S(2)}) collective-permute-start(bf16[512,1024]{1,0:T(8,128)(2,1)} %collective-permute-done.3), channel_id=1, source_target_pairs={{4,0},{8,12},{5,1},{9,13},{6,2},{10,14},{7,3},{11,15},{20,16},{24,... | collective-permute-start | bytes 3145736 | tf_op jit(solution)/shard_map/ppermute | solution.py:69
  29.1 20.4 %collective-permute-start.1 = (bf16[512,64]{0,1:T(8,128)(2,1)S(1)}, bf16[512,64]{0,1:T(8,128)(2,1)S(1)}, u32[]{:S(2)}, u32[]{:S(2)}) collective-permute-start(bf16[512,64]{0,1:T(8,128)(2,1)S(1)} %get-tuple-element.28), channel_id=1, source_target_pairs={{0,4},{12,8},{1,5},{13,9},{2,6},{14,10},{3,7},{15,11},{16,20},{28,... | collective-permute-start | bytes 196616 | tf_op jit(solution)/shard_map/ppermute | solution.py:69
  38.0 37.7 %copy-start.2 = (f32[512,2048]{1,0:T(8,128)S(1)}, f32[512,2048]{1,0:T(8,128)}, u32[]{:S(2)}) copy-start(f32[512,2048]{1,0:T(8,128)} %fusion.11) | copy-start | bytes 12582916
  38.0 117.9 %collective-permute-start.5 = (bf16[512,1024]{1,0:T(8,128)(2,1)}, bf16[512,1024]{1,0:T(8,128)(2,1)S(1)}, u32[]{:S(2)}, u32[]{:S(2)}) collective-permute-start(bf16[512,1024]{1,0:T(8,128)(2,1)} %collective-permute-done.2), channel_id=1, source_target_pairs={{4,0},{8,12},{5,1},{9,13},{6,2},{10,14},{7,3},{11,15},{20,16},{24,... | collective-permute-start | bytes 3145736 | tf_op jit(solution)/shard_map/ppermute | solution.py:69
  73.5 17.0 %collective-permute-start.9 = (bf16[512,1024]{1,0:T(8,128)(2,1)S(1)}, bf16[512,1024]{1,0:T(8,128)(2,1)S(1)}, u32[]{:S(2)}, u32[]{:S(2)}) collective-permute-start(bf16[512,1024]{1,0:T(8,128)(2,1)S(1)} %slice.57), channel_id=1, source_target_pairs={{4,8},{8,4},{5,9},{9,5},{6,10},{10,6},{7,11},{11,7},{20,24},{24,20... | collective-permute-start | bytes 3145736 | tf_op jit(solution)/shard_map/ppermute | solution.py:69
  74.3 9.0 %collective-permute-start.7 = (bf16[2,512,64]{1,2,0:T(8,128)(2,1)S(1)}, bf16[2,512,64]{1,2,0:T(8,128)(2,1)S(1)}, u32[]{:S(2)}, u32[]{:S(2)}) collective-permute-start(bf16[2,512,64]{1,2,0:T(8,128)(2,1)S(1)} %pad_maximum_fusion), channel_id=1, source_target_pairs={{4,8},{8,4},{5,9},{9,5},{6,10},{10,6},{7,11},{11,7},{20,24},{24,20... | collective-permute-start | bytes 393224 | tf_op jit(solution)/shard_map/ppermute | solution.py:69
  74.9 8.4 %collective-permute-start.6 = (bf16[512,1024]{1,0:T(8,128)(2,1)S(1)}, bf16[512,1024]{1,0:T(8,128)(2,1)S(1)}, u32[]{:S(2)}, u32[]{:S(2)}) collective-permute-start(bf16[512,1024]{1,0:T(8,128)(2,1)S(1)} %slice.54), channel_id=1, source_target_pairs={{4,8},{8,4},{5,9},{9,5},{6,10},{10,6},{7,11},{11,7},{20,24},{24,20... | collective-permute-start | bytes 3145736 | tf_op jit(solution)/shard_map/ppermute | solution.py:69
  83.3 45.6 %collective-permute-start.8 = (bf16[512,64]{0,1:T(8,128)(2,1)S(1)}, bf16[512,64]{0,1:T(8,128)(2,1)S(1)}, u32[]{:S(2)}, u32[]{:S(2)}) collective-permute-start(bf16[512,64]{0,1:T(8,128)(2,1)S(1)} %fusion.54), channel_id=1, source_target_pairs={{4,0},{8,12},{5,1},{9,13},{6,2},{10,14},{7,3},{11,15},{20,16},{24,... | collective-permute-start | bytes 196616 | tf_op jit(solution)/shard_map/ppermute | solution.py:69
  84.6 66.8 %collective-permute-start.10 = (bf16[512,1024]{1,0:T(8,128)(2,1)S(1)}, bf16[512,1024]{1,0:T(8,128)(2,1)S(1)}, u32[]{:S(2)}, u32[]{:S(2)}) collective-permute-start(bf16[512,1024]{1,0:T(8,128)(2,1)S(1)} %collective-permute-done.6), channel_id=1, source_target_pairs={{4,0},{8,12},{5,1},{9,13},{6,2},{10,14},{7,3},{11,15},{20,16},{24,... | collective-permute-start | bytes 3145736 | tf_op jit(solution)/shard_map/ppermute | solution.py:69
  90.6 77.5 %collective-permute-start.11 = (bf16[512,768]{1,0:T(8,128)(2,1)S(1)}, bf16[512,768]{1,0:T(8,128)(2,1)S(1)}, u32[]{:S(2)}, u32[]{:S(2)}) collective-permute-start(bf16[512,768]{1,0:T(8,128)(2,1)S(1)} %slice.60), channel_id=1, source_target_pairs={{4,0},{8,12},{5,1},{9,13},{6,2},{10,14},{7,3},{11,15},{20,16},{24,... | collective-permute-start | bytes 2359304 | tf_op jit(solution)/shard_map/ppermute | solution.py:69
  91.9 79.9 %collective-permute-start.12 = (bf16[512,256]{1,0:T(8,128)(2,1)S(1)}, bf16[512,256]{1,0:T(8,128)(2,1)S(1)}, u32[]{:S(2)}, u32[]{:S(2)}) collective-permute-start(bf16[512,256]{1,0:T(8,128)(2,1)S(1)} %slice.61), channel_id=1, source_target_pairs={{4,0},{8,12},{5,1},{9,13},{6,2},{10,14},{7,3},{11,15},{20,16},{24,... | collective-permute-start | bytes 786440 | tf_op jit(solution)/shard_map/ppermute | solution.py:69

commit v16 on v13

--- a/solution.py
+++ b/solution.py
@@ -96,12 +96,12 @@
 
     mid_out = [send(after(mid[0], total), OUTWARD)]
     mate, mate_partial = lax.optimization_barrier((mate, mate_partial, mid[0], total))[:2]
-    first, second = mate[:, :half], mate[:, half:]
     both = send(jnp.stack([partial, mate_partial]), ACROSS)
+    first = mate[:, :half]
     end = [send(first, ACROSS)]
+    end.append(send(after(mate, end[0])[:, half:], ACROSS))
     mid_out.append(send(after(mid[1], first), OUTWARD))
     total = total + product(mate, here ^ 1)
-    end.append(send(after(second, total), ACROSS))
 
     end[0], both = lax.optimization_barrier((end[0], both, total))[:2]
     end_out = [send(end[0], OUTWARD)]

time: 169 us -> 144 us (0.85)
  waiting for transfers between devices: 87.2 us -> 66 us
  matrix products: 48 us -> 44.2 us
    ppermute x13, waiting for transfers between devices: 87.2 us -> 66 us  [send(): return lax.ppermute(block, 'tensor', pairs)]
    dot_general x7, matrix products: 43.5 us -> 39.7 us  [product(): return jnp.dot(block, part, preferred_element_type=F32)]
  transfers between devices with their start and end apart: 13 -> 13, of which waited for: 7 -> 7; matrix products, arithmetic and copies ran while one was open for 31% -> 34% of each run, Pallas kernels for 0% -> 0%
where the time goes in v16:
time: 144 us; the launch traced here: 143 us
  waiting for transfers between devices  66 us (46%)
  matrix products  44.2 us (31%)
  starting transfers between devices  22 us (15%)
  local copies, waits for them, and re-layouts  7.43 us (5%)
  between operations  3.79 us (3%)
    ppermute x13, waiting for transfers between devices, send(): return lax.ppermute(block, 'tensor', pairs)  66 us
    dot_general x7, matrix products, product(): return jnp.dot(block, part, preferred_element_type=F32)  39.7 us
    ppermute x13, starting transfers between devices, send(): return lax.ppermute(block, 'tensor', pairs)  22 us
    dot_general x2, matrix products, shrink(): jnp.dot(inputs[c], shrink_table[adapter_ids[c]], preferred_element_type=F32)  3.52 us
  transfers between devices with their start and end apart: 13, of which 7 were waited for; matrix products, arithmetic and copies ran while one was open for 34% of the time, Pallas kernels for 0%

profile of v16, /device:TPU:0, one launch (start us, length us, event | category | flops | bytes accessed | tf_op | source)
XLA Modules:
  0.0 143.4 jit_solution(321036892468841934)
XLA Ops:
  0.0 3.0 %collective-permute-start = (bf16[512,2048]{1,0:T(8,128)(2,1)}, bf16[512,2048]{1,0:T(8,128)(2,1)}, u32[]{:S(2)}, u32[]{:S(2)}) collective-permute-start(bf16[512,2048]{1,0:T(8,128)(2,1)} %bitcast.39), channel_id=1, source_target_pairs={{0,4},{12,8},{4,0},{8,12},{1,5},{13,9},{5,1},{9,13},{2,6},{14,10},... | collective-permute-start | bytes 6291464 | tf_op jit(solution)/shard_map/ppermute | solution.py:69
  3.0 2.3 %slice.62 = bf16[512,1024]{1,0:T(8,128)(2,1)} slice(bf16[512,2048]{1,0:T(8,128)(2,1)} %bitcast.40), slice={[0:512], [0:1024]} | slice | bytes 2097152 | tf_op jit(solution)/shard_map/slice | solution.py:91
  5.3 1.7 %collective-permute-start.2 = (bf16[512,1024]{1,0:T(8,128)(2,1)}, bf16[512,1024]{1,0:T(8,128)(2,1)}, u32[]{:S(2)}, u32[]{:S(2)}) collective-permute-start(bf16[512,1024]{1,0:T(8,128)(2,1)} %slice.62), channel_id=1, source_target_pairs={{4,8},{8,4},{5,9},{9,5},{6,10},{10,6},{7,11},{11,7},{20,24},{24,20... | collective-permute-start | bytes 3145736 | tf_op jit(solution)/shard_map/ppermute | solution.py:69
  11.8 1.8 %fusion.27 = bf16[256,64]{0,1:T(8,128)(2,1)S(1)} fusion(bf16[2,256,2048]{2,1,0:T(8,128)(2,1)} %param.5, bf16[4,2048,64]{1,2,0:T(8,128)(2,1)} %param.7, s32[]{:T(128)S(6)} %select_n.77), kind=kOutput, calls=%fused_computation.21 | convolution fusion | flops 67125248 | bytes 1343492 | tf_op jit(solution)/shard_map/dot_general | solution.py:12
  13.6 1.8 %fusion.28 = bf16[256,64]{0,1:T(8,128)(2,1)S(1)} fusion(bf16[2,256,2048]{2,1,0:T(8,128)(2,1)} %param.5, bf16[4,2048,64]{1,2,0:T(8,128)(2,1)} %param.7, s32[]{:T(128)S(6)} %select_n.78), kind=kOutput, calls=%fused_computation.22 | convolution fusion | flops 67125248 | bytes 1343492 | tf_op jit(solution)/shard_map/dot_general | solution.py:12
  16.5 1.7 %collective-permute-start.4 = (bf16[512,1024]{1,0:T(8,128)(2,1)}, bf16[512,1024]{1,0:T(8,128)(2,1)}, u32[]{:S(2)}, u32[]{:S(2)}) collective-permute-start(bf16[512,1024]{1,0:T(8,128)(2,1)} %slice.53), channel_id=1, source_target_pairs={{4,8},{8,4},{5,9},{9,5},{6,10},{10,6},{7,11},{11,7},{20,24},{24,20... | collective-permute-start | bytes 3145736 | tf_op jit(solution)/shard_map/ppermute | solution.py:69
  18.2 5.5 %collective-permute-start.1 = (bf16[512,64]{0,1:T(8,128)(2,1)S(1)}, bf16[512,64]{0,1:T(8,128)(2,1)S(1)}, u32[]{:S(2)}, u32[]{:S(2)}) collective-permute-start(bf16[512,64]{0,1:T(8,128)(2,1)S(1)} %get-tuple-element.30), channel_id=1, source_target_pairs={{0,4},{12,8},{1,5},{13,9},{2,6},{14,10},{3,7},{15,11},{16,20},{28,... | collective-permute-start | bytes 196616 | tf_op jit(solution)/shard_map/ppermute | solution.py:69
  23.8 9.4 %fusion.11 = f32[512,2048]{1,0:T(8,128)} fusion(bf16[512,2048]{1,0:T(8,128)(2,1)S(1)} %bitcast.42, bf16[8192,2048]{1,0:T(8,128)(2,1)} %param.6, s32[]{:T(128)S(6)} %select_n.76), kind=kOutput, calls=%fused_computation.13 | convolution fusion | flops 4294967296 | bytes 14680068 | tf_op jit(solution)/shard_map/dot_general | solution.py:88
  34.5 15.1 %collective-permute-done.1 = bf16[512,64]{0,1:T(8,128)(2,1)S(1)} collective-permute-done((bf16[512,64]{0,1:T(8,128)(2,1)S(1)}, bf16[512,64]{0,1:T(8,128)(2,1)S(1)}, u32[]{:S(2)}, u32[]{:S(2)}) %collective-permute-start.1) | collective-permute-done | bytes 65568 | tf_op jit(solution)/shard_map/ppermute | solution.py:69
  49.8 1.3 slice.54
  51.9 1.3 collective-permute-start.5
  53.2 9.7 %fusion.16 = f32[512,2048]{1,0:T(8,128)S(1)} fusion(f32[512,2048]{1,0:T(8,128)} %fusion.11, bf16[512,2048]{1,0:T(8,128)(2,1)} %collective-permute-done, bf16[8192,2048]{1,0:T(8,128)(2,1)} %param.6, s32[]{:T(128)S(6)} %select_n.79), kind=kOutput, calls=%fused_computation.16 | convolution fusion | flops 4296015872 | bytes 18874372 | tf_op jit(solution)/shard_map/dot_general | solution.py:88
  63.6 1.3 slice.57
  65.6 6.6 %collective-permute-done.3 = bf16[512,1024]{1,0:T(8,128)(2,1)S(1)} collective-permute-done((bf16[512,1024]{1,0:T(8,128)(2,1)}, bf16[512,1024]{1,0:T(8,128)(2,1)S(1)}, u32[]{:S(2)}, u32[]{:S(2)}) %collective-permute-start.3) | collective-permute-done | bytes 1048608 | tf_op jit(solution)/shard_map/ppermute | solution.py:69
  72.2 4.5 %fusion.22 = f32[512,2048]{1,0:T(8,128)S(1)} fusion(f32[512,2048]{1,0:T(8,128)S(1)} %fusion.16, bf16[8192,2048]{1,0:T(8,128)(2,1)} %param.6, s32[]{:T(128)S(6)} %select_n.83, bf16[512,1024]{1,0:T(8,128)(2,1)S(1)} %collective-permute-done.3, bf16[512,1024]{1,0:T(8,128)(2,1)} %collective-permute-done.2, pred[]{:T(512)S(6)} %or.3), kind=kOutput, calls=%fused_computation.18 | convolution fusion | flops 2149056512 | bytes 14680069 | tf_op jit(solution)/shard_map/dot_general | solution.py:88
  79.4 15.3 %collective-permute-done.5 = bf16[512,1024]{1,0:T(8,128)(2,1)S(1)} collective-permute-done((bf16[512,1024]{1,0:T(8,128)(2,1)}, bf16[512,1024]{1,0:T(8,128)(2,1)S(1)}, u32[]{:S(2)}, u32[]{:S(2)}) %collective-permute-start.5) | collective-permute-done | bytes 1048608 | tf_op jit(solution)/shard_map/ppermute | solution.py:69
  94.7 4.5 %fusion.7 = f32[512,2048]{1,0:T(8,128)S(1)} fusion(bf16[8192,2048]{1,0:T(8,128)(2,1)} %param.6, s32[]{:T(128)S(6)} %select_n.85, bf16[512,1024]{1,0:T(8,128)(2,1)S(1)} %collective-permute-done.5, bf16[512,1024]{1,0:T(8,128)(2,1)} %collective-permute-done.4, pred[]{:T(512)S(6)} %or.3), kind=kOutput, calls=%fused_computation.9 | convolution fusion | flops 2148007936 | bytes 10485765 | tf_op jit(solution)/shard_map/dot_general | solution.py:88
  99.4 1.3 collective-permute-start.11
  100.7 1.5 %collective-permute-start.12 = (bf16[512,256]{1,0:T(8,128)(2,1)S(1)}, bf16[512,256]{1,0:T(8,128)(2,1)S(1)}, u32[]{:S(2)}, u32[]{:S(2)}) collective-permute-start(bf16[512,256]{1,0:T(8,128)(2,1)S(1)} %slice.61), channel_id=1, source_target_pairs={{4,0},{8,12},{5,1},{9,13},{6,2},{10,14},{7,3},{11,15},{20,16},{24,... | collective-permute-start | bytes 786440 | tf_op jit(solution)/shard_map/ppermute | solution.py:69
  103.1 15.5 %collective-permute-done.10 = bf16[512,1024]{1,0:T(8,128)(2,1)S(1)} collective-permute-done((bf16[512,1024]{1,0:T(8,128)(2,1)S(1)}, bf16[512,1024]{1,0:T(8,128)(2,1)S(1)}, u32[]{:S(2)}, u32[]{:S(2)}) %collective-permute-start.10) | collective-permute-done | bytes 1048608 | tf_op jit(solution)/shard_map/ppermute | solution.py:69
  118.5 4.6 %fusion.4 = f32[512,2048]{1,0:T(8,128)S(1)} fusion(f32[256,2048]{1,0:T(8,128)S(1)} %fusion.42, f32[256,2048]{1,0:T(8,128)S(1)} %fusion.44, f32[512,2048]{1,0:T(8,128)S(1)} %fusion.22, f32[512,2048]{1,0:T(8,128)S(1)} %fusion.7, bf16[8192,2048]{1,0:T(8,128)(2,1)} %param.6, s32[]{:T(128)S(6)} %select_n.90, bf16[512,1024]{1,0:T(8,128)(2,1)S(1)} %collective-permute-done.10, ...), kind=kOutput, calls=%fused_computation.5 | convolution fusion | flops 2152202240 | bytes 23068676 | tf_op jit(solution)/shard_map/dot_general | solution.py:88
  123.2 12.2 %collective-permute-done.11 = bf16[512,768]{1,0:T(8,128)(2,1)S(1)} collective-permute-done((bf16[512,768]{1,0:T(8,128)(2,1)S(1)}, bf16[512,768]{1,0:T(8,128)(2,1)S(1)}, u32[]{:S(2)}, u32[]{:S(2)}) %collective-permute-start.11) | collective-permute-done | bytes 786464 | tf_op jit(solution)/shard_map/ppermute | solution.py:69
  135.4 3.7 %fusion.19 = f32[512,2048]{1,0:T(8,128)S(1)} fusion(f32[512,2048]{1,0:T(8,128)S(1)} %fusion.4, bf16[8192,2048]{1,0:T(8,128)(2,1)} %param.6, s32[]{:T(128)S(6)} %select_n.93, bf16[512,768]{1,0:T(8,128)(2,1)S(1)} %collective-permute-done.11, pred[]{:T(512)S(6)} %or.3, bf16[512,1024]{1,0:T(8,128)(2,1)S(1)} %collective-permute-done.9), kind=kOutput, calls=%fused_computation.17 | convolution fusion | flops 1612054528 | bytes 13107205 | tf_op jit(solution)/shard_map/dot_general | solution.py:88
  140.2 3.3 %add_convert_fusion = bf16[512,2048]{1,0:T(8,128)(2,1)} fusion(f32[512,2048]{1,0:T(8,128)S(1)} %fusion.19, bf16[8192,2048]{1,0:T(8,128)(2,1)} %param.6, s32[]{:T(128)S(6)} %select_n.96, bf16[512,256]{1,0:T(8,128)(2,1)S(1)} %collective-permute-done.12, pred[]{:T(512)S(6)} %or.3, bf16[512,1024]{1,0:T(8,128)(2,1)S(1)} %collective-permute-done.9), kind=kOutput, calls=%fused_computation.6 | convolution fusion | flops 539099136 | bytes 7864325 | tf_op jit(solution)/shard_map/dot_general | solution.py:88
  (28 shorter events, 10.9 us)
Async XLA Ops:
  0.0 102.2 %copy-start = (bf16[4,64,2048]{2,1,0:T(8,128)(2,1)S(1)}, bf16[4,64,2048]{2,1,0:T(8,128)(2,1)}, u32[]{:S(2)}) copy-start(bf16[4,64,2048]{2,1,0:T(8,128)(2,1)} %param.8) | copy-start | bytes 3145732
  0.0 15.3 %copy-start.1 = (bf16[2,256,2048]{2,1,0:T(8,128)(2,1)S(1)}, bf16[2,256,2048]{2,1,0:T(8,128)(2,1)}, u32[]{:S(2)}) copy-start(bf16[2,256,2048]{2,1,0:T(8,128)(2,1)} %param.5) | copy-start | bytes 6291460
  0.0 49.8 %collective-permute-start = (bf16[512,2048]{1,0:T(8,128)(2,1)}, bf16[512,2048]{1,0:T(8,128)(2,1)}, u32[]{:S(2)}, u32[]{:S(2)}) collective-permute-start(bf16[512,2048]{1,0:T(8,128)(2,1)} %bitcast.39), channel_id=1, source_target_pairs={{0,4},{12,8},{4,0},{8,12},{1,5},{13,9},{5,1},{9,13},{2,6},{14,10},... | collective-permute-start | bytes 6291464 | tf_op jit(solution)/shard_map/ppermute | solution.py:69
  5.3 27.8 %collective-permute-start.2 = (bf16[512,1024]{1,0:T(8,128)(2,1)}, bf16[512,1024]{1,0:T(8,128)(2,1)}, u32[]{:S(2)}, u32[]{:S(2)}) collective-permute-start(bf16[512,1024]{1,0:T(8,128)(2,1)} %slice.62), channel_id=1, source_target_pairs={{4,8},{8,4},{5,9},{9,5},{6,10},{10,6},{7,11},{11,7},{20,24},{24,20... | collective-permute-start | bytes 3145736 | tf_op jit(solution)/shard_map/ppermute | solution.py:69
  16.5 35.4 %collective-permute-start.4 = (bf16[512,1024]{1,0:T(8,128)(2,1)}, bf16[512,1024]{1,0:T(8,128)(2,1)}, u32[]{:S(2)}, u32[]{:S(2)}) collective-permute-start(bf16[512,1024]{1,0:T(8,128)(2,1)} %slice.53), channel_id=1, source_target_pairs={{4,8},{8,4},{5,9},{9,5},{6,10},{10,6},{7,11},{11,7},{20,24},{24,20... | collective-permute-start | bytes 3145736 | tf_op jit(solution)/shard_map/ppermute | solution.py:69
  18.2 31.3 %collective-permute-start.1 = (bf16[512,64]{0,1:T(8,128)(2,1)S(1)}, bf16[512,64]{0,1:T(8,128)(2,1)S(1)}, u32[]{:S(2)}, u32[]{:S(2)}) collective-permute-start(bf16[512,64]{0,1:T(8,128)(2,1)S(1)} %get-tuple-element.30), channel_id=1, source_target_pairs={{0,4},{12,8},{1,5},{13,9},{2,6},{14,10},{3,7},{15,11},{16,20},{28,... | collective-permute-start | bytes 196616 | tf_op jit(solution)/shard_map/ppermute | solution.py:69
  33.2 39.0 %collective-permute-start.3 = (bf16[512,1024]{1,0:T(8,128)(2,1)}, bf16[512,1024]{1,0:T(8,128)(2,1)S(1)}, u32[]{:S(2)}, u32[]{:S(2)}) collective-permute-start(bf16[512,1024]{1,0:T(8,128)(2,1)} %collective-permute-done.2), channel_id=1, source_target_pairs={{4,0},{8,12},{5,1},{9,13},{6,2},{10,14},{7,3},{11,15},{20,16},{24,... | collective-permute-start | bytes 3145736 | tf_op jit(solution)/shard_map/ppermute | solution.py:69
  51.1 12.4 %collective-permute-start.6 = (bf16[512,1024]{1,0:T(8,128)(2,1)S(1)}, bf16[512,1024]{1,0:T(8,128)(2,1)S(1)}, u32[]{:S(2)}, u32[]{:S(2)}) collective-permute-start(bf16[512,1024]{1,0:T(8,128)(2,1)S(1)} %slice.54), channel_id=1, source_target_pairs={{4,8},{8,4},{5,9},{9,5},{6,10},{10,6},{7,11},{11,7},{20,24},{24,20... | collective-permute-start | bytes 3145736 | tf_op jit(solution)/shard_map/ppermute | solution.py:69
  51.9 42.8 %collective-permute-start.5 = (bf16[512,1024]{1,0:T(8,128)(2,1)}, bf16[512,1024]{1,0:T(8,128)(2,1)S(1)}, u32[]{:S(2)}, u32[]{:S(2)}) collective-permute-start(bf16[512,1024]{1,0:T(8,128)(2,1)} %collective-permute-done.4), channel_id=1, source_target_pairs={{4,0},{8,12},{5,1},{9,13},{6,2},{10,14},{7,3},{11,15},{20,16},{24,... | collective-permute-start | bytes 3145736 | tf_op jit(solution)/shard_map/ppermute | solution.py:69
  62.9 13.9 %collective-permute-start.7 = (bf16[2,512,64]{1,2,0:T(8,128)(2,1)S(1)}, bf16[2,512,64]{1,2,0:T(8,128)(2,1)S(1)}, u32[]{:S(2)}, u32[]{:S(2)}) collective-permute-start(bf16[2,512,64]{1,2,0:T(8,128)(2,1)S(1)} %pad_maximum_fusion), channel_id=1, source_target_pairs={{4,8},{8,4},{5,9},{9,5},{6,10},{10,6},{7,11},{11,7},{20,24},{24,20... | collective-permute-start | bytes 393224 | tf_op jit(solution)/shard_map/ppermute | solution.py:69
  64.9 34.4 %collective-permute-start.9 = (bf16[512,1024]{1,0:T(8,128)(2,1)S(1)}, bf16[512,1024]{1,0:T(8,128)(2,1)S(1)}, u32[]{:S(2)}, u32[]{:S(2)}) collective-permute-start(bf16[512,1024]{1,0:T(8,128)(2,1)S(1)} %slice.57), channel_id=1, source_target_pairs={{4,8},{8,4},{5,9},{9,5},{6,10},{10,6},{7,11},{11,7},{20,24},{24,20... | collective-permute-start | bytes 3145736 | tf_op jit(solution)/shard_map/ppermute | solution.py:69
  76.8 22.4 %collective-permute-start.8 = (bf16[512,64]{0,1:T(8,128)(2,1)S(1)}, bf16[512,64]{0,1:T(8,128)(2,1)S(1)}, u32[]{:S(2)}, u32[]{:S(2)}) collective-permute-start(bf16[512,64]{0,1:T(8,128)(2,1)S(1)} %fusion.54), channel_id=1, source_target_pairs={{4,0},{8,12},{5,1},{9,13},{6,2},{10,14},{7,3},{11,15},{20,16},{24,... | collective-permute-start | bytes 196616 | tf_op jit(solution)/shard_map/ppermute | solution.py:69
  78.1 40.4 %collective-permute-start.10 = (bf16[512,1024]{1,0:T(8,128)(2,1)S(1)}, bf16[512,1024]{1,0:T(8,128)(2,1)S(1)}, u32[]{:S(2)}, u32[]{:S(2)}) collective-permute-start(bf16[512,1024]{1,0:T(8,128)(2,1)S(1)} %collective-permute-done.6), channel_id=1, source_target_pairs={{4,0},{8,12},{5,1},{9,13},{6,2},{10,14},{7,3},{11,15},{20,16},{24,... | collective-permute-start | bytes 3145736 | tf_op jit(solution)/shard_map/ppermute | solution.py:69
  99.4 36.0 %collective-permute-start.11 = (bf16[512,768]{1,0:T(8,128)(2,1)S(1)}, bf16[512,768]{1,0:T(8,128)(2,1)S(1)}, u32[]{:S(2)}, u32[]{:S(2)}) collective-permute-start(bf16[512,768]{1,0:T(8,128)(2,1)S(1)} %slice.60), channel_id=1, source_target_pairs={{4,0},{8,12},{5,1},{9,13},{6,2},{10,14},{7,3},{11,15},{20,16},{24,... | collective-permute-start | bytes 2359304 | tf_op jit(solution)/shard_map/ppermute | solution.py:69
  100.7 39.5 %collective-permute-start.12 = (bf16[512,256]{1,0:T(8,128)(2,1)S(1)}, bf16[512,256]{1,0:T(8,128)(2,1)S(1)}, u32[]{:S(2)}, u32[]{:S(2)}) collective-permute-start(bf16[512,256]{1,0:T(8,128)(2,1)S(1)} %slice.61), channel_id=1, source_target_pairs={{4,0},{8,12},{5,1},{9,13},{6,2},{10,14},{7,3},{11,15},{20,16},{24,... | collective-permute-start | bytes 786440 | tf_op jit(solution)/shard_map/ppermute | solution.py:69

commit v17 on v16

--- a/solution.py
+++ b/solution.py
@@ -81,7 +81,7 @@
     far_mid = jnp.where(here < 2, 2, 1)
     far_end = jnp.where(here < 2, 3, 0)
     own = inputs.reshape(rows, width)
-    half, last = width // 2, width // 8
+    half, quarter = width // 2, width // 4
 
     def product(block, owner, first=0):
         part = lax.dynamic_slice_in_dim(base_weight, owner * width + first, block.shape[1], axis=0)
@@ -108,19 +108,22 @@
     shrunk = (
         partial.astype(F32) + mate_partial.astype(F32) + both[0].astype(F32) + both[1].astype(F32)
     ).astype(BF16)
-    shrunk = jnp.where(is_end, send(shrunk, OUTWARD), shrunk)
     total = total + product(jnp.where(is_end, mid_out[0], mid[0]), far_mid)
 
     late = after(end[1], total)
-    shrunk = after(shrunk, late)
-    end_out += [send(late[:, : half - last], OUTWARD), send(late[:, half - last :], OUTWARD)]
+    rider = shrunk.reshape(-1, quarter)
+    end_out += [
+        send(jnp.concatenate([late[:, :quarter], rider]), OUTWARD),
+        send(late[:, quarter:], OUTWARD),
+    ]
     total = total + product(jnp.where(is_end, mid_out[1], mid[1]), far_mid, half)
+    total = total + product(jnp.where(is_end, after(end_out[0], total), end[0]), far_end)
+    ridden = after(end_out[1], total)
+    shrunk = jnp.where(is_end, ridden[rows:].reshape(shrunk.shape), shrunk)
     total = total + jnp.concatenate(expand(shrunk, expand_table, adapter_ids))
-    total = total + product(jnp.where(is_end, end_out[0], end[0]), far_end)
-    block = jnp.where(is_end, after(end_out[1], total), late[:, : half - last])
-    total = total + product(block, far_end, half)
-    block = jnp.where(is_end, after(end_out[2], total), late[:, half - last :])
-    total = total + product(block, far_end, width - last)
+    total = total + product(jnp.where(is_end, ridden[:rows], late[:, :quarter]), far_end, half)
+    block = jnp.where(is_end, after(end_out[2], total), late[:, quarter:])
+    total = total + product(block, far_end, half + quarter)
     return total.astype(BF16).reshape(chats, span, -1)
 
 

time: 144 us -> 151 us (1.049)
  matrix products: 44.2 us -> 49.9 us
  local copies, waits for them, and re-layouts: 7.43 us -> 10.4 us
    dot_general x7, matrix products: 39.7 us -> 45.5 us  [product(): return jnp.dot(block, part, preferred_element_type=F32)]
    ppermute x13 -> x12, waiting for transfers between devices: 66 us -> 64.7 us  [send(): return lax.ppermute(block, 'tensor', pairs)]
    ppermute x13 -> x12, starting transfers between devices: 22 us -> 20.8 us  [send(): return lax.ppermute(block, 'tensor', pairs)]
  transfers between devices with their start and end apart: 13 -> 12, of which waited for: 7 -> 6; matrix products, arithmetic and copies ran while one was open for 34% -> 37% of each run, Pallas kernels for 0% -> 0%
where the time goes in v17:
time: 151 us; the launch traced here: 150 us
  waiting for transfers between devices  64.7 us (43%)
  matrix products  49.9 us (33%)
  starting transfers between devices  20.8 us (14%)
  local copies, waits for them, and re-layouts  10.4 us (7%)
  between operations  4 us (3%)
    ppermute x12, waiting for transfers between devices, send(): return lax.ppermute(block, 'tensor', pairs)  64.7 us
    dot_general x7, matrix products, product(): return jnp.dot(block, part, preferred_element_type=F32)  45.5 us
    ppermute x12, starting transfers between devices, send(): return lax.ppermute(block, 'tensor', pairs)  20.8 us
    dot_general x2, matrix products, shrink(): jnp.dot(inputs[c], shrink_table[adapter_ids[c]], preferred_element_type=F32)  3.52 us
  transfers between devices with their start and end apart: 12, of which 6 were waited for; matrix products, arithmetic and copies ran while one was open for 37% of the time, Pallas kernels for 0%

profile of v17, /device:TPU:0, one launch (start us, length us, event | category | flops | bytes accessed | tf_op | source)
XLA Modules:
  0.0 149.9 jit_solution(12062683018501227198)
XLA Ops:
  0.0 3.0 %collective-permute-start = (bf16[512,2048]{1,0:T(8,128)(2,1)}, bf16[512,2048]{1,0:T(8,128)(2,1)}, u32[]{:S(2)}, u32[]{:S(2)}) collective-permute-start(bf16[512,2048]{1,0:T(8,128)(2,1)} %bitcast.39), channel_id=1, source_target_pairs={{0,4},{12,8},{4,0},{8,12},{1,5},{13,9},{5,1},{9,13},{2,6},{14,10},... | collective-permute-start | bytes 6291464 | tf_op jit(solution)/shard_map/ppermute | solution.py:69
  3.0 2.3 %slice.70 = bf16[512,1024]{1,0:T(8,128)(2,1)} slice(bf16[512,2048]{1,0:T(8,128)(2,1)} %bitcast.40), slice={[0:512], [0:1024]} | slice | bytes 2097152 | tf_op jit(solution)/shard_map/slice | solution.py:91
  5.3 1.6 %collective-permute-start.2 = (bf16[512,1024]{1,0:T(8,128)(2,1)}, bf16[512,1024]{1,0:T(8,128)(2,1)}, u32[]{:S(2)}, u32[]{:S(2)}) collective-permute-start(bf16[512,1024]{1,0:T(8,128)(2,1)} %slice.70), channel_id=1, source_target_pairs={{4,8},{8,4},{5,9},{9,5},{6,10},{10,6},{7,11},{11,7},{20,24},{24,20... | collective-permute-start | bytes 3145736 | tf_op jit(solution)/shard_map/ppermute | solution.py:69
  7.0 1.3 fusion.73
  12.0 1.8 %fusion.28 = bf16[256,64]{0,1:T(8,128)(2,1)S(1)} fusion(bf16[2,256,2048]{2,1,0:T(8,128)(2,1)} %param.5, bf16[4,2048,64]{1,2,0:T(8,128)(2,1)} %param.7, s32[]{:T(128)S(6)} %select_n.73), kind=kOutput, calls=%fused_computation.22 | convolution fusion | flops 67125248 | bytes 1343492 | tf_op jit(solution)/shard_map/dot_general | solution.py:12
  13.8 1.8 %fusion.29 = bf16[256,64]{0,1:T(8,128)(2,1)S(1)} fusion(bf16[2,256,2048]{2,1,0:T(8,128)(2,1)} %param.5, bf16[4,2048,64]{1,2,0:T(8,128)(2,1)} %param.7, s32[]{:T(128)S(6)} %select_n.74), kind=kOutput, calls=%fused_computation.23 | convolution fusion | flops 67125248 | bytes 1343492 | tf_op jit(solution)/shard_map/dot_general | solution.py:12
  16.7 1.7 %collective-permute-start.4 = (bf16[512,1024]{1,0:T(8,128)(2,1)}, bf16[512,1024]{1,0:T(8,128)(2,1)}, u32[]{:S(2)}, u32[]{:S(2)}) collective-permute-start(bf16[512,1024]{1,0:T(8,128)(2,1)} %slice.59), channel_id=1, source_target_pairs={{4,8},{8,4},{5,9},{9,5},{6,10},{10,6},{7,11},{11,7},{20,24},{24,20... | collective-permute-start | bytes 3145736 | tf_op jit(solution)/shard_map/ppermute | solution.py:69
  18.4 5.6 %collective-permute-start.1 = (bf16[512,64]{0,1:T(8,128)(2,1)S(1)}, bf16[512,64]{0,1:T(8,128)(2,1)S(1)}, u32[]{:S(2)}, u32[]{:S(2)}) collective-permute-start(bf16[512,64]{0,1:T(8,128)(2,1)S(1)} %get-tuple-element.32), channel_id=1, source_target_pairs={{0,4},{12,8},{1,5},{13,9},{2,6},{14,10},{3,7},{15,11},{16,20},{28,... | collective-permute-start | bytes 196616 | tf_op jit(solution)/shard_map/ppermute | solution.py:69
  24.0 9.4 %fusion.11 = f32[512,2048]{1,0:T(8,128)} fusion(bf16[512,2048]{1,0:T(8,128)(2,1)S(1)} %bitcast.42, bf16[8192,2048]{1,0:T(8,128)(2,1)} %param.6, s32[]{:T(128)S(6)} %select_n.72), kind=kOutput, calls=%fused_computation.13 | convolution fusion | flops 4294967296 | bytes 14680068 | tf_op jit(solution)/shard_map/dot_general | solution.py:88
  34.7 14.8 %collective-permute-done.1 = bf16[512,64]{0,1:T(8,128)(2,1)S(1)} collective-permute-done((bf16[512,64]{0,1:T(8,128)(2,1)S(1)}, bf16[512,64]{0,1:T(8,128)(2,1)S(1)}, u32[]{:S(2)}, u32[]{:S(2)}) %collective-permute-start.1) | collective-permute-done | bytes 65568 | tf_op jit(solution)/shard_map/ppermute | solution.py:69
  50.5 1.3 slice.60
  53.9 9.7 %fusion.14 = f32[512,2048]{1,0:T(8,128)S(1)} fusion(f32[512,2048]{1,0:T(8,128)} %fusion.11, bf16[512,2048]{1,0:T(8,128)(2,1)} %collective-permute-done, bf16[8192,2048]{1,0:T(8,128)(2,1)} %param.6, s32[]{:T(128)S(6)} %select_n.75), kind=kOutput, calls=%fused_computation.14 | convolution fusion | flops 4296015872 | bytes 18874372 | tf_op jit(solution)/shard_map/dot_general | solution.py:88
  63.6 1.7 %slice.61 = bf16[512,1024]{1,0:T(8,128)(2,1)S(1)} slice(bf16[512,2048]{1,0:T(8,128)(2,1)} %collective-permute-done), slice={[0:512], [1024:2048]} | slice | bytes 2097152 | tf_op jit(solution)/shard_map/slice | solution.py:102
  66.0 6.2 %collective-permute-done.3 = bf16[512,1024]{1,0:T(8,128)(2,1)S(1)} collective-permute-done((bf16[512,1024]{1,0:T(8,128)(2,1)}, bf16[512,1024]{1,0:T(8,128)(2,1)S(1)}, u32[]{:S(2)}, u32[]{:S(2)}) %collective-permute-start.3) | collective-permute-done | bytes 1048608 | tf_op jit(solution)/shard_map/ppermute | solution.py:69
  72.2 6.5 %fusion.17 = f32[512,2048]{1,0:T(8,128)} fusion(f32[512,2048]{1,0:T(8,128)S(1)} %fusion.14, bf16[8192,2048]{1,0:T(8,128)(2,1)} %param.6, s32[]{:T(128)S(6)} %select_n.79, bf16[512,1024]{1,0:T(8,128)(2,1)S(1)} %collective-permute-done.3, bf16[512,1024]{1,0:T(8,128)(2,1)} %collective-permute-done.2, pred[]{:T(512)S(6)} %or.3), kind=kOutput, calls=%fused_computation.15 | convolution fusion | flops 2149056512 | bytes 14680069 | tf_op jit(solution)/shard_map/dot_general | solution.py:88
  79.1 1.4 collective-permute-start.8
  80.5 13.4 %collective-permute-done.5 = bf16[512,1024]{1,0:T(8,128)(2,1)} collective-permute-done((bf16[512,1024]{1,0:T(8,128)(2,1)}, bf16[512,1024]{1,0:T(8,128)(2,1)}, u32[]{:S(2)}, u32[]{:S(2)}) %collective-permute-start.5) | collective-permute-done | bytes 1048608 | tf_op jit(solution)/shard_map/ppermute | solution.py:69
  93.9 6.1 %fusion.20 = f32[512,2048]{1,0:T(8,128)S(1)} fusion(f32[512,2048]{1,0:T(8,128)} %fusion.17, bf16[8192,2048]{1,0:T(8,128)(2,1)} %param.6, s32[]{:T(128)S(6)} %select_n.81, bf16[512,1024]{1,0:T(8,128)(2,1)} %collective-permute-done.5, bf16[512,1024]{1,0:T(8,128)(2,1)} %collective-permute-done.4, pred[]{:T(512)S(6)} %or.3), kind=kOutput, calls=%fused_computation.16 | convolution fusion | flops 2149056512 | bytes 14680069 | tf_op jit(solution)/shard_map/dot_general | solution.py:88
  102.3 1.5 collective-permute-start.10
  103.8 15.8 %collective-permute-done.8 = bf16[512,1024]{1,0:T(8,128)(2,1)S(1)} collective-permute-done((bf16[512,1024]{1,0:T(8,128)(2,1)}, bf16[512,1024]{1,0:T(8,128)(2,1)S(1)}, u32[]{:S(2)}, u32[]{:S(2)}) %collective-permute-start.8) | collective-permute-done | bytes 1048608 | tf_op jit(solution)/shard_map/ppermute | solution.py:69
  119.5 6.6 %fusion.23 = f32[512,2048]{1,0:T(8,128)} fusion(f32[512,2048]{1,0:T(8,128)S(1)} %fusion.20, bf16[8192,2048]{1,0:T(8,128)(2,1)} %param.6, s32[]{:T(128)S(6)} %select_n.84, bf16[512,1024]{1,0:T(8,128)(2,1)S(1)} %collective-permute-done.8, bf16[512,1024]{1,0:T(8,128)(2,1)S(1)} %copy-done.4, pred[]{:T(512)S(6)} %or.3), kind=kOutput, calls=%fused_computation.17 | convolution fusion | flops 2149056512 | bytes 14680069 | tf_op jit(solution)/shard_map/dot_general | solution.py:88
  126.1 14.1 %collective-permute-done.10 = bf16[576,512]{1,0:T(8,128)(2,1)S(1)} collective-permute-done((bf16[576,512]{1,0:T(8,128)(2,1)S(1)}, bf16[576,512]{1,0:T(8,128)(2,1)S(1)}, u32[]{:S(2)}, u32[]{:S(2)}) %collective-permute-start.10) | collective-permute-done | bytes 589856 | tf_op jit(solution)/shard_map/ppermute | solution.py:69
  142.7 2.9 %fusion.4 = f32[512,2048]{1,0:T(8,128)S(1)} fusion(f32[512,2048]{1,0:T(8,128)S(1)} %copy-done.1, f32[256,2048]{1,0:T(8,128)S(1)} %fusion.45, f32[256,2048]{1,0:T(8,128)S(1)} %fusion.47, bf16[8192,2048]{1,0:T(8,128)(2,1)} %param.6, s32[]{:T(128)S(6)} %select_n.89, bf16[576,512]{1,0:T(8,128)(2,1)S(1)} %collective-permute-done.10, pred[]{:T(512)S(6)} %or.3, ...), kind=kOutput, calls=%fused_computation.5 | convolution fusion | flops 1077149696 | bytes 15728645 | tf_op jit(solution)/shard_map/dot_general | solution.py:88
  145.6 4.2 %add_convert_fusion = bf16[512,2048]{1,0:T(8,128)(2,1)} fusion(f32[512,2048]{1,0:T(8,128)S(1)} %fusion.4, bf16[8192,2048]{1,0:T(8,128)(2,1)} %param.6, s32[]{:T(128)S(6)} %select_n.91, bf16[512,512]{1,0:T(8,128)(2,1)S(1)} %collective-permute-done.11, pred[]{:T(512)S(6)} %or.3, bf16[512,1024]{1,0:T(8,128)(2,1)S(1)} %collective-permute-done.9), kind=kOutput, calls=%fused_computation.6 | convolution fusion | flops 1076101120 | bytes 9437189 | tf_op jit(solution)/shard_map/dot_general | solution.py:88
  (37 shorter events, 11.1 us)
Async XLA Ops:
  0.0 140.5 %copy-start = (bf16[4,64,2048]{2,1,0:T(8,128)(2,1)S(1)}, bf16[4,64,2048]{2,1,0:T(8,128)(2,1)}, u32[]{:S(2)}) copy-start(bf16[4,64,2048]{2,1,0:T(8,128)(2,1)} %param.8) | copy-start | bytes 3145732
  0.0 15.6 %copy-start.2 = (bf16[2,256,2048]{2,1,0:T(8,128)(2,1)S(1)}, bf16[2,256,2048]{2,1,0:T(8,128)(2,1)}, u32[]{:S(2)}) copy-start(bf16[2,256,2048]{2,1,0:T(8,128)(2,1)} %param.5) | copy-start | bytes 6291460
  0.0 49.8 %collective-permute-start = (bf16[512,2048]{1,0:T(8,128)(2,1)}, bf16[512,2048]{1,0:T(8,128)(2,1)}, u32[]{:S(2)}, u32[]{:S(2)}) collective-permute-start(bf16[512,2048]{1,0:T(8,128)(2,1)} %bitcast.39), channel_id=1, source_target_pairs={{0,4},{12,8},{4,0},{8,12},{1,5},{13,9},{5,1},{9,13},{2,6},{14,10},... | collective-permute-start | bytes 6291464 | tf_op jit(solution)/shard_map/ppermute | solution.py:69
  5.3 28.1 %collective-permute-start.2 = (bf16[512,1024]{1,0:T(8,128)(2,1)}, bf16[512,1024]{1,0:T(8,128)(2,1)}, u32[]{:S(2)}, u32[]{:S(2)}) collective-permute-start(bf16[512,1024]{1,0:T(8,128)(2,1)} %slice.70), channel_id=1, source_target_pairs={{4,8},{8,4},{5,9},{9,5},{6,10},{10,6},{7,11},{11,7},{20,24},{24,20... | collective-permute-start | bytes 3145736 | tf_op jit(solution)/shard_map/ppermute | solution.py:69
  16.7 35.8 %collective-permute-start.4 = (bf16[512,1024]{1,0:T(8,128)(2,1)}, bf16[512,1024]{1,0:T(8,128)(2,1)}, u32[]{:S(2)}, u32[]{:S(2)}) collective-permute-start(bf16[512,1024]{1,0:T(8,128)(2,1)} %slice.59), channel_id=1, source_target_pairs={{4,8},{8,4},{5,9},{9,5},{6,10},{10,6},{7,11},{11,7},{20,24},{24,20... | collective-permute-start | bytes 3145736 | tf_op jit(solution)/shard_map/ppermute | solution.py:69
  18.4 31.1 %collective-permute-start.1 = (bf16[512,64]{0,1:T(8,128)(2,1)S(1)}, bf16[512,64]{0,1:T(8,128)(2,1)S(1)}, u32[]{:S(2)}, u32[]{:S(2)}) collective-permute-start(bf16[512,64]{0,1:T(8,128)(2,1)S(1)} %get-tuple-element.32), channel_id=1, source_target_pairs={{0,4},{12,8},{1,5},{13,9},{2,6},{14,10},{3,7},{15,11},{16,20},{28,... | collective-permute-start | bytes 196616 | tf_op jit(solution)/shard_map/ppermute | solution.py:69
  33.4 38.8 %collective-permute-start.3 = (bf16[512,1024]{1,0:T(8,128)(2,1)}, bf16[512,1024]{1,0:T(8,128)(2,1)S(1)}, u32[]{:S(2)}, u32[]{:S(2)}) collective-permute-start(bf16[512,1024]{1,0:T(8,128)(2,1)} %collective-permute-done.2), channel_id=1, source_target_pairs={{4,0},{8,12},{5,1},{9,13},{6,2},{10,14},{7,3},{11,15},{20,16},{24,... | collective-permute-start | bytes 3145736 | tf_op jit(solution)/shard_map/ppermute | solution.py:69
  49.9 28.9 %collective-permute-start.7 = (bf16[2,512,64]{1,2,0:T(8,128)(2,1)S(1)}, bf16[2,512,64]{1,2,0:T(8,128)(2,1)S(1)}, u32[]{:S(2)}, u32[]{:S(2)}) collective-permute-start(bf16[2,512,64]{1,2,0:T(8,128)(2,1)S(1)} %pad_maximum_fusion.1), channel_id=1, source_target_pairs={{4,8},{8,4},{5,9},{9,5},{6,10},{10,6},{7,11},{11,7},{20,24},{24,20... | collective-permute-start | bytes 393224 | tf_op jit(solution)/shard_map/ppermute | solution.py:69
  51.8 11.7 %collective-permute-start.6 = (bf16[512,1024]{1,0:T(8,128)(2,1)S(1)}, bf16[512,1024]{1,0:T(8,128)(2,1)S(1)}, u32[]{:S(2)}, u32[]{:S(2)}) collective-permute-start(bf16[512,1024]{1,0:T(8,128)(2,1)S(1)} %slice.60), channel_id=1, source_target_pairs={{4,8},{8,4},{5,9},{9,5},{6,10},{10,6},{7,11},{11,7},{20,24},{24,20... | collective-permute-start | bytes 3145736 | tf_op jit(solution)/shard_map/ppermute | solution.py:69
  52.6 41.4 %collective-permute-start.5 = (bf16[512,1024]{1,0:T(8,128)(2,1)}, bf16[512,1024]{1,0:T(8,128)(2,1)}, u32[]{:S(2)}, u32[]{:S(2)}) collective-permute-start(bf16[512,1024]{1,0:T(8,128)(2,1)} %collective-permute-done.4), channel_id=1, source_target_pairs={{4,0},{8,12},{5,1},{9,13},{6,2},{10,14},{7,3},{11,15},{20,16},{24,... | collective-permute-start | bytes 3145736 | tf_op jit(solution)/shard_map/ppermute | solution.py:69
  63.6 15.2 %copy-start.3 = (bf16[512,1024]{1,0:T(8,128)(2,1)}, bf16[512,1024]{1,0:T(8,128)(2,1)S(1)}, u32[]{:S(2)}) copy-start(bf16[512,1024]{1,0:T(8,128)(2,1)S(1)} %collective-permute-done.6) | copy-start | bytes 3145732
  65.2 34.8 %collective-permute-start.9 = (bf16[512,1024]{1,0:T(8,128)(2,1)S(1)}, bf16[512,1024]{1,0:T(8,128)(2,1)S(1)}, u32[]{:S(2)}, u32[]{:S(2)}) collective-permute-start(bf16[512,1024]{1,0:T(8,128)(2,1)S(1)} %slice.61), channel_id=1, source_target_pairs={{4,8},{8,4},{5,9},{9,5},{6,10},{10,6},{7,11},{11,7},{20,24},{24,20... | collective-permute-start | bytes 3145736 | tf_op jit(solution)/shard_map/ppermute | solution.py:69
  79.1 40.5 %copy-start.4 = (bf16[512,1024]{1,0:T(8,128)(2,1)S(1)}, bf16[512,1024]{1,0:T(8,128)(2,1)}, u32[]{:S(2)}) copy-start(bf16[512,1024]{1,0:T(8,128)(2,1)} %copy-done.3) | copy-start | bytes 3145732
  79.1 40.5 %collective-permute-start.8 = (bf16[512,1024]{1,0:T(8,128)(2,1)}, bf16[512,1024]{1,0:T(8,128)(2,1)S(1)}, u32[]{:S(2)}, u32[]{:S(2)}) collective-permute-start(bf16[512,1024]{1,0:T(8,128)(2,1)} %copy-done.3), channel_id=1, source_target_pairs={{4,0},{8,12},{5,1},{9,13},{6,2},{10,14},{7,3},{11,15},{20,16},{24,... | collective-permute-start | bytes 3145736 | tf_op jit(solution)/shard_map/ppermute | solution.py:69
  101.0 44.7 %collective-permute-start.11 = (bf16[512,512]{1,0:T(8,128)(2,1)}, bf16[512,512]{1,0:T(8,128)(2,1)S(1)}, u32[]{:S(2)}, u32[]{:S(2)}) collective-permute-start(bf16[512,512]{1,0:T(8,128)(2,1)} %get-tuple-element.29), channel_id=1, source_target_pairs={{4,0},{8,12},{5,1},{9,13},{6,2},{10,14},{7,3},{11,15},{20,16},{24,... | collective-permute-start | bytes 1572872 | tf_op jit(solution)/shard_map/ppermute | solution.py:69
  102.3 37.9 %collective-permute-start.10 = (bf16[576,512]{1,0:T(8,128)(2,1)S(1)}, bf16[576,512]{1,0:T(8,128)(2,1)S(1)}, u32[]{:S(2)}, u32[]{:S(2)}) collective-permute-start(bf16[576,512]{1,0:T(8,128)(2,1)S(1)} %pad_maximum_fusion), channel_id=1, source_target_pairs={{4,0},{8,12},{5,1},{9,13},{6,2},{10,14},{7,3},{11,15},{20,16},{24,... | collective-permute-start | bytes 1769480 | tf_op jit(solution)/shard_map/ppermute | solution.py:69
  140.5 2.2 %copy-start.1 = (f32[512,2048]{1,0:T(8,128)S(1)}, f32[512,2048]{1,0:T(8,128)}, u32[]{:S(2)}) copy-start(f32[512,2048]{1,0:T(8,128)} %fusion.23) | copy-start | bytes 12582916

commit v18 on v16

--- a/solution.py
+++ b/solution.py
@@ -1,6 +1,8 @@
 import jax
 import jax.numpy as jnp
 from jax import lax
+from jax.experimental import pallas as pl
+from jax.experimental.pallas import tpu as pltpu
 from jax.sharding import PartitionSpec as P
 
 F32, BF16 = jnp.float32, jnp.bfloat16
@@ -73,6 +75,31 @@
     return lax.optimization_barrier((block,) + earlier)[0]
 
 
+def resident(block, cuts):
+    def kernel(source, *refs):
+        outs, sems = refs[: len(cuts)], refs[len(cuts)]
+        copies = [
+            pltpu.make_async_copy(source.at[:, cut], out, sems.at[i])
+            for i, (cut, out) in enumerate(zip(cuts, outs))
+        ]
+        for copy in copies:
+            copy.start()
+        for copy in copies:
+            copy.wait()
+
+    rows = block.shape[0]
+    size = sum(cut.size for cut in cuts) * rows * block.dtype.itemsize
+    return pl.pallas_call(
+        kernel,
+        out_shape=[pltpu.VMEM((rows, cut.size), block.dtype) for cut in cuts],
+        in_specs=[pl.BlockSpec(memory_space=pl.ANY)],
+        out_specs=[pl.BlockSpec(memory_space=pltpu.VMEM) for _ in cuts],
+        scratch_shapes=[pltpu.SemaphoreType.DMA((len(cuts),))],
+        compiler_params=pltpu.CompilerParams(vmem_limit_bytes=4 * 2**20),
+        cost_estimate=pl.CostEstimate(flops=0, bytes_accessed=2 * size, transcendentals=0),
+    )(block)
+
+
 def line(inputs, base_weight, shrink_table, expand_table, adapter_ids):
     chats, span, width = inputs.shape
     rows = chats * span
@@ -87,10 +114,11 @@
         part = lax.dynamic_slice_in_dim(base_weight, owner * width + first, block.shape[1], axis=0)
         return jnp.dot(block, part, preferred_element_type=F32)
 
-    mate = send(own, SWAP)
-    mid = [send(own[:, :half], ACROSS)]
+    whole, left, right = resident(own, [pl.ds(0, width), pl.ds(0, half), pl.ds(half, half)])
+    mate = send(whole, SWAP)
+    mid = [send(left, ACROSS)]
     partial = shrink(inputs, shrink_table, adapter_ids)
-    mid.append(send(after(own, partial)[:, half:], ACROSS))
+    mid.append(send(after(right, partial), ACROSS))
     mate_partial = send(partial, INWARD)
     total = product(own, here)
 

time: 144 us -> 149 us (1.035)
  waiting for transfers between devices: 66 us -> 69.2 us
  Pallas kernels: 0 us -> 2.3 us
    slice x2 -> x0, local copies, waits for them, and re-layouts: 3.45 us -> none  [the longest x1 2.29 us: line(): mid = [send(own[:, :half], ACROSS)]]
    ppermute x13, waiting for transfers between devices: 66 us -> 69.2 us  [send(): return lax.ppermute(block, 'tensor', pairs)]
    unnamed x4 -> x8, local copies, waits for them, and re-layouts: 0.01 us -> 2.74 us
    pallas_call x0 -> x1, Pallas kernels: none -> 2.3 us  [resident(): pl.pallas_call(kernel, out_shape=[pltpu.VMEM((rows, cut.size), block.dtyp...]
  transfers between devices with their start and end apart: 13 -> 13, of which waited for: 7 -> 7; matrix products, arithmetic and copies ran while one was open for 34% -> 30% of each run, Pallas kernels for 0% -> 0%
where the time goes in v18:
time: 149 us; the launch traced here: 148 us
  waiting for transfers between devices  69.2 us (46%)
  matrix products  44.1 us (30%)
  starting transfers between devices  22 us (15%)
  local copies, waits for them, and re-layouts  6.75 us (5%)
  between operations  4.01 us (3%)
  Pallas kernels  2.3 us (2%)
    ppermute x13, waiting for transfers between devices, send(): return lax.ppermute(block, 'tensor', pairs)  69.2 us
    dot_general x7, matrix products, product(): return jnp.dot(block, part, preferred_element_type=F32)  39.7 us
    ppermute x13, starting transfers between devices, send(): return lax.ppermute(block, 'tensor', pairs)  22 us
    dot_general x2, matrix products, shrink(): jnp.dot(inputs[c], shrink_table[adapter_ids[c]], preferred_element_type=F32)  3.52 us
  transfers between devices with their start and end apart: 13, of which 7 were waited for; matrix products, arithmetic and copies ran while one was open for 30% of the time, Pallas kernels for 0%

profile of v18, /device:TPU:0, one launch (start us, length us, event | category | flops | bytes accessed | tf_op | source)
XLA Modules:
  0.0 148.5 jit_solution(11410669444412198602)
XLA Ops:
  0.0 1.7 %copy-done.1 = bf16[2,256,2048]{2,1,0:T(8,128)(2,1)S(1)} copy-done((bf16[2,256,2048]{2,1,0:T(8,128)(2,1)S(1)}, bf16[2,256,2048]{2,1,0:T(8,128)(2,1)}, u32[]{:S(2)}) %copy-start.1) | copy-done | bytes 2097176
  1.7 2.3 %shard_map.55 = (bf16[512,2048]{1,0:T(8,128)(2,1)}, bf16[512,1024]{1,0:T(8,128)(2,1)}, bf16[512,1024]{1,0:T(8,128)(2,1)S(1)}) custom-call(bf16[512,2048]{1,0:T(8,128)(2,1)S(1)} %bitcast.39), custom_call_target="tpu_custom_call" | custom-call | bytes 8388608 | tf_op jit(solution)/shard_map/pallas_call | solution.py:92
  5.0 3.0 %collective-permute-start = (bf16[512,2048]{1,0:T(8,128)(2,1)}, bf16[512,2048]{1,0:T(8,128)(2,1)}, u32[]{:S(2)}, u32[]{:S(2)}) collective-permute-start(bf16[512,2048]{1,0:T(8,128)(2,1)} %get-tuple-element.20), channel_id=1, source_target_pairs={{0,4},{12,8},{4,0},{8,12},{1,5},{13,9},{5,1},{9,13},{2,6},{14,10},... | collective-permute-start | bytes 6291464 | tf_op jit(solution)/shard_map/ppermute | solution.py:71
  8.1 1.6 %collective-permute-start.2 = (bf16[512,1024]{1,0:T(8,128)(2,1)}, bf16[512,1024]{1,0:T(8,128)(2,1)}, u32[]{:S(2)}, u32[]{:S(2)}) collective-permute-start(bf16[512,1024]{1,0:T(8,128)(2,1)} %get-tuple-element.21), channel_id=1, source_target_pairs={{4,8},{8,4},{5,9},{9,5},{6,10},{10,6},{7,11},{11,7},{20,24},{24,20... | collective-permute-start | bytes 3145736 | tf_op jit(solution)/shard_map/ppermute | solution.py:71
  9.7 1.3 fusion.71
  14.8 1.8 %fusion.28 = bf16[256,64]{0,1:T(8,128)(2,1)S(1)} fusion(bf16[2,256,2048]{2,1,0:T(8,128)(2,1)} %param.5, bf16[4,2048,64]{1,2,0:T(8,128)(2,1)} %param.7, s32[]{:T(128)S(6)} %select_n.80), kind=kOutput, calls=%fused_computation.22 | convolution fusion | flops 67125248 | bytes 1343492 | tf_op jit(solution)/shard_map/dot_general | solution.py:14
  16.5 1.8 %fusion.27 = bf16[256,64]{0,1:T(8,128)(2,1)S(1)} fusion(bf16[2,256,2048]{2,1,0:T(8,128)(2,1)} %param.5, bf16[4,2048,64]{1,2,0:T(8,128)(2,1)} %param.7, s32[]{:T(128)S(6)} %select_n.79), kind=kOutput, calls=%fused_computation.21 | convolution fusion | flops 67125248 | bytes 1343492 | tf_op jit(solution)/shard_map/dot_general | solution.py:14
  18.3 1.7 %collective-permute-start.4 = (bf16[512,1024]{1,0:T(8,128)(2,1)}, bf16[512,1024]{1,0:T(8,128)(2,1)}, u32[]{:S(2)}, u32[]{:S(2)}) collective-permute-start(bf16[512,1024]{1,0:T(8,128)(2,1)} %copy-done.3), channel_id=1, source_target_pairs={{4,8},{8,4},{5,9},{9,5},{6,10},{10,6},{7,11},{11,7},{20,24},{24,20... | collective-permute-start | bytes 3145736 | tf_op jit(solution)/shard_map/ppermute | solution.py:71
  20.0 5.6 %collective-permute-start.1 = (bf16[512,64]{0,1:T(8,128)(2,1)S(1)}, bf16[512,64]{0,1:T(8,128)(2,1)S(1)}, u32[]{:S(2)}, u32[]{:S(2)}) collective-permute-start(bf16[512,64]{0,1:T(8,128)(2,1)S(1)} %get-tuple-element.36), channel_id=1, source_target_pairs={{0,4},{12,8},{1,5},{13,9},{2,6},{14,10},{3,7},{15,11},{16,20},{28,... | collective-permute-start | bytes 196616 | tf_op jit(solution)/shard_map/ppermute | solution.py:71
  25.6 9.4 %fusion.11 = f32[512,2048]{1,0:T(8,128)} fusion(bf16[512,2048]{1,0:T(8,128)(2,1)S(1)} %bitcast.40, bf16[8192,2048]{1,0:T(8,128)(2,1)} %param.6, s32[]{:T(128)S(6)} %select_n.78), kind=kOutput, calls=%fused_computation.13 | convolution fusion | flops 4294967296 | bytes 14680068 | tf_op jit(solution)/shard_map/dot_general | solution.py:115
  36.3 18.3 %collective-permute-done.1 = bf16[512,64]{0,1:T(8,128)(2,1)S(1)} collective-permute-done((bf16[512,64]{0,1:T(8,128)(2,1)S(1)}, bf16[512,64]{0,1:T(8,128)(2,1)S(1)}, u32[]{:S(2)}, u32[]{:S(2)}) %collective-permute-start.1) | collective-permute-done | bytes 65568 | tf_op jit(solution)/shard_map/ppermute | solution.py:71
  54.8 1.3 slice.46
  58.9 9.7 %fusion.16 = f32[512,2048]{1,0:T(8,128)S(1)} fusion(f32[512,2048]{1,0:T(8,128)} %fusion.11, bf16[512,2048]{1,0:T(8,128)(2,1)} %collective-permute-done, bf16[8192,2048]{1,0:T(8,128)(2,1)} %param.6, s32[]{:T(128)S(6)} %select_n.81), kind=kOutput, calls=%fused_computation.16 | convolution fusion | flops 4296015872 | bytes 18874372 | tf_op jit(solution)/shard_map/dot_general | solution.py:115
  68.6 1.3 slice.49
  70.6 6.6 %collective-permute-done.3 = bf16[512,1024]{1,0:T(8,128)(2,1)S(1)} collective-permute-done((bf16[512,1024]{1,0:T(8,128)(2,1)}, bf16[512,1024]{1,0:T(8,128)(2,1)S(1)}, u32[]{:S(2)}, u32[]{:S(2)}) %collective-permute-start.3) | collective-permute-done | bytes 1048608 | tf_op jit(solution)/shard_map/ppermute | solution.py:71
  77.2 4.5 %fusion.22 = f32[512,2048]{1,0:T(8,128)S(1)} fusion(f32[512,2048]{1,0:T(8,128)S(1)} %fusion.16, bf16[8192,2048]{1,0:T(8,128)(2,1)} %param.6, s32[]{:T(128)S(6)} %select_n.85, bf16[512,1024]{1,0:T(8,128)(2,1)S(1)} %collective-permute-done.3, bf16[512,1024]{1,0:T(8,128)(2,1)} %collective-permute-done.2, pred[]{:T(512)S(6)} %or.3), kind=kOutput, calls=%fused_computation.18 | convolution fusion | flops 2149056512 | bytes 14680069 | tf_op jit(solution)/shard_map/dot_general | solution.py:115
  84.4 15.3 %collective-permute-done.5 = bf16[512,1024]{1,0:T(8,128)(2,1)S(1)} collective-permute-done((bf16[512,1024]{1,0:T(8,128)(2,1)}, bf16[512,1024]{1,0:T(8,128)(2,1)S(1)}, u32[]{:S(2)}, u32[]{:S(2)}) %collective-permute-start.5) | collective-permute-done | bytes 1048608 | tf_op jit(solution)/shard_map/ppermute | solution.py:71
  99.7 4.5 %fusion.7 = f32[512,2048]{1,0:T(8,128)S(1)} fusion(bf16[8192,2048]{1,0:T(8,128)(2,1)} %param.6, s32[]{:T(128)S(6)} %select_n.87, bf16[512,1024]{1,0:T(8,128)(2,1)S(1)} %collective-permute-done.5, bf16[512,1024]{1,0:T(8,128)(2,1)} %collective-permute-done.4, pred[]{:T(512)S(6)} %or.3), kind=kOutput, calls=%fused_computation.9 | convolution fusion | flops 2148007936 | bytes 10485765 | tf_op jit(solution)/shard_map/dot_general | solution.py:115
  105.7 1.5 collective-permute-start.12
  108.1 15.5 %collective-permute-done.10 = bf16[512,1024]{1,0:T(8,128)(2,1)S(1)} collective-permute-done((bf16[512,1024]{1,0:T(8,128)(2,1)S(1)}, bf16[512,1024]{1,0:T(8,128)(2,1)S(1)}, u32[]{:S(2)}, u32[]{:S(2)}) %collective-permute-start.10) | collective-permute-done | bytes 1048608 | tf_op jit(solution)/shard_map/ppermute | solution.py:71
  123.6 4.6 %fusion.4 = f32[512,2048]{1,0:T(8,128)S(1)} fusion(f32[256,2048]{1,0:T(8,128)S(1)} %fusion.42, f32[256,2048]{1,0:T(8,128)S(1)} %fusion.44, f32[512,2048]{1,0:T(8,128)S(1)} %fusion.22, f32[512,2048]{1,0:T(8,128)S(1)} %fusion.7, bf16[8192,2048]{1,0:T(8,128)(2,1)} %param.6, s32[]{:T(128)S(6)} %select_n.92, bf16[512,1024]{1,0:T(8,128)(2,1)S(1)} %collective-permute-done.10, ...), kind=kOutput, calls=%fused_computation.5 | convolution fusion | flops 2152202240 | bytes 23068676 | tf_op jit(solution)/shard_map/dot_general | solution.py:115
  128.2 12.2 %collective-permute-done.11 = bf16[512,768]{1,0:T(8,128)(2,1)S(1)} collective-permute-done((bf16[512,768]{1,0:T(8,128)(2,1)S(1)}, bf16[512,768]{1,0:T(8,128)(2,1)S(1)}, u32[]{:S(2)}, u32[]{:S(2)}) %collective-permute-start.11) | collective-permute-done | bytes 786464 | tf_op jit(solution)/shard_map/ppermute | solution.py:71
  140.4 3.7 %fusion.19 = f32[512,2048]{1,0:T(8,128)S(1)} fusion(f32[512,2048]{1,0:T(8,128)S(1)} %fusion.4, bf16[8192,2048]{1,0:T(8,128)(2,1)} %param.6, s32[]{:T(128)S(6)} %select_n.95, bf16[512,768]{1,0:T(8,128)(2,1)S(1)} %collective-permute-done.11, pred[]{:T(512)S(6)} %or.3, bf16[512,1024]{1,0:T(8,128)(2,1)S(1)} %collective-permute-done.9), kind=kOutput, calls=%fused_computation.17 | convolution fusion | flops 1612054528 | bytes 13107205 | tf_op jit(solution)/shard_map/dot_general | solution.py:115
  145.2 3.3 %add_convert_fusion = bf16[512,2048]{1,0:T(8,128)(2,1)} fusion(f32[512,2048]{1,0:T(8,128)S(1)} %fusion.19, bf16[8192,2048]{1,0:T(8,128)(2,1)} %param.6, s32[]{:T(128)S(6)} %select_n.98, bf16[512,256]{1,0:T(8,128)(2,1)S(1)} %collective-permute-done.12, pred[]{:T(512)S(6)} %or.3, bf16[512,1024]{1,0:T(8,128)(2,1)S(1)} %collective-permute-done.9), kind=kOutput, calls=%fused_computation.6 | convolution fusion | flops 539099136 | bytes 7864325 | tf_op jit(solution)/shard_map/dot_general | solution.py:115
  (31 shorter events, 12.1 us)
Async XLA Ops:
  0.0 107.2 %copy-start = (bf16[4,64,2048]{2,1,0:T(8,128)(2,1)S(1)}, bf16[4,64,2048]{2,1,0:T(8,128)(2,1)}, u32[]{:S(2)}) copy-start(bf16[4,64,2048]{2,1,0:T(8,128)(2,1)} %param.8) | copy-start | bytes 3145732
  0.0 1.7 %copy-start.1 = (bf16[2,256,2048]{2,1,0:T(8,128)(2,1)S(1)}, bf16[2,256,2048]{2,1,0:T(8,128)(2,1)}, u32[]{:S(2)}) copy-start(bf16[2,256,2048]{2,1,0:T(8,128)(2,1)} %param.5) | copy-start | bytes 6291460
  1.7 23.9 %copy-start.2 = (bf16[2,256,2048]{2,1,0:T(8,128)(2,1)S(1)}, bf16[2,256,2048]{2,1,0:T(8,128)(2,1)}, u32[]{:S(2)}) copy-start(bf16[2,256,2048]{2,1,0:T(8,128)(2,1)} %param.5) | copy-start | bytes 6291460
  4.0 1.1 copy-start.3
  5.0 49.8 %collective-permute-start = (bf16[512,2048]{1,0:T(8,128)(2,1)}, bf16[512,2048]{1,0:T(8,128)(2,1)}, u32[]{:S(2)}, u32[]{:S(2)}) collective-permute-start(bf16[512,2048]{1,0:T(8,128)(2,1)} %get-tuple-element.20), channel_id=1, source_target_pairs={{0,4},{12,8},{4,0},{8,12},{1,5},{13,9},{5,1},{9,13},{2,6},{14,10},... | collective-permute-start | bytes 6291464 | tf_op jit(solution)/shard_map/ppermute | solution.py:71
  8.1 26.9 %collective-permute-start.2 = (bf16[512,1024]{1,0:T(8,128)(2,1)}, bf16[512,1024]{1,0:T(8,128)(2,1)}, u32[]{:S(2)}, u32[]{:S(2)}) collective-permute-start(bf16[512,1024]{1,0:T(8,128)(2,1)} %get-tuple-element.21), channel_id=1, source_target_pairs={{4,8},{8,4},{5,9},{9,5},{6,10},{10,6},{7,11},{11,7},{20,24},{24,20... | collective-permute-start | bytes 3145736 | tf_op jit(solution)/shard_map/ppermute | solution.py:71
  18.3 39.2 %collective-permute-start.4 = (bf16[512,1024]{1,0:T(8,128)(2,1)}, bf16[512,1024]{1,0:T(8,128)(2,1)}, u32[]{:S(2)}, u32[]{:S(2)}) collective-permute-start(bf16[512,1024]{1,0:T(8,128)(2,1)} %copy-done.3), channel_id=1, source_target_pairs={{4,8},{8,4},{5,9},{9,5},{6,10},{10,6},{7,11},{11,7},{20,24},{24,20... | collective-permute-start | bytes 3145736 | tf_op jit(solution)/shard_map/ppermute | solution.py:71
  20.0 34.6 %collective-permute-start.1 = (bf16[512,64]{0,1:T(8,128)(2,1)S(1)}, bf16[512,64]{0,1:T(8,128)(2,1)S(1)}, u32[]{:S(2)}, u32[]{:S(2)}) collective-permute-start(bf16[512,64]{0,1:T(8,128)(2,1)S(1)} %get-tuple-element.36), channel_id=1, source_target_pairs={{0,4},{12,8},{1,5},{13,9},{2,6},{14,10},{3,7},{15,11},{16,20},{28,... | collective-permute-start | bytes 196616 | tf_op jit(solution)/shard_map/ppermute | solution.py:71
  35.0 42.2 %collective-permute-start.3 = (bf16[512,1024]{1,0:T(8,128)(2,1)}, bf16[512,1024]{1,0:T(8,128)(2,1)S(1)}, u32[]{:S(2)}, u32[]{:S(2)}) collective-permute-start(bf16[512,1024]{1,0:T(8,128)(2,1)} %collective-permute-done.2), channel_id=1, source_target_pairs={{4,0},{8,12},{5,1},{9,13},{6,2},{10,14},{7,3},{11,15},{20,16},{24,... | collective-permute-start | bytes 3145736 | tf_op jit(solution)/shard_map/ppermute | solution.py:71
  56.1 12.4 %collective-permute-start.6 = (bf16[512,1024]{1,0:T(8,128)(2,1)S(1)}, bf16[512,1024]{1,0:T(8,128)(2,1)S(1)}, u32[]{:S(2)}, u32[]{:S(2)}) collective-permute-start(bf16[512,1024]{1,0:T(8,128)(2,1)S(1)} %slice.46), channel_id=1, source_target_pairs={{4,8},{8,4},{5,9},{9,5},{6,10},{10,6},{7,11},{11,7},{20,24},{24,20... | collective-permute-start | bytes 3145736 | tf_op jit(solution)/shard_map/ppermute | solution.py:71
  56.9 24.9 %collective-permute-start.7 = (bf16[2,512,64]{1,2,0:T(8,128)(2,1)S(1)}, bf16[2,512,64]{1,2,0:T(8,128)(2,1)S(1)}, u32[]{:S(2)}, u32[]{:S(2)}) collective-permute-start(bf16[2,512,64]{1,2,0:T(8,128)(2,1)S(1)} %pad_maximum_fusion), channel_id=1, source_target_pairs={{4,8},{8,4},{5,9},{9,5},{6,10},{10,6},{7,11},{11,7},{20,24},{24,20... | collective-permute-start | bytes 393224 | tf_op jit(solution)/shard_map/ppermute | solution.py:71
  57.6 42.1 %collective-permute-start.5 = (bf16[512,1024]{1,0:T(8,128)(2,1)}, bf16[512,1024]{1,0:T(8,128)(2,1)S(1)}, u32[]{:S(2)}, u32[]{:S(2)}) collective-permute-start(bf16[512,1024]{1,0:T(8,128)(2,1)} %collective-permute-done.4), channel_id=1, source_target_pairs={{4,0},{8,12},{5,1},{9,13},{6,2},{10,14},{7,3},{11,15},{20,16},{24,... | collective-permute-start | bytes 3145736 | tf_op jit(solution)/shard_map/ppermute | solution.py:71
  69.9 34.4 %collective-permute-start.9 = (bf16[512,1024]{1,0:T(8,128)(2,1)S(1)}, bf16[512,1024]{1,0:T(8,128)(2,1)S(1)}, u32[]{:S(2)}, u32[]{:S(2)}) collective-permute-start(bf16[512,1024]{1,0:T(8,128)(2,1)S(1)} %slice.49), channel_id=1, source_target_pairs={{4,8},{8,4},{5,9},{9,5},{6,10},{10,6},{7,11},{11,7},{20,24},{24,20... | collective-permute-start | bytes 3145736 | tf_op jit(solution)/shard_map/ppermute | solution.py:71
  81.8 22.4 %collective-permute-start.8 = (bf16[512,64]{0,1:T(8,128)(2,1)S(1)}, bf16[512,64]{0,1:T(8,128)(2,1)S(1)}, u32[]{:S(2)}, u32[]{:S(2)}) collective-permute-start(bf16[512,64]{0,1:T(8,128)(2,1)S(1)} %fusion.54), channel_id=1, source_target_pairs={{4,0},{8,12},{5,1},{9,13},{6,2},{10,14},{7,3},{11,15},{20,16},{24,... | collective-permute-start | bytes 196616 | tf_op jit(solution)/shard_map/ppermute | solution.py:71
  83.1 40.4 %collective-permute-start.10 = (bf16[512,1024]{1,0:T(8,128)(2,1)S(1)}, bf16[512,1024]{1,0:T(8,128)(2,1)S(1)}, u32[]{:S(2)}, u32[]{:S(2)}) collective-permute-start(bf16[512,1024]{1,0:T(8,128)(2,1)S(1)} %collective-permute-done.6), channel_id=1, source_target_pairs={{4,0},{8,12},{5,1},{9,13},{6,2},{10,14},{7,3},{11,15},{20,16},{24,... | collective-permute-start | bytes 3145736 | tf_op jit(solution)/shard_map/ppermute | solution.py:71
  104.4 36.0 %collective-permute-start.11 = (bf16[512,768]{1,0:T(8,128)(2,1)S(1)}, bf16[512,768]{1,0:T(8,128)(2,1)S(1)}, u32[]{:S(2)}, u32[]{:S(2)}) collective-permute-start(bf16[512,768]{1,0:T(8,128)(2,1)S(1)} %slice.52), channel_id=1, source_target_pairs={{4,0},{8,12},{5,1},{9,13},{6,2},{10,14},{7,3},{11,15},{20,16},{24,... | collective-permute-start | bytes 2359304 | tf_op jit(solution)/shard_map/ppermute | solution.py:71
  105.7 39.5 %collective-permute-start.12 = (bf16[512,256]{1,0:T(8,128)(2,1)S(1)}, bf16[512,256]{1,0:T(8,128)(2,1)S(1)}, u32[]{:S(2)}, u32[]{:S(2)}) collective-permute-start(bf16[512,256]{1,0:T(8,128)(2,1)S(1)} %slice.53), channel_id=1, source_target_pairs={{4,0},{8,12},{5,1},{9,13},{6,2},{10,14},{7,3},{11,15},{20,16},{24,... | collective-permute-start | bytes 786440 | tf_op jit(solution)/shard_map/ppermute | solution.py:71

commit v19 on v15

--- a/solution.py
+++ b/solution.py
@@ -62,6 +62,7 @@
 INWARD = [(0, 1), (3, 2)]
 OUTWARD = [(1, 0), (2, 3)]
 ACROSS = [(1, 2), (2, 1)]
+FAR = [(0, 2), (3, 1)]
 SWAP = INWARD + OUTWARD
 
 
@@ -88,17 +89,18 @@
         return jnp.dot(block, part, preferred_element_type=F32)
 
     mate = send(own, SWAP)
-    mid = [send(own[:, :half], ACROSS)]
+    left = own[:, :half]
+    mid = [send(left, ACROSS)]
     partial = shrink(inputs, shrink_table, adapter_ids)
-    mid.append(send(after(own, partial)[:, half:], ACROSS))
+    left, right = after(left, partial), after(own, partial)[:, half:]
+    mid.append(send(right, ACROSS))
+    end = [send(left, FAR), send(right, FAR)]
     mate_partial = send(partial, INWARD)
     total = product(own, here)
 
     mid_out = [send(after(mid[0], total), OUTWARD)]
     mate, mate_partial = lax.optimization_barrier((mate, mate_partial, mid[1], total))[:2]
     both = send(jnp.stack([partial, mate_partial]), ACROSS)
-    end = [send(mate[:, :half], ACROSS)]
-    end.append(send(after(mate, mid_out[0])[:, half:], ACROSS))
     mid_out.append(send(mid[1], OUTWARD))
     total = total + product(mate, here ^ 1)
 

time: 176 us -> 175 us (level)
  matrix products: 42.1 us -> 45.3 us
  waiting for transfers between devices: 95.9 us -> 94 us
    dot_general x7, matrix products: 37.7 us -> 40.8 us  [product(): return jnp.dot(block, part, preferred_element_type=F32)]
    ppermute x13, waiting for transfers between devices: 95.9 us -> 94 us  [send(): return lax.ppermute(block, 'tensor', pairs)]
    slice x4 -> x2, local copies, waits for them, and re-layouts: 6.03 us -> 4.61 us  [the longest x1 2.31 us: line(): left, right = (after(left, partial), after(own, partial)[:, half:])]
  transfers between devices with their start and end apart: 13 -> 13, of which waited for: 6 -> 6; matrix products, arithmetic and copies ran while one was open for 27% -> 28% of each run, Pallas kernels for 0% -> 0%
where the time goes in v19:
time: 175 us; the launch traced here: 174 us
  waiting for transfers between devices  94 us (54%)
  matrix products  45.3 us (26%)
  starting transfers between devices  24.6 us (14%)
  local copies, waits for them, and re-layouts  6.05 us (3%)
  between operations  4 us (2%)
    ppermute x13, waiting for transfers between devices, send(): return lax.ppermute(block, 'tensor', pairs)  94 us
    dot_general x7, matrix products, product(): return jnp.dot(block, part, preferred_element_type=F32)  40.8 us
    ppermute x13, starting transfers between devices, send(): return lax.ppermute(block, 'tensor', pairs)  24.6 us
    dot_general x2, matrix products, shrink(): jnp.dot(inputs[c], shrink_table[adapter_ids[c]], preferred_element_type=F32)  3.52 us
  transfers between devices with their start and end apart: 13, of which 6 were waited for; matrix products, arithmetic and copies ran while one was open for 28% of the time, Pallas kernels for 0%

profile of v19, /device:TPU:0, one launch (start us, length us, event | category | flops | bytes accessed | tf_op | source)
XLA Modules:
  0.0 174.0 jit_solution(6832117428724051567)
XLA Ops:
  0.0 3.0 %collective-permute-start = (bf16[512,2048]{1,0:T(8,128)(2,1)}, bf16[512,2048]{1,0:T(8,128)(2,1)}, u32[]{:S(2)}, u32[]{:S(2)}) collective-permute-start(bf16[512,2048]{1,0:T(8,128)(2,1)} %bitcast.39), channel_id=1, source_target_pairs={{0,4},{12,8},{4,0},{8,12},{1,5},{13,9},{5,1},{9,13},{2,6},{14,10},... | collective-permute-start | bytes 6291464 | tf_op jit(solution)/shard_map/ppermute | solution.py:70
  3.0 2.3 %slice.54 = bf16[512,1024]{1,0:T(8,128)(2,1)} slice(bf16[512,2048]{1,0:T(8,128)(2,1)} %bitcast.40), slice={[0:512], [0:1024]} | slice | bytes 2097152 | tf_op jit(solution)/shard_map/slice | solution.py:92
  5.3 1.7 collective-permute-start.3
  7.0 1.3 fusion.71
  12.1 1.8 %fusion.27 = bf16[256,64]{0,1:T(8,128)(2,1)S(1)} fusion(bf16[2,256,2048]{2,1,0:T(8,128)(2,1)} %param.5, bf16[4,2048,64]{1,2,0:T(8,128)(2,1)} %param.7, s32[]{:T(128)S(6)} %select_n.77), kind=kOutput, calls=%fused_computation.21 | convolution fusion | flops 67125248 | bytes 1343492 | tf_op jit(solution)/shard_map/dot_general | solution.py:12
  13.9 1.8 %fusion.28 = bf16[256,64]{0,1:T(8,128)(2,1)S(1)} fusion(bf16[2,256,2048]{2,1,0:T(8,128)(2,1)} %param.5, bf16[4,2048,64]{1,2,0:T(8,128)(2,1)} %param.7, s32[]{:T(128)S(6)} %select_n.78), kind=kOutput, calls=%fused_computation.22 | convolution fusion | flops 67125248 | bytes 1343492 | tf_op jit(solution)/shard_map/dot_general | solution.py:12
  15.6 2.3 %slice.46 = bf16[512,1024]{1,0:T(8,128)(2,1)} slice(bf16[512,2048]{1,0:T(8,128)(2,1)} %bitcast.41), slice={[0:512], [1024:2048]} | slice | bytes 2097152 | tf_op jit(solution)/shard_map/slice | solution.py:95
  18.7 6.5 %collective-permute-start.1 = (bf16[512,64]{0,1:T(8,128)(2,1)S(1)}, bf16[512,64]{0,1:T(8,128)(2,1)S(1)}, u32[]{:S(2)}, u32[]{:S(2)}) collective-permute-start(bf16[512,64]{0,1:T(8,128)(2,1)S(1)} %get-tuple-element.28), channel_id=1, source_target_pairs={{0,4},{12,8},{1,5},{13,9},{2,6},{14,10},{3,7},{15,11},{16,20},{28,... | collective-permute-start | bytes 196616 | tf_op jit(solution)/shard_map/ppermute | solution.py:70
  25.2 2.8 %collective-permute-start.9 = (bf16[512,1024]{1,0:T(8,128)(2,1)}, bf16[512,1024]{1,0:T(8,128)(2,1)S(1)}, u32[]{:S(2)}, u32[]{:S(2)}) collective-permute-start(bf16[512,1024]{1,0:T(8,128)(2,1)} %slice.46), channel_id=1, source_target_pairs={{0,8},{12,4},{1,9},{13,5},{2,10},{14,6},{3,11},{15,7},{16,24},{28,... | collective-permute-start | bytes 3145736 | tf_op jit(solution)/shard_map/ppermute | solution.py:70
  28.0 10.5 %fusion.11 = f32[512,2048]{1,0:T(8,128)} fusion(bf16[512,2048]{1,0:T(8,128)(2,1)} %bitcast.42, bf16[8192,2048]{1,0:T(8,128)(2,1)} %param.6, s32[]{:T(128)S(6)} %select_n.76), kind=kOutput, calls=%fused_computation.13 | convolution fusion | flops 4294967296 | bytes 14680068 | tf_op jit(solution)/shard_map/dot_general | solution.py:89
  38.5 1.3 collective-permute-start.6
  39.8 10.9 %collective-permute-done.1 = bf16[512,64]{0,1:T(8,128)(2,1)S(1)} collective-permute-done((bf16[512,64]{0,1:T(8,128)(2,1)S(1)}, bf16[512,64]{0,1:T(8,128)(2,1)S(1)}, u32[]{:S(2)}, u32[]{:S(2)}) %collective-permute-start.1) | collective-permute-done | bytes 65568 | tf_op jit(solution)/shard_map/ppermute | solution.py:70
  52.0 1.3 collective-permute-start.5
  54.0 9.7 %fusion.16 = f32[512,2048]{1,0:T(8,128)S(1)} fusion(f32[512,2048]{1,0:T(8,128)} %fusion.11, bf16[512,2048]{1,0:T(8,128)(2,1)} %collective-permute-done, bf16[8192,2048]{1,0:T(8,128)(2,1)} %param.6, s32[]{:T(128)S(6)} %select_n.79), kind=kOutput, calls=%fused_computation.16 | convolution fusion | flops 4296015872 | bytes 18874372 | tf_op jit(solution)/shard_map/dot_general | solution.py:89
  63.7 31.0 %collective-permute-done.6 = bf16[512,1024]{1,0:T(8,128)(2,1)S(1)} collective-permute-done((bf16[512,1024]{1,0:T(8,128)(2,1)}, bf16[512,1024]{1,0:T(8,128)(2,1)S(1)}, u32[]{:S(2)}, u32[]{:S(2)}) %collective-permute-start.6) | collective-permute-done | bytes 1048608 | tf_op jit(solution)/shard_map/ppermute | solution.py:70
  97.3 4.6 %fusion.22 = f32[512,2048]{1,0:T(8,128)S(1)} fusion(f32[512,2048]{1,0:T(8,128)S(1)} %fusion.16, bf16[8192,2048]{1,0:T(8,128)(2,1)} %param.6, s32[]{:T(128)S(6)} %select_n.83, bf16[512,1024]{1,0:T(8,128)(2,1)S(1)} %collective-permute-done.4, bf16[512,1024]{1,0:T(8,128)(2,1)} %collective-permute-done.3, pred[]{:T(512)S(6)} %or.3), kind=kOutput, calls=%fused_computation.18 | convolution fusion | flops 2149056512 | bytes 14680069 | tf_op jit(solution)/shard_map/dot_general | solution.py:89
  103.3 1.5 collective-permute-start.12
  104.8 22.9 %collective-permute-done.8 = bf16[512,64]{0,1:T(8,128)(2,1)S(1)} collective-permute-done((bf16[512,64]{0,1:T(8,128)(2,1)S(1)}, bf16[512,64]{0,1:T(8,128)(2,1)S(1)}, u32[]{:S(2)}, u32[]{:S(2)}) %collective-permute-start.8) | collective-permute-done | bytes 65568 | tf_op jit(solution)/shard_map/ppermute | solution.py:70
  128.5 21.5 %collective-permute-done.10 = bf16[512,1024]{1,0:T(8,128)(2,1)S(1)} collective-permute-done((bf16[512,1024]{1,0:T(8,128)(2,1)S(1)}, bf16[512,1024]{1,0:T(8,128)(2,1)S(1)}, u32[]{:S(2)}, u32[]{:S(2)}) %collective-permute-start.10) | collective-permute-done | bytes 1048608 | tf_op jit(solution)/shard_map/ppermute | solution.py:70
  150.1 4.5 %fusion.5 = f32[512,2048]{1,0:T(8,128)S(1)} fusion(bf16[8192,2048]{1,0:T(8,128)(2,1)} %param.6, s32[]{:T(128)S(6)} %select_n.90, bf16[512,1024]{1,0:T(8,128)(2,1)S(1)} %collective-permute-done.10, bf16[512,1024]{1,0:T(8,128)(2,1)S(1)} %collective-permute-done.6, pred[]{:T(512)S(6)} %or.3), kind=kOutput, calls=%fused_computation.7 | convolution fusion | flops 2148007936 | bytes 10485765 | tf_op jit(solution)/shard_map/dot_general | solution.py:89
  154.6 4.7 %fusion.4 = f32[512,2048]{1,0:T(8,128)S(1)} fusion(f32[512,2048]{1,0:T(8,128)S(1)} %fusion.5, f32[256,2048]{1,0:T(8,128)S(1)} %fusion.42, f32[256,2048]{1,0:T(8,128)S(1)} %fusion.44, f32[512,2048]{1,0:T(8,128)S(1)} %fusion.22, bf16[8192,2048]{1,0:T(8,128)(2,1)} %param.6, s32[]{:T(128)S(6)} %select_n.85, bf16[512,1024]{1,0:T(8,128)(2,1)S(1)} %collective-permute-done.5, ...), kind=kOutput, calls=%fused_computation.5 | convolution fusion | flops 2152202240 | bytes 23068676 | tf_op jit(solution)/shard_map/dot_general | solution.py:89
  159.3 7.6 %collective-permute-done.11 = bf16[512,768]{1,0:T(8,128)(2,1)S(1)} collective-permute-done((bf16[512,768]{1,0:T(8,128)(2,1)S(1)}, bf16[512,768]{1,0:T(8,128)(2,1)S(1)}, u32[]{:S(2)}, u32[]{:S(2)}) %collective-permute-start.11) | collective-permute-done | bytes 786464 | tf_op jit(solution)/shard_map/ppermute | solution.py:70
  166.9 3.7 %fusion.19 = f32[512,2048]{1,0:T(8,128)S(1)} fusion(f32[512,2048]{1,0:T(8,128)S(1)} %fusion.4, bf16[8192,2048]{1,0:T(8,128)(2,1)} %param.6, s32[]{:T(128)S(6)} %select_n.93, bf16[512,768]{1,0:T(8,128)(2,1)S(1)} %collective-permute-done.11, pred[]{:T(512)S(6)} %or.3, bf16[512,1024]{1,0:T(8,128)(2,1)S(1)} %collective-permute-done.9), kind=kOutput, calls=%fused_computation.17 | convolution fusion | flops 1612054528 | bytes 13107205 | tf_op jit(solution)/shard_map/dot_general | solution.py:89
  170.8 3.3 %add_convert_fusion = bf16[512,2048]{1,0:T(8,128)(2,1)} fusion(f32[512,2048]{1,0:T(8,128)S(1)} %fusion.19, bf16[8192,2048]{1,0:T(8,128)(2,1)} %param.6, s32[]{:T(128)S(6)} %select_n.96, bf16[512,256]{1,0:T(8,128)(2,1)S(1)} %collective-permute-done.12, pred[]{:T(512)S(6)} %or.3, bf16[512,1024]{1,0:T(8,128)(2,1)S(1)} %collective-permute-done.9), kind=kOutput, calls=%fused_computation.6 | convolution fusion | flops 539099136 | bytes 7864325 | tf_op jit(solution)/shard_map/dot_general | solution.py:89
  (24 shorter events, 7.8 us)
Async XLA Ops:
  0.0 127.6 %copy-start = (bf16[4,64,2048]{2,1,0:T(8,128)(2,1)S(1)}, bf16[4,64,2048]{2,1,0:T(8,128)(2,1)}, u32[]{:S(2)}) copy-start(bf16[4,64,2048]{2,1,0:T(8,128)(2,1)} %param.8) | copy-start | bytes 3145732
  0.0 53.3 %collective-permute-start = (bf16[512,2048]{1,0:T(8,128)(2,1)}, bf16[512,2048]{1,0:T(8,128)(2,1)}, u32[]{:S(2)}, u32[]{:S(2)}) collective-permute-start(bf16[512,2048]{1,0:T(8,128)(2,1)} %bitcast.39), channel_id=1, source_target_pairs={{0,4},{12,8},{4,0},{8,12},{1,5},{13,9},{5,1},{9,13},{2,6},{14,10},... | collective-permute-start | bytes 6291464 | tf_op jit(solution)/shard_map/ppermute | solution.py:70
  5.3 33.1 %collective-permute-start.3 = (bf16[512,1024]{1,0:T(8,128)(2,1)}, bf16[512,1024]{1,0:T(8,128)(2,1)}, u32[]{:S(2)}, u32[]{:S(2)}) collective-permute-start(bf16[512,1024]{1,0:T(8,128)(2,1)} %slice.54), channel_id=1, source_target_pairs={{4,8},{8,4},{5,9},{9,5},{6,10},{10,6},{7,11},{11,7},{20,24},{24,20... | collective-permute-start | bytes 3145736 | tf_op jit(solution)/shard_map/ppermute | solution.py:70
  17.9 34.0 %collective-permute-start.2 = (bf16[512,1024]{1,0:T(8,128)(2,1)}, bf16[512,1024]{1,0:T(8,128)(2,1)S(1)}, u32[]{:S(2)}, u32[]{:S(2)}) collective-permute-start(bf16[512,1024]{1,0:T(8,128)(2,1)} %slice.46), channel_id=1, source_target_pairs={{4,8},{8,4},{5,9},{9,5},{6,10},{10,6},{7,11},{11,7},{20,24},{24,20... | collective-permute-start | bytes 3145736 | tf_op jit(solution)/shard_map/ppermute | solution.py:70
  18.7 32.0 %collective-permute-start.1 = (bf16[512,64]{0,1:T(8,128)(2,1)S(1)}, bf16[512,64]{0,1:T(8,128)(2,1)S(1)}, u32[]{:S(2)}, u32[]{:S(2)}) collective-permute-start(bf16[512,64]{0,1:T(8,128)(2,1)S(1)} %get-tuple-element.28), channel_id=1, source_target_pairs={{0,4},{12,8},{1,5},{13,9},{2,6},{14,10},{3,7},{15,11},{16,20},{28,... | collective-permute-start | bytes 196616 | tf_op jit(solution)/shard_map/ppermute | solution.py:70
  25.2 76.7 %collective-permute-start.9 = (bf16[512,1024]{1,0:T(8,128)(2,1)}, bf16[512,1024]{1,0:T(8,128)(2,1)S(1)}, u32[]{:S(2)}, u32[]{:S(2)}) collective-permute-start(bf16[512,1024]{1,0:T(8,128)(2,1)} %slice.46), channel_id=1, source_target_pairs={{0,8},{12,4},{1,9},{13,5},{2,10},{14,6},{3,11},{15,7},{16,24},{28,... | collective-permute-start | bytes 3145736 | tf_op jit(solution)/shard_map/ppermute | solution.py:70
  38.5 56.2 %collective-permute-start.6 = (bf16[512,1024]{1,0:T(8,128)(2,1)}, bf16[512,1024]{1,0:T(8,128)(2,1)S(1)}, u32[]{:S(2)}, u32[]{:S(2)}) collective-permute-start(bf16[512,1024]{1,0:T(8,128)(2,1)} %slice.54), channel_id=1, source_target_pairs={{0,8},{12,4},{1,9},{13,5},{2,10},{14,6},{3,11},{15,7},{16,24},{28,... | collective-permute-start | bytes 3145736 | tf_op jit(solution)/shard_map/ppermute | solution.py:70
  50.7 46.6 %collective-permute-start.4 = (bf16[512,1024]{1,0:T(8,128)(2,1)}, bf16[512,1024]{1,0:T(8,128)(2,1)S(1)}, u32[]{:S(2)}, u32[]{:S(2)}) collective-permute-start(bf16[512,1024]{1,0:T(8,128)(2,1)} %collective-permute-done.3), channel_id=1, source_target_pairs={{4,0},{8,12},{5,1},{9,13},{6,2},{10,14},{7,3},{11,15},{20,16},{24,... | collective-permute-start | bytes 3145736 | tf_op jit(solution)/shard_map/ppermute | solution.py:70
  52.0 102.7 %collective-permute-start.5 = (bf16[512,1024]{1,0:T(8,128)(2,1)S(1)}, bf16[512,1024]{1,0:T(8,128)(2,1)S(1)}, u32[]{:S(2)}, u32[]{:S(2)}) collective-permute-start(bf16[512,1024]{1,0:T(8,128)(2,1)S(1)} %collective-permute-done.2), channel_id=1, source_target_pairs={{4,0},{8,12},{5,1},{9,13},{6,2},{10,14},{7,3},{11,15},{20,16},{24,... | collective-permute-start | bytes 3145736 | tf_op jit(solution)/shard_map/ppermute | solution.py:70
  53.3 41.3 %collective-permute-start.7 = (bf16[2,512,64]{1,2,0:T(8,128)(2,1)S(1)}, bf16[2,512,64]{1,2,0:T(8,128)(2,1)S(1)}, u32[]{:S(2)}, u32[]{:S(2)}) collective-permute-start(bf16[2,512,64]{1,2,0:T(8,128)(2,1)S(1)} %pad_maximum_fusion), channel_id=1, source_target_pairs={{4,8},{8,4},{5,9},{9,5},{6,10},{10,6},{7,11},{11,7},{20,24},{24,20... | collective-permute-start | bytes 393224 | tf_op jit(solution)/shard_map/ppermute | solution.py:70
  94.7 32.9 %collective-permute-start.8 = (bf16[512,64]{0,1:T(8,128)(2,1)S(1)}, bf16[512,64]{0,1:T(8,128)(2,1)S(1)}, u32[]{:S(2)}, u32[]{:S(2)}) collective-permute-start(bf16[512,64]{0,1:T(8,128)(2,1)S(1)} %fusion.54), channel_id=1, source_target_pairs={{4,0},{8,12},{5,1},{9,13},{6,2},{10,14},{7,3},{11,15},{20,16},{24,... | collective-permute-start | bytes 196616 | tf_op jit(solution)/shard_map/ppermute | solution.py:70
  96.0 54.1 %collective-permute-start.10 = (bf16[512,1024]{1,0:T(8,128)(2,1)S(1)}, bf16[512,1024]{1,0:T(8,128)(2,1)S(1)}, u32[]{:S(2)}, u32[]{:S(2)}) collective-permute-start(bf16[512,1024]{1,0:T(8,128)(2,1)S(1)} %collective-permute-done.6), channel_id=1, source_target_pairs={{4,0},{8,12},{5,1},{9,13},{6,2},{10,14},{7,3},{11,15},{20,16},{24,... | collective-permute-start | bytes 3145736 | tf_op jit(solution)/shard_map/ppermute | solution.py:70
  102.0 65.0 %collective-permute-start.11 = (bf16[512,768]{1,0:T(8,128)(2,1)S(1)}, bf16[512,768]{1,0:T(8,128)(2,1)S(1)}, u32[]{:S(2)}, u32[]{:S(2)}) collective-permute-start(bf16[512,768]{1,0:T(8,128)(2,1)S(1)} %slice.52), channel_id=1, source_target_pairs={{4,0},{8,12},{5,1},{9,13},{6,2},{10,14},{7,3},{11,15},{20,16},{24,... | collective-permute-start | bytes 2359304 | tf_op jit(solution)/shard_map/ppermute | solution.py:70
  103.3 67.5 %collective-permute-start.12 = (bf16[512,256]{1,0:T(8,128)(2,1)S(1)}, bf16[512,256]{1,0:T(8,128)(2,1)S(1)}, u32[]{:S(2)}, u32[]{:S(2)}) collective-permute-start(bf16[512,256]{1,0:T(8,128)(2,1)S(1)} %slice.53), channel_id=1, source_target_pairs={{4,0},{8,12},{5,1},{9,13},{6,2},{10,14},{7,3},{11,15},{20,16},{24,... | collective-permute-start | bytes 786440 | tf_op jit(solution)/shard_map/ppermute | solution.py:70

commit v20 on v19

--- a/solution.py
+++ b/solution.py
@@ -92,13 +92,13 @@
     left = own[:, :half]
     mid = [send(left, ACROSS)]
     partial = shrink(inputs, shrink_table, adapter_ids)
-    left, right = after(left, partial), after(own, partial)[:, half:]
+    right = after(own, partial)[:, half:]
     mid.append(send(right, ACROSS))
-    end = [send(left, FAR), send(right, FAR)]
     mate_partial = send(partial, INWARD)
     total = product(own, here)
 
     mid_out = [send(after(mid[0], total), OUTWARD)]
+    end = [send(after(left, mid[0], total), FAR), send(after(right, mid[1]), FAR)]
     mate, mate_partial = lax.optimization_barrier((mate, mate_partial, mid[1], total))[:2]
     both = send(jnp.stack([partial, mate_partial]), ACROSS)
     mid_out.append(send(mid[1], OUTWARD))

time: 175 us -> 161 us (0.920)
  waiting for transfers between devices: 94 us -> 60.6 us
  starting transfers between devices: 24.6 us -> 46.6 us
    ppermute x13, waiting for transfers between devices: 94 us -> 60.6 us  [send(): return lax.ppermute(block, 'tensor', pairs)]
    ppermute x13, starting transfers between devices: 24.6 us -> 46.6 us  [send(): return lax.ppermute(block, 'tensor', pairs)]
  transfers between devices with their start and end apart: 13 -> 13, of which waited for: 6 -> 4; matrix products, arithmetic and copies ran while one was open for 28% -> 29% of each run, Pallas kernels for 0% -> 0%
where the time goes in v20:
time: 161 us; the launch traced here: 160 us
  waiting for transfers between devices  60.6 us (38%)
  starting transfers between devices  46.6 us (29%)
  matrix products  44.2 us (27%)
  local copies, waits for them, and re-layouts  4.83 us (3%)
  between operations  3.79 us (2%)
    ppermute x13, waiting for transfers between devices, send(): return lax.ppermute(block, 'tensor', pairs)  60.6 us
    ppermute x13, starting transfers between devices, send(): return lax.ppermute(block, 'tensor', pairs)  46.6 us
    dot_general x7, matrix products, product(): return jnp.dot(block, part, preferred_element_type=F32)  39.8 us
    dot_general x2, matrix products, shrink(): jnp.dot(inputs[c], shrink_table[adapter_ids[c]], preferred_element_type=F32)  3.52 us
  transfers between devices with their start and end apart: 13, of which 4 were waited for; matrix products, arithmetic and copies ran while one was open for 29% of the time, Pallas kernels for 0%

profile of v20, /device:TPU:0, one launch (start us, length us, event | category | flops | bytes accessed | tf_op | source)
XLA Modules:
  0.0 160.1 jit_solution(13437792057092227841)
XLA Ops:
  0.0 3.0 %collective-permute-start = (bf16[512,2048]{1,0:T(8,128)(2,1)}, bf16[512,2048]{1,0:T(8,128)(2,1)}, u32[]{:S(2)}, u32[]{:S(2)}) collective-permute-start(bf16[512,2048]{1,0:T(8,128)(2,1)} %bitcast.39), channel_id=1, source_target_pairs={{0,4},{12,8},{4,0},{8,12},{1,5},{13,9},{5,1},{9,13},{2,6},{14,10},... | collective-permute-start | bytes 6291464 | tf_op jit(solution)/shard_map/ppermute | solution.py:70
  3.0 2.3 %slice.54 = bf16[512,1024]{1,0:T(8,128)(2,1)} slice(bf16[512,2048]{1,0:T(8,128)(2,1)} %bitcast.40), slice={[0:512], [0:1024]} | slice | bytes 2097152 | tf_op jit(solution)/shard_map/slice | solution.py:92
  5.3 1.7 %collective-permute-start.3 = (bf16[512,1024]{1,0:T(8,128)(2,1)}, bf16[512,1024]{1,0:T(8,128)(2,1)}, u32[]{:S(2)}, u32[]{:S(2)}) collective-permute-start(bf16[512,1024]{1,0:T(8,128)(2,1)} %slice.54), channel_id=1, source_target_pairs={{4,8},{8,4},{5,9},{9,5},{6,10},{10,6},{7,11},{11,7},{20,24},{24,20... | collective-permute-start | bytes 3145736 | tf_op jit(solution)/shard_map/ppermute | solution.py:70
  11.8 1.8 %fusion.27 = bf16[256,64]{0,1:T(8,128)(2,1)S(1)} fusion(bf16[2,256,2048]{2,1,0:T(8,128)(2,1)} %param.5, bf16[4,2048,64]{1,2,0:T(8,128)(2,1)} %param.7, s32[]{:T(128)S(6)} %select_n.77), kind=kOutput, calls=%fused_computation.21 | convolution fusion | flops 67125248 | bytes 1343492 | tf_op jit(solution)/shard_map/dot_general | solution.py:12
  13.6 1.8 %fusion.28 = bf16[256,64]{0,1:T(8,128)(2,1)S(1)} fusion(bf16[2,256,2048]{2,1,0:T(8,128)(2,1)} %param.5, bf16[4,2048,64]{1,2,0:T(8,128)(2,1)} %param.7, s32[]{:T(128)S(6)} %select_n.78), kind=kOutput, calls=%fused_computation.22 | convolution fusion | flops 67125248 | bytes 1343492 | tf_op jit(solution)/shard_map/dot_general | solution.py:12
  16.5 1.7 %collective-permute-start.2 = (bf16[512,1024]{1,0:T(8,128)(2,1)}, bf16[512,1024]{1,0:T(8,128)(2,1)}, u32[]{:S(2)}, u32[]{:S(2)}) collective-permute-start(bf16[512,1024]{1,0:T(8,128)(2,1)} %slice.46), channel_id=1, source_target_pairs={{4,8},{8,4},{5,9},{9,5},{6,10},{10,6},{7,11},{11,7},{20,24},{24,20... | collective-permute-start | bytes 3145736 | tf_op jit(solution)/shard_map/ppermute | solution.py:70
  18.2 5.5 %collective-permute-start.1 = (bf16[512,64]{0,1:T(8,128)(2,1)S(1)}, bf16[512,64]{0,1:T(8,128)(2,1)S(1)}, u32[]{:S(2)}, u32[]{:S(2)}) collective-permute-start(bf16[512,64]{0,1:T(8,128)(2,1)S(1)} %get-tuple-element.30), channel_id=1, source_target_pairs={{0,4},{12,8},{1,5},{13,9},{2,6},{14,10},{3,7},{15,11},{16,20},{28,... | collective-permute-start | bytes 196616 | tf_op jit(solution)/shard_map/ppermute | solution.py:70
  23.7 9.4 %fusion.11 = f32[512,2048]{1,0:T(8,128)} fusion(bf16[512,2048]{1,0:T(8,128)(2,1)S(1)} %bitcast.42, bf16[8192,2048]{1,0:T(8,128)(2,1)} %param.6, s32[]{:T(128)S(6)} %select_n.76), kind=kOutput, calls=%fused_computation.13 | convolution fusion | flops 4294967296 | bytes 14680068 | tf_op jit(solution)/shard_map/dot_general | solution.py:89
  34.5 24.7 %collective-permute-start.9 = (bf16[512,1024]{1,0:T(8,128)(2,1)}, bf16[512,1024]{1,0:T(8,128)(2,1)S(1)}, u32[]{:S(2)}, u32[]{:S(2)}) collective-permute-start(bf16[512,1024]{1,0:T(8,128)(2,1)} %slice.46), channel_id=1, source_target_pairs={{0,8},{12,4},{1,9},{13,5},{2,10},{14,6},{3,11},{15,7},{16,24},{28,... | collective-permute-start | bytes 3145736 | tf_op jit(solution)/shard_map/ppermute | solution.py:70
  59.2 1.4 collective-permute-start.6
  60.5 1.3 collective-permute-start.5
  62.6 9.7 %fusion.16 = f32[512,2048]{1,0:T(8,128)S(1)} fusion(f32[512,2048]{1,0:T(8,128)} %fusion.11, bf16[512,2048]{1,0:T(8,128)(2,1)} %collective-permute-done, bf16[8192,2048]{1,0:T(8,128)(2,1)} %param.6, s32[]{:T(128)S(6)} %select_n.79), kind=kOutput, calls=%fused_computation.16 | convolution fusion | flops 4296015872 | bytes 18874372 | tf_op jit(solution)/shard_map/dot_general | solution.py:89
  72.2 30.9 %collective-permute-done.6 = bf16[512,1024]{1,0:T(8,128)(2,1)S(1)} collective-permute-done((bf16[512,1024]{1,0:T(8,128)(2,1)}, bf16[512,1024]{1,0:T(8,128)(2,1)S(1)}, u32[]{:S(2)}, u32[]{:S(2)}) %collective-permute-start.6) | collective-permute-done | bytes 1048608 | tf_op jit(solution)/shard_map/ppermute | solution.py:70
  103.2 1.3 collective-permute-start.8
  104.5 1.3 collective-permute-start.10
  105.8 4.6 %fusion.22 = f32[512,2048]{1,0:T(8,128)S(1)} fusion(f32[512,2048]{1,0:T(8,128)S(1)} %fusion.16, bf16[8192,2048]{1,0:T(8,128)(2,1)} %param.6, s32[]{:T(128)S(6)} %select_n.83, bf16[512,1024]{1,0:T(8,128)(2,1)S(1)} %collective-permute-done.4, bf16[512,1024]{1,0:T(8,128)(2,1)} %collective-permute-done.3, pred[]{:T(512)S(6)} %or.3), kind=kOutput, calls=%fused_computation.18 | convolution fusion | flops 2149056512 | bytes 14680069 | tf_op jit(solution)/shard_map/dot_general | solution.py:89
  111.8 1.5 collective-permute-start.12
  114.2 20.7 %collective-permute-done.10 = bf16[512,1024]{1,0:T(8,128)(2,1)S(1)} collective-permute-done((bf16[512,1024]{1,0:T(8,128)(2,1)S(1)}, bf16[512,1024]{1,0:T(8,128)(2,1)S(1)}, u32[]{:S(2)}, u32[]{:S(2)}) %collective-permute-start.10) | collective-permute-done | bytes 1048608 | tf_op jit(solution)/shard_map/ppermute | solution.py:70
  134.9 4.5 %fusion.5 = f32[512,2048]{1,0:T(8,128)S(1)} fusion(bf16[8192,2048]{1,0:T(8,128)(2,1)} %param.6, s32[]{:T(128)S(6)} %select_n.90, bf16[512,1024]{1,0:T(8,128)(2,1)S(1)} %collective-permute-done.10, bf16[512,1024]{1,0:T(8,128)(2,1)S(1)} %collective-permute-done.6, pred[]{:T(512)S(6)} %or.3), kind=kOutput, calls=%fused_computation.7 | convolution fusion | flops 2148007936 | bytes 10485765 | tf_op jit(solution)/shard_map/dot_general | solution.py:89
  139.5 4.7 %fusion.4 = f32[512,2048]{1,0:T(8,128)S(1)} fusion(f32[512,2048]{1,0:T(8,128)S(1)} %fusion.5, f32[256,2048]{1,0:T(8,128)S(1)} %fusion.42, f32[256,2048]{1,0:T(8,128)S(1)} %fusion.44, f32[512,2048]{1,0:T(8,128)S(1)} %fusion.22, bf16[8192,2048]{1,0:T(8,128)(2,1)} %param.6, s32[]{:T(128)S(6)} %select_n.85, bf16[512,1024]{1,0:T(8,128)(2,1)S(1)} %collective-permute-done.5, ...), kind=kOutput, calls=%fused_computation.5 | convolution fusion | flops 2152202240 | bytes 23068676 | tf_op jit(solution)/shard_map/dot_general | solution.py:89
  144.1 7.6 %collective-permute-done.11 = bf16[512,768]{1,0:T(8,128)(2,1)S(1)} collective-permute-done((bf16[512,768]{1,0:T(8,128)(2,1)S(1)}, bf16[512,768]{1,0:T(8,128)(2,1)S(1)}, u32[]{:S(2)}, u32[]{:S(2)}) %collective-permute-start.11) | collective-permute-done | bytes 786464 | tf_op jit(solution)/shard_map/ppermute | solution.py:70
  151.8 3.7 %fusion.19 = f32[512,2048]{1,0:T(8,128)S(1)} fusion(f32[512,2048]{1,0:T(8,128)S(1)} %fusion.4, bf16[8192,2048]{1,0:T(8,128)(2,1)} %param.6, s32[]{:T(128)S(6)} %select_n.93, bf16[512,768]{1,0:T(8,128)(2,1)S(1)} %collective-permute-done.11, pred[]{:T(512)S(6)} %or.3, bf16[512,1024]{1,0:T(8,128)(2,1)S(1)} %collective-permute-done.9), kind=kOutput, calls=%fused_computation.17 | convolution fusion | flops 1612054528 | bytes 13107205 | tf_op jit(solution)/shard_map/dot_general | solution.py:89
  155.5 1.4 collective-permute-done.12
  156.9 3.3 %add_convert_fusion = bf16[512,2048]{1,0:T(8,128)(2,1)} fusion(f32[512,2048]{1,0:T(8,128)S(1)} %fusion.19, bf16[8192,2048]{1,0:T(8,128)(2,1)} %param.6, s32[]{:T(128)S(6)} %select_n.96, bf16[512,256]{1,0:T(8,128)(2,1)S(1)} %collective-permute-done.12, pred[]{:T(512)S(6)} %or.3, bf16[512,1024]{1,0:T(8,128)(2,1)S(1)} %collective-permute-done.9), kind=kOutput, calls=%fused_computation.6 | convolution fusion | flops 539099136 | bytes 7864325 | tf_op jit(solution)/shard_map/dot_general | solution.py:89
  (26 shorter events, 6.8 us)
Async XLA Ops:
  0.0 113.3 %copy-start = (bf16[4,64,2048]{2,1,0:T(8,128)(2,1)S(1)}, bf16[4,64,2048]{2,1,0:T(8,128)(2,1)}, u32[]{:S(2)}) copy-start(bf16[4,64,2048]{2,1,0:T(8,128)(2,1)} %param.8) | copy-start | bytes 3145732
  0.0 15.3 %copy-start.1 = (bf16[2,256,2048]{2,1,0:T(8,128)(2,1)S(1)}, bf16[2,256,2048]{2,1,0:T(8,128)(2,1)}, u32[]{:S(2)}) copy-start(bf16[2,256,2048]{2,1,0:T(8,128)(2,1)} %param.5) | copy-start | bytes 6291460
  0.0 61.8 %collective-permute-start = (bf16[512,2048]{1,0:T(8,128)(2,1)}, bf16[512,2048]{1,0:T(8,128)(2,1)}, u32[]{:S(2)}, u32[]{:S(2)}) collective-permute-start(bf16[512,2048]{1,0:T(8,128)(2,1)} %bitcast.39), channel_id=1, source_target_pairs={{0,4},{12,8},{4,0},{8,12},{1,5},{13,9},{5,1},{9,13},{2,6},{14,10},... | collective-permute-start | bytes 6291464 | tf_op jit(solution)/shard_map/ppermute | solution.py:70
  5.3 27.8 %collective-permute-start.3 = (bf16[512,1024]{1,0:T(8,128)(2,1)}, bf16[512,1024]{1,0:T(8,128)(2,1)}, u32[]{:S(2)}, u32[]{:S(2)}) collective-permute-start(bf16[512,1024]{1,0:T(8,128)(2,1)} %slice.54), channel_id=1, source_target_pairs={{4,8},{8,4},{5,9},{9,5},{6,10},{10,6},{7,11},{11,7},{20,24},{24,20... | collective-permute-start | bytes 3145736 | tf_op jit(solution)/shard_map/ppermute | solution.py:70
  16.5 17.9 %collective-permute-start.2 = (bf16[512,1024]{1,0:T(8,128)(2,1)}, bf16[512,1024]{1,0:T(8,128)(2,1)}, u32[]{:S(2)}, u32[]{:S(2)}) collective-permute-start(bf16[512,1024]{1,0:T(8,128)(2,1)} %slice.46), channel_id=1, source_target_pairs={{4,8},{8,4},{5,9},{9,5},{6,10},{10,6},{7,11},{11,7},{20,24},{24,20... | collective-permute-start | bytes 3145736 | tf_op jit(solution)/shard_map/ppermute | solution.py:70
  18.2 42.3 %collective-permute-start.1 = (bf16[512,64]{0,1:T(8,128)(2,1)S(1)}, bf16[512,64]{0,1:T(8,128)(2,1)S(1)}, u32[]{:S(2)}, u32[]{:S(2)}) collective-permute-start(bf16[512,64]{0,1:T(8,128)(2,1)S(1)} %get-tuple-element.30), channel_id=1, source_target_pairs={{0,4},{12,8},{1,5},{13,9},{2,6},{14,10},{3,7},{15,11},{16,20},{28,... | collective-permute-start | bytes 196616 | tf_op jit(solution)/shard_map/ppermute | solution.py:70
  33.2 72.6 %collective-permute-start.4 = (bf16[512,1024]{1,0:T(8,128)(2,1)}, bf16[512,1024]{1,0:T(8,128)(2,1)S(1)}, u32[]{:S(2)}, u32[]{:S(2)}) collective-permute-start(bf16[512,1024]{1,0:T(8,128)(2,1)} %collective-permute-done.3), channel_id=1, source_target_pairs={{4,0},{8,12},{5,1},{9,13},{6,2},{10,14},{7,3},{11,15},{20,16},{24,... | collective-permute-start | bytes 3145736 | tf_op jit(solution)/shard_map/ppermute | solution.py:70
  34.5 75.9 %collective-permute-start.9 = (bf16[512,1024]{1,0:T(8,128)(2,1)}, bf16[512,1024]{1,0:T(8,128)(2,1)S(1)}, u32[]{:S(2)}, u32[]{:S(2)}) collective-permute-start(bf16[512,1024]{1,0:T(8,128)(2,1)} %slice.46), channel_id=1, source_target_pairs={{0,8},{12,4},{1,9},{13,5},{2,10},{14,6},{3,11},{15,7},{16,24},{28,... | collective-permute-start | bytes 3145736 | tf_op jit(solution)/shard_map/ppermute | solution.py:70
  59.2 44.0 %collective-permute-start.6 = (bf16[512,1024]{1,0:T(8,128)(2,1)}, bf16[512,1024]{1,0:T(8,128)(2,1)S(1)}, u32[]{:S(2)}, u32[]{:S(2)}) collective-permute-start(bf16[512,1024]{1,0:T(8,128)(2,1)} %slice.54), channel_id=1, source_target_pairs={{0,8},{12,4},{1,9},{13,5},{2,10},{14,6},{3,11},{15,7},{16,24},{28,... | collective-permute-start | bytes 3145736 | tf_op jit(solution)/shard_map/ppermute | solution.py:70
  60.5 78.9 %collective-permute-start.5 = (bf16[512,1024]{1,0:T(8,128)(2,1)}, bf16[512,1024]{1,0:T(8,128)(2,1)S(1)}, u32[]{:S(2)}, u32[]{:S(2)}) collective-permute-start(bf16[512,1024]{1,0:T(8,128)(2,1)} %collective-permute-done.2), channel_id=1, source_target_pairs={{4,0},{8,12},{5,1},{9,13},{6,2},{10,14},{7,3},{11,15},{20,16},{24,... | collective-permute-start | bytes 3145736 | tf_op jit(solution)/shard_map/ppermute | solution.py:70
  61.9 41.3 %collective-permute-start.7 = (bf16[2,512,64]{1,2,0:T(8,128)(2,1)S(1)}, bf16[2,512,64]{1,2,0:T(8,128)(2,1)S(1)}, u32[]{:S(2)}, u32[]{:S(2)}) collective-permute-start(bf16[2,512,64]{1,2,0:T(8,128)(2,1)S(1)} %pad_maximum_fusion), channel_id=1, source_target_pairs={{4,8},{8,4},{5,9},{9,5},{6,10},{10,6},{7,11},{11,7},{20,24},{24,20... | collective-permute-start | bytes 393224 | tf_op jit(solution)/shard_map/ppermute | solution.py:70
  103.2 10.1 %collective-permute-start.8 = (bf16[512,64]{0,1:T(8,128)(2,1)S(1)}, bf16[512,64]{0,1:T(8,128)(2,1)S(1)}, u32[]{:S(2)}, u32[]{:S(2)}) collective-permute-start(bf16[512,64]{0,1:T(8,128)(2,1)S(1)} %fusion.54), channel_id=1, source_target_pairs={{4,0},{8,12},{5,1},{9,13},{6,2},{10,14},{7,3},{11,15},{20,16},{24,... | collective-permute-start | bytes 196616 | tf_op jit(solution)/shard_map/ppermute | solution.py:70
  104.5 30.4 %collective-permute-start.10 = (bf16[512,1024]{1,0:T(8,128)(2,1)S(1)}, bf16[512,1024]{1,0:T(8,128)(2,1)S(1)}, u32[]{:S(2)}, u32[]{:S(2)}) collective-permute-start(bf16[512,1024]{1,0:T(8,128)(2,1)S(1)} %collective-permute-done.6), channel_id=1, source_target_pairs={{4,0},{8,12},{5,1},{9,13},{6,2},{10,14},{7,3},{11,15},{20,16},{24,... | collective-permute-start | bytes 3145736 | tf_op jit(solution)/shard_map/ppermute | solution.py:70
  110.5 41.3 %collective-permute-start.11 = (bf16[512,768]{1,0:T(8,128)(2,1)S(1)}, bf16[512,768]{1,0:T(8,128)(2,1)S(1)}, u32[]{:S(2)}, u32[]{:S(2)}) collective-permute-start(bf16[512,768]{1,0:T(8,128)(2,1)S(1)} %slice.52), channel_id=1, source_target_pairs={{4,0},{8,12},{5,1},{9,13},{6,2},{10,14},{7,3},{11,15},{20,16},{24,... | collective-permute-start | bytes 2359304 | tf_op jit(solution)/shard_map/ppermute | solution.py:70
  111.8 45.1 %collective-permute-start.12 = (bf16[512,256]{1,0:T(8,128)(2,1)S(1)}, bf16[512,256]{1,0:T(8,128)(2,1)S(1)}, u32[]{:S(2)}, u32[]{:S(2)}) collective-permute-start(bf16[512,256]{1,0:T(8,128)(2,1)S(1)} %slice.53), channel_id=1, source_target_pairs={{4,0},{8,12},{5,1},{9,13},{6,2},{10,14},{7,3},{11,15},{20,16},{24,... | collective-permute-start | bytes 786440 | tf_op jit(solution)/shard_map/ppermute | solution.py:70

commit v21 on v16

--- a/solution.py
+++ b/solution.py
@@ -81,7 +81,7 @@
     far_mid = jnp.where(here < 2, 2, 1)
     far_end = jnp.where(here < 2, 3, 0)
     own = inputs.reshape(rows, width)
-    half, last = width // 2, width // 8
+    half, low = width // 2, rows // 4 * 3
 
     def product(block, owner, first=0):
         part = lax.dynamic_slice_in_dim(base_weight, owner * width + first, block.shape[1], axis=0)
@@ -113,15 +113,16 @@
 
     late = after(end[1], total)
     shrunk = after(shrunk, late)
-    end_out += [send(late[:, : half - last], OUTWARD), send(late[:, half - last :], OUTWARD)]
+    end_out += [send(late[:low], OUTWARD), send(late[low:], OUTWARD)]
     total = total + product(jnp.where(is_end, mid_out[1], mid[1]), far_mid, half)
     total = total + jnp.concatenate(expand(shrunk, expand_table, adapter_ids))
     total = total + product(jnp.where(is_end, end_out[0], end[0]), far_end)
-    block = jnp.where(is_end, after(end_out[1], total), late[:, : half - last])
-    total = total + product(block, far_end, half)
-    block = jnp.where(is_end, after(end_out[2], total), late[:, half - last :])
-    total = total + product(block, far_end, width - last)
-    return total.astype(BF16).reshape(chats, span, -1)
+    out = total.astype(BF16)
+    for piece, first in ((1, 0), (2, low)):
+        block = jnp.where(is_end, after(end_out[piece], out), late[first:][: end_out[piece].shape[0]])
+        part = total[first:][: block.shape[0]] + product(block, far_end, half)
+        out = lax.dynamic_update_slice(out, part.astype(BF16), (first, 0))
+    return out.reshape(chats, span, -1)
 
 
 def solution(mesh):

time: 144 us -> 145 us (level)
  no operation moved by 1% of the time
where the time goes in v21:
time: 145 us
  waiting for transfers between devices  64.7 us (45%)
  matrix products  44.8 us (31%)
  starting transfers between devices  22 us (15%)
  local copies, waits for them, and re-layouts  8.81 us (6%)
  between operations  4.39 us (3%)
    ppermute x13, waiting for transfers between devices, send(): return lax.ppermute(block, 'tensor', pairs)  64.7 us
    dot_general x7, matrix products, product(): return jnp.dot(block, part, preferred_element_type=F32)  40.3 us
    ppermute x13, starting transfers between devices, send(): return lax.ppermute(block, 'tensor', pairs)  22 us
    dot_general x2, matrix products, shrink(): jnp.dot(inputs[c], shrink_table[adapter_ids[c]], preferred_element_type=F32)  3.52 us
  transfers between devices with their start and end apart: 13, of which 7 were waited for; matrix products, arithmetic and copies ran while one was open for 34% of the time, Pallas kernels for 0%

profile of v21, /device:TPU:0, one launch (start us, length us, event | category | flops | bytes accessed | tf_op | source)
XLA Modules:
  0.0 144.7 jit_solution(15240623673148190336)
XLA Ops:
  0.0 3.0 %collective-permute-start = (bf16[512,2048]{1,0:T(8,128)(2,1)}, bf16[512,2048]{1,0:T(8,128)(2,1)}, u32[]{:S(2)}, u32[]{:S(2)}) collective-permute-start(bf16[512,2048]{1,0:T(8,128)(2,1)} %bitcast.39), channel_id=1, source_target_pairs={{0,4},{12,8},{4,0},{8,12},{1,5},{13,9},{5,1},{9,13},{2,6},{14,10},... | collective-permute-start | bytes 6291464 | tf_op jit(solution)/shard_map/ppermute | solution.py:69
  3.0 2.3 %slice.70 = bf16[512,1024]{1,0:T(8,128)(2,1)} slice(bf16[512,2048]{1,0:T(8,128)(2,1)} %bitcast.40), slice={[0:512], [0:1024]} | slice | bytes 2097152 | tf_op jit(solution)/shard_map/slice | solution.py:91
  5.3 1.6 %collective-permute-start.2 = (bf16[512,1024]{1,0:T(8,128)(2,1)}, bf16[512,1024]{1,0:T(8,128)(2,1)}, u32[]{:S(2)}, u32[]{:S(2)}) collective-permute-start(bf16[512,1024]{1,0:T(8,128)(2,1)} %slice.70), channel_id=1, source_target_pairs={{4,8},{8,4},{5,9},{9,5},{6,10},{10,6},{7,11},{11,7},{20,24},{24,20... | collective-permute-start | bytes 3145736 | tf_op jit(solution)/shard_map/ppermute | solution.py:69
  7.0 1.4 fusion.81
  12.5 1.8 %fusion.28 = bf16[256,64]{0,1:T(8,128)(2,1)S(1)} fusion(bf16[2,256,2048]{2,1,0:T(8,128)(2,1)} %param.5, bf16[4,2048,64]{1,2,0:T(8,128)(2,1)} %param.7, s32[]{:T(128)S(6)} %select_n.75), kind=kOutput, calls=%fused_computation.24 | convolution fusion | flops 67125248 | bytes 1343492 | tf_op jit(solution)/shard_map/dot_general | solution.py:12
  14.3 1.8 %fusion.29 = bf16[256,64]{0,1:T(8,128)(2,1)S(1)} fusion(bf16[2,256,2048]{2,1,0:T(8,128)(2,1)} %param.5, bf16[4,2048,64]{1,2,0:T(8,128)(2,1)} %param.7, s32[]{:T(128)S(6)} %select_n.76), kind=kOutput, calls=%fused_computation.25 | convolution fusion | flops 67125248 | bytes 1343492 | tf_op jit(solution)/shard_map/dot_general | solution.py:12
  17.2 1.7 %collective-permute-start.4 = (bf16[512,1024]{1,0:T(8,128)(2,1)}, bf16[512,1024]{1,0:T(8,128)(2,1)}, u32[]{:S(2)}, u32[]{:S(2)}) collective-permute-start(bf16[512,1024]{1,0:T(8,128)(2,1)} %slice.59), channel_id=1, source_target_pairs={{4,8},{8,4},{5,9},{9,5},{6,10},{10,6},{7,11},{11,7},{20,24},{24,20... | collective-permute-start | bytes 3145736 | tf_op jit(solution)/shard_map/ppermute | solution.py:69
  18.9 5.6 %collective-permute-start.1 = (bf16[512,64]{0,1:T(8,128)(2,1)S(1)}, bf16[512,64]{0,1:T(8,128)(2,1)S(1)}, u32[]{:S(2)}, u32[]{:S(2)}) collective-permute-start(bf16[512,64]{0,1:T(8,128)(2,1)S(1)} %get-tuple-element.30), channel_id=1, source_target_pairs={{0,4},{12,8},{1,5},{13,9},{2,6},{14,10},{3,7},{15,11},{16,20},{28,... | collective-permute-start | bytes 196616 | tf_op jit(solution)/shard_map/ppermute | solution.py:69
  24.4 9.4 %fusion.15 = f32[512,2048]{1,0:T(8,128)} fusion(bf16[512,2048]{1,0:T(8,128)(2,1)S(1)} %bitcast.42, bf16[8192,2048]{1,0:T(8,128)(2,1)} %param.6, s32[]{:T(128)S(6)} %select_n.74), kind=kOutput, calls=%fused_computation.16 | convolution fusion | flops 4294967296 | bytes 14680068 | tf_op jit(solution)/shard_map/dot_general | solution.py:88
  35.1 14.4 %collective-permute-done.1 = bf16[512,64]{0,1:T(8,128)(2,1)S(1)} collective-permute-done((bf16[512,64]{0,1:T(8,128)(2,1)S(1)}, bf16[512,64]{0,1:T(8,128)(2,1)S(1)}, u32[]{:S(2)}, u32[]{:S(2)}) %collective-permute-start.1) | collective-permute-done | bytes 65568 | tf_op jit(solution)/shard_map/ppermute | solution.py:69
  49.8 1.3 slice.60
  53.2 9.7 %fusion.19 = f32[512,2048]{1,0:T(8,128)S(1)} fusion(f32[512,2048]{1,0:T(8,128)} %fusion.15, bf16[512,2048]{1,0:T(8,128)(2,1)} %collective-permute-done, bf16[8192,2048]{1,0:T(8,128)(2,1)} %param.6, s32[]{:T(128)S(6)} %select_n.77), kind=kOutput, calls=%fused_computation.19 | convolution fusion | flops 4296015872 | bytes 18874372 | tf_op jit(solution)/shard_map/dot_general | solution.py:88
  63.6 1.3 slice.63
  65.6 6.6 %collective-permute-done.3 = bf16[512,1024]{1,0:T(8,128)(2,1)S(1)} collective-permute-done((bf16[512,1024]{1,0:T(8,128)(2,1)}, bf16[512,1024]{1,0:T(8,128)(2,1)S(1)}, u32[]{:S(2)}, u32[]{:S(2)}) %collective-permute-start.3) | collective-permute-done | bytes 1048608 | tf_op jit(solution)/shard_map/ppermute | solution.py:69
  72.2 4.6 %fusion.22 = f32[512,2048]{1,0:T(8,128)S(1)} fusion(f32[512,2048]{1,0:T(8,128)S(1)} %fusion.19, bf16[8192,2048]{1,0:T(8,128)(2,1)} %param.6, s32[]{:T(128)S(6)} %select_n.81, bf16[512,1024]{1,0:T(8,128)(2,1)S(1)} %collective-permute-done.3, bf16[512,1024]{1,0:T(8,128)(2,1)} %collective-permute-done.2, pred[]{:T(512)S(6)} %or.3), kind=kOutput, calls=%fused_computation.20 | convolution fusion | flops 2149056512 | bytes 14680069 | tf_op jit(solution)/shard_map/dot_general | solution.py:88
  79.4 15.2 %collective-permute-done.5 = bf16[512,1024]{1,0:T(8,128)(2,1)S(1)} collective-permute-done((bf16[512,1024]{1,0:T(8,128)(2,1)}, bf16[512,1024]{1,0:T(8,128)(2,1)S(1)}, u32[]{:S(2)}, u32[]{:S(2)}) %collective-permute-start.5) | collective-permute-done | bytes 1048608 | tf_op jit(solution)/shard_map/ppermute | solution.py:69
  94.7 4.5 %fusion.7 = f32[512,2048]{1,0:T(8,128)S(1)} fusion(bf16[8192,2048]{1,0:T(8,128)(2,1)} %param.6, s32[]{:T(128)S(6)} %select_n.83, bf16[512,1024]{1,0:T(8,128)(2,1)S(1)} %collective-permute-done.5, bf16[512,1024]{1,0:T(8,128)(2,1)} %collective-permute-done.4, pred[]{:T(512)S(6)} %or.3), kind=kOutput, calls=%fused_computation.8 | convolution fusion | flops 2148007936 | bytes 10485765 | tf_op jit(solution)/shard_map/dot_general | solution.py:88
  100.6 1.5 %collective-permute-start.12 = (bf16[128,1024]{1,0:T(8,128)(2,1)S(1)}, bf16[128,1024]{1,0:T(8,128)(2,1)}, u32[]{:S(2)}, u32[]{:S(2)}) collective-permute-start(bf16[128,1024]{1,0:T(8,128)(2,1)S(1)} %slice.69), channel_id=1, source_target_pairs={{4,0},{8,12},{5,1},{9,13},{6,2},{10,14},{7,3},{11,15},{20,16},{24,... | collective-permute-start | bytes 786440 | tf_op jit(solution)/shard_map/ppermute | solution.py:69
  103.0 15.5 %collective-permute-done.10 = bf16[512,1024]{1,0:T(8,128)(2,1)S(1)} collective-permute-done((bf16[512,1024]{1,0:T(8,128)(2,1)S(1)}, bf16[512,1024]{1,0:T(8,128)(2,1)S(1)}, u32[]{:S(2)}, u32[]{:S(2)}) %collective-permute-start.10) | collective-permute-done | bytes 1048608 | tf_op jit(solution)/shard_map/ppermute | solution.py:69
  118.5 4.8 %fusion.82 = (bf16[512,2048]{1,0:T(8,128)(2,1)S(1)}, f32[512,2048]{1,0:T(8,128)S(1)}) fusion(bf16[8192,2048]{1,0:T(8,128)(2,1)} %param.6, s32[]{:T(128)S(6)} %select_n.88, bf16[512,1024]{1,0:T(8,128)(2,1)S(1)} %collective-permute-done.10, bf16[512,1024]{1,0:T(8,128)(2,1)S(1)} %collective-permute-done.6, pred[]{:T(512)S(6)} %or.3, ...), kind=kOutput, calls=%fused_computation.76 | convolution fusion | flops 2153250816 | bytes 25165828 | tf_op jit(solution)/shard_map/dot_general | solution.py:88
  123.3 12.2 %collective-permute-done.11 = bf16[384,1024]{1,0:T(8,128)(2,1)} collective-permute-done((bf16[384,1024]{1,0:T(8,128)(2,1)S(1)}, bf16[384,1024]{1,0:T(8,128)(2,1)}, u32[]{:S(2)}, u32[]{:S(2)}) %collective-permute-start.11) | collective-permute-done | bytes 786464 | tf_op jit(solution)/shard_map/ppermute | solution.py:69
  135.5 4.3 %fusion.27 = bf16[512,2048]{1,0:T(8,128)(2,1)S(1)} fusion(bf16[512,2048]{1,0:T(8,128)(2,1)S(1)} %get-tuple-element.33, f32[512,2048]{1,0:T(8,128)S(1)} %get-tuple-element.34, bf16[8192,2048]{1,0:T(8,128)(2,1)} %param.6, s32[]{:T(128)S(6)} %select_n.91, bf16[384,1024]{1,0:T(8,128)(2,1)} %collective-permute-done.11, pred[]{:T(512)S(6)} %or.3, ...), kind=kOutput, calls=%fused_computation.21 | convolution fusion | flops 1612578816 | bytes 10485765 | tf_op jit(solution)/shard_map/dot_general | solution.py:88
  140.3 3.1 %fusion.47 = bf16[512,2048]{1,0:T(8,128)(2,1)S(1)} fusion(bf16[512,2048]{1,0:T(8,128)(2,1)S(1)} %fusion.27, f32[512,2048]{1,0:T(8,128)S(1)} %get-tuple-element.34, bf16[8192,2048]{1,0:T(8,128)(2,1)} %param.6, s32[]{:T(128)S(6)} %select_n.91, bf16[128,1024]{1,0:T(8,128)(2,1)} %collective-permute-done.12, pred[]{:T(512)S(6)} %or.3, ...), kind=kOutput, calls=%fused_computation.40 | convolution fusion | flops 537526272 | bytes 6291461 | tf_op jit(solution)/shard_map/dot_general | solution.py:88
  143.4 1.3 copy-done.1
  (30 shorter events, 11.6 us)
Async XLA Ops:
  0.0 102.1 %copy-start = (bf16[4,64,2048]{2,1,0:T(8,128)(2,1)S(1)}, bf16[4,64,2048]{2,1,0:T(8,128)(2,1)}, u32[]{:S(2)}) copy-start(bf16[4,64,2048]{2,1,0:T(8,128)(2,1)} %param.8) | copy-start | bytes 3145732
  0.0 16.0 %copy-start.2 = (bf16[2,256,2048]{2,1,0:T(8,128)(2,1)S(1)}, bf16[2,256,2048]{2,1,0:T(8,128)(2,1)}, u32[]{:S(2)}) copy-start(bf16[2,256,2048]{2,1,0:T(8,128)(2,1)} %param.5) | copy-start | bytes 6291460
  0.0 49.8 %collective-permute-start = (bf16[512,2048]{1,0:T(8,128)(2,1)}, bf16[512,2048]{1,0:T(8,128)(2,1)}, u32[]{:S(2)}, u32[]{:S(2)}) collective-permute-start(bf16[512,2048]{1,0:T(8,128)(2,1)} %bitcast.39), channel_id=1, source_target_pairs={{0,4},{12,8},{4,0},{8,12},{1,5},{13,9},{5,1},{9,13},{2,6},{14,10},... | collective-permute-start | bytes 6291464 | tf_op jit(solution)/shard_map/ppermute | solution.py:69
  5.3 28.5 %collective-permute-start.2 = (bf16[512,1024]{1,0:T(8,128)(2,1)}, bf16[512,1024]{1,0:T(8,128)(2,1)}, u32[]{:S(2)}, u32[]{:S(2)}) collective-permute-start(bf16[512,1024]{1,0:T(8,128)(2,1)} %slice.70), channel_id=1, source_target_pairs={{4,8},{8,4},{5,9},{9,5},{6,10},{10,6},{7,11},{11,7},{20,24},{24,20... | collective-permute-start | bytes 3145736 | tf_op jit(solution)/shard_map/ppermute | solution.py:69
  17.2 34.7 %collective-permute-start.4 = (bf16[512,1024]{1,0:T(8,128)(2,1)}, bf16[512,1024]{1,0:T(8,128)(2,1)}, u32[]{:S(2)}, u32[]{:S(2)}) collective-permute-start(bf16[512,1024]{1,0:T(8,128)(2,1)} %slice.59), channel_id=1, source_target_pairs={{4,8},{8,4},{5,9},{9,5},{6,10},{10,6},{7,11},{11,7},{20,24},{24,20... | collective-permute-start | bytes 3145736 | tf_op jit(solution)/shard_map/ppermute | solution.py:69
  18.9 30.7 %collective-permute-start.1 = (bf16[512,64]{0,1:T(8,128)(2,1)S(1)}, bf16[512,64]{0,1:T(8,128)(2,1)S(1)}, u32[]{:S(2)}, u32[]{:S(2)}) collective-permute-start(bf16[512,64]{0,1:T(8,128)(2,1)S(1)} %get-tuple-element.30), channel_id=1, source_target_pairs={{0,4},{12,8},{1,5},{13,9},{2,6},{14,10},{3,7},{15,11},{16,20},{28,... | collective-permute-start | bytes 196616 | tf_op jit(solution)/shard_map/ppermute | solution.py:69
  33.8 38.4 %collective-permute-start.3 = (bf16[512,1024]{1,0:T(8,128)(2,1)}, bf16[512,1024]{1,0:T(8,128)(2,1)S(1)}, u32[]{:S(2)}, u32[]{:S(2)}) collective-permute-start(bf16[512,1024]{1,0:T(8,128)(2,1)} %collective-permute-done.2), channel_id=1, source_target_pairs={{4,0},{8,12},{5,1},{9,13},{6,2},{10,14},{7,3},{11,15},{20,16},{24,... | collective-permute-start | bytes 3145736 | tf_op jit(solution)/shard_map/ppermute | solution.py:69
  51.1 12.4 %collective-permute-start.6 = (bf16[512,1024]{1,0:T(8,128)(2,1)S(1)}, bf16[512,1024]{1,0:T(8,128)(2,1)S(1)}, u32[]{:S(2)}, u32[]{:S(2)}) collective-permute-start(bf16[512,1024]{1,0:T(8,128)(2,1)S(1)} %slice.60), channel_id=1, source_target_pairs={{4,8},{8,4},{5,9},{9,5},{6,10},{10,6},{7,11},{11,7},{20,24},{24,20... | collective-permute-start | bytes 3145736 | tf_op jit(solution)/shard_map/ppermute | solution.py:69
  51.9 42.8 %collective-permute-start.5 = (bf16[512,1024]{1,0:T(8,128)(2,1)}, bf16[512,1024]{1,0:T(8,128)(2,1)S(1)}, u32[]{:S(2)}, u32[]{:S(2)}) collective-permute-start(bf16[512,1024]{1,0:T(8,128)(2,1)} %collective-permute-done.4), channel_id=1, source_target_pairs={{4,0},{8,12},{5,1},{9,13},{6,2},{10,14},{7,3},{11,15},{20,16},{24,... | collective-permute-start | bytes 3145736 | tf_op jit(solution)/shard_map/ppermute | solution.py:69
  62.9 13.9 %collective-permute-start.7 = (bf16[2,512,64]{1,2,0:T(8,128)(2,1)S(1)}, bf16[2,512,64]{1,2,0:T(8,128)(2,1)S(1)}, u32[]{:S(2)}, u32[]{:S(2)}) collective-permute-start(bf16[2,512,64]{1,2,0:T(8,128)(2,1)S(1)} %pad_maximum_fusion), channel_id=1, source_target_pairs={{4,8},{8,4},{5,9},{9,5},{6,10},{10,6},{7,11},{11,7},{20,24},{24,20... | collective-permute-start | bytes 393224 | tf_op jit(solution)/shard_map/ppermute | solution.py:69
  64.9 34.4 %collective-permute-start.9 = (bf16[512,1024]{1,0:T(8,128)(2,1)S(1)}, bf16[512,1024]{1,0:T(8,128)(2,1)S(1)}, u32[]{:S(2)}, u32[]{:S(2)}) collective-permute-start(bf16[512,1024]{1,0:T(8,128)(2,1)S(1)} %slice.63), channel_id=1, source_target_pairs={{4,8},{8,4},{5,9},{9,5},{6,10},{10,6},{7,11},{11,7},{20,24},{24,20... | collective-permute-start | bytes 3145736 | tf_op jit(solution)/shard_map/ppermute | solution.py:69
  76.8 22.4 %collective-permute-start.8 = (bf16[512,64]{0,1:T(8,128)(2,1)S(1)}, bf16[512,64]{0,1:T(8,128)(2,1)S(1)}, u32[]{:S(2)}, u32[]{:S(2)}) collective-permute-start(bf16[512,64]{0,1:T(8,128)(2,1)S(1)} %fusion.64), channel_id=1, source_target_pairs={{4,0},{8,12},{5,1},{9,13},{6,2},{10,14},{7,3},{11,15},{20,16},{24,... | collective-permute-start | bytes 196616 | tf_op jit(solution)/shard_map/ppermute | solution.py:69
  78.1 40.4 %collective-permute-start.10 = (bf16[512,1024]{1,0:T(8,128)(2,1)S(1)}, bf16[512,1024]{1,0:T(8,128)(2,1)S(1)}, u32[]{:S(2)}, u32[]{:S(2)}) collective-permute-start(bf16[512,1024]{1,0:T(8,128)(2,1)S(1)} %collective-permute-done.6), channel_id=1, source_target_pairs={{4,0},{8,12},{5,1},{9,13},{6,2},{10,14},{7,3},{11,15},{20,16},{24,... | collective-permute-start | bytes 3145736 | tf_op jit(solution)/shard_map/ppermute | solution.py:69
  99.3 36.2 %collective-permute-start.11 = (bf16[384,1024]{1,0:T(8,128)(2,1)S(1)}, bf16[384,1024]{1,0:T(8,128)(2,1)}, u32[]{:S(2)}, u32[]{:S(2)}) collective-permute-start(bf16[384,1024]{1,0:T(8,128)(2,1)S(1)} %slice.67), channel_id=1, source_target_pairs={{4,0},{8,12},{5,1},{9,13},{6,2},{10,14},{7,3},{11,15},{20,16},{24,... | collective-permute-start | bytes 2359304 | tf_op jit(solution)/shard_map/ppermute | solution.py:69
  100.6 39.7 %collective-permute-start.12 = (bf16[128,1024]{1,0:T(8,128)(2,1)S(1)}, bf16[128,1024]{1,0:T(8,128)(2,1)}, u32[]{:S(2)}, u32[]{:S(2)}) collective-permute-start(bf16[128,1024]{1,0:T(8,128)(2,1)S(1)} %slice.69), channel_id=1, source_target_pairs={{4,0},{8,12},{5,1},{9,13},{6,2},{10,14},{7,3},{11,15},{20,16},{24,... | collective-permute-start | bytes 786440 | tf_op jit(solution)/shard_map/ppermute | solution.py:69
  143.4 1.3 copy-start.1

commit v22 on v16

--- a/solution.py
+++ b/solution.py
@@ -112,6 +112,9 @@
     total = total + product(jnp.where(is_end, mid_out[0], mid[0]), far_mid)
 
     late = after(end[1], total)
+    last_rows = after(
+        lax.dynamic_slice_in_dim(base_weight, (far_end + 1) * width - last, last, axis=0), late
+    )
     shrunk = after(shrunk, late)
     end_out += [send(late[:, : half - last], OUTWARD), send(late[:, half - last :], OUTWARD)]
     total = total + product(jnp.where(is_end, mid_out[1], mid[1]), far_mid, half)
@@ -120,7 +123,7 @@
     block = jnp.where(is_end, after(end_out[1], total), late[:, : half - last])
     total = total + product(block, far_end, half)
     block = jnp.where(is_end, after(end_out[2], total), late[:, half - last :])
-    total = total + product(block, far_end, width - last)
+    total = total + jnp.dot(block, last_rows, preferred_element_type=F32)
     return total.astype(BF16).reshape(chats, span, -1)
 
 

time: 144 us -> 149 us (1.035)
  waiting for transfers between devices: 66 us -> 74.4 us
  starting transfers between devices: 22 us -> 18.5 us
    ppermute x13, waiting for transfers between devices: 66 us -> 74.4 us  [send(): return lax.ppermute(block, 'tensor', pairs)]
    ppermute x13, starting transfers between devices: 22 us -> 18.5 us  [send(): return lax.ppermute(block, 'tensor', pairs)]
    dot_general x7 -> x6, matrix products: 39.7 us -> 36.4 us  [product(): return jnp.dot(block, part, preferred_element_type=F32)]
    dot_general x0 -> x1, matrix products: none -> 2.04 us  [line(): total = total + jnp.dot(block, last_rows, preferred_element_type=F32)]
  transfers between devices with their start and end apart: 13 -> 13, of which waited for: 7 -> 7; matrix products, arithmetic and copies ran while one was open for 34% -> 33% of each run, Pallas kernels for 0% -> 0%
where the time goes in v22:
time: 149 us
  waiting for transfers between devices  74.4 us (50%)
  matrix products  42.9 us (29%)
  starting transfers between devices  18.5 us (12%)
  local copies, waits for them, and re-layouts  8.75 us (6%)
  between operations  4.11 us (3%)
    ppermute x13, waiting for transfers between devices, send(): return lax.ppermute(block, 'tensor', pairs)  74.4 us
    dot_general x6, matrix products, product(): return jnp.dot(block, part, preferred_element_type=F32)  36.4 us
    ppermute x13, starting transfers between devices, send(): return lax.ppermute(block, 'tensor', pairs)  18.5 us
    dot_general x2, matrix products, shrink(): jnp.dot(inputs[c], shrink_table[adapter_ids[c]], preferred_element_type=F32)  3.52 us
  transfers between devices with their start and end apart: 13, of which 7 were waited for; matrix products, arithmetic and copies ran while one was open for 33% of the time, Pallas kernels for 0%

profile of v22, /device:TPU:0, one launch (start us, length us, event | category | flops | bytes accessed | tf_op | source)
XLA Modules:
  0.0 148.7 jit_solution(9294612155454773606)
XLA Ops:
  0.0 3.0 %collective-permute-start = (bf16[512,2048]{1,0:T(8,128)(2,1)}, bf16[512,2048]{1,0:T(8,128)(2,1)}, u32[]{:S(2)}, u32[]{:S(2)}) collective-permute-start(bf16[512,2048]{1,0:T(8,128)(2,1)} %bitcast.40), channel_id=1, source_target_pairs={{0,4},{12,8},{4,0},{8,12},{1,5},{13,9},{5,1},{9,13},{2,6},{14,10},... | collective-permute-start | bytes 6291464 | tf_op jit(solution)/shard_map/ppermute | solution.py:69
  3.0 1.3 fusion.69
  8.2 1.8 %fusion.28 = bf16[256,64]{0,1:T(8,128)(2,1)S(1)} fusion(bf16[2,256,2048]{2,1,0:T(8,128)(2,1)} %param.5, bf16[4,2048,64]{1,2,0:T(8,128)(2,1)} %param.7, s32[]{:T(128)S(6)} %select_n.78), kind=kOutput, calls=%fused_computation.22 | convolution fusion | flops 67125248 | bytes 1343492 | tf_op jit(solution)/shard_map/dot_general | solution.py:12
  10.0 1.8 %fusion.27 = bf16[256,64]{0,1:T(8,128)(2,1)S(1)} fusion(bf16[2,256,2048]{2,1,0:T(8,128)(2,1)} %param.5, bf16[4,2048,64]{1,2,0:T(8,128)(2,1)} %param.7, s32[]{:T(128)S(6)} %select_n.77), kind=kOutput, calls=%fused_computation.21 | convolution fusion | flops 67125248 | bytes 1343492 | tf_op jit(solution)/shard_map/dot_general | solution.py:12
  11.8 2.0 %collective-permute-start.1 = (bf16[512,64]{0,1:T(8,128)(2,1)S(1)}, bf16[512,64]{0,1:T(8,128)(2,1)S(1)}, u32[]{:S(2)}, u32[]{:S(2)}) collective-permute-start(bf16[512,64]{0,1:T(8,128)(2,1)S(1)} %get-tuple-element.32), channel_id=1, source_target_pairs={{0,4},{12,8},{1,5},{13,9},{2,6},{14,10},{3,7},{15,11},{16,20},{28,... | collective-permute-start | bytes 196616 | tf_op jit(solution)/shard_map/ppermute | solution.py:69
  13.8 2.3 %slice.62 = bf16[512,1024]{1,0:T(8,128)(2,1)} slice(bf16[512,2048]{1,0:T(8,128)(2,1)} %bitcast.41), slice={[0:512], [0:1024]} | slice | bytes 2097152 | tf_op jit(solution)/shard_map/slice | solution.py:91
  16.0 1.7 %collective-permute-start.2 = (bf16[512,1024]{1,0:T(8,128)(2,1)}, bf16[512,1024]{1,0:T(8,128)(2,1)}, u32[]{:S(2)}, u32[]{:S(2)}) collective-permute-start(bf16[512,1024]{1,0:T(8,128)(2,1)} %slice.62), channel_id=1, source_target_pairs={{4,8},{8,4},{5,9},{9,5},{6,10},{10,6},{7,11},{11,7},{20,24},{24,20... | collective-permute-start | bytes 3145736 | tf_op jit(solution)/shard_map/ppermute | solution.py:69
  18.9 1.7 %collective-permute-start.4 = (bf16[512,1024]{1,0:T(8,128)(2,1)}, bf16[512,1024]{1,0:T(8,128)(2,1)}, u32[]{:S(2)}, u32[]{:S(2)}) collective-permute-start(bf16[512,1024]{1,0:T(8,128)(2,1)} %slice.53), channel_id=1, source_target_pairs={{4,8},{8,4},{5,9},{9,5},{6,10},{10,6},{7,11},{11,7},{20,24},{24,20... | collective-permute-start | bytes 3145736 | tf_op jit(solution)/shard_map/ppermute | solution.py:69
  20.6 9.4 %fusion.11 = f32[512,2048]{1,0:T(8,128)} fusion(bf16[512,2048]{1,0:T(8,128)(2,1)S(1)} %bitcast.43, bf16[8192,2048]{1,0:T(8,128)(2,1)} %param.6, s32[]{:T(128)S(6)} %select_n.76), kind=kOutput, calls=%fused_computation.13 | convolution fusion | flops 4294967296 | bytes 14680068 | tf_op jit(solution)/shard_map/dot_general | solution.py:88
  32.6 17.0 %collective-permute-done.1 = bf16[512,64]{0,1:T(8,128)(2,1)S(1)} collective-permute-done((bf16[512,64]{0,1:T(8,128)(2,1)S(1)}, bf16[512,64]{0,1:T(8,128)(2,1)S(1)}, u32[]{:S(2)}, u32[]{:S(2)}) %collective-permute-start.1) | collective-permute-done | bytes 65568 | tf_op jit(solution)/shard_map/ppermute | solution.py:69
  49.8 1.3 slice.54
  53.9 9.7 %fusion.16 = f32[512,2048]{1,0:T(8,128)S(1)} fusion(f32[512,2048]{1,0:T(8,128)} %fusion.11, bf16[512,2048]{1,0:T(8,128)(2,1)} %collective-permute-done, bf16[8192,2048]{1,0:T(8,128)(2,1)} %param.6, s32[]{:T(128)S(6)} %select_n.79), kind=kOutput, calls=%fused_computation.16 | convolution fusion | flops 4296015872 | bytes 18874372 | tf_op jit(solution)/shard_map/dot_general | solution.py:88
  63.6 1.3 slice.57
  65.6 6.6 %collective-permute-done.3 = bf16[512,1024]{1,0:T(8,128)(2,1)S(1)} collective-permute-done((bf16[512,1024]{1,0:T(8,128)(2,1)}, bf16[512,1024]{1,0:T(8,128)(2,1)S(1)}, u32[]{:S(2)}, u32[]{:S(2)}) %collective-permute-start.3) | collective-permute-done | bytes 1048608 | tf_op jit(solution)/shard_map/ppermute | solution.py:69
  72.2 4.5 %fusion.22 = f32[512,2048]{1,0:T(8,128)S(1)} fusion(f32[512,2048]{1,0:T(8,128)S(1)} %fusion.16, bf16[8192,2048]{1,0:T(8,128)(2,1)} %param.6, s32[]{:T(128)S(6)} %select_n.83, bf16[512,1024]{1,0:T(8,128)(2,1)S(1)} %collective-permute-done.3, bf16[512,1024]{1,0:T(8,128)(2,1)} %collective-permute-done.2, pred[]{:T(512)S(6)} %or.3), kind=kOutput, calls=%fused_computation.18 | convolution fusion | flops 2149056512 | bytes 14680069 | tf_op jit(solution)/shard_map/dot_general | solution.py:88
  79.4 14.4 %collective-permute-done.5 = bf16[512,1024]{1,0:T(8,128)(2,1)S(1)} collective-permute-done((bf16[512,1024]{1,0:T(8,128)(2,1)}, bf16[512,1024]{1,0:T(8,128)(2,1)S(1)}, u32[]{:S(2)}, u32[]{:S(2)}) %collective-permute-start.5) | collective-permute-done | bytes 1048608 | tf_op jit(solution)/shard_map/ppermute | solution.py:69
  93.8 4.5 %fusion.7 = f32[512,2048]{1,0:T(8,128)S(1)} fusion(bf16[8192,2048]{1,0:T(8,128)(2,1)} %param.6, s32[]{:T(128)S(6)} %select_n.85, bf16[512,1024]{1,0:T(8,128)(2,1)S(1)} %collective-permute-done.5, bf16[512,1024]{1,0:T(8,128)(2,1)} %collective-permute-done.4, pred[]{:T(512)S(6)} %or.3), kind=kOutput, calls=%fused_computation.9 | convolution fusion | flops 2148007936 | bytes 10485765 | tf_op jit(solution)/shard_map/dot_general | solution.py:88
  98.4 5.6 %collective-permute-done.8 = bf16[512,64]{0,1:T(8,128)(2,1)S(1)} collective-permute-done((bf16[512,64]{0,1:T(8,128)(2,1)S(1)}, bf16[512,64]{0,1:T(8,128)(2,1)S(1)}, u32[]{:S(2)}, u32[]{:S(2)}) %collective-permute-start.8) | collective-permute-done | bytes 65568 | tf_op jit(solution)/shard_map/ppermute | solution.py:69
  105.4 1.5 collective-permute-start.12
  107.8 18.6 %collective-permute-done.10 = bf16[512,1024]{1,0:T(8,128)(2,1)S(1)} collective-permute-done((bf16[512,1024]{1,0:T(8,128)(2,1)S(1)}, bf16[512,1024]{1,0:T(8,128)(2,1)S(1)}, u32[]{:S(2)}, u32[]{:S(2)}) %collective-permute-start.10) | collective-permute-done | bytes 1048608 | tf_op jit(solution)/shard_map/ppermute | solution.py:69
  126.4 4.6 %fusion.4 = f32[512,2048]{1,0:T(8,128)S(1)} fusion(f32[256,2048]{1,0:T(8,128)S(1)} %fusion.41, f32[256,2048]{1,0:T(8,128)S(1)} %fusion.43, f32[512,2048]{1,0:T(8,128)S(1)} %fusion.22, f32[512,2048]{1,0:T(8,128)S(1)} %fusion.7, bf16[8192,2048]{1,0:T(8,128)(2,1)} %param.6, s32[]{:T(128)S(6)} %select_n.90, bf16[512,1024]{1,0:T(8,128)(2,1)S(1)} %collective-permute-done.10, ...), kind=kOutput, calls=%fused_computation.5 | convolution fusion | flops 2152202240 | bytes 23068676 | tf_op jit(solution)/shard_map/dot_general | solution.py:88
  131.1 11.8 %collective-permute-done.11 = bf16[512,768]{1,0:T(8,128)(2,1)S(1)} collective-permute-done((bf16[512,768]{1,0:T(8,128)(2,1)S(1)}, bf16[512,768]{1,0:T(8,128)(2,1)S(1)}, u32[]{:S(2)}, u32[]{:S(2)}) %collective-permute-start.11) | collective-permute-done | bytes 786464 | tf_op jit(solution)/shard_map/ppermute | solution.py:69
  142.9 3.7 %fusion.19 = f32[512,2048]{1,0:T(8,128)S(1)} fusion(f32[512,2048]{1,0:T(8,128)S(1)} %fusion.4, bf16[8192,2048]{1,0:T(8,128)(2,1)} %param.6, s32[]{:T(128)S(6)} %select_n.93, bf16[512,768]{1,0:T(8,128)(2,1)S(1)} %collective-permute-done.11, pred[]{:T(512)S(6)} %or.3, bf16[512,1024]{1,0:T(8,128)(2,1)S(1)} %collective-permute-done.9), kind=kOutput, calls=%fused_computation.17 | convolution fusion | flops 1612054528 | bytes 13107205 | tf_op jit(solution)/shard_map/dot_general | solution.py:88
  146.6 2.0 %add_convert_fusion = bf16[512,2048]{1,0:T(8,128)(2,1)} fusion(f32[512,2048]{1,0:T(8,128)S(1)} %fusion.19, bf16[256,2048]{1,0:T(8,128)(2,1)S(1)} %constant_dynamic-slice_fusion, bf16[512,256]{1,0:T(8,128)(2,1)S(1)} %collective-permute-done.12, pred[]{:T(512)S(6)} %or.3, bf16[512,1024]{1,0:T(8,128)(2,1)S(1)} %collective-permute-done.9), kind=kOutput, calls=%fused_computation.6 | convolution fusion | flops 539099136 | bytes 7864321 | tf_op jit(solution)/shard_map/dot_general | solution.py:126
  (29 shorter events, 12.4 us)
Async XLA Ops:
  0.0 106.9 %copy-start = (bf16[4,64,2048]{2,1,0:T(8,128)(2,1)S(1)}, bf16[4,64,2048]{2,1,0:T(8,128)(2,1)}, u32[]{:S(2)}) copy-start(bf16[4,64,2048]{2,1,0:T(8,128)(2,1)} %param.8) | copy-start | bytes 3145732
  0.0 17.7 %copy-start.1 = (bf16[2,256,2048]{2,1,0:T(8,128)(2,1)S(1)}, bf16[2,256,2048]{2,1,0:T(8,128)(2,1)}, u32[]{:S(2)}) copy-start(bf16[2,256,2048]{2,1,0:T(8,128)(2,1)} %param.5) | copy-start | bytes 6291460
  0.0 49.8 %collective-permute-start = (bf16[512,2048]{1,0:T(8,128)(2,1)}, bf16[512,2048]{1,0:T(8,128)(2,1)}, u32[]{:S(2)}, u32[]{:S(2)}) collective-permute-start(bf16[512,2048]{1,0:T(8,128)(2,1)} %bitcast.40), channel_id=1, source_target_pairs={{0,4},{12,8},{4,0},{8,12},{1,5},{13,9},{5,1},{9,13},{2,6},{14,10},... | collective-permute-start | bytes 6291464 | tf_op jit(solution)/shard_map/ppermute | solution.py:69
  11.8 37.8 %collective-permute-start.1 = (bf16[512,64]{0,1:T(8,128)(2,1)S(1)}, bf16[512,64]{0,1:T(8,128)(2,1)S(1)}, u32[]{:S(2)}, u32[]{:S(2)}) collective-permute-start(bf16[512,64]{0,1:T(8,128)(2,1)S(1)} %get-tuple-element.32), channel_id=1, source_target_pairs={{0,4},{12,8},{1,5},{13,9},{2,6},{14,10},{3,7},{15,11},{16,20},{28,... | collective-permute-start | bytes 196616 | tf_op jit(solution)/shard_map/ppermute | solution.py:69
  16.0 15.2 %collective-permute-start.2 = (bf16[512,1024]{1,0:T(8,128)(2,1)}, bf16[512,1024]{1,0:T(8,128)(2,1)}, u32[]{:S(2)}, u32[]{:S(2)}) collective-permute-start(bf16[512,1024]{1,0:T(8,128)(2,1)} %slice.62), channel_id=1, source_target_pairs={{4,8},{8,4},{5,9},{9,5},{6,10},{10,6},{7,11},{11,7},{20,24},{24,20... | collective-permute-start | bytes 3145736 | tf_op jit(solution)/shard_map/ppermute | solution.py:69
  18.9 33.7 %collective-permute-start.4 = (bf16[512,1024]{1,0:T(8,128)(2,1)}, bf16[512,1024]{1,0:T(8,128)(2,1)}, u32[]{:S(2)}, u32[]{:S(2)}) collective-permute-start(bf16[512,1024]{1,0:T(8,128)(2,1)} %slice.53), channel_id=1, source_target_pairs={{4,8},{8,4},{5,9},{9,5},{6,10},{10,6},{7,11},{11,7},{20,24},{24,20... | collective-permute-start | bytes 3145736 | tf_op jit(solution)/shard_map/ppermute | solution.py:69
  31.3 40.9 %collective-permute-start.3 = (bf16[512,1024]{1,0:T(8,128)(2,1)}, bf16[512,1024]{1,0:T(8,128)(2,1)S(1)}, u32[]{:S(2)}, u32[]{:S(2)}) collective-permute-start(bf16[512,1024]{1,0:T(8,128)(2,1)} %collective-permute-done.2), channel_id=1, source_target_pairs={{4,0},{8,12},{5,1},{9,13},{6,2},{10,14},{7,3},{11,15},{20,16},{24,... | collective-permute-start | bytes 3145736 | tf_op jit(solution)/shard_map/ppermute | solution.py:69
  51.1 12.4 %collective-permute-start.6 = (bf16[512,1024]{1,0:T(8,128)(2,1)S(1)}, bf16[512,1024]{1,0:T(8,128)(2,1)S(1)}, u32[]{:S(2)}, u32[]{:S(2)}) collective-permute-start(bf16[512,1024]{1,0:T(8,128)(2,1)S(1)} %slice.54), channel_id=1, source_target_pairs={{4,8},{8,4},{5,9},{9,5},{6,10},{10,6},{7,11},{11,7},{20,24},{24,20... | collective-permute-start | bytes 3145736 | tf_op jit(solution)/shard_map/ppermute | solution.py:69
  51.9 24.9 %collective-permute-start.7 = (bf16[2,512,64]{1,2,0:T(8,128)(2,1)S(1)}, bf16[2,512,64]{1,2,0:T(8,128)(2,1)S(1)}, u32[]{:S(2)}, u32[]{:S(2)}) collective-permute-start(bf16[2,512,64]{1,2,0:T(8,128)(2,1)S(1)} %pad_maximum_fusion), channel_id=1, source_target_pairs={{4,8},{8,4},{5,9},{9,5},{6,10},{10,6},{7,11},{11,7},{20,24},{24,20... | collective-permute-start | bytes 393224 | tf_op jit(solution)/shard_map/ppermute | solution.py:69
  52.6 41.3 %collective-permute-start.5 = (bf16[512,1024]{1,0:T(8,128)(2,1)}, bf16[512,1024]{1,0:T(8,128)(2,1)S(1)}, u32[]{:S(2)}, u32[]{:S(2)}) collective-permute-start(bf16[512,1024]{1,0:T(8,128)(2,1)} %collective-permute-done.4), channel_id=1, source_target_pairs={{4,0},{8,12},{5,1},{9,13},{6,2},{10,14},{7,3},{11,15},{20,16},{24,... | collective-permute-start | bytes 3145736 | tf_op jit(solution)/shard_map/ppermute | solution.py:69
  64.9 39.1 %collective-permute-start.9 = (bf16[512,1024]{1,0:T(8,128)(2,1)S(1)}, bf16[512,1024]{1,0:T(8,128)(2,1)S(1)}, u32[]{:S(2)}, u32[]{:S(2)}) collective-permute-start(bf16[512,1024]{1,0:T(8,128)(2,1)S(1)} %slice.57), channel_id=1, source_target_pairs={{4,8},{8,4},{5,9},{9,5},{6,10},{10,6},{7,11},{11,7},{20,24},{24,20... | collective-permute-start | bytes 3145736 | tf_op jit(solution)/shard_map/ppermute | solution.py:69
  76.8 27.2 %collective-permute-start.8 = (bf16[512,64]{0,1:T(8,128)(2,1)S(1)}, bf16[512,64]{0,1:T(8,128)(2,1)S(1)}, u32[]{:S(2)}, u32[]{:S(2)}) collective-permute-start(bf16[512,64]{0,1:T(8,128)(2,1)S(1)} %fusion.53), channel_id=1, source_target_pairs={{4,0},{8,12},{5,1},{9,13},{6,2},{10,14},{7,3},{11,15},{20,16},{24,... | collective-permute-start | bytes 196616 | tf_op jit(solution)/shard_map/ppermute | solution.py:69
  78.1 48.4 %collective-permute-start.10 = (bf16[512,1024]{1,0:T(8,128)(2,1)S(1)}, bf16[512,1024]{1,0:T(8,128)(2,1)S(1)}, u32[]{:S(2)}, u32[]{:S(2)}) collective-permute-start(bf16[512,1024]{1,0:T(8,128)(2,1)S(1)} %collective-permute-done.6), channel_id=1, source_target_pairs={{4,0},{8,12},{5,1},{9,13},{6,2},{10,14},{7,3},{11,15},{20,16},{24,... | collective-permute-start | bytes 3145736 | tf_op jit(solution)/shard_map/ppermute | solution.py:69
  104.1 38.8 %collective-permute-start.11 = (bf16[512,768]{1,0:T(8,128)(2,1)S(1)}, bf16[512,768]{1,0:T(8,128)(2,1)S(1)}, u32[]{:S(2)}, u32[]{:S(2)}) collective-permute-start(bf16[512,768]{1,0:T(8,128)(2,1)S(1)} %slice.60), channel_id=1, source_target_pairs={{4,0},{8,12},{5,1},{9,13},{6,2},{10,14},{7,3},{11,15},{20,16},{24,... | collective-permute-start | bytes 2359304 | tf_op jit(solution)/shard_map/ppermute | solution.py:69
  105.4 41.2 %collective-permute-start.12 = (bf16[512,256]{1,0:T(8,128)(2,1)S(1)}, bf16[512,256]{1,0:T(8,128)(2,1)S(1)}, u32[]{:S(2)}, u32[]{:S(2)}) collective-permute-start(bf16[512,256]{1,0:T(8,128)(2,1)S(1)} %slice.61), channel_id=1, source_target_pairs={{4,0},{8,12},{5,1},{9,13},{6,2},{10,14},{7,3},{11,15},{20,16},{24,... | collective-permute-start | bytes 786440 | tf_op jit(solution)/shard_map/ppermute | solution.py:69

commit v23 on v16

--- a/solution.py
+++ b/solution.py
@@ -112,15 +112,18 @@
     total = total + product(jnp.where(is_end, mid_out[0], mid[0]), far_mid)
 
     late = after(end[1], total)
+    begin = (after(far_end, late) + 1) * width - last
+    last_rows = lax.dynamic_slice_in_dim(base_weight, begin, last, axis=0)
     shrunk = after(shrunk, late)
     end_out += [send(late[:, : half - last], OUTWARD), send(late[:, half - last :], OUTWARD)]
     total = total + product(jnp.where(is_end, mid_out[1], mid[1]), far_mid, half)
     total = total + jnp.concatenate(expand(shrunk, expand_table, adapter_ids))
+    end_out[0], last_rows = lax.optimization_barrier((end_out[0], last_rows))
     total = total + product(jnp.where(is_end, end_out[0], end[0]), far_end)
     block = jnp.where(is_end, after(end_out[1], total), late[:, : half - last])
     total = total + product(block, far_end, half)
     block = jnp.where(is_end, after(end_out[2], total), late[:, half - last :])
-    total = total + product(block, far_end, width - last)
+    total = total + jnp.dot(block, last_rows, preferred_element_type=F32)
     return total.astype(BF16).reshape(chats, span, -1)
 
 

time: 144 us -> 147 us (1.021)
  waiting for transfers between devices: 66 us -> 61.2 us
  matrix products: 44.2 us -> 48.5 us
  local copies, waits for them, and re-layouts: 7.43 us -> 9.85 us
    ppermute x13, waiting for transfers between devices: 66 us -> 61.2 us  [send(): return lax.ppermute(block, 'tensor', pairs)]
    dot_general x7 -> x6, matrix products: 39.7 us -> 42 us  [product(): return jnp.dot(block, part, preferred_element_type=F32)]
    dot_general x0 -> x1, matrix products: none -> 2.04 us  [line(): total = total + jnp.dot(block, last_rows, preferred_element_type=F32)]
  transfers between devices with their start and end apart: 13 -> 13, of which waited for: 7 -> 6; matrix products, arithmetic and copies ran while one was open for 34% -> 39% of each run, Pallas kernels for 0% -> 0%
where the time goes in v23:
time: 147 us; the launch traced here: 146 us
  waiting for transfers between devices  61.2 us (42%)
  matrix products  48.5 us (33%)
  starting transfers between devices  21.9 us (15%)
  local copies, waits for them, and re-layouts  9.85 us (7%)
  between operations  4.37 us (3%)
    ppermute x13, waiting for transfers between devices, send(): return lax.ppermute(block, 'tensor', pairs)  61.2 us
    dot_general x6, matrix products, product(): return jnp.dot(block, part, preferred_element_type=F32)  42 us
    ppermute x13, starting transfers between devices, send(): return lax.ppermute(block, 'tensor', pairs)  21.9 us
    dot_general x2, matrix products, shrink(): jnp.dot(inputs[c], shrink_table[adapter_ids[c]], preferred_element_type=F32)  3.52 us
  transfers between devices with their start and end apart: 13, of which 6 were waited for; matrix products, arithmetic and copies ran while one was open for 39% of the time, Pallas kernels for 0%

profile of v23, /device:TPU:0, one launch (start us, length us, event | category | flops | bytes accessed | tf_op | source)
XLA Modules:
  0.0 145.9 jit_solution(3402971969642016891)
XLA Ops:
  0.0 3.0 %collective-permute-start = (bf16[512,2048]{1,0:T(8,128)(2,1)}, bf16[512,2048]{1,0:T(8,128)(2,1)}, u32[]{:S(2)}, u32[]{:S(2)}) collective-permute-start(bf16[512,2048]{1,0:T(8,128)(2,1)} %bitcast.40), channel_id=1, source_target_pairs={{0,4},{12,8},{4,0},{8,12},{1,5},{13,9},{5,1},{9,13},{2,6},{14,10},... | collective-permute-start | bytes 6291464 | tf_op jit(solution)/shard_map/ppermute | solution.py:69
  3.0 2.3 %slice.62 = bf16[512,1024]{1,0:T(8,128)(2,1)} slice(bf16[512,2048]{1,0:T(8,128)(2,1)} %bitcast.41), slice={[0:512], [0:1024]} | slice | bytes 2097152 | tf_op jit(solution)/shard_map/slice | solution.py:91
  5.3 1.6 %collective-permute-start.2 = (bf16[512,1024]{1,0:T(8,128)(2,1)}, bf16[512,1024]{1,0:T(8,128)(2,1)}, u32[]{:S(2)}, u32[]{:S(2)}) collective-permute-start(bf16[512,1024]{1,0:T(8,128)(2,1)} %slice.62), channel_id=1, source_target_pairs={{4,8},{8,4},{5,9},{9,5},{6,10},{10,6},{7,11},{11,7},{20,24},{24,20... | collective-permute-start | bytes 3145736 | tf_op jit(solution)/shard_map/ppermute | solution.py:69
  7.0 1.4 fusion.69
  12.5 1.8 %fusion.28 = bf16[256,64]{0,1:T(8,128)(2,1)S(1)} fusion(bf16[2,256,2048]{2,1,0:T(8,128)(2,1)} %param.5, bf16[4,2048,64]{1,2,0:T(8,128)(2,1)} %param.7, s32[]{:T(128)S(6)} %select_n.78), kind=kOutput, calls=%fused_computation.22 | convolution fusion | flops 67125248 | bytes 1343492 | tf_op jit(solution)/shard_map/dot_general | solution.py:12
  14.3 1.8 %fusion.27 = bf16[256,64]{0,1:T(8,128)(2,1)S(1)} fusion(bf16[2,256,2048]{2,1,0:T(8,128)(2,1)} %param.5, bf16[4,2048,64]{1,2,0:T(8,128)(2,1)} %param.7, s32[]{:T(128)S(6)} %select_n.77), kind=kOutput, calls=%fused_computation.21 | convolution fusion | flops 67125248 | bytes 1343492 | tf_op jit(solution)/shard_map/dot_general | solution.py:12
  17.2 1.7 %collective-permute-start.4 = (bf16[512,1024]{1,0:T(8,128)(2,1)}, bf16[512,1024]{1,0:T(8,128)(2,1)}, u32[]{:S(2)}, u32[]{:S(2)}) collective-permute-start(bf16[512,1024]{1,0:T(8,128)(2,1)} %slice.53), channel_id=1, source_target_pairs={{4,8},{8,4},{5,9},{9,5},{6,10},{10,6},{7,11},{11,7},{20,24},{24,20... | collective-permute-start | bytes 3145736 | tf_op jit(solution)/shard_map/ppermute | solution.py:69
  18.9 5.5 %collective-permute-start.1 = (bf16[512,64]{0,1:T(8,128)(2,1)S(1)}, bf16[512,64]{0,1:T(8,128)(2,1)S(1)}, u32[]{:S(2)}, u32[]{:S(2)}) collective-permute-start(bf16[512,64]{0,1:T(8,128)(2,1)S(1)} %get-tuple-element.36), channel_id=1, source_target_pairs={{0,4},{12,8},{1,5},{13,9},{2,6},{14,10},{3,7},{15,11},{16,20},{28,... | collective-permute-start | bytes 196616 | tf_op jit(solution)/shard_map/ppermute | solution.py:69
  24.4 9.4 %fusion.11 = f32[512,2048]{1,0:T(8,128)} fusion(bf16[512,2048]{1,0:T(8,128)(2,1)S(1)} %bitcast.43, bf16[8192,2048]{1,0:T(8,128)(2,1)} %param.6, s32[]{:T(128)S(6)} %select_n.76), kind=kOutput, calls=%fused_computation.13 | convolution fusion | flops 4294967296 | bytes 14680068 | tf_op jit(solution)/shard_map/dot_general | solution.py:88
  35.1 14.4 %collective-permute-done.1 = bf16[512,64]{0,1:T(8,128)(2,1)S(1)} collective-permute-done((bf16[512,64]{0,1:T(8,128)(2,1)S(1)}, bf16[512,64]{0,1:T(8,128)(2,1)S(1)}, u32[]{:S(2)}, u32[]{:S(2)}) %collective-permute-start.1) | collective-permute-done | bytes 65568 | tf_op jit(solution)/shard_map/ppermute | solution.py:69
  49.8 1.3 slice.54
  53.9 9.7 %fusion.16 = f32[512,2048]{1,0:T(8,128)S(1)} fusion(f32[512,2048]{1,0:T(8,128)} %fusion.11, bf16[512,2048]{1,0:T(8,128)(2,1)} %collective-permute-done, bf16[8192,2048]{1,0:T(8,128)(2,1)} %param.6, s32[]{:T(128)S(6)} %select_n.79), kind=kOutput, calls=%fused_computation.16 | convolution fusion | flops 4296015872 | bytes 18874372 | tf_op jit(solution)/shard_map/dot_general | solution.py:88
  63.6 1.3 slice.57
  65.6 6.6 %collective-permute-done.3 = bf16[512,1024]{1,0:T(8,128)(2,1)S(1)} collective-permute-done((bf16[512,1024]{1,0:T(8,128)(2,1)}, bf16[512,1024]{1,0:T(8,128)(2,1)S(1)}, u32[]{:S(2)}, u32[]{:S(2)}) %collective-permute-start.3) | collective-permute-done | bytes 1048608 | tf_op jit(solution)/shard_map/ppermute | solution.py:69
  72.2 6.5 %fusion.22 = f32[512,2048]{1,0:T(8,128)} fusion(f32[512,2048]{1,0:T(8,128)S(1)} %fusion.16, bf16[8192,2048]{1,0:T(8,128)(2,1)} %param.6, s32[]{:T(128)S(6)} %select_n.83, bf16[512,1024]{1,0:T(8,128)(2,1)S(1)} %collective-permute-done.3, bf16[512,1024]{1,0:T(8,128)(2,1)} %collective-permute-done.2, pred[]{:T(512)S(6)} %or.3), kind=kOutput, calls=%fused_computation.18 | convolution fusion | flops 2149056512 | bytes 14680069 | tf_op jit(solution)/shard_map/dot_general | solution.py:88
  81.4 13.3 %collective-permute-done.5 = bf16[512,1024]{1,0:T(8,128)(2,1)S(1)} collective-permute-done((bf16[512,1024]{1,0:T(8,128)(2,1)}, bf16[512,1024]{1,0:T(8,128)(2,1)S(1)}, u32[]{:S(2)}, u32[]{:S(2)}) %collective-permute-start.5) | collective-permute-done | bytes 1048608 | tf_op jit(solution)/shard_map/ppermute | solution.py:69
  94.7 6.5 %fusion.7 = f32[512,2048]{1,0:T(8,128)} fusion(bf16[8192,2048]{1,0:T(8,128)(2,1)} %param.6, s32[]{:T(128)S(6)} %select_n.85, bf16[512,1024]{1,0:T(8,128)(2,1)S(1)} %collective-permute-done.5, bf16[512,1024]{1,0:T(8,128)(2,1)} %collective-permute-done.4, pred[]{:T(512)S(6)} %or.3), kind=kOutput, calls=%fused_computation.9 | convolution fusion | flops 2148007936 | bytes 10485765 | tf_op jit(solution)/shard_map/dot_general | solution.py:88
  102.2 1.4 constant_dynamic-slice_fusion
  104.6 13.2 %collective-permute-done.10 = bf16[512,1024]{1,0:T(8,128)(2,1)} collective-permute-done((bf16[512,1024]{1,0:T(8,128)(2,1)S(1)}, bf16[512,1024]{1,0:T(8,128)(2,1)}, u32[]{:S(2)}, u32[]{:S(2)}) %collective-permute-start.10) | collective-permute-done | bytes 1048608 | tf_op jit(solution)/shard_map/ppermute | solution.py:69
  117.8 1.5 %collective-permute-start.11 = (bf16[512,768]{1,0:T(8,128)(2,1)S(1)}, bf16[512,768]{1,0:T(8,128)(2,1)S(1)}, u32[]{:S(2)}, u32[]{:S(2)}) collective-permute-start(bf16[512,768]{1,0:T(8,128)(2,1)S(1)} %copy-done.3), channel_id=1, source_target_pairs={{4,0},{8,12},{5,1},{9,13},{6,2},{10,14},{7,3},{11,15},{20,16},{24,... | collective-permute-start | bytes 2359304 | tf_op jit(solution)/shard_map/ppermute | solution.py:69
  120.6 6.2 %fusion.4 = f32[512,2048]{1,0:T(8,128)S(1)} fusion(f32[256,2048]{1,0:T(8,128)S(1)} %fusion.41, f32[256,2048]{1,0:T(8,128)S(1)} %fusion.43, f32[512,2048]{1,0:T(8,128)S(1)} %copy-done.1, f32[512,2048]{1,0:T(8,128)} %fusion.7, bf16[8192,2048]{1,0:T(8,128)(2,1)} %param.6, s32[]{:T(128)S(6)} %select_n.91, bf16[512,1024]{1,0:T(8,128)(2,1)} %collective-permute-done.10, ...), kind=kOutput, calls=%fused_computation.5 | convolution fusion | flops 2152202240 | bytes 23068676 | tf_op jit(solution)/shard_map/dot_general | solution.py:88
  126.8 13.3 %collective-permute-done.11 = bf16[512,768]{1,0:T(8,128)(2,1)S(1)} collective-permute-done((bf16[512,768]{1,0:T(8,128)(2,1)S(1)}, bf16[512,768]{1,0:T(8,128)(2,1)S(1)}, u32[]{:S(2)}, u32[]{:S(2)}) %collective-permute-start.11) | collective-permute-done | bytes 786464 | tf_op jit(solution)/shard_map/ppermute | solution.py:69
  140.2 3.7 %fusion.19 = f32[512,2048]{1,0:T(8,128)S(1)} fusion(f32[512,2048]{1,0:T(8,128)S(1)} %fusion.4, bf16[8192,2048]{1,0:T(8,128)(2,1)} %param.6, s32[]{:T(128)S(6)} %select_n.94, bf16[512,768]{1,0:T(8,128)(2,1)S(1)} %collective-permute-done.11, pred[]{:T(512)S(6)} %or.3, bf16[512,1024]{1,0:T(8,128)(2,1)S(1)} %collective-permute-done.9), kind=kOutput, calls=%fused_computation.17 | convolution fusion | flops 1612054528 | bytes 13107205 | tf_op jit(solution)/shard_map/dot_general | solution.py:88
  143.9 2.0 %add_convert_fusion = bf16[512,2048]{1,0:T(8,128)(2,1)} fusion(f32[512,2048]{1,0:T(8,128)S(1)} %fusion.19, bf16[256,2048]{1,0:T(8,128)(2,1)S(1)} %constant_dynamic-slice_fusion, bf16[512,256]{1,0:T(8,128)(2,1)S(1)} %collective-permute-done.12, pred[]{:T(512)S(6)} %or.3, bf16[512,1024]{1,0:T(8,128)(2,1)S(1)} %collective-permute-done.9), kind=kOutput, calls=%fused_computation.6 | convolution fusion | flops 539099136 | bytes 7864321 | tf_op jit(solution)/shard_map/dot_general | solution.py:126
  (33 shorter events, 12.0 us)
Async XLA Ops:
  0.0 103.7 %copy-start = (bf16[4,64,2048]{2,1,0:T(8,128)(2,1)S(1)}, bf16[4,64,2048]{2,1,0:T(8,128)(2,1)}, u32[]{:S(2)}) copy-start(bf16[4,64,2048]{2,1,0:T(8,128)(2,1)} %param.8) | copy-start | bytes 3145732
  0.0 16.0 %copy-start.2 = (bf16[2,256,2048]{2,1,0:T(8,128)(2,1)S(1)}, bf16[2,256,2048]{2,1,0:T(8,128)(2,1)}, u32[]{:S(2)}) copy-start(bf16[2,256,2048]{2,1,0:T(8,128)(2,1)} %param.5) | copy-start | bytes 6291460
  0.0 49.8 %collective-permute-start = (bf16[512,2048]{1,0:T(8,128)(2,1)}, bf16[512,2048]{1,0:T(8,128)(2,1)}, u32[]{:S(2)}, u32[]{:S(2)}) collective-permute-start(bf16[512,2048]{1,0:T(8,128)(2,1)} %bitcast.40), channel_id=1, source_target_pairs={{0,4},{12,8},{4,0},{8,12},{1,5},{13,9},{5,1},{9,13},{2,6},{14,10},... | collective-permute-start | bytes 6291464 | tf_op jit(solution)/shard_map/ppermute | solution.py:69
  5.3 28.5 %collective-permute-start.2 = (bf16[512,1024]{1,0:T(8,128)(2,1)}, bf16[512,1024]{1,0:T(8,128)(2,1)}, u32[]{:S(2)}, u32[]{:S(2)}) collective-permute-start(bf16[512,1024]{1,0:T(8,128)(2,1)} %slice.62), channel_id=1, source_target_pairs={{4,8},{8,4},{5,9},{9,5},{6,10},{10,6},{7,11},{11,7},{20,24},{24,20... | collective-permute-start | bytes 3145736 | tf_op jit(solution)/shard_map/ppermute | solution.py:69
  17.2 35.4 %collective-permute-start.4 = (bf16[512,1024]{1,0:T(8,128)(2,1)}, bf16[512,1024]{1,0:T(8,128)(2,1)}, u32[]{:S(2)}, u32[]{:S(2)}) collective-permute-start(bf16[512,1024]{1,0:T(8,128)(2,1)} %slice.53), channel_id=1, source_target_pairs={{4,8},{8,4},{5,9},{9,5},{6,10},{10,6},{7,11},{11,7},{20,24},{24,20... | collective-permute-start | bytes 3145736 | tf_op jit(solution)/shard_map/ppermute | solution.py:69
  18.9 30.7 %collective-permute-start.1 = (bf16[512,64]{0,1:T(8,128)(2,1)S(1)}, bf16[512,64]{0,1:T(8,128)(2,1)S(1)}, u32[]{:S(2)}, u32[]{:S(2)}) collective-permute-start(bf16[512,64]{0,1:T(8,128)(2,1)S(1)} %get-tuple-element.36), channel_id=1, source_target_pairs={{0,4},{12,8},{1,5},{13,9},{2,6},{14,10},{3,7},{15,11},{16,20},{28,... | collective-permute-start | bytes 196616 | tf_op jit(solution)/shard_map/ppermute | solution.py:69
  33.8 38.4 %collective-permute-start.3 = (bf16[512,1024]{1,0:T(8,128)(2,1)}, bf16[512,1024]{1,0:T(8,128)(2,1)S(1)}, u32[]{:S(2)}, u32[]{:S(2)}) collective-permute-start(bf16[512,1024]{1,0:T(8,128)(2,1)} %collective-permute-done.2), channel_id=1, source_target_pairs={{4,0},{8,12},{5,1},{9,13},{6,2},{10,14},{7,3},{11,15},{20,16},{24,... | collective-permute-start | bytes 3145736 | tf_op jit(solution)/shard_map/ppermute | solution.py:69
  51.1 12.4 %collective-permute-start.6 = (bf16[512,1024]{1,0:T(8,128)(2,1)S(1)}, bf16[512,1024]{1,0:T(8,128)(2,1)S(1)}, u32[]{:S(2)}, u32[]{:S(2)}) collective-permute-start(bf16[512,1024]{1,0:T(8,128)(2,1)S(1)} %slice.54), channel_id=1, source_target_pairs={{4,8},{8,4},{5,9},{9,5},{6,10},{10,6},{7,11},{11,7},{20,24},{24,20... | collective-permute-start | bytes 3145736 | tf_op jit(solution)/shard_map/ppermute | solution.py:69
  51.9 26.9 %collective-permute-start.7 = (bf16[2,512,64]{1,2,0:T(8,128)(2,1)S(1)}, bf16[2,512,64]{1,2,0:T(8,128)(2,1)S(1)}, u32[]{:S(2)}, u32[]{:S(2)}) collective-permute-start(bf16[2,512,64]{1,2,0:T(8,128)(2,1)S(1)} %pad_maximum_fusion), channel_id=1, source_target_pairs={{4,8},{8,4},{5,9},{9,5},{6,10},{10,6},{7,11},{11,7},{20,24},{24,20... | collective-permute-start | bytes 393224 | tf_op jit(solution)/shard_map/ppermute | solution.py:69
  52.6 42.1 %collective-permute-start.5 = (bf16[512,1024]{1,0:T(8,128)(2,1)}, bf16[512,1024]{1,0:T(8,128)(2,1)S(1)}, u32[]{:S(2)}, u32[]{:S(2)}) collective-permute-start(bf16[512,1024]{1,0:T(8,128)(2,1)} %collective-permute-done.4), channel_id=1, source_target_pairs={{4,0},{8,12},{5,1},{9,13},{6,2},{10,14},{7,3},{11,15},{20,16},{24,... | collective-permute-start | bytes 3145736 | tf_op jit(solution)/shard_map/ppermute | solution.py:69
  64.9 36.4 %collective-permute-start.9 = (bf16[512,1024]{1,0:T(8,128)(2,1)S(1)}, bf16[512,1024]{1,0:T(8,128)(2,1)S(1)}, u32[]{:S(2)}, u32[]{:S(2)}) collective-permute-start(bf16[512,1024]{1,0:T(8,128)(2,1)S(1)} %slice.57), channel_id=1, source_target_pairs={{4,8},{8,4},{5,9},{9,5},{6,10},{10,6},{7,11},{11,7},{20,24},{24,20... | collective-permute-start | bytes 3145736 | tf_op jit(solution)/shard_map/ppermute | solution.py:69
  78.8 22.4 %collective-permute-start.8 = (bf16[512,64]{0,1:T(8,128)(2,1)S(1)}, bf16[512,64]{0,1:T(8,128)(2,1)S(1)}, u32[]{:S(2)}, u32[]{:S(2)}) collective-permute-start(bf16[512,64]{0,1:T(8,128)(2,1)S(1)} %fusion.53), channel_id=1, source_target_pairs={{4,0},{8,12},{5,1},{9,13},{6,2},{10,14},{7,3},{11,15},{20,16},{24,... | collective-permute-start | bytes 196616 | tf_op jit(solution)/shard_map/ppermute | solution.py:69
  80.1 37.7 %collective-permute-start.10 = (bf16[512,1024]{1,0:T(8,128)(2,1)S(1)}, bf16[512,1024]{1,0:T(8,128)(2,1)}, u32[]{:S(2)}, u32[]{:S(2)}) collective-permute-start(bf16[512,1024]{1,0:T(8,128)(2,1)S(1)} %collective-permute-done.6), channel_id=1, source_target_pairs={{4,0},{8,12},{5,1},{9,13},{6,2},{10,14},{7,3},{11,15},{20,16},{24,... | collective-permute-start | bytes 3145736 | tf_op jit(solution)/shard_map/ppermute | solution.py:69
  102.2 15.6 %copy-start.3 = (bf16[512,768]{1,0:T(8,128)(2,1)S(1)}, bf16[512,768]{1,0:T(8,128)(2,1)}, u32[]{:S(2)}) copy-start(bf16[512,768]{1,0:T(8,128)(2,1)} %slice.60) | copy-start | bytes 2359300
  102.2 18.4 %copy-start.1 = (f32[512,2048]{1,0:T(8,128)S(1)}, f32[512,2048]{1,0:T(8,128)}, u32[]{:S(2)}) copy-start(f32[512,2048]{1,0:T(8,128)} %fusion.22) | copy-start | bytes 12582916
  117.8 22.4 %collective-permute-start.11 = (bf16[512,768]{1,0:T(8,128)(2,1)S(1)}, bf16[512,768]{1,0:T(8,128)(2,1)S(1)}, u32[]{:S(2)}, u32[]{:S(2)}) collective-permute-start(bf16[512,768]{1,0:T(8,128)(2,1)S(1)} %copy-done.3), channel_id=1, source_target_pairs={{4,0},{8,12},{5,1},{9,13},{6,2},{10,14},{7,3},{11,15},{20,16},{24,... | collective-permute-start | bytes 2359304 | tf_op jit(solution)/shard_map/ppermute | solution.py:69
  119.3 24.6 %collective-permute-start.12 = (bf16[512,256]{1,0:T(8,128)(2,1)S(1)}, bf16[512,256]{1,0:T(8,128)(2,1)S(1)}, u32[]{:S(2)}, u32[]{:S(2)}) collective-permute-start(bf16[512,256]{1,0:T(8,128)(2,1)S(1)} %slice.61), channel_id=1, source_target_pairs={{4,0},{8,12},{5,1},{9,13},{6,2},{10,14},{7,3},{11,15},{20,16},{24,... | collective-permute-start | bytes 786440 | tf_op jit(solution)/shard_map/ppermute | solution.py:69

commit v24 on v23

--- a/solution.py
+++ b/solution.py
@@ -114,11 +114,11 @@
     late = after(end[1], total)
     begin = (after(far_end, late) + 1) * width - last
     last_rows = lax.dynamic_slice_in_dim(base_weight, begin, last, axis=0)
+    late, last_rows = lax.optimization_barrier((late, last_rows))
     shrunk = after(shrunk, late)
     end_out += [send(late[:, : half - last], OUTWARD), send(late[:, half - last :], OUTWARD)]
     total = total + product(jnp.where(is_end, mid_out[1], mid[1]), far_mid, half)
     total = total + jnp.concatenate(expand(shrunk, expand_table, adapter_ids))
-    end_out[0], last_rows = lax.optimization_barrier((end_out[0], last_rows))
     total = total + product(jnp.where(is_end, end_out[0], end[0]), far_end)
     block = jnp.where(is_end, after(end_out[1], total), late[:, : half - last])
     total = total + product(block, far_end, half)

time: 147 us -> 143 us (0.973)
  waiting for transfers between devices: 61.2 us -> 59.4 us
    ppermute x13, waiting for transfers between devices: 61.2 us -> 59.4 us  [send(): return lax.ppermute(block, 'tensor', pairs)]
  transfers between devices with their start and end apart: 13 -> 13, of which waited for: 6 -> 7; matrix products, arithmetic and copies ran while one was open for 39% -> 38% of each run, Pallas kernels for 0% -> 0%
where the time goes in v24:
time: 143 us; the launch traced here: 142 us
  waiting for transfers between devices  59.4 us (42%)
  matrix products  47.2 us (33%)
  starting transfers between devices  22.2 us (16%)
  local copies, waits for them, and re-layouts  8.97 us (6%)
  between operations  4.37 us (3%)
    ppermute x13, waiting for transfers between devices, send(): return lax.ppermute(block, 'tensor', pairs)  59.4 us
    dot_general x6, matrix products, product(): return jnp.dot(block, part, preferred_element_type=F32)  40.8 us
    ppermute x13, starting transfers between devices, send(): return lax.ppermute(block, 'tensor', pairs)  22.2 us
    dot_general x2, matrix products, shrink(): jnp.dot(inputs[c], shrink_table[adapter_ids[c]], preferred_element_type=F32)  3.52 us
  transfers between devices with their start and end apart: 13, of which 7 were waited for; matrix products, arithmetic and copies ran while one was open for 38% of the time, Pallas kernels for 0%

profile of v24, /device:TPU:0, one launch (start us, length us, event | category | flops | bytes accessed | tf_op | source)
XLA Modules:
  0.0 142.2 jit_solution(12951162749364869431)
XLA Ops:
  0.0 3.0 %collective-permute-start = (bf16[512,2048]{1,0:T(8,128)(2,1)}, bf16[512,2048]{1,0:T(8,128)(2,1)}, u32[]{:S(2)}, u32[]{:S(2)}) collective-permute-start(bf16[512,2048]{1,0:T(8,128)(2,1)} %bitcast.40), channel_id=1, source_target_pairs={{0,4},{12,8},{4,0},{8,12},{1,5},{13,9},{5,1},{9,13},{2,6},{14,10},... | collective-permute-start | bytes 6291464 | tf_op jit(solution)/shard_map/ppermute | solution.py:69
  3.0 2.3 %slice.62 = bf16[512,1024]{1,0:T(8,128)(2,1)} slice(bf16[512,2048]{1,0:T(8,128)(2,1)} %bitcast.41), slice={[0:512], [0:1024]} | slice | bytes 2097152 | tf_op jit(solution)/shard_map/slice | solution.py:91
  5.3 1.6 %collective-permute-start.2 = (bf16[512,1024]{1,0:T(8,128)(2,1)}, bf16[512,1024]{1,0:T(8,128)(2,1)}, u32[]{:S(2)}, u32[]{:S(2)}) collective-permute-start(bf16[512,1024]{1,0:T(8,128)(2,1)} %slice.62), channel_id=1, source_target_pairs={{4,8},{8,4},{5,9},{9,5},{6,10},{10,6},{7,11},{11,7},{20,24},{24,20... | collective-permute-start | bytes 3145736 | tf_op jit(solution)/shard_map/ppermute | solution.py:69
  7.0 1.4 fusion.69
  12.5 1.8 %fusion.28 = bf16[256,64]{0,1:T(8,128)(2,1)S(1)} fusion(bf16[2,256,2048]{2,1,0:T(8,128)(2,1)} %param.5, bf16[4,2048,64]{1,2,0:T(8,128)(2,1)} %param.7, s32[]{:T(128)S(6)} %select_n.78), kind=kOutput, calls=%fused_computation.22 | convolution fusion | flops 67125248 | bytes 1343492 | tf_op jit(solution)/shard_map/dot_general | solution.py:12
  14.3 1.8 %fusion.27 = bf16[256,64]{0,1:T(8,128)(2,1)S(1)} fusion(bf16[2,256,2048]{2,1,0:T(8,128)(2,1)} %param.5, bf16[4,2048,64]{1,2,0:T(8,128)(2,1)} %param.7, s32[]{:T(128)S(6)} %select_n.77), kind=kOutput, calls=%fused_computation.21 | convolution fusion | flops 67125248 | bytes 1343492 | tf_op jit(solution)/shard_map/dot_general | solution.py:12
  17.2 1.7 %collective-permute-start.4 = (bf16[512,1024]{1,0:T(8,128)(2,1)}, bf16[512,1024]{1,0:T(8,128)(2,1)}, u32[]{:S(2)}, u32[]{:S(2)}) collective-permute-start(bf16[512,1024]{1,0:T(8,128)(2,1)} %slice.53), channel_id=1, source_target_pairs={{4,8},{8,4},{5,9},{9,5},{6,10},{10,6},{7,11},{11,7},{20,24},{24,20... | collective-permute-start | bytes 3145736 | tf_op jit(solution)/shard_map/ppermute | solution.py:69
  18.9 5.5 %collective-permute-start.1 = (bf16[512,64]{0,1:T(8,128)(2,1)S(1)}, bf16[512,64]{0,1:T(8,128)(2,1)S(1)}, u32[]{:S(2)}, u32[]{:S(2)}) collective-permute-start(bf16[512,64]{0,1:T(8,128)(2,1)S(1)} %get-tuple-element.36), channel_id=1, source_target_pairs={{0,4},{12,8},{1,5},{13,9},{2,6},{14,10},{3,7},{15,11},{16,20},{28,... | collective-permute-start | bytes 196616 | tf_op jit(solution)/shard_map/ppermute | solution.py:69
  24.4 9.4 %fusion.11 = f32[512,2048]{1,0:T(8,128)} fusion(bf16[512,2048]{1,0:T(8,128)(2,1)S(1)} %bitcast.43, bf16[8192,2048]{1,0:T(8,128)(2,1)} %param.6, s32[]{:T(128)S(6)} %select_n.76), kind=kOutput, calls=%fused_computation.13 | convolution fusion | flops 4294967296 | bytes 14680068 | tf_op jit(solution)/shard_map/dot_general | solution.py:88
  35.1 14.4 %collective-permute-done.1 = bf16[512,64]{0,1:T(8,128)(2,1)S(1)} collective-permute-done((bf16[512,64]{0,1:T(8,128)(2,1)S(1)}, bf16[512,64]{0,1:T(8,128)(2,1)S(1)}, u32[]{:S(2)}, u32[]{:S(2)}) %collective-permute-start.1) | collective-permute-done | bytes 65568 | tf_op jit(solution)/shard_map/ppermute | solution.py:69
  53.9 9.7 %fusion.16 = f32[512,2048]{1,0:T(8,128)S(1)} fusion(f32[512,2048]{1,0:T(8,128)} %fusion.11, bf16[512,2048]{1,0:T(8,128)(2,1)} %collective-permute-done, bf16[8192,2048]{1,0:T(8,128)(2,1)} %param.6, s32[]{:T(128)S(6)} %select_n.79), kind=kOutput, calls=%fused_computation.16 | convolution fusion | flops 4296015872 | bytes 18874372 | tf_op jit(solution)/shard_map/dot_general | solution.py:88
  63.6 1.3 slice.57
  65.6 6.6 %collective-permute-done.3 = bf16[512,1024]{1,0:T(8,128)(2,1)S(1)} collective-permute-done((bf16[512,1024]{1,0:T(8,128)(2,1)}, bf16[512,1024]{1,0:T(8,128)(2,1)S(1)}, u32[]{:S(2)}, u32[]{:S(2)}) %collective-permute-start.3) | collective-permute-done | bytes 1048608 | tf_op jit(solution)/shard_map/ppermute | solution.py:69
  72.2 6.5 %fusion.22 = f32[512,2048]{1,0:T(8,128)} fusion(f32[512,2048]{1,0:T(8,128)S(1)} %fusion.16, bf16[8192,2048]{1,0:T(8,128)(2,1)} %param.6, s32[]{:T(128)S(6)} %select_n.83, bf16[512,1024]{1,0:T(8,128)(2,1)S(1)} %collective-permute-done.3, bf16[512,1024]{1,0:T(8,128)(2,1)} %collective-permute-done.2, pred[]{:T(512)S(6)} %or.3), kind=kOutput, calls=%fused_computation.18 | convolution fusion | flops 2149056512 | bytes 14680069 | tf_op jit(solution)/shard_map/dot_general | solution.py:88
  81.4 13.3 %collective-permute-done.5 = bf16[512,1024]{1,0:T(8,128)(2,1)S(1)} collective-permute-done((bf16[512,1024]{1,0:T(8,128)(2,1)}, bf16[512,1024]{1,0:T(8,128)(2,1)S(1)}, u32[]{:S(2)}, u32[]{:S(2)}) %collective-permute-start.5) | collective-permute-done | bytes 1048608 | tf_op jit(solution)/shard_map/ppermute | solution.py:69
  94.7 6.5 %fusion.7 = f32[512,2048]{1,0:T(8,128)} fusion(bf16[8192,2048]{1,0:T(8,128)(2,1)} %param.6, s32[]{:T(128)S(6)} %select_n.85, bf16[512,1024]{1,0:T(8,128)(2,1)S(1)} %collective-permute-done.5, bf16[512,1024]{1,0:T(8,128)(2,1)} %collective-permute-done.4, pred[]{:T(512)S(6)} %or.3), kind=kOutput, calls=%fused_computation.9 | convolution fusion | flops 2148007936 | bytes 10485765 | tf_op jit(solution)/shard_map/dot_general | solution.py:88
  101.2 1.4 %constant_dynamic-slice_fusion = bf16[256,2048]{1,0:T(8,128)(2,1)S(1)} fusion(bf16[8192,2048]{1,0:T(8,128)(2,1)} %param.6, s32[]{:T(128)S(6)} %select_n.89), kind=kLoop, calls=%fused_computation.59 | loop fusion | bytes 2097156 | tf_op jit(solution)/shard_map/dynamic_slice | solution.py:116
  102.8 1.6 %collective-permute-start.11 = (bf16[512,768]{1,0:T(8,128)(2,1)S(1)}, bf16[512,768]{1,0:T(8,128)(2,1)S(1)}, u32[]{:S(2)}, u32[]{:S(2)}) collective-permute-start(bf16[512,768]{1,0:T(8,128)(2,1)S(1)} %slice.60), channel_id=1, source_target_pairs={{4,0},{8,12},{5,1},{9,13},{6,2},{10,14},{7,3},{11,15},{20,16},{24,... | collective-permute-start | bytes 2359304 | tf_op jit(solution)/shard_map/ppermute | solution.py:69
  104.4 1.5 %collective-permute-start.12 = (bf16[512,256]{1,0:T(8,128)(2,1)S(1)}, bf16[512,256]{1,0:T(8,128)(2,1)S(1)}, u32[]{:S(2)}, u32[]{:S(2)}) collective-permute-start(bf16[512,256]{1,0:T(8,128)(2,1)S(1)} %slice.61), channel_id=1, source_target_pairs={{4,0},{8,12},{5,1},{9,13},{6,2},{10,14},{7,3},{11,15},{20,16},{24,... | collective-permute-start | bytes 786440 | tf_op jit(solution)/shard_map/ppermute | solution.py:69
  106.8 12.6 %collective-permute-done.10 = bf16[512,1024]{1,0:T(8,128)(2,1)} collective-permute-done((bf16[512,1024]{1,0:T(8,128)(2,1)S(1)}, bf16[512,1024]{1,0:T(8,128)(2,1)}, u32[]{:S(2)}, u32[]{:S(2)}) %collective-permute-start.10) | collective-permute-done | bytes 1048608 | tf_op jit(solution)/shard_map/ppermute | solution.py:69
  119.3 5.0 %fusion.4 = f32[512,2048]{1,0:T(8,128)S(1)} fusion(f32[256,2048]{1,0:T(8,128)S(1)} %fusion.41, f32[256,2048]{1,0:T(8,128)S(1)} %fusion.43, f32[512,2048]{1,0:T(8,128)S(1)} %copy-done.1, f32[512,2048]{1,0:T(8,128)S(1)} %copy-done.2, bf16[8192,2048]{1,0:T(8,128)(2,1)} %param.6, s32[]{:T(128)S(6)} %select_n.91, bf16[512,1024]{1,0:T(8,128)(2,1)} %collective-permute-done.10, ...), kind=kOutput, calls=%fused_computation.5 | convolution fusion | flops 2152202240 | bytes 23068676 | tf_op jit(solution)/shard_map/dot_general | solution.py:88
  124.3 11.8 %collective-permute-done.11 = bf16[512,768]{1,0:T(8,128)(2,1)S(1)} collective-permute-done((bf16[512,768]{1,0:T(8,128)(2,1)S(1)}, bf16[512,768]{1,0:T(8,128)(2,1)S(1)}, u32[]{:S(2)}, u32[]{:S(2)}) %collective-permute-start.11) | collective-permute-done | bytes 786464 | tf_op jit(solution)/shard_map/ppermute | solution.py:69
  136.1 3.7 %fusion.19 = f32[512,2048]{1,0:T(8,128)S(1)} fusion(f32[512,2048]{1,0:T(8,128)S(1)} %fusion.4, bf16[8192,2048]{1,0:T(8,128)(2,1)} %param.6, s32[]{:T(128)S(6)} %select_n.94, bf16[512,768]{1,0:T(8,128)(2,1)S(1)} %collective-permute-done.11, pred[]{:T(512)S(6)} %or.3, bf16[512,1024]{1,0:T(8,128)(2,1)S(1)} %collective-permute-done.9), kind=kOutput, calls=%fused_computation.17 | convolution fusion | flops 1612054528 | bytes 13107205 | tf_op jit(solution)/shard_map/dot_general | solution.py:88
  140.2 2.0 %add_convert_fusion = bf16[512,2048]{1,0:T(8,128)(2,1)} fusion(f32[512,2048]{1,0:T(8,128)S(1)} %fusion.19, bf16[256,2048]{1,0:T(8,128)(2,1)S(1)} %constant_dynamic-slice_fusion, bf16[512,256]{1,0:T(8,128)(2,1)S(1)} %collective-permute-done.12, pred[]{:T(512)S(6)} %or.3, bf16[512,1024]{1,0:T(8,128)(2,1)S(1)} %collective-permute-done.9), kind=kOutput, calls=%fused_computation.6 | convolution fusion | flops 539099136 | bytes 7864321 | tf_op jit(solution)/shard_map/dot_general | solution.py:126
  (33 shorter events, 11.5 us)
Async XLA Ops:
  0.0 105.9 %copy-start = (bf16[4,64,2048]{2,1,0:T(8,128)(2,1)S(1)}, bf16[4,64,2048]{2,1,0:T(8,128)(2,1)}, u32[]{:S(2)}) copy-start(bf16[4,64,2048]{2,1,0:T(8,128)(2,1)} %param.8) | copy-start | bytes 3145732
  0.0 16.0 %copy-start.3 = (bf16[2,256,2048]{2,1,0:T(8,128)(2,1)S(1)}, bf16[2,256,2048]{2,1,0:T(8,128)(2,1)}, u32[]{:S(2)}) copy-start(bf16[2,256,2048]{2,1,0:T(8,128)(2,1)} %param.5) | copy-start | bytes 6291460
  0.0 49.8 %collective-permute-start = (bf16[512,2048]{1,0:T(8,128)(2,1)}, bf16[512,2048]{1,0:T(8,128)(2,1)}, u32[]{:S(2)}, u32[]{:S(2)}) collective-permute-start(bf16[512,2048]{1,0:T(8,128)(2,1)} %bitcast.40), channel_id=1, source_target_pairs={{0,4},{12,8},{4,0},{8,12},{1,5},{13,9},{5,1},{9,13},{2,6},{14,10},... | collective-permute-start | bytes 6291464 | tf_op jit(solution)/shard_map/ppermute | solution.py:69
  5.3 28.5 %collective-permute-start.2 = (bf16[512,1024]{1,0:T(8,128)(2,1)}, bf16[512,1024]{1,0:T(8,128)(2,1)}, u32[]{:S(2)}, u32[]{:S(2)}) collective-permute-start(bf16[512,1024]{1,0:T(8,128)(2,1)} %slice.62), channel_id=1, source_target_pairs={{4,8},{8,4},{5,9},{9,5},{6,10},{10,6},{7,11},{11,7},{20,24},{24,20... | collective-permute-start | bytes 3145736 | tf_op jit(solution)/shard_map/ppermute | solution.py:69
  17.2 35.4 %collective-permute-start.4 = (bf16[512,1024]{1,0:T(8,128)(2,1)}, bf16[512,1024]{1,0:T(8,128)(2,1)}, u32[]{:S(2)}, u32[]{:S(2)}) collective-permute-start(bf16[512,1024]{1,0:T(8,128)(2,1)} %slice.53), channel_id=1, source_target_pairs={{4,8},{8,4},{5,9},{9,5},{6,10},{10,6},{7,11},{11,7},{20,24},{24,20... | collective-permute-start | bytes 3145736 | tf_op jit(solution)/shard_map/ppermute | solution.py:69
  18.9 30.7 %collective-permute-start.1 = (bf16[512,64]{0,1:T(8,128)(2,1)S(1)}, bf16[512,64]{0,1:T(8,128)(2,1)S(1)}, u32[]{:S(2)}, u32[]{:S(2)}) collective-permute-start(bf16[512,64]{0,1:T(8,128)(2,1)S(1)} %get-tuple-element.36), channel_id=1, source_target_pairs={{0,4},{12,8},{1,5},{13,9},{2,6},{14,10},{3,7},{15,11},{16,20},{28,... | collective-permute-start | bytes 196616 | tf_op jit(solution)/shard_map/ppermute | solution.py:69
  33.8 38.4 %collective-permute-start.3 = (bf16[512,1024]{1,0:T(8,128)(2,1)}, bf16[512,1024]{1,0:T(8,128)(2,1)S(1)}, u32[]{:S(2)}, u32[]{:S(2)}) collective-permute-start(bf16[512,1024]{1,0:T(8,128)(2,1)} %collective-permute-done.2), channel_id=1, source_target_pairs={{4,0},{8,12},{5,1},{9,13},{6,2},{10,14},{7,3},{11,15},{20,16},{24,... | collective-permute-start | bytes 3145736 | tf_op jit(solution)/shard_map/ppermute | solution.py:69
  51.1 12.4 %collective-permute-start.6 = (bf16[512,1024]{1,0:T(8,128)(2,1)S(1)}, bf16[512,1024]{1,0:T(8,128)(2,1)S(1)}, u32[]{:S(2)}, u32[]{:S(2)}) collective-permute-start(bf16[512,1024]{1,0:T(8,128)(2,1)S(1)} %slice.54), channel_id=1, source_target_pairs={{4,8},{8,4},{5,9},{9,5},{6,10},{10,6},{7,11},{11,7},{20,24},{24,20... | collective-permute-start | bytes 3145736 | tf_op jit(solution)/shard_map/ppermute | solution.py:69
  51.9 26.9 %collective-permute-start.7 = (bf16[2,512,64]{1,2,0:T(8,128)(2,1)S(1)}, bf16[2,512,64]{1,2,0:T(8,128)(2,1)S(1)}, u32[]{:S(2)}, u32[]{:S(2)}) collective-permute-start(bf16[2,512,64]{1,2,0:T(8,128)(2,1)S(1)} %pad_maximum_fusion), channel_id=1, source_target_pairs={{4,8},{8,4},{5,9},{9,5},{6,10},{10,6},{7,11},{11,7},{20,24},{24,20... | collective-permute-start | bytes 393224 | tf_op jit(solution)/shard_map/ppermute | solution.py:69
  52.6 42.1 %collective-permute-start.5 = (bf16[512,1024]{1,0:T(8,128)(2,1)}, bf16[512,1024]{1,0:T(8,128)(2,1)S(1)}, u32[]{:S(2)}, u32[]{:S(2)}) collective-permute-start(bf16[512,1024]{1,0:T(8,128)(2,1)} %collective-permute-done.4), channel_id=1, source_target_pairs={{4,0},{8,12},{5,1},{9,13},{6,2},{10,14},{7,3},{11,15},{20,16},{24,... | collective-permute-start | bytes 3145736 | tf_op jit(solution)/shard_map/ppermute | solution.py:69
  64.9 36.4 %collective-permute-start.9 = (bf16[512,1024]{1,0:T(8,128)(2,1)S(1)}, bf16[512,1024]{1,0:T(8,128)(2,1)S(1)}, u32[]{:S(2)}, u32[]{:S(2)}) collective-permute-start(bf16[512,1024]{1,0:T(8,128)(2,1)S(1)} %slice.57), channel_id=1, source_target_pairs={{4,8},{8,4},{5,9},{9,5},{6,10},{10,6},{7,11},{11,7},{20,24},{24,20... | collective-permute-start | bytes 3145736 | tf_op jit(solution)/shard_map/ppermute | solution.py:69
  78.8 22.4 %collective-permute-start.8 = (bf16[512,64]{0,1:T(8,128)(2,1)S(1)}, bf16[512,64]{0,1:T(8,128)(2,1)S(1)}, u32[]{:S(2)}, u32[]{:S(2)}) collective-permute-start(bf16[512,64]{0,1:T(8,128)(2,1)S(1)} %fusion.53), channel_id=1, source_target_pairs={{4,0},{8,12},{5,1},{9,13},{6,2},{10,14},{7,3},{11,15},{20,16},{24,... | collective-permute-start | bytes 196616 | tf_op jit(solution)/shard_map/ppermute | solution.py:69
  80.1 39.2 %collective-permute-start.10 = (bf16[512,1024]{1,0:T(8,128)(2,1)S(1)}, bf16[512,1024]{1,0:T(8,128)(2,1)}, u32[]{:S(2)}, u32[]{:S(2)}) collective-permute-start(bf16[512,1024]{1,0:T(8,128)(2,1)S(1)} %collective-permute-done.6), channel_id=1, source_target_pairs={{4,0},{8,12},{5,1},{9,13},{6,2},{10,14},{7,3},{11,15},{20,16},{24,... | collective-permute-start | bytes 3145736 | tf_op jit(solution)/shard_map/ppermute | solution.py:69
  101.2 18.1 %copy-start.1 = (f32[512,2048]{1,0:T(8,128)S(1)}, f32[512,2048]{1,0:T(8,128)}, u32[]{:S(2)}) copy-start(f32[512,2048]{1,0:T(8,128)} %fusion.22) | copy-start | bytes 12582916
  101.2 18.1 %copy-start.2 = (f32[512,2048]{1,0:T(8,128)S(1)}, f32[512,2048]{1,0:T(8,128)}, u32[]{:S(2)}) copy-start(f32[512,2048]{1,0:T(8,128)} %fusion.7) | copy-start | bytes 12582916
  102.8 33.3 %collective-permute-start.11 = (bf16[512,768]{1,0:T(8,128)(2,1)S(1)}, bf16[512,768]{1,0:T(8,128)(2,1)S(1)}, u32[]{:S(2)}, u32[]{:S(2)}) collective-permute-start(bf16[512,768]{1,0:T(8,128)(2,1)S(1)} %slice.60), channel_id=1, source_target_pairs={{4,0},{8,12},{5,1},{9,13},{6,2},{10,14},{7,3},{11,15},{20,16},{24,... | collective-permute-start | bytes 2359304 | tf_op jit(solution)/shard_map/ppermute | solution.py:69
  104.4 35.8 %collective-permute-start.12 = (bf16[512,256]{1,0:T(8,128)(2,1)S(1)}, bf16[512,256]{1,0:T(8,128)(2,1)S(1)}, u32[]{:S(2)}, u32[]{:S(2)}) collective-permute-start(bf16[512,256]{1,0:T(8,128)(2,1)S(1)} %slice.61), channel_id=1, source_target_pairs={{4,0},{8,12},{5,1},{9,13},{6,2},{10,14},{7,3},{11,15},{20,16},{24,... | collective-permute-start | bytes 786440 | tf_op jit(solution)/shard_map/ppermute | solution.py:69

commit v25 on v24

--- a/solution.py
+++ b/solution.py
@@ -109,14 +109,14 @@
         partial.astype(F32) + mate_partial.astype(F32) + both[0].astype(F32) + both[1].astype(F32)
     ).astype(BF16)
     shrunk = jnp.where(is_end, send(shrunk, OUTWARD), shrunk)
-    total = total + product(jnp.where(is_end, mid_out[0], mid[0]), far_mid)
 
     late = after(end[1], total)
     begin = (after(far_end, late) + 1) * width - last
     last_rows = lax.dynamic_slice_in_dim(base_weight, begin, last, axis=0)
     late, last_rows = lax.optimization_barrier((late, last_rows))
-    shrunk = after(shrunk, late)
+    mid_out[0], shrunk = lax.optimization_barrier((mid_out[0], shrunk, late))[:2]
     end_out += [send(late[:, : half - last], OUTWARD), send(late[:, half - last :], OUTWARD)]
+    total = total + product(jnp.where(is_end, mid_out[0], mid[0]), far_mid)
     total = total + product(jnp.where(is_end, mid_out[1], mid[1]), far_mid, half)
     total = total + jnp.concatenate(expand(shrunk, expand_table, adapter_ids))
     total = total + product(jnp.where(is_end, end_out[0], end[0]), far_end)

time: 143 us -> 152 us (1.063)
  waiting for transfers between devices: 59.4 us -> 65.5 us
  matrix products: 47.2 us -> 51.7 us
    ppermute x13, waiting for transfers between devices: 59.4 us -> 65.5 us  [send(): return lax.ppermute(block, 'tensor', pairs)]
    dot_general x6, matrix products: 40.8 us -> 45.2 us  [product(): return jnp.dot(block, part, preferred_element_type=F32)]
  transfers between devices with their start and end apart: 13 -> 13, of which waited for: 7 -> 4; matrix products, arithmetic and copies ran while one was open for 38% -> 38% of each run, Pallas kernels for 0% -> 0%
where the time goes in v25:
time: 152 us
  waiting for transfers between devices  65.5 us (43%)
  matrix products  51.7 us (34%)
  starting transfers between devices  21.7 us (14%)
  local copies, waits for them, and re-layouts  8.75 us (6%)
  between operations  4.11 us (3%)
    ppermute x13, waiting for transfers between devices, send(): return lax.ppermute(block, 'tensor', pairs)  65.5 us
    dot_general x6, matrix products, product(): return jnp.dot(block, part, preferred_element_type=F32)  45.2 us
    ppermute x13, starting transfers between devices, send(): return lax.ppermute(block, 'tensor', pairs)  21.7 us
    dot_general x2, matrix products, shrink(): jnp.dot(inputs[c], shrink_table[adapter_ids[c]], preferred_element_type=F32)  3.52 us
  transfers between devices with their start and end apart: 13, of which 4 were waited for; matrix products, arithmetic and copies ran while one was open for 38% of the time, Pallas kernels for 0%

profile of v25, /device:TPU:0, one launch (start us, length us, event | category | flops | bytes accessed | tf_op | source)
XLA Modules:
  0.0 151.8 jit_solution(13620207503917444701)
XLA Ops:
  0.0 3.0 %collective-permute-start = (bf16[512,2048]{1,0:T(8,128)(2,1)}, bf16[512,2048]{1,0:T(8,128)(2,1)}, u32[]{:S(2)}, u32[]{:S(2)}) collective-permute-start(bf16[512,2048]{1,0:T(8,128)(2,1)} %bitcast.40), channel_id=1, source_target_pairs={{0,4},{12,8},{4,0},{8,12},{1,5},{13,9},{5,1},{9,13},{2,6},{14,10},... | collective-permute-start | bytes 6291464 | tf_op jit(solution)/shard_map/ppermute | solution.py:69
  3.0 2.3 %slice.62 = bf16[512,1024]{1,0:T(8,128)(2,1)} slice(bf16[512,2048]{1,0:T(8,128)(2,1)} %bitcast.41), slice={[0:512], [0:1024]} | slice | bytes 2097152 | tf_op jit(solution)/shard_map/slice | solution.py:91
  5.3 1.7 %collective-permute-start.2 = (bf16[512,1024]{1,0:T(8,128)(2,1)}, bf16[512,1024]{1,0:T(8,128)(2,1)}, u32[]{:S(2)}, u32[]{:S(2)}) collective-permute-start(bf16[512,1024]{1,0:T(8,128)(2,1)} %slice.62), channel_id=1, source_target_pairs={{4,8},{8,4},{5,9},{9,5},{6,10},{10,6},{7,11},{11,7},{20,24},{24,20... | collective-permute-start | bytes 3145736 | tf_op jit(solution)/shard_map/ppermute | solution.py:69
  7.0 1.4 fusion.66
  12.2 1.8 %fusion.25 = bf16[256,64]{0,1:T(8,128)(2,1)S(1)} fusion(bf16[2,256,2048]{2,1,0:T(8,128)(2,1)} %param.5, bf16[4,2048,64]{1,2,0:T(8,128)(2,1)} %param.7, s32[]{:T(128)S(6)} %select_n.78), kind=kOutput, calls=%fused_computation.21 | convolution fusion | flops 67125248 | bytes 1343492 | tf_op jit(solution)/shard_map/dot_general | solution.py:12
  14.0 1.8 %fusion.24 = bf16[256,64]{0,1:T(8,128)(2,1)S(1)} fusion(bf16[2,256,2048]{2,1,0:T(8,128)(2,1)} %param.5, bf16[4,2048,64]{1,2,0:T(8,128)(2,1)} %param.7, s32[]{:T(128)S(6)} %select_n.77), kind=kOutput, calls=%fused_computation.20 | convolution fusion | flops 67125248 | bytes 1343492 | tf_op jit(solution)/shard_map/dot_general | solution.py:12
  15.8 5.3 %collective-permute-start.1 = (bf16[512,64]{0,1:T(8,128)(2,1)S(1)}, bf16[512,64]{0,1:T(8,128)(2,1)S(1)}, u32[]{:S(2)}, u32[]{:S(2)}) collective-permute-start(bf16[512,64]{0,1:T(8,128)(2,1)S(1)} %get-tuple-element.38), channel_id=1, source_target_pairs={{0,4},{12,8},{1,5},{13,9},{2,6},{14,10},{3,7},{15,11},{16,20},{28,... | collective-permute-start | bytes 196616 | tf_op jit(solution)/shard_map/ppermute | solution.py:69
  22.2 1.6 %collective-permute-start.8 = (bf16[512,1024]{1,0:T(8,128)(2,1)}, bf16[512,1024]{1,0:T(8,128)(2,1)}, u32[]{:S(2)}, u32[]{:S(2)}) collective-permute-start(bf16[512,1024]{1,0:T(8,128)(2,1)} %slice.57), channel_id=1, source_target_pairs={{4,8},{8,4},{5,9},{9,5},{6,10},{10,6},{7,11},{11,7},{20,24},{24,20... | collective-permute-start | bytes 3145736 | tf_op jit(solution)/shard_map/ppermute | solution.py:69
  23.8 9.4 %fusion.11 = f32[512,2048]{1,0:T(8,128)} fusion(bf16[512,2048]{1,0:T(8,128)(2,1)S(1)} %bitcast.43, bf16[8192,2048]{1,0:T(8,128)(2,1)} %param.6, s32[]{:T(128)S(6)} %select_n.76), kind=kOutput, calls=%fused_computation.13 | convolution fusion | flops 4294967296 | bytes 14680068 | tf_op jit(solution)/shard_map/dot_general | solution.py:88
  33.2 16.4 %collective-permute-done.1 = bf16[512,64]{0,1:T(8,128)(2,1)S(1)} collective-permute-done((bf16[512,64]{0,1:T(8,128)(2,1)S(1)}, bf16[512,64]{0,1:T(8,128)(2,1)S(1)}, u32[]{:S(2)}, u32[]{:S(2)}) %collective-permute-start.1) | collective-permute-done | bytes 65568 | tf_op jit(solution)/shard_map/ppermute | solution.py:69
  49.5 1.3 slice.53
  51.6 1.3 collective-permute-start.3
  54.9 1.3 slice.56
  57.0 11.6 %fusion.16 = f32[512,2048]{1,0:T(8,128)} fusion(f32[512,2048]{1,0:T(8,128)} %fusion.11, bf16[512,2048]{1,0:T(8,128)(2,1)} %collective-permute-done, bf16[8192,2048]{1,0:T(8,128)(2,1)} %param.6, s32[]{:T(128)S(6)} %select_n.79), kind=kOutput, calls=%fused_computation.16 | convolution fusion | flops 4296015872 | bytes 18874372 | tf_op jit(solution)/shard_map/dot_general | solution.py:88
  71.2 33.6 %collective-permute-done.9 = bf16[512,1024]{1,0:T(8,128)(2,1)S(1)} collective-permute-done((bf16[512,1024]{1,0:T(8,128)(2,1)}, bf16[512,1024]{1,0:T(8,128)(2,1)S(1)}, u32[]{:S(2)}, u32[]{:S(2)}) %collective-permute-start.9) | collective-permute-done | bytes 1048608 | tf_op jit(solution)/shard_map/ppermute | solution.py:69
  104.9 6.5 %fusion.7 = f32[512,2048]{1,0:T(8,128)} fusion(bf16[8192,2048]{1,0:T(8,128)(2,1)} %param.6, s32[]{:T(128)S(6)} %select_n.89, bf16[512,1024]{1,0:T(8,128)(2,1)S(1)} %collective-permute-done.9, bf16[512,1024]{1,0:T(8,128)(2,1)} %collective-permute-done.8, pred[]{:T(512)S(6)} %or.3), kind=kOutput, calls=%fused_computation.9 | convolution fusion | flops 2148007936 | bytes 10485765 | tf_op jit(solution)/shard_map/dot_general | solution.py:88
  111.4 1.3 constant_dynamic-slice_fusion
  114.1 1.5 collective-permute-start.12
  116.6 7.0 %fusion.9 = f32[512,2048]{1,0:T(8,128)} fusion(bf16[8192,2048]{1,0:T(8,128)(2,1)} %param.6, s32[]{:T(128)S(6)} %select_n.87, bf16[512,1024]{1,0:T(8,128)(2,1)} %collective-permute-done.3, bf16[512,1024]{1,0:T(8,128)(2,1)} %collective-permute-done.2, pred[]{:T(512)S(6)} %or.3), kind=kOutput, calls=%fused_computation.11 | convolution fusion | flops 2148007936 | bytes 10485765 | tf_op jit(solution)/shard_map/dot_general | solution.py:88
  123.5 5.3 %collective-permute-done.10 = bf16[512,1024]{1,0:T(8,128)(2,1)} collective-permute-done((bf16[512,1024]{1,0:T(8,128)(2,1)S(1)}, bf16[512,1024]{1,0:T(8,128)(2,1)}, u32[]{:S(2)}, u32[]{:S(2)}) %collective-permute-start.10) | collective-permute-done | bytes 1048608 | tf_op jit(solution)/shard_map/ppermute | solution.py:69
  128.9 6.7 %fusion.4 = f32[512,2048]{1,0:T(8,128)S(1)} fusion(f32[256,2048]{1,0:T(8,128)S(1)} %fusion.38, f32[256,2048]{1,0:T(8,128)S(1)} %fusion.40, f32[512,2048]{1,0:T(8,128)S(1)} %copy-done.2, f32[512,2048]{1,0:T(8,128)S(1)} %copy-done.1, f32[512,2048]{1,0:T(8,128)} %fusion.9, bf16[8192,2048]{1,0:T(8,128)(2,1)} %param.6, s32[]{:T(128)S(6)} %select_n.91, ...), kind=kOutput, calls=%fused_computation.5 | convolution fusion | flops 2153250816 | bytes 27262980 | tf_op jit(solution)/shard_map/dot_general | solution.py:88
  135.5 10.2 %collective-permute-done.11 = bf16[512,768]{1,0:T(8,128)(2,1)} collective-permute-done((bf16[512,768]{1,0:T(8,128)(2,1)S(1)}, bf16[512,768]{1,0:T(8,128)(2,1)}, u32[]{:S(2)}, u32[]{:S(2)}) %collective-permute-start.11) | collective-permute-done | bytes 786464 | tf_op jit(solution)/shard_map/ppermute | solution.py:69
  145.7 4.0 %fusion.19 = f32[512,2048]{1,0:T(8,128)S(1)} fusion(f32[512,2048]{1,0:T(8,128)S(1)} %fusion.4, bf16[8192,2048]{1,0:T(8,128)(2,1)} %param.6, s32[]{:T(128)S(6)} %select_n.94, bf16[512,768]{1,0:T(8,128)(2,1)} %collective-permute-done.11, pred[]{:T(512)S(6)} %or.3, bf16[512,1024]{1,0:T(8,128)(2,1)S(1)} %collective-permute-done.7), kind=kOutput, calls=%fused_computation.17 | convolution fusion | flops 1612054528 | bytes 13107205 | tf_op jit(solution)/shard_map/dot_general | solution.py:88
  149.7 2.1 %add_convert_fusion = bf16[512,2048]{1,0:T(8,128)(2,1)} fusion(f32[512,2048]{1,0:T(8,128)S(1)} %fusion.19, bf16[256,2048]{1,0:T(8,128)(2,1)S(1)} %constant_dynamic-slice_fusion, bf16[512,256]{1,0:T(8,128)(2,1)S(1)} %collective-permute-done.12, pred[]{:T(512)S(6)} %or.3, bf16[512,1024]{1,0:T(8,128)(2,1)S(1)} %collective-permute-done.7), kind=kOutput, calls=%fused_computation.6 | convolution fusion | flops 539099136 | bytes 7864321 | tf_op jit(solution)/shard_map/dot_general | solution.py:126
  (33 shorter events, 9.5 us)
Async XLA Ops:
  0.0 115.6 %copy-start = (bf16[4,64,2048]{2,1,0:T(8,128)(2,1)S(1)}, bf16[4,64,2048]{2,1,0:T(8,128)(2,1)}, u32[]{:S(2)}) copy-start(bf16[4,64,2048]{2,1,0:T(8,128)(2,1)} %param.8) | copy-start | bytes 3145732
  0.0 21.1 %copy-start.3 = (bf16[2,256,2048]{2,1,0:T(8,128)(2,1)S(1)}, bf16[2,256,2048]{2,1,0:T(8,128)(2,1)}, u32[]{:S(2)}) copy-start(bf16[2,256,2048]{2,1,0:T(8,128)(2,1)} %param.5) | copy-start | bytes 6291460
  0.0 49.5 %collective-permute-start = (bf16[512,2048]{1,0:T(8,128)(2,1)}, bf16[512,2048]{1,0:T(8,128)(2,1)}, u32[]{:S(2)}, u32[]{:S(2)}) collective-permute-start(bf16[512,2048]{1,0:T(8,128)(2,1)} %bitcast.40), channel_id=1, source_target_pairs={{0,4},{12,8},{4,0},{8,12},{1,5},{13,9},{5,1},{9,13},{2,6},{14,10},... | collective-permute-start | bytes 6291464 | tf_op jit(solution)/shard_map/ppermute | solution.py:69
  5.3 44.2 %collective-permute-start.2 = (bf16[512,1024]{1,0:T(8,128)(2,1)}, bf16[512,1024]{1,0:T(8,128)(2,1)}, u32[]{:S(2)}, u32[]{:S(2)}) collective-permute-start(bf16[512,1024]{1,0:T(8,128)(2,1)} %slice.62), channel_id=1, source_target_pairs={{4,8},{8,4},{5,9},{9,5},{6,10},{10,6},{7,11},{11,7},{20,24},{24,20... | collective-permute-start | bytes 3145736 | tf_op jit(solution)/shard_map/ppermute | solution.py:69
  15.8 33.7 %collective-permute-start.1 = (bf16[512,64]{0,1:T(8,128)(2,1)S(1)}, bf16[512,64]{0,1:T(8,128)(2,1)S(1)}, u32[]{:S(2)}, u32[]{:S(2)}) collective-permute-start(bf16[512,64]{0,1:T(8,128)(2,1)S(1)} %get-tuple-element.38), channel_id=1, source_target_pairs={{0,4},{12,8},{1,5},{13,9},{2,6},{14,10},{3,7},{15,11},{16,20},{28,... | collective-permute-start | bytes 196616 | tf_op jit(solution)/shard_map/ppermute | solution.py:69
  22.2 31.4 %collective-permute-start.8 = (bf16[512,1024]{1,0:T(8,128)(2,1)}, bf16[512,1024]{1,0:T(8,128)(2,1)}, u32[]{:S(2)}, u32[]{:S(2)}) collective-permute-start(bf16[512,1024]{1,0:T(8,128)(2,1)} %slice.57), channel_id=1, source_target_pairs={{4,8},{8,4},{5,9},{9,5},{6,10},{10,6},{7,11},{11,7},{20,24},{24,20... | collective-permute-start | bytes 3145736 | tf_op jit(solution)/shard_map/ppermute | solution.py:69
  50.8 4.1 %collective-permute-start.4 = (bf16[512,1024]{1,0:T(8,128)(2,1)S(1)}, bf16[512,1024]{1,0:T(8,128)(2,1)S(1)}, u32[]{:S(2)}, u32[]{:S(2)}) collective-permute-start(bf16[512,1024]{1,0:T(8,128)(2,1)S(1)} %slice.53), channel_id=1, source_target_pairs={{4,8},{8,4},{5,9},{9,5},{6,10},{10,6},{7,11},{11,7},{20,24},{24,20... | collective-permute-start | bytes 3145736 | tf_op jit(solution)/shard_map/ppermute | solution.py:69
  51.6 61.2 %collective-permute-start.3 = (bf16[512,1024]{1,0:T(8,128)(2,1)}, bf16[512,1024]{1,0:T(8,128)(2,1)}, u32[]{:S(2)}, u32[]{:S(2)}) collective-permute-start(bf16[512,1024]{1,0:T(8,128)(2,1)} %collective-permute-done.2), channel_id=1, source_target_pairs={{4,0},{8,12},{5,1},{9,13},{6,2},{10,14},{7,3},{11,15},{20,16},{24,... | collective-permute-start | bytes 3145736 | tf_op jit(solution)/shard_map/ppermute | solution.py:69
  52.9 15.7 %collective-permute-start.5 = (bf16[2,512,64]{1,2,0:T(8,128)(2,1)S(1)}, bf16[2,512,64]{1,2,0:T(8,128)(2,1)S(1)}, u32[]{:S(2)}, u32[]{:S(2)}) collective-permute-start(bf16[2,512,64]{1,2,0:T(8,128)(2,1)S(1)} %pad_maximum_fusion), channel_id=1, source_target_pairs={{4,8},{8,4},{5,9},{9,5},{6,10},{10,6},{7,11},{11,7},{20,24},{24,20... | collective-permute-start | bytes 393224 | tf_op jit(solution)/shard_map/ppermute | solution.py:69
  53.6 51.3 %collective-permute-start.9 = (bf16[512,1024]{1,0:T(8,128)(2,1)}, bf16[512,1024]{1,0:T(8,128)(2,1)S(1)}, u32[]{:S(2)}, u32[]{:S(2)}) collective-permute-start(bf16[512,1024]{1,0:T(8,128)(2,1)} %collective-permute-done.8), channel_id=1, source_target_pairs={{4,0},{8,12},{5,1},{9,13},{6,2},{10,14},{7,3},{11,15},{20,16},{24,... | collective-permute-start | bytes 3145736 | tf_op jit(solution)/shard_map/ppermute | solution.py:69
  56.2 55.2 %collective-permute-start.7 = (bf16[512,1024]{1,0:T(8,128)(2,1)S(1)}, bf16[512,1024]{1,0:T(8,128)(2,1)S(1)}, u32[]{:S(2)}, u32[]{:S(2)}) collective-permute-start(bf16[512,1024]{1,0:T(8,128)(2,1)S(1)} %slice.56), channel_id=1, source_target_pairs={{4,8},{8,4},{5,9},{9,5},{6,10},{10,6},{7,11},{11,7},{20,24},{24,20... | collective-permute-start | bytes 3145736 | tf_op jit(solution)/shard_map/ppermute | solution.py:69
  68.6 42.7 %collective-permute-start.6 = (bf16[512,64]{0,1:T(8,128)(2,1)S(1)}, bf16[512,64]{0,1:T(8,128)(2,1)S(1)}, u32[]{:S(2)}, u32[]{:S(2)}) collective-permute-start(bf16[512,64]{0,1:T(8,128)(2,1)S(1)} %fusion.50), channel_id=1, source_target_pairs={{4,0},{8,12},{5,1},{9,13},{6,2},{10,14},{7,3},{11,15},{20,16},{24,... | collective-permute-start | bytes 196616 | tf_op jit(solution)/shard_map/ppermute | solution.py:69
  69.9 58.9 %collective-permute-start.10 = (bf16[512,1024]{1,0:T(8,128)(2,1)S(1)}, bf16[512,1024]{1,0:T(8,128)(2,1)}, u32[]{:S(2)}, u32[]{:S(2)}) collective-permute-start(bf16[512,1024]{1,0:T(8,128)(2,1)S(1)} %collective-permute-done.4), channel_id=1, source_target_pairs={{4,0},{8,12},{5,1},{9,13},{6,2},{10,14},{7,3},{11,15},{20,16},{24,... | collective-permute-start | bytes 3145736 | tf_op jit(solution)/shard_map/ppermute | solution.py:69
  112.8 32.9 %collective-permute-start.11 = (bf16[512,768]{1,0:T(8,128)(2,1)S(1)}, bf16[512,768]{1,0:T(8,128)(2,1)}, u32[]{:S(2)}, u32[]{:S(2)}) collective-permute-start(bf16[512,768]{1,0:T(8,128)(2,1)S(1)} %slice.60), channel_id=1, source_target_pairs={{4,0},{8,12},{5,1},{9,13},{6,2},{10,14},{7,3},{11,15},{20,16},{24,... | collective-permute-start | bytes 2359304 | tf_op jit(solution)/shard_map/ppermute | solution.py:69
  114.1 35.6 %collective-permute-start.12 = (bf16[512,256]{1,0:T(8,128)(2,1)S(1)}, bf16[512,256]{1,0:T(8,128)(2,1)S(1)}, u32[]{:S(2)}, u32[]{:S(2)}) collective-permute-start(bf16[512,256]{1,0:T(8,128)(2,1)S(1)} %slice.61), channel_id=1, source_target_pairs={{4,0},{8,12},{5,1},{9,13},{6,2},{10,14},{7,3},{11,15},{20,16},{24,... | collective-permute-start | bytes 786440 | tf_op jit(solution)/shard_map/ppermute | solution.py:69
  116.5 12.3 %copy-start.1 = (f32[512,2048]{1,0:T(8,128)S(1)}, f32[512,2048]{1,0:T(8,128)}, u32[]{:S(2)}) copy-start(f32[512,2048]{1,0:T(8,128)} %fusion.16) | copy-start | bytes 12582916
  116.5 12.3 %copy-start.2 = (f32[512,2048]{1,0:T(8,128)S(1)}, f32[512,2048]{1,0:T(8,128)}, u32[]{:S(2)}) copy-start(f32[512,2048]{1,0:T(8,128)} %fusion.7) | copy-start | bytes 12582916

commit v26 on v24

--- a/solution.py
+++ b/solution.py
@@ -108,7 +108,6 @@
     shrunk = (
         partial.astype(F32) + mate_partial.astype(F32) + both[0].astype(F32) + both[1].astype(F32)
     ).astype(BF16)
-    shrunk = jnp.where(is_end, send(shrunk, OUTWARD), shrunk)
     total = total + product(jnp.where(is_end, mid_out[0], mid[0]), far_mid)
 
     late = after(end[1], total)
@@ -116,6 +115,7 @@
     last_rows = lax.dynamic_slice_in_dim(base_weight, begin, last, axis=0)
     late, last_rows = lax.optimization_barrier((late, last_rows))
     shrunk = after(shrunk, late)
+    shrunk = jnp.where(is_end, send(shrunk, OUTWARD), shrunk)
     end_out += [send(late[:, : half - last], OUTWARD), send(late[:, half - last :], OUTWARD)]
     total = total + product(jnp.where(is_end, mid_out[1], mid[1]), far_mid, half)
     total = total + jnp.concatenate(expand(shrunk, expand_table, adapter_ids))

time: 143 us -> 176 us (1.23)
  waiting for transfers between devices: 59.4 us -> 93.3 us
  matrix products: 47.2 us -> 45.3 us
    ppermute x13, waiting for transfers between devices: 59.4 us -> 93.3 us  [send(): return lax.ppermute(block, 'tensor', pairs)]
    dot_general x6, matrix products: 40.8 us -> 38.8 us  [product(): return jnp.dot(block, part, preferred_element_type=F32)]
  transfers between devices with their start and end apart: 13 -> 13, of which waited for: 7 -> 5; matrix products, arithmetic and copies ran while one was open for 38% -> 29% of each run, Pallas kernels for 0% -> 0%
where the time goes in v26:
time: 176 us; the launch traced here: 175 us
  waiting for transfers between devices  93.3 us (53%)
  matrix products  45.3 us (26%)
  starting transfers between devices  23 us (13%)
  local copies, waits for them, and re-layouts  9.73 us (6%)
  between operations  3.94 us (2%)
    ppermute x13, waiting for transfers between devices, send(): return lax.ppermute(block, 'tensor', pairs)  93.3 us
    dot_general x6, matrix products, product(): return jnp.dot(block, part, preferred_element_type=F32)  38.8 us
    ppermute x13, starting transfers between devices, send(): return lax.ppermute(block, 'tensor', pairs)  23 us
    dot_general x2, matrix products, shrink(): jnp.dot(inputs[c], shrink_table[adapter_ids[c]], preferred_element_type=F32)  3.52 us
  transfers between devices with their start and end apart: 13, of which 5 were waited for; matrix products, arithmetic and copies ran while one was open for 29% of the time, Pallas kernels for 0%

profile of v26, /device:TPU:0, one launch (start us, length us, event | category | flops | bytes accessed | tf_op | source)
XLA Modules:
  0.0 175.3 jit_solution(25058849158954055)
XLA Ops:
  0.0 3.0 %collective-permute-start = (bf16[512,2048]{1,0:T(8,128)(2,1)}, bf16[512,2048]{1,0:T(8,128)(2,1)}, u32[]{:S(2)}, u32[]{:S(2)}) collective-permute-start(bf16[512,2048]{1,0:T(8,128)(2,1)} %bitcast.40), channel_id=1, source_target_pairs={{0,4},{12,8},{4,0},{8,12},{1,5},{13,9},{5,1},{9,13},{2,6},{14,10},... | collective-permute-start | bytes 6291464 | tf_op jit(solution)/shard_map/ppermute | solution.py:69
  3.0 2.3 %slice.62 = bf16[512,1024]{1,0:T(8,128)(2,1)} slice(bf16[512,2048]{1,0:T(8,128)(2,1)} %bitcast.41), slice={[0:512], [0:1024]} | slice | bytes 2097152 | tf_op jit(solution)/shard_map/slice | solution.py:91
  5.3 1.7 collective-permute-start.2
  7.0 1.4 fusion.69
  12.1 1.8 %fusion.28 = bf16[256,64]{0,1:T(8,128)(2,1)S(1)} fusion(bf16[2,256,2048]{2,1,0:T(8,128)(2,1)} %param.5, bf16[4,2048,64]{1,2,0:T(8,128)(2,1)} %param.7, s32[]{:T(128)S(6)} %select_n.78), kind=kOutput, calls=%fused_computation.22 | convolution fusion | flops 67125248 | bytes 1343492 | tf_op jit(solution)/shard_map/dot_general | solution.py:12
  13.8 1.8 %fusion.27 = bf16[256,64]{0,1:T(8,128)(2,1)S(1)} fusion(bf16[2,256,2048]{2,1,0:T(8,128)(2,1)} %param.5, bf16[4,2048,64]{1,2,0:T(8,128)(2,1)} %param.7, s32[]{:T(128)S(6)} %select_n.77), kind=kOutput, calls=%fused_computation.21 | convolution fusion | flops 67125248 | bytes 1343492 | tf_op jit(solution)/shard_map/dot_general | solution.py:12
  15.6 5.3 %collective-permute-start.1 = (bf16[512,64]{0,1:T(8,128)(2,1)S(1)}, bf16[512,64]{0,1:T(8,128)(2,1)S(1)}, u32[]{:S(2)}, u32[]{:S(2)}) collective-permute-start(bf16[512,64]{0,1:T(8,128)(2,1)S(1)} %get-tuple-element.36), channel_id=1, source_target_pairs={{0,4},{12,8},{1,5},{13,9},{2,6},{14,10},{3,7},{15,11},{16,20},{28,... | collective-permute-start | bytes 196616 | tf_op jit(solution)/shard_map/ppermute | solution.py:69
  20.9 9.4 %fusion.11 = f32[512,2048]{1,0:T(8,128)} fusion(bf16[512,2048]{1,0:T(8,128)(2,1)S(1)} %bitcast.42, bf16[8192,2048]{1,0:T(8,128)(2,1)} %param.6, s32[]{:T(128)S(6)} %select_n.76), kind=kOutput, calls=%fused_computation.13 | convolution fusion | flops 4294967296 | bytes 14680068 | tf_op jit(solution)/shard_map/dot_general | solution.py:88
  30.3 19.2 %collective-permute-done.1 = bf16[512,64]{0,1:T(8,128)(2,1)S(1)} collective-permute-done((bf16[512,64]{0,1:T(8,128)(2,1)S(1)}, bf16[512,64]{0,1:T(8,128)(2,1)S(1)}, u32[]{:S(2)}, u32[]{:S(2)}) %collective-permute-start.1) | collective-permute-done | bytes 65568 | tf_op jit(solution)/shard_map/ppermute | solution.py:69
  49.5 2.3 %slice.54 = bf16[512,1024]{1,0:T(8,128)(2,1)} slice(bf16[512,2048]{1,0:T(8,128)(2,1)} %collective-permute-done), slice={[0:512], [0:1024]} | slice | bytes 2097152 | tf_op jit(solution)/shard_map/slice | solution.py:100
  51.8 1.7 collective-permute-start.6
  54.6 1.7 collective-permute-start.4
  60.3 9.7 %fusion.16 = f32[512,2048]{1,0:T(8,128)S(1)} fusion(f32[512,2048]{1,0:T(8,128)} %fusion.11, bf16[512,2048]{1,0:T(8,128)(2,1)} %collective-permute-done, bf16[8192,2048]{1,0:T(8,128)(2,1)} %param.6, s32[]{:T(128)S(6)} %select_n.79), kind=kOutput, calls=%fused_computation.16 | convolution fusion | flops 4296015872 | bytes 18874372 | tf_op jit(solution)/shard_map/dot_general | solution.py:88
  71.3 13.2 %collective-permute-done.3 = bf16[512,1024]{1,0:T(8,128)(2,1)S(1)} collective-permute-done((bf16[512,1024]{1,0:T(8,128)(2,1)}, bf16[512,1024]{1,0:T(8,128)(2,1)S(1)}, u32[]{:S(2)}, u32[]{:S(2)}) %collective-permute-start.3) | collective-permute-done | bytes 1048608 | tf_op jit(solution)/shard_map/ppermute | solution.py:69
  84.5 6.5 %fusion.22 = f32[512,2048]{1,0:T(8,128)} fusion(f32[512,2048]{1,0:T(8,128)S(1)} %fusion.16, bf16[8192,2048]{1,0:T(8,128)(2,1)} %param.6, s32[]{:T(128)S(6)} %select_n.83, bf16[512,1024]{1,0:T(8,128)(2,1)S(1)} %collective-permute-done.3, bf16[512,1024]{1,0:T(8,128)(2,1)} %collective-permute-done.2, pred[]{:T(512)S(6)} %or.3), kind=kOutput, calls=%fused_computation.18 | convolution fusion | flops 2149056512 | bytes 14680069 | tf_op jit(solution)/shard_map/dot_general | solution.py:88
  95.0 35.7 %collective-permute-done.5 = bf16[512,1024]{1,0:T(8,128)(2,1)} collective-permute-done((bf16[512,1024]{1,0:T(8,128)(2,1)}, bf16[512,1024]{1,0:T(8,128)(2,1)}, u32[]{:S(2)}, u32[]{:S(2)}) %collective-permute-start.5) | collective-permute-done | bytes 1048608 | tf_op jit(solution)/shard_map/ppermute | solution.py:69
  130.7 4.9 %fusion.7 = f32[512,2048]{1,0:T(8,128)S(1)} fusion(bf16[8192,2048]{1,0:T(8,128)(2,1)} %param.6, s32[]{:T(128)S(6)} %select_n.85, bf16[512,1024]{1,0:T(8,128)(2,1)} %collective-permute-done.5, bf16[512,1024]{1,0:T(8,128)(2,1)} %collective-permute-done.4, pred[]{:T(512)S(6)} %or.3), kind=kOutput, calls=%fused_computation.9 | convolution fusion | flops 2148007936 | bytes 10485765 | tf_op jit(solution)/shard_map/dot_general | solution.py:88
  135.7 1.6 collective-permute-start.11
  137.3 1.5 collective-permute-start.12
  138.7 15.7 %collective-permute-done.9 = bf16[512,64]{0,1:T(8,128)(2,1)S(1)} collective-permute-done((bf16[512,64]{0,1:T(8,128)(2,1)S(1)}, bf16[512,64]{0,1:T(8,128)(2,1)S(1)}, u32[]{:S(2)}, u32[]{:S(2)}) %collective-permute-start.9) | collective-permute-done | bytes 65568 | tf_op jit(solution)/shard_map/ppermute | solution.py:69
  155.4 4.6 %fusion.4 = f32[512,2048]{1,0:T(8,128)S(1)} fusion(f32[256,2048]{1,0:T(8,128)S(1)} %fusion.41, f32[256,2048]{1,0:T(8,128)S(1)} %fusion.43, f32[512,2048]{1,0:T(8,128)S(1)} %copy-done.1, f32[512,2048]{1,0:T(8,128)S(1)} %fusion.7, bf16[8192,2048]{1,0:T(8,128)(2,1)} %param.6, s32[]{:T(128)S(6)} %select_n.91, bf16[512,1024]{1,0:T(8,128)(2,1)S(1)} %collective-permute-done.10, ...), kind=kOutput, calls=%fused_computation.5 | convolution fusion | flops 2152202240 | bytes 23068676 | tf_op jit(solution)/shard_map/dot_general | solution.py:88
  160.1 9.5 %collective-permute-done.11 = bf16[512,768]{1,0:T(8,128)(2,1)S(1)} collective-permute-done((bf16[512,768]{1,0:T(8,128)(2,1)S(1)}, bf16[512,768]{1,0:T(8,128)(2,1)S(1)}, u32[]{:S(2)}, u32[]{:S(2)}) %collective-permute-start.11) | collective-permute-done | bytes 786464 | tf_op jit(solution)/shard_map/ppermute | solution.py:69
  169.6 3.7 %fusion.19 = f32[512,2048]{1,0:T(8,128)S(1)} fusion(f32[512,2048]{1,0:T(8,128)S(1)} %fusion.4, bf16[8192,2048]{1,0:T(8,128)(2,1)} %param.6, s32[]{:T(128)S(6)} %select_n.94, bf16[512,768]{1,0:T(8,128)(2,1)S(1)} %collective-permute-done.11, pred[]{:T(512)S(6)} %or.3, bf16[512,1024]{1,0:T(8,128)(2,1)S(1)} %collective-permute-done.8), kind=kOutput, calls=%fused_computation.17 | convolution fusion | flops 1612054528 | bytes 13107205 | tf_op jit(solution)/shard_map/dot_general | solution.py:88
  173.3 2.0 %add_convert_fusion = bf16[512,2048]{1,0:T(8,128)(2,1)} fusion(f32[512,2048]{1,0:T(8,128)S(1)} %fusion.19, bf16[256,2048]{1,0:T(8,128)(2,1)S(1)} %constant_dynamic-slice_fusion, bf16[512,256]{1,0:T(8,128)(2,1)S(1)} %collective-permute-done.12, pred[]{:T(512)S(6)} %or.3, bf16[512,1024]{1,0:T(8,128)(2,1)S(1)} %collective-permute-done.8), kind=kOutput, calls=%fused_computation.6 | convolution fusion | flops 539099136 | bytes 7864321 | tf_op jit(solution)/shard_map/dot_general | solution.py:126
  (31 shorter events, 11.3 us)
Async XLA Ops:
  0.0 154.5 %copy-start = (bf16[4,64,2048]{2,1,0:T(8,128)(2,1)S(1)}, bf16[4,64,2048]{2,1,0:T(8,128)(2,1)}, u32[]{:S(2)}) copy-start(bf16[4,64,2048]{2,1,0:T(8,128)(2,1)} %param.8) | copy-start | bytes 3145732
  0.0 20.9 %copy-start.2 = (bf16[2,256,2048]{2,1,0:T(8,128)(2,1)S(1)}, bf16[2,256,2048]{2,1,0:T(8,128)(2,1)}, u32[]{:S(2)}) copy-start(bf16[2,256,2048]{2,1,0:T(8,128)(2,1)} %param.5) | copy-start | bytes 6291460
  0.0 49.5 %collective-permute-start = (bf16[512,2048]{1,0:T(8,128)(2,1)}, bf16[512,2048]{1,0:T(8,128)(2,1)}, u32[]{:S(2)}, u32[]{:S(2)}) collective-permute-start(bf16[512,2048]{1,0:T(8,128)(2,1)} %bitcast.40), channel_id=1, source_target_pairs={{0,4},{12,8},{4,0},{8,12},{1,5},{13,9},{5,1},{9,13},{2,6},{14,10},... | collective-permute-start | bytes 6291464 | tf_op jit(solution)/shard_map/ppermute | solution.py:69
  5.3 44.2 %collective-permute-start.2 = (bf16[512,1024]{1,0:T(8,128)(2,1)}, bf16[512,1024]{1,0:T(8,128)(2,1)}, u32[]{:S(2)}, u32[]{:S(2)}) collective-permute-start(bf16[512,1024]{1,0:T(8,128)(2,1)} %slice.62), channel_id=1, source_target_pairs={{4,8},{8,4},{5,9},{9,5},{6,10},{10,6},{7,11},{11,7},{20,24},{24,20... | collective-permute-start | bytes 3145736 | tf_op jit(solution)/shard_map/ppermute | solution.py:69
  15.6 33.9 %collective-permute-start.1 = (bf16[512,64]{0,1:T(8,128)(2,1)S(1)}, bf16[512,64]{0,1:T(8,128)(2,1)S(1)}, u32[]{:S(2)}, u32[]{:S(2)}) collective-permute-start(bf16[512,64]{0,1:T(8,128)(2,1)S(1)} %get-tuple-element.36), channel_id=1, source_target_pairs={{0,4},{12,8},{1,5},{13,9},{2,6},{14,10},{3,7},{15,11},{16,20},{28,... | collective-permute-start | bytes 196616 | tf_op jit(solution)/shard_map/ppermute | solution.py:69
  51.8 6.5 %collective-permute-start.6 = (bf16[512,1024]{1,0:T(8,128)(2,1)}, bf16[512,1024]{1,0:T(8,128)(2,1)}, u32[]{:S(2)}, u32[]{:S(2)}) collective-permute-start(bf16[512,1024]{1,0:T(8,128)(2,1)} %slice.54), channel_id=1, source_target_pairs={{4,8},{8,4},{5,9},{9,5},{6,10},{10,6},{7,11},{11,7},{20,24},{24,20... | collective-permute-start | bytes 3145736 | tf_op jit(solution)/shard_map/ppermute | solution.py:69
  54.6 15.4 %collective-permute-start.4 = (bf16[512,1024]{1,0:T(8,128)(2,1)}, bf16[512,1024]{1,0:T(8,128)(2,1)}, u32[]{:S(2)}, u32[]{:S(2)}) collective-permute-start(bf16[512,1024]{1,0:T(8,128)(2,1)} %slice.53), channel_id=1, source_target_pairs={{4,8},{8,4},{5,9},{9,5},{6,10},{10,6},{7,11},{11,7},{20,24},{24,20... | collective-permute-start | bytes 3145736 | tf_op jit(solution)/shard_map/ppermute | solution.py:69
  56.3 28.3 %collective-permute-start.3 = (bf16[512,1024]{1,0:T(8,128)(2,1)}, bf16[512,1024]{1,0:T(8,128)(2,1)S(1)}, u32[]{:S(2)}, u32[]{:S(2)}) collective-permute-start(bf16[512,1024]{1,0:T(8,128)(2,1)} %collective-permute-done.2), channel_id=1, source_target_pairs={{4,0},{8,12},{5,1},{9,13},{6,2},{10,14},{7,3},{11,15},{20,16},{24,... | collective-permute-start | bytes 3145736 | tf_op jit(solution)/shard_map/ppermute | solution.py:69
  57.6 33.5 %collective-permute-start.7 = (bf16[2,512,64]{1,2,0:T(8,128)(2,1)S(1)}, bf16[2,512,64]{1,2,0:T(8,128)(2,1)S(1)}, u32[]{:S(2)}, u32[]{:S(2)}) collective-permute-start(bf16[2,512,64]{1,2,0:T(8,128)(2,1)S(1)} %pad_maximum_fusion), channel_id=1, source_target_pairs={{4,8},{8,4},{5,9},{9,5},{6,10},{10,6},{7,11},{11,7},{20,24},{24,20... | collective-permute-start | bytes 393224 | tf_op jit(solution)/shard_map/ppermute | solution.py:69
  59.6 32.8 %collective-permute-start.8 = (bf16[512,1024]{1,0:T(8,128)(2,1)S(1)}, bf16[512,1024]{1,0:T(8,128)(2,1)S(1)}, u32[]{:S(2)}, u32[]{:S(2)}) collective-permute-start(bf16[512,1024]{1,0:T(8,128)(2,1)S(1)} %slice.57), channel_id=1, source_target_pairs={{4,8},{8,4},{5,9},{9,5},{6,10},{10,6},{7,11},{11,7},{20,24},{24,20... | collective-permute-start | bytes 3145736 | tf_op jit(solution)/shard_map/ppermute | solution.py:69
  70.0 60.7 %collective-permute-start.5 = (bf16[512,1024]{1,0:T(8,128)(2,1)}, bf16[512,1024]{1,0:T(8,128)(2,1)}, u32[]{:S(2)}, u32[]{:S(2)}) collective-permute-start(bf16[512,1024]{1,0:T(8,128)(2,1)} %collective-permute-done.4), channel_id=1, source_target_pairs={{4,0},{8,12},{5,1},{9,13},{6,2},{10,14},{7,3},{11,15},{20,16},{24,... | collective-permute-start | bytes 3145736 | tf_op jit(solution)/shard_map/ppermute | solution.py:69
  91.1 64.3 %collective-permute-start.10 = (bf16[512,1024]{1,0:T(8,128)(2,1)}, bf16[512,1024]{1,0:T(8,128)(2,1)S(1)}, u32[]{:S(2)}, u32[]{:S(2)}) collective-permute-start(bf16[512,1024]{1,0:T(8,128)(2,1)} %collective-permute-done.6), channel_id=1, source_target_pairs={{4,0},{8,12},{5,1},{9,13},{6,2},{10,14},{7,3},{11,15},{20,16},{24,... | collective-permute-start | bytes 3145736 | tf_op jit(solution)/shard_map/ppermute | solution.py:69
  93.7 60.7 %collective-permute-start.9 = (bf16[512,64]{0,1:T(8,128)(2,1)S(1)}, bf16[512,64]{0,1:T(8,128)(2,1)S(1)}, u32[]{:S(2)}, u32[]{:S(2)}) collective-permute-start(bf16[512,64]{0,1:T(8,128)(2,1)S(1)} %fusion.53), channel_id=1, source_target_pairs={{4,0},{8,12},{5,1},{9,13},{6,2},{10,14},{7,3},{11,15},{20,16},{24,... | collective-permute-start | bytes 196616 | tf_op jit(solution)/shard_map/ppermute | solution.py:69
  135.6 19.9 %copy-start.1 = (f32[512,2048]{1,0:T(8,128)S(1)}, f32[512,2048]{1,0:T(8,128)}, u32[]{:S(2)}) copy-start(f32[512,2048]{1,0:T(8,128)} %fusion.22) | copy-start | bytes 12582916
  135.7 33.9 %collective-permute-start.11 = (bf16[512,768]{1,0:T(8,128)(2,1)S(1)}, bf16[512,768]{1,0:T(8,128)(2,1)S(1)}, u32[]{:S(2)}, u32[]{:S(2)}) collective-permute-start(bf16[512,768]{1,0:T(8,128)(2,1)S(1)} %slice.60), channel_id=1, source_target_pairs={{4,0},{8,12},{5,1},{9,13},{6,2},{10,14},{7,3},{11,15},{20,16},{24,... | collective-permute-start | bytes 2359304 | tf_op jit(solution)/shard_map/ppermute | solution.py:69
  137.3 36.0 %collective-permute-start.12 = (bf16[512,256]{1,0:T(8,128)(2,1)S(1)}, bf16[512,256]{1,0:T(8,128)(2,1)S(1)}, u32[]{:S(2)}, u32[]{:S(2)}) collective-permute-start(bf16[512,256]{1,0:T(8,128)(2,1)S(1)} %slice.61), channel_id=1, source_target_pairs={{4,0},{8,12},{5,1},{9,13},{6,2},{10,14},{7,3},{11,15},{20,16},{24,... | collective-permute-start | bytes 786440 | tf_op jit(solution)/shard_map/ppermute | solution.py:69

commit v27 on v24

--- a/solution.py
+++ b/solution.py
@@ -81,7 +81,7 @@
     far_mid = jnp.where(here < 2, 2, 1)
     far_end = jnp.where(here < 2, 3, 0)
     own = inputs.reshape(rows, width)
-    half, last = width // 2, width // 8
+    half, cut, last = width // 2, width // 16 * 7, width // 8
 
     def product(block, owner, first=0):
         part = lax.dynamic_slice_in_dim(base_weight, owner * width + first, block.shape[1], axis=0)
@@ -97,9 +97,9 @@
     mid_out = [send(after(mid[0], total), OUTWARD)]
     mate, mate_partial = lax.optimization_barrier((mate, mate_partial, mid[0], total))[:2]
     both = send(jnp.stack([partial, mate_partial]), ACROSS)
-    first = mate[:, :half]
+    first = mate[:, :cut]
     end = [send(first, ACROSS)]
-    end.append(send(after(mate, end[0])[:, half:], ACROSS))
+    end.append(send(after(mate, end[0])[:, cut:], ACROSS))
     mid_out.append(send(after(mid[1], first), OUTWARD))
     total = total + product(mate, here ^ 1)
 
@@ -116,13 +116,13 @@
     last_rows = lax.dynamic_slice_in_dim(base_weight, begin, last, axis=0)
     late, last_rows = lax.optimization_barrier((late, last_rows))
     shrunk = after(shrunk, late)
-    end_out += [send(late[:, : half - last], OUTWARD), send(late[:, half - last :], OUTWARD)]
+    end_out += [send(late[:, :-last], OUTWARD), send(late[:, -last:], OUTWARD)]
     total = total + product(jnp.where(is_end, mid_out[1], mid[1]), far_mid, half)
     total = total + jnp.concatenate(expand(shrunk, expand_table, adapter_ids))
     total = total + product(jnp.where(is_end, end_out[0], end[0]), far_end)
-    block = jnp.where(is_end, after(end_out[1], total), late[:, : half - last])
-    total = total + product(block, far_end, half)
-    block = jnp.where(is_end, after(end_out[2], total), late[:, half - last :])
+    block = jnp.where(is_end, after(end_out[1], total), late[:, :-last])
+    total = total + product(block, far_end, cut)
+    block = jnp.where(is_end, after(end_out[2], total), late[:, -last:])
     total = total + jnp.dot(block, last_rows, preferred_element_type=F32)
     return total.astype(BF16).reshape(chats, span, -1)
 

time: 143 us -> 143 us (level)
  waiting for transfers between devices: 59.4 us -> 56 us
  local copies, waits for them, and re-layouts: 8.97 us -> 11.5 us
    ppermute x13, waiting for transfers between devices: 59.4 us -> 56 us  [send(): return lax.ppermute(block, 'tensor', pairs)]
  transfers between devices with their start and end apart: 13 -> 13, of which waited for: 7 -> 7; matrix products, arithmetic and copies ran while one was open for 38% -> 40% of each run, Pallas kernels for 0% -> 0%
where the time goes in v27:
time: 143 us; the launch traced here: 142 us
  waiting for transfers between devices  56 us (39%)
  matrix products  47.9 us (33%)
  starting transfers between devices  22.7 us (16%)
  local copies, waits for them, and re-layouts  11.5 us (8%)
  between operations  3.97 us (3%)
    ppermute x13, waiting for transfers between devices, send(): return lax.ppermute(block, 'tensor', pairs)  56 us
    dot_general x6, matrix products, product(): return jnp.dot(block, part, preferred_element_type=F32)  41.4 us
    ppermute x13, starting transfers between devices, send(): return lax.ppermute(block, 'tensor', pairs)  22.7 us
    dot_general x2, matrix products, shrink(): jnp.dot(inputs[c], shrink_table[adapter_ids[c]], preferred_element_type=F32)  3.52 us
    slice x2, local copies, waits for them, and re-layouts, line(): end_out += [send(late[:, :-last], OUTWARD), send(late[:, -last:], OUTWARD)]  2.92 us
  transfers between devices with their start and end apart: 13, of which 7 were waited for; matrix products, arithmetic and copies ran while one was open for 40% of the time, Pallas kernels for 0%

profile of v27, /device:TPU:0, one launch (start us, length us, event | category | flops | bytes accessed | tf_op | source)
XLA Modules:
  0.0 142.2 jit_solution(1229597644626799927)
XLA Ops:
  0.0 3.0 %collective-permute-start = (bf16[512,2048]{1,0:T(8,128)(2,1)}, bf16[512,2048]{1,0:T(8,128)(2,1)S(1)}, u32[]{:S(2)}, u32[]{:S(2)}) collective-permute-start(bf16[512,2048]{1,0:T(8,128)(2,1)} %bitcast.40), channel_id=1, source_target_pairs={{0,4},{12,8},{4,0},{8,12},{1,5},{13,9},{5,1},{9,13},{2,6},{14,10},... | collective-permute-start | bytes 6291464 | tf_op jit(solution)/shard_map/ppermute | solution.py:69
  3.0 2.3 %slice.62 = bf16[512,1024]{1,0:T(8,128)(2,1)} slice(bf16[512,2048]{1,0:T(8,128)(2,1)} %bitcast.41), slice={[0:512], [0:1024]} | slice | bytes 2097152 | tf_op jit(solution)/shard_map/slice | solution.py:91
  5.3 1.6 %collective-permute-start.2 = (bf16[512,1024]{1,0:T(8,128)(2,1)}, bf16[512,1024]{1,0:T(8,128)(2,1)}, u32[]{:S(2)}, u32[]{:S(2)}) collective-permute-start(bf16[512,1024]{1,0:T(8,128)(2,1)} %slice.62), channel_id=1, source_target_pairs={{4,8},{8,4},{5,9},{9,5},{6,10},{10,6},{7,11},{11,7},{20,24},{24,20... | collective-permute-start | bytes 3145736 | tf_op jit(solution)/shard_map/ppermute | solution.py:69
  12.0 1.8 %fusion.28 = bf16[256,64]{0,1:T(8,128)(2,1)S(1)} fusion(bf16[2,256,2048]{2,1,0:T(8,128)(2,1)} %param.5, bf16[4,2048,64]{1,2,0:T(8,128)(2,1)} %param.7, s32[]{:T(128)S(6)} %select_n.78), kind=kOutput, calls=%fused_computation.22 | convolution fusion | flops 67125248 | bytes 1343492 | tf_op jit(solution)/shard_map/dot_general | solution.py:12
  13.8 1.8 %fusion.27 = bf16[256,64]{0,1:T(8,128)(2,1)S(1)} fusion(bf16[2,256,2048]{2,1,0:T(8,128)(2,1)} %param.5, bf16[4,2048,64]{1,2,0:T(8,128)(2,1)} %param.7, s32[]{:T(128)S(6)} %select_n.77), kind=kOutput, calls=%fused_computation.21 | convolution fusion | flops 67125248 | bytes 1343492 | tf_op jit(solution)/shard_map/dot_general | solution.py:12
  15.6 5.3 %collective-permute-start.1 = (bf16[512,64]{0,1:T(8,128)(2,1)S(1)}, bf16[512,64]{0,1:T(8,128)(2,1)S(1)}, u32[]{:S(2)}, u32[]{:S(2)}) collective-permute-start(bf16[512,64]{0,1:T(8,128)(2,1)S(1)} %get-tuple-element.36), channel_id=1, source_target_pairs={{0,4},{12,8},{1,5},{13,9},{2,6},{14,10},{3,7},{15,11},{16,20},{28,... | collective-permute-start | bytes 196616 | tf_op jit(solution)/shard_map/ppermute | solution.py:69
  20.9 2.3 %slice.53 = bf16[512,1024]{1,0:T(8,128)(2,1)} slice(bf16[512,2048]{1,0:T(8,128)(2,1)} %bitcast.42), slice={[0:512], [1024:2048]} | slice | bytes 2097152 | tf_op jit(solution)/shard_map/slice | solution.py:93
  23.2 1.7 %collective-permute-start.4 = (bf16[512,1024]{1,0:T(8,128)(2,1)}, bf16[512,1024]{1,0:T(8,128)(2,1)}, u32[]{:S(2)}, u32[]{:S(2)}) collective-permute-start(bf16[512,1024]{1,0:T(8,128)(2,1)} %slice.53), channel_id=1, source_target_pairs={{4,8},{8,4},{5,9},{9,5},{6,10},{10,6},{7,11},{11,7},{20,24},{24,20... | collective-permute-start | bytes 3145736 | tf_op jit(solution)/shard_map/ppermute | solution.py:69
  24.9 10.5 %fusion.13 = f32[512,2048]{1,0:T(8,128)} fusion(bf16[512,2048]{1,0:T(8,128)(2,1)} %bitcast.43, bf16[8192,2048]{1,0:T(8,128)(2,1)} %param.6, s32[]{:T(128)S(6)} %select_n.76), kind=kOutput, calls=%fused_computation.15 | convolution fusion | flops 4294967296 | bytes 14680068 | tf_op jit(solution)/shard_map/dot_general | solution.py:88
  36.7 12.8 %collective-permute-done.1 = bf16[512,64]{0,1:T(8,128)(2,1)S(1)} collective-permute-done((bf16[512,64]{0,1:T(8,128)(2,1)S(1)}, bf16[512,64]{0,1:T(8,128)(2,1)S(1)}, u32[]{:S(2)}, u32[]{:S(2)}) %collective-permute-start.1) | collective-permute-done | bytes 65568 | tf_op jit(solution)/shard_map/ppermute | solution.py:69
  49.8 1.6 %collective-permute-start.6 = (bf16[512,896]{1,0:T(8,128)(2,1)S(1)}, bf16[512,896]{1,0:T(8,128)(2,1)}, u32[]{:S(2)}, u32[]{:S(2)}) collective-permute-start(bf16[512,896]{1,0:T(8,128)(2,1)S(1)} %slice.54), channel_id=1, source_target_pairs={{4,8},{8,4},{5,9},{9,5},{6,10},{10,6},{7,11},{11,7},{20,24},{24,20... | collective-permute-start | bytes 2752520 | tf_op jit(solution)/shard_map/ppermute | solution.py:69
  52.1 8.8 %fusion.16 = f32[512,2048]{1,0:T(8,128)S(1)} fusion(f32[512,2048]{1,0:T(8,128)} %fusion.13, bf16[512,2048]{1,0:T(8,128)(2,1)S(1)} %collective-permute-done, bf16[8192,2048]{1,0:T(8,128)(2,1)} %param.6, s32[]{:T(128)S(6)} %select_n.79), kind=kOutput, calls=%fused_computation.16 | convolution fusion | flops 4296015872 | bytes 18874372 | tf_op jit(solution)/shard_map/dot_general | solution.py:88
  64.4 7.8 %collective-permute-done.3 = bf16[512,1024]{1,0:T(8,128)(2,1)S(1)} collective-permute-done((bf16[512,1024]{1,0:T(8,128)(2,1)}, bf16[512,1024]{1,0:T(8,128)(2,1)S(1)}, u32[]{:S(2)}, u32[]{:S(2)}) %collective-permute-start.3) | collective-permute-done | bytes 1048608 | tf_op jit(solution)/shard_map/ppermute | solution.py:69
  72.2 6.5 %fusion.22 = f32[512,2048]{1,0:T(8,128)} fusion(f32[512,2048]{1,0:T(8,128)S(1)} %fusion.16, bf16[8192,2048]{1,0:T(8,128)(2,1)} %param.6, s32[]{:T(128)S(6)} %select_n.83, bf16[512,1024]{1,0:T(8,128)(2,1)S(1)} %collective-permute-done.3, bf16[512,1024]{1,0:T(8,128)(2,1)} %collective-permute-done.2, pred[]{:T(512)S(6)} %or.3), kind=kOutput, calls=%fused_computation.18 | convolution fusion | flops 2149056512 | bytes 14680069 | tf_op jit(solution)/shard_map/dot_general | solution.py:88
  80.0 16.0 %collective-permute-done.8 = bf16[512,64]{0,1:T(8,128)(2,1)S(1)} collective-permute-done((bf16[512,64]{0,1:T(8,128)(2,1)S(1)}, bf16[512,64]{0,1:T(8,128)(2,1)S(1)}, u32[]{:S(2)}, u32[]{:S(2)}) %collective-permute-start.8) | collective-permute-done | bytes 65568 | tf_op jit(solution)/shard_map/ppermute | solution.py:69
  96.1 6.5 %fusion.5 = f32[512,2048]{1,0:T(8,128)} fusion(bf16[8192,2048]{1,0:T(8,128)(2,1)} %param.6, s32[]{:T(128)S(6)} %select_n.85, bf16[512,1024]{1,0:T(8,128)(2,1)S(1)} %collective-permute-done.5, bf16[512,1024]{1,0:T(8,128)(2,1)} %collective-permute-done.4, pred[]{:T(512)S(6)} %or.3), kind=kOutput, calls=%fused_computation.7 | convolution fusion | flops 2148007936 | bytes 10485765 | tf_op jit(solution)/shard_map/dot_general | solution.py:88
  103.6 1.5 %constant_dynamic-slice_fusion = bf16[256,2048]{1,0:T(8,128)(2,1)S(1)} fusion(bf16[8192,2048]{1,0:T(8,128)(2,1)} %param.6, s32[]{:T(128)S(6)} %select_n.89), kind=kLoop, calls=%fused_computation.59 | loop fusion | bytes 2097156 | tf_op jit(solution)/shard_map/dynamic_slice | solution.py:116
  105.1 1.9 %slice.60 = bf16[512,896]{1,0:T(8,128)(2,1)S(1)} slice(bf16[512,1152]{1,0:T(8,128)(2,1)} %copy-done.3), slice={[0:512], [0:896]} | slice | bytes 1835008 | tf_op jit(solution)/shard_map/slice | solution.py:119
  110.3 1.6 %collective-permute-start.12 = (bf16[512,256]{1,0:T(8,128)(2,1)S(1)}, bf16[512,256]{1,0:T(8,128)(2,1)S(1)}, u32[]{:S(2)}, u32[]{:S(2)}) collective-permute-start(bf16[512,256]{1,0:T(8,128)(2,1)S(1)} %slice.61), channel_id=1, source_target_pairs={{4,0},{8,12},{5,1},{9,13},{6,2},{10,14},{7,3},{11,15},{20,16},{24,... | collective-permute-start | bytes 786440 | tf_op jit(solution)/shard_map/ppermute | solution.py:69
  111.9 3.9 %collective-permute-done.10 = bf16[512,896]{1,0:T(8,128)(2,1)} collective-permute-done((bf16[512,896]{1,0:T(8,128)(2,1)}, bf16[512,896]{1,0:T(8,128)(2,1)}, u32[]{:S(2)}, u32[]{:S(2)}) %collective-permute-start.10) | collective-permute-done | bytes 917536 | tf_op jit(solution)/shard_map/ppermute | solution.py:69
  115.8 4.8 %fusion.4 = f32[512,2048]{1,0:T(8,128)S(1)} fusion(f32[256,2048]{1,0:T(8,128)S(1)} %fusion.41, f32[256,2048]{1,0:T(8,128)S(1)} %fusion.43, f32[512,2048]{1,0:T(8,128)S(1)} %copy-done.1, f32[512,2048]{1,0:T(8,128)S(1)} %copy-done.2, bf16[8192,2048]{1,0:T(8,128)(2,1)} %param.6, s32[]{:T(128)S(6)} %select_n.92, bf16[512,896]{1,0:T(8,128)(2,1)} %collective-permute-done.10, ...), kind=kOutput, calls=%fused_computation.5 | convolution fusion | flops 1883701248 | bytes 22282244 | tf_op jit(solution)/shard_map/dot_general | solution.py:88
  120.6 14.8 %collective-permute-done.11 = bf16[512,896]{1,0:T(8,128)(2,1)S(1)} collective-permute-done((bf16[512,896]{1,0:T(8,128)(2,1)S(1)}, bf16[512,896]{1,0:T(8,128)(2,1)S(1)}, u32[]{:S(2)}, u32[]{:S(2)}) %collective-permute-start.11) | collective-permute-done | bytes 917536 | tf_op jit(solution)/shard_map/ppermute | solution.py:69
  135.4 4.4 %fusion.19 = f32[512,2048]{1,0:T(8,128)S(1)} fusion(f32[512,2048]{1,0:T(8,128)S(1)} %fusion.4, bf16[8192,2048]{1,0:T(8,128)(2,1)} %param.6, s32[]{:T(128)S(6)} %select_n.94, bf16[512,896]{1,0:T(8,128)(2,1)S(1)} %collective-permute-done.11, pred[]{:T(512)S(6)} %or.3, bf16[512,1152]{1,0:T(8,128)(2,1)S(1)} %copy-done.4), kind=kOutput, calls=%fused_computation.17 | convolution fusion | flops 1880555520 | bytes 13893637 | tf_op jit(solution)/shard_map/dot_general | solution.py:88
  140.2 2.0 %add_convert_fusion = bf16[512,2048]{1,0:T(8,128)(2,1)} fusion(f32[512,2048]{1,0:T(8,128)S(1)} %fusion.19, bf16[256,2048]{1,0:T(8,128)(2,1)S(1)} %constant_dynamic-slice_fusion, bf16[512,256]{1,0:T(8,128)(2,1)S(1)} %collective-permute-done.12, pred[]{:T(512)S(6)} %or.3, bf16[512,1152]{1,0:T(8,128)(2,1)S(1)} %copy-done.4), kind=kOutput, calls=%fused_computation.6 | convolution fusion | flops 539099136 | bytes 7864321 | tf_op jit(solution)/shard_map/dot_general | solution.py:126
  (35 shorter events, 12.9 us)
Async XLA Ops:
  0.0 108.4 %copy-start = (bf16[4,64,2048]{2,1,0:T(8,128)(2,1)S(1)}, bf16[4,64,2048]{2,1,0:T(8,128)(2,1)}, u32[]{:S(2)}) copy-start(bf16[4,64,2048]{2,1,0:T(8,128)(2,1)} %param.8) | copy-start | bytes 3145732
  0.0 49.7 %collective-permute-start = (bf16[512,2048]{1,0:T(8,128)(2,1)}, bf16[512,2048]{1,0:T(8,128)(2,1)S(1)}, u32[]{:S(2)}, u32[]{:S(2)}) collective-permute-start(bf16[512,2048]{1,0:T(8,128)(2,1)} %bitcast.40), channel_id=1, source_target_pairs={{0,4},{12,8},{4,0},{8,12},{1,5},{13,9},{5,1},{9,13},{2,6},{14,10},... | collective-permute-start | bytes 6291464 | tf_op jit(solution)/shard_map/ppermute | solution.py:69
  5.3 30.1 %collective-permute-start.2 = (bf16[512,1024]{1,0:T(8,128)(2,1)}, bf16[512,1024]{1,0:T(8,128)(2,1)}, u32[]{:S(2)}, u32[]{:S(2)}) collective-permute-start(bf16[512,1024]{1,0:T(8,128)(2,1)} %slice.62), channel_id=1, source_target_pairs={{4,8},{8,4},{5,9},{9,5},{6,10},{10,6},{7,11},{11,7},{20,24},{24,20... | collective-permute-start | bytes 3145736 | tf_op jit(solution)/shard_map/ppermute | solution.py:69
  15.6 34.0 %collective-permute-start.1 = (bf16[512,64]{0,1:T(8,128)(2,1)S(1)}, bf16[512,64]{0,1:T(8,128)(2,1)S(1)}, u32[]{:S(2)}, u32[]{:S(2)}) collective-permute-start(bf16[512,64]{0,1:T(8,128)(2,1)S(1)} %get-tuple-element.36), channel_id=1, source_target_pairs={{0,4},{12,8},{1,5},{13,9},{2,6},{14,10},{3,7},{15,11},{16,20},{28,... | collective-permute-start | bytes 196616 | tf_op jit(solution)/shard_map/ppermute | solution.py:69
  23.2 37.6 %collective-permute-start.4 = (bf16[512,1024]{1,0:T(8,128)(2,1)}, bf16[512,1024]{1,0:T(8,128)(2,1)}, u32[]{:S(2)}, u32[]{:S(2)}) collective-permute-start(bf16[512,1024]{1,0:T(8,128)(2,1)} %slice.53), channel_id=1, source_target_pairs={{4,8},{8,4},{5,9},{9,5},{6,10},{10,6},{7,11},{11,7},{20,24},{24,20... | collective-permute-start | bytes 3145736 | tf_op jit(solution)/shard_map/ppermute | solution.py:69
  35.4 36.8 %collective-permute-start.3 = (bf16[512,1024]{1,0:T(8,128)(2,1)}, bf16[512,1024]{1,0:T(8,128)(2,1)S(1)}, u32[]{:S(2)}, u32[]{:S(2)}) collective-permute-start(bf16[512,1024]{1,0:T(8,128)(2,1)} %collective-permute-done.2), channel_id=1, source_target_pairs={{4,0},{8,12},{5,1},{9,13},{6,2},{10,14},{7,3},{11,15},{20,16},{24,... | collective-permute-start | bytes 3145736 | tf_op jit(solution)/shard_map/ppermute | solution.py:69
  49.8 12.4 %collective-permute-start.6 = (bf16[512,896]{1,0:T(8,128)(2,1)S(1)}, bf16[512,896]{1,0:T(8,128)(2,1)}, u32[]{:S(2)}, u32[]{:S(2)}) collective-permute-start(bf16[512,896]{1,0:T(8,128)(2,1)S(1)} %slice.54), channel_id=1, source_target_pairs={{4,8},{8,4},{5,9},{9,5},{6,10},{10,6},{7,11},{11,7},{20,24},{24,20... | collective-permute-start | bytes 2752520 | tf_op jit(solution)/shard_map/ppermute | solution.py:69
  51.4 10.8 %collective-permute-start.7 = (bf16[2,512,64]{1,2,0:T(8,128)(2,1)S(1)}, bf16[2,512,64]{1,2,0:T(8,128)(2,1)S(1)}, u32[]{:S(2)}, u32[]{:S(2)}) collective-permute-start(bf16[2,512,64]{1,2,0:T(8,128)(2,1)S(1)} %pad_maximum_fusion), channel_id=1, source_target_pairs={{4,8},{8,4},{5,9},{9,5},{6,10},{10,6},{7,11},{11,7},{20,24},{24,20... | collective-permute-start | bytes 393224 | tf_op jit(solution)/shard_map/ppermute | solution.py:69
  60.8 35.2 %collective-permute-start.5 = (bf16[512,1024]{1,0:T(8,128)(2,1)}, bf16[512,1024]{1,0:T(8,128)(2,1)S(1)}, u32[]{:S(2)}, u32[]{:S(2)}) collective-permute-start(bf16[512,1024]{1,0:T(8,128)(2,1)} %collective-permute-done.4), channel_id=1, source_target_pairs={{4,0},{8,12},{5,1},{9,13},{6,2},{10,14},{7,3},{11,15},{20,16},{24,... | collective-permute-start | bytes 3145736 | tf_op jit(solution)/shard_map/ppermute | solution.py:69
  62.2 33.8 %collective-permute-start.8 = (bf16[512,64]{0,1:T(8,128)(2,1)S(1)}, bf16[512,64]{0,1:T(8,128)(2,1)S(1)}, u32[]{:S(2)}, u32[]{:S(2)}) collective-permute-start(bf16[512,64]{0,1:T(8,128)(2,1)S(1)} %fusion.53), channel_id=1, source_target_pairs={{4,0},{8,12},{5,1},{9,13},{6,2},{10,14},{7,3},{11,15},{20,16},{24,... | collective-permute-start | bytes 196616 | tf_op jit(solution)/shard_map/ppermute | solution.py:69
  63.6 39.0 %collective-permute-start.9 = (bf16[512,1152]{1,0:T(8,128)(2,1)S(1)}, bf16[512,1152]{1,0:T(8,128)(2,1)S(1)}, u32[]{:S(2)}, u32[]{:S(2)}) collective-permute-start(bf16[512,1152]{1,0:T(8,128)(2,1)S(1)} %slice.57), channel_id=1, source_target_pairs={{4,8},{8,4},{5,9},{9,5},{6,10},{10,6},{7,11},{11,7},{20,24},{24,20... | collective-permute-start | bytes 3538952 | tf_op jit(solution)/shard_map/ppermute | solution.py:69
  78.7 37.1 %collective-permute-start.10 = (bf16[512,896]{1,0:T(8,128)(2,1)}, bf16[512,896]{1,0:T(8,128)(2,1)}, u32[]{:S(2)}, u32[]{:S(2)}) collective-permute-start(bf16[512,896]{1,0:T(8,128)(2,1)} %collective-permute-done.6), channel_id=1, source_target_pairs={{4,0},{8,12},{5,1},{9,13},{6,2},{10,14},{7,3},{11,15},{20,16},{24,... | collective-permute-start | bytes 2752520 | tf_op jit(solution)/shard_map/ppermute | solution.py:69
  102.6 1.0 copy-start.3
  103.6 12.2 %copy-start.1 = (f32[512,2048]{1,0:T(8,128)S(1)}, f32[512,2048]{1,0:T(8,128)}, u32[]{:S(2)}) copy-start(f32[512,2048]{1,0:T(8,128)} %fusion.22) | copy-start | bytes 12582916
  103.6 12.2 %copy-start.2 = (f32[512,2048]{1,0:T(8,128)S(1)}, f32[512,2048]{1,0:T(8,128)}, u32[]{:S(2)}) copy-start(f32[512,2048]{1,0:T(8,128)} %fusion.5) | copy-start | bytes 12582916
  107.1 28.3 %collective-permute-start.11 = (bf16[512,896]{1,0:T(8,128)(2,1)S(1)}, bf16[512,896]{1,0:T(8,128)(2,1)S(1)}, u32[]{:S(2)}, u32[]{:S(2)}) collective-permute-start(bf16[512,896]{1,0:T(8,128)(2,1)S(1)} %slice.60), channel_id=1, source_target_pairs={{4,0},{8,12},{5,1},{9,13},{6,2},{10,14},{7,3},{11,15},{20,16},{24,... | collective-permute-start | bytes 2752520 | tf_op jit(solution)/shard_map/ppermute | solution.py:69
  110.3 25.1 %copy-start.4 = (bf16[512,1152]{1,0:T(8,128)(2,1)S(1)}, bf16[512,1152]{1,0:T(8,128)(2,1)}, u32[]{:S(2)}) copy-start(bf16[512,1152]{1,0:T(8,128)(2,1)} %copy-done.3) | copy-start | bytes 3538948
  110.3 29.9 %collective-permute-start.12 = (bf16[512,256]{1,0:T(8,128)(2,1)S(1)}, bf16[512,256]{1,0:T(8,128)(2,1)S(1)}, u32[]{:S(2)}, u32[]{:S(2)}) collective-permute-start(bf16[512,256]{1,0:T(8,128)(2,1)S(1)} %slice.61), channel_id=1, source_target_pairs={{4,0},{8,12},{5,1},{9,13},{6,2},{10,14},{7,3},{11,15},{20,16},{24,... | collective-permute-start | bytes 786440 | tf_op jit(solution)/shard_map/ppermute | solution.py:69

commit v28 on v26

--- a/solution.py
+++ b/solution.py
@@ -104,22 +104,23 @@
     total = total + product(mate, here ^ 1)
 
     end[0], both = lax.optimization_barrier((end[0], both, total))[:2]
-    end_out = [send(end[0], OUTWARD)]
     shrunk = (
         partial.astype(F32) + mate_partial.astype(F32) + both[0].astype(F32) + both[1].astype(F32)
     ).astype(BF16)
+    rider = shrunk.reshape(-1, half)
+    end_out = [send(jnp.concatenate([end[0], rider]), OUTWARD)]
     total = total + product(jnp.where(is_end, mid_out[0], mid[0]), far_mid)
 
     late = after(end[1], total)
     begin = (after(far_end, late) + 1) * width - last
     last_rows = lax.dynamic_slice_in_dim(base_weight, begin, last, axis=0)
     late, last_rows = lax.optimization_barrier((late, last_rows))
-    shrunk = after(shrunk, late)
-    shrunk = jnp.where(is_end, send(shrunk, OUTWARD), shrunk)
     end_out += [send(late[:, : half - last], OUTWARD), send(late[:, half - last :], OUTWARD)]
     total = total + product(jnp.where(is_end, mid_out[1], mid[1]), far_mid, half)
+    ridden = end_out[0]
+    shrunk = jnp.where(is_end, ridden[rows:].reshape(shrunk.shape), shrunk)
     total = total + jnp.concatenate(expand(shrunk, expand_table, adapter_ids))
-    total = total + product(jnp.where(is_end, end_out[0], end[0]), far_end)
+    total = total + product(jnp.where(is_end, ridden[:rows], end[0]), far_end)
     block = jnp.where(is_end, after(end_out[1], total), late[:, : half - last])
     total = total + product(block, far_end, half)
     block = jnp.where(is_end, after(end_out[2], total), late[:, half - last :])

time: 176 us -> 148 us (0.84)
  waiting for transfers between devices: 93.3 us -> 51.1 us
  matrix products: 45.3 us -> 53.7 us
  local copies, waits for them, and re-layouts: 9.73 us -> 17 us
  starting transfers between devices: 23 us -> 20.6 us
    ppermute x13 -> x12, waiting for transfers between devices: 93.3 us -> 51.1 us  [send(): return lax.ppermute(block, 'tensor', pairs)]
    dot_general x6, matrix products: 38.8 us -> 46.2 us  [product(): return jnp.dot(block, part, preferred_element_type=F32)]
    ppermute x13 -> x12, starting transfers between devices: 23 us -> 20.6 us  [send(): return lax.ppermute(block, 'tensor', pairs)]
    unnamed x6 -> x10, local copies, waits for them, and re-layouts: 0.01 us -> 2.24 us
    slice x1, local copies, waits for them, and re-layouts: 0.07 us -> 2.07 us  [line(): late[:, :half - last]]
  transfers between devices with their start and end apart: 13 -> 12, of which waited for: 5 -> 6; matrix products, arithmetic and copies ran while one was open for 29% -> 45% of each run, Pallas kernels for 0% -> 0%
where the time goes in v28:
time: 148 us; the launch traced here: 147 us
  matrix products  53.7 us (36%)
  waiting for transfers between devices  51.1 us (35%)
  starting transfers between devices  20.6 us (14%)
  local copies, waits for them, and re-layouts  17 us (11%)
  between operations  3.79 us (3%)
    ppermute x12, waiting for transfers between devices, send(): return lax.ppermute(block, 'tensor', pairs)  51.1 us
    dot_general x6, matrix products, product(): return jnp.dot(block, part, preferred_element_type=F32)  46.2 us
    ppermute x12, starting transfers between devices, send(): return lax.ppermute(block, 'tensor', pairs)  20.6 us
    dot_general x2, matrix products, shrink(): jnp.dot(inputs[c], shrink_table[adapter_ids[c]], preferred_element_type=F32)  3.52 us
    dot_general x1, matrix products, line(): total = total + jnp.dot(block, last_rows, preferred_element_type=F32)  3 us
  transfers between devices with their start and end apart: 12, of which 6 were waited for; matrix products, arithmetic and copies ran while one was open for 45% of the time, Pallas kernels for 0%

profile of v28, /device:TPU:0, one launch (start us, length us, event | category | flops | bytes accessed | tf_op | source)
XLA Modules:
  0.0 147.2 jit_solution(5647262050144396729)
XLA Ops:
  0.0 3.0 %collective-permute-start = (bf16[512,2048]{1,0:T(8,128)(2,1)}, bf16[512,2048]{1,0:T(8,128)(2,1)}, u32[]{:S(2)}, u32[]{:S(2)}) collective-permute-start(bf16[512,2048]{1,0:T(8,128)(2,1)} %bitcast.40), channel_id=1, source_target_pairs={{0,4},{12,8},{4,0},{8,12},{1,5},{13,9},{5,1},{9,13},{2,6},{14,10},... | collective-permute-start | bytes 6291464 | tf_op jit(solution)/shard_map/ppermute | solution.py:69
  3.0 2.3 %slice.70 = bf16[512,1024]{1,0:T(8,128)(2,1)} slice(bf16[512,2048]{1,0:T(8,128)(2,1)} %bitcast.41), slice={[0:512], [0:1024]} | slice | bytes 2097152 | tf_op jit(solution)/shard_map/slice | solution.py:91
  5.3 1.6 %collective-permute-start.2 = (bf16[512,1024]{1,0:T(8,128)(2,1)}, bf16[512,1024]{1,0:T(8,128)(2,1)}, u32[]{:S(2)}, u32[]{:S(2)}) collective-permute-start(bf16[512,1024]{1,0:T(8,128)(2,1)} %slice.70), channel_id=1, source_target_pairs={{4,8},{8,4},{5,9},{9,5},{6,10},{10,6},{7,11},{11,7},{20,24},{24,20... | collective-permute-start | bytes 3145736 | tf_op jit(solution)/shard_map/ppermute | solution.py:69
  7.0 1.3 fusion.68
  11.8 1.8 %fusion.27 = bf16[256,64]{0,1:T(8,128)(2,1)S(1)} fusion(bf16[2,256,2048]{2,1,0:T(8,128)(2,1)} %param.5, bf16[4,2048,64]{1,2,0:T(8,128)(2,1)} %param.7, s32[]{:T(128)S(6)} %select_n.77), kind=kOutput, calls=%fused_computation.22 | convolution fusion | flops 67125248 | bytes 1343492 | tf_op jit(solution)/shard_map/dot_general | solution.py:12
  13.6 1.8 %fusion.28 = bf16[256,64]{0,1:T(8,128)(2,1)S(1)} fusion(bf16[2,256,2048]{2,1,0:T(8,128)(2,1)} %param.5, bf16[4,2048,64]{1,2,0:T(8,128)(2,1)} %param.7, s32[]{:T(128)S(6)} %select_n.78), kind=kOutput, calls=%fused_computation.23 | convolution fusion | flops 67125248 | bytes 1343492 | tf_op jit(solution)/shard_map/dot_general | solution.py:12
  16.5 1.6 %collective-permute-start.4 = (bf16[512,1024]{1,0:T(8,128)(2,1)}, bf16[512,1024]{1,0:T(8,128)(2,1)}, u32[]{:S(2)}, u32[]{:S(2)}) collective-permute-start(bf16[512,1024]{1,0:T(8,128)(2,1)} %slice.59), channel_id=1, source_target_pairs={{4,8},{8,4},{5,9},{9,5},{6,10},{10,6},{7,11},{11,7},{20,24},{24,20... | collective-permute-start | bytes 3145736 | tf_op jit(solution)/shard_map/ppermute | solution.py:69
  18.2 5.6 %collective-permute-start.1 = (bf16[512,64]{0,1:T(8,128)(2,1)S(1)}, bf16[512,64]{0,1:T(8,128)(2,1)S(1)}, u32[]{:S(2)}, u32[]{:S(2)}) collective-permute-start(bf16[512,64]{0,1:T(8,128)(2,1)S(1)} %get-tuple-element.34), channel_id=1, source_target_pairs={{0,4},{12,8},{1,5},{13,9},{2,6},{14,10},{3,7},{15,11},{16,20},{28,... | collective-permute-start | bytes 196616 | tf_op jit(solution)/shard_map/ppermute | solution.py:69
  23.8 9.4 %fusion.11 = f32[512,2048]{1,0:T(8,128)} fusion(bf16[512,2048]{1,0:T(8,128)(2,1)S(1)} %bitcast.43, bf16[8192,2048]{1,0:T(8,128)(2,1)} %param.6, s32[]{:T(128)S(6)} %select_n.76), kind=kOutput, calls=%fused_computation.13 | convolution fusion | flops 4294967296 | bytes 14680068 | tf_op jit(solution)/shard_map/dot_general | solution.py:88
  34.5 15.0 %collective-permute-done.1 = bf16[512,64]{0,1:T(8,128)(2,1)S(1)} collective-permute-done((bf16[512,64]{0,1:T(8,128)(2,1)S(1)}, bf16[512,64]{0,1:T(8,128)(2,1)S(1)}, u32[]{:S(2)}, u32[]{:S(2)}) %collective-permute-start.1) | collective-permute-done | bytes 65568 | tf_op jit(solution)/shard_map/ppermute | solution.py:69
  50.5 1.3 slice.60
  53.9 11.7 %fusion.16 = f32[512,2048]{1,0:T(8,128)} fusion(f32[512,2048]{1,0:T(8,128)} %fusion.11, bf16[512,2048]{1,0:T(8,128)(2,1)} %collective-permute-done, bf16[8192,2048]{1,0:T(8,128)(2,1)} %param.6, s32[]{:T(128)S(6)} %select_n.79), kind=kOutput, calls=%fused_computation.16 | convolution fusion | flops 4296015872 | bytes 18874372 | tf_op jit(solution)/shard_map/dot_general | solution.py:88
  65.5 2.3 %slice.67 = bf16[512,1024]{1,0:T(8,128)(2,1)} slice(bf16[512,2048]{1,0:T(8,128)(2,1)} %collective-permute-done), slice={[0:512], [1024:2048]} | slice | bytes 2097152 | tf_op jit(solution)/shard_map/slice | solution.py:102
  72.3 8.1 %fusion.22 = f32[512,2048]{1,0:T(8,128)} fusion(f32[512,2048]{1,0:T(8,128)} %fusion.16, bf16[8192,2048]{1,0:T(8,128)(2,1)} %param.6, s32[]{:T(128)S(6)} %select_n.83, bf16[512,1024]{1,0:T(8,128)(2,1)} %collective-permute-done.3, bf16[512,1024]{1,0:T(8,128)(2,1)} %collective-permute-done.2, pred[]{:T(512)S(6)} %or.3), kind=kOutput, calls=%fused_computation.18 | convolution fusion | flops 2149056512 | bytes 14680069 | tf_op jit(solution)/shard_map/dot_general | solution.py:88
  80.4 14.4 %collective-permute-done.5 = bf16[512,1024]{1,0:T(8,128)(2,1)} collective-permute-done((bf16[512,1024]{1,0:T(8,128)(2,1)}, bf16[512,1024]{1,0:T(8,128)(2,1)}, u32[]{:S(2)}, u32[]{:S(2)}) %collective-permute-start.5) | collective-permute-done | bytes 1048608 | tf_op jit(solution)/shard_map/ppermute | solution.py:69
  94.8 6.8 %fusion.7 = f32[512,2048]{1,0:T(8,128)} fusion(bf16[8192,2048]{1,0:T(8,128)(2,1)} %param.6, s32[]{:T(128)S(6)} %select_n.85, bf16[512,1024]{1,0:T(8,128)(2,1)} %collective-permute-done.5, bf16[512,1024]{1,0:T(8,128)(2,1)} %collective-permute-done.4, pred[]{:T(512)S(6)} %or.3), kind=kOutput, calls=%fused_computation.9 | convolution fusion | flops 2148007936 | bytes 10485765 | tf_op jit(solution)/shard_map/dot_general | solution.py:88
  103.9 1.7 %slice.69 = bf16[512,256]{1,0:T(8,128)(2,1)} slice(bf16[512,1024]{1,0:T(8,128)(2,1)} %copy-done.2), slice={[0:512], [768:1024]} | slice | bytes 524288 | tf_op jit(solution)/shard_map/slice | solution.py:118
  105.6 2.1 %slice.68 = bf16[512,768]{1,0:T(8,128)(2,1)} slice(bf16[512,1024]{1,0:T(8,128)(2,1)} %copy-done.2), slice={[0:512], [0:768]} | slice | bytes 1572864 | tf_op jit(solution)/shard_map/slice | solution.py:118
  108.9 1.5 %collective-permute-start.10 = (bf16[512,768]{1,0:T(8,128)(2,1)}, bf16[512,768]{1,0:T(8,128)(2,1)}, u32[]{:S(2)}, u32[]{:S(2)}) collective-permute-start(bf16[512,768]{1,0:T(8,128)(2,1)} %slice.68), channel_id=1, source_target_pairs={{4,0},{8,12},{5,1},{9,13},{6,2},{10,14},{7,3},{11,15},{20,16},{24,... | collective-permute-start | bytes 2359304 | tf_op jit(solution)/shard_map/ppermute | solution.py:69
  110.4 8.2 %collective-permute-done.8 = bf16[544,1024]{1,0:T(8,128)(2,1)} collective-permute-done((bf16[544,1024]{1,0:T(8,128)(2,1)}, bf16[544,1024]{1,0:T(8,128)(2,1)}, u32[]{:S(2)}, u32[]{:S(2)}) %collective-permute-start.8) | collective-permute-done | bytes 1114144 | tf_op jit(solution)/shard_map/ppermute | solution.py:69
  121.9 6.3 %fusion.4 = f32[512,2048]{1,0:T(8,128)S(1)} fusion(f32[256,2048]{1,0:T(8,128)S(1)} %fusion.40, f32[256,2048]{1,0:T(8,128)S(1)} %fusion.42, f32[512,2048]{1,0:T(8,128)S(1)} %copy-done.1, f32[512,2048]{1,0:T(8,128)} %fusion.7, bf16[8192,2048]{1,0:T(8,128)(2,1)} %param.6, s32[]{:T(128)S(6)} %select_n.90, bf16[512,1024]{1,0:T(8,128)(2,1)S(1)} %collective-permute-done.6, ...), kind=kOutput, calls=%fused_computation.5 | convolution fusion | flops 2152202240 | bytes 23068676 | tf_op jit(solution)/shard_map/dot_general | solution.py:88
  128.2 12.1 %collective-permute-done.10 = bf16[512,768]{1,0:T(8,128)(2,1)} collective-permute-done((bf16[512,768]{1,0:T(8,128)(2,1)}, bf16[512,768]{1,0:T(8,128)(2,1)}, u32[]{:S(2)}, u32[]{:S(2)}) %collective-permute-start.10) | collective-permute-done | bytes 786464 | tf_op jit(solution)/shard_map/ppermute | solution.py:69
  140.3 3.9 %fusion.19 = f32[512,2048]{1,0:T(8,128)S(1)} fusion(f32[512,2048]{1,0:T(8,128)S(1)} %fusion.4, bf16[8192,2048]{1,0:T(8,128)(2,1)} %param.6, s32[]{:T(128)S(6)} %select_n.94, bf16[512,768]{1,0:T(8,128)(2,1)} %collective-permute-done.10, pred[]{:T(512)S(6)} %or.3, bf16[512,1024]{1,0:T(8,128)(2,1)S(1)} %copy-done.3), kind=kOutput, calls=%fused_computation.17 | convolution fusion | flops 1612054528 | bytes 13107205 | tf_op jit(solution)/shard_map/dot_general | solution.py:88
  144.3 3.0 %add_convert_fusion = bf16[512,2048]{1,0:T(8,128)(2,1)} fusion(f32[512,2048]{1,0:T(8,128)S(1)} %fusion.19, bf16[256,2048]{1,0:T(8,128)(2,1)S(1)} %constant_dynamic-slice_fusion, bf16[512,256]{1,0:T(8,128)(2,1)} %collective-permute-done.11, pred[]{:T(512)S(6)} %or.3, bf16[512,1024]{1,0:T(8,128)(2,1)S(1)} %copy-done.3), kind=kOutput, calls=%fused_computation.6 | convolution fusion | flops 539099136 | bytes 7864321 | tf_op jit(solution)/shard_map/dot_general | solution.py:127
  (39 shorter events, 16.7 us)
Async XLA Ops:
  0.0 119.8 %copy-start = (bf16[4,64,2048]{2,1,0:T(8,128)(2,1)S(1)}, bf16[4,64,2048]{2,1,0:T(8,128)(2,1)}, u32[]{:S(2)}) copy-start(bf16[4,64,2048]{2,1,0:T(8,128)(2,1)} %param.8) | copy-start | bytes 3145732
  0.0 15.4 %copy-start.4 = (bf16[2,256,2048]{2,1,0:T(8,128)(2,1)S(1)}, bf16[2,256,2048]{2,1,0:T(8,128)(2,1)}, u32[]{:S(2)}) copy-start(bf16[2,256,2048]{2,1,0:T(8,128)(2,1)} %param.5) | copy-start | bytes 6291460
  0.0 49.8 %collective-permute-start = (bf16[512,2048]{1,0:T(8,128)(2,1)}, bf16[512,2048]{1,0:T(8,128)(2,1)}, u32[]{:S(2)}, u32[]{:S(2)}) collective-permute-start(bf16[512,2048]{1,0:T(8,128)(2,1)} %bitcast.40), channel_id=1, source_target_pairs={{0,4},{12,8},{4,0},{8,12},{1,5},{13,9},{5,1},{9,13},{2,6},{14,10},... | collective-permute-start | bytes 6291464 | tf_op jit(solution)/shard_map/ppermute | solution.py:69
  5.3 27.9 %collective-permute-start.2 = (bf16[512,1024]{1,0:T(8,128)(2,1)}, bf16[512,1024]{1,0:T(8,128)(2,1)}, u32[]{:S(2)}, u32[]{:S(2)}) collective-permute-start(bf16[512,1024]{1,0:T(8,128)(2,1)} %slice.70), channel_id=1, source_target_pairs={{4,8},{8,4},{5,9},{9,5},{6,10},{10,6},{7,11},{11,7},{20,24},{24,20... | collective-permute-start | bytes 3145736 | tf_op jit(solution)/shard_map/ppermute | solution.py:69
  16.5 36.0 %collective-permute-start.4 = (bf16[512,1024]{1,0:T(8,128)(2,1)}, bf16[512,1024]{1,0:T(8,128)(2,1)}, u32[]{:S(2)}, u32[]{:S(2)}) collective-permute-start(bf16[512,1024]{1,0:T(8,128)(2,1)} %slice.59), channel_id=1, source_target_pairs={{4,8},{8,4},{5,9},{9,5},{6,10},{10,6},{7,11},{11,7},{20,24},{24,20... | collective-permute-start | bytes 3145736 | tf_op jit(solution)/shard_map/ppermute | solution.py:69
  18.2 31.3 %collective-permute-start.1 = (bf16[512,64]{0,1:T(8,128)(2,1)S(1)}, bf16[512,64]{0,1:T(8,128)(2,1)S(1)}, u32[]{:S(2)}, u32[]{:S(2)}) collective-permute-start(bf16[512,64]{0,1:T(8,128)(2,1)S(1)} %get-tuple-element.34), channel_id=1, source_target_pairs={{0,4},{12,8},{1,5},{13,9},{2,6},{14,10},{3,7},{15,11},{16,20},{28,... | collective-permute-start | bytes 196616 | tf_op jit(solution)/shard_map/ppermute | solution.py:69
  33.3 39.1 %collective-permute-start.3 = (bf16[512,1024]{1,0:T(8,128)(2,1)}, bf16[512,1024]{1,0:T(8,128)(2,1)}, u32[]{:S(2)}, u32[]{:S(2)}) collective-permute-start(bf16[512,1024]{1,0:T(8,128)(2,1)} %collective-permute-done.2), channel_id=1, source_target_pairs={{4,0},{8,12},{5,1},{9,13},{6,2},{10,14},{7,3},{11,15},{20,16},{24,... | collective-permute-start | bytes 3145736 | tf_op jit(solution)/shard_map/ppermute | solution.py:69
  49.9 18.7 %collective-permute-start.7 = (bf16[2,512,64]{1,2,0:T(8,128)(2,1)S(1)}, bf16[2,512,64]{1,2,0:T(8,128)(2,1)S(1)}, u32[]{:S(2)}, u32[]{:S(2)}) collective-permute-start(bf16[2,512,64]{1,2,0:T(8,128)(2,1)S(1)} %pad_maximum_fusion.1), channel_id=1, source_target_pairs={{4,8},{8,4},{5,9},{9,5},{6,10},{10,6},{7,11},{11,7},{20,24},{24,20... | collective-permute-start | bytes 393224 | tf_op jit(solution)/shard_map/ppermute | solution.py:69
  51.8 13.7 %collective-permute-start.6 = (bf16[512,1024]{1,0:T(8,128)(2,1)S(1)}, bf16[512,1024]{1,0:T(8,128)(2,1)S(1)}, u32[]{:S(2)}, u32[]{:S(2)}) collective-permute-start(bf16[512,1024]{1,0:T(8,128)(2,1)S(1)} %slice.60), channel_id=1, source_target_pairs={{4,8},{8,4},{5,9},{9,5},{6,10},{10,6},{7,11},{11,7},{20,24},{24,20... | collective-permute-start | bytes 3145736 | tf_op jit(solution)/shard_map/ppermute | solution.py:69
  52.6 42.2 %collective-permute-start.5 = (bf16[512,1024]{1,0:T(8,128)(2,1)}, bf16[512,1024]{1,0:T(8,128)(2,1)}, u32[]{:S(2)}, u32[]{:S(2)}) collective-permute-start(bf16[512,1024]{1,0:T(8,128)(2,1)} %collective-permute-done.4), channel_id=1, source_target_pairs={{4,0},{8,12},{5,1},{9,13},{6,2},{10,14},{7,3},{11,15},{20,16},{24,... | collective-permute-start | bytes 3145736 | tf_op jit(solution)/shard_map/ppermute | solution.py:69
  67.8 33.8 %collective-permute-start.9 = (bf16[512,1024]{1,0:T(8,128)(2,1)}, bf16[512,1024]{1,0:T(8,128)(2,1)S(1)}, u32[]{:S(2)}, u32[]{:S(2)}) collective-permute-start(bf16[512,1024]{1,0:T(8,128)(2,1)} %slice.67), channel_id=1, source_target_pairs={{4,8},{8,4},{5,9},{9,5},{6,10},{10,6},{7,11},{11,7},{20,24},{24,20... | collective-permute-start | bytes 3145736 | tf_op jit(solution)/shard_map/ppermute | solution.py:69
  69.9 48.7 %collective-permute-start.8 = (bf16[544,1024]{1,0:T(8,128)(2,1)}, bf16[544,1024]{1,0:T(8,128)(2,1)}, u32[]{:S(2)}, u32[]{:S(2)}) collective-permute-start(bf16[544,1024]{1,0:T(8,128)(2,1)} %pad_maximum_fusion), channel_id=1, source_target_pairs={{4,0},{8,12},{5,1},{9,13},{6,2},{10,14},{7,3},{11,15},{20,16},{24,... | collective-permute-start | bytes 3342344 | tf_op jit(solution)/shard_map/ppermute | solution.py:69
  101.6 1.0 copy-start.2
  107.6 36.6 %collective-permute-start.11 = (bf16[512,256]{1,0:T(8,128)(2,1)}, bf16[512,256]{1,0:T(8,128)(2,1)}, u32[]{:S(2)}, u32[]{:S(2)}) collective-permute-start(bf16[512,256]{1,0:T(8,128)(2,1)} %slice.69), channel_id=1, source_target_pairs={{4,0},{8,12},{5,1},{9,13},{6,2},{10,14},{7,3},{11,15},{20,16},{24,... | collective-permute-start | bytes 786440 | tf_op jit(solution)/shard_map/ppermute | solution.py:69
  108.9 31.4 %collective-permute-start.10 = (bf16[512,768]{1,0:T(8,128)(2,1)}, bf16[512,768]{1,0:T(8,128)(2,1)}, u32[]{:S(2)}, u32[]{:S(2)}) collective-permute-start(bf16[512,768]{1,0:T(8,128)(2,1)} %slice.68), channel_id=1, source_target_pairs={{4,0},{8,12},{5,1},{9,13},{6,2},{10,14},{7,3},{11,15},{20,16},{24,... | collective-permute-start | bytes 2359304 | tf_op jit(solution)/shard_map/ppermute | solution.py:69
  119.8 2.2 %copy-start.1 = (f32[512,2048]{1,0:T(8,128)S(1)}, f32[512,2048]{1,0:T(8,128)}, u32[]{:S(2)}) copy-start(f32[512,2048]{1,0:T(8,128)} %fusion.22) | copy-start | bytes 12582916
  121.9 18.4 %copy-start.3 = (bf16[512,1024]{1,0:T(8,128)(2,1)S(1)}, bf16[512,1024]{1,0:T(8,128)(2,1)}, u32[]{:S(2)}) copy-start(bf16[512,1024]{1,0:T(8,128)(2,1)} %copy-done.2) | copy-start | bytes 3145732

commit v29 on v24

--- a/solution.py
+++ b/solution.py
@@ -88,11 +88,11 @@
         return jnp.dot(block, part, preferred_element_type=F32)
 
     mate = send(own, SWAP)
-    mid = [send(own[:, :half], ACROSS)]
     partial = shrink(inputs, shrink_table, adapter_ids)
-    mid.append(send(after(own, partial)[:, half:], ACROSS))
+    mid = [send(after(own, partial)[:, :half], ACROSS)]
     mate_partial = send(partial, INWARD)
     total = product(own, here)
+    mid.append(send(after(own, total)[:, half:], ACROSS))
 
     mid_out = [send(after(mid[0], total), OUTWARD)]
     mate, mate_partial = lax.optimization_barrier((mate, mate_partial, mid[0], total))[:2]

time: 143 us -> 150 us (1.049)
  waiting for transfers between devices: 59.4 us -> 66.8 us
    ppermute x13, waiting for transfers between devices: 59.4 us -> 66.8 us  [send(): return lax.ppermute(block, 'tensor', pairs)]
  transfers between devices with their start and end apart: 13 -> 13, of which waited for: 7 -> 7; matrix products, arithmetic and copies ran while one was open for 38% -> 36% of each run, Pallas kernels for 0% -> 0%
where the time goes in v29:
time: 150 us
  waiting for transfers between devices  66.8 us (45%)
  matrix products  47.2 us (31%)
  starting transfers between devices  22.3 us (15%)
  local copies, waits for them, and re-layouts  8.94 us (6%)
  between operations  4.28 us (3%)
    ppermute x13, waiting for transfers between devices, send(): return lax.ppermute(block, 'tensor', pairs)  66.8 us
    dot_general x6, matrix products, product(): return jnp.dot(block, part, preferred_element_type=F32)  40.8 us
    ppermute x13, starting transfers between devices, send(): return lax.ppermute(block, 'tensor', pairs)  22.3 us
    dot_general x2, matrix products, shrink(): jnp.dot(inputs[c], shrink_table[adapter_ids[c]], preferred_element_type=F32)  3.52 us
  transfers between devices with their start and end apart: 13, of which 7 were waited for; matrix products, arithmetic and copies ran while one was open for 36% of the time, Pallas kernels for 0%

profile of v29, /device:TPU:0, one launch (start us, length us, event | category | flops | bytes accessed | tf_op | source)
XLA Modules:
  0.0 149.6 jit_solution(15221055528177295550)
XLA Ops:
  0.0 3.0 %collective-permute-start = (bf16[512,2048]{1,0:T(8,128)(2,1)}, bf16[512,2048]{1,0:T(8,128)(2,1)}, u32[]{:S(2)}, u32[]{:S(2)}) collective-permute-start(bf16[512,2048]{1,0:T(8,128)(2,1)} %bitcast.40), channel_id=1, source_target_pairs={{0,4},{12,8},{4,0},{8,12},{1,5},{13,9},{5,1},{9,13},{2,6},{14,10},... | collective-permute-start | bytes 6291464 | tf_op jit(solution)/shard_map/ppermute | solution.py:69
  3.0 1.4 fusion.69
  7.8 1.8 %fusion.28 = bf16[256,64]{0,1:T(8,128)(2,1)S(1)} fusion(bf16[2,256,2048]{2,1,0:T(8,128)(2,1)} %param.5, bf16[4,2048,64]{1,2,0:T(8,128)(2,1)} %param.7, s32[]{:T(128)S(6)} %select_n.78), kind=kOutput, calls=%fused_computation.22 | convolution fusion | flops 67125248 | bytes 1343492 | tf_op jit(solution)/shard_map/dot_general | solution.py:12
  10.2 1.8 %fusion.27 = bf16[256,64]{0,1:T(8,128)(2,1)S(1)} fusion(bf16[2,256,2048]{2,1,0:T(8,128)(2,1)} %param.5, bf16[4,2048,64]{1,2,0:T(8,128)(2,1)} %param.7, s32[]{:T(128)S(6)} %select_n.77), kind=kOutput, calls=%fused_computation.21 | convolution fusion | flops 67125248 | bytes 1343492 | tf_op jit(solution)/shard_map/dot_general | solution.py:12
  12.0 2.3 %slice.52 = bf16[512,1024]{1,0:T(8,128)(2,1)} slice(bf16[512,2048]{1,0:T(8,128)(2,1)} %bitcast.41), slice={[0:512], [0:1024]} | slice | bytes 2097152 | tf_op jit(solution)/shard_map/slice | solution.py:92
  14.2 1.6 %collective-permute-start.2 = (bf16[512,1024]{1,0:T(8,128)(2,1)}, bf16[512,1024]{1,0:T(8,128)(2,1)}, u32[]{:S(2)}, u32[]{:S(2)}) collective-permute-start(bf16[512,1024]{1,0:T(8,128)(2,1)} %slice.52), channel_id=1, source_target_pairs={{4,8},{8,4},{5,9},{9,5},{6,10},{10,6},{7,11},{11,7},{20,24},{24,20... | collective-permute-start | bytes 3145736 | tf_op jit(solution)/shard_map/ppermute | solution.py:69
  15.9 9.4 %fusion.11 = f32[512,2048]{1,0:T(8,128)} fusion(bf16[512,2048]{1,0:T(8,128)(2,1)S(1)} %bitcast.42, bf16[8192,2048]{1,0:T(8,128)(2,1)} %param.6, s32[]{:T(128)S(6)} %select_n.76), kind=kOutput, calls=%fused_computation.13 | convolution fusion | flops 4294967296 | bytes 14680068 | tf_op jit(solution)/shard_map/dot_general | solution.py:88
  26.4 1.7 %collective-permute-start.4 = (bf16[512,1024]{1,0:T(8,128)(2,1)}, bf16[512,1024]{1,0:T(8,128)(2,1)}, u32[]{:S(2)}, u32[]{:S(2)}) collective-permute-start(bf16[512,1024]{1,0:T(8,128)(2,1)} %slice.53), channel_id=1, source_target_pairs={{4,8},{8,4},{5,9},{9,5},{6,10},{10,6},{7,11},{11,7},{20,24},{24,20... | collective-permute-start | bytes 3145736 | tf_op jit(solution)/shard_map/ppermute | solution.py:69
  28.1 5.6 %collective-permute-start.1 = (bf16[512,64]{0,1:T(8,128)(2,1)S(1)}, bf16[512,64]{0,1:T(8,128)(2,1)S(1)}, u32[]{:S(2)}, u32[]{:S(2)}) collective-permute-start(bf16[512,64]{0,1:T(8,128)(2,1)S(1)} %get-tuple-element.38), channel_id=1, source_target_pairs={{0,4},{12,8},{1,5},{13,9},{2,6},{14,10},{3,7},{15,11},{16,20},{28,... | collective-permute-start | bytes 196616 | tf_op jit(solution)/shard_map/ppermute | solution.py:69
  35.0 14.5 %collective-permute-done.1 = bf16[512,64]{0,1:T(8,128)(2,1)S(1)} collective-permute-done((bf16[512,64]{0,1:T(8,128)(2,1)S(1)}, bf16[512,64]{0,1:T(8,128)(2,1)S(1)}, u32[]{:S(2)}, u32[]{:S(2)}) %collective-permute-start.1) | collective-permute-done | bytes 65568 | tf_op jit(solution)/shard_map/ppermute | solution.py:69
  53.9 9.7 %fusion.16 = f32[512,2048]{1,0:T(8,128)S(1)} fusion(f32[512,2048]{1,0:T(8,128)} %fusion.11, bf16[512,2048]{1,0:T(8,128)(2,1)} %collective-permute-done, bf16[8192,2048]{1,0:T(8,128)(2,1)} %param.6, s32[]{:T(128)S(6)} %select_n.79), kind=kOutput, calls=%fused_computation.16 | convolution fusion | flops 4296015872 | bytes 18874372 | tf_op jit(solution)/shard_map/dot_general | solution.py:88
  65.6 6.6 %collective-permute-done.3 = bf16[512,1024]{1,0:T(8,128)(2,1)S(1)} collective-permute-done((bf16[512,1024]{1,0:T(8,128)(2,1)}, bf16[512,1024]{1,0:T(8,128)(2,1)S(1)}, u32[]{:S(2)}, u32[]{:S(2)}) %collective-permute-start.3) | collective-permute-done | bytes 1048608 | tf_op jit(solution)/shard_map/ppermute | solution.py:69
  72.2 6.5 %fusion.22 = f32[512,2048]{1,0:T(8,128)} fusion(f32[512,2048]{1,0:T(8,128)S(1)} %fusion.16, bf16[8192,2048]{1,0:T(8,128)(2,1)} %param.6, s32[]{:T(128)S(6)} %select_n.83, bf16[512,1024]{1,0:T(8,128)(2,1)S(1)} %collective-permute-done.3, bf16[512,1024]{1,0:T(8,128)(2,1)} %collective-permute-done.2, pred[]{:T(512)S(6)} %or.3), kind=kOutput, calls=%fused_computation.18 | convolution fusion | flops 2149056512 | bytes 14680069 | tf_op jit(solution)/shard_map/dot_general | solution.py:88
  81.4 12.5 %collective-permute-done.5 = bf16[512,1024]{1,0:T(8,128)(2,1)S(1)} collective-permute-done((bf16[512,1024]{1,0:T(8,128)(2,1)}, bf16[512,1024]{1,0:T(8,128)(2,1)S(1)}, u32[]{:S(2)}, u32[]{:S(2)}) %collective-permute-start.5) | collective-permute-done | bytes 1048608 | tf_op jit(solution)/shard_map/ppermute | solution.py:69
  93.8 6.5 %fusion.7 = f32[512,2048]{1,0:T(8,128)} fusion(bf16[8192,2048]{1,0:T(8,128)(2,1)} %param.6, s32[]{:T(128)S(6)} %select_n.85, bf16[512,1024]{1,0:T(8,128)(2,1)S(1)} %collective-permute-done.5, bf16[512,1024]{1,0:T(8,128)(2,1)} %collective-permute-done.4, pred[]{:T(512)S(6)} %or.3), kind=kOutput, calls=%fused_computation.9 | convolution fusion | flops 2148007936 | bytes 10485765 | tf_op jit(solution)/shard_map/dot_general | solution.py:88
  100.4 4.5 %collective-permute-done.8 = bf16[512,64]{0,1:T(8,128)(2,1)S(1)} collective-permute-done((bf16[512,64]{0,1:T(8,128)(2,1)S(1)}, bf16[512,64]{0,1:T(8,128)(2,1)S(1)}, u32[]{:S(2)}, u32[]{:S(2)}) %collective-permute-start.8) | collective-permute-done | bytes 65568 | tf_op jit(solution)/shard_map/ppermute | solution.py:69
  104.9 1.4 constant_dynamic-slice_fusion
  106.5 1.6 %collective-permute-start.11 = (bf16[512,768]{1,0:T(8,128)(2,1)S(1)}, bf16[512,768]{1,0:T(8,128)(2,1)S(1)}, u32[]{:S(2)}, u32[]{:S(2)}) collective-permute-start(bf16[512,768]{1,0:T(8,128)(2,1)S(1)} %slice.60), channel_id=1, source_target_pairs={{4,0},{8,12},{5,1},{9,13},{6,2},{10,14},{7,3},{11,15},{20,16},{24,... | collective-permute-start | bytes 2359304 | tf_op jit(solution)/shard_map/ppermute | solution.py:69
  108.1 1.5 collective-permute-start.12
  110.5 17.0 %collective-permute-done.10 = bf16[512,1024]{1,0:T(8,128)(2,1)} collective-permute-done((bf16[512,1024]{1,0:T(8,128)(2,1)S(1)}, bf16[512,1024]{1,0:T(8,128)(2,1)}, u32[]{:S(2)}, u32[]{:S(2)}) %collective-permute-start.10) | collective-permute-done | bytes 1048608 | tf_op jit(solution)/shard_map/ppermute | solution.py:69
  127.5 5.0 %fusion.4 = f32[512,2048]{1,0:T(8,128)S(1)} fusion(f32[256,2048]{1,0:T(8,128)S(1)} %fusion.41, f32[256,2048]{1,0:T(8,128)S(1)} %fusion.43, f32[512,2048]{1,0:T(8,128)S(1)} %copy-done.1, f32[512,2048]{1,0:T(8,128)S(1)} %copy-done.2, bf16[8192,2048]{1,0:T(8,128)(2,1)} %param.6, s32[]{:T(128)S(6)} %select_n.91, bf16[512,1024]{1,0:T(8,128)(2,1)} %collective-permute-done.10, ...), kind=kOutput, calls=%fused_computation.5 | convolution fusion | flops 2152202240 | bytes 23068676 | tf_op jit(solution)/shard_map/dot_general | solution.py:88
  132.4 11.4 %collective-permute-done.11 = bf16[512,768]{1,0:T(8,128)(2,1)S(1)} collective-permute-done((bf16[512,768]{1,0:T(8,128)(2,1)S(1)}, bf16[512,768]{1,0:T(8,128)(2,1)S(1)}, u32[]{:S(2)}, u32[]{:S(2)}) %collective-permute-start.11) | collective-permute-done | bytes 786464 | tf_op jit(solution)/shard_map/ppermute | solution.py:69
  143.8 3.7 %fusion.19 = f32[512,2048]{1,0:T(8,128)S(1)} fusion(f32[512,2048]{1,0:T(8,128)S(1)} %fusion.4, bf16[8192,2048]{1,0:T(8,128)(2,1)} %param.6, s32[]{:T(128)S(6)} %select_n.94, bf16[512,768]{1,0:T(8,128)(2,1)S(1)} %collective-permute-done.11, pred[]{:T(512)S(6)} %or.3, bf16[512,1024]{1,0:T(8,128)(2,1)S(1)} %collective-permute-done.9), kind=kOutput, calls=%fused_computation.17 | convolution fusion | flops 1612054528 | bytes 13107205 | tf_op jit(solution)/shard_map/dot_general | solution.py:88
  147.5 2.0 %add_convert_fusion = bf16[512,2048]{1,0:T(8,128)(2,1)} fusion(f32[512,2048]{1,0:T(8,128)S(1)} %fusion.19, bf16[256,2048]{1,0:T(8,128)(2,1)S(1)} %constant_dynamic-slice_fusion, bf16[512,256]{1,0:T(8,128)(2,1)S(1)} %collective-permute-done.12, pred[]{:T(512)S(6)} %or.3, bf16[512,1024]{1,0:T(8,128)(2,1)S(1)} %collective-permute-done.9), kind=kOutput, calls=%fused_computation.6 | convolution fusion | flops 539099136 | bytes 7864321 | tf_op jit(solution)/shard_map/dot_general | solution.py:126
  (33 shorter events, 12.4 us)
Async XLA Ops:
  0.0 109.5 %copy-start = (bf16[4,64,2048]{2,1,0:T(8,128)(2,1)S(1)}, bf16[4,64,2048]{2,1,0:T(8,128)(2,1)}, u32[]{:S(2)}) copy-start(bf16[4,64,2048]{2,1,0:T(8,128)(2,1)} %param.8) | copy-start | bytes 3145732
  0.0 15.9 %copy-start.3 = (bf16[2,256,2048]{2,1,0:T(8,128)(2,1)S(1)}, bf16[2,256,2048]{2,1,0:T(8,128)(2,1)}, u32[]{:S(2)}) copy-start(bf16[2,256,2048]{2,1,0:T(8,128)(2,1)} %param.5) | copy-start | bytes 6291460
  0.0 49.8 %collective-permute-start = (bf16[512,2048]{1,0:T(8,128)(2,1)}, bf16[512,2048]{1,0:T(8,128)(2,1)}, u32[]{:S(2)}, u32[]{:S(2)}) collective-permute-start(bf16[512,2048]{1,0:T(8,128)(2,1)} %bitcast.40), channel_id=1, source_target_pairs={{0,4},{12,8},{4,0},{8,12},{1,5},{13,9},{5,1},{9,13},{2,6},{14,10},... | collective-permute-start | bytes 6291464 | tf_op jit(solution)/shard_map/ppermute | solution.py:69
  14.2 19.5 %collective-permute-start.2 = (bf16[512,1024]{1,0:T(8,128)(2,1)}, bf16[512,1024]{1,0:T(8,128)(2,1)}, u32[]{:S(2)}, u32[]{:S(2)}) collective-permute-start(bf16[512,1024]{1,0:T(8,128)(2,1)} %slice.52), channel_id=1, source_target_pairs={{4,8},{8,4},{5,9},{9,5},{6,10},{10,6},{7,11},{11,7},{20,24},{24,20... | collective-permute-start | bytes 3145736 | tf_op jit(solution)/shard_map/ppermute | solution.py:69
  26.4 26.2 %collective-permute-start.4 = (bf16[512,1024]{1,0:T(8,128)(2,1)}, bf16[512,1024]{1,0:T(8,128)(2,1)}, u32[]{:S(2)}, u32[]{:S(2)}) collective-permute-start(bf16[512,1024]{1,0:T(8,128)(2,1)} %slice.53), channel_id=1, source_target_pairs={{4,8},{8,4},{5,9},{9,5},{6,10},{10,6},{7,11},{11,7},{20,24},{24,20... | collective-permute-start | bytes 3145736 | tf_op jit(solution)/shard_map/ppermute | solution.py:69
  28.1 21.4 %collective-permute-start.1 = (bf16[512,64]{0,1:T(8,128)(2,1)S(1)}, bf16[512,64]{0,1:T(8,128)(2,1)S(1)}, u32[]{:S(2)}, u32[]{:S(2)}) collective-permute-start(bf16[512,64]{0,1:T(8,128)(2,1)S(1)} %get-tuple-element.38), channel_id=1, source_target_pairs={{0,4},{12,8},{1,5},{13,9},{2,6},{14,10},{3,7},{15,11},{16,20},{28,... | collective-permute-start | bytes 196616 | tf_op jit(solution)/shard_map/ppermute | solution.py:69
  33.7 38.5 %collective-permute-start.3 = (bf16[512,1024]{1,0:T(8,128)(2,1)}, bf16[512,1024]{1,0:T(8,128)(2,1)S(1)}, u32[]{:S(2)}, u32[]{:S(2)}) collective-permute-start(bf16[512,1024]{1,0:T(8,128)(2,1)} %collective-permute-done.2), channel_id=1, source_target_pairs={{4,0},{8,12},{5,1},{9,13},{6,2},{10,14},{7,3},{11,15},{20,16},{24,... | collective-permute-start | bytes 3145736 | tf_op jit(solution)/shard_map/ppermute | solution.py:69
  51.1 12.4 %collective-permute-start.6 = (bf16[512,1024]{1,0:T(8,128)(2,1)S(1)}, bf16[512,1024]{1,0:T(8,128)(2,1)S(1)}, u32[]{:S(2)}, u32[]{:S(2)}) collective-permute-start(bf16[512,1024]{1,0:T(8,128)(2,1)S(1)} %slice.54), channel_id=1, source_target_pairs={{4,8},{8,4},{5,9},{9,5},{6,10},{10,6},{7,11},{11,7},{20,24},{24,20... | collective-permute-start | bytes 3145736 | tf_op jit(solution)/shard_map/ppermute | solution.py:69
  51.9 26.9 %collective-permute-start.7 = (bf16[2,512,64]{1,2,0:T(8,128)(2,1)S(1)}, bf16[2,512,64]{1,2,0:T(8,128)(2,1)S(1)}, u32[]{:S(2)}, u32[]{:S(2)}) collective-permute-start(bf16[2,512,64]{1,2,0:T(8,128)(2,1)S(1)} %pad_maximum_fusion), channel_id=1, source_target_pairs={{4,8},{8,4},{5,9},{9,5},{6,10},{10,6},{7,11},{11,7},{20,24},{24,20... | collective-permute-start | bytes 393224 | tf_op jit(solution)/shard_map/ppermute | solution.py:69
  52.6 41.3 %collective-permute-start.5 = (bf16[512,1024]{1,0:T(8,128)(2,1)}, bf16[512,1024]{1,0:T(8,128)(2,1)S(1)}, u32[]{:S(2)}, u32[]{:S(2)}) collective-permute-start(bf16[512,1024]{1,0:T(8,128)(2,1)} %collective-permute-done.4), channel_id=1, source_target_pairs={{4,0},{8,12},{5,1},{9,13},{6,2},{10,14},{7,3},{11,15},{20,16},{24,... | collective-permute-start | bytes 3145736 | tf_op jit(solution)/shard_map/ppermute | solution.py:69
  64.9 40.0 %collective-permute-start.9 = (bf16[512,1024]{1,0:T(8,128)(2,1)S(1)}, bf16[512,1024]{1,0:T(8,128)(2,1)S(1)}, u32[]{:S(2)}, u32[]{:S(2)}) collective-permute-start(bf16[512,1024]{1,0:T(8,128)(2,1)S(1)} %slice.57), channel_id=1, source_target_pairs={{4,8},{8,4},{5,9},{9,5},{6,10},{10,6},{7,11},{11,7},{20,24},{24,20... | collective-permute-start | bytes 3145736 | tf_op jit(solution)/shard_map/ppermute | solution.py:69
  78.8 26.1 %collective-permute-start.8 = (bf16[512,64]{0,1:T(8,128)(2,1)S(1)}, bf16[512,64]{0,1:T(8,128)(2,1)S(1)}, u32[]{:S(2)}, u32[]{:S(2)}) collective-permute-start(bf16[512,64]{0,1:T(8,128)(2,1)S(1)} %fusion.53), channel_id=1, source_target_pairs={{4,0},{8,12},{5,1},{9,13},{6,2},{10,14},{7,3},{11,15},{20,16},{24,... | collective-permute-start | bytes 196616 | tf_op jit(solution)/shard_map/ppermute | solution.py:69
  80.1 47.4 %collective-permute-start.10 = (bf16[512,1024]{1,0:T(8,128)(2,1)S(1)}, bf16[512,1024]{1,0:T(8,128)(2,1)}, u32[]{:S(2)}, u32[]{:S(2)}) collective-permute-start(bf16[512,1024]{1,0:T(8,128)(2,1)S(1)} %collective-permute-done.6), channel_id=1, source_target_pairs={{4,0},{8,12},{5,1},{9,13},{6,2},{10,14},{7,3},{11,15},{20,16},{24,... | collective-permute-start | bytes 3145736 | tf_op jit(solution)/shard_map/ppermute | solution.py:69
  104.9 22.5 %copy-start.1 = (f32[512,2048]{1,0:T(8,128)S(1)}, f32[512,2048]{1,0:T(8,128)}, u32[]{:S(2)}) copy-start(f32[512,2048]{1,0:T(8,128)} %fusion.22) | copy-start | bytes 12582916
  104.9 22.5 %copy-start.2 = (f32[512,2048]{1,0:T(8,128)S(1)}, f32[512,2048]{1,0:T(8,128)}, u32[]{:S(2)}) copy-start(f32[512,2048]{1,0:T(8,128)} %fusion.7) | copy-start | bytes 12582916
  106.5 37.3 %collective-permute-start.11 = (bf16[512,768]{1,0:T(8,128)(2,1)S(1)}, bf16[512,768]{1,0:T(8,128)(2,1)S(1)}, u32[]{:S(2)}, u32[]{:S(2)}) collective-permute-start(bf16[512,768]{1,0:T(8,128)(2,1)S(1)} %slice.60), channel_id=1, source_target_pairs={{4,0},{8,12},{5,1},{9,13},{6,2},{10,14},{7,3},{11,15},{20,16},{24,... | collective-permute-start | bytes 2359304 | tf_op jit(solution)/shard_map/ppermute | solution.py:69
  108.1 39.5 %collective-permute-start.12 = (bf16[512,256]{1,0:T(8,128)(2,1)S(1)}, bf16[512,256]{1,0:T(8,128)(2,1)S(1)}, u32[]{:S(2)}, u32[]{:S(2)}) collective-permute-start(bf16[512,256]{1,0:T(8,128)(2,1)S(1)} %slice.61), channel_id=1, source_target_pairs={{4,0},{8,12},{5,1},{9,13},{6,2},{10,14},{7,3},{11,15},{20,16},{24,... | collective-permute-start | bytes 786440 | tf_op jit(solution)/shard_map/ppermute | solution.py:69

commit v30 on v24

--- a/solution.py
+++ b/solution.py
@@ -120,10 +120,9 @@
     total = total + product(jnp.where(is_end, mid_out[1], mid[1]), far_mid, half)
     total = total + jnp.concatenate(expand(shrunk, expand_table, adapter_ids))
     total = total + product(jnp.where(is_end, end_out[0], end[0]), far_end)
-    block = jnp.where(is_end, after(end_out[1], total), late[:, : half - last])
-    total = total + product(block, far_end, half)
-    block = jnp.where(is_end, after(end_out[2], total), late[:, half - last :])
-    total = total + jnp.dot(block, last_rows, preferred_element_type=F32)
+    total = total + product(late, far_end, half)
+    total = total + product(after(end_out[1], total), far_end, half)
+    total = total + jnp.dot(after(end_out[2], total), last_rows, preferred_element_type=F32)
     return total.astype(BF16).reshape(chats, span, -1)
 
 

time: 143 us -> 147 us (1.028)
  matrix products: 47.2 us -> 52.9 us
  waiting for transfers between devices: 59.4 us -> 55.6 us
  local copies, waits for them, and re-layouts: 8.97 us -> 11.1 us
    dot_general x6 -> x7, matrix products: 40.8 us -> 46.4 us  [product(): return jnp.dot(block, part, preferred_element_type=F32)]
    ppermute x13, waiting for transfers between devices: 59.4 us -> 55.6 us  [send(): return lax.ppermute(block, 'tensor', pairs)]
  transfers between devices with their start and end apart: 13 -> 13, of which waited for: 7 -> 6; matrix products, arithmetic and copies ran while one was open for 38% -> 42% of each run, Pallas kernels for 0% -> 0%
where the time goes in v30:
time: 147 us; the launch traced here: 146 us
  waiting for transfers between devices  55.6 us (38%)
  matrix products  52.9 us (36%)
  starting transfers between devices  23 us (16%)
  local copies, waits for them, and re-layouts  11.1 us (8%)
  between operations  3.8 us (3%)
    ppermute x13, waiting for transfers between devices, send(): return lax.ppermute(block, 'tensor', pairs)  55.6 us
    dot_general x7, matrix products, product(): return jnp.dot(block, part, preferred_element_type=F32)  46.4 us
    ppermute x13, starting transfers between devices, send(): return lax.ppermute(block, 'tensor', pairs)  23 us
    dot_general x2, matrix products, shrink(): jnp.dot(inputs[c], shrink_table[adapter_ids[c]], preferred_element_type=F32)  3.52 us
  transfers between devices with their start and end apart: 13, of which 6 were waited for; matrix products, arithmetic and copies ran while one was open for 42% of the time, Pallas kernels for 0%

profile of v30, /device:TPU:0, one launch (start us, length us, event | category | flops | bytes accessed | tf_op | source)
XLA Modules:
  0.0 146.4 jit_solution(13810271501522590278)
XLA Ops:
  0.0 3.0 %collective-permute-start = (bf16[512,2048]{1,0:T(8,128)(2,1)}, bf16[512,2048]{1,0:T(8,128)(2,1)}, u32[]{:S(2)}, u32[]{:S(2)}) collective-permute-start(bf16[512,2048]{1,0:T(8,128)(2,1)} %bitcast.43), channel_id=1, source_target_pairs={{0,4},{12,8},{4,0},{8,12},{1,5},{13,9},{5,1},{9,13},{2,6},{14,10},... | collective-permute-start | bytes 6291464 | tf_op jit(solution)/shard_map/ppermute | solution.py:69
  3.0 2.3 %slice.60 = bf16[512,1024]{1,0:T(8,128)(2,1)} slice(bf16[512,2048]{1,0:T(8,128)(2,1)} %bitcast.44), slice={[0:512], [0:1024]} | slice | bytes 2097152 | tf_op jit(solution)/shard_map/slice | solution.py:91
  5.3 1.6 %collective-permute-start.2 = (bf16[512,1024]{1,0:T(8,128)(2,1)}, bf16[512,1024]{1,0:T(8,128)(2,1)}, u32[]{:S(2)}, u32[]{:S(2)}) collective-permute-start(bf16[512,1024]{1,0:T(8,128)(2,1)} %slice.60), channel_id=1, source_target_pairs={{4,8},{8,4},{5,9},{9,5},{6,10},{10,6},{7,11},{11,7},{20,24},{24,20... | collective-permute-start | bytes 3145736 | tf_op jit(solution)/shard_map/ppermute | solution.py:69
  7.0 1.3 fusion.67
  11.8 1.8 %fusion.30 = bf16[256,64]{0,1:T(8,128)(2,1)S(1)} fusion(bf16[2,256,2048]{2,1,0:T(8,128)(2,1)} %param.5, bf16[4,2048,64]{1,2,0:T(8,128)(2,1)} %param.7, s32[]{:T(128)S(6)} %select_n.62), kind=kOutput, calls=%fused_computation.24 | convolution fusion | flops 67125248 | bytes 1343492 | tf_op jit(solution)/shard_map/dot_general | solution.py:12
  13.6 1.8 %fusion.31 = bf16[256,64]{0,1:T(8,128)(2,1)S(1)} fusion(bf16[2,256,2048]{2,1,0:T(8,128)(2,1)} %param.5, bf16[4,2048,64]{1,2,0:T(8,128)(2,1)} %param.7, s32[]{:T(128)S(6)} %select_n.63), kind=kOutput, calls=%fused_computation.25 | convolution fusion | flops 67125248 | bytes 1343492 | tf_op jit(solution)/shard_map/dot_general | solution.py:12
  16.5 1.7 %collective-permute-start.4 = (bf16[512,1024]{1,0:T(8,128)(2,1)}, bf16[512,1024]{1,0:T(8,128)(2,1)}, u32[]{:S(2)}, u32[]{:S(2)}) collective-permute-start(bf16[512,1024]{1,0:T(8,128)(2,1)} %slice.51), channel_id=1, source_target_pairs={{4,8},{8,4},{5,9},{9,5},{6,10},{10,6},{7,11},{11,7},{20,24},{24,20... | collective-permute-start | bytes 3145736 | tf_op jit(solution)/shard_map/ppermute | solution.py:69
  18.2 5.6 %collective-permute-start.1 = (bf16[512,64]{0,1:T(8,128)(2,1)S(1)}, bf16[512,64]{0,1:T(8,128)(2,1)S(1)}, u32[]{:S(2)}, u32[]{:S(2)}) collective-permute-start(bf16[512,64]{0,1:T(8,128)(2,1)S(1)} %get-tuple-element.36), channel_id=1, source_target_pairs={{0,4},{12,8},{1,5},{13,9},{2,6},{14,10},{3,7},{15,11},{16,20},{28,... | collective-permute-start | bytes 196616 | tf_op jit(solution)/shard_map/ppermute | solution.py:69
  23.8 9.4 %fusion.14 = f32[512,2048]{1,0:T(8,128)} fusion(bf16[512,2048]{1,0:T(8,128)(2,1)S(1)} %bitcast.46, bf16[8192,2048]{1,0:T(8,128)(2,1)} %param.6, s32[]{:T(128)S(6)} %select_n.61), kind=kOutput, calls=%fused_computation.16 | convolution fusion | flops 4294967296 | bytes 14680068 | tf_op jit(solution)/shard_map/dot_general | solution.py:88
  34.5 15.1 %collective-permute-done.1 = bf16[512,64]{0,1:T(8,128)(2,1)S(1)} collective-permute-done((bf16[512,64]{0,1:T(8,128)(2,1)S(1)}, bf16[512,64]{0,1:T(8,128)(2,1)S(1)}, u32[]{:S(2)}, u32[]{:S(2)}) %collective-permute-start.1) | collective-permute-done | bytes 65568 | tf_op jit(solution)/shard_map/ppermute | solution.py:69
  51.8 1.7 %collective-permute-start.6 = (bf16[512,1024]{1,0:T(8,128)(2,1)S(1)}, bf16[512,1024]{1,0:T(8,128)(2,1)}, u32[]{:S(2)}, u32[]{:S(2)}) collective-permute-start(bf16[512,1024]{1,0:T(8,128)(2,1)S(1)} %slice.52), channel_id=1, source_target_pairs={{4,8},{8,4},{5,9},{9,5},{6,10},{10,6},{7,11},{11,7},{20,24},{24,20... | collective-permute-start | bytes 3145736 | tf_op jit(solution)/shard_map/ppermute | solution.py:69
  54.9 9.7 %fusion.19 = f32[512,2048]{1,0:T(8,128)S(1)} fusion(f32[512,2048]{1,0:T(8,128)} %fusion.14, bf16[512,2048]{1,0:T(8,128)(2,1)} %collective-permute-done, bf16[8192,2048]{1,0:T(8,128)(2,1)} %param.6, s32[]{:T(128)S(6)} %select_n.64), kind=kOutput, calls=%fused_computation.19 | convolution fusion | flops 4296015872 | bytes 18874372 | tf_op jit(solution)/shard_map/dot_general | solution.py:88
  66.6 5.6 %collective-permute-done.3 = bf16[512,1024]{1,0:T(8,128)(2,1)S(1)} collective-permute-done((bf16[512,1024]{1,0:T(8,128)(2,1)}, bf16[512,1024]{1,0:T(8,128)(2,1)S(1)}, u32[]{:S(2)}, u32[]{:S(2)}) %collective-permute-start.3) | collective-permute-done | bytes 1048608 | tf_op jit(solution)/shard_map/ppermute | solution.py:69
  72.2 6.5 %fusion.25 = f32[512,2048]{1,0:T(8,128)} fusion(f32[512,2048]{1,0:T(8,128)S(1)} %fusion.19, bf16[8192,2048]{1,0:T(8,128)(2,1)} %param.6, s32[]{:T(128)S(6)} %select_n.68, bf16[512,1024]{1,0:T(8,128)(2,1)S(1)} %collective-permute-done.3, bf16[512,1024]{1,0:T(8,128)(2,1)} %collective-permute-done.2, pred[]{:T(512)S(6)} %or.3), kind=kOutput, calls=%fused_computation.21 | convolution fusion | flops 2149056512 | bytes 14680069 | tf_op jit(solution)/shard_map/dot_general | solution.py:88
  81.4 13.2 %collective-permute-done.5 = bf16[512,1024]{1,0:T(8,128)(2,1)S(1)} collective-permute-done((bf16[512,1024]{1,0:T(8,128)(2,1)}, bf16[512,1024]{1,0:T(8,128)(2,1)S(1)}, u32[]{:S(2)}, u32[]{:S(2)}) %collective-permute-start.5) | collective-permute-done | bytes 1048608 | tf_op jit(solution)/shard_map/ppermute | solution.py:69
  94.5 6.5 %fusion.10 = f32[512,2048]{1,0:T(8,128)} fusion(bf16[8192,2048]{1,0:T(8,128)(2,1)} %param.6, s32[]{:T(128)S(6)} %select_n.70, bf16[512,1024]{1,0:T(8,128)(2,1)S(1)} %collective-permute-done.5, bf16[512,1024]{1,0:T(8,128)(2,1)} %collective-permute-done.4, pred[]{:T(512)S(6)} %or.3), kind=kOutput, calls=%fused_computation.12 | convolution fusion | flops 2148007936 | bytes 10485765 | tf_op jit(solution)/shard_map/dot_general | solution.py:88
  101.1 2.7 %constant_dynamic-slice_fusion = bf16[256,2048]{1,0:T(8,128)(2,1)} fusion(bf16[8192,2048]{1,0:T(8,128)(2,1)} %param.6, s32[]{:T(128)S(6)} %select_n.74), kind=kLoop, calls=%fused_computation.59 | loop fusion | bytes 2097156 | tf_op jit(solution)/shard_map/dynamic_slice | solution.py:116
  106.1 1.5 %collective-permute-start.11 = (bf16[512,768]{1,0:T(8,128)(2,1)}, bf16[512,768]{1,0:T(8,128)(2,1)}, u32[]{:S(2)}, u32[]{:S(2)}) collective-permute-start(bf16[512,768]{1,0:T(8,128)(2,1)} %slice.58), channel_id=1, source_target_pairs={{4,0},{8,12},{5,1},{9,13},{6,2},{10,14},{7,3},{11,15},{20,16},{24,... | collective-permute-start | bytes 2359304 | tf_op jit(solution)/shard_map/ppermute | solution.py:69
  108.5 5.0 %fusion.6 = f32[512,2048]{1,0:T(8,128)S(1)} fusion(bf16[512,1024]{1,0:T(8,128)(2,1)} %copy-done.5, bf16[8192,2048]{1,0:T(8,128)(2,1)} %param.6, s32[]{:T(128)S(6)} %select_n.77), kind=kOutput, calls=%fused_computation.8 | convolution fusion | flops 2147483648 | bytes 9437188 | tf_op jit(solution)/shard_map/dot_general | solution.py:88
  113.5 6.7 %collective-permute-done.10 = bf16[512,1024]{1,0:T(8,128)(2,1)} collective-permute-done((bf16[512,1024]{1,0:T(8,128)(2,1)}, bf16[512,1024]{1,0:T(8,128)(2,1)}, u32[]{:S(2)}, u32[]{:S(2)}) %collective-permute-start.10) | collective-permute-done | bytes 1048608 | tf_op jit(solution)/shard_map/ppermute | solution.py:69
  120.2 5.2 %fusion.5 = f32[512,2048]{1,0:T(8,128)S(1)} fusion(f32[512,2048]{1,0:T(8,128)S(1)} %fusion.6, f32[256,2048]{1,0:T(8,128)S(1)} %fusion.42, f32[256,2048]{1,0:T(8,128)S(1)} %fusion.44, f32[512,2048]{1,0:T(8,128)S(1)} %copy-done.1, f32[512,2048]{1,0:T(8,128)S(1)} %copy-done.2, bf16[8192,2048]{1,0:T(8,128)(2,1)} %param.6, s32[]{:T(128)S(6)} %select_n.76, ...), kind=kOutput, calls=%fused_computation.6 | convolution fusion | flops 2153250816 | bytes 27262980 | tf_op jit(solution)/shard_map/dot_general | solution.py:88
  125.5 14.8 %collective-permute-done.11 = bf16[512,768]{1,0:T(8,128)(2,1)} collective-permute-done((bf16[512,768]{1,0:T(8,128)(2,1)}, bf16[512,768]{1,0:T(8,128)(2,1)}, u32[]{:S(2)}, u32[]{:S(2)}) %collective-permute-start.11) | collective-permute-done | bytes 786464 | tf_op jit(solution)/shard_map/ppermute | solution.py:69
  140.3 4.0 %fusion.22 = f32[512,2048]{1,0:T(8,128)S(1)} fusion(f32[512,2048]{1,0:T(8,128)S(1)} %fusion.5, bf16[512,768]{1,0:T(8,128)(2,1)} %collective-permute-done.11, bf16[8192,2048]{1,0:T(8,128)(2,1)} %param.6, s32[]{:T(128)S(6)} %select_n.77), kind=kOutput, calls=%fused_computation.20 | convolution fusion | flops 1611661312 | bytes 12320772 | tf_op jit(solution)/shard_map/dot_general | solution.py:88
  144.3 2.1 %add_convert_fusion = bf16[512,2048]{1,0:T(8,128)(2,1)} fusion(f32[512,2048]{1,0:T(8,128)S(1)} %fusion.22, bf16[512,256]{1,0:T(8,128)(2,1)S(1)} %collective-permute-done.12, bf16[256,2048]{1,0:T(8,128)(2,1)S(1)} %copy-done.3), kind=kOutput, calls=%fused_computation.7 | convolution fusion | flops 538968064 | bytes 7602176 | tf_op jit(solution)/shard_map/dot_general | solution.py:125
  (38 shorter events, 13.9 us)
Async XLA Ops:
  0.0 107.6 %copy-start = (bf16[4,64,2048]{2,1,0:T(8,128)(2,1)S(1)}, bf16[4,64,2048]{2,1,0:T(8,128)(2,1)}, u32[]{:S(2)}) copy-start(bf16[4,64,2048]{2,1,0:T(8,128)(2,1)} %param.8) | copy-start | bytes 3145732
  0.0 15.4 %copy-start.4 = (bf16[2,256,2048]{2,1,0:T(8,128)(2,1)S(1)}, bf16[2,256,2048]{2,1,0:T(8,128)(2,1)}, u32[]{:S(2)}) copy-start(bf16[2,256,2048]{2,1,0:T(8,128)(2,1)} %param.5) | copy-start | bytes 6291460
  0.0 49.8 %collective-permute-start = (bf16[512,2048]{1,0:T(8,128)(2,1)}, bf16[512,2048]{1,0:T(8,128)(2,1)}, u32[]{:S(2)}, u32[]{:S(2)}) collective-permute-start(bf16[512,2048]{1,0:T(8,128)(2,1)} %bitcast.43), channel_id=1, source_target_pairs={{0,4},{12,8},{4,0},{8,12},{1,5},{13,9},{5,1},{9,13},{2,6},{14,10},... | collective-permute-start | bytes 6291464 | tf_op jit(solution)/shard_map/ppermute | solution.py:69
  5.3 27.9 %collective-permute-start.2 = (bf16[512,1024]{1,0:T(8,128)(2,1)}, bf16[512,1024]{1,0:T(8,128)(2,1)}, u32[]{:S(2)}, u32[]{:S(2)}) collective-permute-start(bf16[512,1024]{1,0:T(8,128)(2,1)} %slice.60), channel_id=1, source_target_pairs={{4,8},{8,4},{5,9},{9,5},{6,10},{10,6},{7,11},{11,7},{20,24},{24,20... | collective-permute-start | bytes 3145736 | tf_op jit(solution)/shard_map/ppermute | solution.py:69
  16.5 37.0 %collective-permute-start.4 = (bf16[512,1024]{1,0:T(8,128)(2,1)}, bf16[512,1024]{1,0:T(8,128)(2,1)}, u32[]{:S(2)}, u32[]{:S(2)}) collective-permute-start(bf16[512,1024]{1,0:T(8,128)(2,1)} %slice.51), channel_id=1, source_target_pairs={{4,8},{8,4},{5,9},{9,5},{6,10},{10,6},{7,11},{11,7},{20,24},{24,20... | collective-permute-start | bytes 3145736 | tf_op jit(solution)/shard_map/ppermute | solution.py:69
  18.2 31.3 %collective-permute-start.1 = (bf16[512,64]{0,1:T(8,128)(2,1)S(1)}, bf16[512,64]{0,1:T(8,128)(2,1)S(1)}, u32[]{:S(2)}, u32[]{:S(2)}) collective-permute-start(bf16[512,64]{0,1:T(8,128)(2,1)S(1)} %get-tuple-element.36), channel_id=1, source_target_pairs={{0,4},{12,8},{1,5},{13,9},{2,6},{14,10},{3,7},{15,11},{16,20},{28,... | collective-permute-start | bytes 196616 | tf_op jit(solution)/shard_map/ppermute | solution.py:69
  33.2 39.0 %collective-permute-start.3 = (bf16[512,1024]{1,0:T(8,128)(2,1)}, bf16[512,1024]{1,0:T(8,128)(2,1)S(1)}, u32[]{:S(2)}, u32[]{:S(2)}) collective-permute-start(bf16[512,1024]{1,0:T(8,128)(2,1)} %collective-permute-done.2), channel_id=1, source_target_pairs={{4,0},{8,12},{5,1},{9,13},{6,2},{10,14},{7,3},{11,15},{20,16},{24,... | collective-permute-start | bytes 3145736 | tf_op jit(solution)/shard_map/ppermute | solution.py:69
  49.9 28.9 %collective-permute-start.7 = (bf16[2,512,64]{1,2,0:T(8,128)(2,1)S(1)}, bf16[2,512,64]{1,2,0:T(8,128)(2,1)S(1)}, u32[]{:S(2)}, u32[]{:S(2)}) collective-permute-start(bf16[2,512,64]{1,2,0:T(8,128)(2,1)S(1)} %pad_maximum_fusion), channel_id=1, source_target_pairs={{4,8},{8,4},{5,9},{9,5},{6,10},{10,6},{7,11},{11,7},{20,24},{24,20... | collective-permute-start | bytes 393224 | tf_op jit(solution)/shard_map/ppermute | solution.py:69
  51.8 12.7 %collective-permute-start.6 = (bf16[512,1024]{1,0:T(8,128)(2,1)S(1)}, bf16[512,1024]{1,0:T(8,128)(2,1)}, u32[]{:S(2)}, u32[]{:S(2)}) collective-permute-start(bf16[512,1024]{1,0:T(8,128)(2,1)S(1)} %slice.52), channel_id=1, source_target_pairs={{4,8},{8,4},{5,9},{9,5},{6,10},{10,6},{7,11},{11,7},{20,24},{24,20... | collective-permute-start | bytes 3145736 | tf_op jit(solution)/shard_map/ppermute | solution.py:69
  53.6 41.0 %collective-permute-start.5 = (bf16[512,1024]{1,0:T(8,128)(2,1)}, bf16[512,1024]{1,0:T(8,128)(2,1)S(1)}, u32[]{:S(2)}, u32[]{:S(2)}) collective-permute-start(bf16[512,1024]{1,0:T(8,128)(2,1)} %collective-permute-done.4), channel_id=1, source_target_pairs={{4,0},{8,12},{5,1},{9,13},{6,2},{10,14},{7,3},{11,15},{20,16},{24,... | collective-permute-start | bytes 3145736 | tf_op jit(solution)/shard_map/ppermute | solution.py:69
  65.9 35.2 %collective-permute-start.9 = (bf16[512,1024]{1,0:T(8,128)(2,1)S(1)}, bf16[512,1024]{1,0:T(8,128)(2,1)S(1)}, u32[]{:S(2)}, u32[]{:S(2)}) collective-permute-start(bf16[512,1024]{1,0:T(8,128)(2,1)S(1)} %slice.55), channel_id=1, source_target_pairs={{4,8},{8,4},{5,9},{9,5},{6,10},{10,6},{7,11},{11,7},{20,24},{24,20... | collective-permute-start | bytes 3145736 | tf_op jit(solution)/shard_map/ppermute | solution.py:69
  78.8 22.3 %collective-permute-start.8 = (bf16[512,64]{0,1:T(8,128)(2,1)S(1)}, bf16[512,64]{0,1:T(8,128)(2,1)S(1)}, u32[]{:S(2)}, u32[]{:S(2)}) collective-permute-start(bf16[512,64]{0,1:T(8,128)(2,1)S(1)} %fusion.52), channel_id=1, source_target_pairs={{4,0},{8,12},{5,1},{9,13},{6,2},{10,14},{7,3},{11,15},{20,16},{24,... | collective-permute-start | bytes 196616 | tf_op jit(solution)/shard_map/ppermute | solution.py:69
  80.1 40.2 %collective-permute-start.10 = (bf16[512,1024]{1,0:T(8,128)(2,1)}, bf16[512,1024]{1,0:T(8,128)(2,1)}, u32[]{:S(2)}, u32[]{:S(2)}) collective-permute-start(bf16[512,1024]{1,0:T(8,128)(2,1)} %collective-permute-done.6), channel_id=1, source_target_pairs={{4,0},{8,12},{5,1},{9,13},{6,2},{10,14},{7,3},{11,15},{20,16},{24,... | collective-permute-start | bytes 3145736 | tf_op jit(solution)/shard_map/ppermute | solution.py:69
  101.1 7.0 %copy-start.5 = (bf16[512,1024]{1,0:T(8,128)(2,1)}, bf16[512,1024]{1,0:T(8,128)(2,1)S(1)}, u32[]{:S(2)}) copy-start(bf16[512,1024]{1,0:T(8,128)(2,1)S(1)} %collective-permute-done.9) | copy-start | bytes 3145732
  104.8 39.5 %collective-permute-start.12 = (bf16[512,256]{1,0:T(8,128)(2,1)S(1)}, bf16[512,256]{1,0:T(8,128)(2,1)S(1)}, u32[]{:S(2)}, u32[]{:S(2)}) collective-permute-start(bf16[512,256]{1,0:T(8,128)(2,1)S(1)} %slice.59), channel_id=1, source_target_pairs={{4,0},{8,12},{5,1},{9,13},{6,2},{10,14},{7,3},{11,15},{20,16},{24,... | collective-permute-start | bytes 786440 | tf_op jit(solution)/shard_map/ppermute | solution.py:69
  106.1 34.2 %collective-permute-start.11 = (bf16[512,768]{1,0:T(8,128)(2,1)}, bf16[512,768]{1,0:T(8,128)(2,1)}, u32[]{:S(2)}, u32[]{:S(2)}) collective-permute-start(bf16[512,768]{1,0:T(8,128)(2,1)} %slice.58), channel_id=1, source_target_pairs={{4,0},{8,12},{5,1},{9,13},{6,2},{10,14},{7,3},{11,15},{20,16},{24,... | collective-permute-start | bytes 2359304 | tf_op jit(solution)/shard_map/ppermute | solution.py:69
  108.5 11.7 %copy-start.1 = (f32[512,2048]{1,0:T(8,128)S(1)}, f32[512,2048]{1,0:T(8,128)}, u32[]{:S(2)}) copy-start(f32[512,2048]{1,0:T(8,128)} %fusion.25) | copy-start | bytes 12582916
  108.5 11.7 %copy-start.2 = (f32[512,2048]{1,0:T(8,128)S(1)}, f32[512,2048]{1,0:T(8,128)}, u32[]{:S(2)}) copy-start(f32[512,2048]{1,0:T(8,128)} %fusion.10) | copy-start | bytes 12582916
  125.5 18.8 %copy-start.3 = (bf16[256,2048]{1,0:T(8,128)(2,1)S(1)}, bf16[256,2048]{1,0:T(8,128)(2,1)}, u32[]{:S(2)}) copy-start(bf16[256,2048]{1,0:T(8,128)(2,1)} %constant_dynamic-slice_fusion) | copy-start | bytes 3145732

commit v31 on v24

--- a/solution.py
+++ b/solution.py
@@ -81,7 +81,7 @@
     far_mid = jnp.where(here < 2, 2, 1)
     far_end = jnp.where(here < 2, 3, 0)
     own = inputs.reshape(rows, width)
-    half, last = width // 2, width // 8
+    half, last = width // 2, width // 16 * 3
 
     def product(block, owner, first=0):
         part = lax.dynamic_slice_in_dim(base_weight, owner * width + first, block.shape[1], axis=0)

time: 143 us -> 143 us (level)
  no operation moved by 1% of the time
where the time goes in v31:
time: 143 us
  waiting for transfers between devices  59.3 us (41%)
  matrix products  47.6 us (33%)
  starting transfers between devices  22.2 us (16%)
  local copies, waits for them, and re-layouts  9.19 us (6%)
  between operations  4.37 us (3%)
    ppermute x13, waiting for transfers between devices, send(): return lax.ppermute(block, 'tensor', pairs)  59.3 us
    dot_general x6, matrix products, product(): return jnp.dot(block, part, preferred_element_type=F32)  40.6 us
    ppermute x13, starting transfers between devices, send(): return lax.ppermute(block, 'tensor', pairs)  22.2 us
    dot_general x2, matrix products, shrink(): jnp.dot(inputs[c], shrink_table[adapter_ids[c]], preferred_element_type=F32)  3.52 us
  transfers between devices with their start and end apart: 13, of which 7 were waited for; matrix products, arithmetic and copies ran while one was open for 38% of the time, Pallas kernels for 0%

profile of v31, /device:TPU:0, one launch (start us, length us, event | category | flops | bytes accessed | tf_op | source)
XLA Modules:
  0.0 142.8 jit_solution(250904757492129509)
XLA Ops:
  0.0 3.0 %collective-permute-start = (bf16[512,2048]{1,0:T(8,128)(2,1)}, bf16[512,2048]{1,0:T(8,128)(2,1)}, u32[]{:S(2)}, u32[]{:S(2)}) collective-permute-start(bf16[512,2048]{1,0:T(8,128)(2,1)} %bitcast.40), channel_id=1, source_target_pairs={{0,4},{12,8},{4,0},{8,12},{1,5},{13,9},{5,1},{9,13},{2,6},{14,10},... | collective-permute-start | bytes 6291464 | tf_op jit(solution)/shard_map/ppermute | solution.py:69
  3.0 2.3 %slice.62 = bf16[512,1024]{1,0:T(8,128)(2,1)} slice(bf16[512,2048]{1,0:T(8,128)(2,1)} %bitcast.41), slice={[0:512], [0:1024]} | slice | bytes 2097152 | tf_op jit(solution)/shard_map/slice | solution.py:91
  5.3 1.6 %collective-permute-start.2 = (bf16[512,1024]{1,0:T(8,128)(2,1)}, bf16[512,1024]{1,0:T(8,128)(2,1)}, u32[]{:S(2)}, u32[]{:S(2)}) collective-permute-start(bf16[512,1024]{1,0:T(8,128)(2,1)} %slice.62), channel_id=1, source_target_pairs={{4,8},{8,4},{5,9},{9,5},{6,10},{10,6},{7,11},{11,7},{20,24},{24,20... | collective-permute-start | bytes 3145736 | tf_op jit(solution)/shard_map/ppermute | solution.py:69
  7.0 1.4 fusion.65
  12.5 1.8 %fusion.24 = bf16[256,64]{0,1:T(8,128)(2,1)S(1)} fusion(bf16[2,256,2048]{2,1,0:T(8,128)(2,1)} %param.5, bf16[4,2048,64]{1,2,0:T(8,128)(2,1)} %param.7, s32[]{:T(128)S(6)} %select_n.78), kind=kOutput, calls=%fused_computation.21 | convolution fusion | flops 67125248 | bytes 1343492 | tf_op jit(solution)/shard_map/dot_general | solution.py:12
  14.3 1.8 %fusion.23 = bf16[256,64]{0,1:T(8,128)(2,1)S(1)} fusion(bf16[2,256,2048]{2,1,0:T(8,128)(2,1)} %param.5, bf16[4,2048,64]{1,2,0:T(8,128)(2,1)} %param.7, s32[]{:T(128)S(6)} %select_n.77), kind=kOutput, calls=%fused_computation.20 | convolution fusion | flops 67125248 | bytes 1343492 | tf_op jit(solution)/shard_map/dot_general | solution.py:12
  17.2 1.7 %collective-permute-start.4 = (bf16[512,1024]{1,0:T(8,128)(2,1)}, bf16[512,1024]{1,0:T(8,128)(2,1)}, u32[]{:S(2)}, u32[]{:S(2)}) collective-permute-start(bf16[512,1024]{1,0:T(8,128)(2,1)} %slice.53), channel_id=1, source_target_pairs={{4,8},{8,4},{5,9},{9,5},{6,10},{10,6},{7,11},{11,7},{20,24},{24,20... | collective-permute-start | bytes 3145736 | tf_op jit(solution)/shard_map/ppermute | solution.py:69
  18.9 5.5 %collective-permute-start.1 = (bf16[512,64]{0,1:T(8,128)(2,1)S(1)}, bf16[512,64]{0,1:T(8,128)(2,1)S(1)}, u32[]{:S(2)}, u32[]{:S(2)}) collective-permute-start(bf16[512,64]{0,1:T(8,128)(2,1)S(1)} %get-tuple-element.36), channel_id=1, source_target_pairs={{0,4},{12,8},{1,5},{13,9},{2,6},{14,10},{3,7},{15,11},{16,20},{28,... | collective-permute-start | bytes 196616 | tf_op jit(solution)/shard_map/ppermute | solution.py:69
  24.4 9.4 %fusion.11 = f32[512,2048]{1,0:T(8,128)} fusion(bf16[512,2048]{1,0:T(8,128)(2,1)S(1)} %bitcast.43, bf16[8192,2048]{1,0:T(8,128)(2,1)} %param.6, s32[]{:T(128)S(6)} %select_n.76), kind=kOutput, calls=%fused_computation.13 | convolution fusion | flops 4294967296 | bytes 14680068 | tf_op jit(solution)/shard_map/dot_general | solution.py:88
  35.1 14.4 %collective-permute-done.1 = bf16[512,64]{0,1:T(8,128)(2,1)S(1)} collective-permute-done((bf16[512,64]{0,1:T(8,128)(2,1)S(1)}, bf16[512,64]{0,1:T(8,128)(2,1)S(1)}, u32[]{:S(2)}, u32[]{:S(2)}) %collective-permute-start.1) | collective-permute-done | bytes 65568 | tf_op jit(solution)/shard_map/ppermute | solution.py:69
  53.9 9.7 %fusion.14 = f32[512,2048]{1,0:T(8,128)S(1)} fusion(f32[512,2048]{1,0:T(8,128)} %fusion.11, bf16[512,2048]{1,0:T(8,128)(2,1)} %collective-permute-done, bf16[8192,2048]{1,0:T(8,128)(2,1)} %param.6, s32[]{:T(128)S(6)} %select_n.79), kind=kOutput, calls=%fused_computation.15 | convolution fusion | flops 4296015872 | bytes 18874372 | tf_op jit(solution)/shard_map/dot_general | solution.py:88
  65.6 6.6 %collective-permute-done.3 = bf16[512,1024]{1,0:T(8,128)(2,1)S(1)} collective-permute-done((bf16[512,1024]{1,0:T(8,128)(2,1)}, bf16[512,1024]{1,0:T(8,128)(2,1)S(1)}, u32[]{:S(2)}, u32[]{:S(2)}) %collective-permute-start.3) | collective-permute-done | bytes 1048608 | tf_op jit(solution)/shard_map/ppermute | solution.py:69
  72.2 6.5 %fusion.17 = f32[512,2048]{1,0:T(8,128)} fusion(f32[512,2048]{1,0:T(8,128)S(1)} %fusion.14, bf16[8192,2048]{1,0:T(8,128)(2,1)} %param.6, s32[]{:T(128)S(6)} %select_n.83, bf16[512,1024]{1,0:T(8,128)(2,1)S(1)} %collective-permute-done.3, bf16[512,1024]{1,0:T(8,128)(2,1)} %collective-permute-done.2, pred[]{:T(512)S(6)} %or.3), kind=kOutput, calls=%fused_computation.16 | convolution fusion | flops 2149056512 | bytes 14680069 | tf_op jit(solution)/shard_map/dot_general | solution.py:88
  81.4 13.3 %collective-permute-done.5 = bf16[512,1024]{1,0:T(8,128)(2,1)S(1)} collective-permute-done((bf16[512,1024]{1,0:T(8,128)(2,1)}, bf16[512,1024]{1,0:T(8,128)(2,1)S(1)}, u32[]{:S(2)}, u32[]{:S(2)}) %collective-permute-start.5) | collective-permute-done | bytes 1048608 | tf_op jit(solution)/shard_map/ppermute | solution.py:69
  94.7 6.5 %fusion.7 = f32[512,2048]{1,0:T(8,128)} fusion(bf16[8192,2048]{1,0:T(8,128)(2,1)} %param.6, s32[]{:T(128)S(6)} %select_n.85, bf16[512,1024]{1,0:T(8,128)(2,1)S(1)} %collective-permute-done.5, bf16[512,1024]{1,0:T(8,128)(2,1)} %collective-permute-done.4, pred[]{:T(512)S(6)} %or.3), kind=kOutput, calls=%fused_computation.9 | convolution fusion | flops 2148007936 | bytes 10485765 | tf_op jit(solution)/shard_map/dot_general | solution.py:88
  101.2 1.7 %constant_dynamic-slice_fusion = bf16[384,2048]{1,0:T(8,128)(2,1)S(1)} fusion(bf16[8192,2048]{1,0:T(8,128)(2,1)} %param.6, s32[]{:T(128)S(6)} %select_n.89), kind=kLoop, calls=%fused_computation.58 | loop fusion | bytes 3145732 | tf_op jit(solution)/shard_map/dynamic_slice | solution.py:116
  103.0 1.6 %collective-permute-start.11 = (bf16[512,640]{1,0:T(8,128)(2,1)S(1)}, bf16[512,640]{1,0:T(8,128)(2,1)S(1)}, u32[]{:S(2)}, u32[]{:S(2)}) collective-permute-start(bf16[512,640]{1,0:T(8,128)(2,1)S(1)} %slice.60), channel_id=1, source_target_pairs={{4,0},{8,12},{5,1},{9,13},{6,2},{10,14},{7,3},{11,15},{20,16},{24,... | collective-permute-start | bytes 1966088 | tf_op jit(solution)/shard_map/ppermute | solution.py:69
  104.6 1.5 %collective-permute-start.12 = (bf16[512,384]{1,0:T(8,128)(2,1)S(1)}, bf16[512,384]{1,0:T(8,128)(2,1)S(1)}, u32[]{:S(2)}, u32[]{:S(2)}) collective-permute-start(bf16[512,384]{1,0:T(8,128)(2,1)S(1)} %slice.61), channel_id=1, source_target_pairs={{4,0},{8,12},{5,1},{9,13},{6,2},{10,14},{7,3},{11,15},{20,16},{24,... | collective-permute-start | bytes 1179656 | tf_op jit(solution)/shard_map/ppermute | solution.py:69
  107.0 12.3 %collective-permute-done.10 = bf16[512,1024]{1,0:T(8,128)(2,1)} collective-permute-done((bf16[512,1024]{1,0:T(8,128)(2,1)S(1)}, bf16[512,1024]{1,0:T(8,128)(2,1)}, u32[]{:S(2)}, u32[]{:S(2)}) %collective-permute-start.10) | collective-permute-done | bytes 1048608 | tf_op jit(solution)/shard_map/ppermute | solution.py:69
  119.3 5.0 %fusion.4 = f32[512,2048]{1,0:T(8,128)S(1)} fusion(f32[256,2048]{1,0:T(8,128)S(1)} %fusion.39, f32[256,2048]{1,0:T(8,128)S(1)} %fusion.41, f32[512,2048]{1,0:T(8,128)S(1)} %copy-done.1, f32[512,2048]{1,0:T(8,128)S(1)} %copy-done.2, bf16[8192,2048]{1,0:T(8,128)(2,1)} %param.6, s32[]{:T(128)S(6)} %select_n.91, bf16[512,1024]{1,0:T(8,128)(2,1)} %collective-permute-done.10, ...), kind=kOutput, calls=%fused_computation.5 | convolution fusion | flops 2152202240 | bytes 23068676 | tf_op jit(solution)/shard_map/dot_general | solution.py:88
  124.3 9.0 %collective-permute-done.11 = bf16[512,640]{1,0:T(8,128)(2,1)S(1)} collective-permute-done((bf16[512,640]{1,0:T(8,128)(2,1)S(1)}, bf16[512,640]{1,0:T(8,128)(2,1)S(1)}, u32[]{:S(2)}, u32[]{:S(2)}) %collective-permute-start.11) | collective-permute-done | bytes 655392 | tf_op jit(solution)/shard_map/ppermute | solution.py:69
  133.3 3.5 %convolution_add_fusion = f32[512,2048]{1,0:T(8,128)S(1)} fusion(f32[512,2048]{1,0:T(8,128)S(1)} %fusion.4, bf16[8192,2048]{1,0:T(8,128)(2,1)} %param.6, s32[]{:T(128)S(6)} %select_n.94, bf16[512,640]{1,0:T(8,128)(2,1)S(1)} %collective-permute-done.11, pred[]{:T(512)S(6)} %or.3, bf16[512,1024]{1,0:T(8,128)(2,1)S(1)} %collective-permute-done.9), kind=kOutput, calls=%fused_computation.14 | convolution fusion | flops 1343553536 | bytes 12320773 | tf_op jit(solution)/shard_map/dot_general | solution.py:88
  136.8 3.4 %collective-permute-done.12 = bf16[512,384]{1,0:T(8,128)(2,1)S(1)} collective-permute-done((bf16[512,384]{1,0:T(8,128)(2,1)S(1)}, bf16[512,384]{1,0:T(8,128)(2,1)S(1)}, u32[]{:S(2)}, u32[]{:S(2)}) %collective-permute-start.12) | collective-permute-done | bytes 393248 | tf_op jit(solution)/shard_map/ppermute | solution.py:69
  140.2 2.6 %add_convert_fusion = bf16[512,2048]{1,0:T(8,128)(2,1)} fusion(f32[512,2048]{1,0:T(8,128)S(1)} %convolution_add_fusion, bf16[384,2048]{1,0:T(8,128)(2,1)S(1)} %constant_dynamic-slice_fusion, bf16[512,384]{1,0:T(8,128)(2,1)S(1)} %collective-permute-done.12, pred[]{:T(512)S(6)} %or.3, bf16[512,1024]{1,0:T(8,128)(2,1)S(1)} %collective-permute-done.9), kind=kOutput, calls=%fused_computation.6 | convolution fusion | flops 807600128 | bytes 8650753 | tf_op jit(solution)/shard_map/dot_general | solution.py:126
  (33 shorter events, 12.4 us)
Async XLA Ops:
  0.0 106.1 %copy-start = (bf16[4,64,2048]{2,1,0:T(8,128)(2,1)S(1)}, bf16[4,64,2048]{2,1,0:T(8,128)(2,1)}, u32[]{:S(2)}) copy-start(bf16[4,64,2048]{2,1,0:T(8,128)(2,1)} %param.8) | copy-start | bytes 3145732
  0.0 16.0 %copy-start.3 = (bf16[2,256,2048]{2,1,0:T(8,128)(2,1)S(1)}, bf16[2,256,2048]{2,1,0:T(8,128)(2,1)}, u32[]{:S(2)}) copy-start(bf16[2,256,2048]{2,1,0:T(8,128)(2,1)} %param.5) | copy-start | bytes 6291460
  0.0 49.8 %collective-permute-start = (bf16[512,2048]{1,0:T(8,128)(2,1)}, bf16[512,2048]{1,0:T(8,128)(2,1)}, u32[]{:S(2)}, u32[]{:S(2)}) collective-permute-start(bf16[512,2048]{1,0:T(8,128)(2,1)} %bitcast.40), channel_id=1, source_target_pairs={{0,4},{12,8},{4,0},{8,12},{1,5},{13,9},{5,1},{9,13},{2,6},{14,10},... | collective-permute-start | bytes 6291464 | tf_op jit(solution)/shard_map/ppermute | solution.py:69
  5.3 28.5 %collective-permute-start.2 = (bf16[512,1024]{1,0:T(8,128)(2,1)}, bf16[512,1024]{1,0:T(8,128)(2,1)}, u32[]{:S(2)}, u32[]{:S(2)}) collective-permute-start(bf16[512,1024]{1,0:T(8,128)(2,1)} %slice.62), channel_id=1, source_target_pairs={{4,8},{8,4},{5,9},{9,5},{6,10},{10,6},{7,11},{11,7},{20,24},{24,20... | collective-permute-start | bytes 3145736 | tf_op jit(solution)/shard_map/ppermute | solution.py:69
  17.2 35.4 %collective-permute-start.4 = (bf16[512,1024]{1,0:T(8,128)(2,1)}, bf16[512,1024]{1,0:T(8,128)(2,1)}, u32[]{:S(2)}, u32[]{:S(2)}) collective-permute-start(bf16[512,1024]{1,0:T(8,128)(2,1)} %slice.53), channel_id=1, source_target_pairs={{4,8},{8,4},{5,9},{9,5},{6,10},{10,6},{7,11},{11,7},{20,24},{24,20... | collective-permute-start | bytes 3145736 | tf_op jit(solution)/shard_map/ppermute | solution.py:69
  18.9 30.7 %collective-permute-start.1 = (bf16[512,64]{0,1:T(8,128)(2,1)S(1)}, bf16[512,64]{0,1:T(8,128)(2,1)S(1)}, u32[]{:S(2)}, u32[]{:S(2)}) collective-permute-start(bf16[512,64]{0,1:T(8,128)(2,1)S(1)} %get-tuple-element.36), channel_id=1, source_target_pairs={{0,4},{12,8},{1,5},{13,9},{2,6},{14,10},{3,7},{15,11},{16,20},{28,... | collective-permute-start | bytes 196616 | tf_op jit(solution)/shard_map/ppermute | solution.py:69
  33.8 38.4 %collective-permute-start.3 = (bf16[512,1024]{1,0:T(8,128)(2,1)}, bf16[512,1024]{1,0:T(8,128)(2,1)S(1)}, u32[]{:S(2)}, u32[]{:S(2)}) collective-permute-start(bf16[512,1024]{1,0:T(8,128)(2,1)} %collective-permute-done.2), channel_id=1, source_target_pairs={{4,0},{8,12},{5,1},{9,13},{6,2},{10,14},{7,3},{11,15},{20,16},{24,... | collective-permute-start | bytes 3145736 | tf_op jit(solution)/shard_map/ppermute | solution.py:69
  51.1 12.4 %collective-permute-start.6 = (bf16[512,1024]{1,0:T(8,128)(2,1)S(1)}, bf16[512,1024]{1,0:T(8,128)(2,1)S(1)}, u32[]{:S(2)}, u32[]{:S(2)}) collective-permute-start(bf16[512,1024]{1,0:T(8,128)(2,1)S(1)} %slice.54), channel_id=1, source_target_pairs={{4,8},{8,4},{5,9},{9,5},{6,10},{10,6},{7,11},{11,7},{20,24},{24,20... | collective-permute-start | bytes 3145736 | tf_op jit(solution)/shard_map/ppermute | solution.py:69
  51.9 26.9 %collective-permute-start.7 = (bf16[2,512,64]{1,2,0:T(8,128)(2,1)S(1)}, bf16[2,512,64]{1,2,0:T(8,128)(2,1)S(1)}, u32[]{:S(2)}, u32[]{:S(2)}) collective-permute-start(bf16[2,512,64]{1,2,0:T(8,128)(2,1)S(1)} %pad_maximum_fusion), channel_id=1, source_target_pairs={{4,8},{8,4},{5,9},{9,5},{6,10},{10,6},{7,11},{11,7},{20,24},{24,20... | collective-permute-start | bytes 393224 | tf_op jit(solution)/shard_map/ppermute | solution.py:69
  52.6 42.1 %collective-permute-start.5 = (bf16[512,1024]{1,0:T(8,128)(2,1)}, bf16[512,1024]{1,0:T(8,128)(2,1)S(1)}, u32[]{:S(2)}, u32[]{:S(2)}) collective-permute-start(bf16[512,1024]{1,0:T(8,128)(2,1)} %collective-permute-done.4), channel_id=1, source_target_pairs={{4,0},{8,12},{5,1},{9,13},{6,2},{10,14},{7,3},{11,15},{20,16},{24,... | collective-permute-start | bytes 3145736 | tf_op jit(solution)/shard_map/ppermute | solution.py:69
  64.9 36.4 %collective-permute-start.9 = (bf16[512,1024]{1,0:T(8,128)(2,1)S(1)}, bf16[512,1024]{1,0:T(8,128)(2,1)S(1)}, u32[]{:S(2)}, u32[]{:S(2)}) collective-permute-start(bf16[512,1024]{1,0:T(8,128)(2,1)S(1)} %slice.57), channel_id=1, source_target_pairs={{4,8},{8,4},{5,9},{9,5},{6,10},{10,6},{7,11},{11,7},{20,24},{24,20... | collective-permute-start | bytes 3145736 | tf_op jit(solution)/shard_map/ppermute | solution.py:69
  78.8 22.4 %collective-permute-start.8 = (bf16[512,64]{0,1:T(8,128)(2,1)S(1)}, bf16[512,64]{0,1:T(8,128)(2,1)S(1)}, u32[]{:S(2)}, u32[]{:S(2)}) collective-permute-start(bf16[512,64]{0,1:T(8,128)(2,1)S(1)} %fusion.49), channel_id=1, source_target_pairs={{4,0},{8,12},{5,1},{9,13},{6,2},{10,14},{7,3},{11,15},{20,16},{24,... | collective-permute-start | bytes 196616 | tf_op jit(solution)/shard_map/ppermute | solution.py:69
  80.1 39.2 %collective-permute-start.10 = (bf16[512,1024]{1,0:T(8,128)(2,1)S(1)}, bf16[512,1024]{1,0:T(8,128)(2,1)}, u32[]{:S(2)}, u32[]{:S(2)}) collective-permute-start(bf16[512,1024]{1,0:T(8,128)(2,1)S(1)} %collective-permute-done.6), channel_id=1, source_target_pairs={{4,0},{8,12},{5,1},{9,13},{6,2},{10,14},{7,3},{11,15},{20,16},{24,... | collective-permute-start | bytes 3145736 | tf_op jit(solution)/shard_map/ppermute | solution.py:69
  101.2 18.1 %copy-start.2 = (f32[512,2048]{1,0:T(8,128)S(1)}, f32[512,2048]{1,0:T(8,128)}, u32[]{:S(2)}) copy-start(f32[512,2048]{1,0:T(8,128)} %fusion.7) | copy-start | bytes 12582916
  102.9 16.4 %copy-start.1 = (f32[512,2048]{1,0:T(8,128)S(1)}, f32[512,2048]{1,0:T(8,128)}, u32[]{:S(2)}) copy-start(f32[512,2048]{1,0:T(8,128)} %fusion.17) | copy-start | bytes 12582916
  103.0 30.2 %collective-permute-start.11 = (bf16[512,640]{1,0:T(8,128)(2,1)S(1)}, bf16[512,640]{1,0:T(8,128)(2,1)S(1)}, u32[]{:S(2)}, u32[]{:S(2)}) collective-permute-start(bf16[512,640]{1,0:T(8,128)(2,1)S(1)} %slice.60), channel_id=1, source_target_pairs={{4,0},{8,12},{5,1},{9,13},{6,2},{10,14},{7,3},{11,15},{20,16},{24,... | collective-permute-start | bytes 1966088 | tf_op jit(solution)/shard_map/ppermute | solution.py:69
  104.6 35.6 %collective-permute-start.12 = (bf16[512,384]{1,0:T(8,128)(2,1)S(1)}, bf16[512,384]{1,0:T(8,128)(2,1)S(1)}, u32[]{:S(2)}, u32[]{:S(2)}) collective-permute-start(bf16[512,384]{1,0:T(8,128)(2,1)S(1)} %slice.61), channel_id=1, source_target_pairs={{4,0},{8,12},{5,1},{9,13},{6,2},{10,14},{7,3},{11,15},{20,16},{24,... | collective-permute-start | bytes 1179656 | tf_op jit(solution)/shard_map/ppermute | solution.py:69

commit v32 on v29

--- a/solution.py
+++ b/solution.py
@@ -87,20 +87,18 @@
         part = lax.dynamic_slice_in_dim(base_weight, owner * width + first, block.shape[1], axis=0)
         return jnp.dot(block, part, preferred_element_type=F32)
 
+    mid = send(own, ACROSS)
     mate = send(own, SWAP)
     partial = shrink(inputs, shrink_table, adapter_ids)
-    mid = [send(after(own, partial)[:, :half], ACROSS)]
     mate_partial = send(partial, INWARD)
     total = product(own, here)
-    mid.append(send(after(own, total)[:, half:], ACROSS))
 
-    mid_out = [send(after(mid[0], total), OUTWARD)]
-    mate, mate_partial = lax.optimization_barrier((mate, mate_partial, mid[0], total))[:2]
+    mid_out = send(after(mid, total), OUTWARD)
+    mate, mate_partial = lax.optimization_barrier((mate, mate_partial, mid, total))[:2]
     both = send(jnp.stack([partial, mate_partial]), ACROSS)
     first = mate[:, :half]
     end = [send(first, ACROSS)]
     end.append(send(after(mate, end[0])[:, half:], ACROSS))
-    mid_out.append(send(after(mid[1], first), OUTWARD))
     total = total + product(mate, here ^ 1)
 
     end[0], both = lax.optimization_barrier((end[0], both, total))[:2]
@@ -109,15 +107,14 @@
         partial.astype(F32) + mate_partial.astype(F32) + both[0].astype(F32) + both[1].astype(F32)
     ).astype(BF16)
     shrunk = jnp.where(is_end, send(shrunk, OUTWARD), shrunk)
-    total = total + product(jnp.where(is_end, mid_out[0], mid[0]), far_mid)
 
     late = after(end[1], total)
     begin = (after(far_end, late) + 1) * width - last
     last_rows = lax.dynamic_slice_in_dim(base_weight, begin, last, axis=0)
     late, last_rows = lax.optimization_barrier((late, last_rows))
-    shrunk = after(shrunk, late)
+    mid_out, shrunk = lax.optimization_barrier((mid_out, shrunk, late))[:2]
     end_out += [send(late[:, : half - last], OUTWARD), send(late[:, half - last :], OUTWARD)]
-    total = total + product(jnp.where(is_end, mid_out[1], mid[1]), far_mid, half)
+    total = total + product(jnp.where(is_end, mid_out, mid), far_mid)
     total = total + jnp.concatenate(expand(shrunk, expand_table, adapter_ids))
     total = total + product(jnp.where(is_end, end_out[0], end[0]), far_end)
     block = jnp.where(is_end, after(end_out[1], total), late[:, : half - last])

time: 150 us -> 154 us (1.027)
  waiting for transfers between devices: 66.8 us -> 81.2 us
  local copies, waits for them, and re-layouts: 8.94 us -> 4.98 us
  starting transfers between devices: 22.3 us -> 18.6 us
  matrix products: 47.2 us -> 44.6 us
    ppermute x13 -> x11, waiting for transfers between devices: 66.8 us -> 81.2 us  [send(): return lax.ppermute(block, 'tensor', pairs)]
    ppermute x13 -> x11, starting transfers between devices: 22.3 us -> 18.6 us  [send(): return lax.ppermute(block, 'tensor', pairs)]
    slice x2 -> x0, local copies, waits for them, and re-layouts: 3.39 us -> none  [the longest x1 2.26 us: line(): mid = [send(after(own, partial)[:, :half], ACROSS)]]
    dot_general x6 -> x5, matrix products: 40.8 us -> 38.1 us  [product(): return jnp.dot(block, part, preferred_element_type=F32)]
  transfers between devices with their start and end apart: 13 -> 11, of which waited for: 7 -> 4; matrix products, arithmetic and copies ran while one was open for 36% -> 30% of each run, Pallas kernels for 0% -> 0%
where the time goes in v32:
time: 154 us
  waiting for transfers between devices  81.2 us (53%)
  matrix products  44.6 us (29%)
  starting transfers between devices  18.6 us (12%)
  local copies, waits for them, and re-layouts  4.98 us (3%)
  between operations  4.08 us (3%)
    ppermute x11, waiting for transfers between devices, send(): return lax.ppermute(block, 'tensor', pairs)  81.2 us
    dot_general x5, matrix products, product(): return jnp.dot(block, part, preferred_element_type=F32)  38.1 us
    ppermute x11, starting transfers between devices, send(): return lax.ppermute(block, 'tensor', pairs)  18.6 us
    dot_general x2, matrix products, shrink(): jnp.dot(inputs[c], shrink_table[adapter_ids[c]], preferred_element_type=F32)  3.52 us
  transfers between devices with their start and end apart: 11, of which 4 were waited for; matrix products, arithmetic and copies ran while one was open for 30% of the time, Pallas kernels for 0%

profile of v32, /device:TPU:0, one launch (start us, length us, event | category | flops | bytes accessed | tf_op | source)
XLA Modules:
  0.0 153.5 jit_solution(13491734004975569978)
XLA Ops:
  0.0 2.1 %collective-permute-start.2 = (bf16[512,2048]{1,0:T(8,128)(2,1)}, bf16[512,2048]{1,0:T(8,128)(2,1)}, u32[]{:S(2)}, u32[]{:S(2)}) collective-permute-start(bf16[512,2048]{1,0:T(8,128)(2,1)} %bitcast.41), channel_id=1, source_target_pairs={{4,8},{8,4},{5,9},{9,5},{6,10},{10,6},{7,11},{11,7},{20,24},{24,20... | collective-permute-start | bytes 6291464 | tf_op jit(solution)/shard_map/ppermute | solution.py:69
  2.1 4.6 %collective-permute-start = (bf16[512,2048]{1,0:T(8,128)(2,1)}, bf16[512,2048]{1,0:T(8,128)(2,1)S(1)}, u32[]{:S(2)}, u32[]{:S(2)}) collective-permute-start(bf16[512,2048]{1,0:T(8,128)(2,1)} %bitcast.42), channel_id=1, source_target_pairs={{0,4},{12,8},{4,0},{8,12},{1,5},{13,9},{5,1},{9,13},{2,6},{14,10},... | collective-permute-start | bytes 6291464 | tf_op jit(solution)/shard_map/ppermute | solution.py:69
  6.7 1.3 fusion.61
  11.9 1.8 %fusion.24 = bf16[256,64]{0,1:T(8,128)(2,1)S(1)} fusion(bf16[2,256,2048]{2,1,0:T(8,128)(2,1)} %param.5, bf16[4,2048,64]{1,2,0:T(8,128)(2,1)} %param.7, s32[]{:T(128)S(6)} %select_n.74), kind=kOutput, calls=%fused_computation.20 | convolution fusion | flops 67125248 | bytes 1343492 | tf_op jit(solution)/shard_map/dot_general | solution.py:12
  13.7 1.8 %fusion.25 = bf16[256,64]{0,1:T(8,128)(2,1)S(1)} fusion(bf16[2,256,2048]{2,1,0:T(8,128)(2,1)} %param.5, bf16[4,2048,64]{1,2,0:T(8,128)(2,1)} %param.7, s32[]{:T(128)S(6)} %select_n.75), kind=kOutput, calls=%fused_computation.21 | convolution fusion | flops 67125248 | bytes 1343492 | tf_op jit(solution)/shard_map/dot_general | solution.py:12
  15.4 1.9 %collective-permute-start.1 = (bf16[512,64]{0,1:T(8,128)(2,1)S(1)}, bf16[512,64]{0,1:T(8,128)(2,1)S(1)}, u32[]{:S(2)}, u32[]{:S(2)}) collective-permute-start(bf16[512,64]{0,1:T(8,128)(2,1)S(1)} %get-tuple-element.34), channel_id=1, source_target_pairs={{0,4},{12,8},{1,5},{13,9},{2,6},{14,10},{3,7},{15,11},{16,20},{28,... | collective-permute-start | bytes 196616 | tf_op jit(solution)/shard_map/ppermute | solution.py:69
  17.4 10.5 %fusion.9 = f32[512,2048]{1,0:T(8,128)} fusion(bf16[512,2048]{1,0:T(8,128)(2,1)} %bitcast.43, bf16[8192,2048]{1,0:T(8,128)(2,1)} %param.6, s32[]{:T(128)S(6)} %select_n.73), kind=kOutput, calls=%fused_computation.11 | convolution fusion | flops 4294967296 | bytes 14680068 | tf_op jit(solution)/shard_map/dot_general | solution.py:88
  27.9 25.1 %collective-permute-done.1 = bf16[512,64]{0,1:T(8,128)(2,1)S(1)} collective-permute-done((bf16[512,64]{0,1:T(8,128)(2,1)S(1)}, bf16[512,64]{0,1:T(8,128)(2,1)S(1)}, u32[]{:S(2)}, u32[]{:S(2)}) %collective-permute-start.1) | collective-permute-done | bytes 65568 | tf_op jit(solution)/shard_map/ppermute | solution.py:69
  52.9 1.2 slice.46
  54.1 1.7 %collective-permute-start.4 = (bf16[512,1024]{1,0:T(8,128)(2,1)}, bf16[512,1024]{1,0:T(8,128)(2,1)}, u32[]{:S(2)}, u32[]{:S(2)}) collective-permute-start(bf16[512,1024]{1,0:T(8,128)(2,1)} %slice.46), channel_id=1, source_target_pairs={{4,8},{8,4},{5,9},{9,5},{6,10},{10,6},{7,11},{11,7},{20,24},{24,20... | collective-permute-start | bytes 3145736 | tf_op jit(solution)/shard_map/ppermute | solution.py:69
  55.8 1.3 collective-permute-start.3
  59.6 11.6 %fusion.14 = f32[512,2048]{1,0:T(8,128)} fusion(f32[512,2048]{1,0:T(8,128)} %fusion.9, bf16[512,2048]{1,0:T(8,128)(2,1)} %copy-done.3, bf16[8192,2048]{1,0:T(8,128)(2,1)} %param.6, s32[]{:T(128)S(6)} %select_n.76), kind=kOutput, calls=%fused_computation.14 | convolution fusion | flops 4296015872 | bytes 18874372 | tf_op jit(solution)/shard_map/dot_general | solution.py:88
  71.3 1.3 collective-permute-start.6
  72.6 1.3 collective-permute-start.8
  73.9 34.4 %collective-permute-done.6 = bf16[512,64]{0,1:T(8,128)(2,1)S(1)} collective-permute-done((bf16[512,64]{0,1:T(8,128)(2,1)S(1)}, bf16[512,64]{0,1:T(8,128)(2,1)S(1)}, u32[]{:S(2)}, u32[]{:S(2)}) %collective-permute-start.6) | collective-permute-done | bytes 65568 | tf_op jit(solution)/shard_map/ppermute | solution.py:69
  108.4 1.3 constant_dynamic-slice_fusion
  110.8 1.6 %collective-permute-start.9 = (bf16[512,768]{1,0:T(8,128)(2,1)S(1)}, bf16[512,768]{1,0:T(8,128)(2,1)S(1)}, u32[]{:S(2)}, u32[]{:S(2)}) collective-permute-start(bf16[512,768]{1,0:T(8,128)(2,1)S(1)} %slice.52), channel_id=1, source_target_pairs={{4,0},{8,12},{5,1},{9,13},{6,2},{10,14},{7,3},{11,15},{20,16},{24,... | collective-permute-start | bytes 2359304 | tf_op jit(solution)/shard_map/ppermute | solution.py:69
  112.3 1.5 collective-permute-start.10
  113.8 7.6 %fusion = f32[512,2048]{1,0:T(8,128)S(1)} fusion(bf16[8192,2048]{1,0:T(8,128)(2,1)} %param.6, s32[]{:T(128)S(6)} %select_n.84, bf16[512,2048]{1,0:T(8,128)(2,1)} %collective-permute-done.3, bf16[512,2048]{1,0:T(8,128)(2,1)} %collective-permute-done.2, pred[]{:T(512)S(6)} %or.3), kind=kOutput, calls=%fused_computation | convolution fusion | flops 4296015872 | bytes 16777220 | tf_op jit(solution)/shard_map/dot_general | solution.py:88
  121.4 9.4 %collective-permute-done.8 = bf16[512,1024]{1,0:T(8,128)(2,1)S(1)} collective-permute-done((bf16[512,1024]{1,0:T(8,128)(2,1)}, bf16[512,1024]{1,0:T(8,128)(2,1)S(1)}, u32[]{:S(2)}, u32[]{:S(2)}) %collective-permute-start.8) | collective-permute-done | bytes 1048608 | tf_op jit(solution)/shard_map/ppermute | solution.py:69
  130.8 4.6 %fusion.6 = f32[512,2048]{1,0:T(8,128)S(1)} fusion(f32[256,2048]{1,0:T(8,128)S(1)} %fusion.34, f32[256,2048]{1,0:T(8,128)S(1)} %fusion.36, f32[512,2048]{1,0:T(8,128)S(1)} %copy-done.2, f32[512,2048]{1,0:T(8,128)S(1)} %fusion, bf16[8192,2048]{1,0:T(8,128)(2,1)} %param.6, s32[]{:T(128)S(6)} %select_n.87, bf16[512,1024]{1,0:T(8,128)(2,1)S(1)} %collective-permute-done.8, ...), kind=kOutput, calls=%fused_computation.7 | convolution fusion | flops 2152202240 | bytes 23068676 | tf_op jit(solution)/shard_map/dot_general | solution.py:88
  135.5 12.2 %collective-permute-done.9 = bf16[512,768]{1,0:T(8,128)(2,1)S(1)} collective-permute-done((bf16[512,768]{1,0:T(8,128)(2,1)S(1)}, bf16[512,768]{1,0:T(8,128)(2,1)S(1)}, u32[]{:S(2)}, u32[]{:S(2)}) %collective-permute-start.9) | collective-permute-done | bytes 786464 | tf_op jit(solution)/shard_map/ppermute | solution.py:69
  147.7 3.8 %fusion.17 = f32[512,2048]{1,0:T(8,128)S(1)} fusion(f32[512,2048]{1,0:T(8,128)S(1)} %fusion.6, bf16[8192,2048]{1,0:T(8,128)(2,1)} %param.6, s32[]{:T(128)S(6)} %select_n.90, bf16[512,768]{1,0:T(8,128)(2,1)S(1)} %collective-permute-done.9, pred[]{:T(512)S(6)} %or.3, bf16[512,1024]{1,0:T(8,128)(2,1)S(1)} %collective-permute-done.7), kind=kOutput, calls=%fused_computation.15 | convolution fusion | flops 1612054528 | bytes 13107205 | tf_op jit(solution)/shard_map/dot_general | solution.py:88
  151.5 2.0 %add_convert_fusion = bf16[512,2048]{1,0:T(8,128)(2,1)} fusion(f32[512,2048]{1,0:T(8,128)S(1)} %fusion.17, bf16[256,2048]{1,0:T(8,128)(2,1)S(1)} %constant_dynamic-slice_fusion, bf16[512,256]{1,0:T(8,128)(2,1)S(1)} %collective-permute-done.10, pred[]{:T(512)S(6)} %or.3, bf16[512,1024]{1,0:T(8,128)(2,1)S(1)} %collective-permute-done.7), kind=kOutput, calls=%fused_computation.8 | convolution fusion | flops 539099136 | bytes 7864321 | tf_op jit(solution)/shard_map/dot_general | solution.py:123
  (26 shorter events, 3.6 us)
Async XLA Ops:
  0.0 109.7 %copy-start = (bf16[4,64,2048]{2,1,0:T(8,128)(2,1)S(1)}, bf16[4,64,2048]{2,1,0:T(8,128)(2,1)}, u32[]{:S(2)}) copy-start(bf16[4,64,2048]{2,1,0:T(8,128)(2,1)} %param.8) | copy-start | bytes 3145732
  0.0 52.9 %collective-permute-start.2 = (bf16[512,2048]{1,0:T(8,128)(2,1)}, bf16[512,2048]{1,0:T(8,128)(2,1)}, u32[]{:S(2)}, u32[]{:S(2)}) collective-permute-start(bf16[512,2048]{1,0:T(8,128)(2,1)} %bitcast.41), channel_id=1, source_target_pairs={{4,8},{8,4},{5,9},{9,5},{6,10},{10,6},{7,11},{11,7},{20,24},{24,20... | collective-permute-start | bytes 6291464 | tf_op jit(solution)/shard_map/ppermute | solution.py:69
  2.1 50.8 %collective-permute-start = (bf16[512,2048]{1,0:T(8,128)(2,1)}, bf16[512,2048]{1,0:T(8,128)(2,1)S(1)}, u32[]{:S(2)}, u32[]{:S(2)}) collective-permute-start(bf16[512,2048]{1,0:T(8,128)(2,1)} %bitcast.42), channel_id=1, source_target_pairs={{0,4},{12,8},{4,0},{8,12},{1,5},{13,9},{5,1},{9,13},{2,6},{14,10},... | collective-permute-start | bytes 6291464 | tf_op jit(solution)/shard_map/ppermute | solution.py:69
  15.4 37.5 %collective-permute-start.1 = (bf16[512,64]{0,1:T(8,128)(2,1)S(1)}, bf16[512,64]{0,1:T(8,128)(2,1)S(1)}, u32[]{:S(2)}, u32[]{:S(2)}) collective-permute-start(bf16[512,64]{0,1:T(8,128)(2,1)S(1)} %get-tuple-element.34), channel_id=1, source_target_pairs={{0,4},{12,8},{1,5},{13,9},{2,6},{14,10},{3,7},{15,11},{16,20},{28,... | collective-permute-start | bytes 196616 | tf_op jit(solution)/shard_map/ppermute | solution.py:69
  52.9 4.9 %copy-start.3 = (bf16[512,2048]{1,0:T(8,128)(2,1)}, bf16[512,2048]{1,0:T(8,128)(2,1)S(1)}, u32[]{:S(2)}) copy-start(bf16[512,2048]{1,0:T(8,128)(2,1)S(1)} %collective-permute-done) | copy-start | bytes 6291460
  54.1 3.7 %collective-permute-start.4 = (bf16[512,1024]{1,0:T(8,128)(2,1)}, bf16[512,1024]{1,0:T(8,128)(2,1)}, u32[]{:S(2)}, u32[]{:S(2)}) collective-permute-start(bf16[512,1024]{1,0:T(8,128)(2,1)} %slice.46), channel_id=1, source_target_pairs={{4,8},{8,4},{5,9},{9,5},{6,10},{10,6},{7,11},{11,7},{20,24},{24,20... | collective-permute-start | bytes 3145736 | tf_op jit(solution)/shard_map/ppermute | solution.py:69
  55.8 53.9 %collective-permute-start.3 = (bf16[512,2048]{1,0:T(8,128)(2,1)}, bf16[512,2048]{1,0:T(8,128)(2,1)}, u32[]{:S(2)}, u32[]{:S(2)}) collective-permute-start(bf16[512,2048]{1,0:T(8,128)(2,1)} %collective-permute-done.2), channel_id=1, source_target_pairs={{4,0},{8,12},{5,1},{9,13},{6,2},{10,14},{7,3},{11,15},{20,16},{24,... | collective-permute-start | bytes 6291464 | tf_op jit(solution)/shard_map/ppermute | solution.py:69
  57.1 14.1 %collective-permute-start.5 = (bf16[2,512,64]{1,2,0:T(8,128)(2,1)S(1)}, bf16[2,512,64]{1,2,0:T(8,128)(2,1)S(1)}, u32[]{:S(2)}, u32[]{:S(2)}) collective-permute-start(bf16[2,512,64]{1,2,0:T(8,128)(2,1)S(1)} %pad_maximum_fusion), channel_id=1, source_target_pairs={{4,8},{8,4},{5,9},{9,5},{6,10},{10,6},{7,11},{11,7},{20,24},{24,20... | collective-permute-start | bytes 393224 | tf_op jit(solution)/shard_map/ppermute | solution.py:69
  58.9 49.5 %collective-permute-start.7 = (bf16[512,1024]{1,0:T(8,128)(2,1)}, bf16[512,1024]{1,0:T(8,128)(2,1)S(1)}, u32[]{:S(2)}, u32[]{:S(2)}) collective-permute-start(bf16[512,1024]{1,0:T(8,128)(2,1)} %slice.49), channel_id=1, source_target_pairs={{4,8},{8,4},{5,9},{9,5},{6,10},{10,6},{7,11},{11,7},{20,24},{24,20... | collective-permute-start | bytes 3145736 | tf_op jit(solution)/shard_map/ppermute | solution.py:69
  71.3 37.1 %collective-permute-start.6 = (bf16[512,64]{0,1:T(8,128)(2,1)S(1)}, bf16[512,64]{0,1:T(8,128)(2,1)S(1)}, u32[]{:S(2)}, u32[]{:S(2)}) collective-permute-start(bf16[512,64]{0,1:T(8,128)(2,1)S(1)} %fusion.46), channel_id=1, source_target_pairs={{4,0},{8,12},{5,1},{9,13},{6,2},{10,14},{7,3},{11,15},{20,16},{24,... | collective-permute-start | bytes 196616 | tf_op jit(solution)/shard_map/ppermute | solution.py:69
  72.6 58.2 %collective-permute-start.8 = (bf16[512,1024]{1,0:T(8,128)(2,1)}, bf16[512,1024]{1,0:T(8,128)(2,1)S(1)}, u32[]{:S(2)}, u32[]{:S(2)}) collective-permute-start(bf16[512,1024]{1,0:T(8,128)(2,1)} %collective-permute-done.4), channel_id=1, source_target_pairs={{4,0},{8,12},{5,1},{9,13},{6,2},{10,14},{7,3},{11,15},{20,16},{24,... | collective-permute-start | bytes 3145736 | tf_op jit(solution)/shard_map/ppermute | solution.py:69
  110.7 20.1 %copy-start.2 = (f32[512,2048]{1,0:T(8,128)S(1)}, f32[512,2048]{1,0:T(8,128)}, u32[]{:S(2)}) copy-start(f32[512,2048]{1,0:T(8,128)} %fusion.14) | copy-start | bytes 12582916
  110.8 36.9 %collective-permute-start.9 = (bf16[512,768]{1,0:T(8,128)(2,1)S(1)}, bf16[512,768]{1,0:T(8,128)(2,1)S(1)}, u32[]{:S(2)}, u32[]{:S(2)}) collective-permute-start(bf16[512,768]{1,0:T(8,128)(2,1)S(1)} %slice.52), channel_id=1, source_target_pairs={{4,0},{8,12},{5,1},{9,13},{6,2},{10,14},{7,3},{11,15},{20,16},{24,... | collective-permute-start | bytes 2359304 | tf_op jit(solution)/shard_map/ppermute | solution.py:69
  112.3 39.2 %collective-permute-start.10 = (bf16[512,256]{1,0:T(8,128)(2,1)S(1)}, bf16[512,256]{1,0:T(8,128)(2,1)S(1)}, u32[]{:S(2)}, u32[]{:S(2)}) collective-permute-start(bf16[512,256]{1,0:T(8,128)(2,1)S(1)} %slice.53), channel_id=1, source_target_pairs={{4,0},{8,12},{5,1},{9,13},{6,2},{10,14},{7,3},{11,15},{20,16},{24,... | collective-permute-start | bytes 786440 | tf_op jit(solution)/shard_map/ppermute | solution.py:69
  147.7 5.8 %copy-start.1 = (bf16[4,64,2048]{2,1,0:T(8,128)(2,1)S(1)}, bf16[4,64,2048]{2,1,0:T(8,128)(2,1)}, u32[]{:S(2)}) copy-start(bf16[4,64,2048]{2,1,0:T(8,128)(2,1)} %param.8) | copy-start | bytes 3145732

commit v33 on v27

--- a/solution.py
+++ b/solution.py
@@ -81,7 +81,7 @@
     far_mid = jnp.where(here < 2, 2, 1)
     far_end = jnp.where(here < 2, 3, 0)
     own = inputs.reshape(rows, width)
-    half, cut, last = width // 2, width // 16 * 7, width // 8
+    half, cut, last = width // 2, width // 16 * 7, width // 16 * 3
 
     def product(block, owner, first=0):
         part = lax.dynamic_slice_in_dim(base_weight, owner * width + first, block.shape[1], axis=0)

time: 143 us -> 143 us (level)
  waiting for transfers between devices: 56 us -> 60.4 us
  local copies, waits for them, and re-layouts: 11.5 us -> 8.01 us
    ppermute x13, waiting for transfers between devices: 56 us -> 60.4 us  [send(): return lax.ppermute(block, 'tensor', pairs)]
    slice x2, local copies, waits for them, and re-layouts: 2.92 us -> 0.09 us  [line(): end_out += [send(late[:, :-last], OUTWARD), send(late[:, -last:], OUTWARD)]]
  transfers between devices with their start and end apart: 13 -> 13, of which waited for: 7 -> 7; matrix products, arithmetic and copies ran while one was open for 40% -> 37% of each run, Pallas kernels for 0% -> 0%
where the time goes in v33:
time: 143 us
  waiting for transfers between devices  60.4 us (42%)
  matrix products  47.5 us (33%)
  starting transfers between devices  22.9 us (16%)
  local copies, waits for them, and re-layouts  8.01 us (6%)
  between operations  3.92 us (3%)
    ppermute x13, waiting for transfers between devices, send(): return lax.ppermute(block, 'tensor', pairs)  60.4 us
    dot_general x6, matrix products, product(): return jnp.dot(block, part, preferred_element_type=F32)  40.5 us
    ppermute x13, starting transfers between devices, send(): return lax.ppermute(block, 'tensor', pairs)  22.9 us
    dot_general x2, matrix products, shrink(): jnp.dot(inputs[c], shrink_table[adapter_ids[c]], preferred_element_type=F32)  3.52 us
  transfers between devices with their start and end apart: 13, of which 7 were waited for; matrix products, arithmetic and copies ran while one was open for 37% of the time, Pallas kernels for 0%

profile of v33, /device:TPU:0, one launch (start us, length us, event | category | flops | bytes accessed | tf_op | source)
XLA Modules:
  0.0 142.7 jit_solution(679935803573906490)
XLA Ops:
  0.0 3.0 %collective-permute-start = (bf16[512,2048]{1,0:T(8,128)(2,1)}, bf16[512,2048]{1,0:T(8,128)(2,1)S(1)}, u32[]{:S(2)}, u32[]{:S(2)}) collective-permute-start(bf16[512,2048]{1,0:T(8,128)(2,1)} %bitcast.40), channel_id=1, source_target_pairs={{0,4},{12,8},{4,0},{8,12},{1,5},{13,9},{5,1},{9,13},{2,6},{14,10},... | collective-permute-start | bytes 6291464 | tf_op jit(solution)/shard_map/ppermute | solution.py:69
  3.0 2.3 %slice.62 = bf16[512,1024]{1,0:T(8,128)(2,1)} slice(bf16[512,2048]{1,0:T(8,128)(2,1)} %bitcast.41), slice={[0:512], [0:1024]} | slice | bytes 2097152 | tf_op jit(solution)/shard_map/slice | solution.py:91
  5.3 1.6 %collective-permute-start.2 = (bf16[512,1024]{1,0:T(8,128)(2,1)}, bf16[512,1024]{1,0:T(8,128)(2,1)}, u32[]{:S(2)}, u32[]{:S(2)}) collective-permute-start(bf16[512,1024]{1,0:T(8,128)(2,1)} %slice.62), channel_id=1, source_target_pairs={{4,8},{8,4},{5,9},{9,5},{6,10},{10,6},{7,11},{11,7},{20,24},{24,20... | collective-permute-start | bytes 3145736 | tf_op jit(solution)/shard_map/ppermute | solution.py:69
  12.1 1.8 %fusion.28 = bf16[256,64]{0,1:T(8,128)(2,1)S(1)} fusion(bf16[2,256,2048]{2,1,0:T(8,128)(2,1)} %param.5, bf16[4,2048,64]{1,2,0:T(8,128)(2,1)} %param.7, s32[]{:T(128)S(6)} %select_n.82), kind=kOutput, calls=%fused_computation.22 | convolution fusion | flops 67125248 | bytes 1343492 | tf_op jit(solution)/shard_map/dot_general | solution.py:12
  13.8 1.8 %fusion.27 = bf16[256,64]{0,1:T(8,128)(2,1)S(1)} fusion(bf16[2,256,2048]{2,1,0:T(8,128)(2,1)} %param.5, bf16[4,2048,64]{1,2,0:T(8,128)(2,1)} %param.7, s32[]{:T(128)S(6)} %select_n.81), kind=kOutput, calls=%fused_computation.21 | convolution fusion | flops 67125248 | bytes 1343492 | tf_op jit(solution)/shard_map/dot_general | solution.py:12
  15.6 5.3 %collective-permute-start.1 = (bf16[512,64]{0,1:T(8,128)(2,1)S(1)}, bf16[512,64]{0,1:T(8,128)(2,1)S(1)}, u32[]{:S(2)}, u32[]{:S(2)}) collective-permute-start(bf16[512,64]{0,1:T(8,128)(2,1)S(1)} %get-tuple-element.36), channel_id=1, source_target_pairs={{0,4},{12,8},{1,5},{13,9},{2,6},{14,10},{3,7},{15,11},{16,20},{28,... | collective-permute-start | bytes 196616 | tf_op jit(solution)/shard_map/ppermute | solution.py:69
  20.9 2.3 %slice.53 = bf16[512,1024]{1,0:T(8,128)(2,1)} slice(bf16[512,2048]{1,0:T(8,128)(2,1)} %bitcast.42), slice={[0:512], [1024:2048]} | slice | bytes 2097152 | tf_op jit(solution)/shard_map/slice | solution.py:93
  23.2 1.7 %collective-permute-start.4 = (bf16[512,1024]{1,0:T(8,128)(2,1)}, bf16[512,1024]{1,0:T(8,128)(2,1)}, u32[]{:S(2)}, u32[]{:S(2)}) collective-permute-start(bf16[512,1024]{1,0:T(8,128)(2,1)} %slice.53), channel_id=1, source_target_pairs={{4,8},{8,4},{5,9},{9,5},{6,10},{10,6},{7,11},{11,7},{20,24},{24,20... | collective-permute-start | bytes 3145736 | tf_op jit(solution)/shard_map/ppermute | solution.py:69
  24.9 10.5 %fusion.11 = f32[512,2048]{1,0:T(8,128)} fusion(bf16[512,2048]{1,0:T(8,128)(2,1)} %bitcast.43, bf16[8192,2048]{1,0:T(8,128)(2,1)} %param.6, s32[]{:T(128)S(6)} %select_n.80), kind=kOutput, calls=%fused_computation.13 | convolution fusion | flops 4294967296 | bytes 14680068 | tf_op jit(solution)/shard_map/dot_general | solution.py:88
  36.7 12.8 %collective-permute-done.1 = bf16[512,64]{0,1:T(8,128)(2,1)S(1)} collective-permute-done((bf16[512,64]{0,1:T(8,128)(2,1)S(1)}, bf16[512,64]{0,1:T(8,128)(2,1)S(1)}, u32[]{:S(2)}, u32[]{:S(2)}) %collective-permute-start.1) | collective-permute-done | bytes 65568 | tf_op jit(solution)/shard_map/ppermute | solution.py:69
  49.8 1.6 %collective-permute-start.6 = (bf16[512,896]{1,0:T(8,128)(2,1)S(1)}, bf16[512,896]{1,0:T(8,128)(2,1)}, u32[]{:S(2)}, u32[]{:S(2)}) collective-permute-start(bf16[512,896]{1,0:T(8,128)(2,1)S(1)} %slice.54), channel_id=1, source_target_pairs={{4,8},{8,4},{5,9},{9,5},{6,10},{10,6},{7,11},{11,7},{20,24},{24,20... | collective-permute-start | bytes 2752520 | tf_op jit(solution)/shard_map/ppermute | solution.py:69
  52.1 8.8 %fusion.16 = f32[512,2048]{1,0:T(8,128)S(1)} fusion(f32[512,2048]{1,0:T(8,128)} %fusion.11, bf16[512,2048]{1,0:T(8,128)(2,1)S(1)} %collective-permute-done, bf16[8192,2048]{1,0:T(8,128)(2,1)} %param.6, s32[]{:T(128)S(6)} %select_n.83), kind=kOutput, calls=%fused_computation.16 | convolution fusion | flops 4296015872 | bytes 18874372 | tf_op jit(solution)/shard_map/dot_general | solution.py:88
  64.4 7.8 %collective-permute-done.3 = bf16[512,1024]{1,0:T(8,128)(2,1)S(1)} collective-permute-done((bf16[512,1024]{1,0:T(8,128)(2,1)}, bf16[512,1024]{1,0:T(8,128)(2,1)S(1)}, u32[]{:S(2)}, u32[]{:S(2)}) %collective-permute-start.3) | collective-permute-done | bytes 1048608 | tf_op jit(solution)/shard_map/ppermute | solution.py:69
  72.2 6.5 %fusion.22 = f32[512,2048]{1,0:T(8,128)} fusion(f32[512,2048]{1,0:T(8,128)S(1)} %fusion.16, bf16[8192,2048]{1,0:T(8,128)(2,1)} %param.6, s32[]{:T(128)S(6)} %select_n.87, bf16[512,1024]{1,0:T(8,128)(2,1)S(1)} %collective-permute-done.3, bf16[512,1024]{1,0:T(8,128)(2,1)} %collective-permute-done.2, pred[]{:T(512)S(6)} %or.3), kind=kOutput, calls=%fused_computation.18 | convolution fusion | flops 2149056512 | bytes 14680069 | tf_op jit(solution)/shard_map/dot_general | solution.py:88
  80.0 16.0 %collective-permute-done.8 = bf16[512,64]{0,1:T(8,128)(2,1)S(1)} collective-permute-done((bf16[512,64]{0,1:T(8,128)(2,1)S(1)}, bf16[512,64]{0,1:T(8,128)(2,1)S(1)}, u32[]{:S(2)}, u32[]{:S(2)}) %collective-permute-start.8) | collective-permute-done | bytes 65568 | tf_op jit(solution)/shard_map/ppermute | solution.py:69
  96.1 6.5 %fusion.5 = f32[512,2048]{1,0:T(8,128)} fusion(bf16[8192,2048]{1,0:T(8,128)(2,1)} %param.6, s32[]{:T(128)S(6)} %select_n.89, bf16[512,1024]{1,0:T(8,128)(2,1)S(1)} %collective-permute-done.5, bf16[512,1024]{1,0:T(8,128)(2,1)} %collective-permute-done.4, pred[]{:T(512)S(6)} %or.3), kind=kOutput, calls=%fused_computation.7 | convolution fusion | flops 2148007936 | bytes 10485765 | tf_op jit(solution)/shard_map/dot_general | solution.py:88
  102.6 1.7 %constant_dynamic-slice_fusion = bf16[384,2048]{1,0:T(8,128)(2,1)S(1)} fusion(bf16[8192,2048]{1,0:T(8,128)(2,1)} %param.6, s32[]{:T(128)S(6)} %select_n.93), kind=kLoop, calls=%fused_computation.59 | loop fusion | bytes 3145732 | tf_op jit(solution)/shard_map/dynamic_slice | solution.py:116
  104.5 1.6 %collective-permute-start.11 = (bf16[512,768]{1,0:T(8,128)(2,1)S(1)}, bf16[512,768]{1,0:T(8,128)(2,1)S(1)}, u32[]{:S(2)}, u32[]{:S(2)}) collective-permute-start(bf16[512,768]{1,0:T(8,128)(2,1)S(1)} %slice.60), channel_id=1, source_target_pairs={{4,0},{8,12},{5,1},{9,13},{6,2},{10,14},{7,3},{11,15},{20,16},{24,... | collective-permute-start | bytes 2359304 | tf_op jit(solution)/shard_map/ppermute | solution.py:69
  108.4 7.3 %collective-permute-done.10 = bf16[512,896]{1,0:T(8,128)(2,1)S(1)} collective-permute-done((bf16[512,896]{1,0:T(8,128)(2,1)}, bf16[512,896]{1,0:T(8,128)(2,1)S(1)}, u32[]{:S(2)}, u32[]{:S(2)}) %collective-permute-start.10) | collective-permute-done | bytes 917536 | tf_op jit(solution)/shard_map/ppermute | solution.py:69
  115.7 4.5 %fusion.4 = f32[512,2048]{1,0:T(8,128)S(1)} fusion(f32[256,2048]{1,0:T(8,128)S(1)} %fusion.43, f32[256,2048]{1,0:T(8,128)S(1)} %fusion.45, f32[512,2048]{1,0:T(8,128)S(1)} %copy-done.1, f32[512,2048]{1,0:T(8,128)S(1)} %copy-done.2, bf16[8192,2048]{1,0:T(8,128)(2,1)} %param.6, s32[]{:T(128)S(6)} %select_n.96, ...), kind=kOutput, calls=%fused_computation.5 | convolution fusion | flops 1883701248 | bytes 22282244 | tf_op jit(solution)/shard_map/dot_general | solution.py:88
  120.2 12.4 %collective-permute-done.11 = bf16[512,768]{1,0:T(8,128)(2,1)S(1)} collective-permute-done((bf16[512,768]{1,0:T(8,128)(2,1)S(1)}, bf16[512,768]{1,0:T(8,128)(2,1)S(1)}, u32[]{:S(2)}, u32[]{:S(2)}) %collective-permute-start.11) | collective-permute-done | bytes 786464 | tf_op jit(solution)/shard_map/ppermute | solution.py:69
  132.6 3.7 %fusion.19 = f32[512,2048]{1,0:T(8,128)S(1)} fusion(f32[512,2048]{1,0:T(8,128)S(1)} %fusion.4, bf16[8192,2048]{1,0:T(8,128)(2,1)} %param.6, s32[]{:T(128)S(6)} %select_n.99, bf16[512,768]{1,0:T(8,128)(2,1)S(1)} %collective-permute-done.11, pred[]{:T(512)S(6)} %or.3, bf16[512,1152]{1,0:T(8,128)(2,1)S(1)} %collective-permute-done.9), kind=kOutput, calls=%fused_computation.17 | convolution fusion | flops 1612054528 | bytes 13107205 | tf_op jit(solution)/shard_map/dot_general | solution.py:88
  136.2 3.9 %collective-permute-done.12 = bf16[512,384]{1,0:T(8,128)(2,1)S(1)} collective-permute-done((bf16[512,384]{1,0:T(8,128)(2,1)S(1)}, bf16[512,384]{1,0:T(8,128)(2,1)S(1)}, u32[]{:S(2)}, u32[]{:S(2)}) %collective-permute-start.12) | collective-permute-done | bytes 393248 | tf_op jit(solution)/shard_map/ppermute | solution.py:69
  140.2 2.6 %add_convert_fusion = bf16[512,2048]{1,0:T(8,128)(2,1)} fusion(f32[512,2048]{1,0:T(8,128)S(1)} %fusion.19, bf16[384,2048]{1,0:T(8,128)(2,1)S(1)} %constant_dynamic-slice_fusion, bf16[512,384]{1,0:T(8,128)(2,1)S(1)} %collective-permute-done.12, pred[]{:T(512)S(6)} %or.3, bf16[512,1152]{1,0:T(8,128)(2,1)S(1)} %collective-permute-done.9), kind=kOutput, calls=%fused_computation.6 | convolution fusion | flops 807600128 | bytes 8650753 | tf_op jit(solution)/shard_map/dot_general | solution.py:126
  (31 shorter events, 10.9 us)
Async XLA Ops:
  0.0 107.5 %copy-start = (bf16[4,64,2048]{2,1,0:T(8,128)(2,1)S(1)}, bf16[4,64,2048]{2,1,0:T(8,128)(2,1)}, u32[]{:S(2)}) copy-start(bf16[4,64,2048]{2,1,0:T(8,128)(2,1)} %param.8) | copy-start | bytes 3145732
  0.0 49.7 %collective-permute-start = (bf16[512,2048]{1,0:T(8,128)(2,1)}, bf16[512,2048]{1,0:T(8,128)(2,1)S(1)}, u32[]{:S(2)}, u32[]{:S(2)}) collective-permute-start(bf16[512,2048]{1,0:T(8,128)(2,1)} %bitcast.40), channel_id=1, source_target_pairs={{0,4},{12,8},{4,0},{8,12},{1,5},{13,9},{5,1},{9,13},{2,6},{14,10},... | collective-permute-start | bytes 6291464 | tf_op jit(solution)/shard_map/ppermute | solution.py:69
  5.3 30.1 %collective-permute-start.2 = (bf16[512,1024]{1,0:T(8,128)(2,1)}, bf16[512,1024]{1,0:T(8,128)(2,1)}, u32[]{:S(2)}, u32[]{:S(2)}) collective-permute-start(bf16[512,1024]{1,0:T(8,128)(2,1)} %slice.62), channel_id=1, source_target_pairs={{4,8},{8,4},{5,9},{9,5},{6,10},{10,6},{7,11},{11,7},{20,24},{24,20... | collective-permute-start | bytes 3145736 | tf_op jit(solution)/shard_map/ppermute | solution.py:69
  15.6 33.9 %collective-permute-start.1 = (bf16[512,64]{0,1:T(8,128)(2,1)S(1)}, bf16[512,64]{0,1:T(8,128)(2,1)S(1)}, u32[]{:S(2)}, u32[]{:S(2)}) collective-permute-start(bf16[512,64]{0,1:T(8,128)(2,1)S(1)} %get-tuple-element.36), channel_id=1, source_target_pairs={{0,4},{12,8},{1,5},{13,9},{2,6},{14,10},{3,7},{15,11},{16,20},{28,... | collective-permute-start | bytes 196616 | tf_op jit(solution)/shard_map/ppermute | solution.py:69
  23.2 37.6 %collective-permute-start.4 = (bf16[512,1024]{1,0:T(8,128)(2,1)}, bf16[512,1024]{1,0:T(8,128)(2,1)}, u32[]{:S(2)}, u32[]{:S(2)}) collective-permute-start(bf16[512,1024]{1,0:T(8,128)(2,1)} %slice.53), channel_id=1, source_target_pairs={{4,8},{8,4},{5,9},{9,5},{6,10},{10,6},{7,11},{11,7},{20,24},{24,20... | collective-permute-start | bytes 3145736 | tf_op jit(solution)/shard_map/ppermute | solution.py:69
  35.4 36.7 %collective-permute-start.3 = (bf16[512,1024]{1,0:T(8,128)(2,1)}, bf16[512,1024]{1,0:T(8,128)(2,1)S(1)}, u32[]{:S(2)}, u32[]{:S(2)}) collective-permute-start(bf16[512,1024]{1,0:T(8,128)(2,1)} %collective-permute-done.2), channel_id=1, source_target_pairs={{4,0},{8,12},{5,1},{9,13},{6,2},{10,14},{7,3},{11,15},{20,16},{24,... | collective-permute-start | bytes 3145736 | tf_op jit(solution)/shard_map/ppermute | solution.py:69
  49.8 12.4 %collective-permute-start.6 = (bf16[512,896]{1,0:T(8,128)(2,1)S(1)}, bf16[512,896]{1,0:T(8,128)(2,1)}, u32[]{:S(2)}, u32[]{:S(2)}) collective-permute-start(bf16[512,896]{1,0:T(8,128)(2,1)S(1)} %slice.54), channel_id=1, source_target_pairs={{4,8},{8,4},{5,9},{9,5},{6,10},{10,6},{7,11},{11,7},{20,24},{24,20... | collective-permute-start | bytes 2752520 | tf_op jit(solution)/shard_map/ppermute | solution.py:69
  51.4 10.8 %collective-permute-start.7 = (bf16[2,512,64]{1,2,0:T(8,128)(2,1)S(1)}, bf16[2,512,64]{1,2,0:T(8,128)(2,1)S(1)}, u32[]{:S(2)}, u32[]{:S(2)}) collective-permute-start(bf16[2,512,64]{1,2,0:T(8,128)(2,1)S(1)} %pad_maximum_fusion), channel_id=1, source_target_pairs={{4,8},{8,4},{5,9},{9,5},{6,10},{10,6},{7,11},{11,7},{20,24},{24,20... | collective-permute-start | bytes 393224 | tf_op jit(solution)/shard_map/ppermute | solution.py:69
  60.8 35.2 %collective-permute-start.5 = (bf16[512,1024]{1,0:T(8,128)(2,1)}, bf16[512,1024]{1,0:T(8,128)(2,1)S(1)}, u32[]{:S(2)}, u32[]{:S(2)}) collective-permute-start(bf16[512,1024]{1,0:T(8,128)(2,1)} %collective-permute-done.4), channel_id=1, source_target_pairs={{4,0},{8,12},{5,1},{9,13},{6,2},{10,14},{7,3},{11,15},{20,16},{24,... | collective-permute-start | bytes 3145736 | tf_op jit(solution)/shard_map/ppermute | solution.py:69
  62.2 33.8 %collective-permute-start.8 = (bf16[512,64]{0,1:T(8,128)(2,1)S(1)}, bf16[512,64]{0,1:T(8,128)(2,1)S(1)}, u32[]{:S(2)}, u32[]{:S(2)}) collective-permute-start(bf16[512,64]{0,1:T(8,128)(2,1)S(1)} %fusion.53), channel_id=1, source_target_pairs={{4,0},{8,12},{5,1},{9,13},{6,2},{10,14},{7,3},{11,15},{20,16},{24,... | collective-permute-start | bytes 196616 | tf_op jit(solution)/shard_map/ppermute | solution.py:69
  63.6 39.0 %collective-permute-start.9 = (bf16[512,1152]{1,0:T(8,128)(2,1)S(1)}, bf16[512,1152]{1,0:T(8,128)(2,1)S(1)}, u32[]{:S(2)}, u32[]{:S(2)}) collective-permute-start(bf16[512,1152]{1,0:T(8,128)(2,1)S(1)} %slice.57), channel_id=1, source_target_pairs={{4,8},{8,4},{5,9},{9,5},{6,10},{10,6},{7,11},{11,7},{20,24},{24,20... | collective-permute-start | bytes 3538952 | tf_op jit(solution)/shard_map/ppermute | solution.py:69
  78.7 37.0 %collective-permute-start.10 = (bf16[512,896]{1,0:T(8,128)(2,1)}, bf16[512,896]{1,0:T(8,128)(2,1)S(1)}, u32[]{:S(2)}, u32[]{:S(2)}) collective-permute-start(bf16[512,896]{1,0:T(8,128)(2,1)} %collective-permute-done.6), channel_id=1, source_target_pairs={{4,0},{8,12},{5,1},{9,13},{6,2},{10,14},{7,3},{11,15},{20,16},{24,... | collective-permute-start | bytes 2752520 | tf_op jit(solution)/shard_map/ppermute | solution.py:69
  102.6 13.1 %copy-start.2 = (f32[512,2048]{1,0:T(8,128)S(1)}, f32[512,2048]{1,0:T(8,128)}, u32[]{:S(2)}) copy-start(f32[512,2048]{1,0:T(8,128)} %fusion.5) | copy-start | bytes 12582916
  104.3 11.4 %copy-start.1 = (f32[512,2048]{1,0:T(8,128)S(1)}, f32[512,2048]{1,0:T(8,128)}, u32[]{:S(2)}) copy-start(f32[512,2048]{1,0:T(8,128)} %fusion.22) | copy-start | bytes 12582916
  104.5 28.1 %collective-permute-start.11 = (bf16[512,768]{1,0:T(8,128)(2,1)S(1)}, bf16[512,768]{1,0:T(8,128)(2,1)S(1)}, u32[]{:S(2)}, u32[]{:S(2)}) collective-permute-start(bf16[512,768]{1,0:T(8,128)(2,1)S(1)} %slice.60), channel_id=1, source_target_pairs={{4,0},{8,12},{5,1},{9,13},{6,2},{10,14},{7,3},{11,15},{20,16},{24,... | collective-permute-start | bytes 2359304 | tf_op jit(solution)/shard_map/ppermute | solution.py:69
  106.0 34.1 %collective-permute-start.12 = (bf16[512,384]{1,0:T(8,128)(2,1)S(1)}, bf16[512,384]{1,0:T(8,128)(2,1)S(1)}, u32[]{:S(2)}, u32[]{:S(2)}) collective-permute-start(bf16[512,384]{1,0:T(8,128)(2,1)S(1)} %slice.61), channel_id=1, source_target_pairs={{4,0},{8,12},{5,1},{9,13},{6,2},{10,14},{7,3},{11,15},{20,16},{24,... | collective-permute-start | bytes 1179656 | tf_op jit(solution)/shard_map/ppermute | solution.py:69

commit v34 on v27

--- a/solution.py
+++ b/solution.py
@@ -114,14 +114,15 @@
     late = after(end[1], total)
     begin = (after(far_end, late) + 1) * width - last
     last_rows = lax.dynamic_slice_in_dim(base_weight, begin, last, axis=0)
-    late, last_rows = lax.optimization_barrier((late, last_rows))
+    next_rows = lax.dynamic_slice_in_dim(base_weight, begin + last - width + cut, width - cut - last)
+    late, last_rows, next_rows = lax.optimization_barrier((late, last_rows, next_rows))
     shrunk = after(shrunk, late)
     end_out += [send(late[:, :-last], OUTWARD), send(late[:, -last:], OUTWARD)]
     total = total + product(jnp.where(is_end, mid_out[1], mid[1]), far_mid, half)
     total = total + jnp.concatenate(expand(shrunk, expand_table, adapter_ids))
     total = total + product(jnp.where(is_end, end_out[0], end[0]), far_end)
     block = jnp.where(is_end, after(end_out[1], total), late[:, :-last])
-    total = total + product(block, far_end, cut)
+    total = total + jnp.dot(block, next_rows, preferred_element_type=F32)
     block = jnp.where(is_end, after(end_out[2], total), late[:, -last:])
     total = total + jnp.dot(block, last_rows, preferred_element_type=F32)
     return total.astype(BF16).reshape(chats, span, -1)

time: 143 us -> 143 us (level)
  matrix products: 47.9 us -> 45.9 us
    dot_general x6 -> x5, matrix products: 41.4 us -> 37.1 us  [product(): return jnp.dot(block, part, preferred_element_type=F32)]
    dynamic_slice x0 -> x1, local copies, waits for them, and re-layouts: none -> 2.68 us  [line(): lax.dynamic_slice_in_dim(base_weight, begin + last - width + cut, width -...]
    dot_general x0 -> x1, matrix products: none -> 2.34 us  [line(): total = total + jnp.dot(block, next_rows, preferred_element_type=F32)]
    slice x2, local copies, waits for them, and re-layouts: 2.92 us -> 1.42 us  [line(): end_out += [send(late[:, :-last], OUTWARD), send(late[:, -last:], OUTWARD)]]
  transfers between devices with their start and end apart: 13 -> 13, of which waited for: 7 -> 7; matrix products, arithmetic and copies ran while one was open for 40% -> 39% of each run, Pallas kernels for 0% -> 0%
where the time goes in v34:
time: 143 us; the launch traced here: 142 us
  waiting for transfers between devices  56.9 us (40%)
  matrix products  45.9 us (32%)
  starting transfers between devices  22.7 us (16%)
  local copies, waits for them, and re-layouts  12.6 us (9%)
  between operations  4 us (3%)
    ppermute x13, waiting for transfers between devices, send(): return lax.ppermute(block, 'tensor', pairs)  56.9 us
    dot_general x5, matrix products, product(): return jnp.dot(block, part, preferred_element_type=F32)  37.1 us
    ppermute x13, starting transfers between devices, send(): return lax.ppermute(block, 'tensor', pairs)  22.7 us
    dot_general x2, matrix products, shrink(): jnp.dot(inputs[c], shrink_table[adapter_ids[c]], preferred_element_type=F32)  3.52 us
  transfers between devices with their start and end apart: 13, of which 7 were waited for; matrix products, arithmetic and copies ran while one was open for 39% of the time, Pallas kernels for 0%

profile of v34, /device:TPU:0, one launch (start us, length us, event | category | flops | bytes accessed | tf_op | source)
XLA Modules:
  0.0 142.2 jit_solution(13045205579769389642)
XLA Ops:
  0.0 3.0 %collective-permute-start = (bf16[512,2048]{1,0:T(8,128)(2,1)}, bf16[512,2048]{1,0:T(8,128)(2,1)S(1)}, u32[]{:S(2)}, u32[]{:S(2)}) collective-permute-start(bf16[512,2048]{1,0:T(8,128)(2,1)} %bitcast.41), channel_id=1, source_target_pairs={{0,4},{12,8},{4,0},{8,12},{1,5},{13,9},{5,1},{9,13},{2,6},{14,10},... | collective-permute-start | bytes 6291464 | tf_op jit(solution)/shard_map/ppermute | solution.py:69
  3.0 2.3 %slice.62 = bf16[512,1024]{1,0:T(8,128)(2,1)} slice(bf16[512,2048]{1,0:T(8,128)(2,1)} %bitcast.42), slice={[0:512], [0:1024]} | slice | bytes 2097152 | tf_op jit(solution)/shard_map/slice | solution.py:91
  5.3 1.6 %collective-permute-start.2 = (bf16[512,1024]{1,0:T(8,128)(2,1)}, bf16[512,1024]{1,0:T(8,128)(2,1)}, u32[]{:S(2)}, u32[]{:S(2)}) collective-permute-start(bf16[512,1024]{1,0:T(8,128)(2,1)} %slice.62), channel_id=1, source_target_pairs={{4,8},{8,4},{5,9},{9,5},{6,10},{10,6},{7,11},{11,7},{20,24},{24,20... | collective-permute-start | bytes 3145736 | tf_op jit(solution)/shard_map/ppermute | solution.py:69
  12.0 1.8 %fusion.23 = bf16[256,64]{0,1:T(8,128)(2,1)S(1)} fusion(bf16[2,256,2048]{2,1,0:T(8,128)(2,1)} %param.5, bf16[4,2048,64]{1,2,0:T(8,128)(2,1)} %param.7, s32[]{:T(128)S(6)} %select_n.78), kind=kOutput, calls=%fused_computation.20 | convolution fusion | flops 67125248 | bytes 1343492 | tf_op jit(solution)/shard_map/dot_general | solution.py:12
  13.8 1.8 %fusion.22 = bf16[256,64]{0,1:T(8,128)(2,1)S(1)} fusion(bf16[2,256,2048]{2,1,0:T(8,128)(2,1)} %param.5, bf16[4,2048,64]{1,2,0:T(8,128)(2,1)} %param.7, s32[]{:T(128)S(6)} %select_n.77), kind=kOutput, calls=%fused_computation.19 | convolution fusion | flops 67125248 | bytes 1343492 | tf_op jit(solution)/shard_map/dot_general | solution.py:12
  15.6 5.3 %collective-permute-start.1 = (bf16[512,64]{0,1:T(8,128)(2,1)S(1)}, bf16[512,64]{0,1:T(8,128)(2,1)S(1)}, u32[]{:S(2)}, u32[]{:S(2)}) collective-permute-start(bf16[512,64]{0,1:T(8,128)(2,1)S(1)} %get-tuple-element.38), channel_id=1, source_target_pairs={{0,4},{12,8},{1,5},{13,9},{2,6},{14,10},{3,7},{15,11},{16,20},{28,... | collective-permute-start | bytes 196616 | tf_op jit(solution)/shard_map/ppermute | solution.py:69
  20.9 2.3 %slice.53 = bf16[512,1024]{1,0:T(8,128)(2,1)} slice(bf16[512,2048]{1,0:T(8,128)(2,1)} %bitcast.43), slice={[0:512], [1024:2048]} | slice | bytes 2097152 | tf_op jit(solution)/shard_map/slice | solution.py:93
  23.2 1.7 %collective-permute-start.4 = (bf16[512,1024]{1,0:T(8,128)(2,1)}, bf16[512,1024]{1,0:T(8,128)(2,1)}, u32[]{:S(2)}, u32[]{:S(2)}) collective-permute-start(bf16[512,1024]{1,0:T(8,128)(2,1)} %slice.53), channel_id=1, source_target_pairs={{4,8},{8,4},{5,9},{9,5},{6,10},{10,6},{7,11},{11,7},{20,24},{24,20... | collective-permute-start | bytes 3145736 | tf_op jit(solution)/shard_map/ppermute | solution.py:69
  24.9 10.5 %fusion.11 = f32[512,2048]{1,0:T(8,128)} fusion(bf16[512,2048]{1,0:T(8,128)(2,1)} %bitcast.44, bf16[8192,2048]{1,0:T(8,128)(2,1)} %param.6, s32[]{:T(128)S(6)} %select_n.76), kind=kOutput, calls=%fused_computation.13 | convolution fusion | flops 4294967296 | bytes 14680068 | tf_op jit(solution)/shard_map/dot_general | solution.py:88
  36.7 12.8 %collective-permute-done.1 = bf16[512,64]{0,1:T(8,128)(2,1)S(1)} collective-permute-done((bf16[512,64]{0,1:T(8,128)(2,1)S(1)}, bf16[512,64]{0,1:T(8,128)(2,1)S(1)}, u32[]{:S(2)}, u32[]{:S(2)}) %collective-permute-start.1) | collective-permute-done | bytes 65568 | tf_op jit(solution)/shard_map/ppermute | solution.py:69
  49.8 1.6 %collective-permute-start.6 = (bf16[512,896]{1,0:T(8,128)(2,1)S(1)}, bf16[512,896]{1,0:T(8,128)(2,1)}, u32[]{:S(2)}, u32[]{:S(2)}) collective-permute-start(bf16[512,896]{1,0:T(8,128)(2,1)S(1)} %slice.54), channel_id=1, source_target_pairs={{4,8},{8,4},{5,9},{9,5},{6,10},{10,6},{7,11},{11,7},{20,24},{24,20... | collective-permute-start | bytes 2752520 | tf_op jit(solution)/shard_map/ppermute | solution.py:69
  52.1 8.8 %fusion.14 = f32[512,2048]{1,0:T(8,128)S(1)} fusion(f32[512,2048]{1,0:T(8,128)} %fusion.11, bf16[512,2048]{1,0:T(8,128)(2,1)S(1)} %collective-permute-done, bf16[8192,2048]{1,0:T(8,128)(2,1)} %param.6, s32[]{:T(128)S(6)} %select_n.79), kind=kOutput, calls=%fused_computation.14 | convolution fusion | flops 4296015872 | bytes 18874372 | tf_op jit(solution)/shard_map/dot_general | solution.py:88
  64.4 7.8 %collective-permute-done.3 = bf16[512,1024]{1,0:T(8,128)(2,1)S(1)} collective-permute-done((bf16[512,1024]{1,0:T(8,128)(2,1)}, bf16[512,1024]{1,0:T(8,128)(2,1)S(1)}, u32[]{:S(2)}, u32[]{:S(2)}) %collective-permute-start.3) | collective-permute-done | bytes 1048608 | tf_op jit(solution)/shard_map/ppermute | solution.py:69
  72.2 6.5 %fusion.17 = f32[512,2048]{1,0:T(8,128)} fusion(f32[512,2048]{1,0:T(8,128)S(1)} %fusion.14, bf16[8192,2048]{1,0:T(8,128)(2,1)} %param.6, s32[]{:T(128)S(6)} %select_n.83, bf16[512,1024]{1,0:T(8,128)(2,1)S(1)} %collective-permute-done.3, bf16[512,1024]{1,0:T(8,128)(2,1)} %collective-permute-done.2, pred[]{:T(512)S(6)} %or.3), kind=kOutput, calls=%fused_computation.15 | convolution fusion | flops 2149056512 | bytes 14680069 | tf_op jit(solution)/shard_map/dot_general | solution.py:88
  80.0 16.0 %collective-permute-done.8 = bf16[512,64]{0,1:T(8,128)(2,1)S(1)} collective-permute-done((bf16[512,64]{0,1:T(8,128)(2,1)S(1)}, bf16[512,64]{0,1:T(8,128)(2,1)S(1)}, u32[]{:S(2)}, u32[]{:S(2)}) %collective-permute-start.8) | collective-permute-done | bytes 65568 | tf_op jit(solution)/shard_map/ppermute | solution.py:69
  96.1 6.5 %fusion.5 = f32[512,2048]{1,0:T(8,128)} fusion(bf16[8192,2048]{1,0:T(8,128)(2,1)} %param.6, s32[]{:T(128)S(6)} %select_n.85, bf16[512,1024]{1,0:T(8,128)(2,1)S(1)} %collective-permute-done.5, bf16[512,1024]{1,0:T(8,128)(2,1)} %collective-permute-done.4, pred[]{:T(512)S(6)} %or.3), kind=kOutput, calls=%fused_computation.7 | convolution fusion | flops 2148007936 | bytes 10485765 | tf_op jit(solution)/shard_map/dot_general | solution.py:88
  105.0 2.7 %constant_dynamic-slice_fusion = bf16[896,2048]{1,0:T(8,128)(2,1)S(1)} fusion(bf16[8192,2048]{1,0:T(8,128)(2,1)} %param.6, s32[]{:T(128)S(6)} %select_n.90), kind=kLoop, calls=%fused_computation.56 | loop fusion | bytes 7340036 | tf_op jit(solution)/shard_map/dynamic_slice | solution.py:117
  107.7 1.4 slice.60
  109.1 1.6 %collective-permute-start.11 = (bf16[512,896]{1,0:T(8,128)(2,1)S(1)}, bf16[512,896]{1,0:T(8,128)(2,1)S(1)}, u32[]{:S(2)}, u32[]{:S(2)}) collective-permute-start(bf16[512,896]{1,0:T(8,128)(2,1)S(1)} %slice.60), channel_id=1, source_target_pairs={{4,0},{8,12},{5,1},{9,13},{6,2},{10,14},{7,3},{11,15},{20,16},{24,... | collective-permute-start | bytes 2752520 | tf_op jit(solution)/shard_map/ppermute | solution.py:69
  113.0 2.0 %collective-permute-done.10 = bf16[512,896]{1,0:T(8,128)(2,1)} collective-permute-done((bf16[512,896]{1,0:T(8,128)(2,1)}, bf16[512,896]{1,0:T(8,128)(2,1)}, u32[]{:S(2)}, u32[]{:S(2)}) %collective-permute-start.10) | collective-permute-done | bytes 917536 | tf_op jit(solution)/shard_map/ppermute | solution.py:69
  115.0 4.8 %fusion.4 = f32[512,2048]{1,0:T(8,128)S(1)} fusion(f32[256,2048]{1,0:T(8,128)S(1)} %fusion.36, f32[256,2048]{1,0:T(8,128)S(1)} %fusion.38, f32[512,2048]{1,0:T(8,128)S(1)} %copy-done.1, f32[512,2048]{1,0:T(8,128)S(1)} %copy-done.2, bf16[8192,2048]{1,0:T(8,128)(2,1)} %param.6, s32[]{:T(128)S(6)} %select_n.93, bf16[512,896]{1,0:T(8,128)(2,1)} %collective-permute-done.10, ...), kind=kOutput, calls=%fused_computation.5 | convolution fusion | flops 1883701248 | bytes 22282244 | tf_op jit(solution)/shard_map/dot_general | solution.py:88
  119.8 17.6 %collective-permute-done.11 = bf16[512,896]{1,0:T(8,128)(2,1)S(1)} collective-permute-done((bf16[512,896]{1,0:T(8,128)(2,1)S(1)}, bf16[512,896]{1,0:T(8,128)(2,1)S(1)}, u32[]{:S(2)}, u32[]{:S(2)}) %collective-permute-start.11) | collective-permute-done | bytes 917536 | tf_op jit(solution)/shard_map/ppermute | solution.py:69
  137.3 2.3 %convolution_add_fusion = f32[512,2048]{1,0:T(8,128)S(1)} fusion(f32[512,2048]{1,0:T(8,128)S(1)} %fusion.4, bf16[896,2048]{1,0:T(8,128)(2,1)S(1)} %constant_dynamic-slice_fusion, bf16[512,896]{1,0:T(8,128)(2,1)S(1)} %collective-permute-done.11, pred[]{:T(512)S(6)} %or.3, bf16[512,1152]{1,0:T(8,128)(2,1)S(1)} %copy-done.4), kind=kOutput, calls=%fused_computation.16 | convolution fusion | flops 1880555520 | bytes 13893633 | tf_op jit(solution)/shard_map/dot_general | solution.py:125
  140.2 2.0 %add_convert_fusion = bf16[512,2048]{1,0:T(8,128)(2,1)} fusion(f32[512,2048]{1,0:T(8,128)S(1)} %convolution_add_fusion, bf16[256,2048]{1,0:T(8,128)(2,1)S(1)} %constant_dynamic-slice_fusion.1, bf16[512,256]{1,0:T(8,128)(2,1)S(1)} %collective-permute-done.12, pred[]{:T(512)S(6)} %or.3, bf16[512,1152]{1,0:T(8,128)(2,1)S(1)} %copy-done.4), kind=kOutput, calls=%fused_computation.6 | convolution fusion | flops 539099136 | bytes 7864321 | tf_op jit(solution)/shard_map/dot_general | solution.py:127
  (36 shorter events, 13.3 us)
Async XLA Ops:
  0.0 110.7 %copy-start = (bf16[4,64,2048]{2,1,0:T(8,128)(2,1)S(1)}, bf16[4,64,2048]{2,1,0:T(8,128)(2,1)}, u32[]{:S(2)}) copy-start(bf16[4,64,2048]{2,1,0:T(8,128)(2,1)} %param.8) | copy-start | bytes 3145732
  0.0 49.7 %collective-permute-start = (bf16[512,2048]{1,0:T(8,128)(2,1)}, bf16[512,2048]{1,0:T(8,128)(2,1)S(1)}, u32[]{:S(2)}, u32[]{:S(2)}) collective-permute-start(bf16[512,2048]{1,0:T(8,128)(2,1)} %bitcast.41), channel_id=1, source_target_pairs={{0,4},{12,8},{4,0},{8,12},{1,5},{13,9},{5,1},{9,13},{2,6},{14,10},... | collective-permute-start | bytes 6291464 | tf_op jit(solution)/shard_map/ppermute | solution.py:69
  5.3 30.1 %collective-permute-start.2 = (bf16[512,1024]{1,0:T(8,128)(2,1)}, bf16[512,1024]{1,0:T(8,128)(2,1)}, u32[]{:S(2)}, u32[]{:S(2)}) collective-permute-start(bf16[512,1024]{1,0:T(8,128)(2,1)} %slice.62), channel_id=1, source_target_pairs={{4,8},{8,4},{5,9},{9,5},{6,10},{10,6},{7,11},{11,7},{20,24},{24,20... | collective-permute-start | bytes 3145736 | tf_op jit(solution)/shard_map/ppermute | solution.py:69
  15.6 34.0 %collective-permute-start.1 = (bf16[512,64]{0,1:T(8,128)(2,1)S(1)}, bf16[512,64]{0,1:T(8,128)(2,1)S(1)}, u32[]{:S(2)}, u32[]{:S(2)}) collective-permute-start(bf16[512,64]{0,1:T(8,128)(2,1)S(1)} %get-tuple-element.38), channel_id=1, source_target_pairs={{0,4},{12,8},{1,5},{13,9},{2,6},{14,10},{3,7},{15,11},{16,20},{28,... | collective-permute-start | bytes 196616 | tf_op jit(solution)/shard_map/ppermute | solution.py:69
  23.2 37.6 %collective-permute-start.4 = (bf16[512,1024]{1,0:T(8,128)(2,1)}, bf16[512,1024]{1,0:T(8,128)(2,1)}, u32[]{:S(2)}, u32[]{:S(2)}) collective-permute-start(bf16[512,1024]{1,0:T(8,128)(2,1)} %slice.53), channel_id=1, source_target_pairs={{4,8},{8,4},{5,9},{9,5},{6,10},{10,6},{7,11},{11,7},{20,24},{24,20... | collective-permute-start | bytes 3145736 | tf_op jit(solution)/shard_map/ppermute | solution.py:69
  35.4 36.8 %collective-permute-start.3 = (bf16[512,1024]{1,0:T(8,128)(2,1)}, bf16[512,1024]{1,0:T(8,128)(2,1)S(1)}, u32[]{:S(2)}, u32[]{:S(2)}) collective-permute-start(bf16[512,1024]{1,0:T(8,128)(2,1)} %collective-permute-done.2), channel_id=1, source_target_pairs={{4,0},{8,12},{5,1},{9,13},{6,2},{10,14},{7,3},{11,15},{20,16},{24,... | collective-permute-start | bytes 3145736 | tf_op jit(solution)/shard_map/ppermute | solution.py:69
  49.8 12.4 %collective-permute-start.6 = (bf16[512,896]{1,0:T(8,128)(2,1)S(1)}, bf16[512,896]{1,0:T(8,128)(2,1)}, u32[]{:S(2)}, u32[]{:S(2)}) collective-permute-start(bf16[512,896]{1,0:T(8,128)(2,1)S(1)} %slice.54), channel_id=1, source_target_pairs={{4,8},{8,4},{5,9},{9,5},{6,10},{10,6},{7,11},{11,7},{20,24},{24,20... | collective-permute-start | bytes 2752520 | tf_op jit(solution)/shard_map/ppermute | solution.py:69
  51.4 10.8 %collective-permute-start.7 = (bf16[2,512,64]{1,2,0:T(8,128)(2,1)S(1)}, bf16[2,512,64]{1,2,0:T(8,128)(2,1)S(1)}, u32[]{:S(2)}, u32[]{:S(2)}) collective-permute-start(bf16[2,512,64]{1,2,0:T(8,128)(2,1)S(1)} %pad_maximum_fusion), channel_id=1, source_target_pairs={{4,8},{8,4},{5,9},{9,5},{6,10},{10,6},{7,11},{11,7},{20,24},{24,20... | collective-permute-start | bytes 393224 | tf_op jit(solution)/shard_map/ppermute | solution.py:69
  60.8 35.2 %collective-permute-start.5 = (bf16[512,1024]{1,0:T(8,128)(2,1)}, bf16[512,1024]{1,0:T(8,128)(2,1)S(1)}, u32[]{:S(2)}, u32[]{:S(2)}) collective-permute-start(bf16[512,1024]{1,0:T(8,128)(2,1)} %collective-permute-done.4), channel_id=1, source_target_pairs={{4,0},{8,12},{5,1},{9,13},{6,2},{10,14},{7,3},{11,15},{20,16},{24,... | collective-permute-start | bytes 3145736 | tf_op jit(solution)/shard_map/ppermute | solution.py:69
  62.2 33.8 %collective-permute-start.8 = (bf16[512,64]{0,1:T(8,128)(2,1)S(1)}, bf16[512,64]{0,1:T(8,128)(2,1)S(1)}, u32[]{:S(2)}, u32[]{:S(2)}) collective-permute-start(bf16[512,64]{0,1:T(8,128)(2,1)S(1)} %fusion.48), channel_id=1, source_target_pairs={{4,0},{8,12},{5,1},{9,13},{6,2},{10,14},{7,3},{11,15},{20,16},{24,... | collective-permute-start | bytes 196616 | tf_op jit(solution)/shard_map/ppermute | solution.py:69
  63.6 39.0 %collective-permute-start.9 = (bf16[512,1152]{1,0:T(8,128)(2,1)S(1)}, bf16[512,1152]{1,0:T(8,128)(2,1)S(1)}, u32[]{:S(2)}, u32[]{:S(2)}) collective-permute-start(bf16[512,1152]{1,0:T(8,128)(2,1)S(1)} %slice.57), channel_id=1, source_target_pairs={{4,8},{8,4},{5,9},{9,5},{6,10},{10,6},{7,11},{11,7},{20,24},{24,20... | collective-permute-start | bytes 3538952 | tf_op jit(solution)/shard_map/ppermute | solution.py:69
  78.7 36.3 %collective-permute-start.10 = (bf16[512,896]{1,0:T(8,128)(2,1)}, bf16[512,896]{1,0:T(8,128)(2,1)}, u32[]{:S(2)}, u32[]{:S(2)}) collective-permute-start(bf16[512,896]{1,0:T(8,128)(2,1)} %collective-permute-done.6), channel_id=1, source_target_pairs={{4,0},{8,12},{5,1},{9,13},{6,2},{10,14},{7,3},{11,15},{20,16},{24,... | collective-permute-start | bytes 2752520 | tf_op jit(solution)/shard_map/ppermute | solution.py:69
  102.6 1.0 copy-start.3
  105.0 10.0 %copy-start.2 = (f32[512,2048]{1,0:T(8,128)S(1)}, f32[512,2048]{1,0:T(8,128)}, u32[]{:S(2)}) copy-start(f32[512,2048]{1,0:T(8,128)} %fusion.5) | copy-start | bytes 12582916
  107.7 4.0 %copy-start.4 = (bf16[512,1152]{1,0:T(8,128)(2,1)S(1)}, bf16[512,1152]{1,0:T(8,128)(2,1)}, u32[]{:S(2)}) copy-start(bf16[512,1152]{1,0:T(8,128)(2,1)} %copy-done.3) | copy-start | bytes 3538948
  107.7 7.3 %copy-start.1 = (f32[512,2048]{1,0:T(8,128)S(1)}, f32[512,2048]{1,0:T(8,128)}, u32[]{:S(2)}) copy-start(f32[512,2048]{1,0:T(8,128)} %fusion.17) | copy-start | bytes 12582916
  109.1 28.3 %collective-permute-start.11 = (bf16[512,896]{1,0:T(8,128)(2,1)S(1)}, bf16[512,896]{1,0:T(8,128)(2,1)S(1)}, u32[]{:S(2)}, u32[]{:S(2)}) collective-permute-start(bf16[512,896]{1,0:T(8,128)(2,1)S(1)} %slice.60), channel_id=1, source_target_pairs={{4,0},{8,12},{5,1},{9,13},{6,2},{10,14},{7,3},{11,15},{20,16},{24,... | collective-permute-start | bytes 2752520 | tf_op jit(solution)/shard_map/ppermute | solution.py:69
  111.7 28.5 %collective-permute-start.12 = (bf16[512,256]{1,0:T(8,128)(2,1)S(1)}, bf16[512,256]{1,0:T(8,128)(2,1)S(1)}, u32[]{:S(2)}, u32[]{:S(2)}) collective-permute-start(bf16[512,256]{1,0:T(8,128)(2,1)S(1)} %slice.61), channel_id=1, source_target_pairs={{4,0},{8,12},{5,1},{9,13},{6,2},{10,14},{7,3},{11,15},{20,16},{24,... | collective-permute-start | bytes 786440 | tf_op jit(solution)/shard_map/ppermute | solution.py:69

commit v35 on v34

--- a/solution.py
+++ b/solution.py
@@ -81,7 +81,7 @@
     far_mid = jnp.where(here < 2, 2, 1)
     far_end = jnp.where(here < 2, 3, 0)
     own = inputs.reshape(rows, width)
-    half, cut, last = width // 2, width // 16 * 7, width // 8
+    half, cut, last = width // 2, width // 16 * 7, width // 16
 
     def product(block, owner, first=0):
         part = lax.dynamic_slice_in_dim(base_weight, owner * width + first, block.shape[1], axis=0)

time: 143 us -> 143 us (level)
  waiting for transfers between devices: 56.9 us -> 59.5 us
  local copies, waits for them, and re-layouts: 12.6 us -> 10.3 us
    ppermute x13, waiting for transfers between devices: 56.9 us -> 59.5 us  [send(): return lax.ppermute(block, 'tensor', pairs)]
  transfers between devices with their start and end apart: 13 -> 13, of which waited for: 7 -> 6; matrix products, arithmetic and copies ran while one was open for 39% -> 38% of each run, Pallas kernels for 0% -> 0%
where the time goes in v35:
time: 143 us
  waiting for transfers between devices  59.5 us (42%)
  matrix products  45.9 us (32%)
  starting transfers between devices  22.9 us (16%)
  local copies, waits for them, and re-layouts  10.3 us (7%)
  between operations  3.94 us (3%)
    ppermute x13, waiting for transfers between devices, send(): return lax.ppermute(block, 'tensor', pairs)  59.5 us
    dot_general x5, matrix products, product(): return jnp.dot(block, part, preferred_element_type=F32)  37.1 us
    ppermute x13, starting transfers between devices, send(): return lax.ppermute(block, 'tensor', pairs)  22.9 us
    dot_general x2, matrix products, shrink(): jnp.dot(inputs[c], shrink_table[adapter_ids[c]], preferred_element_type=F32)  3.52 us
    dynamic_slice x1, local copies, waits for them, and re-layouts, line(): lax.dynamic_slice_in_dim(base_weight, begin + last - width + cut, width -...  2.92 us
  transfers between devices with their start and end apart: 13, of which 6 were waited for; matrix products, arithmetic and copies ran while one was open for 38% of the time, Pallas kernels for 0%

profile of v35, /device:TPU:0, one launch (start us, length us, event | category | flops | bytes accessed | tf_op | source)
XLA Modules:
  0.0 142.5 jit_solution(13872861519952004507)
XLA Ops:
  0.0 3.0 %collective-permute-start = (bf16[512,2048]{1,0:T(8,128)(2,1)}, bf16[512,2048]{1,0:T(8,128)(2,1)S(1)}, u32[]{:S(2)}, u32[]{:S(2)}) collective-permute-start(bf16[512,2048]{1,0:T(8,128)(2,1)} %bitcast.41), channel_id=1, source_target_pairs={{0,4},{12,8},{4,0},{8,12},{1,5},{13,9},{5,1},{9,13},{2,6},{14,10},... | collective-permute-start | bytes 6291464 | tf_op jit(solution)/shard_map/ppermute | solution.py:69
  3.0 2.3 %slice.62 = bf16[512,1024]{1,0:T(8,128)(2,1)} slice(bf16[512,2048]{1,0:T(8,128)(2,1)} %bitcast.42), slice={[0:512], [0:1024]} | slice | bytes 2097152 | tf_op jit(solution)/shard_map/slice | solution.py:91
  5.3 1.6 %collective-permute-start.2 = (bf16[512,1024]{1,0:T(8,128)(2,1)}, bf16[512,1024]{1,0:T(8,128)(2,1)}, u32[]{:S(2)}, u32[]{:S(2)}) collective-permute-start(bf16[512,1024]{1,0:T(8,128)(2,1)} %slice.62), channel_id=1, source_target_pairs={{4,8},{8,4},{5,9},{9,5},{6,10},{10,6},{7,11},{11,7},{20,24},{24,20... | collective-permute-start | bytes 3145736 | tf_op jit(solution)/shard_map/ppermute | solution.py:69
  12.1 1.8 %fusion.23 = bf16[256,64]{0,1:T(8,128)(2,1)S(1)} fusion(bf16[2,256,2048]{2,1,0:T(8,128)(2,1)} %param.5, bf16[4,2048,64]{1,2,0:T(8,128)(2,1)} %param.7, s32[]{:T(128)S(6)} %select_n.78), kind=kOutput, calls=%fused_computation.20 | convolution fusion | flops 67125248 | bytes 1343492 | tf_op jit(solution)/shard_map/dot_general | solution.py:12
  13.8 1.8 %fusion.22 = bf16[256,64]{0,1:T(8,128)(2,1)S(1)} fusion(bf16[2,256,2048]{2,1,0:T(8,128)(2,1)} %param.5, bf16[4,2048,64]{1,2,0:T(8,128)(2,1)} %param.7, s32[]{:T(128)S(6)} %select_n.77), kind=kOutput, calls=%fused_computation.19 | convolution fusion | flops 67125248 | bytes 1343492 | tf_op jit(solution)/shard_map/dot_general | solution.py:12
  15.6 5.3 %collective-permute-start.1 = (bf16[512,64]{0,1:T(8,128)(2,1)S(1)}, bf16[512,64]{0,1:T(8,128)(2,1)S(1)}, u32[]{:S(2)}, u32[]{:S(2)}) collective-permute-start(bf16[512,64]{0,1:T(8,128)(2,1)S(1)} %get-tuple-element.38), channel_id=1, source_target_pairs={{0,4},{12,8},{1,5},{13,9},{2,6},{14,10},{3,7},{15,11},{16,20},{28,... | collective-permute-start | bytes 196616 | tf_op jit(solution)/shard_map/ppermute | solution.py:69
  20.9 2.3 %slice.53 = bf16[512,1024]{1,0:T(8,128)(2,1)} slice(bf16[512,2048]{1,0:T(8,128)(2,1)} %bitcast.43), slice={[0:512], [1024:2048]} | slice | bytes 2097152 | tf_op jit(solution)/shard_map/slice | solution.py:93
  23.2 1.7 %collective-permute-start.4 = (bf16[512,1024]{1,0:T(8,128)(2,1)}, bf16[512,1024]{1,0:T(8,128)(2,1)}, u32[]{:S(2)}, u32[]{:S(2)}) collective-permute-start(bf16[512,1024]{1,0:T(8,128)(2,1)} %slice.53), channel_id=1, source_target_pairs={{4,8},{8,4},{5,9},{9,5},{6,10},{10,6},{7,11},{11,7},{20,24},{24,20... | collective-permute-start | bytes 3145736 | tf_op jit(solution)/shard_map/ppermute | solution.py:69
  24.9 10.5 %fusion.11 = f32[512,2048]{1,0:T(8,128)} fusion(bf16[512,2048]{1,0:T(8,128)(2,1)} %bitcast.44, bf16[8192,2048]{1,0:T(8,128)(2,1)} %param.6, s32[]{:T(128)S(6)} %select_n.76), kind=kOutput, calls=%fused_computation.13 | convolution fusion | flops 4294967296 | bytes 14680068 | tf_op jit(solution)/shard_map/dot_general | solution.py:88
  36.7 12.8 %collective-permute-done.1 = bf16[512,64]{0,1:T(8,128)(2,1)S(1)} collective-permute-done((bf16[512,64]{0,1:T(8,128)(2,1)S(1)}, bf16[512,64]{0,1:T(8,128)(2,1)S(1)}, u32[]{:S(2)}, u32[]{:S(2)}) %collective-permute-start.1) | collective-permute-done | bytes 65568 | tf_op jit(solution)/shard_map/ppermute | solution.py:69
  49.8 1.6 %collective-permute-start.6 = (bf16[512,896]{1,0:T(8,128)(2,1)S(1)}, bf16[512,896]{1,0:T(8,128)(2,1)}, u32[]{:S(2)}, u32[]{:S(2)}) collective-permute-start(bf16[512,896]{1,0:T(8,128)(2,1)S(1)} %slice.54), channel_id=1, source_target_pairs={{4,8},{8,4},{5,9},{9,5},{6,10},{10,6},{7,11},{11,7},{20,24},{24,20... | collective-permute-start | bytes 2752520 | tf_op jit(solution)/shard_map/ppermute | solution.py:69
  52.1 8.8 %fusion.14 = f32[512,2048]{1,0:T(8,128)S(1)} fusion(f32[512,2048]{1,0:T(8,128)} %fusion.11, bf16[512,2048]{1,0:T(8,128)(2,1)S(1)} %collective-permute-done, bf16[8192,2048]{1,0:T(8,128)(2,1)} %param.6, s32[]{:T(128)S(6)} %select_n.79), kind=kOutput, calls=%fused_computation.14 | convolution fusion | flops 4296015872 | bytes 18874372 | tf_op jit(solution)/shard_map/dot_general | solution.py:88
  64.4 7.8 %collective-permute-done.3 = bf16[512,1024]{1,0:T(8,128)(2,1)S(1)} collective-permute-done((bf16[512,1024]{1,0:T(8,128)(2,1)}, bf16[512,1024]{1,0:T(8,128)(2,1)S(1)}, u32[]{:S(2)}, u32[]{:S(2)}) %collective-permute-start.3) | collective-permute-done | bytes 1048608 | tf_op jit(solution)/shard_map/ppermute | solution.py:69
  72.2 6.5 %fusion.17 = f32[512,2048]{1,0:T(8,128)} fusion(f32[512,2048]{1,0:T(8,128)S(1)} %fusion.14, bf16[8192,2048]{1,0:T(8,128)(2,1)} %param.6, s32[]{:T(128)S(6)} %select_n.83, bf16[512,1024]{1,0:T(8,128)(2,1)S(1)} %collective-permute-done.3, bf16[512,1024]{1,0:T(8,128)(2,1)} %collective-permute-done.2, pred[]{:T(512)S(6)} %or.3), kind=kOutput, calls=%fused_computation.15 | convolution fusion | flops 2149056512 | bytes 14680069 | tf_op jit(solution)/shard_map/dot_general | solution.py:88
  80.0 16.0 %collective-permute-done.8 = bf16[512,64]{0,1:T(8,128)(2,1)S(1)} collective-permute-done((bf16[512,64]{0,1:T(8,128)(2,1)S(1)}, bf16[512,64]{0,1:T(8,128)(2,1)S(1)}, u32[]{:S(2)}, u32[]{:S(2)}) %collective-permute-start.8) | collective-permute-done | bytes 65568 | tf_op jit(solution)/shard_map/ppermute | solution.py:69
  96.1 6.5 %fusion.5 = f32[512,2048]{1,0:T(8,128)} fusion(bf16[8192,2048]{1,0:T(8,128)(2,1)} %param.6, s32[]{:T(128)S(6)} %select_n.85, bf16[512,1024]{1,0:T(8,128)(2,1)S(1)} %collective-permute-done.5, bf16[512,1024]{1,0:T(8,128)(2,1)} %collective-permute-done.4, pred[]{:T(512)S(6)} %or.3), kind=kOutput, calls=%fused_computation.7 | convolution fusion | flops 2148007936 | bytes 10485765 | tf_op jit(solution)/shard_map/dot_general | solution.py:88
  103.7 2.9 %constant_dynamic-slice_fusion = bf16[1024,2048]{1,0:T(8,128)(2,1)S(1)} fusion(bf16[8192,2048]{1,0:T(8,128)(2,1)} %param.6, s32[]{:T(128)S(6)} %select_n.90), kind=kLoop, calls=%fused_computation.56 | loop fusion | bytes 8388612 | tf_op jit(solution)/shard_map/dynamic_slice | solution.py:117
  106.8 1.6 %collective-permute-start.11 = (bf16[512,1024]{1,0:T(8,128)(2,1)S(1)}, bf16[512,1024]{1,0:T(8,128)(2,1)S(1)}, u32[]{:S(2)}, u32[]{:S(2)}) collective-permute-start(bf16[512,1024]{1,0:T(8,128)(2,1)S(1)} %slice.60), channel_id=1, source_target_pairs={{4,0},{8,12},{5,1},{9,13},{6,2},{10,14},{7,3},{11,15},{20,16},{24,... | collective-permute-start | bytes 3145736 | tf_op jit(solution)/shard_map/ppermute | solution.py:69
  108.4 1.5 %collective-permute-start.12 = (bf16[512,128]{1,0:T(8,128)(2,1)S(1)}, bf16[512,128]{1,0:T(8,128)(2,1)S(1)}, u32[]{:S(2)}, u32[]{:S(2)}) collective-permute-start(bf16[512,128]{1,0:T(8,128)(2,1)S(1)} %slice.61), channel_id=1, source_target_pairs={{4,0},{8,12},{5,1},{9,13},{6,2},{10,14},{7,3},{11,15},{20,16},{24,... | collective-permute-start | bytes 393224 | tf_op jit(solution)/shard_map/ppermute | solution.py:69
  110.8 5.0 %collective-permute-done.10 = bf16[512,896]{1,0:T(8,128)(2,1)} collective-permute-done((bf16[512,896]{1,0:T(8,128)(2,1)}, bf16[512,896]{1,0:T(8,128)(2,1)}, u32[]{:S(2)}, u32[]{:S(2)}) %collective-permute-start.10) | collective-permute-done | bytes 917536 | tf_op jit(solution)/shard_map/ppermute | solution.py:69
  115.8 4.8 %fusion.4 = f32[512,2048]{1,0:T(8,128)S(1)} fusion(f32[256,2048]{1,0:T(8,128)S(1)} %fusion.36, f32[256,2048]{1,0:T(8,128)S(1)} %fusion.38, f32[512,2048]{1,0:T(8,128)S(1)} %copy-done.1, f32[512,2048]{1,0:T(8,128)S(1)} %copy-done.2, bf16[8192,2048]{1,0:T(8,128)(2,1)} %param.6, s32[]{:T(128)S(6)} %select_n.93, bf16[512,896]{1,0:T(8,128)(2,1)} %collective-permute-done.10, ...), kind=kOutput, calls=%fused_computation.5 | convolution fusion | flops 1883701248 | bytes 22282244 | tf_op jit(solution)/shard_map/dot_general | solution.py:88
  120.6 17.6 %collective-permute-done.11 = bf16[512,1024]{1,0:T(8,128)(2,1)S(1)} collective-permute-done((bf16[512,1024]{1,0:T(8,128)(2,1)S(1)}, bf16[512,1024]{1,0:T(8,128)(2,1)S(1)}, u32[]{:S(2)}, u32[]{:S(2)}) %collective-permute-start.11) | collective-permute-done | bytes 1048608 | tf_op jit(solution)/shard_map/ppermute | solution.py:69
  138.2 2.3 %convolution_add_fusion = f32[512,2048]{1,0:T(8,128)S(1)} fusion(f32[512,2048]{1,0:T(8,128)S(1)} %fusion.4, bf16[1024,2048]{1,0:T(8,128)(2,1)S(1)} %constant_dynamic-slice_fusion, bf16[512,1024]{1,0:T(8,128)(2,1)S(1)} %collective-permute-done.11, pred[]{:T(512)S(6)} %or.3, bf16[512,1152]{1,0:T(8,128)(2,1)S(1)} %collective-permute-done.9), kind=kOutput, calls=%fused_computation.16 | convolution fusion | flops 2149056512 | bytes 14680065 | tf_op jit(solution)/shard_map/dot_general | solution.py:125
  140.5 2.0 %add_convert_fusion = bf16[512,2048]{1,0:T(8,128)(2,1)} fusion(f32[512,2048]{1,0:T(8,128)S(1)} %convolution_add_fusion, bf16[128,2048]{1,0:T(8,128)(2,1)S(1)} %constant_dynamic-slice_fusion.1, bf16[512,128]{1,0:T(8,128)(2,1)S(1)} %collective-permute-done.12, pred[]{:T(512)S(6)} %or.3, bf16[512,1152]{1,0:T(8,128)(2,1)S(1)} %collective-permute-done.9), kind=kOutput, calls=%fused_computation.6 | convolution fusion | flops 270598144 | bytes 7077889 | tf_op jit(solution)/shard_map/dot_general | solution.py:127
  (32 shorter events, 10.5 us)
Async XLA Ops:
  0.0 109.8 %copy-start = (bf16[4,64,2048]{2,1,0:T(8,128)(2,1)S(1)}, bf16[4,64,2048]{2,1,0:T(8,128)(2,1)}, u32[]{:S(2)}) copy-start(bf16[4,64,2048]{2,1,0:T(8,128)(2,1)} %param.8) | copy-start | bytes 3145732
  0.0 49.7 %collective-permute-start = (bf16[512,2048]{1,0:T(8,128)(2,1)}, bf16[512,2048]{1,0:T(8,128)(2,1)S(1)}, u32[]{:S(2)}, u32[]{:S(2)}) collective-permute-start(bf16[512,2048]{1,0:T(8,128)(2,1)} %bitcast.41), channel_id=1, source_target_pairs={{0,4},{12,8},{4,0},{8,12},{1,5},{13,9},{5,1},{9,13},{2,6},{14,10},... | collective-permute-start | bytes 6291464 | tf_op jit(solution)/shard_map/ppermute | solution.py:69
  5.3 30.1 %collective-permute-start.2 = (bf16[512,1024]{1,0:T(8,128)(2,1)}, bf16[512,1024]{1,0:T(8,128)(2,1)}, u32[]{:S(2)}, u32[]{:S(2)}) collective-permute-start(bf16[512,1024]{1,0:T(8,128)(2,1)} %slice.62), channel_id=1, source_target_pairs={{4,8},{8,4},{5,9},{9,5},{6,10},{10,6},{7,11},{11,7},{20,24},{24,20... | collective-permute-start | bytes 3145736 | tf_op jit(solution)/shard_map/ppermute | solution.py:69
  15.6 33.9 %collective-permute-start.1 = (bf16[512,64]{0,1:T(8,128)(2,1)S(1)}, bf16[512,64]{0,1:T(8,128)(2,1)S(1)}, u32[]{:S(2)}, u32[]{:S(2)}) collective-permute-start(bf16[512,64]{0,1:T(8,128)(2,1)S(1)} %get-tuple-element.38), channel_id=1, source_target_pairs={{0,4},{12,8},{1,5},{13,9},{2,6},{14,10},{3,7},{15,11},{16,20},{28,... | collective-permute-start | bytes 196616 | tf_op jit(solution)/shard_map/ppermute | solution.py:69
  23.2 37.6 %collective-permute-start.4 = (bf16[512,1024]{1,0:T(8,128)(2,1)}, bf16[512,1024]{1,0:T(8,128)(2,1)}, u32[]{:S(2)}, u32[]{:S(2)}) collective-permute-start(bf16[512,1024]{1,0:T(8,128)(2,1)} %slice.53), channel_id=1, source_target_pairs={{4,8},{8,4},{5,9},{9,5},{6,10},{10,6},{7,11},{11,7},{20,24},{24,20... | collective-permute-start | bytes 3145736 | tf_op jit(solution)/shard_map/ppermute | solution.py:69
  35.4 36.7 %collective-permute-start.3 = (bf16[512,1024]{1,0:T(8,128)(2,1)}, bf16[512,1024]{1,0:T(8,128)(2,1)S(1)}, u32[]{:S(2)}, u32[]{:S(2)}) collective-permute-start(bf16[512,1024]{1,0:T(8,128)(2,1)} %collective-permute-done.2), channel_id=1, source_target_pairs={{4,0},{8,12},{5,1},{9,13},{6,2},{10,14},{7,3},{11,15},{20,16},{24,... | collective-permute-start | bytes 3145736 | tf_op jit(solution)/shard_map/ppermute | solution.py:69
  49.8 12.4 %collective-permute-start.6 = (bf16[512,896]{1,0:T(8,128)(2,1)S(1)}, bf16[512,896]{1,0:T(8,128)(2,1)}, u32[]{:S(2)}, u32[]{:S(2)}) collective-permute-start(bf16[512,896]{1,0:T(8,128)(2,1)S(1)} %slice.54), channel_id=1, source_target_pairs={{4,8},{8,4},{5,9},{9,5},{6,10},{10,6},{7,11},{11,7},{20,24},{24,20... | collective-permute-start | bytes 2752520 | tf_op jit(solution)/shard_map/ppermute | solution.py:69
  51.4 10.8 %collective-permute-start.7 = (bf16[2,512,64]{1,2,0:T(8,128)(2,1)S(1)}, bf16[2,512,64]{1,2,0:T(8,128)(2,1)S(1)}, u32[]{:S(2)}, u32[]{:S(2)}) collective-permute-start(bf16[2,512,64]{1,2,0:T(8,128)(2,1)S(1)} %pad_maximum_fusion), channel_id=1, source_target_pairs={{4,8},{8,4},{5,9},{9,5},{6,10},{10,6},{7,11},{11,7},{20,24},{24,20... | collective-permute-start | bytes 393224 | tf_op jit(solution)/shard_map/ppermute | solution.py:69
  60.8 35.2 %collective-permute-start.5 = (bf16[512,1024]{1,0:T(8,128)(2,1)}, bf16[512,1024]{1,0:T(8,128)(2,1)S(1)}, u32[]{:S(2)}, u32[]{:S(2)}) collective-permute-start(bf16[512,1024]{1,0:T(8,128)(2,1)} %collective-permute-done.4), channel_id=1, source_target_pairs={{4,0},{8,12},{5,1},{9,13},{6,2},{10,14},{7,3},{11,15},{20,16},{24,... | collective-permute-start | bytes 3145736 | tf_op jit(solution)/shard_map/ppermute | solution.py:69
  62.2 33.8 %collective-permute-start.8 = (bf16[512,64]{0,1:T(8,128)(2,1)S(1)}, bf16[512,64]{0,1:T(8,128)(2,1)S(1)}, u32[]{:S(2)}, u32[]{:S(2)}) collective-permute-start(bf16[512,64]{0,1:T(8,128)(2,1)S(1)} %fusion.46), channel_id=1, source_target_pairs={{4,0},{8,12},{5,1},{9,13},{6,2},{10,14},{7,3},{11,15},{20,16},{24,... | collective-permute-start | bytes 196616 | tf_op jit(solution)/shard_map/ppermute | solution.py:69
  63.6 39.0 %collective-permute-start.9 = (bf16[512,1152]{1,0:T(8,128)(2,1)S(1)}, bf16[512,1152]{1,0:T(8,128)(2,1)S(1)}, u32[]{:S(2)}, u32[]{:S(2)}) collective-permute-start(bf16[512,1152]{1,0:T(8,128)(2,1)S(1)} %slice.57), channel_id=1, source_target_pairs={{4,8},{8,4},{5,9},{9,5},{6,10},{10,6},{7,11},{11,7},{20,24},{24,20... | collective-permute-start | bytes 3538952 | tf_op jit(solution)/shard_map/ppermute | solution.py:69
  78.7 37.1 %collective-permute-start.10 = (bf16[512,896]{1,0:T(8,128)(2,1)}, bf16[512,896]{1,0:T(8,128)(2,1)}, u32[]{:S(2)}, u32[]{:S(2)}) collective-permute-start(bf16[512,896]{1,0:T(8,128)(2,1)} %collective-permute-done.6), channel_id=1, source_target_pairs={{4,0},{8,12},{5,1},{9,13},{6,2},{10,14},{7,3},{11,15},{20,16},{24,... | collective-permute-start | bytes 2752520 | tf_op jit(solution)/shard_map/ppermute | solution.py:69
  103.7 12.1 %copy-start.2 = (f32[512,2048]{1,0:T(8,128)S(1)}, f32[512,2048]{1,0:T(8,128)}, u32[]{:S(2)}) copy-start(f32[512,2048]{1,0:T(8,128)} %fusion.5) | copy-start | bytes 12582916
  106.6 9.2 %copy-start.1 = (f32[512,2048]{1,0:T(8,128)S(1)}, f32[512,2048]{1,0:T(8,128)}, u32[]{:S(2)}) copy-start(f32[512,2048]{1,0:T(8,128)} %fusion.17) | copy-start | bytes 12582916
  106.8 31.4 %collective-permute-start.11 = (bf16[512,1024]{1,0:T(8,128)(2,1)S(1)}, bf16[512,1024]{1,0:T(8,128)(2,1)S(1)}, u32[]{:S(2)}, u32[]{:S(2)}) collective-permute-start(bf16[512,1024]{1,0:T(8,128)(2,1)S(1)} %slice.60), channel_id=1, source_target_pairs={{4,0},{8,12},{5,1},{9,13},{6,2},{10,14},{7,3},{11,15},{20,16},{24,... | collective-permute-start | bytes 3145736 | tf_op jit(solution)/shard_map/ppermute | solution.py:69
  108.4 32.2 %collective-permute-start.12 = (bf16[512,128]{1,0:T(8,128)(2,1)S(1)}, bf16[512,128]{1,0:T(8,128)(2,1)S(1)}, u32[]{:S(2)}, u32[]{:S(2)}) collective-permute-start(bf16[512,128]{1,0:T(8,128)(2,1)S(1)} %slice.61), channel_id=1, source_target_pairs={{4,0},{8,12},{5,1},{9,13},{6,2},{10,14},{7,3},{11,15},{20,16},{24,... | collective-permute-start | bytes 393224 | tf_op jit(solution)/shard_map/ppermute | solution.py:69
